TPU v7x, 32 devices: a whole 2x2x4 slice. The times are simulated.
32 devices in a mesh: left: 8 (over z, y), right: 4 (over x, core).
Axes of the slice: x: 2, y: 2, z: 4, core: 2. Of those that a mesh axis runs over, the one named last changes fastest.
Arguments:
- left_table: float32 [4096, 400], P(('left', 'right')), may hold values from -2 to 2
- left_state: float32 [4096], P(('left', 'right')), may hold values from 0.05 to 0.5
- right_table: float32 [4096, 400], P(('left', 'right')), may hold values from -2 to 2
- right_state: float32 [4096], P(('left', 'right')), may hold values from 0.05 to 0.5
- relation_table: float32 [256, 400], replicated, may hold values from -6 to 6
- relation_state: float32 [256], replicated, may hold values from 0.05 to 0.5
- source_ids: int32 [8, 4, 1024], P('left', 'right'), may hold values from 0 to 511
- target_ids: int32 [8, 4, 1024], P('left', 'right'), may hold values from 0 to 1023
- relation_ids: int32 [8, 4, 1024], P('left', 'right'), may hold values from 0 to 255
- negative_ids: int32 [8, 4, 2, 1024], P('left', 'right'), may hold values from 0 to 1023
Outputs:
- left_new: float32 [4096, 400], P(('left', 'right'))
- left_state_new: float32 [4096], P(('left', 'right'))
- right_new: float32 [4096, 400], P(('left', 'right'))
- right_state_new: float32 [4096], P(('left', 'right'))
- relation_new: float32 [256, 400], replicated
- relation_state_new: float32 [256], replicated
All inputs are finite; a program needn't handle non-finite values.
Results may differ from a plain program's by a relative error of at most 0.0021.
Values may be sent and summed in bfloat16 or wider, within the bound.
No kernel may reach another device: no remote copies, remote signals or barrier semaphores. Data moves between devices by JAX's collectives and lax.ppermute only.
A program may use at most 64 MiB of HBM per device.

v0:
```python
import jax
import jax.numpy as jnp
from jax import lax
from jax.sharding import PartitionSpec as P

LEARN_RATE = 0.1
NEG_WEIGHT = 0.03125


def from_behind(value, axis, by):
    devices = lax.axis_size(axis)
    return lax.ppermute(value, axis, [(i, (i + by) % devices) for i in range(devices)])


def complex_product(first, second):
    half_width = first.shape[-1] // 2
    a_re, a_im = (first[..., :half_width], first[..., half_width:])
    b_re, b_im = (second[..., :half_width], second[..., half_width:])
    return jnp.concatenate([a_re * b_re - a_im * b_im, a_re * b_im + a_im * b_re], axis=-1)


def complex_back(grad, other):
    half_width = grad.shape[-1] // 2
    g_re, g_im = (grad[..., :half_width], grad[..., half_width:])
    o_re, o_im = (other[..., :half_width], other[..., half_width:])
    return jnp.concatenate([g_re * o_re + g_im * o_im, g_im * o_re - g_re * o_im], axis=-1)


def adagrad(table, state, grad):
    state_new = state + jnp.mean(grad * grad, axis=-1)
    return (table - LEARN_RATE * grad / jnp.sqrt(state_new)[:, None], state_new)


def one_hot_rows(ids, count):
    columns = jnp.arange(count, dtype=jnp.int32)
    return (ids[:, None] == columns[None, :]).astype(jnp.bfloat16)


def per_device(
    left_table,
    left_state,
    right_table,
    right_state,
    relation_table,
    relation_state,
    source_ids,
    target_ids,
    relation_ids,
    negative_ids,
):
    row_count = left_table.shape[0]
    width = left_table.shape[1]
    source = source_ids.reshape(-1)
    target = target_ids.reshape(-1)
    relation = relation_ids.reshape(-1)
    negative = negative_ids.reshape(negative_ids.shape[2], negative_ids.shape[3])
    groups = negative.shape[0]
    edge_count = source.shape[0]
    moved_table, moved_state = from_behind((right_table, right_state), "right", 1)
    right_part = lax.all_gather(moved_table.astype(jnp.bfloat16), "left", axis=0, tiled=True)
    piece = lax.all_gather(left_table.astype(jnp.bfloat16), "right", axis=0, tiled=True)
    onehot = one_hot_rows(source, piece.shape[0])
    source_emb = jnp.dot(onehot, piece, preferred_element_type=jnp.float32)
    target_hot = one_hot_rows(target, right_part.shape[0])
    target_embedding = jnp.dot(target_hot, right_part, preferred_element_type=jnp.float32)
    relation_bf = relation_table.astype(jnp.bfloat16)
    relation_hot = one_hot_rows(relation, relation_table.shape[0])
    relation_emb = jnp.dot(relation_hot, relation_bf, preferred_element_type=jnp.float32)
    query = complex_product(source_emb, relation_emb)
    positive = jnp.sum(query * target_embedding, axis=-1)
    query_block_rows = query.astype(jnp.bfloat16).reshape(groups, -1, width)
    negative_rows = jnp.take(right_part, negative, axis=0)
    score_matrix = jnp.einsum(
        "wet,wjt->wej", query_block_rows, negative_rows, preferred_element_type=jnp.float32
    )
    positive_score_grad = -jax.nn.sigmoid(-positive)
    negative_score_grad = (NEG_WEIGHT * jax.nn.sigmoid(score_matrix)).astype(jnp.bfloat16)
    from_negatives = jnp.einsum(
        "fjs,fsh->fjh", negative_score_grad, negative_rows, preferred_element_type=jnp.float32
    )
    query_gradient = positive_score_grad[:, None] * target_embedding + from_negatives.reshape(
        edge_count, width
    )
    negative_embedding_grad = (
        jnp.einsum(
            "fre,frl->fel",
            negative_score_grad,
            query_block_rows,
            preferred_element_type=jnp.float32,
        )
        .astype(jnp.bfloat16)
        .reshape(-1, width)
    )
    target_grad = (positive_score_grad[:, None] * query).astype(jnp.bfloat16)
    source_grad = complex_back(query_gradient, relation_emb).astype(jnp.bfloat16)
    relation_grad = complex_back(query_gradient, source_emb).astype(jnp.bfloat16)
    relation_term = jnp.einsum(
        "er,ed->rd", relation_hot, relation_grad, preferred_element_type=jnp.float32
    )
    onehot = one_hot_rows(source, lax.axis_size("right") * row_count)
    left_grad = lax.psum_scatter(
        jnp.einsum("er,ed->rd", onehot, source_grad, preferred_element_type=jnp.float32),
        "right",
        scatter_dimension=0,
        tiled=True,
    )
    all_ids = jnp.concatenate([target, negative.reshape(-1)])
    all_grads = jnp.concatenate([target_grad, negative_embedding_grad], axis=0)
    onehot = one_hot_rows(all_ids, lax.axis_size("left") * row_count)
    right_grad = lax.psum_scatter(
        jnp.einsum("er,ed->rd", onehot, all_grads, preferred_element_type=jnp.float32),
        "left",
        scatter_dimension=0,
        tiled=True,
    )
    left_new, left_state_new = adagrad(left_table, left_state, left_grad)
    right_new, right_state_new = adagrad(moved_table, moved_state, right_grad)
    relation_total = lax.psum(relation_term, ("left", "right"))
    relation_new, relation_state_new = adagrad(relation_table, relation_state, relation_total)
    return (left_new, left_state_new, right_new, right_state_new, relation_new, relation_state_new)


def solution(mesh):
    return jax.shard_map(
        per_device,
        mesh=mesh,
        in_specs=(
            P(("left", "right"), None),
            P(("left", "right")),
            P(("left", "right"), None),
            P(("left", "right")),
            P(),
            P(),
            P("left", "right", None),
            P("left", "right", None),
            P("left", "right", None),
            P("left", "right", None, None),
        ),
        out_specs=(
            P(("left", "right"), None),
            P(("left", "right")),
            P(("left", "right"), None),
            P(("left", "right")),
            P(),
            P(),
        ),
        check_vma=False,
    )
```

profile of v0, /device:TPU:0, one launch (start us, length us, event | category | flops | bytes accessed | tf_op | source)
XLA Modules:
  0.0 221.8 jit_solution(9266575794216112300)
XLA Ops:
  8.0 0.0 copy-start.5
  8.0 0.0 all-reduce.2.cloned.1.call-start
  8.1 0.5 collective-permute-start
  8.6 0.7 fusion.25
  9.3 0.9 convert_element_type.13
  10.2 7.5 %all_gather.6 = bf16[512,400]{0,1:T(8,128)(2,1)S(1)} all-gather(bf16[128,400]{0,1:T(8,128)(2,1)S(1)} %convert_element_type.13), channel_id=1, replica_groups=mesh['left'=8,'right'=4] {'right'}, dimensions={0}, use_global_device_ids=true | all-gather | bytes 512000 | tf_op jit(solution)/shard_map/all_gather | solution.py:61
  17.7 1.5 fusion.8
  19.3 0.5 fusion.11
  19.8 1.6 fusion.34
  21.4 0.6 copy-done.13
  22.1 0.8 copy-done.10
  22.9 0.1 copy-done.8
  23.0 30.5 %all_gather.7 = bf16[1024,400]{0,1:T(8,128)(2,1)S(1)} all-gather(bf16[128,400]{0,1:T(8,128)(2,1)S(1)} %convert_element_type.29), channel_id=1, replica_groups=mesh['left'=8,'right'=4] {'left'}, dimensions={0}, use_global_device_ids=true | all-gather | bytes 921600 | tf_op jit(solution)/shard_map/all_gather | solution.py:60
  53.5 0.5 copy.24
  54.0 9.2 %gather_fusion = bf16[2048,400]{1,0:T(8,128)(2,1)} fusion(bf16[1024,400]{1,0:T(8,128)(2,1)S(1)} %copy.24, s32[2048]{0:T(1024)S(1)} %bitcast_clamp_fusion), kind=kCustom, calls=%fused_computation | custom fusion | bytes 3284992 | tf_op jit(solution)/shard_map/jit(_take)/gather | solution.py:72
  63.2 4.0 %copy.25 = bf16[2,1024,400]{1,2,0:T(8,128)(2,1)} copy(bf16[2,1024,400]{2,1,0:T(8,128)(2,1)} %bitcast.35) | data formatting | bytes 3276800 | tf_op jit(solution)/shard_map/jit(_take)/gather | solution.py:72
  67.2 2.6 %multiply_reduce_fusion = (f32[1024]{0:T(1024)S(1)}, f32[1024,400]{0,1:T(8,128)S(1)}) fusion(f32[1024,200]{0,1:T(8,128)S(1)} %copy-done.2, f32[1024,200]{0,1:T(8,128)} %get-tuple-element.21, bf16[1024,400]{0,1:T(8,128)(2,1)S(1)} %all_gather.7, s32[1024]{0:T(1024)S(1)} %bitcast.44), kind=kOutput, calls=%fused_computation.18 | convolution fusion | flops 841137152 | bytes 4104192 | tf_op jit(solution)/shard_map/dot_general | solution.py:65
  69.8 1.8 multiply_convert_fusion
  71.7 1.0 convolution_bitcast_fusion
  72.7 0.3 copy-done.20
  73.0 0.2 copy.30
  73.2 1.0 copy-done.3
  74.1 0.8 multiply_convert_fusion.1
  74.9 0.7 copy-done.1
  75.6 0.7 add_convert_fusion
  76.2 0.0 copy-start.18
  76.3 1.3 fusion.10
  77.5 0.0 all-reduce.2.cloned.1.call-update
  77.5 0.0 reduce-scatter.3.cloned.1.call-start
  77.6 1.6 fusion.7
  79.2 0.0 reduce-scatter.3.cloned.1.call-update
  79.3 0.2 reduce-scatter.5.cloned.1.call-start
  79.5 2.6 %fusion.9 = bf16[2,50,8,1024]{3,2,1,0:T(8,128)(2,1)S(1)} fusion(bf16[2,512,400]{1,2,0:T(8,128)(2,1)S(1)} %copy-done.12, bf16[2,512,1024]{2,1,0:T(8,128)(2,1)} %copy-done.20), kind=kOutput, calls=%fused_computation.20 | convolution fusion | flops 839680000 | bytes 4554752 | tf_op jit(solution)/shard_map/fre,frl->fel/dot_general | solution.py:85
  82.1 0.2 copy.31
  82.3 4.3 %fusion = f32[1024,400]{0,1:T(8,128)} fusion(s32[3072]{0:T(1024)S(1)} %pad_add_fusion, bf16[2048,400]{0,1:T(8,128)(2,1)S(1)} %bitcast.39, bf16[1024,400]{0,1:T(8,128)(2,1)S(1)} %get-tuple-element.24), kind=kOutput, calls=%fused_computation.2 | convolution fusion | flops 2524643328 | bytes 4108288 | tf_op jit(solution)/shard_map/er,ed->rd/dot_general | solution.py:111
  86.6 0.0 copy-start.7
  86.6 0.0 reduce-scatter.5.cloned.1.call-update
  86.6 0.6 copy-done.19
  87.2 117.4 %all-reduce.2.cloned.1.call-done = f32[256,400]{0,1:T(8,128)} async-done(((f32[256,400]{0,1:T(8,128)}), f32[256,400]{0,1:T(8,128)}) %all-reduce.2.cloned.1.call-update) | async-done | bytes 409616 | tf_op jit(solution)/shard_map/psum | solution.py:118
  204.6 1.1 multiply_reduce_fusion.1
  205.7 0.6 fusion.31
  206.2 1.8 divide_subtract_fusion
  208.1 1.0 multiply_reduce_fusion.3
  209.1 0.5 fusion.33
  209.6 1.6 divide_subtract_fusion.2
  211.2 1.0 multiply_reduce_fusion.2
  212.2 0.5 fusion.32
  212.7 1.6 divide_subtract_fusion.1
  (45 shorter events, 0.2 us)
Async XLA Ops:
  8.0 11.2 %copy-start.5 = (f32[256,400]{0,1:T(8,128)S(1)}, f32[256,400]{0,1:T(8,128)}, u32[]{:S(2)}) copy-start(f32[256,400]{0,1:T(8,128)} %param.14) | copy-start | bytes 1228804
  8.0 11.2 %copy-start.14 = (s32[1,1,1024]{2,1,0:T(1,128)S(1)}, s32[1,1,1024]{2,1,0:T(1,128)}, u32[]{:S(2)}) copy-start(s32[1,1,1024]{2,1,0:T(1,128)} %param.18) | copy-start | bytes 12292
  8.0 196.6 %all-reduce.2.cloned.1.call-start = ((), (), s32[]{:S(2)}) async-start(), calls=%async_computation.4 | async-start | bytes 819200 | tf_op jit(solution)/shard_map/psum | solution.py:118
  8.1 14.0 %collective-permute-start = (f32[128,400]{0,1:T(8,128)}, f32[128,400]{0,1:T(8,128)S(1)}, u32[]{:S(2)}, u32[]{:S(2)}) collective-permute-start(f32[128,400]{0,1:T(8,128)} %param.12), channel_id=1, source_target_pairs={{0,1},{1,2},{2,3},{3,0},{4,5},{5,6},{6,7},{7,4},{8,9},{9,10},{10,1... | collective-permute-start | bytes 614408 | tf_op jit(solution)/shard_map/ppermute | solution.py:12
  19.2 2.1 copy-start
  21.3 0.7 copy-start.13
  22.0 0.9 copy-start.10
  22.1 0.9 copy-start.8
  63.2 4.0 %copy-start.2 = (f32[1024,200]{0,1:T(8,128)S(1)}, f32[1024,200]{0,1:T(8,128)}, u32[]{:S(2)}) copy-start(f32[1024,200]{0,1:T(8,128)} %get-tuple-element.13) | copy-start | bytes 2457604
  63.2 4.0 %copy-start.15 = (s32[1,1,1024]{2,1,0:T(1,128)S(1)}, s32[1,1,1024]{2,1,0:T(1,128)}, u32[]{:S(2)}) copy-start(s32[1,1,1024]{2,1,0:T(1,128)} %param.17) | copy-start | bytes 12292
  67.2 2.6 %copy-start.4 = (bf16[2,1024,400]{1,2,0:T(8,128)(2,1)S(1)}, bf16[2,1024,400]{1,2,0:T(8,128)(2,1)}, u32[]{:S(2)}) copy-start(bf16[2,1024,400]{1,2,0:T(8,128)(2,1)} %copy.25) | copy-start | bytes 4915204
  67.2 2.6 %copy-start.11 = (bf16[2,512,400]{1,2,0:T(8,128)(2,1)S(1)}, bf16[2,512,400]{1,2,0:T(8,128)(2,1)}, u32[]{:S(2)}) copy-start(bf16[2,512,400]{1,2,0:T(8,128)(2,1)} %copy-done.10) | copy-start | bytes 2457604
  71.6 1.3 copy-start.20
  73.0 1.1 copy-start.3
  74.1 1.4 copy-start.1
  76.2 1.3 copy-start.18
  77.5 130.5 %reduce-scatter.3.cloned.1.call-start = ((), (), s32[]{:S(2)}) async-start(), calls=%async_computation.2 | async-start | bytes 1024000 | tf_op jit(solution)/shard_map/reduce_scatter | solution.py:101
  77.6 1.9 copy-start.12
  79.3 132.0 %reduce-scatter.5.cloned.1.call-start = ((), (), s32[]{:S(2)}) async-start(), calls=%async_computation.3 | async-start | bytes 1843200 | tf_op jit(solution)/shard_map/reduce_scatter | solution.py:110
  86.6 0.7 copy-start.19
  86.6 119.1 %copy-start.16 = (f32[256]{0:T(256)S(1)}, f32[256]{0:T(256)}, u32[]{:S(2)}) copy-start(f32[256]{0:T(256)} %param.15) | copy-start | bytes 3076
  86.6 119.7 %copy-start.6 = (f32[256,400]{0,1:T(8,128)S(1)}, f32[256,400]{0,1:T(8,128)}, u32[]{:S(2)}) copy-start(f32[256,400]{0,1:T(8,128)} %param.14) | copy-start | bytes 1228804
  86.6 122.5 %copy-start.17 = (f32[128]{0:T(128)S(1)}, f32[128]{0:T(128)}, u32[]{:S(2)}) copy-start(f32[128]{0:T(128)} %param.11) | copy-start | bytes 1540
  86.6 123.0 %copy-start.7 = (f32[128,400]{0,1:T(8,128)S(1)}, f32[128,400]{0,1:T(8,128)}, u32[]{:S(2)}) copy-start(f32[128,400]{0,1:T(8,128)} %param.10) | copy-start | bytes 614404
  87.2 125.5 %copy-start.9 = (f32[128,400]{0,1:T(8,128)S(1)}, f32[128,400]{0,1:T(8,128)}, u32[]{:S(2)}) copy-start(f32[128,400]{0,1:T(8,128)} %copy-done.8) | copy-start | bytes 614404
  87.2 125.0 %collective-permute-start.1 = (f32[128]{0:T(128)S(1)}, f32[128]{0:T(128)S(1)}, u32[]{:S(2)}, u32[]{:S(2)}) collective-permute-start(f32[128]{0:T(128)S(1)} %copy-done.19), channel_id=1, source_target_pairs={{0,1},{1,2},{2,3},{3,0},{4,5},{5,6},{6,7},{7,4},{8,9},{9,10},{10,1... | collective-permute-start | bytes 1544 | tf_op jit(solution)/shard_map/ppermute | solution.py:12
Sparse Core Ops, SparseCore 0:
  77.7 126.9 all-reduce.1
Sparse Core Ops, SparseCore 1:
  80.5 21.5 reduce-scatter.2
  105.9 63.9 reduce-scatter.4
where the time goes:
time: 223 us; the launch traced here: 222 us
  waiting for transfers between devices  117 us (52%)
  blocking collectives  38 us (17%)
  local copies, waits for them, and re-layouts  18.2 us (8%)
  matrix products  17.2 us (8%)
  between operations  15.8 us (7%)
  other arithmetic  14.4 us (6%)
    psum x1, waiting for transfers between devices, per_device(): relation_total = lax.psum(relation_term, ('left', 'right'))  117 us
    all_gather x1, blocking collectives, per_device(): lax.all_gather(moved_table.astype(jnp.bfloat16), 'left', axis=0, tiled=True)  30.5 us
    gather x2, local copies, waits for them, and re-layouts, per_device(): negative_rows = jnp.take(right_part, negative, axis=0)  13.2 us
    all_gather x1, blocking collectives, per_device(): lax.all_gather(left_table.astype(jnp.bfloat16), 'right', axis=0, tiled=True)  7.51 us
    sub x3, other arithmetic, adagrad(): return (table - LEARN_RATE * grad / jnp.sqrt(state_new)[:, None], state_new)  5.08 us
  transfers between devices with their start and end apart: 5, of which 1 were waited for; matrix products, arithmetic and copies ran while one was open for 10% of the time, Pallas kernels for 0%

commit v1 on v0

v1 whole, which is shorter than its diff:
```python
import jax
import jax.numpy as jnp
from jax import lax
from jax.sharding import PartitionSpec as P

LEARN_RATE = 0.1
NEG_WEIGHT = 0.03125
BF = jnp.bfloat16
F32 = jnp.float32


def dot(a, b, a_dim, b_dim):
    return lax.dot_general(a, b, (((a_dim,), (b_dim,)), ((), ())), preferred_element_type=F32)


def complex_product(a, b):
    half = a.shape[0] // 2
    a_re, a_im, b_re, b_im = a[:half], a[half:], b[:half], b[half:]
    return jnp.concatenate([a_re * b_re - a_im * b_im, a_re * b_im + a_im * b_re], axis=0)


def complex_back(grad, other):
    half = grad.shape[0] // 2
    g_re, g_im, o_re, o_im = grad[:half], grad[half:], other[:half], other[half:]
    return jnp.concatenate([g_re * o_re + g_im * o_im, g_im * o_re - g_re * o_im], axis=0)


def adagrad(table, state, grad):
    state_new = state + jnp.mean(grad * grad, axis=0)
    return table - LEARN_RATE * grad * lax.rsqrt(state_new)[None, :], state_new


def one_hot(ids, count):
    return (jnp.arange(count, dtype=jnp.int32)[:, None] == ids[None, :]).astype(BF)


def build(mesh):
    n_left, n_right = mesh.shape["left"], mesh.shape["right"]
    inner = 2 if n_left % 2 == 0 else 1
    outer = n_left // inner

    def send_left(value, d_outer, d_inner):
        perm = []
        for i in range(n_left):
            o, n = i // inner, i % inner
            perm.append((i, (o + d_outer) % outer * inner + (n + d_inner) % inner))
        return lax.ppermute(value, "left", perm)

    def send_right(value, by):
        return lax.ppermute(value, "right", [(i, (i + by) % n_right) for i in range(n_right)])

    def send_both(value, d_outer, d_right):
        perm = []
        for i in range(n_left):
            for r in range(n_right):
                o, n = i // inner, i % inner
                to = (o + d_outer) % outer * inner + n
                perm.append((i * n_right + r, to * n_right + (r + d_right) % n_right))
        return lax.ppermute(value, ("left", "right"), perm)

    def per_device(
        left_table, left_state, right_table, right_state, relation_table, relation_state,
        source_ids, target_ids, relation_ids, negative_ids,
    ):
        rows = left_table.shape[0]
        width = left_table.shape[1]
        left_t, right_t, relation_t = left_table.T, right_table.T, relation_table.T
        nrel = relation_t.shape[1]
        here_l, here_r = lax.axis_index("left"), lax.axis_index("right")
        here_o, here_n = here_l // inner, here_l % inner
        source = source_ids.reshape(-1)
        target = target_ids.reshape(-1)
        relation = relation_ids.reshape(-1)
        negative = negative_ids.reshape(negative_ids.shape[2], negative_ids.shape[3])
        groups = negative.shape[0]

        right_bf = right_t.astype(BF)
        left_bf = left_t.astype(BF)
        near = [send_both(right_bf, k, 1) for k in range(outer)]
        left_blocks = [left_bf] + [send_right(left_bf, k) for k in range(1, n_right)]
        moved_t, moved_state = send_right((right_t, right_state), 1)
        right_blocks = list(near)
        for n in range(1, inner):
            right_blocks += [send_left(b, 0, n) for b in near]
        left_part = jnp.concatenate(left_blocks, axis=1)

        def local_left(ids):
            return (here_r - ids // rows) % n_right * rows + ids % rows

        def local_right(ids):
            block = ids // rows
            return ((here_n - block % inner) % inner * outer + (here_o - block // inner) % outer) * rows + ids % rows

        source = local_left(source)
        target = local_right(target)
        negative = local_right(negative)

        n_rows = n_left * rows
        counts = [
            jnp.sum((jnp.arange(n_rows, dtype=jnp.int32)[:, None] == negative[c][None, :]).astype(F32), axis=1)
            for c in range(groups)
        ]
        source_hot = one_hot(source, n_right * rows)
        relation_hot = one_hot(relation, nrel)
        source_emb = dot(left_part, source_hot, 1, 0)
        relation_emb = dot(relation_t.astype(BF), relation_hot, 1, 0)
        query = complex_product(source_emb, relation_emb)
        query_bf = query.astype(BF)

        right_part = jnp.concatenate(right_blocks, axis=1)
        scores = dot(right_part, query_bf, 0, 0)
        hit = jnp.arange(n_rows, dtype=jnp.int32)[:, None] == target[None, :]
        edges = scores.shape[1]
        weight = jnp.concatenate(
            [jnp.broadcast_to((NEG_WEIGHT * c)[:, None], (n_rows, edges // groups)) for c in counts], axis=1
        )
        grad_m = (weight * jax.nn.sigmoid(scores) - jnp.where(hit, jax.nn.sigmoid(-scores), 0.0)).astype(BF)
        right_grad = dot(query_bf, grad_m, 1, 1)
        if inner > 1:
            far = right_grad[:, outer * rows:].astype(BF)
            mine = right_grad[:, : outer * rows]
            mine = mine + send_left(far, 0, 1).astype(F32)
        else:
            mine = right_grad
        mine_bf = mine.astype(BF)
        right_sum = mine[:, :rows]
        for k in range(1, outer):
            right_sum = right_sum + send_left(mine_bf[:, k * rows:(k + 1) * rows], -k, 0).astype(F32)

        query_grad = dot(right_part, grad_m, 1, 0)
        relation_grad = complex_back(query_grad, source_emb).astype(BF)
        relation_term = dot(relation_hot, relation_grad, 1, 1)
        source_grad = complex_back(query_grad, relation_emb).astype(BF)
        left_grad = dot(source_grad, source_hot, 1, 1)
        left_sum = left_grad[:, :rows]
        left_grad_bf = left_grad.astype(BF)
        for k in range(1, n_right):
            left_sum = left_sum + send_right(left_grad_bf[:, k * rows:(k + 1) * rows], -k).astype(F32)

        rel_rows = nrel // n_left
        pieces = relation_term.reshape(n_left, rel_rows, width)
        pieces_bf = pieces.astype(BF)

        def left_shift(value, by):
            return lax.ppermute(value, "left", [(i, (i + by) % n_left) for i in range(n_left)])

        total = lax.dynamic_index_in_dim(pieces, here_l, 0, keepdims=False)
        for k in range(1, n_left):
            piece = lax.dynamic_index_in_dim(pieces_bf, (here_l + k) % n_left, 0, keepdims=False)
            total = total + left_shift(piece, k).astype(F32)
        total_bf = total.astype(BF)
        parts = [total_bf] + [send_right(total_bf, k) for k in range(1, n_right)]
        stack = jnp.stack(parts)
        order = (here_r - jnp.arange(n_right)) % n_right
        summed = jnp.sum(jnp.take(stack, order, axis=0).astype(F32), axis=0).astype(BF)
        got = [summed] + [left_shift(summed, k) for k in range(1, n_left)]
        where = (here_l - jnp.arange(n_left)) % n_left
        relation_total = jnp.take(jnp.stack(got), where, axis=0).reshape(nrel, width).astype(F32)

        left_new, left_state_new = adagrad(left_t, left_state, left_sum)
        right_new, right_state_new = adagrad(moved_t, moved_state, right_sum)
        relation_new, relation_state_new = adagrad(relation_t, relation_state, relation_total.T)
        return (left_new.T, left_state_new, right_new.T, right_state_new, relation_new.T, relation_state_new)

    return per_device


def solution(mesh):
    rows = P(("left", "right"), None)
    vector = P(("left", "right"))
    ids = P("left", "right", None)
    return jax.shard_map(
        build(mesh),
        mesh=mesh,
        in_specs=(rows, vector, rows, vector, P(), P(), ids, ids, ids, P("left", "right", None, None)),
        out_specs=(rows, vector, rows, vector, P(), P()),
        check_vma=False,
    )
```

time: 223 us -> 114 us (0.51)
  waiting for transfers between devices: 117 us -> 45.5 us
  starting transfers between devices: 0.81 us -> 40.2 us
  blocking collectives: 38 us -> 0 us
  between operations: 15.8 us -> 1.08 us
  local copies, waits for them, and re-layouts: 18.2 us -> 5.72 us
  matrix products: 17.2 us -> 9.11 us
    psum x1 -> x0, waiting for transfers between devices: 117 us -> none  [per_device(): relation_total = lax.psum(relation_term, ('left', 'right'))]
    ppermute x2 -> x37, waiting for transfers between devices: 0.01 us -> 45.5 us  [the longest x14 29.6 us: left_shift(): lax.ppermute(value, 'left', [(i, (i + by) % n_left) for i in range(n_left)])]
    ppermute x2 -> x37, starting transfers between devices: 0.51 us -> 40.2 us  [the longest x14 16.9 us: left_shift(): lax.ppermute(value, 'left', [(i, (i + by) % n_left) for i in range(n_left)])]
    all_gather x2 -> x0, blocking collectives: 38 us -> none  [the longest x1 30.5 us: per_device(): lax.all_gather(moved_table.astype(jnp.bfloat16), 'left', axis=0, tiled=True)]
    gather x2, local copies, waits for them, and re-layouts: 13.2 us -> 1.12 us  [the longest x1 0.56 us: per_device(): jnp.take(jnp.stack(got), where, axis=0).reshape(nrel, width).astype(F32)]
    dot_general x9 -> x7, matrix products: 17.2 us -> 9.11 us  [dot(): lax.dot_general(a, b, (((a_dim,), (b_dim,)), ((), ())), preferred_element...]
    sub x3 -> x1, other arithmetic: 5.08 us -> 0.15 us  [adagrad(): table - LEARN_RATE * grad * lax.rsqrt(state_new)[None, :]]
    transpose x0 -> x2, other arithmetic: none -> 2.52 us  [per_device(): return (left_new.T, left_state_new, right_new.T, right_state_new, relatio...]
  transfers between devices with their start and end apart: 5 -> 37, of which waited for: 1 -> 16; matrix products, arithmetic and copies ran while one was open for 10% -> 17% of each run, Pallas kernels for 0% -> 0%
where the time goes in v1:
time: 114 us
  waiting for transfers between devices  45.5 us (40%)
  starting transfers between devices  40.2 us (35%)
  other arithmetic  12.3 us (11%)
  matrix products  9.11 us (8%)
  local copies, waits for them, and re-layouts  5.72 us (5%)
    ppermute x14, waiting for transfers between devices, left_shift(): lax.ppermute(value, 'left', [(i, (i + by) % n_left) for i in range(n_left)])  29.6 us
    ppermute x14, starting transfers between devices, left_shift(): lax.ppermute(value, 'left', [(i, (i + by) % n_left) for i in range(n_left)])  16.9 us
    ppermute x8, waiting for transfers between devices, send_left(): return lax.ppermute(value, 'left', perm)  11.9 us
    dot_general x7, matrix products, dot(): lax.dot_general(a, b, (((a_dim,), (b_dim,)), ((), ())), preferred_element...  9.11 us
    ppermute x8, starting transfers between devices, send_left(): return lax.ppermute(value, 'left', perm)  9.02 us
    ppermute x4, starting transfers between devices, send_both(): return lax.ppermute(value, ('left', 'right'), perm)  8.41 us
    ppermute x11, starting transfers between devices, send_right(): lax.ppermute(value, 'right', [(i, (i + by) % n_right) for i in range(n_ri...  5.93 us
    ppermute x11, waiting for transfers between devices, send_right(): lax.ppermute(value, 'right', [(i, (i + by) % n_right) for i in range(n_ri...  2.66 us
  transfers between devices with their start and end apart: 37, of which 16 were waited for; matrix products, arithmetic and copies ran while one was open for 17% of the time, Pallas kernels for 0%

profile of v1, /device:TPU:0, one launch (start us, length us, event | category | flops | bytes accessed | tf_op | source)
XLA Modules:
  0.0 114.0 jit_solution(2350956666813830442)
XLA Ops:
  0.6 1.0 bitcast_convert_fusion.1
  2.1 3.8 %collective-permute-start.1 = (bf16[400,128]{1,0:T(8,128)(2,1)S(1)}, bf16[400,128]{1,0:T(8,128)(2,1)S(1)}, u32[]{:S(2)}, u32[]{:S(2)}) collective-permute-start(bf16[400,128]{1,0:T(8,128)(2,1)S(1)} %bitcast_convert_fusion.1), channel_id=1, source_target_pairs={{0,9},{1,10},{2,11},{3,8},{4,13},{5,14},{6,15},{7,12},{8,17},{9,18... | collective-permute-start | bytes 307208 | tf_op jit(solution)/shard_map/ppermute | solution.py:59
  5.9 0.9 bitcast_convert_fusion
  7.4 1.1 collective-permute-start.9
  8.5 0.8 fusion.41
  11.8 1.2 %copy.20 = f32[256,400]{1,0:T(8,128)S(1)} copy(f32[256,400]{0,1:T(8,128)} %param.14) | data formatting | bytes 819200 | tf_op args[4]
  13.0 1.1 convolution_bitcast_fusion
  14.4 2.6 %collective-permute-start.2 = (bf16[400,128]{1,0:T(8,128)(2,1)S(1)}, bf16[400,128]{1,0:T(8,128)(2,1)S(1)}, u32[]{:S(2)}, u32[]{:S(2)}) collective-permute-start(bf16[400,128]{1,0:T(8,128)(2,1)S(1)} %bitcast_convert_fusion.1), channel_id=1, source_target_pairs={{0,17},{1,18},{2,19},{3,16},{4,21},{5,22},{6,23},{7,20},{8,25},{9,... | collective-permute-start | bytes 307208 | tf_op jit(solution)/shard_map/ppermute | solution.py:59
  17.0 1.5 %collective-permute-start.3 = (bf16[400,128]{1,0:T(8,128)(2,1)S(1)}, bf16[400,128]{1,0:T(8,128)(2,1)S(1)}, u32[]{:S(2)}, u32[]{:S(2)}) collective-permute-start(bf16[400,128]{1,0:T(8,128)(2,1)S(1)} %bitcast_convert_fusion.1), channel_id=1, source_target_pairs={{0,25},{1,26},{2,27},{3,24},{4,29},{5,30},{6,31},{7,28},{8,1},{9,2... | collective-permute-start | bytes 307208 | tf_op jit(solution)/shard_map/ppermute | solution.py:59
  19.6 1.6 %collective-permute-start.4 = (bf16[400,128]{1,0:T(8,128)(2,1)S(1)}, bf16[400,128]{1,0:T(8,128)(2,1)S(1)}, u32[]{:S(2)}, u32[]{:S(2)}) collective-permute-start(bf16[400,128]{1,0:T(8,128)(2,1)S(1)} %collective-permute-done), channel_id=1, source_target_pairs={{0,4},{4,0},{8,12},{12,8},{16,20},{20,16},{24,28},{28,24},{1,5},{5... | collective-permute-start | bytes 307208 | tf_op jit(solution)/shard_map/ppermute | solution.py:47
  21.8 1.4 %collective-permute-done.2 = bf16[400,128]{1,0:T(8,128)(2,1)S(1)} collective-permute-done((bf16[400,128]{1,0:T(8,128)(2,1)S(1)}, bf16[400,128]{1,0:T(8,128)(2,1)S(1)}, u32[]{:S(2)}, u32[]{:S(2)}) %collective-permute-start.2) | collective-permute-done | bytes 102432 | tf_op jit(solution)/shard_map/ppermute | solution.py:59
  23.2 1.5 %collective-permute-start.6 = (bf16[400,128]{1,0:T(8,128)(2,1)S(1)}, bf16[400,128]{1,0:T(8,128)(2,1)S(1)}, u32[]{:S(2)}, u32[]{:S(2)}) collective-permute-start(bf16[400,128]{1,0:T(8,128)(2,1)S(1)} %collective-permute-done.2), channel_id=1, source_target_pairs={{0,4},{4,0},{8,12},{12,8},{16,20},{20,16},{24,28},{28,24},{1,5},{5... | collective-permute-start | bytes 307208 | tf_op jit(solution)/shard_map/ppermute | solution.py:47
  25.4 2.2 %collective-permute-done.5 = bf16[400,128]{1,0:T(8,128)(2,1)S(1)} collective-permute-done((bf16[400,128]{1,0:T(8,128)(2,1)S(1)}, bf16[400,128]{1,0:T(8,128)(2,1)S(1)}, u32[]{:S(2)}, u32[]{:S(2)}) %collective-permute-start.5) | collective-permute-done | bytes 102432 | tf_op jit(solution)/shard_map/ppermute | solution.py:47
  27.6 2.2 %collective-permute-done.6 = bf16[400,128]{1,0:T(8,128)(2,1)S(1)} collective-permute-done((bf16[400,128]{1,0:T(8,128)(2,1)S(1)}, bf16[400,128]{1,0:T(8,128)(2,1)S(1)}, u32[]{:S(2)}, u32[]{:S(2)}) %collective-permute-start.6) | collective-permute-done | bytes 102432 | tf_op jit(solution)/shard_map/ppermute | solution.py:47
  29.8 2.0 %collective-permute-done.7 = bf16[400,128]{1,0:T(8,128)(2,1)S(1)} collective-permute-done((bf16[400,128]{1,0:T(8,128)(2,1)S(1)}, bf16[400,128]{1,0:T(8,128)(2,1)S(1)}, u32[]{:S(2)}, u32[]{:S(2)}) %collective-permute-start.7) | collective-permute-done | bytes 102432 | tf_op jit(solution)/shard_map/ppermute | solution.py:47
  32.3 3.3 %fusion.1 = bf16[1024,1024]{1,0:T(8,128)(2,1)S(1)} fusion(f32[1024,512]{1,0:T(8,128)S(1)} %broadcast_in_dim.51, f32[1024,512]{1,0:T(8,128)S(1)} %broadcast_in_dim.50, s32[1024]{0:T(1024)S(1)} %fusion.53, bf16[400,1024]{1,0:T(8,128)(2,1)S(1)} %constant_dynamic-update-slice_fusion, bf16[200,1024]{1,0:T(8,128)(2,1)S(1)} %get-tuple-element.31, ...), kind=kOutput, calls=%fused_computation.4 | convolution fusion | flops 852033536 | bytes 7933952 | tf_op jit(solution)/shard_map/dot_general | solution.py:13
  35.6 1.0 fusion.76
  37.9 1.6 %collective-permute-start.20 = (bf16[32,400]{1,0:T(8,128)(2,1)S(1)}, bf16[32,400]{1,0:T(8,128)(2,1)S(1)}, u32[]{:S(2)}, u32[]{:S(2)}) collective-permute-start(bf16[32,400]{1,0:T(8,128)(2,1)S(1)} %get-tuple-element.40), channel_id=1, source_target_pairs={{0,4},{4,8},{8,12},{12,16},{16,20},{20,24},{24,28},{28,0},{1,5},{5... | collective-permute-start | bytes 76808 | tf_op jit(solution)/shard_map/ppermute | solution.py:145
  40.1 1.0 fusion.13
  41.2 2.7 %collective-permute-start.22 = (bf16[32,400]{1,0:T(8,128)(2,1)S(1)}, bf16[32,400]{1,0:T(8,128)(2,1)S(1)}, u32[]{:S(2)}, u32[]{:S(2)}) collective-permute-start(bf16[32,400]{1,0:T(8,128)(2,1)S(1)} %get-tuple-element.45), channel_id=1, source_target_pairs={{0,12},{4,16},{8,20},{12,24},{16,28},{20,0},{24,4},{28,8},{1,13},{... | collective-permute-start | bytes 76808 | tf_op jit(solution)/shard_map/ppermute | solution.py:145
  43.9 1.1 collective-permute-start.23
  45.0 2.7 %collective-permute-start.24 = (bf16[32,400]{1,0:T(8,128)(2,1)S(1)}, bf16[32,400]{1,0:T(8,128)(2,1)S(1)}, u32[]{:S(2)}, u32[]{:S(2)}) collective-permute-start(bf16[32,400]{1,0:T(8,128)(2,1)S(1)} %get-tuple-element.43), channel_id=1, source_target_pairs={{0,20},{4,24},{8,28},{12,0},{16,4},{20,8},{24,12},{28,16},{1,21},{... | collective-permute-start | bytes 76808 | tf_op jit(solution)/shard_map/ppermute | solution.py:145
  48.2 1.0 collective-permute-start.26
  49.2 1.6 %fusion.75 = (bf16[400,512]{1,0:T(8,128)(2,1)S(1)}, f32[400,512]{1,0:T(8,128)}) fusion(s32[1024]{0:T(1024)S(1)} %fusion.47, bf16[200,1024]{1,0:T(8,128)(2,1)S(1)} %get-tuple-element.32, bf16[200,1024]{1,0:T(8,128)(2,1)S(1)} %get-tuple-element.33), kind=kOutput, calls=%fused_computation.205 | convolution fusion | flops 421797888 | bytes 2052096 | tf_op jit(solution)/shard_map/dot_general | solution.py:13
  50.8 0.8 slice.145
  51.7 1.1 collective-permute-start.15
  53.3 1.3 %collective-permute-start.28 = (bf16[32,400]{1,0:T(8,128)(2,1)S(1)}, bf16[32,400]{1,0:T(8,128)(2,1)S(1)}, u32[]{:S(2)}, u32[]{:S(2)}) collective-permute-start(bf16[32,400]{1,0:T(8,128)(2,1)S(1)} %fusion.37), channel_id=1, source_target_pairs={{0,2},{1,3},{2,0},{3,1},{4,6},{5,7},{6,4},{7,5},{8,10},{9,11},{10,... | collective-permute-start | bytes 76808 | tf_op jit(solution)/shard_map/ppermute | solution.py:50
  55.0 0.7 fusion.73
  56.2 1.0 collective-permute-done.28
  57.3 1.3 %collective-permute-start.12 = (bf16[400,128]{1,0:T(8,128)(2,1)}, bf16[400,128]{1,0:T(8,128)(2,1)}, u32[]{:S(2)}, u32[]{:S(2)}) collective-permute-start(bf16[400,128]{1,0:T(8,128)(2,1)} %get-tuple-element.39), channel_id=1, source_target_pairs={{0,2},{1,3},{2,0},{3,1},{4,6},{5,7},{6,4},{7,5},{8,10},{9,11},{10,... | collective-permute-start | bytes 307208 | tf_op jit(solution)/shard_map/ppermute | solution.py:50
  59.2 1.6 %collective-permute-start.30 = (bf16[32,400]{1,0:T(8,128)(2,1)S(1)}, bf16[32,400]{1,0:T(8,128)(2,1)S(1)}, u32[]{:S(2)}, u32[]{:S(2)}) collective-permute-start(bf16[32,400]{1,0:T(8,128)(2,1)S(1)} %select_reduce_fusion), channel_id=1, source_target_pairs={{0,4},{4,8},{8,12},{12,16},{16,20},{20,24},{24,28},{28,0},{1,5},{5... | collective-permute-start | bytes 76808 | tf_op jit(solution)/shard_map/ppermute | solution.py:145
  60.8 5.1 %collective-permute-done.30 = bf16[32,400]{1,0:T(8,128)(2,1)S(1)} collective-permute-done((bf16[32,400]{1,0:T(8,128)(2,1)S(1)}, bf16[32,400]{1,0:T(8,128)(2,1)S(1)}, u32[]{:S(2)}, u32[]{:S(2)}) %collective-permute-start.30) | collective-permute-done | bytes 25632 | tf_op jit(solution)/shard_map/ppermute | solution.py:145
  65.9 5.7 %collective-permute-done.31 = bf16[32,400]{1,0:T(8,128)(2,1)S(1)} collective-permute-done((bf16[32,400]{1,0:T(8,128)(2,1)S(1)}, bf16[32,400]{1,0:T(8,128)(2,1)S(1)}, u32[]{:S(2)}, u32[]{:S(2)}) %collective-permute-start.31) | collective-permute-done | bytes 25632 | tf_op jit(solution)/shard_map/ppermute | solution.py:145
  71.6 5.7 %collective-permute-done.32 = bf16[32,400]{1,0:T(8,128)(2,1)S(1)} collective-permute-done((bf16[32,400]{1,0:T(8,128)(2,1)S(1)}, bf16[32,400]{1,0:T(8,128)(2,1)S(1)}, u32[]{:S(2)}, u32[]{:S(2)}) %collective-permute-start.32) | collective-permute-done | bytes 25632 | tf_op jit(solution)/shard_map/ppermute | solution.py:145
  77.3 4.8 %collective-permute-done.33 = bf16[32,400]{1,0:T(8,128)(2,1)S(1)} collective-permute-done((bf16[32,400]{1,0:T(8,128)(2,1)S(1)}, bf16[32,400]{1,0:T(8,128)(2,1)S(1)}, u32[]{:S(2)}, u32[]{:S(2)}) %collective-permute-start.33) | collective-permute-done | bytes 25632 | tf_op jit(solution)/shard_map/ppermute | solution.py:145
  82.4 4.6 %collective-permute-done.34 = bf16[32,400]{1,0:T(8,128)(2,1)S(1)} collective-permute-done((bf16[32,400]{1,0:T(8,128)(2,1)S(1)}, bf16[32,400]{1,0:T(8,128)(2,1)S(1)}, u32[]{:S(2)}, u32[]{:S(2)}) %collective-permute-start.34) | collective-permute-done | bytes 25632 | tf_op jit(solution)/shard_map/ppermute | solution.py:145
  87.0 1.8 %collective-permute-start.35 = (bf16[32,400]{1,0:T(8,128)(2,1)S(1)}, bf16[32,400]{1,0:T(8,128)(2,1)S(1)}, u32[]{:S(2)}, u32[]{:S(2)}) collective-permute-start(bf16[32,400]{1,0:T(8,128)(2,1)S(1)} %select_reduce_fusion), channel_id=1, source_target_pairs={{0,24},{4,28},{8,0},{12,4},{16,8},{20,12},{24,16},{28,20},{1,25},{... | collective-permute-start | bytes 76808 | tf_op jit(solution)/shard_map/ppermute | solution.py:145
  88.8 2.1 %collective-permute-done.35 = bf16[32,400]{1,0:T(8,128)(2,1)S(1)} collective-permute-done((bf16[32,400]{1,0:T(8,128)(2,1)S(1)}, bf16[32,400]{1,0:T(8,128)(2,1)S(1)}, u32[]{:S(2)}, u32[]{:S(2)}) %collective-permute-start.35) | collective-permute-done | bytes 25632 | tf_op jit(solution)/shard_map/ppermute | solution.py:145
  90.9 2.9 %collective-permute-start.36 = (bf16[32,400]{1,0:T(8,128)(2,1)S(1)}, bf16[32,400]{1,0:T(8,128)(2,1)S(1)}, u32[]{:S(2)}, u32[]{:S(2)}) collective-permute-start(bf16[32,400]{1,0:T(8,128)(2,1)S(1)} %select_reduce_fusion), channel_id=1, source_target_pairs={{0,28},{4,0},{8,4},{12,8},{16,12},{20,16},{24,20},{28,24},{1,29},{... | collective-permute-start | bytes 76808 | tf_op jit(solution)/shard_map/ppermute | solution.py:145
  93.8 1.6 %collective-permute-done.36 = bf16[32,400]{1,0:T(8,128)(2,1)S(1)} collective-permute-done((bf16[32,400]{1,0:T(8,128)(2,1)S(1)}, bf16[32,400]{1,0:T(8,128)(2,1)S(1)}, u32[]{:S(2)}, u32[]{:S(2)}) %collective-permute-start.36) | collective-permute-done | bytes 25632 | tf_op jit(solution)/shard_map/ppermute | solution.py:145
  96.9 0.9 copy.21
  98.6 1.2 %collective-permute-done.13 = bf16[400,128]{1,0:T(8,128)(2,1)} collective-permute-done((bf16[400,128]{1,0:T(8,128)(2,1)}, bf16[400,128]{1,0:T(8,128)(2,1)}, u32[]{:S(2)}, u32[]{:S(2)}) %collective-permute-start.13) | collective-permute-done | bytes 102432 | tf_op jit(solution)/shard_map/ppermute | solution.py:50
  99.8 1.1 multiply_reduce_fusion.1
  101.6 3.1 %collective-permute-start.16 = (bf16[400,128]{1,0:T(8,128)(2,1)S(1)}, bf16[400,128]{1,0:T(8,128)(2,1)S(1)}, u32[]{:S(2)}, u32[]{:S(2)}) collective-permute-start(bf16[400,128]{1,0:T(8,128)(2,1)S(1)} %get-tuple-element.34), channel_id=1, source_target_pairs={{0,24},{4,28},{8,0},{12,4},{16,8},{20,12},{24,16},{28,20},{1,25},{... | collective-permute-start | bytes 307208 | tf_op jit(solution)/shard_map/ppermute | solution.py:47
  105.4 1.8 %fusion.29 = f32[128,400]{0,1:T(8,128)} fusion(f32[128,400]{0,1:T(8,128)S(1)} %copy-done.1, f32[128]{0:T(128)S(1)} %get-tuple-element.24, bf16[400,128]{1,0:T(8,128)(2,1)} %collective-permute-done.13, bf16[400,128]{1,0:T(8,128)(2,1)} %collective-permute-done.12, bf16[400,128]{1,0:T(8,128)(2,1)S(1)} %collective-permute-done.11, f32[400,512]{1,0:T(8,128)} %get-tuple-element.50), kind=kLoop, calls=%fused_computation.56 | loop fusion | flops 409600 | bytes 922112 | tf_op jit(solution)/shard_map/transpose | solution.py:163
  107.1 0.9 collective-permute-done.16
  108.1 4.5 %collective-permute-done.17 = bf16[400,128]{1,0:T(8,128)(2,1)S(1)} collective-permute-done((bf16[400,128]{1,0:T(8,128)(2,1)S(1)}, bf16[400,128]{1,0:T(8,128)(2,1)S(1)}, u32[]{:S(2)}, u32[]{:S(2)}) %collective-permute-start.17) | collective-permute-done | bytes 102432 | tf_op jit(solution)/shard_map/ppermute | solution.py:47
  113.2 0.8 subtract_bitcast_fusion
  (105 shorter events, 15.6 us)
Async XLA Ops:
  0.6 12.4 %copy-start = (f32[256,400]{0,1:T(8,128)S(1)}, f32[256,400]{0,1:T(8,128)}, u32[]{:S(2)}) copy-start(f32[256,400]{0,1:T(8,128)} %param.14) | copy-start | bytes 1228804
  1.6 17.9 %collective-permute-start = (bf16[400,128]{1,0:T(8,128)(2,1)S(1)}, bf16[400,128]{1,0:T(8,128)(2,1)S(1)}, u32[]{:S(2)}, u32[]{:S(2)}) collective-permute-start(bf16[400,128]{1,0:T(8,128)(2,1)S(1)} %bitcast_convert_fusion.1), channel_id=1, source_target_pairs={{0,1},{1,2},{2,3},{3,0},{4,5},{5,6},{6,7},{7,4},{8,9},{9,10},{10,1... | collective-permute-start | bytes 307208 | tf_op jit(solution)/shard_map/ppermute | solution.py:59
  2.1 19.1 %collective-permute-start.1 = (bf16[400,128]{1,0:T(8,128)(2,1)S(1)}, bf16[400,128]{1,0:T(8,128)(2,1)S(1)}, u32[]{:S(2)}, u32[]{:S(2)}) collective-permute-start(bf16[400,128]{1,0:T(8,128)(2,1)S(1)} %bitcast_convert_fusion.1), channel_id=1, source_target_pairs={{0,9},{1,10},{2,11},{3,8},{4,13},{5,14},{6,15},{7,12},{8,17},{9,18... | collective-permute-start | bytes 307208 | tf_op jit(solution)/shard_map/ppermute | solution.py:59
  6.9 7.5 %collective-permute-start.10 = (bf16[400,128]{1,0:T(8,128)(2,1)S(1)}, bf16[400,128]{1,0:T(8,128)(2,1)S(1)}, u32[]{:S(2)}, u32[]{:S(2)}) collective-permute-start(bf16[400,128]{1,0:T(8,128)(2,1)S(1)} %bitcast_convert_fusion), channel_id=1, source_target_pairs={{0,3},{1,0},{2,1},{3,2},{4,7},{5,4},{6,5},{7,6},{8,11},{9,8},{10,9... | collective-permute-start | bytes 307208 | tf_op jit(solution)/shard_map/ppermute | solution.py:50
  7.0 10.0 %collective-permute-start.8 = (bf16[400,128]{1,0:T(8,128)(2,1)S(1)}, bf16[400,128]{1,0:T(8,128)(2,1)S(1)}, u32[]{:S(2)}, u32[]{:S(2)}) collective-permute-start(bf16[400,128]{1,0:T(8,128)(2,1)S(1)} %bitcast_convert_fusion), channel_id=1, source_target_pairs={{0,1},{1,2},{2,3},{3,0},{4,5},{5,6},{6,7},{7,4},{8,9},{9,10},{10,1... | collective-permute-start | bytes 307208 | tf_op jit(solution)/shard_map/ppermute | solution.py:50
  7.4 11.1 %collective-permute-start.9 = (bf16[400,128]{1,0:T(8,128)(2,1)S(1)}, bf16[400,128]{1,0:T(8,128)(2,1)S(1)}, u32[]{:S(2)}, u32[]{:S(2)}) collective-permute-start(bf16[400,128]{1,0:T(8,128)(2,1)S(1)} %bitcast_convert_fusion), channel_id=1, source_target_pairs={{0,2},{1,3},{2,0},{3,1},{4,6},{5,7},{6,4},{7,5},{8,10},{9,11},{10,... | collective-permute-start | bytes 307208 | tf_op jit(solution)/shard_map/ppermute | solution.py:50
  14.4 8.8 %collective-permute-start.2 = (bf16[400,128]{1,0:T(8,128)(2,1)S(1)}, bf16[400,128]{1,0:T(8,128)(2,1)S(1)}, u32[]{:S(2)}, u32[]{:S(2)}) collective-permute-start(bf16[400,128]{1,0:T(8,128)(2,1)S(1)} %bitcast_convert_fusion.1), channel_id=1, source_target_pairs={{0,17},{1,18},{2,19},{3,16},{4,21},{5,22},{6,23},{7,20},{8,25},{9,... | collective-permute-start | bytes 307208 | tf_op jit(solution)/shard_map/ppermute | solution.py:59
  17.0 7.8 %collective-permute-start.3 = (bf16[400,128]{1,0:T(8,128)(2,1)S(1)}, bf16[400,128]{1,0:T(8,128)(2,1)S(1)}, u32[]{:S(2)}, u32[]{:S(2)}) collective-permute-start(bf16[400,128]{1,0:T(8,128)(2,1)S(1)} %bitcast_convert_fusion.1), channel_id=1, source_target_pairs={{0,25},{1,26},{2,27},{3,24},{4,29},{5,30},{6,31},{7,28},{8,1},{9,2... | collective-permute-start | bytes 307208 | tf_op jit(solution)/shard_map/ppermute | solution.py:59
  19.6 5.8 %collective-permute-start.4 = (bf16[400,128]{1,0:T(8,128)(2,1)S(1)}, bf16[400,128]{1,0:T(8,128)(2,1)S(1)}, u32[]{:S(2)}, u32[]{:S(2)}) collective-permute-start(bf16[400,128]{1,0:T(8,128)(2,1)S(1)} %collective-permute-done), channel_id=1, source_target_pairs={{0,4},{4,0},{8,12},{12,8},{16,20},{20,16},{24,28},{28,24},{1,5},{5... | collective-permute-start | bytes 307208 | tf_op jit(solution)/shard_map/ppermute | solution.py:47
  21.2 6.4 %collective-permute-start.5 = (bf16[400,128]{1,0:T(8,128)(2,1)S(1)}, bf16[400,128]{1,0:T(8,128)(2,1)S(1)}, u32[]{:S(2)}, u32[]{:S(2)}) collective-permute-start(bf16[400,128]{1,0:T(8,128)(2,1)S(1)} %collective-permute-done.1), channel_id=1, source_target_pairs={{0,4},{4,0},{8,12},{12,8},{16,20},{20,16},{24,28},{28,24},{1,5},{5... | collective-permute-start | bytes 307208 | tf_op jit(solution)/shard_map/ppermute | solution.py:47
  23.2 6.6 %collective-permute-start.6 = (bf16[400,128]{1,0:T(8,128)(2,1)S(1)}, bf16[400,128]{1,0:T(8,128)(2,1)S(1)}, u32[]{:S(2)}, u32[]{:S(2)}) collective-permute-start(bf16[400,128]{1,0:T(8,128)(2,1)S(1)} %collective-permute-done.2), channel_id=1, source_target_pairs={{0,4},{4,0},{8,12},{12,8},{16,20},{20,16},{24,28},{28,24},{1,5},{5... | collective-permute-start | bytes 307208 | tf_op jit(solution)/shard_map/ppermute | solution.py:47
  24.8 7.1 %collective-permute-start.7 = (bf16[400,128]{1,0:T(8,128)(2,1)S(1)}, bf16[400,128]{1,0:T(8,128)(2,1)S(1)}, u32[]{:S(2)}, u32[]{:S(2)}) collective-permute-start(bf16[400,128]{1,0:T(8,128)(2,1)S(1)} %collective-permute-done.3), channel_id=1, source_target_pairs={{0,4},{4,0},{8,12},{12,8},{16,20},{20,16},{24,28},{28,24},{1,5},{5... | collective-permute-start | bytes 307208 | tf_op jit(solution)/shard_map/ppermute | solution.py:47
  36.6 0.7 copy-start.2
  37.9 9.9 %collective-permute-start.20 = (bf16[32,400]{1,0:T(8,128)(2,1)S(1)}, bf16[32,400]{1,0:T(8,128)(2,1)S(1)}, u32[]{:S(2)}, u32[]{:S(2)}) collective-permute-start(bf16[32,400]{1,0:T(8,128)(2,1)S(1)} %get-tuple-element.40), channel_id=1, source_target_pairs={{0,4},{4,8},{8,12},{12,16},{16,20},{20,24},{24,28},{28,0},{1,5},{5... | collective-permute-start | bytes 76808 | tf_op jit(solution)/shard_map/ppermute | solution.py:145
  39.4 8.8 %collective-permute-start.21 = (bf16[32,400]{1,0:T(8,128)(2,1)S(1)}, bf16[32,400]{1,0:T(8,128)(2,1)S(1)}, u32[]{:S(2)}, u32[]{:S(2)}) collective-permute-start(bf16[32,400]{1,0:T(8,128)(2,1)S(1)} %get-tuple-element.46), channel_id=1, source_target_pairs={{0,8},{4,12},{8,16},{12,20},{16,24},{20,28},{24,0},{28,4},{1,9},{5... | collective-permute-start | bytes 76808 | tf_op jit(solution)/shard_map/ppermute | solution.py:145
  41.2 10.5 %copy-start.5 = (f32[128]{0:T(128)S(1)}, f32[128]{0:T(128)}, u32[]{:S(2)}) copy-start(f32[128]{0:T(128)} %param.13) | copy-start | bytes 1540
  41.2 10.5 %collective-permute-start.22 = (bf16[32,400]{1,0:T(8,128)(2,1)S(1)}, bf16[32,400]{1,0:T(8,128)(2,1)S(1)}, u32[]{:S(2)}, u32[]{:S(2)}) collective-permute-start(bf16[32,400]{1,0:T(8,128)(2,1)S(1)} %get-tuple-element.45), channel_id=1, source_target_pairs={{0,12},{4,16},{8,20},{12,24},{16,28},{20,0},{24,4},{28,8},{1,13},{... | collective-permute-start | bytes 76808 | tf_op jit(solution)/shard_map/ppermute | solution.py:145
  43.9 7.8 %collective-permute-start.23 = (bf16[32,400]{1,0:T(8,128)(2,1)S(1)}, bf16[32,400]{1,0:T(8,128)(2,1)S(1)}, u32[]{:S(2)}, u32[]{:S(2)}) collective-permute-start(bf16[32,400]{1,0:T(8,128)(2,1)S(1)} %get-tuple-element.44), channel_id=1, source_target_pairs={{0,16},{4,20},{8,24},{12,28},{16,0},{20,4},{24,8},{28,12},{1,17},{... | collective-permute-start | bytes 76808 | tf_op jit(solution)/shard_map/ppermute | solution.py:145
  45.0 7.7 %collective-permute-start.24 = (bf16[32,400]{1,0:T(8,128)(2,1)S(1)}, bf16[32,400]{1,0:T(8,128)(2,1)S(1)}, u32[]{:S(2)}, u32[]{:S(2)}) collective-permute-start(bf16[32,400]{1,0:T(8,128)(2,1)S(1)} %get-tuple-element.43), channel_id=1, source_target_pairs={{0,20},{4,24},{8,28},{12,0},{16,4},{20,8},{24,12},{28,16},{1,21},{... | collective-permute-start | bytes 76808 | tf_op jit(solution)/shard_map/ppermute | solution.py:145
  47.7 5.0 %collective-permute-start.25 = (bf16[32,400]{1,0:T(8,128)(2,1)S(1)}, bf16[32,400]{1,0:T(8,128)(2,1)S(1)}, u32[]{:S(2)}, u32[]{:S(2)}) collective-permute-start(bf16[32,400]{1,0:T(8,128)(2,1)S(1)} %get-tuple-element.42), channel_id=1, source_target_pairs={{0,24},{4,28},{8,0},{12,4},{16,8},{20,12},{24,16},{28,20},{1,25},{... | collective-permute-start | bytes 76808 | tf_op jit(solution)/shard_map/ppermute | solution.py:145
  48.2 4.5 %collective-permute-start.26 = (bf16[32,400]{1,0:T(8,128)(2,1)S(1)}, bf16[32,400]{1,0:T(8,128)(2,1)S(1)}, u32[]{:S(2)}, u32[]{:S(2)}) collective-permute-start(bf16[32,400]{1,0:T(8,128)(2,1)S(1)} %get-tuple-element.41), channel_id=1, source_target_pairs={{0,28},{4,0},{8,4},{12,8},{16,12},{20,16},{24,20},{28,24},{1,29},{... | collective-permute-start | bytes 76808 | tf_op jit(solution)/shard_map/ppermute | solution.py:145
  50.8 45.4 %copy-start.3 = (f32[256]{0:T(256)S(1)}, f32[256]{0:T(256)}, u32[]{:S(2)}) copy-start(f32[256]{0:T(256)} %param.15) | copy-start | bytes 3076
  51.6 61.0 %collective-permute-start.19 = (f32[128]{0:T(128)S(1)}, f32[128]{0:T(128)S(1)}, u32[]{:S(2)}, u32[]{:S(2)}) collective-permute-start(f32[128]{0:T(128)S(1)} %copy-done.5), channel_id=1, source_target_pairs={{0,1},{1,2},{2,3},{3,0},{4,5},{5,6},{6,7},{7,4},{8,9},{9,10},{10,1... | collective-permute-start | bytes 1544 | tf_op jit(solution)/shard_map/ppermute | solution.py:50
  51.7 49.8 %collective-permute-start.15 = (bf16[400,512]{1,0:T(8,128)(2,1)}, bf16[400,512]{1,0:T(8,128)(2,1)S(1)}, u32[]{:S(2)}, u32[]{:S(2)}) collective-permute-start(bf16[400,512]{1,0:T(8,128)(2,1)} %slice.145), channel_id=1, source_target_pairs={{0,4},{4,0},{8,12},{12,8},{16,20},{20,16},{24,28},{28,24},{1,5},{5... | collective-permute-start | bytes 1228808 | tf_op jit(solution)/shard_map/ppermute | solution.py:47
  52.8 3.4 %collective-permute-start.27 = (bf16[32,400]{1,0:T(8,128)(2,1)S(1)}, bf16[32,400]{1,0:T(8,128)(2,1)S(1)}, u32[]{:S(2)}, u32[]{:S(2)}) collective-permute-start(bf16[32,400]{1,0:T(8,128)(2,1)S(1)} %fusion.37), channel_id=1, source_target_pairs={{0,1},{1,2},{2,3},{3,0},{4,5},{5,6},{6,7},{7,4},{8,9},{9,10},{10,1... | collective-permute-start | bytes 76808 | tf_op jit(solution)/shard_map/ppermute | solution.py:50
  53.3 3.9 %collective-permute-start.28 = (bf16[32,400]{1,0:T(8,128)(2,1)S(1)}, bf16[32,400]{1,0:T(8,128)(2,1)S(1)}, u32[]{:S(2)}, u32[]{:S(2)}) collective-permute-start(bf16[32,400]{1,0:T(8,128)(2,1)S(1)} %fusion.37), channel_id=1, source_target_pairs={{0,2},{1,3},{2,0},{3,1},{4,6},{5,7},{6,4},{7,5},{8,10},{9,11},{10,... | collective-permute-start | bytes 76808 | tf_op jit(solution)/shard_map/ppermute | solution.py:50
  54.6 3.9 %collective-permute-start.29 = (bf16[32,400]{1,0:T(8,128)(2,1)S(1)}, bf16[32,400]{1,0:T(8,128)(2,1)S(1)}, u32[]{:S(2)}, u32[]{:S(2)}) collective-permute-start(bf16[32,400]{1,0:T(8,128)(2,1)S(1)} %fusion.37), channel_id=1, source_target_pairs={{0,3},{1,0},{2,1},{3,2},{4,7},{5,4},{6,5},{7,6},{8,11},{9,8},{10,9... | collective-permute-start | bytes 76808 | tf_op jit(solution)/shard_map/ppermute | solution.py:50
  56.2 41.7 %collective-permute-start.11 = (bf16[400,128]{1,0:T(8,128)(2,1)}, bf16[400,128]{1,0:T(8,128)(2,1)S(1)}, u32[]{:S(2)}, u32[]{:S(2)}) collective-permute-start(bf16[400,128]{1,0:T(8,128)(2,1)} %get-tuple-element.37), channel_id=1, source_target_pairs={{0,3},{1,0},{2,1},{3,2},{4,7},{5,4},{6,5},{7,6},{8,11},{9,8},{10,9... | collective-permute-start | bytes 307208 | tf_op jit(solution)/shard_map/ppermute | solution.py:50
  57.3 41.3 %collective-permute-start.12 = (bf16[400,128]{1,0:T(8,128)(2,1)}, bf16[400,128]{1,0:T(8,128)(2,1)}, u32[]{:S(2)}, u32[]{:S(2)}) collective-permute-start(bf16[400,128]{1,0:T(8,128)(2,1)} %get-tuple-element.39), channel_id=1, source_target_pairs={{0,2},{1,3},{2,0},{3,1},{4,6},{5,7},{6,4},{7,5},{8,10},{9,11},{10,... | collective-permute-start | bytes 307208 | tf_op jit(solution)/shard_map/ppermute | solution.py:50
  59.1 41.8 %copy-start.4 = (f32[128]{0:T(128)S(1)}, f32[128]{0:T(128)}, u32[]{:S(2)}) copy-start(f32[128]{0:T(128)} %param.11) | copy-start | bytes 1540
  59.2 6.7 %collective-permute-start.30 = (bf16[32,400]{1,0:T(8,128)(2,1)S(1)}, bf16[32,400]{1,0:T(8,128)(2,1)S(1)}, u32[]{:S(2)}, u32[]{:S(2)}) collective-permute-start(bf16[32,400]{1,0:T(8,128)(2,1)S(1)} %select_reduce_fusion), channel_id=1, source_target_pairs={{0,4},{4,8},{8,12},{12,16},{16,20},{20,24},{24,28},{28,0},{1,5},{5... | collective-permute-start | bytes 76808 | tf_op jit(solution)/shard_map/ppermute | solution.py:145
  65.9 5.7 %collective-permute-start.31 = (bf16[32,400]{1,0:T(8,128)(2,1)S(1)}, bf16[32,400]{1,0:T(8,128)(2,1)S(1)}, u32[]{:S(2)}, u32[]{:S(2)}) collective-permute-start(bf16[32,400]{1,0:T(8,128)(2,1)S(1)} %select_reduce_fusion), channel_id=1, source_target_pairs={{0,8},{4,12},{8,16},{12,20},{16,24},{20,28},{24,0},{28,4},{1,9},{5... | collective-permute-start | bytes 76808 | tf_op jit(solution)/shard_map/ppermute | solution.py:145
  71.6 5.7 %collective-permute-start.32 = (bf16[32,400]{1,0:T(8,128)(2,1)S(1)}, bf16[32,400]{1,0:T(8,128)(2,1)S(1)}, u32[]{:S(2)}, u32[]{:S(2)}) collective-permute-start(bf16[32,400]{1,0:T(8,128)(2,1)S(1)} %select_reduce_fusion), channel_id=1, source_target_pairs={{0,12},{4,16},{8,20},{12,24},{16,28},{20,0},{24,4},{28,8},{1,13},{... | collective-permute-start | bytes 76808 | tf_op jit(solution)/shard_map/ppermute | solution.py:145
  77.3 4.8 %collective-permute-start.33 = (bf16[32,400]{1,0:T(8,128)(2,1)S(1)}, bf16[32,400]{1,0:T(8,128)(2,1)S(1)}, u32[]{:S(2)}, u32[]{:S(2)}) collective-permute-start(bf16[32,400]{1,0:T(8,128)(2,1)S(1)} %select_reduce_fusion), channel_id=1, source_target_pairs={{0,16},{4,20},{8,24},{12,28},{16,0},{20,4},{24,8},{28,12},{1,17},{... | collective-permute-start | bytes 76808 | tf_op jit(solution)/shard_map/ppermute | solution.py:145
  82.2 4.8 %collective-permute-start.34 = (bf16[32,400]{1,0:T(8,128)(2,1)S(1)}, bf16[32,400]{1,0:T(8,128)(2,1)S(1)}, u32[]{:S(2)}, u32[]{:S(2)}) collective-permute-start(bf16[32,400]{1,0:T(8,128)(2,1)S(1)} %select_reduce_fusion), channel_id=1, source_target_pairs={{0,20},{4,24},{8,28},{12,0},{16,4},{20,8},{24,12},{28,16},{1,21},{... | collective-permute-start | bytes 76808 | tf_op jit(solution)/shard_map/ppermute | solution.py:145
  87.0 3.9 %collective-permute-start.35 = (bf16[32,400]{1,0:T(8,128)(2,1)S(1)}, bf16[32,400]{1,0:T(8,128)(2,1)S(1)}, u32[]{:S(2)}, u32[]{:S(2)}) collective-permute-start(bf16[32,400]{1,0:T(8,128)(2,1)S(1)} %select_reduce_fusion), channel_id=1, source_target_pairs={{0,24},{4,28},{8,0},{12,4},{16,8},{20,12},{24,16},{28,20},{1,25},{... | collective-permute-start | bytes 76808 | tf_op jit(solution)/shard_map/ppermute | solution.py:145
  90.9 4.5 %collective-permute-start.36 = (bf16[32,400]{1,0:T(8,128)(2,1)S(1)}, bf16[32,400]{1,0:T(8,128)(2,1)S(1)}, u32[]{:S(2)}, u32[]{:S(2)}) collective-permute-start(bf16[32,400]{1,0:T(8,128)(2,1)S(1)} %select_reduce_fusion), channel_id=1, source_target_pairs={{0,28},{4,0},{8,4},{12,8},{16,12},{20,16},{24,20},{28,24},{1,29},{... | collective-permute-start | bytes 76808 | tf_op jit(solution)/shard_map/ppermute | solution.py:145
  95.4 4.4 %collective-permute-start.13 = (bf16[400,128]{1,0:T(8,128)(2,1)}, bf16[400,128]{1,0:T(8,128)(2,1)}, u32[]{:S(2)}, u32[]{:S(2)}) collective-permute-start(bf16[400,128]{1,0:T(8,128)(2,1)} %get-tuple-element.38), channel_id=1, source_target_pairs={{0,1},{1,2},{2,3},{3,0},{4,5},{5,6},{6,7},{7,4},{8,9},{9,10},{10,1... | collective-permute-start | bytes 307208 | tf_op jit(solution)/shard_map/ppermute | solution.py:50
  96.9 8.4 %copy-start.1 = (f32[128,400]{0,1:T(8,128)S(1)}, f32[128,400]{0,1:T(8,128)}, u32[]{:S(2)}) copy-start(f32[128,400]{0,1:T(8,128)} %param.10) | copy-start | bytes 614404
  97.9 15.3 %collective-permute-start.14 = (f32[400,128]{1,0:T(8,128)}, f32[400,128]{1,0:T(8,128)S(1)}, u32[]{:S(2)}, u32[]{:S(2)}) collective-permute-start(f32[400,128]{1,0:T(8,128)} %bitcast.99), channel_id=1, source_target_pairs={{0,1},{1,2},{2,3},{3,0},{4,5},{5,6},{6,7},{7,4},{8,9},{9,10},{10,1... | collective-permute-start | bytes 614408 | tf_op jit(solution)/shard_map/ppermute | solution.py:50
  101.6 6.4 %collective-permute-start.16 = (bf16[400,128]{1,0:T(8,128)(2,1)S(1)}, bf16[400,128]{1,0:T(8,128)(2,1)S(1)}, u32[]{:S(2)}, u32[]{:S(2)}) collective-permute-start(bf16[400,128]{1,0:T(8,128)(2,1)S(1)} %get-tuple-element.34), channel_id=1, source_target_pairs={{0,24},{4,28},{8,0},{12,4},{16,8},{20,12},{24,16},{28,20},{1,25},{... | collective-permute-start | bytes 307208 | tf_op jit(solution)/shard_map/ppermute | solution.py:47
  104.7 7.9 %collective-permute-start.17 = (bf16[400,128]{1,0:T(8,128)(2,1)S(1)}, bf16[400,128]{1,0:T(8,128)(2,1)S(1)}, u32[]{:S(2)}, u32[]{:S(2)}) collective-permute-start(bf16[400,128]{1,0:T(8,128)(2,1)S(1)} %get-tuple-element.36), channel_id=1, source_target_pairs={{0,16},{4,20},{8,24},{12,28},{16,0},{20,4},{24,8},{28,12},{1,17},{... | collective-permute-start | bytes 307208 | tf_op jit(solution)/shard_map/ppermute | solution.py:47
  104.7 7.9 %collective-permute-start.18 = (bf16[400,128]{1,0:T(8,128)(2,1)S(1)}, bf16[400,128]{1,0:T(8,128)(2,1)S(1)}, u32[]{:S(2)}, u32[]{:S(2)}) collective-permute-start(bf16[400,128]{1,0:T(8,128)(2,1)S(1)} %get-tuple-element.35), channel_id=1, source_target_pairs={{0,8},{4,12},{8,16},{12,20},{16,24},{20,28},{24,0},{28,4},{1,9},{5... | collective-permute-start | bytes 307208 | tf_op jit(solution)/shard_map/ppermute | solution.py:47

commit v2 on v1

v2 whole, which is shorter than its diff:
```python
import jax
import jax.numpy as jnp
from jax import lax
from jax.sharding import PartitionSpec as P

LEARN_RATE = 0.1
NEG_WEIGHT = 0.03125
BF = jnp.bfloat16
F32 = jnp.float32


def dot(a, b, a_dim, b_dim):
    return lax.dot_general(a, b, (((a_dim,), (b_dim,)), ((), ())), preferred_element_type=F32)


def complex_product(a, b):
    half = a.shape[0] // 2
    a_re, a_im, b_re, b_im = a[:half], a[half:], b[:half], b[half:]
    return jnp.concatenate([a_re * b_re - a_im * b_im, a_re * b_im + a_im * b_re], axis=0)


def complex_back(grad, other):
    half = grad.shape[0] // 2
    g_re, g_im, o_re, o_im = grad[:half], grad[half:], other[:half], other[half:]
    return jnp.concatenate([g_re * o_re + g_im * o_im, g_im * o_re - g_re * o_im], axis=0)


def adagrad(table, state, grad):
    state_new = state + jnp.mean(grad * grad, axis=0)
    return table - LEARN_RATE * grad * lax.rsqrt(state_new)[None, :], state_new


def one_hot(ids, count):
    return (jnp.arange(count, dtype=jnp.int32)[:, None] == ids[None, :]).astype(BF)


def build(mesh):
    n_left, n_right = mesh.shape["left"], mesh.shape["right"]
    for count in (n_left, n_right):
        assert count & (count - 1) == 0 and count > 1
    outer = n_left // 2
    far_right = n_right // 2

    def swap_left(value, by):
        return lax.ppermute(value, "left", [(i, i ^ by) for i in range(n_left)])

    def swap_right(value, by):
        return lax.ppermute(value, "right", [(i, i ^ by) for i in range(n_right)])

    def next_column(value, by):
        perm = []
        for i in range(n_left):
            for r in range(n_right):
                perm.append((i * n_right + r, (i ^ by) * n_right + (r + 1) % n_right))
        return lax.ppermute(value, ("left", "right"), perm)

    def tree_sum(values):
        while len(values) > 1:
            values = [values[i] + values[i + 1] for i in range(0, len(values), 2)]
        return values[0]

    def per_device(
        left_table, left_state, right_table, right_state, relation_table, relation_state,
        source_ids, target_ids, relation_ids, negative_ids,
    ):
        rows = left_table.shape[0]
        width = left_table.shape[1]
        left_t, right_t, relation_t = left_table.T, right_table.T, relation_table.T
        nrel = relation_t.shape[1]
        here_l, here_r = lax.axis_index("left"), lax.axis_index("right")
        source = source_ids.reshape(-1)
        target = target_ids.reshape(-1)
        relation = relation_ids.reshape(-1)
        negative = negative_ids.reshape(negative_ids.shape[2], negative_ids.shape[3])
        groups = negative.shape[0]

        right_bf = right_t.astype(BF)
        near = {k: next_column(right_bf, 2 * k) for k in sorted(range(1, outer), key=lambda k: -k)}
        other = {0: next_column(right_bf, 1)}
        left_bf = left_t.astype(BF)
        half_left = [left_bf] + [swap_right(left_bf, 2 * k) for k in range(1, far_right)]
        half_left = jnp.concatenate(half_left, axis=1)
        moved = next_column(jnp.concatenate([right_t, right_state[None, :]], axis=0), 0)
        moved_t, moved_state = moved[:width], moved[width]
        near[0] = moved_t.astype(BF)
        left_part = jnp.concatenate([half_left, swap_right(half_left, 1)], axis=1)
        for k in range(1, outer):
            other[k] = swap_left(near[k], 1)
        right_blocks = [near[k] for k in range(outer)] + [other[k] for k in range(outer)]

        def local(ids, here, half):
            block = (ids // rows) ^ here
            return (block % 2 * half + block // 2) * rows + ids % rows

        source = local(source, here_r, far_right)
        target = local(target, here_l, outer)
        negative = local(negative, here_l, outer)

        n_rows = n_left * rows
        counts = [
            jnp.sum((jnp.arange(n_rows, dtype=jnp.int32)[:, None] == negative[c][None, :]).astype(F32), axis=1)
            for c in range(groups)
        ]
        source_hot = one_hot(source, n_right * rows)
        relation_hot = one_hot(relation, nrel)
        source_emb = dot(left_part, source_hot, 1, 0)
        relation_emb = dot(relation_t.astype(BF), relation_hot, 1, 0)
        query = complex_product(source_emb, relation_emb)
        query_bf = query.astype(BF)

        right_part = jnp.concatenate(right_blocks, axis=1)
        scores = dot(right_part, query_bf, 0, 0)
        hit = jnp.arange(n_rows, dtype=jnp.int32)[:, None] == target[None, :]
        edges = scores.shape[1]
        weight = jnp.concatenate(
            [jnp.broadcast_to((NEG_WEIGHT * c)[:, None], (n_rows, edges // groups)) for c in counts], axis=1
        )
        grad_m = (weight * jax.nn.sigmoid(scores) - jnp.where(hit, jax.nn.sigmoid(-scores), 0.0)).astype(BF)

        half = outer * rows
        cut = half // 2
        far = dot(query_bf, grad_m[half:], 1, 1).astype(BF)
        got_hi = swap_left(far[:, cut:], 1)
        got_lo = swap_left(far[:, :cut], 1)
        mine = dot(query_bf, grad_m[:half], 1, 1)
        hi = mine[:, cut:] + got_hi.astype(F32)
        lo = mine[:, :cut] + got_lo.astype(F32)
        hi_bf, lo_bf = hi.astype(BF), lo.astype(BF)
        right_sum = lo[:, :rows]
        for k in range(outer - 1, 0, -1):
            at = k * rows
            piece = lo_bf[:, at:at + rows] if at < cut else hi_bf[:, at - cut:at - cut + rows]
            right_sum = right_sum + swap_left(piece, 2 * k).astype(F32)

        query_grad = dot(right_part, grad_m, 1, 0)
        relation_grad = complex_back(query_grad, source_emb).astype(BF)
        relation_term = dot(relation_grad, relation_hot, 1, 1)
        source_grad = complex_back(query_grad, relation_emb).astype(BF)
        left_grad = dot(source_grad, source_hot, 1, 1)

        order = [k // 2 + k % 2 * far_right for k in range(n_right)]
        lanes = nrel // 2
        tall = jnp.concatenate([relation_term[:, :lanes], relation_term[:, lanes:]], axis=0)
        pieces = tall.astype(BF).reshape(n_right, -1, lanes)
        piece_rows = pieces.shape[1]
        left_bf_grad = left_grad.astype(BF)
        left_sum = left_grad[:, :rows]
        got = [lax.dynamic_index_in_dim(pieces, here_r, 0, keepdims=False).astype(F32)]
        for k in range(1, n_right):
            block = left_bf_grad[:, order[k] * rows:(order[k] + 1) * rows]
            piece = lax.dynamic_index_in_dim(pieces, here_r ^ k, 0, keepdims=False)
            arrived = swap_right(jnp.concatenate([block, piece], axis=0), k)
            left_sum = left_sum + arrived[:width].astype(F32)
            got.append(arrived[width:].astype(F32))
        relation_piece = tree_sum(got).astype(BF)
        relation_piece = (relation_piece.astype(F32) + swap_left(relation_piece, 1).astype(F32)).astype(BF)
        got = [relation_piece.astype(F32)]
        for k in range(1, outer):
            got.append(swap_left(relation_piece, 2 * k).astype(F32))
        relation_piece = tree_sum(got).astype(BF)
        got = [relation_piece] + [swap_right(relation_piece, k) for k in range(1, n_right)]
        where = here_r ^ jnp.arange(n_right)
        tall = jnp.take(jnp.stack(got), where, axis=0).reshape(-1, lanes).astype(F32)
        relation_total = jnp.concatenate([tall[:width], tall[width:]], axis=1)

        left_new, left_state_new = adagrad(left_t, left_state, left_sum)
        right_new, right_state_new = adagrad(moved_t, moved_state, right_sum)
        relation_new, relation_state_new = adagrad(relation_t, relation_state, relation_total)
        return (left_new.T, left_state_new, right_new.T, right_state_new, relation_new.T, relation_state_new)

    return per_device


def solution(mesh):
    rows = P(("left", "right"), None)
    vector = P(("left", "right"))
    ids = P("left", "right", None)
    return jax.shard_map(
        build(mesh),
        mesh=mesh,
        in_specs=(rows, vector, rows, vector, P(), P(), ids, ids, ids, P("left", "right", None, None)),
        out_specs=(rows, vector, rows, vector, P(), P()),
        check_vma=False,
    )
```

time: 114 us -> 76.9 us (0.67)
  waiting for transfers between devices: 45.5 us -> 23.6 us
  starting transfers between devices: 40.2 us -> 29.8 us
  local copies, waits for them, and re-layouts: 5.72 us -> 1.58 us
    ppermute x37 -> x25, waiting for transfers between devices: 45.5 us -> 23.6 us  [the longest x12 18.6 us: swap_left(): return lax.ppermute(value, 'left', [(i, i ^ by) for i in range(n_left)])]
    ppermute x37 -> x25, starting transfers between devices: 40.2 us -> 29.8 us  [the longest x12 15.2 us: swap_left(): return lax.ppermute(value, 'left', [(i, i ^ by) for i in range(n_left)])]
    unnamed x28 -> x17, local copies, waits for them, and re-layouts: 2.35 us -> 0.21 us
    slice x3 -> x6, local copies, waits for them, and re-layouts: 1.62 us -> 0.16 us  [the longest x1 0.05 us: per_device(): block = left_bf_grad[:, order[k] * rows:(order[k] + 1) * rows]]
    reduce_sum x3, other arithmetic: 1.4 us -> 0.22 us  [adagrad(): state_new = state + jnp.mean(grad * grad, axis=0)]
    add x3 -> x4, other arithmetic: 2.22 us -> 2.71 us  [the longest x3 2.19 us: local(): return (block % 2 * half + block // 2) * rows + ids % rows]
    dot_general x7 -> x8, matrix products: 9.11 us -> 8.72 us  [dot(): lax.dot_general(a, b, (((a_dim,), (b_dim,)), ((), ())), preferred_element...]
    transpose x2 -> x3, other arithmetic: 2.52 us -> 2.3 us  [per_device(): return (left_new.T, left_state_new, right_new.T, right_state_new, relatio...]
  transfers between devices with their start and end apart: 37 -> 25, of which waited for: 16 -> 13; matrix products, arithmetic and copies ran while one was open for 17% -> 15% of each run, Pallas kernels for 0% -> 0%
where the time goes in v2:
time: 76.9 us; the launch traced here: 76.6 us
  starting transfers between devices  29.8 us (39%)
  waiting for transfers between devices  23.6 us (31%)
  other arithmetic  11.8 us (15%)
  matrix products  8.72 us (11%)
  local copies, waits for them, and re-layouts  1.58 us (2%)
  between operations  1.07 us (1%)
    ppermute x12, waiting for transfers between devices, swap_left(): return lax.ppermute(value, 'left', [(i, i ^ by) for i in range(n_left)])  18.6 us
    ppermute x12, starting transfers between devices, swap_left(): return lax.ppermute(value, 'left', [(i, i ^ by) for i in range(n_left)])  15.2 us
    dot_general x8, matrix products, dot(): lax.dot_general(a, b, (((a_dim,), (b_dim,)), ((), ())), preferred_element...  8.72 us
    ppermute x5, starting transfers between devices, next_column(): return lax.ppermute(value, ('left', 'right'), perm)  7.89 us
    ppermute x8, starting transfers between devices, swap_right(): return lax.ppermute(value, 'right', [(i, i ^ by) for i in range(n_right)])  6.76 us
    ppermute x8, waiting for transfers between devices, swap_right(): return lax.ppermute(value, 'right', [(i, i ^ by) for i in range(n_right)])  4.83 us
    transpose x3, other arithmetic, per_device(): return (left_new.T, left_state_new, right_new.T, right_state_new, relatio...  2.3 us
    add x3, other arithmetic, local(): return (block % 2 * half + block // 2) * rows + ids % rows  2.19 us
  transfers between devices with their start and end apart: 25, of which 13 were waited for; matrix products, arithmetic and copies ran while one was open for 15% of the time, Pallas kernels for 0%

profile of v2, /device:TPU:0, one launch (start us, length us, event | category | flops | bytes accessed | tf_op | source)
XLA Modules:
  0.0 76.6 jit_solution(342113498544303533)
XLA Ops:
  0.6 0.9 %bitcast_convert_fusion.3 = bf16[400,128]{1,0:T(8,128)(2,1)S(1)} fusion(f32[128,400]{0,1:T(8,128)} %param.12), kind=kLoop, calls=%fused_computation.171 | loop fusion | flops 51200 | bytes 307200 | tf_op jit(solution)/shard_map/convert_element_type | solution.py:77
  1.6 2.5 %collective-permute-start.1 = (bf16[400,128]{1,0:T(8,128)(2,1)S(1)}, bf16[400,128]{1,0:T(8,128)(2,1)S(1)}, u32[]{:S(2)}, u32[]{:S(2)}) collective-permute-start(bf16[400,128]{1,0:T(8,128)(2,1)S(1)} %bitcast_convert_fusion.3), channel_id=1, source_target_pairs={{0,9},{1,10},{2,11},{3,8},{4,13},{5,14},{6,15},{7,12},{8,1},{9,2},... | collective-permute-start | bytes 307208 | tf_op jit(solution)/shard_map/ppermute | solution.py:55
  4.1 3.8 %collective-permute-start.2 = (bf16[400,128]{1,0:T(8,128)(2,1)S(1)}, bf16[400,128]{1,0:T(8,128)(2,1)S(1)}, u32[]{:S(2)}, u32[]{:S(2)}) collective-permute-start(bf16[400,128]{1,0:T(8,128)(2,1)S(1)} %bitcast_convert_fusion.3), channel_id=1, source_target_pairs={{0,17},{1,18},{2,19},{3,16},{4,21},{5,22},{6,23},{7,20},{8,25},{9,... | collective-permute-start | bytes 307208 | tf_op jit(solution)/shard_map/ppermute | solution.py:55
  7.9 1.0 %pad_maximum_fusion.5 = f32[401,128]{1,0:T(8,128)S(1)} fusion(f32[1,128]{1,0:T(1,128)} %bitcast.98, f32[400,128]{1,0:T(8,128)} %bitcast.85), kind=kLoop, calls=%fused_computation.49 | loop fusion | flops 51328 | bytes 410624 | tf_op jit(solution)/shard_map/concatenate | solution.py:83
  8.9 0.9 %bitcast_convert_fusion.2 = bf16[400,128]{1,0:T(8,128)(2,1)S(1)} fusion(f32[128,400]{0,1:T(8,128)} %param.10), kind=kLoop, calls=%fused_computation.63 | loop fusion | flops 51200 | bytes 307200 | tf_op jit(solution)/shard_map/convert_element_type | solution.py:80
  9.9 1.8 %collective-permute-start.8 = (bf16[400,128]{1,0:T(8,128)(2,1)S(1)}, bf16[400,128]{1,0:T(8,128)(2,1)S(1)}, u32[]{:S(2)}, u32[]{:S(2)}) collective-permute-start(bf16[400,128]{1,0:T(8,128)(2,1)S(1)} %bitcast_convert_fusion.2), channel_id=1, source_target_pairs={{0,2},{1,3},{2,0},{3,1},{4,6},{5,7},{6,4},{7,5},{8,10},{9,11},{10,... | collective-permute-start | bytes 307208 | tf_op jit(solution)/shard_map/ppermute | solution.py:48
  11.7 0.7 fusion.40
  12.4 0.8 %fusion.35 = s32[2,1024]{1,0:T(2,128)S(1)} fusion(s32[1,1,2,1024]{3,2,1,0:T(2,128)} %param.19, s32[]{:T(128)S(6)} %axis_index.23), kind=kLoop, calls=%fused_computation.100 | loop fusion | flops 88064 | bytes 16388 | tf_op jit(solution)/shard_map/add | solution.py:93
  14.2 0.7 fusion.45
  15.1 1.4 %convolution_bitcast_fusion = f32[400,1024]{1,0:T(8,128)S(1)} fusion(s32[1024]{0:T(1024)} %bitcast.92, f32[256,400]{0,1:T(8,128)} %param.14), kind=kOutput, calls=%fused_computation.12 | convolution fusion | flops 209977344 | bytes 2052096 | tf_op jit(solution)/shard_map/dot_general | solution.py:13
  16.9 1.5 %collective-permute-start.4 = (bf16[400,128]{1,0:T(8,128)(2,1)S(1)}, bf16[400,128]{1,0:T(8,128)(2,1)S(1)}, u32[]{:S(2)}, u32[]{:S(2)}) collective-permute-start(bf16[400,128]{1,0:T(8,128)(2,1)S(1)} %bitcast_convert_fusion.3), channel_id=1, source_target_pairs={{0,5},{1,6},{2,7},{3,4},{4,1},{5,2},{6,3},{7,0},{8,13},{9,14},{10,... | collective-permute-start | bytes 307208 | tf_op jit(solution)/shard_map/ppermute | solution.py:55
  18.4 0.9 %collective-permute-start.9 = (bf16[400,256]{1,0:T(8,128)(2,1)S(1)}, bf16[400,256]{1,0:T(8,128)(2,1)S(1)}, u32[]{:S(2)}, u32[]{:S(2)}) collective-permute-start(bf16[400,256]{1,0:T(8,128)(2,1)S(1)} %pad_maximum_fusion.6), channel_id=1, source_target_pairs={{0,1},{1,0},{2,3},{3,2},{4,5},{5,4},{6,7},{7,6},{8,9},{9,8},{10,11... | collective-permute-start | bytes 614408 | tf_op jit(solution)/shard_map/ppermute | solution.py:48
  19.9 1.5 %collective-permute-start.6 = (bf16[400,128]{1,0:T(8,128)(2,1)S(1)}, bf16[400,128]{1,0:T(8,128)(2,1)S(1)}, u32[]{:S(2)}, u32[]{:S(2)}) collective-permute-start(bf16[400,128]{1,0:T(8,128)(2,1)S(1)} %collective-permute-done.2), channel_id=1, source_target_pairs={{0,4},{4,0},{8,12},{12,8},{16,20},{20,16},{24,28},{28,24},{1,5},{5... | collective-permute-start | bytes 307208 | tf_op jit(solution)/shard_map/ppermute | solution.py:45
  22.2 3.1 %collective-permute-done.5 = bf16[400,128]{1,0:T(8,128)(2,1)S(1)} collective-permute-done((bf16[400,128]{1,0:T(8,128)(2,1)S(1)}, bf16[400,128]{1,0:T(8,128)(2,1)S(1)}, u32[]{:S(2)}, u32[]{:S(2)}) %collective-permute-start.5) | collective-permute-done | bytes 102432 | tf_op jit(solution)/shard_map/ppermute | solution.py:45
  25.4 2.2 %collective-permute-done.6 = bf16[400,128]{1,0:T(8,128)(2,1)S(1)} collective-permute-done((bf16[400,128]{1,0:T(8,128)(2,1)S(1)}, bf16[400,128]{1,0:T(8,128)(2,1)S(1)}, u32[]{:S(2)}, u32[]{:S(2)}) %collective-permute-start.6) | collective-permute-done | bytes 102432 | tf_op jit(solution)/shard_map/ppermute | solution.py:45
  27.5 1.6 %collective-permute-done.7 = bf16[400,128]{1,0:T(8,128)(2,1)S(1)} collective-permute-done((bf16[400,128]{1,0:T(8,128)(2,1)S(1)}, bf16[400,128]{1,0:T(8,128)(2,1)S(1)}, u32[]{:S(2)}, u32[]{:S(2)}) %collective-permute-start.7) | collective-permute-done | bytes 102432 | tf_op jit(solution)/shard_map/ppermute | solution.py:45
  29.2 0.6 fusion.3
  30.7 3.3 %fusion.1 = bf16[1024,1024]{1,0:T(8,128)(2,1)S(1)} fusion(f32[1024,512]{1,0:T(8,128)S(1)} %broadcast_in_dim.26, f32[1024,512]{1,0:T(8,128)S(1)} %broadcast_in_dim.25, s32[1024]{0:T(1024)S(1)} %fusion.45, bf16[400,1024]{1,0:T(8,128)(2,1)S(1)} %constant_dynamic-update-slice_fusion, bf16[200,1024]{1,0:T(8,128)(2,1)S(1)} %get-tuple-element.15, ...), kind=kOutput, calls=%fused_computation.3 | convolution fusion | flops 852033536 | bytes 7933952 | tf_op jit(solution)/shard_map/dot_general | solution.py:13
  34.0 1.0 %fusion.78 = f32[400,1024]{1,0:T(8,128)S(1)} fusion(bf16[400,1024]{1,0:T(8,128)(2,1)S(1)} %constant_dynamic-update-slice_fusion, bf16[1024,1024]{1,0:T(8,128)(2,1)S(1)} %fusion.1), kind=kOutput, calls=%fused_computation.180 | convolution fusion | flops 838860800 | bytes 4554752 | tf_op jit(solution)/shard_map/dot_general | solution.py:13
  35.0 0.6 convolution_convert_fusion
  35.6 0.7 add_convert_fusion.1
  36.3 0.7 fusion.75
  37.7 1.1 %collective-permute-start.11 = (bf16[600,128]{1,0:T(8,128)(2,1)S(1)}, bf16[600,128]{1,0:T(8,128)(2,1)S(1)}, u32[]{:S(2)}, u32[]{:S(2)}) collective-permute-start(bf16[600,128]{1,0:T(8,128)(2,1)S(1)} %pad_maximum_fusion.10), channel_id=1, source_target_pairs={{0,2},{1,3},{2,0},{3,1},{4,6},{5,7},{6,4},{7,5},{8,10},{9,11},{10,... | collective-permute-start | bytes 460808 | tf_op jit(solution)/shard_map/ppermute | solution.py:48
  38.9 0.8 %collective-permute-start.12 = (bf16[600,128]{1,0:T(8,128)(2,1)S(1)}, bf16[600,128]{1,0:T(8,128)(2,1)S(1)}, u32[]{:S(2)}, u32[]{:S(2)}) collective-permute-start(bf16[600,128]{1,0:T(8,128)(2,1)S(1)} %pad_maximum_fusion.11), channel_id=1, source_target_pairs={{0,3},{1,2},{2,1},{3,0},{4,7},{5,6},{6,5},{7,4},{8,11},{9,10},{10,... | collective-permute-start | bytes 460808 | tf_op jit(solution)/shard_map/ppermute | solution.py:48
  39.8 1.6 %collective-permute-start.13 = (bf16[400,256]{1,0:T(8,128)(2,1)S(1)}, bf16[400,256]{1,0:T(8,128)(2,1)S(1)}, u32[]{:S(2)}, u32[]{:S(2)}) collective-permute-start(bf16[400,256]{1,0:T(8,128)(2,1)S(1)} %get-tuple-element.23), channel_id=1, source_target_pairs={{0,4},{4,0},{8,12},{12,8},{16,20},{20,16},{24,28},{28,24},{1,5},{5... | collective-permute-start | bytes 614408 | tf_op jit(solution)/shard_map/ppermute | solution.py:45
  41.8 0.6 fusion.5
  42.5 2.1 %collective-permute-done.11 = bf16[600,128]{1,0:T(8,128)(2,1)S(1)} collective-permute-done((bf16[600,128]{1,0:T(8,128)(2,1)S(1)}, bf16[600,128]{1,0:T(8,128)(2,1)S(1)}, u32[]{:S(2)}, u32[]{:S(2)}) %collective-permute-start.11) | collective-permute-done | bytes 153632 | tf_op jit(solution)/shard_map/ppermute | solution.py:48
  44.6 2.5 %collective-permute-done.12 = bf16[600,128]{1,0:T(8,128)(2,1)S(1)} collective-permute-done((bf16[600,128]{1,0:T(8,128)(2,1)S(1)}, bf16[600,128]{1,0:T(8,128)(2,1)S(1)}, u32[]{:S(2)}, u32[]{:S(2)}) %collective-permute-start.12) | collective-permute-done | bytes 153632 | tf_op jit(solution)/shard_map/ppermute | solution.py:48
  47.1 1.6 %collective-permute-start.18 = (bf16[200,128]{1,0:T(8,128)(2,1)S(1)}, bf16[200,128]{1,0:T(8,128)(2,1)S(1)}, u32[]{:S(2)}, u32[]{:S(2)}) collective-permute-start(bf16[200,128]{1,0:T(8,128)(2,1)S(1)} %fusion.32), channel_id=1, source_target_pairs={{0,4},{4,0},{8,12},{12,8},{16,20},{20,16},{24,28},{28,24},{1,5},{5... | collective-permute-start | bytes 153608 | tf_op jit(solution)/shard_map/ppermute | solution.py:45
  48.8 0.5 rsqrt_multiply_fusion.1
  49.3 0.7 fusion.29
  50.0 2.6 %collective-permute-done.18 = bf16[200,128]{1,0:T(8,128)(2,1)S(1)} collective-permute-done((bf16[200,128]{1,0:T(8,128)(2,1)S(1)}, bf16[200,128]{1,0:T(8,128)(2,1)S(1)}, u32[]{:S(2)}, u32[]{:S(2)}) %collective-permute-start.18) | collective-permute-done | bytes 51232 | tf_op jit(solution)/shard_map/ppermute | solution.py:45
  52.6 1.0 %collective-permute-start.19 = (bf16[200,128]{1,0:T(8,128)(2,1)S(1)}, bf16[200,128]{1,0:T(8,128)(2,1)S(1)}, u32[]{:S(2)}, u32[]{:S(2)}) collective-permute-start(bf16[200,128]{1,0:T(8,128)(2,1)S(1)} %add_convert_fusion.4), channel_id=1, source_target_pairs={{0,8},{4,12},{8,0},{12,4},{16,24},{20,28},{24,16},{28,20},{1,9},{5... | collective-permute-start | bytes 153608 | tf_op jit(solution)/shard_map/ppermute | solution.py:45
  53.6 2.6 %collective-permute-start.20 = (bf16[200,128]{1,0:T(8,128)(2,1)S(1)}, bf16[200,128]{1,0:T(8,128)(2,1)S(1)}, u32[]{:S(2)}, u32[]{:S(2)}) collective-permute-start(bf16[200,128]{1,0:T(8,128)(2,1)S(1)} %add_convert_fusion.4), channel_id=1, source_target_pairs={{0,16},{4,20},{8,24},{12,28},{16,0},{20,4},{24,8},{28,12},{1,17},{... | collective-permute-start | bytes 153608 | tf_op jit(solution)/shard_map/ppermute | solution.py:45
  56.2 0.8 %collective-permute-start.21 = (bf16[200,128]{1,0:T(8,128)(2,1)S(1)}, bf16[200,128]{1,0:T(8,128)(2,1)S(1)}, u32[]{:S(2)}, u32[]{:S(2)}) collective-permute-start(bf16[200,128]{1,0:T(8,128)(2,1)S(1)} %add_convert_fusion.4), channel_id=1, source_target_pairs={{0,24},{4,28},{8,16},{12,20},{16,8},{20,12},{24,0},{28,4},{1,25},{... | collective-permute-start | bytes 153608 | tf_op jit(solution)/shard_map/ppermute | solution.py:45
  57.3 1.3 %collective-permute-done.20 = bf16[200,128]{1,0:T(8,128)(2,1)S(1)} collective-permute-done((bf16[200,128]{1,0:T(8,128)(2,1)S(1)}, bf16[200,128]{1,0:T(8,128)(2,1)S(1)}, u32[]{:S(2)}, u32[]{:S(2)}) %collective-permute-start.20) | collective-permute-done | bytes 51232 | tf_op jit(solution)/shard_map/ppermute | solution.py:45
  58.6 3.5 %collective-permute-done.21 = bf16[200,128]{1,0:T(8,128)(2,1)S(1)} collective-permute-done((bf16[200,128]{1,0:T(8,128)(2,1)S(1)}, bf16[200,128]{1,0:T(8,128)(2,1)S(1)}, u32[]{:S(2)}, u32[]{:S(2)}) %collective-permute-start.21) | collective-permute-done | bytes 51232 | tf_op jit(solution)/shard_map/ppermute | solution.py:45
  62.2 1.2 %collective-permute-start.23 = (bf16[200,128]{1,0:T(8,128)(2,1)S(1)}, bf16[200,128]{1,0:T(8,128)(2,1)S(1)}, u32[]{:S(2)}, u32[]{:S(2)}) collective-permute-start(bf16[200,128]{1,0:T(8,128)(2,1)S(1)} %add_convert_fusion.3), channel_id=1, source_target_pairs={{0,2},{1,3},{2,0},{3,1},{4,6},{5,7},{6,4},{7,5},{8,10},{9,11},{10,... | collective-permute-start | bytes 153608 | tf_op jit(solution)/shard_map/ppermute | solution.py:48
  63.4 0.7 collective-permute-start.24
  64.1 1.0 %collective-permute-start.15 = (bf16[400,128]{1,0:T(8,128)(2,1)S(1)}, bf16[400,128]{1,0:T(8,128)(2,1)S(1)}, u32[]{:S(2)}, u32[]{:S(2)}) collective-permute-start(bf16[400,128]{1,0:T(8,128)(2,1)S(1)} %get-tuple-element.27), channel_id=1, source_target_pairs={{0,24},{4,28},{8,16},{12,20},{16,8},{20,12},{24,0},{28,4},{1,25},{... | collective-permute-start | bytes 307208 | tf_op jit(solution)/shard_map/ppermute | solution.py:45
  65.1 3.5 %collective-permute-start.17 = (bf16[400,128]{1,0:T(8,128)(2,1)S(1)}, bf16[400,128]{1,0:T(8,128)(2,1)S(1)}, u32[]{:S(2)}, u32[]{:S(2)}) collective-permute-start(bf16[400,128]{1,0:T(8,128)(2,1)S(1)} %slice.255), channel_id=1, source_target_pairs={{0,8},{4,12},{8,0},{12,4},{16,24},{20,28},{24,16},{28,20},{1,9},{5... | collective-permute-start | bytes 307208 | tf_op jit(solution)/shard_map/ppermute | solution.py:45
  68.7 0.6 gather_fusion
  69.6 0.6 rsqrt_multiply_fusion
  70.2 0.8 %fusion.23 = f32[256,400]{0,1:T(8,128)} fusion(f32[256,400]{0,1:T(8,128)S(1)} %copy-done, f32[400,128]{1,0:T(8,128)S(1)} %get-tuple-element.21, f32[400,128]{1,0:T(8,128)S(1)} %get-tuple-element.20, f32[256]{0:T(256)S(1)} %get-tuple-element.6), kind=kLoop, calls=%fused_computation.47 | loop fusion | flops 307200 | bytes 1229824 | tf_op jit(solution)/shard_map/transpose | solution.py:169
  71.0 0.8 %collective-permute-done.15 = bf16[400,128]{1,0:T(8,128)(2,1)S(1)} collective-permute-done((bf16[400,128]{1,0:T(8,128)(2,1)S(1)}, bf16[400,128]{1,0:T(8,128)(2,1)S(1)}, u32[]{:S(2)}, u32[]{:S(2)}) %collective-permute-start.15) | collective-permute-done | bytes 102432 | tf_op jit(solution)/shard_map/ppermute | solution.py:45
  71.8 3.4 %collective-permute-done.16 = bf16[400,128]{1,0:T(8,128)(2,1)S(1)} collective-permute-done((bf16[400,128]{1,0:T(8,128)(2,1)S(1)}, bf16[400,128]{1,0:T(8,128)(2,1)S(1)}, u32[]{:S(2)}, u32[]{:S(2)}) %collective-permute-start.16) | collective-permute-done | bytes 102432 | tf_op jit(solution)/shard_map/ppermute | solution.py:45
  75.3 0.5 bitcast_add_fusion
  75.8 0.8 subtract_bitcast_fusion
  (77 shorter events, 5.9 us)
Async XLA Ops:
  1.6 16.8 %collective-permute-start.1 = (bf16[400,128]{1,0:T(8,128)(2,1)S(1)}, bf16[400,128]{1,0:T(8,128)(2,1)S(1)}, u32[]{:S(2)}, u32[]{:S(2)}) collective-permute-start(bf16[400,128]{1,0:T(8,128)(2,1)S(1)} %bitcast_convert_fusion.3), channel_id=1, source_target_pairs={{0,9},{1,10},{2,11},{3,8},{4,13},{5,14},{6,15},{7,12},{8,1},{9,2},... | collective-permute-start | bytes 307208 | tf_op jit(solution)/shard_map/ppermute | solution.py:55
  4.1 15.3 %collective-permute-start.2 = (bf16[400,128]{1,0:T(8,128)(2,1)S(1)}, bf16[400,128]{1,0:T(8,128)(2,1)S(1)}, u32[]{:S(2)}, u32[]{:S(2)}) collective-permute-start(bf16[400,128]{1,0:T(8,128)(2,1)S(1)} %bitcast_convert_fusion.3), channel_id=1, source_target_pairs={{0,17},{1,18},{2,19},{3,16},{4,21},{5,22},{6,23},{7,20},{8,25},{9,... | collective-permute-start | bytes 307208 | tf_op jit(solution)/shard_map/ppermute | solution.py:55
  7.9 12.0 %collective-permute-start.3 = (bf16[400,128]{1,0:T(8,128)(2,1)S(1)}, bf16[400,128]{1,0:T(8,128)(2,1)S(1)}, u32[]{:S(2)}, u32[]{:S(2)}) collective-permute-start(bf16[400,128]{1,0:T(8,128)(2,1)S(1)} %bitcast_convert_fusion.3), channel_id=1, source_target_pairs={{0,25},{1,26},{2,27},{3,24},{4,29},{5,30},{6,31},{7,28},{8,17},{9,... | collective-permute-start | bytes 307208 | tf_op jit(solution)/shard_map/ppermute | solution.py:55
  8.9 12.5 %collective-permute-start = (f32[401,128]{1,0:T(8,128)S(1)}, f32[401,128]{1,0:T(8,128)S(1)}, u32[]{:S(2)}, u32[]{:S(2)}) collective-permute-start(f32[401,128]{1,0:T(8,128)S(1)} %pad_maximum_fusion.5), channel_id=1, source_target_pairs={{0,1},{1,2},{2,3},{3,0},{4,5},{5,6},{6,7},{7,4},{8,9},{9,10},{10,1... | collective-permute-start | bytes 615944 | tf_op jit(solution)/shard_map/ppermute | solution.py:55
  9.9 7.0 %collective-permute-start.8 = (bf16[400,128]{1,0:T(8,128)(2,1)S(1)}, bf16[400,128]{1,0:T(8,128)(2,1)S(1)}, u32[]{:S(2)}, u32[]{:S(2)}) collective-permute-start(bf16[400,128]{1,0:T(8,128)(2,1)S(1)} %bitcast_convert_fusion.2), channel_id=1, source_target_pairs={{0,2},{1,3},{2,0},{3,1},{4,6},{5,7},{6,4},{7,5},{8,10},{9,11},{10,... | collective-permute-start | bytes 307208 | tf_op jit(solution)/shard_map/ppermute | solution.py:48
  16.9 5.4 %collective-permute-start.4 = (bf16[400,128]{1,0:T(8,128)(2,1)S(1)}, bf16[400,128]{1,0:T(8,128)(2,1)S(1)}, u32[]{:S(2)}, u32[]{:S(2)}) collective-permute-start(bf16[400,128]{1,0:T(8,128)(2,1)S(1)} %bitcast_convert_fusion.3), channel_id=1, source_target_pairs={{0,5},{1,6},{2,7},{3,4},{4,1},{5,2},{6,3},{7,0},{8,13},{9,14},{10,... | collective-permute-start | bytes 307208 | tf_op jit(solution)/shard_map/ppermute | solution.py:55
  18.4 10.8 %collective-permute-start.9 = (bf16[400,256]{1,0:T(8,128)(2,1)S(1)}, bf16[400,256]{1,0:T(8,128)(2,1)S(1)}, u32[]{:S(2)}, u32[]{:S(2)}) collective-permute-start(bf16[400,256]{1,0:T(8,128)(2,1)S(1)} %pad_maximum_fusion.6), channel_id=1, source_target_pairs={{0,1},{1,0},{2,3},{3,2},{4,5},{5,4},{6,7},{7,6},{8,9},{9,8},{10,11... | collective-permute-start | bytes 614408 | tf_op jit(solution)/shard_map/ppermute | solution.py:48
  19.4 6.0 %collective-permute-start.5 = (bf16[400,128]{1,0:T(8,128)(2,1)S(1)}, bf16[400,128]{1,0:T(8,128)(2,1)S(1)}, u32[]{:S(2)}, u32[]{:S(2)}) collective-permute-start(bf16[400,128]{1,0:T(8,128)(2,1)S(1)} %collective-permute-done.1), channel_id=1, source_target_pairs={{0,4},{4,0},{8,12},{12,8},{16,20},{20,16},{24,28},{28,24},{1,5},{5... | collective-permute-start | bytes 307208 | tf_op jit(solution)/shard_map/ppermute | solution.py:45
  19.9 7.6 %collective-permute-start.6 = (bf16[400,128]{1,0:T(8,128)(2,1)S(1)}, bf16[400,128]{1,0:T(8,128)(2,1)S(1)}, u32[]{:S(2)}, u32[]{:S(2)}) collective-permute-start(bf16[400,128]{1,0:T(8,128)(2,1)S(1)} %collective-permute-done.2), channel_id=1, source_target_pairs={{0,4},{4,0},{8,12},{12,8},{16,20},{20,16},{24,28},{28,24},{1,5},{5... | collective-permute-start | bytes 307208 | tf_op jit(solution)/shard_map/ppermute | solution.py:45
  21.4 7.8 %collective-permute-start.7 = (bf16[400,128]{1,0:T(8,128)(2,1)S(1)}, bf16[400,128]{1,0:T(8,128)(2,1)S(1)}, u32[]{:S(2)}, u32[]{:S(2)}) collective-permute-start(bf16[400,128]{1,0:T(8,128)(2,1)S(1)} %collective-permute-done.3), channel_id=1, source_target_pairs={{0,4},{4,0},{8,12},{12,8},{16,20},{20,16},{24,28},{28,24},{1,5},{5... | collective-permute-start | bytes 307208 | tf_op jit(solution)/shard_map/ppermute | solution.py:45
  36.3 0.8 copy-start.2
  37.6 4.8 %collective-permute-start.10 = (bf16[600,128]{1,0:T(8,128)(2,1)S(1)}, bf16[600,128]{1,0:T(8,128)(2,1)S(1)}, u32[]{:S(2)}, u32[]{:S(2)}) collective-permute-start(bf16[600,128]{1,0:T(8,128)(2,1)S(1)} %pad_maximum_fusion.9), channel_id=1, source_target_pairs={{0,1},{1,0},{2,3},{3,2},{4,5},{5,4},{6,7},{7,6},{8,9},{9,8},{10,11... | collective-permute-start | bytes 460808 | tf_op jit(solution)/shard_map/ppermute | solution.py:48
  37.7 6.8 %collective-permute-start.11 = (bf16[600,128]{1,0:T(8,128)(2,1)S(1)}, bf16[600,128]{1,0:T(8,128)(2,1)S(1)}, u32[]{:S(2)}, u32[]{:S(2)}) collective-permute-start(bf16[600,128]{1,0:T(8,128)(2,1)S(1)} %pad_maximum_fusion.10), channel_id=1, source_target_pairs={{0,2},{1,3},{2,0},{3,1},{4,6},{5,7},{6,4},{7,5},{8,10},{9,11},{10,... | collective-permute-start | bytes 460808 | tf_op jit(solution)/shard_map/ppermute | solution.py:48
  38.9 8.2 %collective-permute-start.12 = (bf16[600,128]{1,0:T(8,128)(2,1)S(1)}, bf16[600,128]{1,0:T(8,128)(2,1)S(1)}, u32[]{:S(2)}, u32[]{:S(2)}) collective-permute-start(bf16[600,128]{1,0:T(8,128)(2,1)S(1)} %pad_maximum_fusion.11), channel_id=1, source_target_pairs={{0,3},{1,2},{2,1},{3,0},{4,7},{5,6},{6,5},{7,4},{8,11},{9,10},{10,... | collective-permute-start | bytes 460808 | tf_op jit(solution)/shard_map/ppermute | solution.py:48
  39.8 17.3 %collective-permute-start.13 = (bf16[400,256]{1,0:T(8,128)(2,1)S(1)}, bf16[400,256]{1,0:T(8,128)(2,1)S(1)}, u32[]{:S(2)}, u32[]{:S(2)}) collective-permute-start(bf16[400,256]{1,0:T(8,128)(2,1)S(1)} %get-tuple-element.23), channel_id=1, source_target_pairs={{0,4},{4,0},{8,12},{12,8},{16,20},{20,16},{24,28},{28,24},{1,5},{5... | collective-permute-start | bytes 614408 | tf_op jit(solution)/shard_map/ppermute | solution.py:45
  41.3 7.4 %copy-start.4 = (f32[128]{0:T(128)S(1)}, f32[128]{0:T(128)}, u32[]{:S(2)}) copy-start(f32[128]{0:T(128)} %param.11) | copy-start | bytes 1540
  41.3 7.9 %copy-start.1 = (f32[128,400]{0,1:T(8,128)S(1)}, f32[128,400]{0,1:T(8,128)}, u32[]{:S(2)}) copy-start(f32[128,400]{0,1:T(8,128)} %param.10) | copy-start | bytes 614404
  41.3 15.7 %collective-permute-start.14 = (bf16[400,256]{1,0:T(8,128)(2,1)S(1)}, bf16[400,256]{1,0:T(8,128)(2,1)S(1)}, u32[]{:S(2)}, u32[]{:S(2)}) collective-permute-start(bf16[400,256]{1,0:T(8,128)(2,1)S(1)} %get-tuple-element.22), channel_id=1, source_target_pairs={{0,4},{4,0},{8,12},{12,8},{16,20},{20,16},{24,28},{28,24},{1,5},{5... | collective-permute-start | bytes 614408 | tf_op jit(solution)/shard_map/ppermute | solution.py:45
  47.1 5.5 %collective-permute-start.18 = (bf16[200,128]{1,0:T(8,128)(2,1)S(1)}, bf16[200,128]{1,0:T(8,128)(2,1)S(1)}, u32[]{:S(2)}, u32[]{:S(2)}) collective-permute-start(bf16[200,128]{1,0:T(8,128)(2,1)S(1)} %fusion.32), channel_id=1, source_target_pairs={{0,4},{4,0},{8,12},{12,8},{16,20},{20,16},{24,28},{28,24},{1,5},{5... | collective-permute-start | bytes 153608 | tf_op jit(solution)/shard_map/ppermute | solution.py:45
  52.6 4.7 %collective-permute-start.19 = (bf16[200,128]{1,0:T(8,128)(2,1)S(1)}, bf16[200,128]{1,0:T(8,128)(2,1)S(1)}, u32[]{:S(2)}, u32[]{:S(2)}) collective-permute-start(bf16[200,128]{1,0:T(8,128)(2,1)S(1)} %add_convert_fusion.4), channel_id=1, source_target_pairs={{0,8},{4,12},{8,0},{12,4},{16,24},{20,28},{24,16},{28,20},{1,9},{5... | collective-permute-start | bytes 153608 | tf_op jit(solution)/shard_map/ppermute | solution.py:45
  53.6 5.0 %collective-permute-start.20 = (bf16[200,128]{1,0:T(8,128)(2,1)S(1)}, bf16[200,128]{1,0:T(8,128)(2,1)S(1)}, u32[]{:S(2)}, u32[]{:S(2)}) collective-permute-start(bf16[200,128]{1,0:T(8,128)(2,1)S(1)} %add_convert_fusion.4), channel_id=1, source_target_pairs={{0,16},{4,20},{8,24},{12,28},{16,0},{20,4},{24,8},{28,12},{1,17},{... | collective-permute-start | bytes 153608 | tf_op jit(solution)/shard_map/ppermute | solution.py:45
  56.2 5.9 %collective-permute-start.21 = (bf16[200,128]{1,0:T(8,128)(2,1)S(1)}, bf16[200,128]{1,0:T(8,128)(2,1)S(1)}, u32[]{:S(2)}, u32[]{:S(2)}) collective-permute-start(bf16[200,128]{1,0:T(8,128)(2,1)S(1)} %add_convert_fusion.4), channel_id=1, source_target_pairs={{0,24},{4,28},{8,16},{12,20},{16,8},{20,12},{24,0},{28,4},{1,25},{... | collective-permute-start | bytes 153608 | tf_op jit(solution)/shard_map/ppermute | solution.py:45
  57.2 12.4 %copy-start.3 = (f32[256]{0:T(256)S(1)}, f32[256]{0:T(256)}, u32[]{:S(2)}) copy-start(f32[256]{0:T(256)} %param.15) | copy-start | bytes 3076
  57.2 13.0 %copy-start = (f32[256,400]{0,1:T(8,128)S(1)}, f32[256,400]{0,1:T(8,128)}, u32[]{:S(2)}) copy-start(f32[256,400]{0,1:T(8,128)} %param.14) | copy-start | bytes 1228804
  62.2 2.9 %collective-permute-start.22 = (bf16[200,128]{1,0:T(8,128)(2,1)S(1)}, bf16[200,128]{1,0:T(8,128)(2,1)S(1)}, u32[]{:S(2)}, u32[]{:S(2)}) collective-permute-start(bf16[200,128]{1,0:T(8,128)(2,1)S(1)} %add_convert_fusion.3), channel_id=1, source_target_pairs={{0,1},{1,0},{2,3},{3,2},{4,5},{5,4},{6,7},{7,6},{8,9},{9,8},{10,11... | collective-permute-start | bytes 153608 | tf_op jit(solution)/shard_map/ppermute | solution.py:48
  62.2 6.4 %collective-permute-start.23 = (bf16[200,128]{1,0:T(8,128)(2,1)S(1)}, bf16[200,128]{1,0:T(8,128)(2,1)S(1)}, u32[]{:S(2)}, u32[]{:S(2)}) collective-permute-start(bf16[200,128]{1,0:T(8,128)(2,1)S(1)} %add_convert_fusion.3), channel_id=1, source_target_pairs={{0,2},{1,3},{2,0},{3,1},{4,6},{5,7},{6,4},{7,5},{8,10},{9,11},{10,... | collective-permute-start | bytes 153608 | tf_op jit(solution)/shard_map/ppermute | solution.py:48
  63.4 5.3 %collective-permute-start.24 = (bf16[200,128]{1,0:T(8,128)(2,1)S(1)}, bf16[200,128]{1,0:T(8,128)(2,1)S(1)}, u32[]{:S(2)}, u32[]{:S(2)}) collective-permute-start(bf16[200,128]{1,0:T(8,128)(2,1)S(1)} %add_convert_fusion.3), channel_id=1, source_target_pairs={{0,3},{1,2},{2,1},{3,0},{4,7},{5,6},{6,5},{7,4},{8,11},{9,10},{10,... | collective-permute-start | bytes 153608 | tf_op jit(solution)/shard_map/ppermute | solution.py:48
  64.1 7.7 %collective-permute-start.15 = (bf16[400,128]{1,0:T(8,128)(2,1)S(1)}, bf16[400,128]{1,0:T(8,128)(2,1)S(1)}, u32[]{:S(2)}, u32[]{:S(2)}) collective-permute-start(bf16[400,128]{1,0:T(8,128)(2,1)S(1)} %get-tuple-element.27), channel_id=1, source_target_pairs={{0,24},{4,28},{8,16},{12,20},{16,8},{20,12},{24,0},{28,4},{1,25},{... | collective-permute-start | bytes 307208 | tf_op jit(solution)/shard_map/ppermute | solution.py:45
  65.1 10.1 %collective-permute-start.16 = (bf16[400,128]{1,0:T(8,128)(2,1)S(1)}, bf16[400,128]{1,0:T(8,128)(2,1)S(1)}, u32[]{:S(2)}, u32[]{:S(2)}) collective-permute-start(bf16[400,128]{1,0:T(8,128)(2,1)S(1)} %get-tuple-element.28), channel_id=1, source_target_pairs={{0,16},{4,20},{8,24},{12,28},{16,0},{20,4},{24,8},{28,12},{1,17},{... | collective-permute-start | bytes 307208 | tf_op jit(solution)/shard_map/ppermute | solution.py:45
  65.1 10.1 %collective-permute-start.17 = (bf16[400,128]{1,0:T(8,128)(2,1)S(1)}, bf16[400,128]{1,0:T(8,128)(2,1)S(1)}, u32[]{:S(2)}, u32[]{:S(2)}) collective-permute-start(bf16[400,128]{1,0:T(8,128)(2,1)S(1)} %slice.255), channel_id=1, source_target_pairs={{0,8},{4,12},{8,0},{12,4},{16,24},{20,28},{24,16},{28,20},{1,9},{5... | collective-permute-start | bytes 307208 | tf_op jit(solution)/shard_map/ppermute | solution.py:45

commit v3 on v2

v3 whole, which is shorter than its diff:
```python
import functools

import jax
import jax.numpy as jnp
from jax import lax
from jax.experimental import pallas as pl
from jax.experimental.pallas import tpu as pltpu
from jax.sharding import PartitionSpec as P

LEARN_RATE = 0.1
NEG_WEIGHT = 0.03125
BF = jnp.bfloat16
F32 = jnp.float32
VMEM_LIMIT = 32 * 1024 * 1024
LANES = 128


def dot(a, b, a_dim, b_dim):
    return lax.dot_general(a, b, (((a_dim,), (b_dim,)), ((), ())), preferred_element_type=F32)


def hot(ids, count):
    spot = lax.broadcasted_iota(jnp.int32, (count, ids.shape[1]), 0)
    return jnp.where(spot == ids, 1.0, 0.0).astype(BF)


def step_of(size, most=256):
    return most if size % most == 0 else size


def call(body, out_shape, flops, scratch=(), here=None):
    def run(*args):
        moved = sum(a.size * a.dtype.itemsize for a in args)
        specs = [pl.BlockSpec(memory_space=pltpu.VMEM)] * len(args)
        if here is not None:
            specs.append(pl.BlockSpec(memory_space=pltpu.SMEM))
            args = (*args, here)
        return pl.pallas_call(
            body,
            out_shape=out_shape,
            in_specs=specs,
            scratch_shapes=list(scratch),
            compiler_params=pltpu.CompilerParams(vmem_limit_bytes=VMEM_LIMIT),
            cost_estimate=pl.CostEstimate(flops=flops, bytes_accessed=moved, transcendentals=0),
        )(*args)

    return run


def shape(*dims, dtype=F32):
    return jax.ShapeDtypeStruct(dims, dtype)


def count_body(ids_ref, out_ref):
    for g in range(out_ref.shape[0]):
        ids = ids_ref[g:g + 1, :]
        for at in range(0, out_ref.shape[1], LANES):
            spot = lax.broadcasted_iota(jnp.int32, (LANES, ids.shape[1]), 0) + at
            total = jnp.sum(jnp.where(spot == ids, NEG_WEIGHT, 0.0), axis=1, keepdims=True)
            out_ref[g, at:at + LANES, :] = jnp.broadcast_to(total, (LANES, LANES))


def query_body(near_ref, sibling_ref, relation_ref, source_ref, kind_ref, s_ref, o_ref, q_ref):
    relation = relation_ref[...].astype(BF)
    half_rows = near_ref.shape[1]
    half = s_ref.shape[0] // 2
    edges = s_ref.shape[1]
    step = step_of(edges)
    for at in range(0, edges, step):
        cols = slice(at, at + step)
        pick = hot(source_ref[:, cols], 2 * half_rows)
        s = dot(near_ref[...], pick[:half_rows], 1, 0) + dot(sibling_ref[...], pick[half_rows:], 1, 0)
        o = dot(relation, hot(kind_ref[:, cols], relation.shape[1]), 1, 0)
        s_ref[:, cols] = s.astype(BF)
        o_ref[:, cols] = o.astype(BF)
        s_re, s_im, o_re, o_im = s[:half], s[half:], o[:half], o[half:]
        q = jnp.concatenate([s_re * o_re - s_im * o_im, s_re * o_im + s_im * o_re], axis=0)
        q_ref[:, cols] = q.astype(BF)


def grad_matrix(rows_ref, q_ref, weight_ref, target_ref, m_ref, base):
    count = rows_ref.shape[1]
    rows_t = rows_ref[...].T
    edges = q_ref.shape[1]
    groups = weight_ref.shape[0]
    step = step_of(edges // groups)
    for at in range(0, edges, step):
        cols = slice(at, at + step)
        scores = dot(rows_t, q_ref[:, cols], 1, 0)
        spot = lax.broadcasted_iota(jnp.int32, (count, step), 0) + base
        h = jnp.where(spot == target_ref[:, cols], 1.0, 0.0)
        w = weight_ref[at // (edges // groups), base:base + count, :]
        w = jnp.concatenate([w] * (step // LANES), axis=1)
        m = (w + h) * (0.5 * jnp.tanh(0.5 * scores) + 0.5) - h
        m_ref[:, cols] = m.astype(BF)


def near_body(blocks, *refs):
    block_refs, refs = refs[:blocks], refs[blocks:]
    q_ref, weight_ref, target_ref, table_ref, state_ref, right_ref, qg_ref, pack_ref, rows_ref, m_ref = refs
    for k, ref in enumerate(block_refs):
        rows_ref[:, k * LANES:(k + 1) * LANES] = ref[...]
    grad_matrix(rows_ref, q_ref, weight_ref, target_ref, m_ref, 0)
    right_ref[...] = dot(q_ref[...], m_ref[...], 1, 1)
    qg_ref[...] = dot(rows_ref[...], m_ref[...], 1, 0)
    width = table_ref.shape[0]
    pack_ref[:width, :] = table_ref[...]
    pack_ref[width:, :] = jnp.broadcast_to(state_ref[...], (pack_ref.shape[0] - width, LANES))


def far_body(blocks, *refs):
    block_refs, refs = refs[:blocks], refs[blocks:]
    q_ref, weight_ref, target_ref, m_ref, hi_ref, lo_ref, rows_ref = refs
    for k, ref in enumerate(block_refs):
        rows_ref[:, k * LANES:(k + 1) * LANES] = ref[...]
    count = rows_ref.shape[1]
    grad_matrix(rows_ref, q_ref, weight_ref, target_ref, m_ref, count)
    far = dot(q_ref[...], m_ref[...], 1, 1).astype(BF)
    hi_ref[...] = far[:, count // 2:]
    lo_ref[...] = far[:, :count // 2]


def back_body(blocks, pieces, *refs):
    block_refs, refs = refs[:blocks], refs[blocks:]
    m_ref, qg_ref, s_ref, o_ref, source_ref, kind_ref, here_ref, near_ref, far_ref = refs[:9]
    piece_refs, refs = refs[9:9 + pieces], refs[9 + pieces:]
    rows_ref, left_ref, kinds_ref, tall_ref = refs
    for k, ref in enumerate(block_refs):
        rows_ref[:, k * LANES:(k + 1) * LANES] = ref[...]
    width, edges = qg_ref.shape
    half = width // 2
    step = step_of(edges)
    for at in range(0, edges, step):
        cols = slice(at, at + step)
        g = qg_ref[:, cols] + dot(rows_ref[...], m_ref[:, cols], 1, 0)
        s = s_ref[:, cols].astype(F32)
        o = o_ref[:, cols].astype(F32)
        g_re, g_im = g[:half], g[half:]
        s_re, s_im, o_re, o_im = s[:half], s[half:], o[:half], o[half:]
        by_kind = jnp.concatenate([g_re * s_re + g_im * s_im, g_im * s_re - g_re * s_im], axis=0).astype(BF)
        by_source = jnp.concatenate([g_re * o_re + g_im * o_im, g_im * o_re - g_re * o_im], axis=0).astype(BF)
        kinds = dot(by_kind, hot(kind_ref[:, cols], kinds_ref.shape[1]), 1, 1)
        left = dot(by_source, hot(source_ref[:, cols], left_ref.shape[1]), 1, 1)
        if at == 0:
            kinds_ref[...] = kinds
            left_ref[...] = left
        else:
            kinds_ref[...] += kinds
            left_ref[...] += left
    cut = left_ref.shape[1] // 2
    near_ref[...] = left_ref[:, :cut]
    far_ref[...] = left_ref[:, cut:].astype(BF)
    parts = kinds_ref.shape[1] // LANES
    for j in range(parts):
        tall_ref[j * width:(j + 1) * width, :] = kinds_ref[:, j * LANES:(j + 1) * LANES]
    rest = tall_ref.shape[0] - parts * width
    if rest:
        tall_ref[parts * width:, :] = jnp.zeros((rest, LANES), F32)
    here = here_ref[0]
    size = tall_ref.shape[0] // pieces
    for k, ref in enumerate(piece_refs):
        start = pl.multiple_of((here ^ k) * size, 16)
        ref[...] = tall_ref[pl.ds(start, size), :].astype(BF)


def relation_body(pieces, *refs):
    piece_refs, refs = refs[:pieces], refs[pieces:]
    table_ref, state_ref, here_ref, new_ref, state_new_ref, tall_ref = refs
    here = here_ref[0]
    size = tall_ref.shape[0] // pieces
    for k, ref in enumerate(piece_refs):
        start = pl.multiple_of((here ^ k) * size, 16)
        tall_ref[pl.ds(start, size), :] = ref[...].astype(F32)
    width, count = table_ref.shape
    for j in range(count // LANES):
        cols = slice(j * LANES, (j + 1) * LANES)
        g = tall_ref[j * width:(j + 1) * width, :]
        state = state_ref[:, cols] + jnp.sum(g * g, axis=0, keepdims=True) * (1.0 / width)
        state_new_ref[:, cols] = state
        new_ref[:, cols] = table_ref[:, cols] - g * (LEARN_RATE * lax.rsqrt(state))


def adagrad(table, state, grad):
    state_new = state + jnp.mean(grad * grad, axis=0)
    return table - LEARN_RATE * grad * lax.rsqrt(state_new)[None, :], state_new


def build(mesh):
    n_left, n_right = mesh.shape["left"], mesh.shape["right"]
    for count in (n_left, n_right):
        assert count & (count - 1) == 0 and count > 3
    outer = n_left // 2
    far_right = n_right // 2

    def swap_left(value, by):
        return lax.ppermute(value, "left", [(i, i ^ by) for i in range(n_left)])

    def swap_right(value, by):
        return lax.ppermute(value, "right", [(i, i ^ by) for i in range(n_right)])

    def next_column(value, by):
        perm = []
        for i in range(n_left):
            for r in range(n_right):
                perm.append((i * n_right + r, (i ^ by) * n_right + (r + 1) % n_right))
        return lax.ppermute(value, ("left", "right"), perm)

    def per_device(
        left_table, left_state, right_table, right_state, relation_table, relation_state,
        source_ids, target_ids, relation_ids, negative_ids,
    ):
        rows = left_table.shape[0]
        width = left_table.shape[1]
        left_t, right_t, relation_t = left_table.T, right_table.T, relation_table.T
        nrel = relation_t.shape[1]
        here_l, here_r = lax.axis_index("left"), lax.axis_index("right")
        me = here_r.astype(jnp.int32).reshape(1)
        source = source_ids.reshape(1, -1)
        target = target_ids.reshape(1, -1)
        kind = relation_ids.reshape(1, -1)
        negative = negative_ids.reshape(negative_ids.shape[2], negative_ids.shape[3])
        groups = negative.shape[0]
        edges = source.shape[1]
        n_rows = n_left * rows
        half = outer * rows

        right_bf = right_t.astype(BF)
        near = {k: next_column(right_bf, 2 * k) for k in range(outer - 1, -1, -1)}
        left_bf = left_t.astype(BF)
        half_left = [left_bf] + [swap_right(left_bf, 2 * k) for k in range(1, far_right)]
        half_left = jnp.concatenate(half_left, axis=1)
        sibling_left = swap_right(half_left, 1)
        other = {k: swap_left(near[k], 1) for k in range(outer)}
        near = [near[k] for k in range(outer)]
        other = [other[k] for k in range(outer)]

        def local(ids, here, half):
            block = (ids // rows) ^ here
            return (block % 2 * half + block // 2) * rows + ids % rows

        source = local(source, here_r, far_right)
        target = local(target, here_l, outer)
        negative = local(negative, here_l, outer)

        flop = 2 * width * edges
        weight = call(count_body, shape(groups, n_rows, LANES), 4 * n_rows * edges)(negative)
        table_bf = shape(width, edges, dtype=BF)
        s, o, q = call(query_body, (table_bf, table_bf, table_bf), flop * (n_right * rows + nrel))(
            half_left, sibling_left, relation_t, source, kind
        )
        part = pltpu.VMEM((width, half), BF)
        right_near, qg_near, pack = call(
            functools.partial(near_body, outer),
            (shape(width, half), shape(width, edges), shape(width + 8, rows)),
            3 * flop * half,
            [part, pltpu.VMEM((half, edges), BF)],
        )(*near, q, weight, target, right_t, right_state[None, :])
        moved = next_column(pack, 0)
        chunk = shape(width, half // 2, dtype=BF)
        m, far_hi, far_lo = call(
            functools.partial(far_body, outer), (shape(half, edges, dtype=BF), chunk, chunk), 2 * flop * half, [part]
        )(*other, q, weight, target)
        got_hi = swap_left(far_hi, 1)
        got_lo = swap_left(far_lo, 1)
        tall = nrel // LANES * width
        size = -(-tall // (n_right * 16)) * 16
        piece = shape(size, LANES, dtype=BF)
        left_rows = n_right * rows
        left_near, left_far, *pieces = call(
            functools.partial(back_body, outer, n_right),
            (shape(width, left_rows // 2), shape(width, left_rows // 2, dtype=BF)) + (piece,) * n_right,
            flop * (half + nrel + left_rows),
            [part, pltpu.VMEM((width, left_rows), F32), pltpu.VMEM((width, nrel), F32),
             pltpu.VMEM((size * n_right, LANES), F32)],
            me,
        )(*other, m, qg_near, s, o, source, kind)

        got = [pieces[0]] + [swap_right(pieces[k], k) for k in range(1, n_right)]
        got = [g.astype(F32) for g in got]
        while len(got) > 1:
            got = [got[i] + got[i + 1] for i in range(0, len(got), 2)]
        mine = got[0].astype(BF)
        bit = 2
        bits = []
        while bit < n_left:
            bits.append(bit)
            bit *= 2
        for bit in bits + [1]:
            mine = (mine.astype(F32) + swap_left(mine, bit).astype(F32)).astype(BF)
        pieces = [mine] + [swap_right(mine, k) for k in range(1, n_right)]

        cut = half // 2
        hi = right_near[:, cut:] + got_hi.astype(F32)
        lo = right_near[:, :cut] + got_lo.astype(F32)
        hi_bf, lo_bf = hi.astype(BF), lo.astype(BF)
        right_sum = lo[:, :rows]
        for k in range(outer - 1, 0, -1):
            at = k * rows
            block = lo_bf[:, at:at + rows] if at < cut else hi_bf[:, at - cut:at - cut + rows]
            right_sum = right_sum + swap_left(block, 2 * k).astype(F32)

        left_near = left_near + swap_right(left_far, 1).astype(F32)
        left_bf_sum = left_near.astype(BF)
        left_sum = left_near[:, :rows]
        for k in range(1, far_right):
            left_sum = left_sum + swap_right(left_bf_sum[:, k * rows:(k + 1) * rows], 2 * k).astype(F32)

        left_new, left_state_new = adagrad(left_t, left_state, left_sum)
        right_new, right_state_new = adagrad(moved[:width], moved[width], right_sum)
        relation_new, relation_state_new = call(
            functools.partial(relation_body, n_right),
            (shape(width, nrel), shape(1, nrel)),
            8 * width * nrel,
            [pltpu.VMEM((size * n_right, LANES), F32)],
            me,
        )(*pieces, relation_t, relation_state[None, :])
        return (
            left_new.T, left_state_new, right_new.T, right_state_new, relation_new.T, relation_state_new.reshape(-1),
        )

    return per_device


def solution(mesh):
    rows = P(("left", "right"), None)
    vector = P(("left", "right"))
    ids = P("left", "right", None)
    return jax.shard_map(
        build(mesh),
        mesh=mesh,
        in_specs=(rows, vector, rows, vector, P(), P(), ids, ids, ids, P("left", "right", None, None)),
        out_specs=(rows, vector, rows, vector, P(), P()),
        check_vma=False,
    )
```

time: 76.9 us -> 77.2 us (level)
  matrix products: 8.72 us -> 0 us
  Pallas kernels: 0 us -> 8.27 us
  waiting for transfers between devices: 23.6 us -> 29.7 us
  other arithmetic: 11.8 us -> 7.14 us
  local copies, waits for them, and re-layouts: 1.58 us -> 0.08 us
  starting transfers between devices: 29.8 us -> 31 us
    dot_general x8 -> x0, matrix products: 8.72 us -> none  [dot(): lax.dot_general(a, b, (((a_dim,), (b_dim,)), ((), ())), preferred_element...]
    pallas_call x0 -> x6, Pallas kernels: none -> 8.27 us  [run(): pl.pallas_call(body, out_shape=out_shape, in_specs=specs, scratch_shapes=...]
    ppermute x8 -> x10, waiting for transfers between devices: 4.83 us -> 8.3 us  [swap_right(): return lax.ppermute(value, 'right', [(i, i ^ by) for i in range(n_right)])]
    ppermute x12, waiting for transfers between devices: 18.6 us -> 21.3 us  [swap_left(): return lax.ppermute(value, 'left', [(i, i ^ by) for i in range(n_left)])]
    ppermute x12, starting transfers between devices: 15.2 us -> 16.9 us  [swap_left(): return lax.ppermute(value, 'left', [(i, i ^ by) for i in range(n_left)])]
    another operation x3 -> x0, other arithmetic: 1.13 us -> none
    concatenate x5 -> x0, other arithmetic: 1.01 us -> none  [the longest x1 0.96 us: per_device(): jnp.concatenate([right_t, right_state[None, :]], axis=0)]
    ppermute x5, starting transfers between devices: 7.89 us -> 6.89 us  [next_column(): return lax.ppermute(value, ('left', 'right'), perm)]
  transfers between devices with their start and end apart: 25 -> 27, of which waited for: 13 -> 13; matrix products, arithmetic and copies ran while one was open for 15% -> 5% of each run, Pallas kernels for 0% -> 6%
where the time goes in v3:
time: 77.2 us; the launch traced here: 76.9 us
  starting transfers between devices  31 us (40%)
  waiting for transfers between devices  29.7 us (38%)
  Pallas kernels  8.27 us (11%)
  other arithmetic  7.14 us (9%)
  between operations  0.83 us (1%)
    ppermute x12, waiting for transfers between devices, swap_left(): return lax.ppermute(value, 'left', [(i, i ^ by) for i in range(n_left)])  21.3 us
    ppermute x12, starting transfers between devices, swap_left(): return lax.ppermute(value, 'left', [(i, i ^ by) for i in range(n_left)])  16.9 us
    ppermute x10, waiting for transfers between devices, swap_right(): return lax.ppermute(value, 'right', [(i, i ^ by) for i in range(n_right)])  8.3 us
    pallas_call x6, Pallas kernels, run(): pl.pallas_call(body, out_shape=out_shape, in_specs=specs, scratch_shapes=...  8.27 us
    ppermute x10, starting transfers between devices, swap_right(): return lax.ppermute(value, 'right', [(i, i ^ by) for i in range(n_right)])  7.15 us
    ppermute x5, starting transfers between devices, next_column(): return lax.ppermute(value, ('left', 'right'), perm)  6.89 us
    add x3, other arithmetic, local(): return (block % 2 * half + block // 2) * rows + ids % rows  2.28 us
  transfers between devices with their start and end apart: 27, of which 13 were waited for; matrix products, arithmetic and copies ran while one was open for 5% of the time, Pallas kernels for 6%

profile of v3, /device:TPU:0, one launch (start us, length us, event | category | flops | bytes accessed | tf_op | source)
XLA Modules:
  0.0 76.9 jit_solution(15582154964916042700)
XLA Ops:
  0.7 1.0 %bitcast_convert_fusion.1 = bf16[400,128]{1,0:T(8,128)(2,1)S(1)} fusion(f32[128,400]{0,1:T(8,128)} %param.12), kind=kLoop, calls=%fused_computation.71 | loop fusion | flops 51200 | bytes 307200 | tf_op jit(solution)/shard_map/convert_element_type | solution.py:227
  1.6 4.5 %collective-permute-start.6 = (bf16[400,128]{1,0:T(8,128)(2,1)S(1)}, bf16[400,128]{1,0:T(8,128)(2,1)S(1)}, u32[]{:S(2)}, u32[]{:S(2)}) collective-permute-start(bf16[400,128]{1,0:T(8,128)(2,1)S(1)} %bitcast_convert_fusion.1), channel_id=1, source_target_pairs={{0,25},{1,26},{2,27},{3,24},{4,29},{5,30},{6,31},{7,28},{8,17},{9,... | collective-permute-start | bytes 307208 | tf_op jit(solution)/shard_map/ppermute | solution.py:206
  6.2 0.6 collective-permute-start.4
  6.8 1.2 %collective-permute-start.2 = (bf16[400,128]{1,0:T(8,128)(2,1)S(1)}, bf16[400,128]{1,0:T(8,128)(2,1)S(1)}, u32[]{:S(2)}, u32[]{:S(2)}) collective-permute-start(bf16[400,128]{1,0:T(8,128)(2,1)S(1)} %bitcast_convert_fusion.1), channel_id=1, source_target_pairs={{0,9},{1,10},{2,11},{3,8},{4,13},{5,14},{6,15},{7,12},{8,1},{9,2},... | collective-permute-start | bytes 307208 | tf_op jit(solution)/shard_map/ppermute | solution.py:206
  8.0 0.9 %bitcast_convert_fusion = bf16[400,128]{1,0:T(8,128)(2,1)S(1)} fusion(f32[128,400]{0,1:T(8,128)} %param.10), kind=kLoop, calls=%fused_computation.13 | loop fusion | flops 51200 | bytes 307200 | tf_op jit(solution)/shard_map/convert_element_type | solution.py:229
  9.0 1.8 %collective-permute-start.8 = (bf16[400,128]{1,0:T(8,128)(2,1)S(1)}, bf16[400,128]{1,0:T(8,128)(2,1)S(1)}, u32[]{:S(2)}, u32[]{:S(2)}) collective-permute-start(bf16[400,128]{1,0:T(8,128)(2,1)S(1)} %bitcast_convert_fusion), channel_id=1, source_target_pairs={{0,2},{1,3},{2,0},{3,1},{4,6},{5,7},{6,4},{7,5},{8,10},{9,11},{10,... | collective-permute-start | bytes 307208 | tf_op jit(solution)/shard_map/ppermute | solution.py:199
  10.8 0.8 fusion.6.ids_ref
  11.5 0.8 fusion.8.refs_6_
  12.3 3.5 %collective-permute-done.8 = bf16[400,128]{1,0:T(8,128)(2,1)S(1)} collective-permute-done((bf16[400,128]{1,0:T(8,128)(2,1)S(1)}, bf16[400,128]{1,0:T(8,128)(2,1)S(1)}, u32[]{:S(2)}, u32[]{:S(2)}) %collective-permute-start.8) | collective-permute-done | bytes 102432 | tf_op jit(solution)/shard_map/ppermute | solution.py:199
  15.8 0.5 collective-permute-start.9
  16.3 0.8 fusion.7.source_ref.refs_8_
  17.1 0.9 %shard_map.146.refs_5_ = f32[2,1024,128]{2,1,0:T(8,128)S(1)} custom-call(s32[2,1024]{1,0:T(2,128)S(1)} %fusion.6.ids_ref), custom_call_target="tpu_custom_call" | custom-call | flops 4194304 | bytes 8192 | tf_op jit(solution)/shard_map/pallas_call | solution.py:38
  18.0 1.7 %collective-permute-start.7 = (bf16[400,128]{1,0:T(8,128)(2,1)S(1)}, bf16[400,128]{1,0:T(8,128)(2,1)S(1)}, u32[]{:S(2)}, u32[]{:S(2)}) collective-permute-start(bf16[400,128]{1,0:T(8,128)(2,1)S(1)} %collective-permute-done.6.refs_3_), channel_id=1, source_target_pairs={{0,4},{4,0},{8,12},{12,8},{16,20},{20,16},{24,28},{28,24},{1,5},{5... | collective-permute-start | bytes 307208 | tf_op jit(solution)/shard_map/ppermute | solution.py:196
  20.1 1.6 %collective-permute-start.3 = (bf16[400,128]{1,0:T(8,128)(2,1)S(1)}, bf16[400,128]{1,0:T(8,128)(2,1)S(1)}, u32[]{:S(2)}, u32[]{:S(2)}) collective-permute-start(bf16[400,128]{1,0:T(8,128)(2,1)S(1)} %collective-permute-done.2.refs_1_), channel_id=1, source_target_pairs={{0,4},{4,0},{8,12},{12,8},{16,20},{20,16},{24,28},{28,24},{1,5},{5... | collective-permute-start | bytes 307208 | tf_op jit(solution)/shard_map/ppermute | solution.py:196
  22.1 0.9 %shard_map.145 = (bf16[400,1024]{1,0:T(8,128)(2,1)S(1)}, bf16[400,1024]{1,0:T(8,128)(2,1)S(1)}, bf16[400,1024]{1,0:T(8,128)(2,1)S(1)}) custom-call(bf16[400,256]{1,0:T(8,128)(2,1)S(1)} %pad_maximum_fusion.near_ref, bf16[400,256]{1,0:T(8,128)(2,1)S(1)} %collective-permute-done.9.sibling_ref, f32[400,256]{1,0:T(8,128)S(1)} %bitcast.70, ...), custom_call_target="tpu_custom_call" | custom-call | flops 629145600 | bytes 827392 | tf_op jit(solution)/shard_map/pallas_call | solution.py:38
  23.0 1.8 %shard_map.148 = (f32[400,512]{1,0:T(8,128)S(1)}, f32[400,1024]{1,0:T(8,128)S(1)}, f32[408,128]{1,0:T(8,128)S(1)}) custom-call(bf16[400,128]{1,0:T(8,128)(2,1)S(1)} %collective-permute-done.refs_0_, bf16[400,128]{1,0:T(8,128)(2,1)S(1)} %collective-permute-done.2.refs_1_, bf16[400,128]{1,0:T(8,128)(2,1)S(1)} %collective-permute-done.4.refs_2_, ...), custom_call_target="tpu_custom_call" | custom-call | flops 1258291200 | bytes 2486784 | tf_op jit(solution)/shard_map/pallas_call | solution.py:38
  24.9 1.1 %collective-permute-done.5.refs_2_ = bf16[400,128]{1,0:T(8,128)(2,1)S(1)} collective-permute-done((bf16[400,128]{1,0:T(8,128)(2,1)S(1)}, bf16[400,128]{1,0:T(8,128)(2,1)S(1)}, u32[]{:S(2)}, u32[]{:S(2)}) %collective-permute-start.5) | collective-permute-done | bytes 102432 | tf_op jit(solution)/shard_map/ppermute | solution.py:196
  25.9 2.2 %collective-permute-done.3.refs_1_ = bf16[400,128]{1,0:T(8,128)(2,1)S(1)} collective-permute-done((bf16[400,128]{1,0:T(8,128)(2,1)S(1)}, bf16[400,128]{1,0:T(8,128)(2,1)S(1)}, u32[]{:S(2)}, u32[]{:S(2)}) %collective-permute-start.3) | collective-permute-done | bytes 102432 | tf_op jit(solution)/shard_map/ppermute | solution.py:196
  28.1 1.5 %collective-permute-done.1.refs_0_ = bf16[400,128]{1,0:T(8,128)(2,1)S(1)} collective-permute-done((bf16[400,128]{1,0:T(8,128)(2,1)S(1)}, bf16[400,128]{1,0:T(8,128)(2,1)S(1)}, u32[]{:S(2)}, u32[]{:S(2)}) %collective-permute-start.1) | collective-permute-done | bytes 102432 | tf_op jit(solution)/shard_map/ppermute | solution.py:196
  29.7 1.5 %shard_map.147 = (bf16[512,1024]{1,0:T(8,128)(2,1)S(1)}, bf16[400,256]{1,0:T(8,128)(2,1)S(1)}, bf16[400,256]{1,0:T(8,128)(2,1)S(1)}) custom-call(bf16[400,128]{1,0:T(8,128)(2,1)S(1)} %collective-permute-done.1.refs_0_, bf16[400,128]{1,0:T(8,128)(2,1)S(1)} %collective-permute-done.3.refs_1_, bf16[400,128]{1,0:T(8,128)(2,1)S(1)} %collective-permute-done.5.refs_2_, ...), custom_call_target="tpu_custom_call" | custom-call | flops 838860800 | bytes 2281472 | tf_op jit(solution)/shard_map/pallas_call | solution.py:38
  31.2 2.2 %shard_map.149 = (f32[400,256]{1,0:T(8,128)S(1)}, bf16[400,256]{1,0:T(8,128)(2,1)S(1)}, bf16[208,128]{1,0:T(8,128)(2,1)S(1)}, bf16[208,128]{1,0:T(8,128)(2,1)S(1...) custom-call(bf16[400,128]{1,0:T(8,128)(2,1)S(1)} %collective-permute-done.1.refs_0_, ...), custom_call_target="tpu_custom_call" | custom-call | flops 1048576000 | bytes 4743168 | tf_op jit(solution)/shard_map/pallas_call | solution.py:38
  33.5 0.9 %collective-permute-start.19 = (bf16[208,128]{1,0:T(8,128)(2,1)S(1)}, bf16[208,128]{1,0:T(8,128)(2,1)S(1)}, u32[]{:S(2)}, u32[]{:S(2)}) collective-permute-start(bf16[208,128]{1,0:T(8,128)(2,1)S(1)} %get-tuple-element.36), channel_id=1, source_target_pairs={{0,2},{1,3},{2,0},{3,1},{4,6},{5,7},{6,4},{7,5},{8,10},{9,11},{10,... | collective-permute-start | bytes 159752 | tf_op jit(solution)/shard_map/ppermute | solution.py:199
  34.4 0.9 %collective-permute-start.20 = (bf16[208,128]{1,0:T(8,128)(2,1)S(1)}, bf16[208,128]{1,0:T(8,128)(2,1)S(1)}, u32[]{:S(2)}, u32[]{:S(2)}) collective-permute-start(bf16[208,128]{1,0:T(8,128)(2,1)S(1)} %get-tuple-element.37), channel_id=1, source_target_pairs={{0,3},{1,2},{2,1},{3,0},{4,7},{5,6},{6,5},{7,4},{8,11},{9,10},{10,... | collective-permute-start | bytes 159752 | tf_op jit(solution)/shard_map/ppermute | solution.py:199
  35.4 2.7 %collective-permute-done.19 = bf16[208,128]{1,0:T(8,128)(2,1)S(1)} collective-permute-done((bf16[208,128]{1,0:T(8,128)(2,1)S(1)}, bf16[208,128]{1,0:T(8,128)(2,1)S(1)}, u32[]{:S(2)}, u32[]{:S(2)}) %collective-permute-start.19) | collective-permute-done | bytes 53280 | tf_op jit(solution)/shard_map/ppermute | solution.py:199
  38.1 0.5 collective-permute-done.20
  38.6 2.0 %collective-permute-start.21 = (bf16[208,128]{1,0:T(8,128)(2,1)S(1)}, bf16[208,128]{1,0:T(8,128)(2,1)S(1)}, u32[]{:S(2)}, u32[]{:S(2)}) collective-permute-start(bf16[208,128]{1,0:T(8,128)(2,1)S(1)} %add_convert_fusion.4), channel_id=1, source_target_pairs={{0,8},{4,12},{8,0},{12,4},{16,24},{20,28},{24,16},{28,20},{1,9},{5... | collective-permute-start | bytes 159752 | tf_op jit(solution)/shard_map/ppermute | solution.py:196
  40.6 2.2 %collective-permute-done.21 = bf16[208,128]{1,0:T(8,128)(2,1)S(1)} collective-permute-done((bf16[208,128]{1,0:T(8,128)(2,1)S(1)}, bf16[208,128]{1,0:T(8,128)(2,1)S(1)}, u32[]{:S(2)}, u32[]{:S(2)}) %collective-permute-start.21) | collective-permute-done | bytes 53280 | tf_op jit(solution)/shard_map/ppermute | solution.py:196
  42.8 2.9 %collective-permute-start.22 = (bf16[208,128]{1,0:T(8,128)(2,1)S(1)}, bf16[208,128]{1,0:T(8,128)(2,1)S(1)}, u32[]{:S(2)}, u32[]{:S(2)}) collective-permute-start(bf16[208,128]{1,0:T(8,128)(2,1)S(1)} %add_convert_fusion.3), channel_id=1, source_target_pairs={{0,16},{4,20},{8,24},{12,28},{16,0},{20,4},{24,8},{28,12},{1,17},{... | collective-permute-start | bytes 159752 | tf_op jit(solution)/shard_map/ppermute | solution.py:196
  45.7 1.5 %collective-permute-start.13 = (bf16[400,256]{1,0:T(8,128)(2,1)S(1)}, bf16[400,256]{1,0:T(8,128)(2,1)S(1)}, u32[]{:S(2)}, u32[]{:S(2)}) collective-permute-start(bf16[400,256]{1,0:T(8,128)(2,1)S(1)} %get-tuple-element.32), channel_id=1, source_target_pairs={{0,4},{4,0},{8,12},{12,8},{16,20},{20,16},{24,28},{28,24},{1,5},{5... | collective-permute-start | bytes 614408 | tf_op jit(solution)/shard_map/ppermute | solution.py:196
  47.2 0.5 collective-permute-start.14
  47.7 0.5 collective-permute-start.12
  48.2 1.6 %collective-permute-start.23 = (bf16[208,128]{1,0:T(8,128)(2,1)S(1)}, bf16[208,128]{1,0:T(8,128)(2,1)S(1)}, u32[]{:S(2)}, u32[]{:S(2)}) collective-permute-start(bf16[208,128]{1,0:T(8,128)(2,1)S(1)} %add_convert_fusion.2), channel_id=1, source_target_pairs={{0,4},{4,0},{8,12},{12,8},{16,20},{20,16},{24,28},{28,24},{1,5},{5... | collective-permute-start | bytes 159752 | tf_op jit(solution)/shard_map/ppermute | solution.py:196
  49.9 1.0 %collective-permute-start.11 = (bf16[400,128]{1,0:T(8,128)(2,1)S(1)}, bf16[400,128]{1,0:T(8,128)(2,1)S(1)}, u32[]{:S(2)}, u32[]{:S(2)}) collective-permute-start(bf16[400,128]{1,0:T(8,128)(2,1)S(1)} %slice.72), channel_id=1, source_target_pairs={{0,2},{1,3},{2,0},{3,1},{4,6},{5,7},{6,4},{7,5},{8,10},{9,11},{10,... | collective-permute-start | bytes 307208 | tf_op jit(solution)/shard_map/ppermute | solution.py:199
  50.9 2.8 %collective-permute-done.13 = bf16[400,256]{1,0:T(8,128)(2,1)S(1)} collective-permute-done((bf16[400,256]{1,0:T(8,128)(2,1)S(1)}, bf16[400,256]{1,0:T(8,128)(2,1)S(1)}, u32[]{:S(2)}, u32[]{:S(2)}) %collective-permute-start.13) | collective-permute-done | bytes 204832 | tf_op jit(solution)/shard_map/ppermute | solution.py:196
  53.7 2.7 %collective-permute-done.14 = bf16[400,256]{1,0:T(8,128)(2,1)S(1)} collective-permute-done((bf16[400,256]{1,0:T(8,128)(2,1)S(1)}, bf16[400,256]{1,0:T(8,128)(2,1)S(1)}, u32[]{:S(2)}, u32[]{:S(2)}) %collective-permute-start.14) | collective-permute-done | bytes 204832 | tf_op jit(solution)/shard_map/ppermute | solution.py:196
  57.0 0.9 %collective-permute-start.25 = (bf16[208,128]{1,0:T(8,128)(2,1)S(1)}, bf16[208,128]{1,0:T(8,128)(2,1)S(1)}, u32[]{:S(2)}, u32[]{:S(2)}) collective-permute-start(bf16[208,128]{1,0:T(8,128)(2,1)S(1)} %add_convert_fusion.1.refs_0_), channel_id=1, source_target_pairs={{0,2},{1,3},{2,0},{3,1},{4,6},{5,7},{6,4},{7,5},{8,10},{9,11},{10,... | collective-permute-start | bytes 159752 | tf_op jit(solution)/shard_map/ppermute | solution.py:199
  58.0 0.9 %collective-permute-start.24 = (bf16[208,128]{1,0:T(8,128)(2,1)S(1)}, bf16[208,128]{1,0:T(8,128)(2,1)S(1)}, u32[]{:S(2)}, u32[]{:S(2)}) collective-permute-start(bf16[208,128]{1,0:T(8,128)(2,1)S(1)} %add_convert_fusion.1.refs_0_), channel_id=1, source_target_pairs={{0,1},{1,0},{2,3},{3,2},{4,5},{5,4},{6,7},{7,6},{8,9},{9,8},{10,11... | collective-permute-start | bytes 159752 | tf_op jit(solution)/shard_map/ppermute | solution.py:199
  58.9 1.7 %collective-permute-done.26.refs_3_ = bf16[208,128]{1,0:T(8,128)(2,1)S(1)} collective-permute-done((bf16[208,128]{1,0:T(8,128)(2,1)S(1)}, bf16[208,128]{1,0:T(8,128)(2,1)S(1)}, u32[]{:S(2)}, u32[]{:S(2)}) %collective-permute-start.26) | collective-permute-done | bytes 53280 | tf_op jit(solution)/shard_map/ppermute | solution.py:199
  60.6 1.7 %collective-permute-start.17 = (bf16[400,128]{1,0:T(8,128)(2,1)S(1)}, bf16[400,128]{1,0:T(8,128)(2,1)S(1)}, u32[]{:S(2)}, u32[]{:S(2)}) collective-permute-start(bf16[400,128]{1,0:T(8,128)(2,1)S(1)} %slice.71), channel_id=1, source_target_pairs={{0,8},{4,12},{8,0},{12,4},{16,24},{20,28},{24,16},{28,20},{1,9},{5... | collective-permute-start | bytes 307208 | tf_op jit(solution)/shard_map/ppermute | solution.py:196
  62.3 1.0 %collective-permute-start.15 = (bf16[400,128]{1,0:T(8,128)(2,1)S(1)}, bf16[400,128]{1,0:T(8,128)(2,1)S(1)}, u32[]{:S(2)}, u32[]{:S(2)}) collective-permute-start(bf16[400,128]{1,0:T(8,128)(2,1)S(1)} %get-tuple-element.44), channel_id=1, source_target_pairs={{0,24},{4,28},{8,16},{12,20},{16,8},{20,12},{24,0},{28,4},{1,25},{... | collective-permute-start | bytes 307208 | tf_op jit(solution)/shard_map/ppermute | solution.py:196
  63.3 1.6 %collective-permute-start.16 = (bf16[400,128]{1,0:T(8,128)(2,1)S(1)}, bf16[400,128]{1,0:T(8,128)(2,1)S(1)}, u32[]{:S(2)}, u32[]{:S(2)}) collective-permute-start(bf16[400,128]{1,0:T(8,128)(2,1)S(1)} %get-tuple-element.45), channel_id=1, source_target_pairs={{0,16},{4,20},{8,24},{12,28},{16,0},{20,4},{24,8},{28,12},{1,17},{... | collective-permute-start | bytes 307208 | tf_op jit(solution)/shard_map/ppermute | solution.py:196
  65.0 0.9 %shard_map.150 = (f32[400,256]{1,0:T(8,128)}, f32[1,256]{1,0:T(1,128)}) custom-call(bf16[208,128]{1,0:T(8,128)(2,1)S(1)} %add_convert_fusion.1.refs_0_, bf16[208,128]{1,0:T(8,128)(2,1)S(1)} %collective-permute-done.24.refs_1_, bf16[208,128]{1,0:T(8,128)(2,1)S(1)} %collective-permute-done.25.refs_2_, bf16[208,128]{1,0:T(8,128)(2,1)S(1)} %collective-permute-done.26.refs_3_, ...), custom_call_target="tpu_custom_call" | custom-call | flops 819200 | bytes 623616 | tf_op jit(solution)/shard_map/pallas_call | solution.py:38
  65.9 3.6 %collective-permute-done.15 = bf16[400,128]{1,0:T(8,128)(2,1)S(1)} collective-permute-done((bf16[400,128]{1,0:T(8,128)(2,1)S(1)}, bf16[400,128]{1,0:T(8,128)(2,1)S(1)}, u32[]{:S(2)}, u32[]{:S(2)}) %collective-permute-start.15) | collective-permute-done | bytes 102432 | tf_op jit(solution)/shard_map/ppermute | solution.py:196
  69.6 4.8 %collective-permute-done.16 = bf16[400,128]{1,0:T(8,128)(2,1)S(1)} collective-permute-done((bf16[400,128]{1,0:T(8,128)(2,1)S(1)}, bf16[400,128]{1,0:T(8,128)(2,1)S(1)}, u32[]{:S(2)}, u32[]{:S(2)}) %collective-permute-start.16) | collective-permute-done | bytes 102432 | tf_op jit(solution)/shard_map/ppermute | solution.py:196
  74.4 0.5 rsqrt_multiply_fusion
  74.9 0.5 bitcast_add_fusion
  75.5 0.7 fusion.3
  76.2 0.8 fusion.2
  (48 shorter events, 1.9 us)
Async XLA Ops:
  0.6 21.5 %copy-start.2 = (s32[1,1,1024]{2,1,0:T(1,128)S(1)}, s32[1,1,1024]{2,1,0:T(1,128)}, u32[]{:S(2)}) copy-start(s32[1,1,1024]{2,1,0:T(1,128)} %param.18) | copy-start | bytes 12292
  0.6 21.5 %copy-start = (f32[256,400]{0,1:T(8,128)S(1)}, f32[256,400]{0,1:T(8,128)}, u32[]{:S(2)}) copy-start(f32[256,400]{0,1:T(8,128)} %param.14) | copy-start | bytes 1228804
  1.6 16.3 %collective-permute-start.6 = (bf16[400,128]{1,0:T(8,128)(2,1)S(1)}, bf16[400,128]{1,0:T(8,128)(2,1)S(1)}, u32[]{:S(2)}, u32[]{:S(2)}) collective-permute-start(bf16[400,128]{1,0:T(8,128)(2,1)S(1)} %bitcast_convert_fusion.1), channel_id=1, source_target_pairs={{0,25},{1,26},{2,27},{3,24},{4,29},{5,30},{6,31},{7,28},{8,17},{9,... | collective-permute-start | bytes 307208 | tf_op jit(solution)/shard_map/ppermute | solution.py:206
  6.2 13.5 %collective-permute-start.4 = (bf16[400,128]{1,0:T(8,128)(2,1)S(1)}, bf16[400,128]{1,0:T(8,128)(2,1)S(1)}, u32[]{:S(2)}, u32[]{:S(2)}) collective-permute-start(bf16[400,128]{1,0:T(8,128)(2,1)S(1)} %bitcast_convert_fusion.1), channel_id=1, source_target_pairs={{0,17},{1,18},{2,19},{3,16},{4,21},{5,22},{6,23},{7,20},{8,25},{9,... | collective-permute-start | bytes 307208 | tf_op jit(solution)/shard_map/ppermute | solution.py:206
  6.8 13.2 %collective-permute-start.2 = (bf16[400,128]{1,0:T(8,128)(2,1)S(1)}, bf16[400,128]{1,0:T(8,128)(2,1)S(1)}, u32[]{:S(2)}, u32[]{:S(2)}) collective-permute-start(bf16[400,128]{1,0:T(8,128)(2,1)S(1)} %bitcast_convert_fusion.1), channel_id=1, source_target_pairs={{0,9},{1,10},{2,11},{3,8},{4,13},{5,14},{6,15},{7,12},{8,1},{9,2},... | collective-permute-start | bytes 307208 | tf_op jit(solution)/shard_map/ppermute | solution.py:206
  8.0 13.7 %collective-permute-start = (bf16[400,128]{1,0:T(8,128)(2,1)S(1)}, bf16[400,128]{1,0:T(8,128)(2,1)S(1)}, u32[]{:S(2)}, u32[]{:S(2)}) collective-permute-start(bf16[400,128]{1,0:T(8,128)(2,1)S(1)} %bitcast_convert_fusion.1), channel_id=1, source_target_pairs={{0,1},{1,2},{2,3},{3,0},{4,5},{5,6},{6,7},{7,4},{8,9},{9,10},{10,1... | collective-permute-start | bytes 307208 | tf_op jit(solution)/shard_map/ppermute | solution.py:206
  9.0 6.8 %collective-permute-start.8 = (bf16[400,128]{1,0:T(8,128)(2,1)S(1)}, bf16[400,128]{1,0:T(8,128)(2,1)S(1)}, u32[]{:S(2)}, u32[]{:S(2)}) collective-permute-start(bf16[400,128]{1,0:T(8,128)(2,1)S(1)} %bitcast_convert_fusion), channel_id=1, source_target_pairs={{0,2},{1,3},{2,0},{3,1},{4,6},{5,7},{6,4},{7,5},{8,10},{9,11},{10,... | collective-permute-start | bytes 307208 | tf_op jit(solution)/shard_map/ppermute | solution.py:199
  15.8 6.3 %collective-permute-start.9 = (bf16[400,256]{1,0:T(8,128)(2,1)S(1)}, bf16[400,256]{1,0:T(8,128)(2,1)S(1)}, u32[]{:S(2)}, u32[]{:S(2)}) collective-permute-start(bf16[400,256]{1,0:T(8,128)(2,1)S(1)} %pad_maximum_fusion.near_ref), channel_id=1, source_target_pairs={{0,1},{1,0},{2,3},{3,2},{4,5},{5,4},{6,7},{7,6},{8,9},{9,8},{10,11... | collective-permute-start | bytes 614408 | tf_op jit(solution)/shard_map/ppermute | solution.py:199
  17.0 6.0 %copy-start.1 = (f32[128,400]{0,1:T(8,128)S(1)}, f32[128,400]{0,1:T(8,128)}, u32[]{:S(2)}) copy-start(f32[128,400]{0,1:T(8,128)} %param.12) | copy-start | bytes 614404
  17.1 6.0 %copy-start.4 = (f32[128]{0:T(128)S(1)}, f32[128]{0:T(128)}, u32[]{:S(2)}) copy-start(f32[128]{0:T(128)} %param.13) | copy-start | bytes 1540
  18.0 6.9 %collective-permute-start.7 = (bf16[400,128]{1,0:T(8,128)(2,1)S(1)}, bf16[400,128]{1,0:T(8,128)(2,1)S(1)}, u32[]{:S(2)}, u32[]{:S(2)}) collective-permute-start(bf16[400,128]{1,0:T(8,128)(2,1)S(1)} %collective-permute-done.6.refs_3_), channel_id=1, source_target_pairs={{0,4},{4,0},{8,12},{12,8},{16,20},{20,16},{24,28},{28,24},{1,5},{5... | collective-permute-start | bytes 307208 | tf_op jit(solution)/shard_map/ppermute | solution.py:196
  19.7 6.3 %collective-permute-start.5 = (bf16[400,128]{1,0:T(8,128)(2,1)S(1)}, bf16[400,128]{1,0:T(8,128)(2,1)S(1)}, u32[]{:S(2)}, u32[]{:S(2)}) collective-permute-start(bf16[400,128]{1,0:T(8,128)(2,1)S(1)} %collective-permute-done.4.refs_2_), channel_id=1, source_target_pairs={{0,4},{4,0},{8,12},{12,8},{16,20},{20,16},{24,28},{28,24},{1,5},{5... | collective-permute-start | bytes 307208 | tf_op jit(solution)/shard_map/ppermute | solution.py:196
  20.1 8.1 %collective-permute-start.3 = (bf16[400,128]{1,0:T(8,128)(2,1)S(1)}, bf16[400,128]{1,0:T(8,128)(2,1)S(1)}, u32[]{:S(2)}, u32[]{:S(2)}) collective-permute-start(bf16[400,128]{1,0:T(8,128)(2,1)S(1)} %collective-permute-done.2.refs_1_), channel_id=1, source_target_pairs={{0,4},{4,0},{8,12},{12,8},{16,20},{20,16},{24,28},{28,24},{1,5},{5... | collective-permute-start | bytes 307208 | tf_op jit(solution)/shard_map/ppermute | solution.py:196
  21.7 7.9 %collective-permute-start.1 = (bf16[400,128]{1,0:T(8,128)(2,1)S(1)}, bf16[400,128]{1,0:T(8,128)(2,1)S(1)}, u32[]{:S(2)}, u32[]{:S(2)}) collective-permute-start(bf16[400,128]{1,0:T(8,128)(2,1)S(1)} %collective-permute-done.refs_0_), channel_id=1, source_target_pairs={{0,4},{4,0},{8,12},{12,8},{16,20},{20,16},{24,28},{28,24},{1,5},{5... | collective-permute-start | bytes 307208 | tf_op jit(solution)/shard_map/ppermute | solution.py:196
  33.4 1.9 %collective-permute-start.18 = (bf16[208,128]{1,0:T(8,128)(2,1)S(1)}, bf16[208,128]{1,0:T(8,128)(2,1)S(1)}, u32[]{:S(2)}, u32[]{:S(2)}) collective-permute-start(bf16[208,128]{1,0:T(8,128)(2,1)S(1)} %get-tuple-element.35), channel_id=1, source_target_pairs={{0,1},{1,0},{2,3},{3,2},{4,5},{5,4},{6,7},{7,6},{8,9},{9,8},{10,11... | collective-permute-start | bytes 159752 | tf_op jit(solution)/shard_map/ppermute | solution.py:199
  33.5 4.6 %collective-permute-start.19 = (bf16[208,128]{1,0:T(8,128)(2,1)S(1)}, bf16[208,128]{1,0:T(8,128)(2,1)S(1)}, u32[]{:S(2)}, u32[]{:S(2)}) collective-permute-start(bf16[208,128]{1,0:T(8,128)(2,1)S(1)} %get-tuple-element.36), channel_id=1, source_target_pairs={{0,2},{1,3},{2,0},{3,1},{4,6},{5,7},{6,4},{7,5},{8,10},{9,11},{10,... | collective-permute-start | bytes 159752 | tf_op jit(solution)/shard_map/ppermute | solution.py:199
  34.4 4.1 %collective-permute-start.20 = (bf16[208,128]{1,0:T(8,128)(2,1)S(1)}, bf16[208,128]{1,0:T(8,128)(2,1)S(1)}, u32[]{:S(2)}, u32[]{:S(2)}) collective-permute-start(bf16[208,128]{1,0:T(8,128)(2,1)S(1)} %get-tuple-element.37), channel_id=1, source_target_pairs={{0,3},{1,2},{2,1},{3,0},{4,7},{5,6},{6,5},{7,4},{8,11},{9,10},{10,... | collective-permute-start | bytes 159752 | tf_op jit(solution)/shard_map/ppermute | solution.py:199
  38.6 4.2 %collective-permute-start.21 = (bf16[208,128]{1,0:T(8,128)(2,1)S(1)}, bf16[208,128]{1,0:T(8,128)(2,1)S(1)}, u32[]{:S(2)}, u32[]{:S(2)}) collective-permute-start(bf16[208,128]{1,0:T(8,128)(2,1)S(1)} %add_convert_fusion.4), channel_id=1, source_target_pairs={{0,8},{4,12},{8,0},{12,4},{16,24},{20,28},{24,16},{28,20},{1,9},{5... | collective-permute-start | bytes 159752 | tf_op jit(solution)/shard_map/ppermute | solution.py:196
  42.8 5.4 %collective-permute-start.22 = (bf16[208,128]{1,0:T(8,128)(2,1)S(1)}, bf16[208,128]{1,0:T(8,128)(2,1)S(1)}, u32[]{:S(2)}, u32[]{:S(2)}) collective-permute-start(bf16[208,128]{1,0:T(8,128)(2,1)S(1)} %add_convert_fusion.3), channel_id=1, source_target_pairs={{0,16},{4,20},{8,24},{12,28},{16,0},{20,4},{24,8},{28,12},{1,17},{... | collective-permute-start | bytes 159752 | tf_op jit(solution)/shard_map/ppermute | solution.py:196
  45.7 8.0 %collective-permute-start.13 = (bf16[400,256]{1,0:T(8,128)(2,1)S(1)}, bf16[400,256]{1,0:T(8,128)(2,1)S(1)}, u32[]{:S(2)}, u32[]{:S(2)}) collective-permute-start(bf16[400,256]{1,0:T(8,128)(2,1)S(1)} %get-tuple-element.32), channel_id=1, source_target_pairs={{0,4},{4,0},{8,12},{12,8},{16,20},{20,16},{24,28},{28,24},{1,5},{5... | collective-permute-start | bytes 614408 | tf_op jit(solution)/shard_map/ppermute | solution.py:196
  47.2 9.2 %collective-permute-start.14 = (bf16[400,256]{1,0:T(8,128)(2,1)S(1)}, bf16[400,256]{1,0:T(8,128)(2,1)S(1)}, u32[]{:S(2)}, u32[]{:S(2)}) collective-permute-start(bf16[400,256]{1,0:T(8,128)(2,1)S(1)} %get-tuple-element.33), channel_id=1, source_target_pairs={{0,4},{4,0},{8,12},{12,8},{16,20},{20,16},{24,28},{28,24},{1,5},{5... | collective-permute-start | bytes 614408 | tf_op jit(solution)/shard_map/ppermute | solution.py:196
  47.7 2.1 %collective-permute-start.10 = (bf16[400,256]{1,0:T(8,128)(2,1)S(1)}, bf16[400,256]{1,0:T(8,128)(2,1)S(1)}, u32[]{:S(2)}, u32[]{:S(2)}) collective-permute-start(bf16[400,256]{1,0:T(8,128)(2,1)S(1)} %get-tuple-element.29), channel_id=1, source_target_pairs={{0,1},{1,0},{2,3},{3,2},{4,5},{5,4},{6,7},{7,6},{8,9},{9,8},{10,11... | collective-permute-start | bytes 614408 | tf_op jit(solution)/shard_map/ppermute | solution.py:199
  47.7 27.2 %collective-permute-start.12 = (f32[408,128]{1,0:T(8,128)S(1)}, f32[408,128]{1,0:T(8,128)S(1)}, u32[]{:S(2)}, u32[]{:S(2)}) collective-permute-start(f32[408,128]{1,0:T(8,128)S(1)} %get-tuple-element.30), channel_id=1, source_target_pairs={{0,1},{1,2},{2,3},{3,0},{4,5},{5,6},{6,7},{7,4},{8,9},{9,10},{10,1... | collective-permute-start | bytes 626696 | tf_op jit(solution)/shard_map/ppermute | solution.py:206
  48.2 8.7 %collective-permute-start.23 = (bf16[208,128]{1,0:T(8,128)(2,1)S(1)}, bf16[208,128]{1,0:T(8,128)(2,1)S(1)}, u32[]{:S(2)}, u32[]{:S(2)}) collective-permute-start(bf16[208,128]{1,0:T(8,128)(2,1)S(1)} %add_convert_fusion.2), channel_id=1, source_target_pairs={{0,4},{4,0},{8,12},{12,8},{16,20},{20,16},{24,28},{28,24},{1,5},{5... | collective-permute-start | bytes 159752 | tf_op jit(solution)/shard_map/ppermute | solution.py:196
  49.9 15.1 %copy-start.3 = (f32[256]{0:T(256)S(1)}, f32[256]{0:T(256)}, u32[]{:S(2)}) copy-start(f32[256]{0:T(256)} %param.15) | copy-start | bytes 3076
  49.9 16.0 %collective-permute-start.11 = (bf16[400,128]{1,0:T(8,128)(2,1)S(1)}, bf16[400,128]{1,0:T(8,128)(2,1)S(1)}, u32[]{:S(2)}, u32[]{:S(2)}) collective-permute-start(bf16[400,128]{1,0:T(8,128)(2,1)S(1)} %slice.72), channel_id=1, source_target_pairs={{0,2},{1,3},{2,0},{3,1},{4,6},{5,7},{6,4},{7,5},{8,10},{9,11},{10,... | collective-permute-start | bytes 307208 | tf_op jit(solution)/shard_map/ppermute | solution.py:199
  56.4 18.0 %copy-start.6 = (f32[128]{0:T(128)S(1)}, f32[128]{0:T(128)}, u32[]{:S(2)}) copy-start(f32[128]{0:T(128)} %param.11) | copy-start | bytes 1540
  56.4 19.1 %copy-start.5 = (f32[128,400]{0,1:T(8,128)S(1)}, f32[128,400]{0,1:T(8,128)}, u32[]{:S(2)}) copy-start(f32[128,400]{0,1:T(8,128)} %param.10) | copy-start | bytes 614404
  57.0 3.6 %collective-permute-start.26 = (bf16[208,128]{1,0:T(8,128)(2,1)S(1)}, bf16[208,128]{1,0:T(8,128)(2,1)S(1)}, u32[]{:S(2)}, u32[]{:S(2)}) collective-permute-start(bf16[208,128]{1,0:T(8,128)(2,1)S(1)} %add_convert_fusion.1.refs_0_), channel_id=1, source_target_pairs={{0,3},{1,2},{2,1},{3,0},{4,7},{5,6},{6,5},{7,4},{8,11},{9,10},{10,... | collective-permute-start | bytes 159752 | tf_op jit(solution)/shard_map/ppermute | solution.py:199
  57.0 5.3 %collective-permute-start.25 = (bf16[208,128]{1,0:T(8,128)(2,1)S(1)}, bf16[208,128]{1,0:T(8,128)(2,1)S(1)}, u32[]{:S(2)}, u32[]{:S(2)}) collective-permute-start(bf16[208,128]{1,0:T(8,128)(2,1)S(1)} %add_convert_fusion.1.refs_0_), channel_id=1, source_target_pairs={{0,2},{1,3},{2,0},{3,1},{4,6},{5,7},{6,4},{7,5},{8,10},{9,11},{10,... | collective-permute-start | bytes 159752 | tf_op jit(solution)/shard_map/ppermute | solution.py:199
  58.0 5.3 %collective-permute-start.24 = (bf16[208,128]{1,0:T(8,128)(2,1)S(1)}, bf16[208,128]{1,0:T(8,128)(2,1)S(1)}, u32[]{:S(2)}, u32[]{:S(2)}) collective-permute-start(bf16[208,128]{1,0:T(8,128)(2,1)S(1)} %add_convert_fusion.1.refs_0_), channel_id=1, source_target_pairs={{0,1},{1,0},{2,3},{3,2},{4,5},{5,4},{6,7},{7,6},{8,9},{9,8},{10,11... | collective-permute-start | bytes 159752 | tf_op jit(solution)/shard_map/ppermute | solution.py:199
  60.6 5.4 %collective-permute-start.17 = (bf16[400,128]{1,0:T(8,128)(2,1)S(1)}, bf16[400,128]{1,0:T(8,128)(2,1)S(1)}, u32[]{:S(2)}, u32[]{:S(2)}) collective-permute-start(bf16[400,128]{1,0:T(8,128)(2,1)S(1)} %slice.71), channel_id=1, source_target_pairs={{0,8},{4,12},{8,0},{12,4},{16,24},{20,28},{24,16},{28,20},{1,9},{5... | collective-permute-start | bytes 307208 | tf_op jit(solution)/shard_map/ppermute | solution.py:196
  62.3 7.2 %collective-permute-start.15 = (bf16[400,128]{1,0:T(8,128)(2,1)S(1)}, bf16[400,128]{1,0:T(8,128)(2,1)S(1)}, u32[]{:S(2)}, u32[]{:S(2)}) collective-permute-start(bf16[400,128]{1,0:T(8,128)(2,1)S(1)} %get-tuple-element.44), channel_id=1, source_target_pairs={{0,24},{4,28},{8,16},{12,20},{16,8},{20,12},{24,0},{28,4},{1,25},{... | collective-permute-start | bytes 307208 | tf_op jit(solution)/shard_map/ppermute | solution.py:196
  63.3 11.0 %collective-permute-start.16 = (bf16[400,128]{1,0:T(8,128)(2,1)S(1)}, bf16[400,128]{1,0:T(8,128)(2,1)S(1)}, u32[]{:S(2)}, u32[]{:S(2)}) collective-permute-start(bf16[400,128]{1,0:T(8,128)(2,1)S(1)} %get-tuple-element.45), channel_id=1, source_target_pairs={{0,16},{4,20},{8,24},{12,28},{16,0},{20,4},{24,8},{28,12},{1,17},{... | collective-permute-start | bytes 307208 | tf_op jit(solution)/shard_map/ppermute | solution.py:196

commit v4 on v3

--- a/solution.py
+++ b/solution.py
@@ -28,15 +28,24 @@
     return most if size % most == 0 else size
 
 
-def call(body, out_shape, flops, scratch=(), here=None):
+def call(body, out_shape, flops, scratch=(), here=None, after=()):
     def run(*args):
         moved = sum(a.size * a.dtype.itemsize for a in args)
         specs = [pl.BlockSpec(memory_space=pltpu.VMEM)] * len(args)
         if here is not None:
             specs.append(pl.BlockSpec(memory_space=pltpu.SMEM))
             args = (*args, here)
+        inner = body
+        if after:
+            used = len(args)
+
+            def inner(*refs):
+                body(*refs[:used], *refs[used + len(after):])
+
+            specs += [pl.BlockSpec(memory_space=pl.ANY)] * len(after)
+            args = (*args, *after)
         return pl.pallas_call(
-            body,
+            inner,
             out_shape=out_shape,
             in_specs=specs,
             scratch_shapes=list(scratch),
@@ -180,9 +189,42 @@
         new_ref[:, cols] = table_ref[:, cols] - g * (LEARN_RATE * lax.rsqrt(state))
 
 
-def adagrad(table, state, grad):
-    state_new = state + jnp.mean(grad * grad, axis=0)
-    return table - LEARN_RATE * grad * lax.rsqrt(state_new)[None, :], state_new
+def cast_body(in_ref, out_ref):
+    out_ref[...] = in_ref[...].astype(BF)
+
+
+def high_body(blocks, pieces, *refs):
+    near_ref, got_ref, refs = refs[0], refs[1], refs[2:]
+    piece_refs, refs = refs[:pieces], refs[pieces:]
+    block_refs, mine_ref = refs[:blocks], refs[blocks]
+    base = near_ref.shape[1] - blocks * LANES
+    for k, ref in enumerate(block_refs):
+        cols = slice(k * LANES, (k + 1) * LANES)
+        ref[...] = (near_ref[:, base + k * LANES:base + (k + 1) * LANES] + got_ref[:, cols].astype(F32)).astype(BF)
+    parts = [ref[...].astype(F32) for ref in piece_refs]
+    while len(parts) > 1:
+        parts = [parts[i] + parts[i + 1] for i in range(0, len(parts), 2)]
+    mine_ref[...] = parts[0].astype(BF)
+
+
+def low_body(blocks, near_ref, got_ref, piece_ref, other_ref, *refs):
+    block_refs, (own_ref, mine_ref) = refs[:blocks - 1], refs[blocks - 1:]
+    own_ref[...] = near_ref[:, :LANES] + got_ref[:, :LANES].astype(F32)
+    for k, ref in enumerate(block_refs):
+        cols = slice((k + 1) * LANES, (k + 2) * LANES)
+        ref[...] = (near_ref[:, cols] + got_ref[:, cols].astype(F32)).astype(BF)
+    mine_ref[...] = (piece_ref[...].astype(F32) + other_ref[...].astype(F32)).astype(BF)
+
+
+def update_body(parts, own_ref, *refs):
+    part_refs, (table_ref, state_ref, new_ref, state_new_ref) = refs[:parts], refs[parts:]
+    g = own_ref[...]
+    for ref in part_refs:
+        g = g + ref[...].astype(F32)
+    width = g.shape[0]
+    state = state_ref[:1, :] + jnp.sum(g * g, axis=0, keepdims=True) * (1.0 / width)
+    state_new_ref[...] = state
+    new_ref[...] = table_ref[:width, :] - g * (LEARN_RATE * lax.rsqrt(state))
 
 
 def build(mesh):
@@ -224,13 +266,18 @@
         n_rows = n_left * rows
         half = outer * rows
 
-        right_bf = right_t.astype(BF)
-        near = {k: next_column(right_bf, 2 * k) for k in range(outer - 1, -1, -1)}
-        left_bf = left_t.astype(BF)
+        one_block = shape(width, rows, dtype=BF)
+        right_bf = call(cast_body, one_block, width * rows)(right_t)
+        near = {k: next_column(right_bf, 2 * k) for k in range(outer - 1, 0, -1)}
+        other = {0: next_column(right_bf, 1)}
+        near[0] = next_column(right_bf, 0)
+        other[1] = swap_left(near[1], 1)
+        left_bf = call(cast_body, one_block, width * rows, after=(near[1], other[0]))(left_t)
         half_left = [left_bf] + [swap_right(left_bf, 2 * k) for k in range(1, far_right)]
         half_left = jnp.concatenate(half_left, axis=1)
         sibling_left = swap_right(half_left, 1)
-        other = {k: swap_left(near[k], 1) for k in range(outer)}
+        for k in range(2, outer):
+            other[k] = swap_left(near[k], 1)
         near = [near[k] for k in range(outer)]
         other = [other[k] for k in range(outer)]
 
@@ -275,38 +322,40 @@
             me,
         )(*other, m, qg_near, s, o, source, kind)
 
-        got = [pieces[0]] + [swap_right(pieces[k], k) for k in range(1, n_right)]
-        got = [g.astype(F32) for g in got]
-        while len(got) > 1:
-            got = [got[i] + got[i + 1] for i in range(0, len(got), 2)]
-        mine = got[0].astype(BF)
-        bit = 2
-        bits = []
+        pieces = [pieces[0]] + [swap_right(pieces[k], k) for k in range(1, n_right)]
+        some = outer // 2
+        *high, mine = call(
+            functools.partial(high_body, some, n_right), (one_block,) * some + (piece,), width * half
+        )(right_near, got_hi, *pieces)
+        arrived = {some + k: swap_left(block, 2 * (some + k)) for k, block in enumerate(high)}
+        *low, own, mine = call(
+            functools.partial(low_body, some),
+            (one_block,) * (some - 1) + (shape(width, rows), piece),
+            width * half,
+        )(right_near, got_lo, mine, swap_left(mine, 2))
+        for k, block in enumerate(low):
+            arrived[k + 1] = swap_left(block, 2 * (k + 1))
+        bit = 4
         while bit < n_left:
-            bits.append(bit)
+            mine = (mine.astype(F32) + swap_left(mine, bit).astype(F32)).astype(BF)
             bit *= 2
-        for bit in bits + [1]:
-            mine = (mine.astype(F32) + swap_left(mine, bit).astype(F32)).astype(BF)
+        mine = (mine.astype(F32) + swap_left(mine, 1).astype(F32)).astype(BF)
         pieces = [mine] + [swap_right(mine, k) for k in range(1, n_right)]
-
-        cut = half // 2
-        hi = right_near[:, cut:] + got_hi.astype(F32)
-        lo = right_near[:, :cut] + got_lo.astype(F32)
-        hi_bf, lo_bf = hi.astype(BF), lo.astype(BF)
-        right_sum = lo[:, :rows]
-        for k in range(outer - 1, 0, -1):
-            at = k * rows
-            block = lo_bf[:, at:at + rows] if at < cut else hi_bf[:, at - cut:at - cut + rows]
-            right_sum = right_sum + swap_left(block, 2 * k).astype(F32)
 
         left_near = left_near + swap_right(left_far, 1).astype(F32)
         left_bf_sum = left_near.astype(BF)
-        left_sum = left_near[:, :rows]
-        for k in range(1, far_right):
-            left_sum = left_sum + swap_right(left_bf_sum[:, k * rows:(k + 1) * rows], 2 * k).astype(F32)
-
-        left_new, left_state_new = adagrad(left_t, left_state, left_sum)
-        right_new, right_state_new = adagrad(moved[:width], moved[width], right_sum)
+        left_got = [
+            swap_right(left_bf_sum[:, k * rows:(k + 1) * rows], 2 * k) for k in range(1, far_right)
+        ]
+
+        def update(own, got, table, state):
+            return call(
+                functools.partial(update_body, len(got)), (shape(width, rows), shape(1, rows)), 8 * width * rows
+            )(own, *got, table, state)
+
+        left_new, left_state_new = update(left_near[:, :rows], left_got, left_t, left_state[None, :])
+        right_got = [arrived[k] for k in range(1, outer)]
+        right_new, right_state_new = update(own, right_got, moved, moved[width:])
         relation_new, relation_state_new = call(
             functools.partial(relation_body, n_right),
             (shape(width, nrel), shape(1, nrel)),
@@ -315,7 +364,8 @@
             me,
         )(*pieces, relation_t, relation_state[None, :])
         return (
-            left_new.T, left_state_new, right_new.T, right_state_new, relation_new.T, relation_state_new.reshape(-1),
+            left_new.T, left_state_new.reshape(-1), right_new.T, right_state_new.reshape(-1),
+            relation_new.T, relation_state_new.reshape(-1),
         )
 
     return per_device

time: 77.2 us -> 62.8 us (0.81)
  waiting for transfers between devices: 29.7 us -> 17 us
  other arithmetic: 7.14 us -> 2.39 us
  local copies, waits for them, and re-layouts: 0.08 us -> 1.93 us
  Pallas kernels: 8.27 us -> 10.1 us
    ppermute x12 -> x11, waiting for transfers between devices: 21.3 us -> 8.05 us  [swap_left(): return lax.ppermute(value, 'left', [(i, i ^ by) for i in range(n_left)])]
    ppermute x5 -> x6, waiting for transfers between devices: 0.01 us -> 4.38 us  [next_column(): return lax.ppermute(value, ('left', 'right'), perm)]
    ppermute x10, waiting for transfers between devices: 8.3 us -> 4.54 us  [swap_right(): return lax.ppermute(value, 'right', [(i, i ^ by) for i in range(n_right)])]
    convert_element_type x4 -> x1, other arithmetic: 2.08 us -> 0.02 us  [per_device(): mine = (mine.astype(F32) + swap_left(mine, 1).astype(F32)).astype(BF)]
    ppermute x10, starting transfers between devices: 7.15 us -> 5.11 us  [swap_right(): return lax.ppermute(value, 'right', [(i, i ^ by) for i in range(n_right)])]
    unnamed x14 -> x18, local copies, waits for them, and re-layouts: 0.03 us -> 1.89 us
    pallas_call x6 -> x12, Pallas kernels: 8.27 us -> 10.1 us  [run(): pl.pallas_call(inner, out_shape=out_shape, in_specs=specs, scratch_shapes...]
    ppermute x5 -> x6, starting transfers between devices: 6.89 us -> 8.6 us  [next_column(): return lax.ppermute(value, ('left', 'right'), perm)]
  transfers between devices with their start and end apart: 27 -> 27, of which waited for: 13 -> 10; matrix products, arithmetic and copies ran while one was open for 5% -> 4% of each run, Pallas kernels for 6% -> 15%
where the time goes in v4:
time: 62.8 us; the launch traced here: 62.5 us
  starting transfers between devices  30.3 us (48%)
  waiting for transfers between devices  17 us (27%)
  Pallas kernels  10.1 us (16%)
  other arithmetic  2.39 us (4%)
  local copies, waits for them, and re-layouts  1.93 us (3%)
  between operations  0.85 us (1%)
    ppermute x11, starting transfers between devices, swap_left(): return lax.ppermute(value, 'left', [(i, i ^ by) for i in range(n_left)])  16.6 us
    pallas_call x12, Pallas kernels, run(): pl.pallas_call(inner, out_shape=out_shape, in_specs=specs, scratch_shapes...  10.1 us
    ppermute x6, starting transfers between devices, next_column(): return lax.ppermute(value, ('left', 'right'), perm)  8.6 us
    ppermute x11, waiting for transfers between devices, swap_left(): return lax.ppermute(value, 'left', [(i, i ^ by) for i in range(n_left)])  8.05 us
    ppermute x10, starting transfers between devices, swap_right(): return lax.ppermute(value, 'right', [(i, i ^ by) for i in range(n_right)])  5.11 us
    ppermute x10, waiting for transfers between devices, swap_right(): return lax.ppermute(value, 'right', [(i, i ^ by) for i in range(n_right)])  4.54 us
    ppermute x6, waiting for transfers between devices, next_column(): return lax.ppermute(value, ('left', 'right'), perm)  4.38 us
    add x3, other arithmetic, local(): return (block % 2 * half + block // 2) * rows + ids % rows  2.28 us
  transfers between devices with their start and end apart: 27, of which 10 were waited for; matrix products, arithmetic and copies ran while one was open for 4% of the time, Pallas kernels for 15%

profile of v4, /device:TPU:0, one launch (start us, length us, event | category | flops | bytes accessed | tf_op | source)
XLA Modules:
  0.0 62.5 jit_solution(10853638922604271465)
XLA Ops:
  0.6 0.9 %copy-done.3 = f32[128,400]{0,1:T(8,128)S(1)} copy-done((f32[128,400]{0,1:T(8,128)S(1)}, f32[128,400]{0,1:T(8,128)}, u32[]{:S(2)}) %copy-start.3) | copy-done | bytes 204824
  1.6 0.5 collective-permute-start.9
  2.1 5.8 %collective-permute-start.5 = (bf16[400,128]{1,0:T(8,128)(2,1)S(1)}, bf16[400,128]{1,0:T(8,128)(2,1)S(1)}, u32[]{:S(2)}, u32[]{:S(2)}) collective-permute-start(bf16[400,128]{1,0:T(8,128)(2,1)S(1)} %shard_map.145), channel_id=1, source_target_pairs={{0,25},{1,26},{2,27},{3,24},{4,29},{5,30},{6,31},{7,28},{8,17},{9,... | collective-permute-start | bytes 307208 | tf_op jit(solution)/shard_map/ppermute | solution.py:248
  7.9 0.1 collective-permute-start.1
  8.0 1.6 %collective-permute-start = (bf16[400,128]{1,0:T(8,128)(2,1)S(1)}, bf16[400,128]{1,0:T(8,128)(2,1)S(1)}, u32[]{:S(2)}, u32[]{:S(2)}) collective-permute-start(bf16[400,128]{1,0:T(8,128)(2,1)S(1)} %shard_map.145), channel_id=1, source_target_pairs={{0,5},{1,6},{2,7},{3,4},{4,1},{5,2},{6,3},{7,0},{8,13},{9,14},{10,... | collective-permute-start | bytes 307208 | tf_op jit(solution)/shard_map/ppermute | solution.py:248
  9.7 0.8 %fusion.2.ids_ref = s32[2,1024]{1,0:T(2,128)S(1)} fusion(s32[1,1,2,1024]{3,2,1,0:T(2,128)} %param.19, s32[]{:T(128)S(6)} %axis_index.25), kind=kLoop, calls=%fused_computation.37 | loop fusion | flops 88064 | bytes 16388 | tf_op jit(solution)/shard_map/add | solution.py:286
  10.4 4.4 %collective-permute-done.1.refs_1_ = bf16[400,128]{1,0:T(8,128)(2,1)S(1)} collective-permute-done((bf16[400,128]{1,0:T(8,128)(2,1)S(1)}, bf16[400,128]{1,0:T(8,128)(2,1)S(1)}, u32[]{:S(2)}, u32[]{:S(2)}) %collective-permute-start.1) | collective-permute-done | bytes 102432 | tf_op jit(solution)/shard_map/ppermute | solution.py:248
  14.8 0.9 %copy-done = f32[128,400]{0,1:T(8,128)S(1)} copy-done((f32[128,400]{0,1:T(8,128)S(1)}, f32[128,400]{0,1:T(8,128)}, u32[]{:S(2)}) %copy-start) | copy-done | bytes 204824
  15.8 0.9 %collective-permute-start.7 = (bf16[400,128]{1,0:T(8,128)(2,1)S(1)}, bf16[400,128]{1,0:T(8,128)(2,1)S(1)}, u32[]{:S(2)}, u32[]{:S(2)}) collective-permute-start(bf16[400,128]{1,0:T(8,128)(2,1)S(1)} %shard_map.146), channel_id=1, source_target_pairs={{0,2},{1,3},{2,0},{3,1},{4,6},{5,7},{6,4},{7,5},{8,10},{9,11},{10,... | collective-permute-start | bytes 307208 | tf_op jit(solution)/shard_map/ppermute | solution.py:241
  16.7 0.8 %fusion.4.refs_6_ = s32[1,1024]{1,0:T(1,128)S(1)} fusion(s32[1,1,1024]{2,1,0:T(1,128)} %param.17, s32[]{:T(128)S(6)} %axis_index.25), kind=kLoop, calls=%fused_computation.41 | loop fusion | flops 44032 | bytes 8196 | tf_op jit(solution)/shard_map/add | solution.py:286
  17.4 1.5 %collective-permute-start.2 = (bf16[400,128]{1,0:T(8,128)(2,1)S(1)}, bf16[400,128]{1,0:T(8,128)(2,1)S(1)}, u32[]{:S(2)}, u32[]{:S(2)}) collective-permute-start(bf16[400,128]{1,0:T(8,128)(2,1)S(1)} %collective-permute-done.1.refs_1_), channel_id=1, source_target_pairs={{0,4},{4,0},{8,12},{12,8},{16,20},{20,16},{24,28},{28,24},{1,5},{5... | collective-permute-start | bytes 307208 | tf_op jit(solution)/shard_map/ppermute | solution.py:238
  18.9 0.6 collective-permute-start.6
  19.5 1.4 %collective-permute-start.4 = (bf16[400,128]{1,0:T(8,128)(2,1)S(1)}, bf16[400,128]{1,0:T(8,128)(2,1)S(1)}, u32[]{:S(2)}, u32[]{:S(2)}) collective-permute-start(bf16[400,128]{1,0:T(8,128)(2,1)S(1)} %collective-permute-done.3.refs_2_), channel_id=1, source_target_pairs={{0,4},{4,0},{8,12},{12,8},{16,20},{20,16},{24,28},{28,24},{1,5},{5... | collective-permute-start | bytes 307208 | tf_op jit(solution)/shard_map/ppermute | solution.py:238
  21.0 0.1 collective-permute-start.8
  21.1 0.8 %fusion.3.source_ref.refs_8_ = s32[1,1024]{1,0:T(1,128)S(1)} fusion(s32[1,1,1024]{2,1,0:T(1,128)} %param.16, s32[]{:T(128)} %axis_index.22), kind=kLoop, calls=%fused_computation.40 | loop fusion | flops 44032 | bytes 8196 | tf_op jit(solution)/shard_map/add | solution.py:286
  21.8 0.9 %shard_map.148.refs_5_ = f32[2,1024,128]{2,1,0:T(8,128)S(1)} custom-call(s32[2,1024]{1,0:T(2,128)S(1)} %fusion.2.ids_ref), custom_call_target="tpu_custom_call" | custom-call | flops 4194304 | bytes 8192 | tf_op jit(solution)/shard_map/pallas_call | solution.py:47
  22.7 0.9 %shard_map.147 = (bf16[400,1024]{1,0:T(8,128)(2,1)S(1)}, bf16[400,1024]{1,0:T(8,128)(2,1)S(1)}, bf16[400,1024]{1,0:T(8,128)(2,1)S(1)}) custom-call(bf16[400,256]{1,0:T(8,128)(2,1)S(1)} %pad_maximum_fusion.near_ref, bf16[400,256]{1,0:T(8,128)(2,1)S(1)} %collective-permute-done.8.sibling_ref, f32[400,256]{1,0:T(8,128)S(1)} %bitcast.56, ...), custom_call_target="tpu_custom_call" | custom-call | flops 629145600 | bytes 827392 | tf_op jit(solution)/shard_map/pallas_call | solution.py:47
  23.7 1.2 %collective-permute-done.6.refs_3_ = bf16[400,128]{1,0:T(8,128)(2,1)S(1)} collective-permute-done((bf16[400,128]{1,0:T(8,128)(2,1)S(1)}, bf16[400,128]{1,0:T(8,128)(2,1)S(1)}, u32[]{:S(2)}, u32[]{:S(2)}) %collective-permute-start.6) | collective-permute-done | bytes 102432 | tf_op jit(solution)/shard_map/ppermute | solution.py:238
  24.9 1.1 %collective-permute-done.4.refs_2_ = bf16[400,128]{1,0:T(8,128)(2,1)S(1)} collective-permute-done((bf16[400,128]{1,0:T(8,128)(2,1)S(1)}, bf16[400,128]{1,0:T(8,128)(2,1)S(1)}, u32[]{:S(2)}, u32[]{:S(2)}) %collective-permute-start.4) | collective-permute-done | bytes 102432 | tf_op jit(solution)/shard_map/ppermute | solution.py:238
  26.0 1.5 %shard_map.149 = (bf16[512,1024]{1,0:T(8,128)(2,1)S(1)}, bf16[400,256]{1,0:T(8,128)(2,1)S(1)}, bf16[400,256]{1,0:T(8,128)(2,1)S(1)}) custom-call(bf16[400,128]{1,0:T(8,128)(2,1)S(1)} %collective-permute-done.refs_2_.refs_0_, bf16[400,128]{1,0:T(8,128)(2,1)S(1)} %collective-permute-done.2.refs_1_, bf16[400,128]{1,0:T(8,128)(2,1)S(1)} %collective-permute-done.4.refs_2_, ...), custom_call_target="tpu_custom_call" | custom-call | flops 838860800 | bytes 2281472 | tf_op jit(solution)/shard_map/pallas_call | solution.py:47
  27.5 1.3 %collective-permute-start.12 = (bf16[400,256]{1,0:T(8,128)(2,1)S(1)}, bf16[400,256]{1,0:T(8,128)(2,1)S(1)}, u32[]{:S(2)}, u32[]{:S(2)}) collective-permute-start(bf16[400,256]{1,0:T(8,128)(2,1)S(1)} %get-tuple-element.43), channel_id=1, source_target_pairs={{0,4},{4,0},{8,12},{12,8},{16,20},{20,16},{24,28},{28,24},{1,5},{5... | collective-permute-start | bytes 614408 | tf_op jit(solution)/shard_map/ppermute | solution.py:238
  28.8 0.8 %collective-permute-start.13 = (bf16[400,256]{1,0:T(8,128)(2,1)S(1)}, bf16[400,256]{1,0:T(8,128)(2,1)S(1)}, u32[]{:S(2)}, u32[]{:S(2)}) collective-permute-start(bf16[400,256]{1,0:T(8,128)(2,1)S(1)} %get-tuple-element.44), channel_id=1, source_target_pairs={{0,4},{4,0},{8,12},{12,8},{16,20},{20,16},{24,28},{28,24},{1,5},{5... | collective-permute-start | bytes 614408 | tf_op jit(solution)/shard_map/ppermute | solution.py:238
  29.6 1.9 %shard_map.150 = (f32[400,512]{1,0:T(8,128)S(1)}, f32[400,1024]{1,0:T(8,128)S(1)}, f32[408,128]{1,0:T(8,128)S(1)}) custom-call(bf16[400,128]{1,0:T(8,128)(2,1)S(1)} %collective-permute-done.9.refs_0_, bf16[400,128]{1,0:T(8,128)(2,1)S(1)} %collective-permute-done.1.refs_1_, bf16[400,128]{1,0:T(8,128)(2,1)S(1)} %collective-permute-done.3.refs_2_, ...), custom_call_target="tpu_custom_call" | custom-call | flops 1258291200 | bytes 2486784 | tf_op jit(solution)/shard_map/pallas_call | solution.py:47
  31.5 2.3 %shard_map.151 = (f32[400,256]{1,0:T(8,128)S(1)}, bf16[400,256]{1,0:T(8,128)(2,1)S(1)}, bf16[208,128]{1,0:T(8,128)(2,1)S(1)}, bf16[208,128]{1,0:T(8,128)(2,1)S(1...) custom-call(bf16[400,128]{1,0:T(8,128)(2,1)S(1)} %collective-permute-done.refs_2_.refs_0_, ...), custom_call_target="tpu_custom_call" | custom-call | flops 1048576000 | bytes 4743168 | tf_op jit(solution)/shard_map/pallas_call | solution.py:47
  33.7 0.1 collective-permute-start.14
  33.8 1.2 %collective-permute-start.15 = (bf16[208,128]{1,0:T(8,128)(2,1)S(1)}, bf16[208,128]{1,0:T(8,128)(2,1)S(1)}, u32[]{:S(2)}, u32[]{:S(2)}) collective-permute-start(bf16[208,128]{1,0:T(8,128)(2,1)S(1)} %get-tuple-element.47), channel_id=1, source_target_pairs={{0,2},{1,3},{2,0},{3,1},{4,6},{5,7},{6,4},{7,5},{8,10},{9,11},{10,... | collective-permute-start | bytes 159752 | tf_op jit(solution)/shard_map/ppermute | solution.py:241
  35.0 0.7 %collective-permute-start.16 = (bf16[208,128]{1,0:T(8,128)(2,1)S(1)}, bf16[208,128]{1,0:T(8,128)(2,1)S(1)}, u32[]{:S(2)}, u32[]{:S(2)}) collective-permute-start(bf16[208,128]{1,0:T(8,128)(2,1)S(1)} %get-tuple-element.48), channel_id=1, source_target_pairs={{0,3},{1,2},{2,1},{3,0},{4,7},{5,6},{6,5},{7,4},{8,11},{9,10},{10,... | collective-permute-start | bytes 159752 | tf_op jit(solution)/shard_map/ppermute | solution.py:241
  35.7 2.5 %collective-permute-done.15.refs_4_ = bf16[208,128]{1,0:T(8,128)(2,1)S(1)} collective-permute-done((bf16[208,128]{1,0:T(8,128)(2,1)S(1)}, bf16[208,128]{1,0:T(8,128)(2,1)S(1)}, u32[]{:S(2)}, u32[]{:S(2)}) %collective-permute-start.15) | collective-permute-done | bytes 53280 | tf_op jit(solution)/shard_map/ppermute | solution.py:241
  38.2 0.7 %collective-permute-done.16.refs_5_ = bf16[208,128]{1,0:T(8,128)(2,1)S(1)} collective-permute-done((bf16[208,128]{1,0:T(8,128)(2,1)S(1)}, bf16[208,128]{1,0:T(8,128)(2,1)S(1)}, u32[]{:S(2)}, u32[]{:S(2)}) %collective-permute-start.16) | collective-permute-done | bytes 53280 | tf_op jit(solution)/shard_map/ppermute | solution.py:241
  39.0 0.1 shard_map.153
  39.1 2.9 %collective-permute-start.17 = (bf16[208,128]{1,0:T(8,128)(2,1)S(1)}, bf16[208,128]{1,0:T(8,128)(2,1)S(1)}, u32[]{:S(2)}, u32[]{:S(2)}) collective-permute-start(bf16[208,128]{1,0:T(8,128)(2,1)S(1)} %get-tuple-element.49.piece_ref), channel_id=1, source_target_pairs={{0,8},{4,12},{8,0},{12,4},{16,24},{20,28},{24,16},{28,20},{1,9},{5... | collective-permute-start | bytes 159752 | tf_op jit(solution)/shard_map/ppermute | solution.py:238
  42.0 2.1 %collective-permute-done.17.other_ref = bf16[208,128]{1,0:T(8,128)(2,1)S(1)} collective-permute-done((bf16[208,128]{1,0:T(8,128)(2,1)S(1)}, bf16[208,128]{1,0:T(8,128)(2,1)S(1)}, u32[]{:S(2)}, u32[]{:S(2)}) %collective-permute-start.17) | collective-permute-done | bytes 53280 | tf_op jit(solution)/shard_map/ppermute | solution.py:238
  44.1 0.1 shard_map.154
  44.2 1.3 %collective-permute-start.22 = (bf16[208,128]{1,0:T(8,128)(2,1)S(1)}, bf16[208,128]{1,0:T(8,128)(2,1)S(1)}, u32[]{:S(2)}, u32[]{:S(2)}) collective-permute-start(bf16[208,128]{1,0:T(8,128)(2,1)S(1)} %get-tuple-element.57), channel_id=1, source_target_pairs={{0,16},{4,20},{8,24},{12,28},{16,0},{20,4},{24,8},{28,12},{1,17},{... | collective-permute-start | bytes 159752 | tf_op jit(solution)/shard_map/ppermute | solution.py:238
  45.5 0.5 collective-permute-start.21
  46.0 1.7 %collective-permute-start.19 = (bf16[400,128]{1,0:T(8,128)(2,1)S(1)}, bf16[400,128]{1,0:T(8,128)(2,1)S(1)}, u32[]{:S(2)}, u32[]{:S(2)}) collective-permute-start(bf16[400,128]{1,0:T(8,128)(2,1)S(1)} %get-tuple-element.52), channel_id=1, source_target_pairs={{0,16},{4,20},{8,24},{12,28},{16,0},{20,4},{24,8},{28,12},{1,17},{... | collective-permute-start | bytes 307208 | tf_op jit(solution)/shard_map/ppermute | solution.py:238
  47.7 2.1 %collective-permute-start.20 = (bf16[400,128]{1,0:T(8,128)(2,1)S(1)}, bf16[400,128]{1,0:T(8,128)(2,1)S(1)}, u32[]{:S(2)}, u32[]{:S(2)}) collective-permute-start(bf16[400,128]{1,0:T(8,128)(2,1)S(1)} %get-tuple-element.53), channel_id=1, source_target_pairs={{0,24},{4,28},{8,16},{12,20},{16,8},{20,12},{24,0},{28,4},{1,25},{... | collective-permute-start | bytes 307208 | tf_op jit(solution)/shard_map/ppermute | solution.py:238
  49.9 1.4 %collective-permute-start.23 = (bf16[208,128]{1,0:T(8,128)(2,1)S(1)}, bf16[208,128]{1,0:T(8,128)(2,1)S(1)}, u32[]{:S(2)}, u32[]{:S(2)}) collective-permute-start(bf16[208,128]{1,0:T(8,128)(2,1)S(1)} %add_convert_fusion.1), channel_id=1, source_target_pairs={{0,4},{4,0},{8,12},{12,8},{16,20},{20,16},{24,28},{28,24},{1,5},{5... | collective-permute-start | bytes 159752 | tf_op jit(solution)/shard_map/ppermute | solution.py:238
  51.3 1.1 %collective-permute-start.11 = (bf16[400,128]{1,0:T(8,128)(2,1)S(1)}, bf16[400,128]{1,0:T(8,128)(2,1)S(1)}, u32[]{:S(2)}, u32[]{:S(2)}) collective-permute-start(bf16[400,128]{1,0:T(8,128)(2,1)S(1)} %slice.16), channel_id=1, source_target_pairs={{0,2},{1,3},{2,0},{3,1},{4,6},{5,7},{6,4},{7,5},{8,10},{9,11},{10,... | collective-permute-start | bytes 307208 | tf_op jit(solution)/shard_map/ppermute | solution.py:241
  52.5 1.6 %collective-permute-done.23 = bf16[208,128]{1,0:T(8,128)(2,1)S(1)} collective-permute-done((bf16[208,128]{1,0:T(8,128)(2,1)S(1)}, bf16[208,128]{1,0:T(8,128)(2,1)S(1)}, u32[]{:S(2)}, u32[]{:S(2)}) %collective-permute-start.23) | collective-permute-done | bytes 53280 | tf_op jit(solution)/shard_map/ppermute | solution.py:238
  54.1 1.5 %collective-permute-start.18 = (bf16[400,128]{1,0:T(8,128)(2,1)S(1)}, bf16[400,128]{1,0:T(8,128)(2,1)S(1)}, u32[]{:S(2)}, u32[]{:S(2)}) collective-permute-start(bf16[400,128]{1,0:T(8,128)(2,1)S(1)} %get-tuple-element.51), channel_id=1, source_target_pairs={{0,8},{4,12},{8,0},{12,4},{16,24},{20,28},{24,16},{28,20},{1,9},{5... | collective-permute-start | bytes 307208 | tf_op jit(solution)/shard_map/ppermute | solution.py:238
  55.7 1.7 %collective-permute-done.19.refs_1_ = bf16[400,128]{1,0:T(8,128)(2,1)S(1)} collective-permute-done((bf16[400,128]{1,0:T(8,128)(2,1)S(1)}, bf16[400,128]{1,0:T(8,128)(2,1)S(1)}, u32[]{:S(2)}, u32[]{:S(2)}) %collective-permute-start.19) | collective-permute-done | bytes 102432 | tf_op jit(solution)/shard_map/ppermute | solution.py:238
  57.5 1.0 %collective-permute-start.25 = (bf16[208,128]{1,0:T(8,128)(2,1)S(1)}, bf16[208,128]{1,0:T(8,128)(2,1)S(1)}, u32[]{:S(2)}, u32[]{:S(2)}) collective-permute-start(bf16[208,128]{1,0:T(8,128)(2,1)S(1)} %add_convert_fusion.refs_0_), channel_id=1, source_target_pairs={{0,2},{1,3},{2,0},{3,1},{4,6},{5,7},{6,4},{7,5},{8,10},{9,11},{10,... | collective-permute-start | bytes 159752 | tf_op jit(solution)/shard_map/ppermute | solution.py:241
  58.5 0.8 %shard_map.152 = (f32[400,128]{1,0:T(8,128)}, f32[1,128]{1,0:T(1,128)}) custom-call(f32[400,128]{1,0:T(8,128)S(1)} %slice.12.own_ref, bf16[400,128]{1,0:T(8,128)(2,1)S(1)} %collective-permute-done.11.refs_0_, f32[400,128]{1,0:T(8,128)S(1)} %bitcast.55, f32[1,128]{1,0:T(1,128)S(1)} %bitcast.63), custom_call_target="tpu_custom_call" | custom-call | flops 409600 | bytes 512512 | tf_op jit(solution)/shard_map/pallas_call | solution.py:47
  59.3 0.3 collective-permute-done.18.refs_0_
  59.5 0.8 %shard_map.155 = (f32[400,128]{1,0:T(8,128)}, f32[1,128]{1,0:T(1,128)}) custom-call(f32[400,128]{1,0:T(8,128)S(1)} %get-tuple-element.50.own_ref, bf16[400,128]{1,0:T(8,128)(2,1)S(1)} %collective-permute-done.18.refs_0_, bf16[400,128]{1,0:T(8,128)(2,1)S(1)} %collective-permute-done.19.refs_1_, bf16[400,128]{1,0:T(8,128)(2,1)S(1)} %collective-permute-done.20.refs_2_, ...), custom_call_target="tpu_custom_call" | custom-call | flops 409600 | bytes 724992 | tf_op jit(solution)/shard_map/pallas_call | solution.py:47
  60.3 1.3 %collective-permute-done.25.refs_2_ = bf16[208,128]{1,0:T(8,128)(2,1)S(1)} collective-permute-done((bf16[208,128]{1,0:T(8,128)(2,1)S(1)}, bf16[208,128]{1,0:T(8,128)(2,1)S(1)}, u32[]{:S(2)}, u32[]{:S(2)}) %collective-permute-start.25) | collective-permute-done | bytes 53280 | tf_op jit(solution)/shard_map/ppermute | solution.py:241
  61.6 0.9 %shard_map.156 = (f32[400,256]{1,0:T(8,128)}, f32[1,256]{1,0:T(1,128)}) custom-call(bf16[208,128]{1,0:T(8,128)(2,1)S(1)} %add_convert_fusion.refs_0_, bf16[208,128]{1,0:T(8,128)(2,1)S(1)} %collective-permute-done.24.refs_1_, bf16[208,128]{1,0:T(8,128)(2,1)S(1)} %collective-permute-done.25.refs_2_, bf16[208,128]{1,0:T(8,128)(2,1)S(1)} %collective-permute-done.26.refs_3_, ...), custom_call_target="tpu_custom_call" | custom-call | flops 819200 | bytes 623616 | tf_op jit(solution)/shard_map/pallas_call | solution.py:47
  (46 shorter events, 0.3 us)
Async XLA Ops:
  0.6 0.9 %copy-start.3 = (f32[128,400]{0,1:T(8,128)S(1)}, f32[128,400]{0,1:T(8,128)}, u32[]{:S(2)}) copy-start(f32[128,400]{0,1:T(8,128)} %param.12) | copy-start | bytes 614404
  1.6 21.2 %copy-start.5 = (s32[1,1,1024]{2,1,0:T(1,128)S(1)}, s32[1,1,1024]{2,1,0:T(1,128)}, u32[]{:S(2)}) copy-start(s32[1,1,1024]{2,1,0:T(1,128)} %param.18) | copy-start | bytes 12292
  1.6 28.0 %collective-permute-start.9 = (bf16[400,128]{1,0:T(8,128)(2,1)S(1)}, bf16[400,128]{1,0:T(8,128)(2,1)S(1)}, u32[]{:S(2)}, u32[]{:S(2)}) collective-permute-start(bf16[400,128]{1,0:T(8,128)(2,1)S(1)} %shard_map.145), channel_id=1, source_target_pairs={{0,1},{1,2},{2,3},{3,0},{4,5},{5,6},{6,7},{7,4},{8,9},{9,10},{10,1... | collective-permute-start | bytes 307208 | tf_op jit(solution)/shard_map/ppermute | solution.py:248
  2.1 16.8 %collective-permute-start.5 = (bf16[400,128]{1,0:T(8,128)(2,1)S(1)}, bf16[400,128]{1,0:T(8,128)(2,1)S(1)}, u32[]{:S(2)}, u32[]{:S(2)}) collective-permute-start(bf16[400,128]{1,0:T(8,128)(2,1)S(1)} %shard_map.145), channel_id=1, source_target_pairs={{0,25},{1,26},{2,27},{3,24},{4,29},{5,30},{6,31},{7,28},{8,17},{9,... | collective-permute-start | bytes 307208 | tf_op jit(solution)/shard_map/ppermute | solution.py:248
  7.9 11.6 %collective-permute-start.3 = (bf16[400,128]{1,0:T(8,128)(2,1)S(1)}, bf16[400,128]{1,0:T(8,128)(2,1)S(1)}, u32[]{:S(2)}, u32[]{:S(2)}) collective-permute-start(bf16[400,128]{1,0:T(8,128)(2,1)S(1)} %shard_map.145), channel_id=1, source_target_pairs={{0,17},{1,18},{2,19},{3,16},{4,21},{5,22},{6,23},{7,20},{8,25},{9,... | collective-permute-start | bytes 307208 | tf_op jit(solution)/shard_map/ppermute | solution.py:248
  7.9 6.9 %collective-permute-start.1 = (bf16[400,128]{1,0:T(8,128)(2,1)S(1)}, bf16[400,128]{1,0:T(8,128)(2,1)S(1)}, u32[]{:S(2)}, u32[]{:S(2)}) collective-permute-start(bf16[400,128]{1,0:T(8,128)(2,1)S(1)} %shard_map.145), channel_id=1, source_target_pairs={{0,9},{1,10},{2,11},{3,8},{4,13},{5,14},{6,15},{7,12},{8,1},{9,2},... | collective-permute-start | bytes 307208 | tf_op jit(solution)/shard_map/ppermute | solution.py:248
  8.0 6.8 %collective-permute-start = (bf16[400,128]{1,0:T(8,128)(2,1)S(1)}, bf16[400,128]{1,0:T(8,128)(2,1)S(1)}, u32[]{:S(2)}, u32[]{:S(2)}) collective-permute-start(bf16[400,128]{1,0:T(8,128)(2,1)S(1)} %shard_map.145), channel_id=1, source_target_pairs={{0,5},{1,6},{2,7},{3,4},{4,1},{5,2},{6,3},{7,0},{8,13},{9,14},{10,... | collective-permute-start | bytes 307208 | tf_op jit(solution)/shard_map/ppermute | solution.py:248
  14.8 0.9 %copy-start = (f32[128,400]{0,1:T(8,128)S(1)}, f32[128,400]{0,1:T(8,128)}, u32[]{:S(2)}) copy-start(f32[128,400]{0,1:T(8,128)} %param.10) | copy-start | bytes 614404
  15.7 7.0 %copy-start.2 = (f32[256,400]{0,1:T(8,128)S(1)}, f32[256,400]{0,1:T(8,128)}, u32[]{:S(2)}) copy-start(f32[256,400]{0,1:T(8,128)} %param.14) | copy-start | bytes 1228804
  15.8 5.2 %collective-permute-start.7 = (bf16[400,128]{1,0:T(8,128)(2,1)S(1)}, bf16[400,128]{1,0:T(8,128)(2,1)S(1)}, u32[]{:S(2)}, u32[]{:S(2)}) collective-permute-start(bf16[400,128]{1,0:T(8,128)(2,1)S(1)} %shard_map.146), channel_id=1, source_target_pairs={{0,2},{1,3},{2,0},{3,1},{4,6},{5,7},{6,4},{7,5},{8,10},{9,11},{10,... | collective-permute-start | bytes 307208 | tf_op jit(solution)/shard_map/ppermute | solution.py:241
  17.4 8.5 %collective-permute-start.2 = (bf16[400,128]{1,0:T(8,128)(2,1)S(1)}, bf16[400,128]{1,0:T(8,128)(2,1)S(1)}, u32[]{:S(2)}, u32[]{:S(2)}) collective-permute-start(bf16[400,128]{1,0:T(8,128)(2,1)S(1)} %collective-permute-done.1.refs_1_), channel_id=1, source_target_pairs={{0,4},{4,0},{8,12},{12,8},{16,20},{20,16},{24,28},{28,24},{1,5},{5... | collective-permute-start | bytes 307208 | tf_op jit(solution)/shard_map/ppermute | solution.py:238
  18.9 6.0 %collective-permute-start.6 = (bf16[400,128]{1,0:T(8,128)(2,1)S(1)}, bf16[400,128]{1,0:T(8,128)(2,1)S(1)}, u32[]{:S(2)}, u32[]{:S(2)}) collective-permute-start(bf16[400,128]{1,0:T(8,128)(2,1)S(1)} %collective-permute-done.5.refs_3_), channel_id=1, source_target_pairs={{0,4},{4,0},{8,12},{12,8},{16,20},{20,16},{24,28},{28,24},{1,5},{5... | collective-permute-start | bytes 307208 | tf_op jit(solution)/shard_map/ppermute | solution.py:238
  19.5 6.4 %collective-permute-start.4 = (bf16[400,128]{1,0:T(8,128)(2,1)S(1)}, bf16[400,128]{1,0:T(8,128)(2,1)S(1)}, u32[]{:S(2)}, u32[]{:S(2)}) collective-permute-start(bf16[400,128]{1,0:T(8,128)(2,1)S(1)} %collective-permute-done.3.refs_2_), channel_id=1, source_target_pairs={{0,4},{4,0},{8,12},{12,8},{16,20},{20,16},{24,28},{28,24},{1,5},{5... | collective-permute-start | bytes 307208 | tf_op jit(solution)/shard_map/ppermute | solution.py:238
  21.0 1.7 %collective-permute-start.8 = (bf16[400,256]{1,0:T(8,128)(2,1)S(1)}, bf16[400,256]{1,0:T(8,128)(2,1)S(1)}, u32[]{:S(2)}, u32[]{:S(2)}) collective-permute-start(bf16[400,256]{1,0:T(8,128)(2,1)S(1)} %pad_maximum_fusion.near_ref), channel_id=1, source_target_pairs={{0,1},{1,0},{2,3},{3,2},{4,5},{5,4},{6,7},{7,6},{8,9},{9,8},{10,11... | collective-permute-start | bytes 614408 | tf_op jit(solution)/shard_map/ppermute | solution.py:241
  23.6 6.0 %copy-start.4 = (f32[128,400]{0,1:T(8,128)S(1)}, f32[128,400]{0,1:T(8,128)}, u32[]{:S(2)}) copy-start(f32[128,400]{0,1:T(8,128)} %param.12) | copy-start | bytes 614404
  23.7 6.0 %copy-start.8 = (f32[128]{0:T(128)S(1)}, f32[128]{0:T(128)}, u32[]{:S(2)}) copy-start(f32[128]{0:T(128)} %param.13) | copy-start | bytes 1540
  27.5 14.5 %collective-permute-start.12 = (bf16[400,256]{1,0:T(8,128)(2,1)S(1)}, bf16[400,256]{1,0:T(8,128)(2,1)S(1)}, u32[]{:S(2)}, u32[]{:S(2)}) collective-permute-start(bf16[400,256]{1,0:T(8,128)(2,1)S(1)} %get-tuple-element.43), channel_id=1, source_target_pairs={{0,4},{4,0},{8,12},{12,8},{16,20},{20,16},{24,28},{28,24},{1,5},{5... | collective-permute-start | bytes 614408 | tf_op jit(solution)/shard_map/ppermute | solution.py:238
  28.8 10.1 %collective-permute-start.13 = (bf16[400,256]{1,0:T(8,128)(2,1)S(1)}, bf16[400,256]{1,0:T(8,128)(2,1)S(1)}, u32[]{:S(2)}, u32[]{:S(2)}) collective-permute-start(bf16[400,256]{1,0:T(8,128)(2,1)S(1)} %get-tuple-element.44), channel_id=1, source_target_pairs={{0,4},{4,0},{8,12},{12,8},{16,20},{20,16},{24,28},{28,24},{1,5},{5... | collective-permute-start | bytes 614408 | tf_op jit(solution)/shard_map/ppermute | solution.py:238
  33.7 1.9 %collective-permute-start.14 = (bf16[208,128]{1,0:T(8,128)(2,1)S(1)}, bf16[208,128]{1,0:T(8,128)(2,1)S(1)}, u32[]{:S(2)}, u32[]{:S(2)}) collective-permute-start(bf16[208,128]{1,0:T(8,128)(2,1)S(1)} %get-tuple-element.46), channel_id=1, source_target_pairs={{0,1},{1,0},{2,3},{3,2},{4,5},{5,4},{6,7},{7,6},{8,9},{9,8},{10,11... | collective-permute-start | bytes 159752 | tf_op jit(solution)/shard_map/ppermute | solution.py:241
  33.8 4.4 %collective-permute-start.15 = (bf16[208,128]{1,0:T(8,128)(2,1)S(1)}, bf16[208,128]{1,0:T(8,128)(2,1)S(1)}, u32[]{:S(2)}, u32[]{:S(2)}) collective-permute-start(bf16[208,128]{1,0:T(8,128)(2,1)S(1)} %get-tuple-element.47), channel_id=1, source_target_pairs={{0,2},{1,3},{2,0},{3,1},{4,6},{5,7},{6,4},{7,5},{8,10},{9,11},{10,... | collective-permute-start | bytes 159752 | tf_op jit(solution)/shard_map/ppermute | solution.py:241
  35.0 4.0 %collective-permute-start.16 = (bf16[208,128]{1,0:T(8,128)(2,1)S(1)}, bf16[208,128]{1,0:T(8,128)(2,1)S(1)}, u32[]{:S(2)}, u32[]{:S(2)}) collective-permute-start(bf16[208,128]{1,0:T(8,128)(2,1)S(1)} %get-tuple-element.48), channel_id=1, source_target_pairs={{0,3},{1,2},{2,1},{3,0},{4,7},{5,6},{6,5},{7,4},{8,11},{9,10},{10,... | collective-permute-start | bytes 159752 | tf_op jit(solution)/shard_map/ppermute | solution.py:241
  39.0 19.4 %copy-start.1 = (f32[128,400]{0,1:T(8,128)S(1)}, f32[128,400]{0,1:T(8,128)}, u32[]{:S(2)}) copy-start(f32[128,400]{0,1:T(8,128)} %param.10) | copy-start | bytes 614404
  39.1 19.4 %copy-start.7 = (f32[128]{0:T(128)S(1)}, f32[128]{0:T(128)}, u32[]{:S(2)}) copy-start(f32[128]{0:T(128)} %param.11) | copy-start | bytes 1540
  39.1 5.1 %collective-permute-start.17 = (bf16[208,128]{1,0:T(8,128)(2,1)S(1)}, bf16[208,128]{1,0:T(8,128)(2,1)S(1)}, u32[]{:S(2)}, u32[]{:S(2)}) collective-permute-start(bf16[208,128]{1,0:T(8,128)(2,1)S(1)} %get-tuple-element.49.piece_ref), channel_id=1, source_target_pairs={{0,8},{4,12},{8,0},{12,4},{16,24},{20,28},{24,16},{28,20},{1,9},{5... | collective-permute-start | bytes 159752 | tf_op jit(solution)/shard_map/ppermute | solution.py:238
  44.2 17.4 %copy-start.6 = (f32[256]{0:T(256)S(1)}, f32[256]{0:T(256)}, u32[]{:S(2)}) copy-start(f32[256]{0:T(256)} %param.15) | copy-start | bytes 3076
  44.2 5.6 %collective-permute-start.22 = (bf16[208,128]{1,0:T(8,128)(2,1)S(1)}, bf16[208,128]{1,0:T(8,128)(2,1)S(1)}, u32[]{:S(2)}, u32[]{:S(2)}) collective-permute-start(bf16[208,128]{1,0:T(8,128)(2,1)S(1)} %get-tuple-element.57), channel_id=1, source_target_pairs={{0,16},{4,20},{8,24},{12,28},{16,0},{20,4},{24,8},{28,12},{1,17},{... | collective-permute-start | bytes 159752 | tf_op jit(solution)/shard_map/ppermute | solution.py:238
  45.5 5.7 %collective-permute-start.10 = (bf16[400,256]{1,0:T(8,128)(2,1)S(1)}, bf16[400,256]{1,0:T(8,128)(2,1)S(1)}, u32[]{:S(2)}, u32[]{:S(2)}) collective-permute-start(bf16[400,256]{1,0:T(8,128)(2,1)S(1)} %get-tuple-element.39), channel_id=1, source_target_pairs={{0,1},{1,0},{2,3},{3,2},{4,5},{5,4},{6,7},{7,6},{8,9},{9,8},{10,11... | collective-permute-start | bytes 614408 | tf_op jit(solution)/shard_map/ppermute | solution.py:241
  45.5 10.1 %collective-permute-start.21 = (f32[408,128]{1,0:T(8,128)S(1)}, f32[408,128]{1,0:T(8,128)S(1)}, u32[]{:S(2)}, u32[]{:S(2)}) collective-permute-start(f32[408,128]{1,0:T(8,128)S(1)} %get-tuple-element.54), channel_id=1, source_target_pairs={{0,1},{1,2},{2,3},{3,0},{4,5},{5,6},{6,7},{7,4},{8,9},{9,10},{10,1... | collective-permute-start | bytes 626696 | tf_op jit(solution)/shard_map/ppermute | solution.py:248
  46.0 11.4 %collective-permute-start.19 = (bf16[400,128]{1,0:T(8,128)(2,1)S(1)}, bf16[400,128]{1,0:T(8,128)(2,1)S(1)}, u32[]{:S(2)}, u32[]{:S(2)}) collective-permute-start(bf16[400,128]{1,0:T(8,128)(2,1)S(1)} %get-tuple-element.52), channel_id=1, source_target_pairs={{0,16},{4,20},{8,24},{12,28},{16,0},{20,4},{24,8},{28,12},{1,17},{... | collective-permute-start | bytes 307208 | tf_op jit(solution)/shard_map/ppermute | solution.py:238
  47.7 11.5 %collective-permute-start.20 = (bf16[400,128]{1,0:T(8,128)(2,1)S(1)}, bf16[400,128]{1,0:T(8,128)(2,1)S(1)}, u32[]{:S(2)}, u32[]{:S(2)}) collective-permute-start(bf16[400,128]{1,0:T(8,128)(2,1)S(1)} %get-tuple-element.53), channel_id=1, source_target_pairs={{0,24},{4,28},{8,16},{12,20},{16,8},{20,12},{24,0},{28,4},{1,25},{... | collective-permute-start | bytes 307208 | tf_op jit(solution)/shard_map/ppermute | solution.py:238
  49.9 4.2 %collective-permute-start.23 = (bf16[208,128]{1,0:T(8,128)(2,1)S(1)}, bf16[208,128]{1,0:T(8,128)(2,1)S(1)}, u32[]{:S(2)}, u32[]{:S(2)}) collective-permute-start(bf16[208,128]{1,0:T(8,128)(2,1)S(1)} %add_convert_fusion.1), channel_id=1, source_target_pairs={{0,4},{4,0},{8,12},{12,8},{16,20},{20,16},{24,28},{28,24},{1,5},{5... | collective-permute-start | bytes 159752 | tf_op jit(solution)/shard_map/ppermute | solution.py:238
  51.3 7.1 %collective-permute-start.11 = (bf16[400,128]{1,0:T(8,128)(2,1)S(1)}, bf16[400,128]{1,0:T(8,128)(2,1)S(1)}, u32[]{:S(2)}, u32[]{:S(2)}) collective-permute-start(bf16[400,128]{1,0:T(8,128)(2,1)S(1)} %slice.16), channel_id=1, source_target_pairs={{0,2},{1,3},{2,0},{3,1},{4,6},{5,7},{6,4},{7,5},{8,10},{9,11},{10,... | collective-permute-start | bytes 307208 | tf_op jit(solution)/shard_map/ppermute | solution.py:241
  54.1 5.5 %collective-permute-start.18 = (bf16[400,128]{1,0:T(8,128)(2,1)S(1)}, bf16[400,128]{1,0:T(8,128)(2,1)S(1)}, u32[]{:S(2)}, u32[]{:S(2)}) collective-permute-start(bf16[400,128]{1,0:T(8,128)(2,1)S(1)} %get-tuple-element.51), channel_id=1, source_target_pairs={{0,8},{4,12},{8,0},{12,4},{16,24},{20,28},{24,16},{28,20},{1,9},{5... | collective-permute-start | bytes 307208 | tf_op jit(solution)/shard_map/ppermute | solution.py:238
  55.6 4.7 %collective-permute-start.26 = (bf16[208,128]{1,0:T(8,128)(2,1)S(1)}, bf16[208,128]{1,0:T(8,128)(2,1)S(1)}, u32[]{:S(2)}, u32[]{:S(2)}) collective-permute-start(bf16[208,128]{1,0:T(8,128)(2,1)S(1)} %add_convert_fusion.refs_0_), channel_id=1, source_target_pairs={{0,3},{1,2},{2,1},{3,0},{4,7},{5,6},{6,5},{7,4},{8,11},{9,10},{10,... | collective-permute-start | bytes 159752 | tf_op jit(solution)/shard_map/ppermute | solution.py:241
  57.5 4.1 %collective-permute-start.25 = (bf16[208,128]{1,0:T(8,128)(2,1)S(1)}, bf16[208,128]{1,0:T(8,128)(2,1)S(1)}, u32[]{:S(2)}, u32[]{:S(2)}) collective-permute-start(bf16[208,128]{1,0:T(8,128)(2,1)S(1)} %add_convert_fusion.refs_0_), channel_id=1, source_target_pairs={{0,2},{1,3},{2,0},{3,1},{4,6},{5,7},{6,4},{7,5},{8,10},{9,11},{10,... | collective-permute-start | bytes 159752 | tf_op jit(solution)/shard_map/ppermute | solution.py:241
  58.4 3.2 %collective-permute-start.24 = (bf16[208,128]{1,0:T(8,128)(2,1)S(1)}, bf16[208,128]{1,0:T(8,128)(2,1)S(1)}, u32[]{:S(2)}, u32[]{:S(2)}) collective-permute-start(bf16[208,128]{1,0:T(8,128)(2,1)S(1)} %add_convert_fusion.refs_0_), channel_id=1, source_target_pairs={{0,1},{1,0},{2,3},{3,2},{4,5},{5,4},{6,7},{7,6},{8,9},{9,8},{10,11... | collective-permute-start | bytes 159752 | tf_op jit(solution)/shard_map/ppermute | solution.py:241

commit v5 on v4

--- a/solution.py
+++ b/solution.py
@@ -60,7 +60,13 @@
     return jax.ShapeDtypeStruct(dims, dtype)
 
 
-def count_body(ids_ref, out_ref):
+def cast_body(left_ref, right_ref, left_bf_ref, right_bf_ref):
+    right_bf_ref[...] = right_ref[...].astype(BF)
+    left_bf_ref[...] = left_ref[...].astype(BF)
+
+
+def count_body(ids_ref, left_ref, out_ref, left_out_ref):
+    left_out_ref[...] = left_ref[...]
     for g in range(out_ref.shape[0]):
         ids = ids_ref[g:g + 1, :]
         for at in range(0, out_ref.shape[1], LANES):
@@ -106,15 +112,12 @@
 
 def near_body(blocks, *refs):
     block_refs, refs = refs[:blocks], refs[blocks:]
-    q_ref, weight_ref, target_ref, table_ref, state_ref, right_ref, qg_ref, pack_ref, rows_ref, m_ref = refs
+    q_ref, weight_ref, target_ref, right_ref, qg_ref, rows_ref, m_ref = refs
     for k, ref in enumerate(block_refs):
         rows_ref[:, k * LANES:(k + 1) * LANES] = ref[...]
     grad_matrix(rows_ref, q_ref, weight_ref, target_ref, m_ref, 0)
     right_ref[...] = dot(q_ref[...], m_ref[...], 1, 1)
     qg_ref[...] = dot(rows_ref[...], m_ref[...], 1, 0)
-    width = table_ref.shape[0]
-    pack_ref[:width, :] = table_ref[...]
-    pack_ref[width:, :] = jnp.broadcast_to(state_ref[...], (pack_ref.shape[0] - width, LANES))
 
 
 def far_body(blocks, *refs):
@@ -131,8 +134,8 @@
 
 def back_body(blocks, pieces, *refs):
     block_refs, refs = refs[:blocks], refs[blocks:]
-    m_ref, qg_ref, s_ref, o_ref, source_ref, kind_ref, here_ref, near_ref, far_ref = refs[:9]
-    piece_refs, refs = refs[9:9 + pieces], refs[9 + pieces:]
+    m_ref, qg_ref, s_ref, o_ref, source_ref, kind_ref, here_ref, near_ref = refs[:8]
+    piece_refs, refs = refs[8:8 + pieces], refs[8 + pieces:]
     rows_ref, left_ref, kinds_ref, tall_ref = refs
     for k, ref in enumerate(block_refs):
         rows_ref[:, k * LANES:(k + 1) * LANES] = ref[...]
@@ -158,7 +161,6 @@
             left_ref[...] += left
     cut = left_ref.shape[1] // 2
     near_ref[...] = left_ref[:, :cut]
-    far_ref[...] = left_ref[:, cut:].astype(BF)
     parts = kinds_ref.shape[1] // LANES
     for j in range(parts):
         tall_ref[j * width:(j + 1) * width, :] = kinds_ref[:, j * LANES:(j + 1) * LANES]
@@ -169,7 +171,14 @@
     size = tall_ref.shape[0] // pieces
     for k, ref in enumerate(piece_refs):
         start = pl.multiple_of((here ^ k) * size, 16)
-        ref[...] = tall_ref[pl.ds(start, size), :].astype(BF)
+        piece = tall_ref[pl.ds(start, size), :].astype(BF)
+        if k == 1:
+            for j in range(cut // LANES):
+                at = cut + j * LANES
+                ref[j * width:(j + 1) * width, :] = left_ref[:, at:at + LANES].astype(BF)
+            ref[cut // LANES * width:, :] = piece
+        else:
+            ref[...] = piece
 
 
 def relation_body(pieces, *refs):
@@ -189,31 +198,43 @@
         new_ref[:, cols] = table_ref[:, cols] - g * (LEARN_RATE * lax.rsqrt(state))
 
 
-def cast_body(in_ref, out_ref):
-    out_ref[...] = in_ref[...].astype(BF)
-
-
-def high_body(blocks, pieces, *refs):
-    near_ref, got_ref, refs = refs[0], refs[1], refs[2:]
+def high_body(blocks, pieces, near_ref, got_ref, left_ref, *refs):
     piece_refs, refs = refs[:pieces], refs[pieces:]
-    block_refs, mine_ref = refs[:blocks], refs[blocks]
+    block_refs, mine_ref, left_own_ref, left_refs = refs[:blocks], refs[blocks], refs[blocks + 1], refs[blocks + 2:]
     base = near_ref.shape[1] - blocks * LANES
     for k, ref in enumerate(block_refs):
         cols = slice(k * LANES, (k + 1) * LANES)
         ref[...] = (near_ref[:, base + k * LANES:base + (k + 1) * LANES] + got_ref[:, cols].astype(F32)).astype(BF)
-    parts = [ref[...].astype(F32) for ref in piece_refs]
+    width = left_ref.shape[0]
+    size = mine_ref.shape[0]
+    core_ref = piece_refs[1]
+    parts = [core_ref[core_ref.shape[0] - size:, :] if k == 1 else ref[...] for k, ref in enumerate(piece_refs)]
+    parts = [part.astype(F32) for part in parts]
     while len(parts) > 1:
         parts = [parts[i] + parts[i + 1] for i in range(0, len(parts), 2)]
     mine_ref[...] = parts[0].astype(BF)
-
-
-def low_body(blocks, near_ref, got_ref, piece_ref, other_ref, *refs):
-    block_refs, (own_ref, mine_ref) = refs[:blocks - 1], refs[blocks - 1:]
-    own_ref[...] = near_ref[:, :LANES] + got_ref[:, :LANES].astype(F32)
+    for k in range(left_ref.shape[1] // LANES):
+        total = left_ref[:, k * LANES:(k + 1) * LANES] + core_ref[k * width:(k + 1) * width, :].astype(F32)
+        if k == 0:
+            left_own_ref[...] = total
+        else:
+            left_refs[k - 1][...] = total.astype(BF)
+
+
+def low_body(blocks, near_ref, got_ref, piece_ref, other_ref, table_ref, state_ref, *refs):
+    block_refs, (own_ref, mine_ref, pack_ref) = refs[:blocks - 1], refs[blocks - 1:]
+    mine_ref[...] = (piece_ref[...].astype(F32) + other_ref[...].astype(F32)).astype(BF)
     for k, ref in enumerate(block_refs):
         cols = slice((k + 1) * LANES, (k + 2) * LANES)
         ref[...] = (near_ref[:, cols] + got_ref[:, cols].astype(F32)).astype(BF)
-    mine_ref[...] = (piece_ref[...].astype(F32) + other_ref[...].astype(F32)).astype(BF)
+    own_ref[...] = near_ref[:, :LANES] + got_ref[:, :LANES].astype(F32)
+    width = table_ref.shape[0]
+    pack_ref[:width, :] = table_ref[...]
+    pack_ref[width:, :] = jnp.broadcast_to(state_ref[...], (pack_ref.shape[0] - width, LANES))
+
+
+def sum_body(piece_ref, other_ref, out_ref):
+    out_ref[...] = (piece_ref[...].astype(F32) + other_ref[...].astype(F32)).astype(BF)
 
 
 def update_body(parts, own_ref, *refs):
@@ -266,56 +287,62 @@
         n_rows = n_left * rows
         half = outer * rows
 
+        def local(ids, here, half):
+            block = (ids // rows) ^ here
+            return (block % 2 * half + block // 2) * rows + ids % rows
+
+        source = local(source, here_r, far_right)
+        target = local(target, here_l, outer)
+        negative = local(negative, here_l, outer)
+
+        flop = 2 * width * edges
         one_block = shape(width, rows, dtype=BF)
-        right_bf = call(cast_body, one_block, width * rows)(right_t)
-        near = {k: next_column(right_bf, 2 * k) for k in range(outer - 1, 0, -1)}
+        table_bf = shape(width, edges, dtype=BF)
+
+        left_bf, right_bf = call(cast_body, (one_block, one_block), width * rows)(left_t, right_t)
+        near = {0: next_column(right_bf, 0)}
+        for k in range(outer - 1, 0, -1):
+            near[k] = next_column(right_bf, 2 * k)
         other = {0: next_column(right_bf, 1)}
-        near[0] = next_column(right_bf, 0)
-        other[1] = swap_left(near[1], 1)
-        left_bf = call(cast_body, one_block, width * rows, after=(near[1], other[0]))(left_t)
+        weight, left_bf = call(
+            count_body, (shape(groups, n_rows, LANES), one_block), 4 * n_rows * edges, after=(near[0],)
+        )(negative, left_bf)
         half_left = [left_bf] + [swap_right(left_bf, 2 * k) for k in range(1, far_right)]
         half_left = jnp.concatenate(half_left, axis=1)
         sibling_left = swap_right(half_left, 1)
-        for k in range(2, outer):
+        for k in range(1, outer):
             other[k] = swap_left(near[k], 1)
         near = [near[k] for k in range(outer)]
         other = [other[k] for k in range(outer)]
 
-        def local(ids, here, half):
-            block = (ids // rows) ^ here
-            return (block % 2 * half + block // 2) * rows + ids % rows
-
-        source = local(source, here_r, far_right)
-        target = local(target, here_l, outer)
-        negative = local(negative, here_l, outer)
-
-        flop = 2 * width * edges
-        weight = call(count_body, shape(groups, n_rows, LANES), 4 * n_rows * edges)(negative)
-        table_bf = shape(width, edges, dtype=BF)
         s, o, q = call(query_body, (table_bf, table_bf, table_bf), flop * (n_right * rows + nrel))(
             half_left, sibling_left, relation_t, source, kind
         )
         part = pltpu.VMEM((width, half), BF)
-        right_near, qg_near, pack = call(
+        right_near, qg_near = call(
             functools.partial(near_body, outer),
-            (shape(width, half), shape(width, edges), shape(width + 8, rows)),
+            (shape(width, half), shape(width, edges)),
             3 * flop * half,
             [part, pltpu.VMEM((half, edges), BF)],
-        )(*near, q, weight, target, right_t, right_state[None, :])
-        moved = next_column(pack, 0)
+        )(*near, q, weight, target)
         chunk = shape(width, half // 2, dtype=BF)
         m, far_hi, far_lo = call(
-            functools.partial(far_body, outer), (shape(half, edges, dtype=BF), chunk, chunk), 2 * flop * half, [part]
+            functools.partial(far_body, outer),
+            (shape(half, edges, dtype=BF), chunk, chunk),
+            2 * flop * half,
+            [part],
+            after=(qg_near,),
         )(*other, q, weight, target)
         got_hi = swap_left(far_hi, 1)
         got_lo = swap_left(far_lo, 1)
         tall = nrel // LANES * width
         size = -(-tall // (n_right * 16)) * 16
         piece = shape(size, LANES, dtype=BF)
+        core_piece = shape(far_right * width + size, LANES, dtype=BF)
         left_rows = n_right * rows
-        left_near, left_far, *pieces = call(
+        left_near, *pieces = call(
             functools.partial(back_body, outer, n_right),
-            (shape(width, left_rows // 2), shape(width, left_rows // 2, dtype=BF)) + (piece,) * n_right,
+            (shape(width, left_rows // 2), piece, core_piece) + (piece,) * (n_right - 2),
             flop * (half + nrel + left_rows),
             [part, pltpu.VMEM((width, left_rows), F32), pltpu.VMEM((width, nrel), F32),
              pltpu.VMEM((size * n_right, LANES), F32)],
@@ -324,37 +351,39 @@
 
         pieces = [pieces[0]] + [swap_right(pieces[k], k) for k in range(1, n_right)]
         some = outer // 2
-        *high, mine = call(
-            functools.partial(high_body, some, n_right), (one_block,) * some + (piece,), width * half
-        )(right_near, got_hi, *pieces)
+        outs = call(
+            functools.partial(high_body, some, n_right),
+            (one_block,) * some + (piece, shape(width, rows)) + (one_block,) * (far_right - 1),
+            width * half,
+        )(right_near, got_hi, left_near, *pieces)
+        high, mine, left_own, left_blocks = outs[:some], outs[some], outs[some + 1], outs[some + 2:]
         arrived = {some + k: swap_left(block, 2 * (some + k)) for k, block in enumerate(high)}
-        *low, own, mine = call(
+        first = swap_left(mine, 2)
+        left_got = [swap_right(block, 2 * (k + 1)) for k, block in enumerate(left_blocks)]
+        *low, own, mine, pack = call(
             functools.partial(low_body, some),
-            (one_block,) * (some - 1) + (shape(width, rows), piece),
+            (one_block,) * (some - 1) + (shape(width, rows), piece, shape(width + 8, rows)),
             width * half,
-        )(right_near, got_lo, mine, swap_left(mine, 2))
+            after=tuple(left_got),
+        )(right_near, got_lo, mine, first, right_t, right_state[None, :])
         for k, block in enumerate(low):
             arrived[k + 1] = swap_left(block, 2 * (k + 1))
+        moved = next_column(pack, 0)
+        right_got = [arrived[k] for k in range(1, outer)]
+        add = functools.partial(call, sum_body, piece, size * LANES)
         bit = 4
         while bit < n_left:
-            mine = (mine.astype(F32) + swap_left(mine, bit).astype(F32)).astype(BF)
+            mine = add()(mine, swap_left(mine, bit))
             bit *= 2
-        mine = (mine.astype(F32) + swap_left(mine, 1).astype(F32)).astype(BF)
+        mine = add(after=(*right_got, moved))(mine, swap_left(mine, 1))
         pieces = [mine] + [swap_right(mine, k) for k in range(1, n_right)]
-
-        left_near = left_near + swap_right(left_far, 1).astype(F32)
-        left_bf_sum = left_near.astype(BF)
-        left_got = [
-            swap_right(left_bf_sum[:, k * rows:(k + 1) * rows], 2 * k) for k in range(1, far_right)
-        ]
 
         def update(own, got, table, state):
             return call(
                 functools.partial(update_body, len(got)), (shape(width, rows), shape(1, rows)), 8 * width * rows
             )(own, *got, table, state)
 
-        left_new, left_state_new = update(left_near[:, :rows], left_got, left_t, left_state[None, :])
-        right_got = [arrived[k] for k in range(1, outer)]
+        left_new, left_state_new = update(left_own, left_got, left_t, left_state[None, :])
         right_new, right_state_new = update(own, right_got, moved, moved[width:])
         relation_new, relation_state_new = call(
             functools.partial(relation_body, n_right),

time: 62.8 us -> 70.9 us (1.13)
  waiting for transfers between devices: 17 us -> 26 us
  starting transfers between devices: 30.3 us -> 27.6 us
  local copies, waits for them, and re-layouts: 1.93 us -> 3.62 us
    ppermute x11, waiting for transfers between devices: 8.05 us -> 14.1 us  [swap_left(): return lax.ppermute(value, 'left', [(i, i ^ by) for i in range(n_left)])]
    ppermute x10 -> x9, waiting for transfers between devices: 4.54 us -> 8.83 us  [swap_right(): return lax.ppermute(value, 'right', [(i, i ^ by) for i in range(n_right)])]
    ppermute x11, starting transfers between devices: 16.6 us -> 12.5 us  [swap_left(): return lax.ppermute(value, 'left', [(i, i ^ by) for i in range(n_left)])]
    ppermute x10 -> x9, starting transfers between devices: 5.11 us -> 7.19 us  [swap_right(): return lax.ppermute(value, 'right', [(i, i ^ by) for i in range(n_right)])]
    unnamed x18 -> x21, local copies, waits for them, and re-layouts: 1.89 us -> 3.59 us
    ppermute x6, waiting for transfers between devices: 4.38 us -> 3.06 us  [next_column(): return lax.ppermute(value, ('left', 'right'), perm)]
    pallas_call x12 -> x13, Pallas kernels: 10.1 us -> 10.2 us  [run(): pl.pallas_call(inner, out_shape=out_shape, in_specs=specs, scratch_shapes...]
  transfers between devices with their start and end apart: 27 -> 26, of which waited for: 10 -> 13; matrix products, arithmetic and copies ran while one was open for 4% -> 3% of each run, Pallas kernels for 15% -> 8%
where the time goes in v5:
time: 70.9 us; the launch traced here: 70.5 us
  starting transfers between devices  27.6 us (39%)
  waiting for transfers between devices  26 us (37%)
  Pallas kernels  10.2 us (14%)
  local copies, waits for them, and re-layouts  3.62 us (5%)
  other arithmetic  2.29 us (3%)
  between operations  0.81 us (1%)
    ppermute x11, waiting for transfers between devices, swap_left(): return lax.ppermute(value, 'left', [(i, i ^ by) for i in range(n_left)])  14.1 us
    ppermute x11, starting transfers between devices, swap_left(): return lax.ppermute(value, 'left', [(i, i ^ by) for i in range(n_left)])  12.5 us
    pallas_call x13, Pallas kernels, run(): pl.pallas_call(inner, out_shape=out_shape, in_specs=specs, scratch_shapes...  10.2 us
    ppermute x9, waiting for transfers between devices, swap_right(): return lax.ppermute(value, 'right', [(i, i ^ by) for i in range(n_right)])  8.83 us
    ppermute x6, starting transfers between devices, next_column(): return lax.ppermute(value, ('left', 'right'), perm)  7.98 us
    ppermute x9, starting transfers between devices, swap_right(): return lax.ppermute(value, 'right', [(i, i ^ by) for i in range(n_right)])  7.19 us
    unnamed x21, local copies, waits for them, and re-layouts  3.59 us
    ppermute x6, waiting for transfers between devices, next_column(): return lax.ppermute(value, ('left', 'right'), perm)  3.06 us
  transfers between devices with their start and end apart: 26, of which 13 were waited for; matrix products, arithmetic and copies ran while one was open for 3% of the time, Pallas kernels for 8%

profile of v5, /device:TPU:0, one launch (start us, length us, event | category | flops | bytes accessed | tf_op | source)
XLA Modules:
  0.0 70.5 jit_solution(10392726467107858812)
XLA Ops:
  0.6 0.9 %copy-done = f32[128,400]{0,1:T(8,128)S(1)} copy-done((f32[128,400]{0,1:T(8,128)S(1)}, f32[128,400]{0,1:T(8,128)}, u32[]{:S(2)}) %copy-start) | copy-done | bytes 204824
  1.6 0.9 %copy-done.2 = f32[128,400]{0,1:T(8,128)S(1)} copy-done((f32[128,400]{0,1:T(8,128)S(1)}, f32[128,400]{0,1:T(8,128)}, u32[]{:S(2)}) %copy-start.2) | copy-done | bytes 204824
  2.5 2.5 %collective-permute-start.6 = (bf16[400,128]{1,0:T(8,128)(2,1)S(1)}, bf16[400,128]{1,0:T(8,128)(2,1)S(1)}, u32[]{:S(2)}, u32[]{:S(2)}) collective-permute-start(bf16[400,128]{1,0:T(8,128)(2,1)S(1)} %get-tuple-element.38), channel_id=1, source_target_pairs={{0,5},{1,6},{2,7},{3,4},{4,1},{5,2},{6,3},{7,0},{8,13},{9,14},{10,... | collective-permute-start | bytes 307208 | tf_op jit(solution)/shard_map/ppermute | solution.py:269
  5.0 4.8 %collective-permute-start.3 = (bf16[400,128]{1,0:T(8,128)(2,1)S(1)}, bf16[400,128]{1,0:T(8,128)(2,1)S(1)}, u32[]{:S(2)}, u32[]{:S(2)}) collective-permute-start(bf16[400,128]{1,0:T(8,128)(2,1)S(1)} %get-tuple-element.38), channel_id=1, source_target_pairs={{0,25},{1,26},{2,27},{3,24},{4,29},{5,30},{6,31},{7,28},{8,17},{9,... | collective-permute-start | bytes 307208 | tf_op jit(solution)/shard_map/ppermute | solution.py:269
  9.8 0.5 collective-permute-start.1
  10.3 0.2 collective-permute-start
  10.4 0.8 %fusion.2.refs_0_ = s32[2,1024]{1,0:T(2,128)S(1)} fusion(s32[1,1,2,1024]{3,2,1,0:T(2,128)} %param.19, s32[]{:T(128)S(6)} %axis_index.23), kind=kLoop, calls=%fused_computation.32 | loop fusion | flops 88064 | bytes 16388 | tf_op jit(solution)/shard_map/add | solution.py:292
  11.2 0.8 %fusion.4.refs_6_ = s32[1,1024]{1,0:T(1,128)S(1)} fusion(s32[1,1,1024]{2,1,0:T(1,128)} %param.17, s32[]{:T(128)S(6)} %axis_index.23), kind=kLoop, calls=%fused_computation.38 | loop fusion | flops 44032 | bytes 8196 | tf_op jit(solution)/shard_map/add | solution.py:292
  12.0 3.0 %collective-permute-done.refs_2_.refs_0_ = bf16[400,128]{1,0:T(8,128)(2,1)S(1)} collective-permute-done((bf16[400,128]{1,0:T(8,128)(2,1)S(1)}, bf16[400,128]{1,0:T(8,128)(2,1)S(1)}, u32[]{:S(2)}, u32[]{:S(2)}) %collective-permute-start) | collective-permute-done | bytes 102432 | tf_op jit(solution)/shard_map/ppermute | solution.py:269
  15.0 0.9 %shard_map.146 = (f32[2,1024,128]{2,1,0:T(8,128)S(1)}, bf16[400,128]{1,0:T(8,128)(2,1)S(1)}) custom-call(s32[2,1024]{1,0:T(2,128)S(1)} %fusion.2.refs_0_, bf16[400,128]{1,0:T(8,128)(2,1)S(1)} %get-tuple-element.39.refs_1_, bf16[400,128]{1,0:T(8,128)(2,1)S(1)} %collective-permute-done.refs_2_.refs_0_), custom_call_target="tpu_custom_call" | custom-call | flops 4194304 | bytes 110592 | tf_op jit(solution)/shard_map/pallas_call | solution.py:47
  15.9 1.7 %collective-permute-start.4 = (bf16[400,128]{1,0:T(8,128)(2,1)S(1)}, bf16[400,128]{1,0:T(8,128)(2,1)S(1)}, u32[]{:S(2)}, u32[]{:S(2)}) collective-permute-start(bf16[400,128]{1,0:T(8,128)(2,1)S(1)} %get-tuple-element.40), channel_id=1, source_target_pairs={{0,2},{1,3},{2,0},{3,1},{4,6},{5,7},{6,4},{7,5},{8,10},{9,11},{10,... | collective-permute-start | bytes 307208 | tf_op jit(solution)/shard_map/ppermute | solution.py:262
  17.7 3.0 %collective-permute-done.4 = bf16[400,128]{1,0:T(8,128)(2,1)S(1)} collective-permute-done((bf16[400,128]{1,0:T(8,128)(2,1)S(1)}, bf16[400,128]{1,0:T(8,128)(2,1)S(1)}, u32[]{:S(2)}, u32[]{:S(2)}) %collective-permute-start.4) | collective-permute-done | bytes 102432 | tf_op jit(solution)/shard_map/ppermute | solution.py:262
  20.8 0.8 %fusion.3.source_ref.refs_8_ = s32[1,1024]{1,0:T(1,128)S(1)} fusion(s32[1,1,1024]{2,1,0:T(1,128)} %param.16, s32[]{:T(128)} %axis_index.25), kind=kLoop, calls=%fused_computation.37 | loop fusion | flops 44032 | bytes 8196 | tf_op jit(solution)/shard_map/add | solution.py:292
  21.5 0.2 collective-permute-start.9
  21.7 1.9 %collective-permute-start.8 = (bf16[400,128]{1,0:T(8,128)(2,1)S(1)}, bf16[400,128]{1,0:T(8,128)(2,1)S(1)}, u32[]{:S(2)}, u32[]{:S(2)}) collective-permute-start(bf16[400,128]{1,0:T(8,128)(2,1)S(1)} %collective-permute-done.2.refs_2_), channel_id=1, source_target_pairs={{0,4},{4,0},{8,12},{12,8},{16,20},{20,16},{24,28},{28,24},{1,5},{5... | collective-permute-start | bytes 307208 | tf_op jit(solution)/shard_map/ppermute | solution.py:259
  23.6 0.2 collective-permute-start.7
  23.8 1.0 %copy-done.4 = f32[256,400]{0,1:T(8,128)S(1)} copy-done((f32[256,400]{0,1:T(8,128)S(1)}, f32[256,400]{0,1:T(8,128)}, u32[]{:S(2)}) %copy-start.4) | copy-done | bytes 409624
  24.8 0.7 copy-done.6
  25.5 0.9 %shard_map.147 = (bf16[400,1024]{1,0:T(8,128)(2,1)S(1)}, bf16[400,1024]{1,0:T(8,128)(2,1)S(1)}, bf16[400,1024]{1,0:T(8,128)(2,1)S(1)}) custom-call(bf16[400,256]{1,0:T(8,128)(2,1)S(1)} %constant_dynamic-update-slice_fusion.near_ref, bf16[400,256]{1,0:T(8,128)(2,1)S(1)} %collective-permute-done.5.sibling_ref, f32[400,256]{1,0:T(8,128)S(1)} %bitcast.58, ...), custom_call_target="tpu_custom_call" | custom-call | flops 629145600 | bytes 827392 | tf_op jit(solution)/shard_map/pallas_call | solution.py:47
  26.4 1.9 %shard_map.148 = (f32[400,512]{1,0:T(8,128)S(1)}, f32[400,1024]{1,0:T(8,128)S(1)}) custom-call(bf16[400,128]{1,0:T(8,128)(2,1)S(1)} %collective-permute-done.refs_2_.refs_0_, bf16[400,128]{1,0:T(8,128)(2,1)S(1)} %collective-permute-done.1.refs_1_, bf16[400,128]{1,0:T(8,128)(2,1)S(1)} %collective-permute-done.2.refs_2_, ...), custom_call_target="tpu_custom_call" | custom-call | flops 1258291200 | bytes 2281472 | tf_op jit(solution)/shard_map/pallas_call | solution.py:47
  28.3 1.2 %collective-permute-done.8.refs_2_ = bf16[400,128]{1,0:T(8,128)(2,1)S(1)} collective-permute-done((bf16[400,128]{1,0:T(8,128)(2,1)S(1)}, bf16[400,128]{1,0:T(8,128)(2,1)S(1)}, u32[]{:S(2)}, u32[]{:S(2)}) %collective-permute-start.8) | collective-permute-done | bytes 102432 | tf_op jit(solution)/shard_map/ppermute | solution.py:259
  29.5 1.8 %collective-permute-done.7.refs_1_ = bf16[400,128]{1,0:T(8,128)(2,1)S(1)} collective-permute-done((bf16[400,128]{1,0:T(8,128)(2,1)S(1)}, bf16[400,128]{1,0:T(8,128)(2,1)S(1)}, u32[]{:S(2)}, u32[]{:S(2)}) %collective-permute-start.7) | collective-permute-done | bytes 102432 | tf_op jit(solution)/shard_map/ppermute | solution.py:259
  31.3 1.5 %shard_map.149 = (bf16[512,1024]{1,0:T(8,128)(2,1)S(1)}, bf16[400,256]{1,0:T(8,128)(2,1)S(1)}, bf16[400,256]{1,0:T(8,128)(2,1)S(1)}) custom-call(bf16[400,128]{1,0:T(8,128)(2,1)S(1)} %collective-permute-done.6.refs_0_, bf16[400,128]{1,0:T(8,128)(2,1)S(1)} %collective-permute-done.7.refs_1_, bf16[400,128]{1,0:T(8,128)(2,1)S(1)} %collective-permute-done.8.refs_2_, ...), custom_call_target="tpu_custom_call" | custom-call | flops 838860800 | bytes 2281472 | tf_op jit(solution)/shard_map/pallas_call | solution.py:47
  32.8 2.2 %shard_map.150 = (f32[400,256]{1,0:T(8,128)S(1)}, bf16[208,128]{1,0:T(8,128)(2,1)S(1)}, bf16[1008,128]{1,0:T(8,128)(2,1)S(1)}, bf16[208,128]{1,0:T(8,128)(2,1)S(1)}, bf16[208,128]{1,0:T(8,128)(2,1)S(1)}) custom-call(bf16[400,128]{1,0:T(8,128)(2,1)S(1)} %collective-permute-done.6.refs_0_, bf16[400,128]{1,0:T(8,128)(2,1)S(1)} %collective-permute-done.7.refs_1_, ...), custom_call_target="tpu_custom_call" | custom-call | flops 1048576000 | bytes 4743168 | tf_op jit(solution)/shard_map/pallas_call | solution.py:47
  35.1 0.3 collective-permute-start.10
  35.5 1.7 %collective-permute-start.15 = (bf16[400,256]{1,0:T(8,128)(2,1)S(1)}, bf16[400,256]{1,0:T(8,128)(2,1)S(1)}, u32[]{:S(2)}, u32[]{:S(2)}) collective-permute-start(bf16[400,256]{1,0:T(8,128)(2,1)S(1)} %get-tuple-element.58), channel_id=1, source_target_pairs={{0,4},{4,0},{8,12},{12,8},{16,20},{20,16},{24,28},{28,24},{1,5},{5... | collective-permute-start | bytes 614408 | tf_op jit(solution)/shard_map/ppermute | solution.py:259
  37.2 1.7 %collective-permute-start.12 = (bf16[208,128]{1,0:T(8,128)(2,1)S(1)}, bf16[208,128]{1,0:T(8,128)(2,1)S(1)}, u32[]{:S(2)}, u32[]{:S(2)}) collective-permute-start(bf16[208,128]{1,0:T(8,128)(2,1)S(1)} %get-tuple-element.52), channel_id=1, source_target_pairs={{0,2},{1,3},{2,0},{3,1},{4,6},{5,7},{6,4},{7,5},{8,10},{9,11},{10,... | collective-permute-start | bytes 159752 | tf_op jit(solution)/shard_map/ppermute | solution.py:262
  38.9 2.5 %collective-permute-done.12.refs_2_ = bf16[208,128]{1,0:T(8,128)(2,1)S(1)} collective-permute-done((bf16[208,128]{1,0:T(8,128)(2,1)S(1)}, bf16[208,128]{1,0:T(8,128)(2,1)S(1)}, u32[]{:S(2)}, u32[]{:S(2)}) %collective-permute-start.12) | collective-permute-done | bytes 53280 | tf_op jit(solution)/shard_map/ppermute | solution.py:262
  41.4 1.4 %collective-permute-done.13.refs_3_ = bf16[208,128]{1,0:T(8,128)(2,1)S(1)} collective-permute-done((bf16[208,128]{1,0:T(8,128)(2,1)S(1)}, bf16[208,128]{1,0:T(8,128)(2,1)S(1)}, u32[]{:S(2)}, u32[]{:S(2)}) %collective-permute-start.13) | collective-permute-done | bytes 53280 | tf_op jit(solution)/shard_map/ppermute | solution.py:262
  42.8 0.3 collective-permute-done.10.got_ref
  43.1 0.1 shard_map.151
  43.2 1.7 %collective-permute-start.14 = (bf16[400,128]{1,0:T(8,128)(2,1)S(1)}, bf16[400,128]{1,0:T(8,128)(2,1)S(1)}, u32[]{:S(2)}, u32[]{:S(2)}) collective-permute-start(bf16[400,128]{1,0:T(8,128)(2,1)S(1)} %get-tuple-element.55), channel_id=1, source_target_pairs={{0,2},{1,3},{2,0},{3,1},{4,6},{5,7},{6,4},{7,5},{8,10},{9,11},{10,... | collective-permute-start | bytes 307208 | tf_op jit(solution)/shard_map/ppermute | solution.py:262
  44.9 0.7 %collective-permute-start.16 = (bf16[208,128]{1,0:T(8,128)(2,1)S(1)}, bf16[208,128]{1,0:T(8,128)(2,1)S(1)}, u32[]{:S(2)}, u32[]{:S(2)}) collective-permute-start(bf16[208,128]{1,0:T(8,128)(2,1)S(1)} %get-tuple-element.59.refs_2_), channel_id=1, source_target_pairs={{0,8},{4,12},{8,0},{12,4},{16,24},{20,28},{24,16},{28,20},{1,9},{5... | collective-permute-start | bytes 159752 | tf_op jit(solution)/shard_map/ppermute | solution.py:259
  45.7 1.3 %collective-permute-done.15.refs_1_ = bf16[400,256]{1,0:T(8,128)(2,1)S(1)} collective-permute-done((bf16[400,256]{1,0:T(8,128)(2,1)S(1)}, bf16[400,256]{1,0:T(8,128)(2,1)S(1)}, u32[]{:S(2)}, u32[]{:S(2)}) %collective-permute-start.15) | collective-permute-done | bytes 204832 | tf_op jit(solution)/shard_map/ppermute | solution.py:259
  47.0 2.1 %collective-permute-done.16.refs_3_ = bf16[208,128]{1,0:T(8,128)(2,1)S(1)} collective-permute-done((bf16[208,128]{1,0:T(8,128)(2,1)S(1)}, bf16[208,128]{1,0:T(8,128)(2,1)S(1)}, u32[]{:S(2)}, u32[]{:S(2)}) %collective-permute-start.16) | collective-permute-done | bytes 53280 | tf_op jit(solution)/shard_map/ppermute | solution.py:259
  49.3 3.1 %collective-permute-start.21 = (bf16[208,128]{1,0:T(8,128)(2,1)S(1)}, bf16[208,128]{1,0:T(8,128)(2,1)S(1)}, u32[]{:S(2)}, u32[]{:S(2)}) collective-permute-start(bf16[208,128]{1,0:T(8,128)(2,1)S(1)} %get-tuple-element.67.piece_ref), channel_id=1, source_target_pairs={{0,16},{4,20},{8,24},{12,28},{16,0},{20,4},{24,8},{28,12},{1,17},{... | collective-permute-start | bytes 159752 | tf_op jit(solution)/shard_map/ppermute | solution.py:259
  52.4 3.7 %collective-permute-start.19 = (bf16[400,128]{1,0:T(8,128)(2,1)S(1)}, bf16[400,128]{1,0:T(8,128)(2,1)S(1)}, u32[]{:S(2)}, u32[]{:S(2)}) collective-permute-start(bf16[400,128]{1,0:T(8,128)(2,1)S(1)} %get-tuple-element.63), channel_id=1, source_target_pairs={{0,24},{4,28},{8,16},{12,20},{16,8},{20,12},{24,0},{28,4},{1,25},{... | collective-permute-start | bytes 307208 | tf_op jit(solution)/shard_map/ppermute | solution.py:259
  56.1 0.5 collective-permute-start.22
  56.7 6.7 %collective-permute-done.18.refs_1_.refs_3_ = bf16[400,128]{1,0:T(8,128)(2,1)S(1)} collective-permute-done((bf16[400,128]{1,0:T(8,128)(2,1)S(1)}, bf16[400,128]{1,0:T(8,128)(2,1)S(1)}, u32[]{:S(2)}, u32[]{:S(2)}) %collective-permute-start.18) | collective-permute-done | bytes 102432 | tf_op jit(solution)/shard_map/ppermute | solution.py:259
  63.4 0.8 %collective-permute-done.17.refs_0_.refs_2_ = bf16[400,128]{1,0:T(8,128)(2,1)S(1)} collective-permute-done((bf16[400,128]{1,0:T(8,128)(2,1)S(1)}, bf16[400,128]{1,0:T(8,128)(2,1)S(1)}, u32[]{:S(2)}, u32[]{:S(2)}) %collective-permute-start.17) | collective-permute-done | bytes 102432 | tf_op jit(solution)/shard_map/ppermute | solution.py:259
  64.2 1.1 %collective-permute-start.25 = (bf16[208,128]{1,0:T(8,128)(2,1)S(1)}, bf16[208,128]{1,0:T(8,128)(2,1)S(1)}, u32[]{:S(2)}, u32[]{:S(2)}) collective-permute-start(bf16[208,128]{1,0:T(8,128)(2,1)S(1)} %shard_map.156.refs_0_), channel_id=1, source_target_pairs={{0,3},{1,2},{2,1},{3,0},{4,7},{5,6},{6,5},{7,4},{8,11},{9,10},{10,... | collective-permute-start | bytes 159752 | tf_op jit(solution)/shard_map/ppermute | solution.py:262
  65.3 0.6 collective-permute-start.24
  65.9 0.3 collective-permute-start.23
  66.1 0.8 %shard_map.152 = (f32[400,128]{1,0:T(8,128)}, f32[1,128]{1,0:T(1,128)}) custom-call(f32[400,128]{1,0:T(8,128)S(1)} %get-tuple-element.54.own_ref, bf16[400,128]{1,0:T(8,128)(2,1)S(1)} %collective-permute-done.14.refs_0_.refs_6_, f32[400,128]{1,0:T(8,128)S(1)} %bitcast.55, f32[1,128]{1,0:T(1,128)S(1)} %bitcast.64), custom_call_target="tpu_custom_call" | custom-call | flops 409600 | bytes 512512 | tf_op jit(solution)/shard_map/pallas_call | solution.py:47
  66.9 0.8 %shard_map.154 = (f32[400,128]{1,0:T(8,128)}, f32[1,128]{1,0:T(1,128)}) custom-call(f32[400,128]{1,0:T(8,128)S(1)} %get-tuple-element.60.own_ref, bf16[400,128]{1,0:T(8,128)(2,1)S(1)} %collective-permute-done.17.refs_0_.refs_2_, bf16[400,128]{1,0:T(8,128)(2,1)S(1)} %collective-permute-done.18.refs_1_.refs_3_, ...), custom_call_target="tpu_custom_call" | custom-call | flops 409600 | bytes 724992 | tf_op jit(solution)/shard_map/pallas_call | solution.py:47
  67.7 0.6 collective-permute-done.25.refs_3_
  68.3 1.3 %collective-permute-done.24.refs_2_ = bf16[208,128]{1,0:T(8,128)(2,1)S(1)} collective-permute-done((bf16[208,128]{1,0:T(8,128)(2,1)S(1)}, bf16[208,128]{1,0:T(8,128)(2,1)S(1)}, u32[]{:S(2)}, u32[]{:S(2)}) %collective-permute-start.24) | collective-permute-done | bytes 53280 | tf_op jit(solution)/shard_map/ppermute | solution.py:262
  69.6 0.9 %shard_map.157 = (f32[400,256]{1,0:T(8,128)}, f32[1,256]{1,0:T(1,128)}) custom-call(bf16[208,128]{1,0:T(8,128)(2,1)S(1)} %shard_map.156.refs_0_, bf16[208,128]{1,0:T(8,128)(2,1)S(1)} %collective-permute-done.23.refs_1_, bf16[208,128]{1,0:T(8,128)(2,1)S(1)} %collective-permute-done.24.refs_2_, bf16[208,128]{1,0:T(8,128)(2,1)S(1)} %collective-permute-done.25.refs_3_, ...), custom_call_target="tpu_custom_call" | custom-call | flops 819200 | bytes 623616 | tf_op jit(solution)/shard_map/pallas_call | solution.py:47
  (43 shorter events, 0.6 us)
Async XLA Ops:
  0.6 0.9 %copy-start = (f32[128,400]{0,1:T(8,128)S(1)}, f32[128,400]{0,1:T(8,128)}, u32[]{:S(2)}) copy-start(f32[128,400]{0,1:T(8,128)} %param.10) | copy-start | bytes 614404
  1.6 0.9 %copy-start.2 = (f32[128,400]{0,1:T(8,128)S(1)}, f32[128,400]{0,1:T(8,128)}, u32[]{:S(2)}) copy-start(f32[128,400]{0,1:T(8,128)} %param.12) | copy-start | bytes 614404
  2.5 25.7 %collective-permute-start.6 = (bf16[400,128]{1,0:T(8,128)(2,1)S(1)}, bf16[400,128]{1,0:T(8,128)(2,1)S(1)}, u32[]{:S(2)}, u32[]{:S(2)}) collective-permute-start(bf16[400,128]{1,0:T(8,128)(2,1)S(1)} %get-tuple-element.38), channel_id=1, source_target_pairs={{0,5},{1,6},{2,7},{3,4},{4,1},{5,2},{6,3},{7,0},{8,13},{9,14},{10,... | collective-permute-start | bytes 307208 | tf_op jit(solution)/shard_map/ppermute | solution.py:269
  5.0 16.5 %collective-permute-start.3 = (bf16[400,128]{1,0:T(8,128)(2,1)S(1)}, bf16[400,128]{1,0:T(8,128)(2,1)S(1)}, u32[]{:S(2)}, u32[]{:S(2)}) collective-permute-start(bf16[400,128]{1,0:T(8,128)(2,1)S(1)} %get-tuple-element.38), channel_id=1, source_target_pairs={{0,25},{1,26},{2,27},{3,24},{4,29},{5,30},{6,31},{7,28},{8,17},{9,... | collective-permute-start | bytes 307208 | tf_op jit(solution)/shard_map/ppermute | solution.py:269
  9.8 12.0 %collective-permute-start.2 = (bf16[400,128]{1,0:T(8,128)(2,1)S(1)}, bf16[400,128]{1,0:T(8,128)(2,1)S(1)}, u32[]{:S(2)}, u32[]{:S(2)}) collective-permute-start(bf16[400,128]{1,0:T(8,128)(2,1)S(1)} %get-tuple-element.38), channel_id=1, source_target_pairs={{0,17},{1,18},{2,19},{3,16},{4,21},{5,22},{6,23},{7,20},{8,25},{9,... | collective-permute-start | bytes 307208 | tf_op jit(solution)/shard_map/ppermute | solution.py:269
  9.8 13.8 %collective-permute-start.1 = (bf16[400,128]{1,0:T(8,128)(2,1)S(1)}, bf16[400,128]{1,0:T(8,128)(2,1)S(1)}, u32[]{:S(2)}, u32[]{:S(2)}) collective-permute-start(bf16[400,128]{1,0:T(8,128)(2,1)S(1)} %get-tuple-element.38), channel_id=1, source_target_pairs={{0,9},{1,10},{2,11},{3,8},{4,13},{5,14},{6,15},{7,12},{8,1},{9,2},... | collective-permute-start | bytes 307208 | tf_op jit(solution)/shard_map/ppermute | solution.py:269
  10.3 4.8 %collective-permute-start = (bf16[400,128]{1,0:T(8,128)(2,1)S(1)}, bf16[400,128]{1,0:T(8,128)(2,1)S(1)}, u32[]{:S(2)}, u32[]{:S(2)}) collective-permute-start(bf16[400,128]{1,0:T(8,128)(2,1)S(1)} %get-tuple-element.38), channel_id=1, source_target_pairs={{0,1},{1,2},{2,3},{3,0},{4,5},{5,6},{6,7},{7,4},{8,9},{9,10},{10,1... | collective-permute-start | bytes 307208 | tf_op jit(solution)/shard_map/ppermute | solution.py:269
  15.9 4.7 %collective-permute-start.4 = (bf16[400,128]{1,0:T(8,128)(2,1)S(1)}, bf16[400,128]{1,0:T(8,128)(2,1)S(1)}, u32[]{:S(2)}, u32[]{:S(2)}) collective-permute-start(bf16[400,128]{1,0:T(8,128)(2,1)S(1)} %get-tuple-element.40), channel_id=1, source_target_pairs={{0,2},{1,3},{2,0},{3,1},{4,6},{5,7},{6,4},{7,5},{8,10},{9,11},{10,... | collective-permute-start | bytes 307208 | tf_op jit(solution)/shard_map/ppermute | solution.py:262
  20.7 3.1 %collective-permute-start.5 = (bf16[400,256]{1,0:T(8,128)(2,1)S(1)}, bf16[400,256]{1,0:T(8,128)(2,1)S(1)}, u32[]{:S(2)}, u32[]{:S(2)}) collective-permute-start(bf16[400,256]{1,0:T(8,128)(2,1)S(1)} %constant_dynamic-update-slice_fusion.near_ref), channel_id=1, source_target_pairs={{0,1},{1,0},{2,3},{3,2},{4,5},{5,4},{6,7},{7,6},{8,9},{9,8},{10,11... | collective-permute-start | bytes 614408 | tf_op jit(solution)/shard_map/ppermute | solution.py:262
  21.5 6.7 %collective-permute-start.9 = (bf16[400,128]{1,0:T(8,128)(2,1)S(1)}, bf16[400,128]{1,0:T(8,128)(2,1)S(1)}, u32[]{:S(2)}, u32[]{:S(2)}) collective-permute-start(bf16[400,128]{1,0:T(8,128)(2,1)S(1)} %collective-permute-done.3.refs_3_), channel_id=1, source_target_pairs={{0,4},{4,0},{8,12},{12,8},{16,20},{20,16},{24,28},{28,24},{1,5},{5... | collective-permute-start | bytes 307208 | tf_op jit(solution)/shard_map/ppermute | solution.py:259
  21.7 7.7 %collective-permute-start.8 = (bf16[400,128]{1,0:T(8,128)(2,1)S(1)}, bf16[400,128]{1,0:T(8,128)(2,1)S(1)}, u32[]{:S(2)}, u32[]{:S(2)}) collective-permute-start(bf16[400,128]{1,0:T(8,128)(2,1)S(1)} %collective-permute-done.2.refs_2_), channel_id=1, source_target_pairs={{0,4},{4,0},{8,12},{12,8},{16,20},{20,16},{24,28},{28,24},{1,5},{5... | collective-permute-start | bytes 307208 | tf_op jit(solution)/shard_map/ppermute | solution.py:259
  23.6 7.6 %collective-permute-start.7 = (bf16[400,128]{1,0:T(8,128)(2,1)S(1)}, bf16[400,128]{1,0:T(8,128)(2,1)S(1)}, u32[]{:S(2)}, u32[]{:S(2)}) collective-permute-start(bf16[400,128]{1,0:T(8,128)(2,1)S(1)} %collective-permute-done.1.refs_1_), channel_id=1, source_target_pairs={{0,4},{4,0},{8,12},{12,8},{16,20},{20,16},{24,28},{28,24},{1,5},{5... | collective-permute-start | bytes 307208 | tf_op jit(solution)/shard_map/ppermute | solution.py:259
  23.8 1.0 %copy-start.4 = (f32[256,400]{0,1:T(8,128)S(1)}, f32[256,400]{0,1:T(8,128)}, u32[]{:S(2)}) copy-start(f32[256,400]{0,1:T(8,128)} %param.14) | copy-start | bytes 1228804
  24.8 0.7 copy-start.6
  35.0 14.1 %copy-start.3 = (f32[128,400]{0,1:T(8,128)S(1)}, f32[128,400]{0,1:T(8,128)}, u32[]{:S(2)}) copy-start(f32[128,400]{0,1:T(8,128)} %param.12) | copy-start | bytes 614404
  35.0 14.1 %copy-start.8 = (f32[128]{0:T(128)S(1)}, f32[128]{0:T(128)}, u32[]{:S(2)}) copy-start(f32[128]{0:T(128)} %param.13) | copy-start | bytes 1540
  35.0 8.0 %collective-permute-start.11 = (bf16[1008,128]{1,0:T(8,128)(2,1)S(1)}, bf16[1008,128]{1,0:T(8,128)(2,1)S(1)}, u32[]{:S(2)}, u32[]{:S(2)}) collective-permute-start(bf16[1008,128]{1,0:T(8,128)(2,1)S(1)} %get-tuple-element.51), channel_id=1, source_target_pairs={{0,1},{1,0},{2,3},{3,2},{4,5},{5,4},{6,7},{7,6},{8,9},{9,8},{10,11... | collective-permute-start | bytes 774152 | tf_op jit(solution)/shard_map/ppermute | solution.py:262
  35.1 7.9 %collective-permute-start.10 = (bf16[400,256]{1,0:T(8,128)(2,1)S(1)}, bf16[400,256]{1,0:T(8,128)(2,1)S(1)}, u32[]{:S(2)}, u32[]{:S(2)}) collective-permute-start(bf16[400,256]{1,0:T(8,128)(2,1)S(1)} %get-tuple-element.45), channel_id=1, source_target_pairs={{0,4},{4,0},{8,12},{12,8},{16,20},{20,16},{24,28},{28,24},{1,5},{5... | collective-permute-start | bytes 614408 | tf_op jit(solution)/shard_map/ppermute | solution.py:259
  35.5 11.5 %collective-permute-start.15 = (bf16[400,256]{1,0:T(8,128)(2,1)S(1)}, bf16[400,256]{1,0:T(8,128)(2,1)S(1)}, u32[]{:S(2)}, u32[]{:S(2)}) collective-permute-start(bf16[400,256]{1,0:T(8,128)(2,1)S(1)} %get-tuple-element.58), channel_id=1, source_target_pairs={{0,4},{4,0},{8,12},{12,8},{16,20},{20,16},{24,28},{28,24},{1,5},{5... | collective-permute-start | bytes 614408 | tf_op jit(solution)/shard_map/ppermute | solution.py:259
  37.2 4.1 %collective-permute-start.12 = (bf16[208,128]{1,0:T(8,128)(2,1)S(1)}, bf16[208,128]{1,0:T(8,128)(2,1)S(1)}, u32[]{:S(2)}, u32[]{:S(2)}) collective-permute-start(bf16[208,128]{1,0:T(8,128)(2,1)S(1)} %get-tuple-element.52), channel_id=1, source_target_pairs={{0,2},{1,3},{2,0},{3,1},{4,6},{5,7},{6,4},{7,5},{8,10},{9,11},{10,... | collective-permute-start | bytes 159752 | tf_op jit(solution)/shard_map/ppermute | solution.py:262
  38.9 3.9 %collective-permute-start.13 = (bf16[208,128]{1,0:T(8,128)(2,1)S(1)}, bf16[208,128]{1,0:T(8,128)(2,1)S(1)}, u32[]{:S(2)}, u32[]{:S(2)}) collective-permute-start(bf16[208,128]{1,0:T(8,128)(2,1)S(1)} %get-tuple-element.53), channel_id=1, source_target_pairs={{0,3},{1,2},{2,1},{3,0},{4,7},{5,6},{6,5},{7,4},{8,11},{9,10},{10,... | collective-permute-start | bytes 159752 | tf_op jit(solution)/shard_map/ppermute | solution.py:262
  43.1 23.0 %copy-start.1 = (f32[128,400]{0,1:T(8,128)S(1)}, f32[128,400]{0,1:T(8,128)}, u32[]{:S(2)}) copy-start(f32[128,400]{0,1:T(8,128)} %param.10) | copy-start | bytes 614404
  43.1 23.0 %copy-start.9 = (f32[128]{0:T(128)S(1)}, f32[128]{0:T(128)}, u32[]{:S(2)}) copy-start(f32[128]{0:T(128)} %param.11) | copy-start | bytes 1540
  43.2 5.9 %collective-permute-start.14 = (bf16[400,128]{1,0:T(8,128)(2,1)S(1)}, bf16[400,128]{1,0:T(8,128)(2,1)S(1)}, u32[]{:S(2)}, u32[]{:S(2)}) collective-permute-start(bf16[400,128]{1,0:T(8,128)(2,1)S(1)} %get-tuple-element.55), channel_id=1, source_target_pairs={{0,2},{1,3},{2,0},{3,1},{4,6},{5,7},{6,4},{7,5},{8,10},{9,11},{10,... | collective-permute-start | bytes 307208 | tf_op jit(solution)/shard_map/ppermute | solution.py:262
  44.9 4.1 %collective-permute-start.16 = (bf16[208,128]{1,0:T(8,128)(2,1)S(1)}, bf16[208,128]{1,0:T(8,128)(2,1)S(1)}, u32[]{:S(2)}, u32[]{:S(2)}) collective-permute-start(bf16[208,128]{1,0:T(8,128)(2,1)S(1)} %get-tuple-element.59.refs_2_), channel_id=1, source_target_pairs={{0,8},{4,12},{8,0},{12,4},{16,24},{20,28},{24,16},{28,20},{1,9},{5... | collective-permute-start | bytes 159752 | tf_op jit(solution)/shard_map/ppermute | solution.py:259
  49.1 20.5 %copy-start.5 = (f32[256,400]{0,1:T(8,128)S(1)}, f32[256,400]{0,1:T(8,128)}, u32[]{:S(2)}) copy-start(f32[256,400]{0,1:T(8,128)} %param.14) | copy-start | bytes 1228804
  49.1 20.5 %copy-start.7 = (f32[256]{0:T(256)S(1)}, f32[256]{0:T(256)}, u32[]{:S(2)}) copy-start(f32[256]{0:T(256)} %param.15) | copy-start | bytes 3076
  49.2 15.0 %collective-permute-start.20 = (f32[408,128]{1,0:T(8,128)S(1)}, f32[408,128]{1,0:T(8,128)S(1)}, u32[]{:S(2)}, u32[]{:S(2)}) collective-permute-start(f32[408,128]{1,0:T(8,128)S(1)} %get-tuple-element.64), channel_id=1, source_target_pairs={{0,1},{1,2},{2,3},{3,0},{4,5},{5,6},{6,7},{7,4},{8,9},{9,10},{10,1... | collective-permute-start | bytes 626696 | tf_op jit(solution)/shard_map/ppermute | solution.py:269
  49.3 6.9 %collective-permute-start.21 = (bf16[208,128]{1,0:T(8,128)(2,1)S(1)}, bf16[208,128]{1,0:T(8,128)(2,1)S(1)}, u32[]{:S(2)}, u32[]{:S(2)}) collective-permute-start(bf16[208,128]{1,0:T(8,128)(2,1)S(1)} %get-tuple-element.67.piece_ref), channel_id=1, source_target_pairs={{0,16},{4,20},{8,24},{12,28},{16,0},{20,4},{24,8},{28,12},{1,17},{... | collective-permute-start | bytes 159752 | tf_op jit(solution)/shard_map/ppermute | solution.py:259
  52.3 11.1 %collective-permute-start.18 = (bf16[400,128]{1,0:T(8,128)(2,1)S(1)}, bf16[400,128]{1,0:T(8,128)(2,1)S(1)}, u32[]{:S(2)}, u32[]{:S(2)}) collective-permute-start(bf16[400,128]{1,0:T(8,128)(2,1)S(1)} %get-tuple-element.62), channel_id=1, source_target_pairs={{0,16},{4,20},{8,24},{12,28},{16,0},{20,4},{24,8},{28,12},{1,17},{... | collective-permute-start | bytes 307208 | tf_op jit(solution)/shard_map/ppermute | solution.py:259
  52.4 11.0 %collective-permute-start.19 = (bf16[400,128]{1,0:T(8,128)(2,1)S(1)}, bf16[400,128]{1,0:T(8,128)(2,1)S(1)}, u32[]{:S(2)}, u32[]{:S(2)}) collective-permute-start(bf16[400,128]{1,0:T(8,128)(2,1)S(1)} %get-tuple-element.63), channel_id=1, source_target_pairs={{0,24},{4,28},{8,16},{12,20},{16,8},{20,12},{24,0},{28,4},{1,25},{... | collective-permute-start | bytes 307208 | tf_op jit(solution)/shard_map/ppermute | solution.py:259
  56.1 8.1 %collective-permute-start.17 = (bf16[400,128]{1,0:T(8,128)(2,1)S(1)}, bf16[400,128]{1,0:T(8,128)(2,1)S(1)}, u32[]{:S(2)}, u32[]{:S(2)}) collective-permute-start(bf16[400,128]{1,0:T(8,128)(2,1)S(1)} %get-tuple-element.61), channel_id=1, source_target_pairs={{0,8},{4,12},{8,0},{12,4},{16,24},{20,28},{24,16},{28,20},{1,9},{5... | collective-permute-start | bytes 307208 | tf_op jit(solution)/shard_map/ppermute | solution.py:259
  56.1 8.0 %collective-permute-start.22 = (bf16[208,128]{1,0:T(8,128)(2,1)S(1)}, bf16[208,128]{1,0:T(8,128)(2,1)S(1)}, u32[]{:S(2)}, u32[]{:S(2)}) collective-permute-start(bf16[208,128]{1,0:T(8,128)(2,1)S(1)} %shard_map.155.refs_0_), channel_id=1, source_target_pairs={{0,4},{4,0},{8,12},{12,8},{16,20},{20,16},{24,28},{28,24},{1,5},{5... | collective-permute-start | bytes 159752 | tf_op jit(solution)/shard_map/ppermute | solution.py:259
  64.2 4.1 %collective-permute-start.25 = (bf16[208,128]{1,0:T(8,128)(2,1)S(1)}, bf16[208,128]{1,0:T(8,128)(2,1)S(1)}, u32[]{:S(2)}, u32[]{:S(2)}) collective-permute-start(bf16[208,128]{1,0:T(8,128)(2,1)S(1)} %shard_map.156.refs_0_), channel_id=1, source_target_pairs={{0,3},{1,2},{2,1},{3,0},{4,7},{5,6},{6,5},{7,4},{8,11},{9,10},{10,... | collective-permute-start | bytes 159752 | tf_op jit(solution)/shard_map/ppermute | solution.py:262
  65.3 4.4 %collective-permute-start.24 = (bf16[208,128]{1,0:T(8,128)(2,1)S(1)}, bf16[208,128]{1,0:T(8,128)(2,1)S(1)}, u32[]{:S(2)}, u32[]{:S(2)}) collective-permute-start(bf16[208,128]{1,0:T(8,128)(2,1)S(1)} %shard_map.156.refs_0_), channel_id=1, source_target_pairs={{0,2},{1,3},{2,0},{3,1},{4,6},{5,7},{6,4},{7,5},{8,10},{9,11},{10,... | collective-permute-start | bytes 159752 | tf_op jit(solution)/shard_map/ppermute | solution.py:262
  65.9 3.8 %collective-permute-start.23 = (bf16[208,128]{1,0:T(8,128)(2,1)S(1)}, bf16[208,128]{1,0:T(8,128)(2,1)S(1)}, u32[]{:S(2)}, u32[]{:S(2)}) collective-permute-start(bf16[208,128]{1,0:T(8,128)(2,1)S(1)} %shard_map.156.refs_0_), channel_id=1, source_target_pairs={{0,1},{1,0},{2,3},{3,2},{4,5},{5,4},{6,7},{7,6},{8,9},{9,8},{10,11... | collective-permute-start | bytes 159752 | tf_op jit(solution)/shard_map/ppermute | solution.py:262

commit v6 on v5

--- a/solution.py
+++ b/solution.py
@@ -28,9 +28,8 @@
     return most if size % most == 0 else size
 
 
-def call(body, out_shape, flops, scratch=(), here=None, after=()):
+def call(body, out_shape, scratch=(), here=None, after=()):
     def run(*args):
-        moved = sum(a.size * a.dtype.itemsize for a in args)
         specs = [pl.BlockSpec(memory_space=pltpu.VMEM)] * len(args)
         if here is not None:
             specs.append(pl.BlockSpec(memory_space=pltpu.SMEM))
@@ -50,7 +49,7 @@
             in_specs=specs,
             scratch_shapes=list(scratch),
             compiler_params=pltpu.CompilerParams(vmem_limit_bytes=VMEM_LIMIT),
-            cost_estimate=pl.CostEstimate(flops=flops, bytes_accessed=moved, transcendentals=0),
+            cost_estimate=pl.CostEstimate(flops=0, bytes_accessed=0, transcendentals=0),
         )(*args)
 
     return run
@@ -60,32 +59,39 @@
     return jax.ShapeDtypeStruct(dims, dtype)
 
 
-def cast_body(left_ref, right_ref, left_bf_ref, right_bf_ref):
-    right_bf_ref[...] = right_ref[...].astype(BF)
-    left_bf_ref[...] = left_ref[...].astype(BF)
-
-
-def count_body(ids_ref, left_ref, out_ref, left_out_ref):
-    left_out_ref[...] = left_ref[...]
-    for g in range(out_ref.shape[0]):
-        ids = ids_ref[g:g + 1, :]
+def cast_body(in_ref, out_ref):
+    out_ref[...] = in_ref[...].astype(BF)
+
+
+def count_body(edges, ids_ref, relation_ref, table_ref, state_ref, out_ref, relation_bf_ref, pack_ref):
+    groups = out_ref.shape[0]
+    slots = (ids_ref.shape[1] - 3 * edges) // groups
+    for g in range(groups):
+        ids = ids_ref[:, 3 * edges + g * slots:3 * edges + (g + 1) * slots]
         for at in range(0, out_ref.shape[1], LANES):
-            spot = lax.broadcasted_iota(jnp.int32, (LANES, ids.shape[1]), 0) + at
+            spot = lax.broadcasted_iota(jnp.int32, (LANES, slots), 0) + at
             total = jnp.sum(jnp.where(spot == ids, NEG_WEIGHT, 0.0), axis=1, keepdims=True)
             out_ref[g, at:at + LANES, :] = jnp.broadcast_to(total, (LANES, LANES))
-
-
-def query_body(near_ref, sibling_ref, relation_ref, source_ref, kind_ref, s_ref, o_ref, q_ref):
-    relation = relation_ref[...].astype(BF)
-    half_rows = near_ref.shape[1]
+    relation_bf_ref[...] = relation_ref[...].astype(BF)
+    width = table_ref.shape[0]
+    pack_ref[:width, :] = table_ref[...]
+    pack_ref[width:, :] = jnp.broadcast_to(state_ref[...], (pack_ref.shape[0] - width, LANES))
+
+
+def query_body(blocks, *refs):
+    near_refs, refs = refs[:blocks], refs[blocks:]
+    sibling_ref, relation_ref, ids_ref, s_ref, o_ref, q_ref = refs
+    relation = relation_ref[...]
     half = s_ref.shape[0] // 2
     edges = s_ref.shape[1]
     step = step_of(edges)
+    near = jnp.concatenate([ref[...] for ref in near_refs], axis=1)
+    half_rows = near.shape[1]
     for at in range(0, edges, step):
         cols = slice(at, at + step)
-        pick = hot(source_ref[:, cols], 2 * half_rows)
-        s = dot(near_ref[...], pick[:half_rows], 1, 0) + dot(sibling_ref[...], pick[half_rows:], 1, 0)
-        o = dot(relation, hot(kind_ref[:, cols], relation.shape[1]), 1, 0)
+        pick = hot(ids_ref[:, cols], 2 * half_rows)
+        s = dot(near, pick[:half_rows], 1, 0) + dot(sibling_ref[...], pick[half_rows:], 1, 0)
+        o = dot(relation, hot(ids_ref[:, 2 * edges + at:2 * edges + at + step], relation.shape[1]), 1, 0)
         s_ref[:, cols] = s.astype(BF)
         o_ref[:, cols] = o.astype(BF)
         s_re, s_im, o_re, o_im = s[:half], s[half:], o[:half], o[half:]
@@ -93,7 +99,7 @@
         q_ref[:, cols] = q.astype(BF)
 
 
-def grad_matrix(rows_ref, q_ref, weight_ref, target_ref, m_ref, base):
+def grad_matrix(rows_ref, q_ref, weight_ref, ids_ref, m_ref, base):
     count = rows_ref.shape[1]
     rows_t = rows_ref[...].T
     edges = q_ref.shape[1]
@@ -103,7 +109,7 @@
         cols = slice(at, at + step)
         scores = dot(rows_t, q_ref[:, cols], 1, 0)
         spot = lax.broadcasted_iota(jnp.int32, (count, step), 0) + base
-        h = jnp.where(spot == target_ref[:, cols], 1.0, 0.0)
+        h = jnp.where(spot == ids_ref[:, edges + at:edges + at + step], 1.0, 0.0)
         w = weight_ref[at // (edges // groups), base:base + count, :]
         w = jnp.concatenate([w] * (step // LANES), axis=1)
         m = (w + h) * (0.5 * jnp.tanh(0.5 * scores) + 0.5) - h
@@ -112,21 +118,21 @@
 
 def near_body(blocks, *refs):
     block_refs, refs = refs[:blocks], refs[blocks:]
-    q_ref, weight_ref, target_ref, right_ref, qg_ref, rows_ref, m_ref = refs
+    q_ref, weight_ref, ids_ref, right_ref, qg_ref, rows_ref, m_ref = refs
     for k, ref in enumerate(block_refs):
         rows_ref[:, k * LANES:(k + 1) * LANES] = ref[...]
-    grad_matrix(rows_ref, q_ref, weight_ref, target_ref, m_ref, 0)
+    grad_matrix(rows_ref, q_ref, weight_ref, ids_ref, m_ref, 0)
     right_ref[...] = dot(q_ref[...], m_ref[...], 1, 1)
     qg_ref[...] = dot(rows_ref[...], m_ref[...], 1, 0)
 
 
 def far_body(blocks, *refs):
     block_refs, refs = refs[:blocks], refs[blocks:]
-    q_ref, weight_ref, target_ref, m_ref, hi_ref, lo_ref, rows_ref = refs
+    q_ref, weight_ref, ids_ref, m_ref, hi_ref, lo_ref, rows_ref = refs
     for k, ref in enumerate(block_refs):
         rows_ref[:, k * LANES:(k + 1) * LANES] = ref[...]
     count = rows_ref.shape[1]
-    grad_matrix(rows_ref, q_ref, weight_ref, target_ref, m_ref, count)
+    grad_matrix(rows_ref, q_ref, weight_ref, ids_ref, m_ref, count)
     far = dot(q_ref[...], m_ref[...], 1, 1).astype(BF)
     hi_ref[...] = far[:, count // 2:]
     lo_ref[...] = far[:, :count // 2]
@@ -134,8 +140,8 @@
 
 def back_body(blocks, pieces, *refs):
     block_refs, refs = refs[:blocks], refs[blocks:]
-    m_ref, qg_ref, s_ref, o_ref, source_ref, kind_ref, here_ref, near_ref = refs[:8]
-    piece_refs, refs = refs[8:8 + pieces], refs[8 + pieces:]
+    m_ref, qg_ref, s_ref, o_ref, ids_ref, here_ref, near_ref = refs[:7]
+    piece_refs, refs = refs[7:7 + pieces], refs[7 + pieces:]
     rows_ref, left_ref, kinds_ref, tall_ref = refs
     for k, ref in enumerate(block_refs):
         rows_ref[:, k * LANES:(k + 1) * LANES] = ref[...]
@@ -151,8 +157,8 @@
         s_re, s_im, o_re, o_im = s[:half], s[half:], o[:half], o[half:]
         by_kind = jnp.concatenate([g_re * s_re + g_im * s_im, g_im * s_re - g_re * s_im], axis=0).astype(BF)
         by_source = jnp.concatenate([g_re * o_re + g_im * o_im, g_im * o_re - g_re * o_im], axis=0).astype(BF)
-        kinds = dot(by_kind, hot(kind_ref[:, cols], kinds_ref.shape[1]), 1, 1)
-        left = dot(by_source, hot(source_ref[:, cols], left_ref.shape[1]), 1, 1)
+        kinds = dot(by_kind, hot(ids_ref[:, 2 * edges + at:2 * edges + at + step], kinds_ref.shape[1]), 1, 1)
+        left = dot(by_source, hot(ids_ref[:, cols], left_ref.shape[1]), 1, 1)
         if at == 0:
             kinds_ref[...] = kinds
             left_ref[...] = left
@@ -221,26 +227,22 @@
             left_refs[k - 1][...] = total.astype(BF)
 
 
-def low_body(blocks, near_ref, got_ref, piece_ref, other_ref, table_ref, state_ref, *refs):
-    block_refs, (own_ref, mine_ref, pack_ref) = refs[:blocks - 1], refs[blocks - 1:]
+def low_body(blocks, near_ref, got_ref, piece_ref, other_ref, *refs):
+    block_refs, mine_ref = refs[:blocks], refs[blocks]
     mine_ref[...] = (piece_ref[...].astype(F32) + other_ref[...].astype(F32)).astype(BF)
     for k, ref in enumerate(block_refs):
-        cols = slice((k + 1) * LANES, (k + 2) * LANES)
+        cols = slice(k * LANES, (k + 1) * LANES)
         ref[...] = (near_ref[:, cols] + got_ref[:, cols].astype(F32)).astype(BF)
-    own_ref[...] = near_ref[:, :LANES] + got_ref[:, :LANES].astype(F32)
-    width = table_ref.shape[0]
-    pack_ref[:width, :] = table_ref[...]
-    pack_ref[width:, :] = jnp.broadcast_to(state_ref[...], (pack_ref.shape[0] - width, LANES))
 
 
 def sum_body(piece_ref, other_ref, out_ref):
     out_ref[...] = (piece_ref[...].astype(F32) + other_ref[...].astype(F32)).astype(BF)
 
 
-def update_body(parts, own_ref, *refs):
+def update_body(parts, *refs):
     part_refs, (table_ref, state_ref, new_ref, state_new_ref) = refs[:parts], refs[parts:]
-    g = own_ref[...]
-    for ref in part_refs:
+    g = part_refs[0][...].astype(F32)
+    for ref in part_refs[1:]:
         g = g + ref[...].astype(F32)
     width = g.shape[0]
     state = state_ref[:1, :] + jnp.sum(g * g, axis=0, keepdims=True) * (1.0 / width)
@@ -278,61 +280,56 @@
         nrel = relation_t.shape[1]
         here_l, here_r = lax.axis_index("left"), lax.axis_index("right")
         me = here_r.astype(jnp.int32).reshape(1)
-        source = source_ids.reshape(1, -1)
-        target = target_ids.reshape(1, -1)
-        kind = relation_ids.reshape(1, -1)
-        negative = negative_ids.reshape(negative_ids.shape[2], negative_ids.shape[3])
-        groups = negative.shape[0]
-        edges = source.shape[1]
+        edges = source_ids.shape[-1]
+        groups = negative_ids.shape[2]
         n_rows = n_left * rows
         half = outer * rows
+        one_block = shape(width, rows, dtype=BF)
+        table_bf = shape(width, edges, dtype=BF)
+
+        right_bf = call(cast_body, one_block)(right_t)
+        near = {k: swap_left(right_bf, 2 * k) for k in range(outer - 1, 0, -1)}
+        near[0] = right_bf
+        other = {0: swap_left(right_bf, 1)}
+        left_bf = call(cast_body, one_block)(left_t)
+        half_left = [left_bf] + [swap_right(left_bf, 2 * k) for k in range(1, far_right)]
 
         def local(ids, here, half):
             block = (ids // rows) ^ here
-            return (block % 2 * half + block // 2) * rows + ids % rows
-
-        source = local(source, here_r, far_right)
-        target = local(target, here_l, outer)
-        negative = local(negative, here_l, outer)
-
-        flop = 2 * width * edges
-        one_block = shape(width, rows, dtype=BF)
-        table_bf = shape(width, edges, dtype=BF)
-
-        left_bf, right_bf = call(cast_body, (one_block, one_block), width * rows)(left_t, right_t)
-        near = {0: next_column(right_bf, 0)}
-        for k in range(outer - 1, 0, -1):
-            near[k] = next_column(right_bf, 2 * k)
-        other = {0: next_column(right_bf, 1)}
-        weight, left_bf = call(
-            count_body, (shape(groups, n_rows, LANES), one_block), 4 * n_rows * edges, after=(near[0],)
-        )(negative, left_bf)
-        half_left = [left_bf] + [swap_right(left_bf, 2 * k) for k in range(1, far_right)]
-        half_left = jnp.concatenate(half_left, axis=1)
-        sibling_left = swap_right(half_left, 1)
+            return ((block % 2 * half + block // 2) * rows + ids % rows).reshape(-1)
+
+        before_r = (here_r + n_right - 1) % n_right
+        ids = [
+            local(source_ids, before_r, far_right), local(target_ids, here_l, outer),
+            relation_ids.reshape(-1), local(negative_ids, here_l, outer),
+        ]
+        ids = lax.ppermute(
+            jnp.concatenate(ids).reshape(1, -1), "right", [(i, (i - 1) % n_right) for i in range(n_right)]
+        )
+        sibling_left = swap_right(jnp.concatenate(half_left, axis=1), 1)
+        weight, relation_bf, pack = call(
+            functools.partial(count_body, edges),
+            (shape(groups, n_rows, LANES), shape(width, nrel, dtype=BF), shape(width + 8, rows)),
+        )(ids, relation_t, right_t, right_state[None, :])
         for k in range(1, outer):
             other[k] = swap_left(near[k], 1)
         near = [near[k] for k in range(outer)]
         other = [other[k] for k in range(outer)]
-
-        s, o, q = call(query_body, (table_bf, table_bf, table_bf), flop * (n_right * rows + nrel))(
-            half_left, sibling_left, relation_t, source, kind
+        moved = next_column(pack, 0)
+
+        s, o, q = call(functools.partial(query_body, far_right), (table_bf, table_bf, table_bf))(
+            *half_left, sibling_left, relation_bf, ids
         )
         part = pltpu.VMEM((width, half), BF)
         right_near, qg_near = call(
             functools.partial(near_body, outer),
             (shape(width, half), shape(width, edges)),
-            3 * flop * half,
             [part, pltpu.VMEM((half, edges), BF)],
-        )(*near, q, weight, target)
+        )(*near, q, weight, ids)
         chunk = shape(width, half // 2, dtype=BF)
         m, far_hi, far_lo = call(
-            functools.partial(far_body, outer),
-            (shape(half, edges, dtype=BF), chunk, chunk),
-            2 * flop * half,
-            [part],
-            after=(qg_near,),
-        )(*other, q, weight, target)
+            functools.partial(far_body, outer), (shape(half, edges, dtype=BF), chunk, chunk), [part], after=(qg_near,)
+        )(*other, q, weight, ids)
         got_hi = swap_left(far_hi, 1)
         got_lo = swap_left(far_lo, 1)
         tall = nrel // LANES * width
@@ -343,52 +340,44 @@
         left_near, *pieces = call(
             functools.partial(back_body, outer, n_right),
             (shape(width, left_rows // 2), piece, core_piece) + (piece,) * (n_right - 2),
-            flop * (half + nrel + left_rows),
             [part, pltpu.VMEM((width, left_rows), F32), pltpu.VMEM((width, nrel), F32),
              pltpu.VMEM((size * n_right, LANES), F32)],
             me,
-        )(*other, m, qg_near, s, o, source, kind)
+            after=(moved,),
+        )(*other, m, qg_near, s, o, ids)
 
         pieces = [pieces[0]] + [swap_right(pieces[k], k) for k in range(1, n_right)]
         some = outer // 2
         outs = call(
             functools.partial(high_body, some, n_right),
             (one_block,) * some + (piece, shape(width, rows)) + (one_block,) * (far_right - 1),
-            width * half,
         )(right_near, got_hi, left_near, *pieces)
         high, mine, left_own, left_blocks = outs[:some], outs[some], outs[some + 1], outs[some + 2:]
-        arrived = {some + k: swap_left(block, 2 * (some + k)) for k, block in enumerate(high)}
+        right_high = [next_column(block, 2 * (some + k)) for k, block in enumerate(high)]
         first = swap_left(mine, 2)
         left_got = [swap_right(block, 2 * (k + 1)) for k, block in enumerate(left_blocks)]
-        *low, own, mine, pack = call(
-            functools.partial(low_body, some),
-            (one_block,) * (some - 1) + (shape(width, rows), piece, shape(width + 8, rows)),
-            width * half,
-            after=tuple(left_got),
-        )(right_near, got_lo, mine, first, right_t, right_state[None, :])
-        for k, block in enumerate(low):
-            arrived[k + 1] = swap_left(block, 2 * (k + 1))
-        moved = next_column(pack, 0)
-        right_got = [arrived[k] for k in range(1, outer)]
-        add = functools.partial(call, sum_body, piece, size * LANES)
+        *low, mine = call(
+            functools.partial(low_body, some), (one_block,) * some + (piece,), after=tuple(left_got)
+        )(right_near, got_lo, mine, first)
+        right_low = [next_column(block, 2 * k) for k, block in enumerate(low)]
+        add = functools.partial(call, sum_body, piece)
         bit = 4
         while bit < n_left:
-            mine = add()(mine, swap_left(mine, bit))
+            mine = add(after=right_high if 2 * bit >= n_left else ())(mine, swap_left(mine, bit))
             bit *= 2
-        mine = add(after=(*right_got, moved))(mine, swap_left(mine, 1))
+        mine = add(after=right_low)(mine, swap_left(mine, 1))
         pieces = [mine] + [swap_right(mine, k) for k in range(1, n_right)]
 
-        def update(own, got, table, state):
-            return call(
-                functools.partial(update_body, len(got)), (shape(width, rows), shape(1, rows)), 8 * width * rows
-            )(own, *got, table, state)
-
-        left_new, left_state_new = update(left_own, left_got, left_t, left_state[None, :])
-        right_new, right_state_new = update(own, right_got, moved, moved[width:])
+        def update(got, table, state):
+            return call(functools.partial(update_body, len(got)), (shape(width, rows), shape(1, rows)))(
+                *got, table, state
+            )
+
+        left_new, left_state_new = update([left_own, *left_got], left_t, left_state[None, :])
+        right_new, right_state_new = update([*right_low, *right_high], moved, moved[width:])
         relation_new, relation_state_new = call(
             functools.partial(relation_body, n_right),
             (shape(width, nrel), shape(1, nrel)),
-            8 * width * nrel,
             [pltpu.VMEM((size * n_right, LANES), F32)],
             me,
         )(*pieces, relation_t, relation_state[None, :])

time: 70.9 us -> 74.8 us (1.055)
  starting transfers between devices: 27.6 us -> 32.4 us
  waiting for transfers between devices: 26 us -> 24.6 us
    ppermute x11 -> x12, starting transfers between devices: 12.5 us -> 16.9 us  [swap_left(): return lax.ppermute(value, 'left', [(i, i ^ by) for i in range(n_left)])]
    ppermute x9, waiting for transfers between devices: 8.83 us -> 5.99 us  [swap_right(): return lax.ppermute(value, 'right', [(i, i ^ by) for i in range(n_right)])]
    ppermute x6 -> x5, starting transfers between devices: 7.98 us -> 5.48 us  [next_column(): return lax.ppermute(value, ('left', 'right'), perm)]
    ppermute x0 -> x1, starting transfers between devices: none -> 1.88 us  [per_device(): lax.ppermute(jnp.concatenate(ids).reshape(1, -1), 'right', [(i, (i - 1) %...]
    ppermute x0 -> x1, waiting for transfers between devices: none -> 1.48 us  [per_device(): lax.ppermute(jnp.concatenate(ids).reshape(1, -1), 'right', [(i, (i - 1) %...]
    ppermute x11 -> x12, waiting for transfers between devices: 14.1 us -> 12.7 us  [swap_left(): return lax.ppermute(value, 'left', [(i, i ^ by) for i in range(n_left)])]
    ppermute x6 -> x5, waiting for transfers between devices: 3.06 us -> 4.37 us  [next_column(): return lax.ppermute(value, ('left', 'right'), perm)]
    ppermute x9, starting transfers between devices: 7.19 us -> 8.12 us  [swap_right(): return lax.ppermute(value, 'right', [(i, i ^ by) for i in range(n_right)])]
  transfers between devices with their start and end apart: 26 -> 27, of which waited for: 13 -> 13; matrix products, arithmetic and copies ran while one was open for 3% -> 4% of each run, Pallas kernels for 8% -> 9%
where the time goes in v6:
time: 74.8 us; the launch traced here: 74.4 us
  starting transfers between devices  32.4 us (43%)
  waiting for transfers between devices  24.6 us (33%)
  Pallas kernels  10.2 us (14%)
  local copies, waits for them, and re-layouts  3.53 us (5%)
  other arithmetic  3.01 us (4%)
  between operations  0.81 us (1%)
    ppermute x12, starting transfers between devices, swap_left(): return lax.ppermute(value, 'left', [(i, i ^ by) for i in range(n_left)])  16.9 us
    ppermute x12, waiting for transfers between devices, swap_left(): return lax.ppermute(value, 'left', [(i, i ^ by) for i in range(n_left)])  12.7 us
    pallas_call x14, Pallas kernels, run(): pl.pallas_call(inner, out_shape=out_shape, in_specs=specs, scratch_shapes...  10.2 us
    ppermute x9, starting transfers between devices, swap_right(): return lax.ppermute(value, 'right', [(i, i ^ by) for i in range(n_right)])  8.12 us
    ppermute x9, waiting for transfers between devices, swap_right(): return lax.ppermute(value, 'right', [(i, i ^ by) for i in range(n_right)])  5.99 us
    ppermute x5, starting transfers between devices, next_column(): return lax.ppermute(value, ('left', 'right'), perm)  5.48 us
    ppermute x5, waiting for transfers between devices, next_column(): return lax.ppermute(value, ('left', 'right'), perm)  4.37 us
    unnamed x17, local copies, waits for them, and re-layouts  3.53 us
  transfers between devices with their start and end apart: 27, of which 13 were waited for; matrix products, arithmetic and copies ran while one was open for 4% of the time, Pallas kernels for 9%

profile of v6, /device:TPU:0, one launch (start us, length us, event | category | flops | bytes accessed | tf_op | source)
XLA Modules:
  0.0 74.4 jit_solution(11531819314359561121)
XLA Ops:
  0.6 0.9 %copy-done.3 = f32[128,400]{0,1:T(8,128)S(1)} copy-done((f32[128,400]{0,1:T(8,128)S(1)}, f32[128,400]{0,1:T(8,128)}, u32[]{:S(2)}) %copy-start.3) | copy-done | bytes 204824
  1.6 3.0 %collective-permute-start.3 = (bf16[400,128]{1,0:T(8,128)(2,1)S(1)}, bf16[400,128]{1,0:T(8,128)(2,1)S(1)}, u32[]{:S(2)}, u32[]{:S(2)}) collective-permute-start(bf16[400,128]{1,0:T(8,128)(2,1)S(1)} %shard_map.146.refs_0_), channel_id=1, source_target_pairs={{0,2},{1,3},{2,0},{3,1},{4,6},{5,7},{6,4},{7,5},{8,10},{9,11},{10,... | collective-permute-start | bytes 307208 | tf_op jit(solution)/shard_map/ppermute | solution.py:264
  4.6 0.8 %fusion.3 = s32[1,8,2,128]{3,2,1,0:T(2,128)S(1)} fusion(s32[1,1,2,1024]{3,2,1,0:T(2,128)} %param.19, s32[]{:T(128)S(6)} %axis_index.25), kind=kLoop, calls=%fused_computation.36 | loop fusion | flops 88064 | bytes 16388
  5.4 0.8 %fusion.5 = s32[1,1,1024]{2,1,0:T(1,128)S(1)} fusion(s32[1,1,1024]{2,1,0:T(1,128)} %param.17, s32[]{:T(128)S(6)} %axis_index.25), kind=kLoop, calls=%fused_computation.38 | loop fusion | flops 44032 | bytes 8196 | tf_op jit(solution)/shard_map/add | solution.py:299
  6.1 0.8 %fusion.4 = s32[1,1,1024]{2,1,0:T(1,128)S(1)} fusion(s32[1,1,1024]{2,1,0:T(1,128)} %param.16, s32[]{:T(128)S(6)} %select_n.58), kind=kLoop, calls=%fused_computation.37 | loop fusion | flops 44032 | bytes 8196 | tf_op jit(solution)/shard_map/add | solution.py:299
  6.9 0.6 collective-permute-done.3.refs_1_
  7.6 0.7 pad_add_fusion
  8.3 1.9 %collective-permute-start.5 = (s32[1,5120]{1,0:T(1,128)S(1)}, s32[1,5120]{1,0:T(1,128)S(1)}, u32[]{:S(2)}, u32[]{:S(2)}) collective-permute-start(s32[1,5120]{1,0:T(1,128)S(1)} %bitcast.32), channel_id=1, source_target_pairs={{0,3},{1,0},{2,1},{3,2},{4,7},{5,4},{6,5},{7,6},{8,11},{9,8},{10,9... | collective-permute-start | bytes 61448 | tf_op jit(solution)/shard_map/ppermute | solution.py:306
  10.1 1.5 %collective-permute-done.5.ids_ref.refs_4_.refs_6_.refs_8_ = s32[1,5120]{1,0:T(1,128)S(1)} collective-permute-done((s32[1,5120]{1,0:T(1,128)S(1)}, s32[1,5120]{1,0:T(1,128)S(1)}, u32[]{:S(2)}, u32[]{:S(2)}) %collective-permute-start.5) | collective-permute-done | bytes 20512 | tf_op jit(solution)/shard_map/ppermute | solution.py:306
  11.6 1.0 %copy-done = f32[256,400]{0,1:T(8,128)S(1)} copy-done((f32[256,400]{0,1:T(8,128)S(1)}, f32[256,400]{0,1:T(8,128)}, u32[]{:S(2)}) %copy-start) | copy-done | bytes 409624
  12.6 0.9 %copy-done.2 = f32[128,400]{0,1:T(8,128)S(1)} copy-done((f32[128,400]{0,1:T(8,128)S(1)}, f32[128,400]{0,1:T(8,128)}, u32[]{:S(2)}) %copy-start.2) | copy-done | bytes 204824
  13.6 0.7 copy-done.7
  14.2 0.9 %shard_map.147 = (f32[2,1024,128]{2,1,0:T(8,128)S(1)}, bf16[400,256]{1,0:T(8,128)(2,1)S(1)}, f32[408,128]{1,0:T(8,128)S(1)}) custom-call(s32[1,5120]{1,0:T(1,128)S(1)} %collective-permute-done.5.ids_ref.refs_4_.refs_6_.refs_8_, f32[400,256]{1,0:T(8,128)S(1)} %bitcast.22, f32[400,128]{1,0:T(8,128)S(1)} %bitcast.24, f32[1,128]{1,0:T(1,128)S(1)} %bitcast.30), custom_call_target="tpu_custom_call" | custom-call | tf_op jit(solution)/shard_map/pallas_call | solution.py:46
  15.1 0.4 collective-permute-start.11
  15.5 1.9 %collective-permute-start = (bf16[400,128]{1,0:T(8,128)(2,1)S(1)}, bf16[400,128]{1,0:T(8,128)(2,1)S(1)}, u32[]{:S(2)}, u32[]{:S(2)}) collective-permute-start(bf16[400,128]{1,0:T(8,128)(2,1)S(1)} %shard_map.145.refs_0_), channel_id=1, source_target_pairs={{0,8},{4,12},{8,0},{12,4},{16,24},{20,28},{24,16},{28,20},{1,9},{5... | collective-permute-start | bytes 307208 | tf_op jit(solution)/shard_map/ppermute | solution.py:261
  17.4 2.6 %collective-permute-start.1 = (bf16[400,128]{1,0:T(8,128)(2,1)S(1)}, bf16[400,128]{1,0:T(8,128)(2,1)S(1)}, u32[]{:S(2)}, u32[]{:S(2)}) collective-permute-start(bf16[400,128]{1,0:T(8,128)(2,1)S(1)} %shard_map.145.refs_0_), channel_id=1, source_target_pairs={{0,16},{4,20},{8,24},{12,28},{16,0},{20,4},{24,8},{28,12},{1,17},{... | collective-permute-start | bytes 307208 | tf_op jit(solution)/shard_map/ppermute | solution.py:261
  20.0 0.5 collective-permute-done.refs_1_
  20.5 1.7 %collective-permute-start.6 = (bf16[400,128]{1,0:T(8,128)(2,1)S(1)}, bf16[400,128]{1,0:T(8,128)(2,1)S(1)}, u32[]{:S(2)}, u32[]{:S(2)}) collective-permute-start(bf16[400,128]{1,0:T(8,128)(2,1)S(1)} %shard_map.145.refs_0_), channel_id=1, source_target_pairs={{0,4},{4,0},{8,12},{12,8},{16,20},{20,16},{24,28},{28,24},{1,5},{5... | collective-permute-start | bytes 307208 | tf_op jit(solution)/shard_map/ppermute | solution.py:261
  22.2 6.2 %collective-permute-done.1.refs_2_ = bf16[400,128]{1,0:T(8,128)(2,1)S(1)} collective-permute-done((bf16[400,128]{1,0:T(8,128)(2,1)S(1)}, bf16[400,128]{1,0:T(8,128)(2,1)S(1)}, u32[]{:S(2)}, u32[]{:S(2)}) %collective-permute-start.1) | collective-permute-done | bytes 102432 | tf_op jit(solution)/shard_map/ppermute | solution.py:261
  28.4 1.5 %collective-permute-start.7 = (bf16[400,128]{1,0:T(8,128)(2,1)S(1)}, bf16[400,128]{1,0:T(8,128)(2,1)S(1)}, u32[]{:S(2)}, u32[]{:S(2)}) collective-permute-start(bf16[400,128]{1,0:T(8,128)(2,1)S(1)} %collective-permute-done.refs_1_), channel_id=1, source_target_pairs={{0,4},{4,0},{8,12},{12,8},{16,20},{20,16},{24,28},{28,24},{1,5},{5... | collective-permute-start | bytes 307208 | tf_op jit(solution)/shard_map/ppermute | solution.py:261
  29.9 0.5 collective-permute-start.8
  30.4 1.5 %collective-permute-start.9 = (bf16[400,128]{1,0:T(8,128)(2,1)S(1)}, bf16[400,128]{1,0:T(8,128)(2,1)S(1)}, u32[]{:S(2)}, u32[]{:S(2)}) collective-permute-start(bf16[400,128]{1,0:T(8,128)(2,1)S(1)} %collective-permute-done.2.refs_3_), channel_id=1, source_target_pairs={{0,4},{4,0},{8,12},{12,8},{16,20},{20,16},{24,28},{28,24},{1,5},{5... | collective-permute-start | bytes 307208 | tf_op jit(solution)/shard_map/ppermute | solution.py:261
  31.9 0.9 %shard_map.148 = (bf16[400,1024]{1,0:T(8,128)(2,1)S(1)}, bf16[400,1024]{1,0:T(8,128)(2,1)S(1)}, bf16[400,1024]{1,0:T(8,128)(2,1)S(1)}) custom-call(bf16[400,128]{1,0:T(8,128)(2,1)S(1)} %shard_map.146.refs_0_, bf16[400,128]{1,0:T(8,128)(2,1)S(1)} %collective-permute-done.3.refs_1_, bf16[400,256]{1,0:T(8,128)(2,1)S(1)} %collective-permute-done.4.refs_2_, ...), custom_call_target="tpu_custom_call" | custom-call | tf_op jit(solution)/shard_map/pallas_call | solution.py:46
  32.9 1.9 %shard_map.149 = (f32[400,512]{1,0:T(8,128)S(1)}, f32[400,1024]{1,0:T(8,128)S(1)}) custom-call(bf16[400,128]{1,0:T(8,128)(2,1)S(1)} %shard_map.145.refs_0_, bf16[400,128]{1,0:T(8,128)(2,1)S(1)} %collective-permute-done.refs_1_, bf16[400,128]{1,0:T(8,128)(2,1)S(1)} %collective-permute-done.1.refs_2_, bf16[400,128]{1,0:T(8,128)(2,1)S(1)} %collective-permute-done.2.refs_3_, ...), custom_call_target="tpu_custom_call" | custom-call | tf_op jit(solution)/shard_map/pallas_call | solution.py:46
  34.8 0.9 %collective-permute-done.9.refs_3_ = bf16[400,128]{1,0:T(8,128)(2,1)S(1)} collective-permute-done((bf16[400,128]{1,0:T(8,128)(2,1)S(1)}, bf16[400,128]{1,0:T(8,128)(2,1)S(1)}, u32[]{:S(2)}, u32[]{:S(2)}) %collective-permute-start.9) | collective-permute-done | bytes 102432 | tf_op jit(solution)/shard_map/ppermute | solution.py:261
  35.7 1.5 %shard_map.150 = (bf16[512,1024]{1,0:T(8,128)(2,1)S(1)}, bf16[400,256]{1,0:T(8,128)(2,1)S(1)}, bf16[400,256]{1,0:T(8,128)(2,1)S(1)}) custom-call(bf16[400,128]{1,0:T(8,128)(2,1)S(1)} %collective-permute-done.6.refs_0_, bf16[400,128]{1,0:T(8,128)(2,1)S(1)} %collective-permute-done.7.refs_1_, bf16[400,128]{1,0:T(8,128)(2,1)S(1)} %collective-permute-done.8.refs_2_, ...), custom_call_target="tpu_custom_call" | custom-call | tf_op jit(solution)/shard_map/pallas_call | solution.py:46
  37.2 2.3 %shard_map.151 = (f32[400,256]{1,0:T(8,128)S(1)}, bf16[208,128]{1,0:T(8,128)(2,1)S(1)}, bf16[1008,128]{1,0:T(8,128)(2,1)S(1)}, bf16[208,128]{1,0:T(8,128)(2,1)S(1)}, bf16[208,128]{1,0:T(8,128)(2,1)S(1)}) custom-call(bf16[400,128]{1,0:T(8,128)(2,1)S(1)} %collective-permute-done.6.refs_0_, bf16[400,128]{1,0:T(8,128)(2,1)S(1)} %collective-permute-done.7.refs_1_, ...), custom_call_target="tpu_custom_call" | custom-call | tf_op jit(solution)/shard_map/pallas_call | solution.py:46
  39.5 1.2 %collective-permute-start.10 = (bf16[400,256]{1,0:T(8,128)(2,1)S(1)}, bf16[400,256]{1,0:T(8,128)(2,1)S(1)}, u32[]{:S(2)}, u32[]{:S(2)}) collective-permute-start(bf16[400,256]{1,0:T(8,128)(2,1)S(1)} %get-tuple-element.41), channel_id=1, source_target_pairs={{0,4},{4,0},{8,12},{12,8},{16,20},{20,16},{24,28},{28,24},{1,5},{5... | collective-permute-start | bytes 614408 | tf_op jit(solution)/shard_map/ppermute | solution.py:261
  40.7 0.9 %collective-permute-start.16 = (bf16[400,256]{1,0:T(8,128)(2,1)S(1)}, bf16[400,256]{1,0:T(8,128)(2,1)S(1)}, u32[]{:S(2)}, u32[]{:S(2)}) collective-permute-start(bf16[400,256]{1,0:T(8,128)(2,1)S(1)} %get-tuple-element.55), channel_id=1, source_target_pairs={{0,4},{4,0},{8,12},{12,8},{16,20},{20,16},{24,28},{28,24},{1,5},{5... | collective-permute-start | bytes 614408 | tf_op jit(solution)/shard_map/ppermute | solution.py:261
  41.6 1.5 %collective-permute-start.13 = (bf16[208,128]{1,0:T(8,128)(2,1)S(1)}, bf16[208,128]{1,0:T(8,128)(2,1)S(1)}, u32[]{:S(2)}, u32[]{:S(2)}) collective-permute-start(bf16[208,128]{1,0:T(8,128)(2,1)S(1)} %get-tuple-element.49), channel_id=1, source_target_pairs={{0,2},{1,3},{2,0},{3,1},{4,6},{5,7},{6,4},{7,5},{8,10},{9,11},{10,... | collective-permute-start | bytes 159752 | tf_op jit(solution)/shard_map/ppermute | solution.py:264
  43.1 2.6 %collective-permute-done.13.refs_2_ = bf16[208,128]{1,0:T(8,128)(2,1)S(1)} collective-permute-done((bf16[208,128]{1,0:T(8,128)(2,1)S(1)}, bf16[208,128]{1,0:T(8,128)(2,1)S(1)}, u32[]{:S(2)}, u32[]{:S(2)}) %collective-permute-start.13) | collective-permute-done | bytes 53280 | tf_op jit(solution)/shard_map/ppermute | solution.py:264
  45.8 1.3 %collective-permute-done.14.refs_3_ = bf16[208,128]{1,0:T(8,128)(2,1)S(1)} collective-permute-done((bf16[208,128]{1,0:T(8,128)(2,1)S(1)}, bf16[208,128]{1,0:T(8,128)(2,1)S(1)}, u32[]{:S(2)}, u32[]{:S(2)}) %collective-permute-start.14) | collective-permute-done | bytes 53280 | tf_op jit(solution)/shard_map/ppermute | solution.py:264
  47.0 0.4 collective-permute-done.10.got_ref
  47.6 1.6 %collective-permute-start.15 = (bf16[400,128]{1,0:T(8,128)(2,1)S(1)}, bf16[400,128]{1,0:T(8,128)(2,1)S(1)}, u32[]{:S(2)}, u32[]{:S(2)}) collective-permute-start(bf16[400,128]{1,0:T(8,128)(2,1)S(1)} %get-tuple-element.52), channel_id=1, source_target_pairs={{0,2},{1,3},{2,0},{3,1},{4,6},{5,7},{6,4},{7,5},{8,10},{9,11},{10,... | collective-permute-start | bytes 307208 | tf_op jit(solution)/shard_map/ppermute | solution.py:264
  49.2 1.4 %collective-permute-start.17 = (bf16[208,128]{1,0:T(8,128)(2,1)S(1)}, bf16[208,128]{1,0:T(8,128)(2,1)S(1)}, u32[]{:S(2)}, u32[]{:S(2)}) collective-permute-start(bf16[208,128]{1,0:T(8,128)(2,1)S(1)} %get-tuple-element.56.refs_2_), channel_id=1, source_target_pairs={{0,8},{4,12},{8,0},{12,4},{16,24},{20,28},{24,16},{28,20},{1,9},{5... | collective-permute-start | bytes 159752 | tf_op jit(solution)/shard_map/ppermute | solution.py:261
  50.8 2.5 %collective-permute-start.21 = (bf16[400,128]{1,0:T(8,128)(2,1)S(1)}, bf16[400,128]{1,0:T(8,128)(2,1)S(1)}, u32[]{:S(2)}, u32[]{:S(2)}) collective-permute-start(bf16[400,128]{1,0:T(8,128)(2,1)S(1)} %get-tuple-element.60), channel_id=1, source_target_pairs={{0,25},{1,26},{2,27},{3,24},{4,29},{5,30},{6,31},{7,28},{8,17},{9,... | collective-permute-start | bytes 307208 | tf_op jit(solution)/shard_map/ppermute | solution.py:271
  53.4 2.0 %collective-permute-start.22 = (bf16[208,128]{1,0:T(8,128)(2,1)S(1)}, bf16[208,128]{1,0:T(8,128)(2,1)S(1)}, u32[]{:S(2)}, u32[]{:S(2)}) collective-permute-start(bf16[208,128]{1,0:T(8,128)(2,1)S(1)} %get-tuple-element.63.refs_0_), channel_id=1, source_target_pairs={{0,16},{4,20},{8,24},{12,28},{16,0},{20,4},{24,8},{28,12},{1,17},{... | collective-permute-start | bytes 159752 | tf_op jit(solution)/shard_map/ppermute | solution.py:261
  55.4 2.4 %collective-permute-start.19 = (bf16[400,128]{1,0:T(8,128)(2,1)S(1)}, bf16[400,128]{1,0:T(8,128)(2,1)S(1)}, u32[]{:S(2)}, u32[]{:S(2)}) collective-permute-start(bf16[400,128]{1,0:T(8,128)(2,1)S(1)} %get-tuple-element.58), channel_id=1, source_target_pairs={{0,9},{1,10},{2,11},{3,8},{4,13},{5,14},{6,15},{7,12},{8,1},{9,2},... | collective-permute-start | bytes 307208 | tf_op jit(solution)/shard_map/ppermute | solution.py:271
  57.9 4.4 %collective-permute-done.20.refs_2_ = bf16[400,128]{1,0:T(8,128)(2,1)S(1)} collective-permute-done((bf16[400,128]{1,0:T(8,128)(2,1)S(1)}, bf16[400,128]{1,0:T(8,128)(2,1)S(1)}, u32[]{:S(2)}, u32[]{:S(2)}) %collective-permute-start.20) | collective-permute-done | bytes 102432 | tf_op jit(solution)/shard_map/ppermute | solution.py:271
  62.2 2.0 %collective-permute-done.22.refs_1_ = bf16[208,128]{1,0:T(8,128)(2,1)S(1)} collective-permute-done((bf16[208,128]{1,0:T(8,128)(2,1)S(1)}, bf16[208,128]{1,0:T(8,128)(2,1)S(1)}, u32[]{:S(2)}, u32[]{:S(2)}) %collective-permute-start.22) | collective-permute-done | bytes 53280 | tf_op jit(solution)/shard_map/ppermute | solution.py:261
  64.2 1.6 %collective-permute-start.23 = (bf16[208,128]{1,0:T(8,128)(2,1)S(1)}, bf16[208,128]{1,0:T(8,128)(2,1)S(1)}, u32[]{:S(2)}, u32[]{:S(2)}) collective-permute-start(bf16[208,128]{1,0:T(8,128)(2,1)S(1)} %shard_map.156.refs_0_), channel_id=1, source_target_pairs={{0,4},{4,0},{8,12},{12,8},{16,20},{20,16},{24,28},{28,24},{1,5},{5... | collective-permute-start | bytes 159752 | tf_op jit(solution)/shard_map/ppermute | solution.py:261
  65.8 2.7 %collective-permute-done.23.refs_1_ = bf16[208,128]{1,0:T(8,128)(2,1)S(1)} collective-permute-done((bf16[208,128]{1,0:T(8,128)(2,1)S(1)}, bf16[208,128]{1,0:T(8,128)(2,1)S(1)}, u32[]{:S(2)}, u32[]{:S(2)}) %collective-permute-start.23) | collective-permute-done | bytes 53280 | tf_op jit(solution)/shard_map/ppermute | solution.py:261
  68.6 0.6 collective-permute-start.25
  69.2 1.3 %collective-permute-start.26 = (bf16[208,128]{1,0:T(8,128)(2,1)S(1)}, bf16[208,128]{1,0:T(8,128)(2,1)S(1)}, u32[]{:S(2)}, u32[]{:S(2)}) collective-permute-start(bf16[208,128]{1,0:T(8,128)(2,1)S(1)} %shard_map.157.refs_0_), channel_id=1, source_target_pairs={{0,3},{1,2},{2,1},{3,0},{4,7},{5,6},{6,5},{7,4},{8,11},{9,10},{10,... | collective-permute-start | bytes 159752 | tf_op jit(solution)/shard_map/ppermute | solution.py:264
  70.5 0.8 %shard_map.153 = (f32[400,128]{1,0:T(8,128)}, f32[1,128]{1,0:T(1,128)}) custom-call(f32[400,128]{1,0:T(8,128)S(1)} %get-tuple-element.51.refs_0_, bf16[400,128]{1,0:T(8,128)(2,1)S(1)} %collective-permute-done.15.refs_1_.refs_4_, f32[400,128]{1,0:T(8,128)S(1)} %bitcast.27, f32[1,128]{1,0:T(1,128)S(1)} %bitcast.29), custom_call_target="tpu_custom_call" | custom-call | tf_op jit(solution)/shard_map/pallas_call | solution.py:46
  71.2 0.8 %shard_map.155 = (f32[400,128]{1,0:T(8,128)}, f32[1,128]{1,0:T(1,128)}) custom-call(bf16[400,128]{1,0:T(8,128)(2,1)S(1)} %collective-permute-done.18.refs_0_.refs_2_, bf16[400,128]{1,0:T(8,128)(2,1)S(1)} %collective-permute-done.19.refs_1_.refs_3_, bf16[400,128]{1,0:T(8,128)(2,1)S(1)} %collective-permute-done.20.refs_2_, ...), custom_call_target="tpu_custom_call" | custom-call | tf_op jit(solution)/shard_map/pallas_call | solution.py:46
  72.0 1.3 %collective-permute-done.25.refs_2_ = bf16[208,128]{1,0:T(8,128)(2,1)S(1)} collective-permute-done((bf16[208,128]{1,0:T(8,128)(2,1)S(1)}, bf16[208,128]{1,0:T(8,128)(2,1)S(1)}, u32[]{:S(2)}, u32[]{:S(2)}) %collective-permute-start.25) | collective-permute-done | bytes 53280 | tf_op jit(solution)/shard_map/ppermute | solution.py:264
  73.5 0.9 %shard_map.158 = (f32[400,256]{1,0:T(8,128)}, f32[1,256]{1,0:T(1,128)}) custom-call(bf16[208,128]{1,0:T(8,128)(2,1)S(1)} %shard_map.157.refs_0_, bf16[208,128]{1,0:T(8,128)(2,1)S(1)} %collective-permute-done.24.refs_1_, bf16[208,128]{1,0:T(8,128)(2,1)S(1)} %collective-permute-done.25.refs_2_, bf16[208,128]{1,0:T(8,128)(2,1)S(1)} %collective-permute-done.26.refs_3_, ...), custom_call_target="tpu_custom_call" | custom-call | tf_op jit(solution)/shard_map/pallas_call | solution.py:46
  (43 shorter events, 1.0 us)
Async XLA Ops:
  0.6 0.9 %copy-start.3 = (f32[128,400]{0,1:T(8,128)S(1)}, f32[128,400]{0,1:T(8,128)}, u32[]{:S(2)}) copy-start(f32[128,400]{0,1:T(8,128)} %param.10) | copy-start | bytes 614404
  1.6 5.9 %collective-permute-start.3 = (bf16[400,128]{1,0:T(8,128)(2,1)S(1)}, bf16[400,128]{1,0:T(8,128)(2,1)S(1)}, u32[]{:S(2)}, u32[]{:S(2)}) collective-permute-start(bf16[400,128]{1,0:T(8,128)(2,1)S(1)} %shard_map.146.refs_0_), channel_id=1, source_target_pairs={{0,2},{1,3},{2,0},{3,1},{4,6},{5,7},{6,4},{7,5},{8,10},{9,11},{10,... | collective-permute-start | bytes 307208 | tf_op jit(solution)/shard_map/ppermute | solution.py:264
  7.5 22.9 %collective-permute-start.4 = (bf16[400,256]{1,0:T(8,128)(2,1)S(1)}, bf16[400,256]{1,0:T(8,128)(2,1)S(1)}, u32[]{:S(2)}, u32[]{:S(2)}) collective-permute-start(bf16[400,256]{1,0:T(8,128)(2,1)S(1)} %pad_maximum_fusion), channel_id=1, source_target_pairs={{0,1},{1,0},{2,3},{3,2},{4,5},{5,4},{6,7},{7,6},{8,9},{9,8},{10,11... | collective-permute-start | bytes 614408 | tf_op jit(solution)/shard_map/ppermute | solution.py:264
  8.3 3.4 %collective-permute-start.5 = (s32[1,5120]{1,0:T(1,128)S(1)}, s32[1,5120]{1,0:T(1,128)S(1)}, u32[]{:S(2)}, u32[]{:S(2)}) collective-permute-start(s32[1,5120]{1,0:T(1,128)S(1)} %bitcast.32), channel_id=1, source_target_pairs={{0,3},{1,0},{2,1},{3,2},{4,7},{5,4},{6,5},{7,6},{8,11},{9,8},{10,9... | collective-permute-start | bytes 61448 | tf_op jit(solution)/shard_map/ppermute | solution.py:306
  11.6 1.0 %copy-start = (f32[256,400]{0,1:T(8,128)S(1)}, f32[256,400]{0,1:T(8,128)}, u32[]{:S(2)}) copy-start(f32[256,400]{0,1:T(8,128)} %param.14) | copy-start | bytes 1228804
  12.6 0.9 %copy-start.2 = (f32[128,400]{0,1:T(8,128)S(1)}, f32[128,400]{0,1:T(8,128)}, u32[]{:S(2)}) copy-start(f32[128,400]{0,1:T(8,128)} %param.12) | copy-start | bytes 614404
  13.6 0.7 copy-start.7
  15.1 22.1 %collective-permute-start.11 = (f32[408,128]{1,0:T(8,128)S(1)}, f32[408,128]{1,0:T(8,128)S(1)}, u32[]{:S(2)}, u32[]{:S(2)}) collective-permute-start(f32[408,128]{1,0:T(8,128)S(1)} %get-tuple-element.45), channel_id=1, source_target_pairs={{0,1},{1,2},{2,3},{3,0},{4,5},{5,6},{6,7},{7,4},{8,9},{9,10},{10,1... | collective-permute-start | bytes 626696 | tf_op jit(solution)/shard_map/ppermute | solution.py:271
  15.5 5.0 %collective-permute-start = (bf16[400,128]{1,0:T(8,128)(2,1)S(1)}, bf16[400,128]{1,0:T(8,128)(2,1)S(1)}, u32[]{:S(2)}, u32[]{:S(2)}) collective-permute-start(bf16[400,128]{1,0:T(8,128)(2,1)S(1)} %shard_map.145.refs_0_), channel_id=1, source_target_pairs={{0,8},{4,12},{8,0},{12,4},{16,24},{20,28},{24,16},{28,20},{1,9},{5... | collective-permute-start | bytes 307208 | tf_op jit(solution)/shard_map/ppermute | solution.py:261
  17.4 10.9 %collective-permute-start.1 = (bf16[400,128]{1,0:T(8,128)(2,1)S(1)}, bf16[400,128]{1,0:T(8,128)(2,1)S(1)}, u32[]{:S(2)}, u32[]{:S(2)}) collective-permute-start(bf16[400,128]{1,0:T(8,128)(2,1)S(1)} %shard_map.145.refs_0_), channel_id=1, source_target_pairs={{0,16},{4,20},{8,24},{12,28},{16,0},{20,4},{24,8},{28,12},{1,17},{... | collective-permute-start | bytes 307208 | tf_op jit(solution)/shard_map/ppermute | solution.py:261
  20.0 9.9 %collective-permute-start.2 = (bf16[400,128]{1,0:T(8,128)(2,1)S(1)}, bf16[400,128]{1,0:T(8,128)(2,1)S(1)}, u32[]{:S(2)}, u32[]{:S(2)}) collective-permute-start(bf16[400,128]{1,0:T(8,128)(2,1)S(1)} %shard_map.145.refs_0_), channel_id=1, source_target_pairs={{0,24},{4,28},{8,16},{12,20},{16,8},{20,12},{24,0},{28,4},{1,25},{... | collective-permute-start | bytes 307208 | tf_op jit(solution)/shard_map/ppermute | solution.py:261
  20.5 14.2 %collective-permute-start.6 = (bf16[400,128]{1,0:T(8,128)(2,1)S(1)}, bf16[400,128]{1,0:T(8,128)(2,1)S(1)}, u32[]{:S(2)}, u32[]{:S(2)}) collective-permute-start(bf16[400,128]{1,0:T(8,128)(2,1)S(1)} %shard_map.145.refs_0_), channel_id=1, source_target_pairs={{0,4},{4,0},{8,12},{12,8},{16,20},{20,16},{24,28},{28,24},{1,5},{5... | collective-permute-start | bytes 307208 | tf_op jit(solution)/shard_map/ppermute | solution.py:261
  28.4 6.4 %collective-permute-start.7 = (bf16[400,128]{1,0:T(8,128)(2,1)S(1)}, bf16[400,128]{1,0:T(8,128)(2,1)S(1)}, u32[]{:S(2)}, u32[]{:S(2)}) collective-permute-start(bf16[400,128]{1,0:T(8,128)(2,1)S(1)} %collective-permute-done.refs_1_), channel_id=1, source_target_pairs={{0,4},{4,0},{8,12},{12,8},{16,20},{20,16},{24,28},{28,24},{1,5},{5... | collective-permute-start | bytes 307208 | tf_op jit(solution)/shard_map/ppermute | solution.py:261
  29.9 4.8 %collective-permute-start.8 = (bf16[400,128]{1,0:T(8,128)(2,1)S(1)}, bf16[400,128]{1,0:T(8,128)(2,1)S(1)}, u32[]{:S(2)}, u32[]{:S(2)}) collective-permute-start(bf16[400,128]{1,0:T(8,128)(2,1)S(1)} %collective-permute-done.1.refs_2_), channel_id=1, source_target_pairs={{0,4},{4,0},{8,12},{12,8},{16,20},{20,16},{24,28},{28,24},{1,5},{5... | collective-permute-start | bytes 307208 | tf_op jit(solution)/shard_map/ppermute | solution.py:261
  30.4 5.2 %collective-permute-start.9 = (bf16[400,128]{1,0:T(8,128)(2,1)S(1)}, bf16[400,128]{1,0:T(8,128)(2,1)S(1)}, u32[]{:S(2)}, u32[]{:S(2)}) collective-permute-start(bf16[400,128]{1,0:T(8,128)(2,1)S(1)} %collective-permute-done.2.refs_3_), channel_id=1, source_target_pairs={{0,4},{4,0},{8,12},{12,8},{16,20},{20,16},{24,28},{28,24},{1,5},{5... | collective-permute-start | bytes 307208 | tf_op jit(solution)/shard_map/ppermute | solution.py:261
  39.5 8.0 %collective-permute-start.12 = (bf16[1008,128]{1,0:T(8,128)(2,1)S(1)}, bf16[1008,128]{1,0:T(8,128)(2,1)S(1)}, u32[]{:S(2)}, u32[]{:S(2)}) collective-permute-start(bf16[1008,128]{1,0:T(8,128)(2,1)S(1)} %get-tuple-element.48), channel_id=1, source_target_pairs={{0,1},{1,0},{2,3},{3,2},{4,5},{5,4},{6,7},{7,6},{8,9},{9,8},{10,11... | collective-permute-start | bytes 774152 | tf_op jit(solution)/shard_map/ppermute | solution.py:264
  39.5 7.9 %collective-permute-start.10 = (bf16[400,256]{1,0:T(8,128)(2,1)S(1)}, bf16[400,256]{1,0:T(8,128)(2,1)S(1)}, u32[]{:S(2)}, u32[]{:S(2)}) collective-permute-start(bf16[400,256]{1,0:T(8,128)(2,1)S(1)} %get-tuple-element.41), channel_id=1, source_target_pairs={{0,4},{4,0},{8,12},{12,8},{16,20},{20,16},{24,28},{28,24},{1,5},{5... | collective-permute-start | bytes 614408 | tf_op jit(solution)/shard_map/ppermute | solution.py:261
  40.7 12.6 %collective-permute-start.16 = (bf16[400,256]{1,0:T(8,128)(2,1)S(1)}, bf16[400,256]{1,0:T(8,128)(2,1)S(1)}, u32[]{:S(2)}, u32[]{:S(2)}) collective-permute-start(bf16[400,256]{1,0:T(8,128)(2,1)S(1)} %get-tuple-element.55), channel_id=1, source_target_pairs={{0,4},{4,0},{8,12},{12,8},{16,20},{20,16},{24,28},{28,24},{1,5},{5... | collective-permute-start | bytes 614408 | tf_op jit(solution)/shard_map/ppermute | solution.py:261
  41.6 4.1 %collective-permute-start.13 = (bf16[208,128]{1,0:T(8,128)(2,1)S(1)}, bf16[208,128]{1,0:T(8,128)(2,1)S(1)}, u32[]{:S(2)}, u32[]{:S(2)}) collective-permute-start(bf16[208,128]{1,0:T(8,128)(2,1)S(1)} %get-tuple-element.49), channel_id=1, source_target_pairs={{0,2},{1,3},{2,0},{3,1},{4,6},{5,7},{6,4},{7,5},{8,10},{9,11},{10,... | collective-permute-start | bytes 159752 | tf_op jit(solution)/shard_map/ppermute | solution.py:264
  43.1 3.9 %collective-permute-start.14 = (bf16[208,128]{1,0:T(8,128)(2,1)S(1)}, bf16[208,128]{1,0:T(8,128)(2,1)S(1)}, u32[]{:S(2)}, u32[]{:S(2)}) collective-permute-start(bf16[208,128]{1,0:T(8,128)(2,1)S(1)} %get-tuple-element.50), channel_id=1, source_target_pairs={{0,3},{1,2},{2,1},{3,0},{4,7},{5,6},{6,5},{7,4},{8,11},{9,10},{10,... | collective-permute-start | bytes 159752 | tf_op jit(solution)/shard_map/ppermute | solution.py:264
  47.5 23.0 %copy-start.4 = (f32[128,400]{0,1:T(8,128)S(1)}, f32[128,400]{0,1:T(8,128)}, u32[]{:S(2)}) copy-start(f32[128,400]{0,1:T(8,128)} %param.10) | copy-start | bytes 614404
  47.5 23.0 %copy-start.6 = (f32[128]{0:T(128)S(1)}, f32[128]{0:T(128)}, u32[]{:S(2)}) copy-start(f32[128]{0:T(128)} %param.11) | copy-start | bytes 1540
  47.6 25.9 %copy-start.1 = (f32[256,400]{0,1:T(8,128)S(1)}, f32[256,400]{0,1:T(8,128)}, u32[]{:S(2)}) copy-start(f32[256,400]{0,1:T(8,128)} %param.14) | copy-start | bytes 1228804
  47.6 25.9 %copy-start.5 = (f32[256]{0:T(256)S(1)}, f32[256]{0:T(256)}, u32[]{:S(2)}) copy-start(f32[256]{0:T(256)} %param.15) | copy-start | bytes 3076
  47.6 5.7 %collective-permute-start.15 = (bf16[400,128]{1,0:T(8,128)(2,1)S(1)}, bf16[400,128]{1,0:T(8,128)(2,1)S(1)}, u32[]{:S(2)}, u32[]{:S(2)}) collective-permute-start(bf16[400,128]{1,0:T(8,128)(2,1)S(1)} %get-tuple-element.52), channel_id=1, source_target_pairs={{0,2},{1,3},{2,0},{3,1},{4,6},{5,7},{6,4},{7,5},{8,10},{9,11},{10,... | collective-permute-start | bytes 307208 | tf_op jit(solution)/shard_map/ppermute | solution.py:264
  49.2 4.1 %collective-permute-start.17 = (bf16[208,128]{1,0:T(8,128)(2,1)S(1)}, bf16[208,128]{1,0:T(8,128)(2,1)S(1)}, u32[]{:S(2)}, u32[]{:S(2)}) collective-permute-start(bf16[208,128]{1,0:T(8,128)(2,1)S(1)} %get-tuple-element.56.refs_2_), channel_id=1, source_target_pairs={{0,8},{4,12},{8,0},{12,4},{16,24},{20,28},{24,16},{28,20},{1,9},{5... | collective-permute-start | bytes 159752 | tf_op jit(solution)/shard_map/ppermute | solution.py:261
  50.6 11.6 %collective-permute-start.20 = (bf16[400,128]{1,0:T(8,128)(2,1)S(1)}, bf16[400,128]{1,0:T(8,128)(2,1)S(1)}, u32[]{:S(2)}, u32[]{:S(2)}) collective-permute-start(bf16[400,128]{1,0:T(8,128)(2,1)S(1)} %get-tuple-element.59), channel_id=1, source_target_pairs={{0,17},{1,18},{2,19},{3,16},{4,21},{5,22},{6,23},{7,20},{8,25},{9,... | collective-permute-start | bytes 307208 | tf_op jit(solution)/shard_map/ppermute | solution.py:271
  50.8 11.4 %collective-permute-start.21 = (bf16[400,128]{1,0:T(8,128)(2,1)S(1)}, bf16[400,128]{1,0:T(8,128)(2,1)S(1)}, u32[]{:S(2)}, u32[]{:S(2)}) collective-permute-start(bf16[400,128]{1,0:T(8,128)(2,1)S(1)} %get-tuple-element.60), channel_id=1, source_target_pairs={{0,25},{1,26},{2,27},{3,24},{4,29},{5,30},{6,31},{7,28},{8,17},{9,... | collective-permute-start | bytes 307208 | tf_op jit(solution)/shard_map/ppermute | solution.py:271
  53.4 10.8 %collective-permute-start.22 = (bf16[208,128]{1,0:T(8,128)(2,1)S(1)}, bf16[208,128]{1,0:T(8,128)(2,1)S(1)}, u32[]{:S(2)}, u32[]{:S(2)}) collective-permute-start(bf16[208,128]{1,0:T(8,128)(2,1)S(1)} %get-tuple-element.63.refs_0_), channel_id=1, source_target_pairs={{0,16},{4,20},{8,24},{12,28},{16,0},{20,4},{24,8},{28,12},{1,17},{... | collective-permute-start | bytes 159752 | tf_op jit(solution)/shard_map/ppermute | solution.py:261
  55.4 10.4 %collective-permute-start.18 = (bf16[400,128]{1,0:T(8,128)(2,1)S(1)}, bf16[400,128]{1,0:T(8,128)(2,1)S(1)}, u32[]{:S(2)}, u32[]{:S(2)}) collective-permute-start(bf16[400,128]{1,0:T(8,128)(2,1)S(1)} %get-tuple-element.57), channel_id=1, source_target_pairs={{0,1},{1,2},{2,3},{3,0},{4,5},{5,6},{6,7},{7,4},{8,9},{9,10},{10,1... | collective-permute-start | bytes 307208 | tf_op jit(solution)/shard_map/ppermute | solution.py:271
  55.4 10.4 %collective-permute-start.19 = (bf16[400,128]{1,0:T(8,128)(2,1)S(1)}, bf16[400,128]{1,0:T(8,128)(2,1)S(1)}, u32[]{:S(2)}, u32[]{:S(2)}) collective-permute-start(bf16[400,128]{1,0:T(8,128)(2,1)S(1)} %get-tuple-element.58), channel_id=1, source_target_pairs={{0,9},{1,10},{2,11},{3,8},{4,13},{5,14},{6,15},{7,12},{8,1},{9,2},... | collective-permute-start | bytes 307208 | tf_op jit(solution)/shard_map/ppermute | solution.py:271
  64.2 4.3 %collective-permute-start.23 = (bf16[208,128]{1,0:T(8,128)(2,1)S(1)}, bf16[208,128]{1,0:T(8,128)(2,1)S(1)}, u32[]{:S(2)}, u32[]{:S(2)}) collective-permute-start(bf16[208,128]{1,0:T(8,128)(2,1)S(1)} %shard_map.156.refs_0_), channel_id=1, source_target_pairs={{0,4},{4,0},{8,12},{12,8},{16,20},{20,16},{24,28},{28,24},{1,5},{5... | collective-permute-start | bytes 159752 | tf_op jit(solution)/shard_map/ppermute | solution.py:261
  68.5 3.5 %collective-permute-start.24 = (bf16[208,128]{1,0:T(8,128)(2,1)S(1)}, bf16[208,128]{1,0:T(8,128)(2,1)S(1)}, u32[]{:S(2)}, u32[]{:S(2)}) collective-permute-start(bf16[208,128]{1,0:T(8,128)(2,1)S(1)} %shard_map.157.refs_0_), channel_id=1, source_target_pairs={{0,1},{1,0},{2,3},{3,2},{4,5},{5,4},{6,7},{7,6},{8,9},{9,8},{10,11... | collective-permute-start | bytes 159752 | tf_op jit(solution)/shard_map/ppermute | solution.py:264
  68.6 4.7 %collective-permute-start.25 = (bf16[208,128]{1,0:T(8,128)(2,1)S(1)}, bf16[208,128]{1,0:T(8,128)(2,1)S(1)}, u32[]{:S(2)}, u32[]{:S(2)}) collective-permute-start(bf16[208,128]{1,0:T(8,128)(2,1)S(1)} %shard_map.157.refs_0_), channel_id=1, source_target_pairs={{0,2},{1,3},{2,0},{3,1},{4,6},{5,7},{6,4},{7,5},{8,10},{9,11},{10,... | collective-permute-start | bytes 159752 | tf_op jit(solution)/shard_map/ppermute | solution.py:264
  69.2 4.3 %collective-permute-start.26 = (bf16[208,128]{1,0:T(8,128)(2,1)S(1)}, bf16[208,128]{1,0:T(8,128)(2,1)S(1)}, u32[]{:S(2)}, u32[]{:S(2)}) collective-permute-start(bf16[208,128]{1,0:T(8,128)(2,1)S(1)} %shard_map.157.refs_0_), channel_id=1, source_target_pairs={{0,3},{1,2},{2,1},{3,0},{4,7},{5,6},{6,5},{7,4},{8,11},{9,10},{10,... | collective-permute-start | bytes 159752 | tf_op jit(solution)/shard_map/ppermute | solution.py:264

commit v7 on v6

--- a/solution.py
+++ b/solution.py
@@ -13,6 +13,10 @@
 F32 = jnp.float32
 VMEM_LIMIT = 32 * 1024 * 1024
 LANES = 128
+COST_JOIN = 6e9
+COST_UPDATE = 6e9
+COST_HIGH = 6e9
+COST_LOW = 6e9
 
 
 def dot(a, b, a_dim, b_dim):
@@ -28,7 +32,7 @@
     return most if size % most == 0 else size
 
 
-def call(body, out_shape, scratch=(), here=None, after=()):
+def call(body, out_shape, scratch=(), here=None, after=(), flops=0):
     def run(*args):
         specs = [pl.BlockSpec(memory_space=pltpu.VMEM)] * len(args)
         if here is not None:
@@ -49,7 +53,7 @@
             in_specs=specs,
             scratch_shapes=list(scratch),
             compiler_params=pltpu.CompilerParams(vmem_limit_bytes=VMEM_LIMIT),
-            cost_estimate=pl.CostEstimate(flops=0, bytes_accessed=0, transcendentals=0),
+            cost_estimate=pl.CostEstimate(flops=int(flops), bytes_accessed=0, transcendentals=0),
         )(*args)
 
     return run
@@ -63,19 +67,36 @@
     out_ref[...] = in_ref[...].astype(BF)
 
 
-def count_body(edges, ids_ref, relation_ref, table_ref, state_ref, out_ref, relation_bf_ref, pack_ref):
-    groups = out_ref.shape[0]
-    slots = (ids_ref.shape[1] - 3 * edges) // groups
-    for g in range(groups):
-        ids = ids_ref[:, 3 * edges + g * slots:3 * edges + (g + 1) * slots]
+def count_body(far_right, outer, rows, slots, ids_ref, relation_ref, place_ref, out_ref, relation_bf_ref, local_ref):
+    def local(ids, here, half):
+        block = (ids // rows) ^ here
+        return (block % 2 * half + block // 2) * rows + ids % rows
+
+    ids = ids_ref[...]
+    local_ref[...] = ids
+    local_ref[0:1, :] = local(ids[0:1], place_ref[0], far_right)
+    local_ref[1:2, :] = local(ids[1:2], place_ref[1], outer)
+    for g in range(out_ref.shape[0]):
+        negative = local(ids[3 + g:4 + g, :slots], place_ref[1], outer)
         for at in range(0, out_ref.shape[1], LANES):
             spot = lax.broadcasted_iota(jnp.int32, (LANES, slots), 0) + at
-            total = jnp.sum(jnp.where(spot == ids, NEG_WEIGHT, 0.0), axis=1, keepdims=True)
+            total = jnp.sum(jnp.where(spot == negative, NEG_WEIGHT, 0.0), axis=1, keepdims=True)
             out_ref[g, at:at + LANES, :] = jnp.broadcast_to(total, (LANES, LANES))
     relation_bf_ref[...] = relation_ref[...].astype(BF)
+
+
+def pack_body(table_ref, state_ref, pack_ref):
     width = table_ref.shape[0]
     pack_ref[:width, :] = table_ref[...]
     pack_ref[width:, :] = jnp.broadcast_to(state_ref[...], (pack_ref.shape[0] - width, LANES))
+
+
+def join_body(*refs):
+    out_ref = refs[-1]
+    at = 0
+    for ref in refs[:-1]:
+        out_ref[:, at:at + ref.shape[1]] = ref[...]
+        at += ref.shape[1]
 
 
 def query_body(blocks, *refs):
@@ -89,9 +110,9 @@
     half_rows = near.shape[1]
     for at in range(0, edges, step):
         cols = slice(at, at + step)
-        pick = hot(ids_ref[:, cols], 2 * half_rows)
+        pick = hot(ids_ref[0:1, cols], 2 * half_rows)
         s = dot(near, pick[:half_rows], 1, 0) + dot(sibling_ref[...], pick[half_rows:], 1, 0)
-        o = dot(relation, hot(ids_ref[:, 2 * edges + at:2 * edges + at + step], relation.shape[1]), 1, 0)
+        o = dot(relation, hot(ids_ref[2:3, cols], relation.shape[1]), 1, 0)
         s_ref[:, cols] = s.astype(BF)
         o_ref[:, cols] = o.astype(BF)
         s_re, s_im, o_re, o_im = s[:half], s[half:], o[:half], o[half:]
@@ -109,7 +130,7 @@
         cols = slice(at, at + step)
         scores = dot(rows_t, q_ref[:, cols], 1, 0)
         spot = lax.broadcasted_iota(jnp.int32, (count, step), 0) + base
-        h = jnp.where(spot == ids_ref[:, edges + at:edges + at + step], 1.0, 0.0)
+        h = jnp.where(spot == ids_ref[1:2, cols], 1.0, 0.0)
         w = weight_ref[at // (edges // groups), base:base + count, :]
         w = jnp.concatenate([w] * (step // LANES), axis=1)
         m = (w + h) * (0.5 * jnp.tanh(0.5 * scores) + 0.5) - h
@@ -119,8 +140,7 @@
 def near_body(blocks, *refs):
     block_refs, refs = refs[:blocks], refs[blocks:]
     q_ref, weight_ref, ids_ref, right_ref, qg_ref, rows_ref, m_ref = refs
-    for k, ref in enumerate(block_refs):
-        rows_ref[:, k * LANES:(k + 1) * LANES] = ref[...]
+    join_body(*block_refs, rows_ref)
     grad_matrix(rows_ref, q_ref, weight_ref, ids_ref, m_ref, 0)
     right_ref[...] = dot(q_ref[...], m_ref[...], 1, 1)
     qg_ref[...] = dot(rows_ref[...], m_ref[...], 1, 0)
@@ -129,8 +149,7 @@
 def far_body(blocks, *refs):
     block_refs, refs = refs[:blocks], refs[blocks:]
     q_ref, weight_ref, ids_ref, m_ref, hi_ref, lo_ref, rows_ref = refs
-    for k, ref in enumerate(block_refs):
-        rows_ref[:, k * LANES:(k + 1) * LANES] = ref[...]
+    join_body(*block_refs, rows_ref)
     count = rows_ref.shape[1]
     grad_matrix(rows_ref, q_ref, weight_ref, ids_ref, m_ref, count)
     far = dot(q_ref[...], m_ref[...], 1, 1).astype(BF)
@@ -143,8 +162,7 @@
     m_ref, qg_ref, s_ref, o_ref, ids_ref, here_ref, near_ref = refs[:7]
     piece_refs, refs = refs[7:7 + pieces], refs[7 + pieces:]
     rows_ref, left_ref, kinds_ref, tall_ref = refs
-    for k, ref in enumerate(block_refs):
-        rows_ref[:, k * LANES:(k + 1) * LANES] = ref[...]
+    join_body(*block_refs, rows_ref)
     width, edges = qg_ref.shape
     half = width // 2
     step = step_of(edges)
@@ -157,8 +175,8 @@
         s_re, s_im, o_re, o_im = s[:half], s[half:], o[:half], o[half:]
         by_kind = jnp.concatenate([g_re * s_re + g_im * s_im, g_im * s_re - g_re * s_im], axis=0).astype(BF)
         by_source = jnp.concatenate([g_re * o_re + g_im * o_im, g_im * o_re - g_re * o_im], axis=0).astype(BF)
-        kinds = dot(by_kind, hot(ids_ref[:, 2 * edges + at:2 * edges + at + step], kinds_ref.shape[1]), 1, 1)
-        left = dot(by_source, hot(ids_ref[:, cols], left_ref.shape[1]), 1, 1)
+        kinds = dot(by_kind, hot(ids_ref[2:3, cols], kinds_ref.shape[1]), 1, 1)
+        left = dot(by_source, hot(ids_ref[0:1, cols], left_ref.shape[1]), 1, 1)
         if at == 0:
             kinds_ref[...] = kinds
             left_ref[...] = left
@@ -204,13 +222,9 @@
         new_ref[:, cols] = table_ref[:, cols] - g * (LEARN_RATE * lax.rsqrt(state))
 
 
-def high_body(blocks, pieces, near_ref, got_ref, left_ref, *refs):
+def piece_body(pieces, left_ref, *refs):
     piece_refs, refs = refs[:pieces], refs[pieces:]
-    block_refs, mine_ref, left_own_ref, left_refs = refs[:blocks], refs[blocks], refs[blocks + 1], refs[blocks + 2:]
-    base = near_ref.shape[1] - blocks * LANES
-    for k, ref in enumerate(block_refs):
-        cols = slice(k * LANES, (k + 1) * LANES)
-        ref[...] = (near_ref[:, base + k * LANES:base + (k + 1) * LANES] + got_ref[:, cols].astype(F32)).astype(BF)
+    mine_ref, left_own_ref, left_refs = refs[0], refs[1], refs[2:]
     width = left_ref.shape[0]
     size = mine_ref.shape[0]
     core_ref = piece_refs[1]
@@ -227,12 +241,11 @@
             left_refs[k - 1][...] = total.astype(BF)
 
 
-def low_body(blocks, near_ref, got_ref, piece_ref, other_ref, *refs):
-    block_refs, mine_ref = refs[:blocks], refs[blocks]
-    mine_ref[...] = (piece_ref[...].astype(F32) + other_ref[...].astype(F32)).astype(BF)
+def chunk_body(base, near_ref, got_ref, *block_refs):
     for k, ref in enumerate(block_refs):
         cols = slice(k * LANES, (k + 1) * LANES)
-        ref[...] = (near_ref[:, cols] + got_ref[:, cols].astype(F32)).astype(BF)
+        total = near_ref[:, base + k * LANES:base + (k + 1) * LANES] + got_ref[:, cols].astype(F32)
+        ref[...] = total.astype(BF)
 
 
 def sum_body(piece_ref, other_ref, out_ref):
@@ -288,34 +301,27 @@
         table_bf = shape(width, edges, dtype=BF)
 
         right_bf = call(cast_body, one_block)(right_t)
-        near = {k: swap_left(right_bf, 2 * k) for k in range(outer - 1, 0, -1)}
-        near[0] = right_bf
-        other = {0: swap_left(right_bf, 1)}
-        left_bf = call(cast_body, one_block)(left_t)
+        near = [right_bf] + [swap_left(right_bf, 2 * k) for k in range(1, outer)]
+        other_own = swap_left(right_bf, 1)
+        blocks = shape(width, half - rows, dtype=BF)
+        joined = call(join_body, blocks, flops=COST_JOIN)(*near[1:])
+        other_rest = swap_left(joined, 1)
+
+        ids = [source_ids, target_ids, relation_ids, negative_ids]
+        longest = max(i.shape[-1] for i in ids)
+        ids = [i.reshape(-1, i.shape[-1]) for i in ids]
+        ids = jnp.concatenate([jnp.pad(i, ((0, 0), (0, longest - i.shape[-1]))) for i in ids], axis=0)
+        ids = lax.ppermute(ids, "right", [(i, (i - 1) % n_right) for i in range(n_right)])
+        left_bf = call(cast_body, one_block, after=(other_own, ids))(left_t)
         half_left = [left_bf] + [swap_right(left_bf, 2 * k) for k in range(1, far_right)]
-
-        def local(ids, here, half):
-            block = (ids // rows) ^ here
-            return ((block % 2 * half + block // 2) * rows + ids % rows).reshape(-1)
-
-        before_r = (here_r + n_right - 1) % n_right
-        ids = [
-            local(source_ids, before_r, far_right), local(target_ids, here_l, outer),
-            relation_ids.reshape(-1), local(negative_ids, here_l, outer),
-        ]
-        ids = lax.ppermute(
-            jnp.concatenate(ids).reshape(1, -1), "right", [(i, (i - 1) % n_right) for i in range(n_right)]
-        )
         sibling_left = swap_right(jnp.concatenate(half_left, axis=1), 1)
-        weight, relation_bf, pack = call(
-            functools.partial(count_body, edges),
-            (shape(groups, n_rows, LANES), shape(width, nrel, dtype=BF), shape(width + 8, rows)),
-        )(ids, relation_t, right_t, right_state[None, :])
-        for k in range(1, outer):
-            other[k] = swap_left(near[k], 1)
-        near = [near[k] for k in range(outer)]
-        other = [other[k] for k in range(outer)]
-        moved = next_column(pack, 0)
+        place = jnp.stack([here_r, here_l]).astype(jnp.int32)
+        weight, relation_bf, ids = call(
+            functools.partial(count_body, far_right, outer, rows, negative_ids.shape[-1]),
+            (shape(groups, n_rows, LANES), shape(width, nrel, dtype=BF), shape(*ids.shape, dtype=jnp.int32)),
+            here=place,
+        )(ids, relation_t)
+        moved = next_column(call(pack_body, shape(width + 8, rows), after=(joined,))(right_t, right_state[None, :]), 0)
 
         s, o, q = call(functools.partial(query_body, far_right), (table_bf, table_bf, table_bf))(
             *half_left, sibling_left, relation_bf, ids
@@ -328,8 +334,8 @@
         )(*near, q, weight, ids)
         chunk = shape(width, half // 2, dtype=BF)
         m, far_hi, far_lo = call(
-            functools.partial(far_body, outer), (shape(half, edges, dtype=BF), chunk, chunk), [part], after=(qg_near,)
-        )(*other, q, weight, ids)
+            functools.partial(far_body, 2), (shape(half, edges, dtype=BF), chunk, chunk), [part], after=(qg_near,)
+        )(other_own, other_rest, q, weight, ids)
         got_hi = swap_left(far_hi, 1)
         got_lo = swap_left(far_lo, 1)
         tall = nrel // LANES * width
@@ -338,43 +344,39 @@
         core_piece = shape(far_right * width + size, LANES, dtype=BF)
         left_rows = n_right * rows
         left_near, *pieces = call(
-            functools.partial(back_body, outer, n_right),
+            functools.partial(back_body, 2, n_right),
             (shape(width, left_rows // 2), piece, core_piece) + (piece,) * (n_right - 2),
             [part, pltpu.VMEM((width, left_rows), F32), pltpu.VMEM((width, nrel), F32),
              pltpu.VMEM((size * n_right, LANES), F32)],
             me,
             after=(moved,),
-        )(*other, m, qg_near, s, o, ids)
+        )(other_own, other_rest, m, qg_near, s, o, ids)
+
+        some = outer // 2
+        outs = (one_block,) * some
+        high = call(functools.partial(chunk_body, half // 2), outs, flops=COST_HIGH)(right_near, got_hi)
+        low = call(functools.partial(chunk_body, 0), outs, flops=COST_LOW)(right_near, got_lo)
+        right_got = [next_column(block, 2 * (some + k)) for k, block in enumerate(high)]
+        right_got += [next_column(block, 2 * k) for k, block in enumerate(low)]
+
+        def update(got, table, state, flops=0):
+            outs = (shape(width, rows), shape(1, rows))
+            return call(functools.partial(update_body, len(got)), outs, flops=flops)(*got, table, state)
+
+        right_new, right_state_new = update(right_got, moved, moved[width:], COST_UPDATE)
 
         pieces = [pieces[0]] + [swap_right(pieces[k], k) for k in range(1, n_right)]
-        some = outer // 2
-        outs = call(
-            functools.partial(high_body, some, n_right),
-            (one_block,) * some + (piece, shape(width, rows)) + (one_block,) * (far_right - 1),
-        )(right_near, got_hi, left_near, *pieces)
-        high, mine, left_own, left_blocks = outs[:some], outs[some], outs[some + 1], outs[some + 2:]
-        right_high = [next_column(block, 2 * (some + k)) for k, block in enumerate(high)]
-        first = swap_left(mine, 2)
+        mine, left_own, *left_blocks = call(
+            functools.partial(piece_body, n_right), (piece, shape(width, rows)) + (one_block,) * (far_right - 1)
+        )(left_near, *pieces)
         left_got = [swap_right(block, 2 * (k + 1)) for k, block in enumerate(left_blocks)]
-        *low, mine = call(
-            functools.partial(low_body, some), (one_block,) * some + (piece,), after=tuple(left_got)
-        )(right_near, got_lo, mine, first)
-        right_low = [next_column(block, 2 * k) for k, block in enumerate(low)]
-        add = functools.partial(call, sum_body, piece)
-        bit = 4
+        bit = 2
         while bit < n_left:
-            mine = add(after=right_high if 2 * bit >= n_left else ())(mine, swap_left(mine, bit))
+            mine = call(sum_body, piece)(mine, swap_left(mine, bit))
             bit *= 2
-        mine = add(after=right_low)(mine, swap_left(mine, 1))
+        mine = call(sum_body, piece, after=(right_state_new,))(mine, swap_left(mine, 1))
         pieces = [mine] + [swap_right(mine, k) for k in range(1, n_right)]
-
-        def update(got, table, state):
-            return call(functools.partial(update_body, len(got)), (shape(width, rows), shape(1, rows)))(
-                *got, table, state
-            )
-
         left_new, left_state_new = update([left_own, *left_got], left_t, left_state[None, :])
-        right_new, right_state_new = update([*right_low, *right_high], moved, moved[width:])
         relation_new, relation_state_new = call(
             functools.partial(relation_body, n_right),
             (shape(width, nrel), shape(1, nrel)),

time: 74.8 us -> 62.3 us (0.83)
  starting transfers between devices: 32.4 us -> 26.6 us
  waiting for transfers between devices: 24.6 us -> 20.4 us
  other arithmetic: 3.01 us -> 0.85 us
  local copies, waits for them, and re-layouts: 3.53 us -> 2.55 us
    ppermute x5, waiting for transfers between devices: 4.37 us -> 0.01 us  [next_column(): return lax.ppermute(value, ('left', 'right'), perm)]
    ppermute x12 -> x10, starting transfers between devices: 16.9 us -> 13.4 us  [swap_left(): return lax.ppermute(value, 'left', [(i, i ^ by) for i in range(n_left)])]
    ppermute x12 -> x10, waiting for transfers between devices: 12.7 us -> 14.9 us  [swap_left(): return lax.ppermute(value, 'left', [(i, i ^ by) for i in range(n_left)])]
    ppermute x9, waiting for transfers between devices: 5.99 us -> 3.89 us  [swap_right(): return lax.ppermute(value, 'right', [(i, i ^ by) for i in range(n_right)])]
    ppermute x1, starting transfers between devices: 1.88 us -> 0.06 us  [per_device(): lax.ppermute(ids, 'right', [(i, (i - 1) % n_right) for i in range(n_right)])]
    add x2 -> x0, other arithmetic: 1.52 us -> none  [local(): return ((block % 2 * half + block // 2) * rows + ids % rows).reshape(-1)]
    ppermute x9, starting transfers between devices: 8.12 us -> 6.73 us  [swap_right(): return lax.ppermute(value, 'right', [(i, i ^ by) for i in range(n_right)])]
    unnamed x17 -> x18, local copies, waits for them, and re-layouts: 3.53 us -> 2.55 us
  transfers between devices with their start and end apart: 27 -> 25, of which waited for: 13 -> 11; matrix products, arithmetic and copies ran while one was open for 4% -> 1% of each run, Pallas kernels for 9% -> 16%
where the time goes in v7:
time: 62.3 us; the launch traced here: 62.1 us
  starting transfers between devices  26.6 us (43%)
  waiting for transfers between devices  20.4 us (33%)
  Pallas kernels  10.8 us (17%)
  local copies, waits for them, and re-layouts  2.55 us (4%)
  other arithmetic  0.85 us (1%)
  between operations  0.83 us (1%)
    ppermute x10, waiting for transfers between devices, swap_left(): return lax.ppermute(value, 'left', [(i, i ^ by) for i in range(n_left)])  14.9 us
    ppermute x10, starting transfers between devices, swap_left(): return lax.ppermute(value, 'left', [(i, i ^ by) for i in range(n_left)])  13.4 us
    pallas_call x18, Pallas kernels, run(): pl.pallas_call(inner, out_shape=out_shape, in_specs=specs, scratch_shapes...  10.8 us
    ppermute x9, starting transfers between devices, swap_right(): return lax.ppermute(value, 'right', [(i, i ^ by) for i in range(n_right)])  6.73 us
    ppermute x5, starting transfers between devices, next_column(): return lax.ppermute(value, ('left', 'right'), perm)  6.38 us
    ppermute x9, waiting for transfers between devices, swap_right(): return lax.ppermute(value, 'right', [(i, i ^ by) for i in range(n_right)])  3.89 us
    unnamed x18, local copies, waits for them, and re-layouts  2.55 us
    ppermute x1, waiting for transfers between devices, per_device(): lax.ppermute(ids, 'right', [(i, (i - 1) % n_right) for i in range(n_right)])  1.59 us
  transfers between devices with their start and end apart: 25, of which 11 were waited for; matrix products, arithmetic and copies ran while one was open for 1% of the time, Pallas kernels for 16%

profile of v7, /device:TPU:0, one launch (start us, length us, event | category | flops | bytes accessed | tf_op | source)
XLA Modules:
  0.0 62.1 jit_solution(16900005757390970717)
XLA Ops:
  0.6 0.9 %copy-done.3 = f32[128,400]{0,1:T(8,128)S(1)} copy-done((f32[128,400]{0,1:T(8,128)S(1)}, f32[128,400]{0,1:T(8,128)}, u32[]{:S(2)}) %copy-start.3) | copy-done | bytes 204824
  1.6 5.1 %collective-permute-start.3 = (bf16[400,128]{1,0:T(8,128)(2,1)S(1)}, bf16[400,128]{1,0:T(8,128)(2,1)S(1)}, u32[]{:S(2)}, u32[]{:S(2)}) collective-permute-start(bf16[400,128]{1,0:T(8,128)(2,1)S(1)} %shard_map.145.refs_0_), channel_id=1, source_target_pairs={{0,24},{4,28},{8,16},{12,20},{16,8},{20,12},{24,0},{28,4},{1,25},{... | collective-permute-start | bytes 307208 | tf_op jit(solution)/shard_map/ppermute | solution.py:274
  6.7 0.6 %collective-permute-start.1 = (bf16[400,128]{1,0:T(8,128)(2,1)S(1)}, bf16[400,128]{1,0:T(8,128)(2,1)S(1)}, u32[]{:S(2)}, u32[]{:S(2)}) collective-permute-start(bf16[400,128]{1,0:T(8,128)(2,1)S(1)} %shard_map.145.refs_0_), channel_id=1, source_target_pairs={{0,8},{4,12},{8,0},{12,4},{16,24},{20,28},{24,16},{28,20},{1,9},{5... | collective-permute-start | bytes 307208 | tf_op jit(solution)/shard_map/ppermute | solution.py:274
  7.3 1.7 %collective-permute-start = (bf16[400,128]{1,0:T(8,128)(2,1)S(1)}, bf16[400,128]{1,0:T(8,128)(2,1)S(1)}, u32[]{:S(2)}, u32[]{:S(2)}) collective-permute-start(bf16[400,128]{1,0:T(8,128)(2,1)S(1)} %shard_map.145.refs_0_), channel_id=1, source_target_pairs={{0,4},{4,0},{8,12},{12,8},{16,20},{20,16},{24,28},{28,24},{1,5},{5... | collective-permute-start | bytes 307208 | tf_op jit(solution)/shard_map/ppermute | solution.py:274
  9.0 0.8 %pad_add_fusion = s32[5,1024]{1,0:T(8,128)S(1)} fusion(s32[2,1024]{1,0:T(2,128)} %bitcast.28, s32[1,1024]{1,0:T(1,128)} %bitcast.29, s32[1,1024]{1,0:T(1,128)} %bitcast.30, s32[1,1024]{1,0:T(1,128)} %bitcast.31), kind=kLoop, calls=%fused_computation.1 | loop fusion | flops 15360 | bytes 40960 | tf_op jit(solution)/shard_map/concatenate | solution.py:313
  9.8 1.6 %collective-permute-done.5.refs_2_.ids_ref = s32[5,1024]{1,0:T(8,128)S(1)} collective-permute-done((s32[5,1024]{1,0:T(8,128)S(1)}, s32[5,1024]{1,0:T(8,128)S(1)}, u32[]{:S(2)}, u32[]{:S(2)}) %collective-permute-start.5) | collective-permute-done | bytes 20512 | tf_op jit(solution)/shard_map/ppermute | solution.py:314
  11.4 0.6 collective-permute-done.refs_1_.refs_0_
  12.0 0.9 %copy-done.1 = f32[128,400]{0,1:T(8,128)S(1)} copy-done((f32[128,400]{0,1:T(8,128)S(1)}, f32[128,400]{0,1:T(8,128)}, u32[]{:S(2)}) %copy-start.1) | copy-done | bytes 204824
  13.0 1.7 %collective-permute-start.6 = (bf16[400,128]{1,0:T(8,128)(2,1)S(1)}, bf16[400,128]{1,0:T(8,128)(2,1)S(1)}, u32[]{:S(2)}, u32[]{:S(2)}) collective-permute-start(bf16[400,128]{1,0:T(8,128)(2,1)S(1)} %shard_map.147.refs_0_), channel_id=1, source_target_pairs={{0,2},{1,3},{2,0},{3,1},{4,6},{5,7},{6,4},{7,5},{8,10},{9,11},{10,... | collective-permute-start | bytes 307208 | tf_op jit(solution)/shard_map/ppermute | solution.py:277
  14.7 0.6 %collective-permute-done.2.refs_1_.refs_2_ = bf16[400,128]{1,0:T(8,128)(2,1)S(1)} collective-permute-done((bf16[400,128]{1,0:T(8,128)(2,1)S(1)}, bf16[400,128]{1,0:T(8,128)(2,1)S(1)}, u32[]{:S(2)}, u32[]{:S(2)}) %collective-permute-start.2) | collective-permute-done | bytes 102432 | tf_op jit(solution)/shard_map/ppermute | solution.py:274
  15.4 1.6 %collective-permute-start.4 = (bf16[400,384]{1,0:T(8,128)(2,1)S(1)}, bf16[400,384]{1,0:T(8,128)(2,1)S(1)}, u32[]{:S(2)}, u32[]{:S(2)}) collective-permute-start(bf16[400,384]{1,0:T(8,128)(2,1)S(1)} %shard_map.146.refs_2_), channel_id=1, source_target_pairs={{0,4},{4,0},{8,12},{12,8},{16,20},{20,16},{24,28},{28,24},{1,5},{5... | collective-permute-start | bytes 921608 | tf_op jit(solution)/shard_map/ppermute | solution.py:274
  17.0 1.8 %collective-permute-done.6.refs_1_ = bf16[400,128]{1,0:T(8,128)(2,1)S(1)} collective-permute-done((bf16[400,128]{1,0:T(8,128)(2,1)S(1)}, bf16[400,128]{1,0:T(8,128)(2,1)S(1)}, u32[]{:S(2)}, u32[]{:S(2)}) %collective-permute-start.6) | collective-permute-done | bytes 102432 | tf_op jit(solution)/shard_map/ppermute | solution.py:277
  18.8 0.2 collective-permute-start.7
  19.0 0.4 collective-permute-start.8
  19.4 0.1 pad_add_fusion.1.place_ref
  19.5 1.6 %shard_map.148 = (f32[2,1024,128]{2,1,0:T(8,128)S(1)}, bf16[400,256]{1,0:T(8,128)(2,1)S(1)}, s32[5,1024]{1,0:T(8,128)S(1)}) custom-call(s32[5,1024]{1,0:T(8,128)S(1)} %collective-permute-done.5.refs_2_.ids_ref, f32[400,256]{1,0:T(8,128)S(1)} %bitcast.18, s32[2]{0:T(128)S(1)} %pad_add_fusion.1.place_ref), custom_call_target="tpu_custom_call" | custom-call | tf_op jit(solution)/shard_map/pallas_call | solution.py:50
  21.1 0.9 %shard_map.149 = (bf16[400,1024]{1,0:T(8,128)(2,1)S(1)}, bf16[400,1024]{1,0:T(8,128)(2,1)S(1)}, bf16[400,1024]{1,0:T(8,128)(2,1)S(1)}) custom-call(bf16[400,128]{1,0:T(8,128)(2,1)S(1)} %shard_map.147.refs_0_, bf16[400,128]{1,0:T(8,128)(2,1)S(1)} %collective-permute-done.6.refs_1_, bf16[400,256]{1,0:T(8,128)(2,1)S(1)} %collective-permute-done.7.refs_2_, ...), custom_call_target="tpu_custom_call" | custom-call | tf_op jit(solution)/shard_map/pallas_call | solution.py:50
  22.0 1.8 %shard_map.150 = (f32[400,512]{1,0:T(8,128)S(1)}, f32[400,1024]{1,0:T(8,128)S(1)}) custom-call(bf16[400,128]{1,0:T(8,128)(2,1)S(1)} %shard_map.145.refs_0_, bf16[400,128]{1,0:T(8,128)(2,1)S(1)} %collective-permute-done.1.refs_0_.refs_1_, bf16[400,128]{1,0:T(8,128)(2,1)S(1)} %collective-permute-done.2.refs_1_.refs_2_, ...), custom_call_target="tpu_custom_call" | custom-call | tf_op jit(solution)/shard_map/pallas_call | solution.py:50
  23.8 1.5 %shard_map.151 = (bf16[512,1024]{1,0:T(8,128)(2,1)S(1)}, bf16[400,256]{1,0:T(8,128)(2,1)S(1)}, bf16[400,256]{1,0:T(8,128)(2,1)S(1)}) custom-call(bf16[400,128]{1,0:T(8,128)(2,1)S(1)} %collective-permute-done.refs_1_.refs_0_, bf16[400,384]{1,0:T(8,128)(2,1)S(1)} %collective-permute-done.4.refs_1_, bf16[400,1024]{1,0:T(8,128)(2,1)S(1)} %get-tuple-element.37.refs_4_.refs_2_, ...), custom_call_target="tpu_custom_call" | custom-call | tf_op jit(solution)/shard_map/pallas_call | solution.py:50
  25.3 1.5 %collective-permute-start.13 = (bf16[400,256]{1,0:T(8,128)(2,1)S(1)}, bf16[400,256]{1,0:T(8,128)(2,1)S(1)}, u32[]{:S(2)}, u32[]{:S(2)}) collective-permute-start(bf16[400,256]{1,0:T(8,128)(2,1)S(1)} %get-tuple-element.53), channel_id=1, source_target_pairs={{0,4},{4,0},{8,12},{12,8},{16,20},{20,16},{24,28},{28,24},{1,5},{5... | collective-permute-start | bytes 614408 | tf_op jit(solution)/shard_map/ppermute | solution.py:274
  26.9 2.2 %shard_map.153 = (f32[400,256]{1,0:T(8,128)S(1)}, bf16[208,128]{1,0:T(8,128)(2,1)S(1)}, bf16[1008,128]{1,0:T(8,128)(2,1)S(1)}, bf16[208,128]{1,0:T(8,128)(2,1)S(1)}, bf16[208,128]{1,0:T(8,128)(2,1)S(1)}) custom-call(bf16[400,128]{1,0:T(8,128)(2,1)S(1)} %collective-permute-done.refs_1_.refs_0_, bf16[400,384]{1,0:T(8,128)(2,1)S(1)} %collective-permute-done.4.refs_1_, ...), custom_call_target="tpu_custom_call" | custom-call | tf_op jit(solution)/shard_map/pallas_call | solution.py:50
  29.1 1.6 %collective-permute-start.10 = (bf16[208,128]{1,0:T(8,128)(2,1)S(1)}, bf16[208,128]{1,0:T(8,128)(2,1)S(1)}, u32[]{:S(2)}, u32[]{:S(2)}) collective-permute-start(bf16[208,128]{1,0:T(8,128)(2,1)S(1)} %get-tuple-element.46), channel_id=1, source_target_pairs={{0,2},{1,3},{2,0},{3,1},{4,6},{5,7},{6,4},{7,5},{8,10},{9,11},{10,... | collective-permute-start | bytes 159752 | tf_op jit(solution)/shard_map/ppermute | solution.py:277
  30.7 0.6 %collective-permute-start.16 = (bf16[400,256]{1,0:T(8,128)(2,1)S(1)}, bf16[400,256]{1,0:T(8,128)(2,1)S(1)}, u32[]{:S(2)}, u32[]{:S(2)}) collective-permute-start(bf16[400,256]{1,0:T(8,128)(2,1)S(1)} %get-tuple-element.56), channel_id=1, source_target_pairs={{0,4},{4,0},{8,12},{12,8},{16,20},{20,16},{24,28},{28,24},{1,5},{5... | collective-permute-start | bytes 614408 | tf_op jit(solution)/shard_map/ppermute | solution.py:274
  31.3 0.3 collective-permute-start.9
  31.6 1.2 %collective-permute-done.13.got_ref = bf16[400,256]{1,0:T(8,128)(2,1)S(1)} collective-permute-done((bf16[400,256]{1,0:T(8,128)(2,1)S(1)}, bf16[400,256]{1,0:T(8,128)(2,1)S(1)}, u32[]{:S(2)}, u32[]{:S(2)}) %collective-permute-start.13) | collective-permute-done | bytes 204832 | tf_op jit(solution)/shard_map/ppermute | solution.py:274
  32.9 0.1 shard_map.156
  32.9 1.7 %collective-permute-start.14 = (bf16[400,128]{1,0:T(8,128)(2,1)S(1)}, bf16[400,128]{1,0:T(8,128)(2,1)S(1)}, u32[]{:S(2)}, u32[]{:S(2)}) collective-permute-start(bf16[400,128]{1,0:T(8,128)(2,1)S(1)} %get-tuple-element.54), channel_id=1, source_target_pairs={{0,17},{1,18},{2,19},{3,16},{4,21},{5,22},{6,23},{7,20},{8,25},{9,... | collective-permute-start | bytes 307208 | tf_op jit(solution)/shard_map/ppermute | solution.py:284
  34.6 2.6 %collective-permute-start.15 = (bf16[400,128]{1,0:T(8,128)(2,1)S(1)}, bf16[400,128]{1,0:T(8,128)(2,1)S(1)}, u32[]{:S(2)}, u32[]{:S(2)}) collective-permute-start(bf16[400,128]{1,0:T(8,128)(2,1)S(1)} %get-tuple-element.55), channel_id=1, source_target_pairs={{0,25},{1,26},{2,27},{3,24},{4,29},{5,30},{6,31},{7,28},{8,17},{9,... | collective-permute-start | bytes 307208 | tf_op jit(solution)/shard_map/ppermute | solution.py:284
  37.2 0.1 shard_map.154
  37.3 0.1 collective-permute-start.19
  37.4 0.9 %collective-permute-done.16.got_ref = bf16[400,256]{1,0:T(8,128)(2,1)S(1)} collective-permute-done((bf16[400,256]{1,0:T(8,128)(2,1)S(1)}, bf16[400,256]{1,0:T(8,128)(2,1)S(1)}, u32[]{:S(2)}, u32[]{:S(2)}) %collective-permute-start.16) | collective-permute-done | bytes 204832 | tf_op jit(solution)/shard_map/ppermute | solution.py:274
  38.3 0.1 shard_map.157
  38.4 1.6 %collective-permute-start.18 = (bf16[400,128]{1,0:T(8,128)(2,1)S(1)}, bf16[400,128]{1,0:T(8,128)(2,1)S(1)}, u32[]{:S(2)}, u32[]{:S(2)}) collective-permute-start(bf16[400,128]{1,0:T(8,128)(2,1)S(1)} %get-tuple-element.58), channel_id=1, source_target_pairs={{0,9},{1,10},{2,11},{3,8},{4,13},{5,14},{6,15},{7,12},{8,1},{9,2},... | collective-permute-start | bytes 307208 | tf_op jit(solution)/shard_map/ppermute | solution.py:284
  40.0 4.6 %collective-permute-done.19.other_ref = bf16[208,128]{1,0:T(8,128)(2,1)S(1)} collective-permute-done((bf16[208,128]{1,0:T(8,128)(2,1)S(1)}, bf16[208,128]{1,0:T(8,128)(2,1)S(1)}, u32[]{:S(2)}, u32[]{:S(2)}) %collective-permute-start.19) | collective-permute-done | bytes 53280 | tf_op jit(solution)/shard_map/ppermute | solution.py:274
  44.7 1.3 %collective-permute-start.20 = (bf16[208,128]{1,0:T(8,128)(2,1)S(1)}, bf16[208,128]{1,0:T(8,128)(2,1)S(1)}, u32[]{:S(2)}, u32[]{:S(2)}) collective-permute-start(bf16[208,128]{1,0:T(8,128)(2,1)S(1)} %shard_map.159.piece_ref), channel_id=1, source_target_pairs={{0,16},{4,20},{8,24},{12,28},{16,0},{20,4},{24,8},{28,12},{1,17},{... | collective-permute-start | bytes 159752 | tf_op jit(solution)/shard_map/ppermute | solution.py:274
  46.0 4.3 %collective-permute-done.20.other_ref = bf16[208,128]{1,0:T(8,128)(2,1)S(1)} collective-permute-done((bf16[208,128]{1,0:T(8,128)(2,1)S(1)}, bf16[208,128]{1,0:T(8,128)(2,1)S(1)}, u32[]{:S(2)}, u32[]{:S(2)}) %collective-permute-start.20) | collective-permute-done | bytes 53280 | tf_op jit(solution)/shard_map/ppermute | solution.py:274
  50.4 1.1 %collective-permute-start.12 = (bf16[400,128]{1,0:T(8,128)(2,1)S(1)}, bf16[400,128]{1,0:T(8,128)(2,1)S(1)}, u32[]{:S(2)}, u32[]{:S(2)}) collective-permute-start(bf16[400,128]{1,0:T(8,128)(2,1)S(1)} %get-tuple-element.49), channel_id=1, source_target_pairs={{0,2},{1,3},{2,0},{3,1},{4,6},{5,7},{6,4},{7,5},{8,10},{9,11},{10,... | collective-permute-start | bytes 307208 | tf_op jit(solution)/shard_map/ppermute | solution.py:277
  51.5 0.9 %collective-permute-start.21 = (bf16[208,128]{1,0:T(8,128)(2,1)S(1)}, bf16[208,128]{1,0:T(8,128)(2,1)S(1)}, u32[]{:S(2)}, u32[]{:S(2)}) collective-permute-start(bf16[208,128]{1,0:T(8,128)(2,1)S(1)} %shard_map.160.refs_0_), channel_id=1, source_target_pairs={{0,4},{4,0},{8,12},{12,8},{16,20},{20,16},{24,28},{28,24},{1,5},{5... | collective-permute-start | bytes 159752 | tf_op jit(solution)/shard_map/ppermute | solution.py:274
  52.3 0.8 %shard_map.158 = (f32[400,128]{1,0:T(8,128)}, f32[1,128]{1,0:T(1,128)}) custom-call(bf16[400,128]{1,0:T(8,128)(2,1)S(1)} %collective-permute-done.14.refs_0_, bf16[400,128]{1,0:T(8,128)(2,1)S(1)} %collective-permute-done.15.refs_1_, bf16[400,128]{1,0:T(8,128)(2,1)S(1)} %collective-permute-done.17.refs_2_, ...), custom_call_target="tpu_custom_call" | custom-call | flops 6000000000 | tf_op jit(solution)/shard_map/pallas_call | solution.py:50
  53.1 2.5 %collective-permute-done.21.refs_1_ = bf16[208,128]{1,0:T(8,128)(2,1)S(1)} collective-permute-done((bf16[208,128]{1,0:T(8,128)(2,1)S(1)}, bf16[208,128]{1,0:T(8,128)(2,1)S(1)}, u32[]{:S(2)}, u32[]{:S(2)}) %collective-permute-start.21) | collective-permute-done | bytes 53280 | tf_op jit(solution)/shard_map/ppermute | solution.py:274
  55.7 0.7 %copy-done.8 = f32[1,128]{1,0:T(1,128)S(1)} copy-done((f32[1,128]{1,0:T(1,128)S(1)}, f32[1,128]{1,0:T(1,128)}, u32[]{:S(2)}) %copy-start.8) | copy-done | bytes 536
  56.4 0.1 collective-permute-start.24
  56.4 1.0 %collective-permute-start.23 = (bf16[208,128]{1,0:T(8,128)(2,1)S(1)}, bf16[208,128]{1,0:T(8,128)(2,1)S(1)}, u32[]{:S(2)}, u32[]{:S(2)}) collective-permute-start(bf16[208,128]{1,0:T(8,128)(2,1)S(1)} %shard_map.161.refs_0_), channel_id=1, source_target_pairs={{0,2},{1,3},{2,0},{3,1},{4,6},{5,7},{6,4},{7,5},{8,10},{9,11},{10,... | collective-permute-start | bytes 159752 | tf_op jit(solution)/shard_map/ppermute | solution.py:277
  57.5 0.8 %collective-permute-start.22 = (bf16[208,128]{1,0:T(8,128)(2,1)S(1)}, bf16[208,128]{1,0:T(8,128)(2,1)S(1)}, u32[]{:S(2)}, u32[]{:S(2)}) collective-permute-start(bf16[208,128]{1,0:T(8,128)(2,1)S(1)} %shard_map.161.refs_0_), channel_id=1, source_target_pairs={{0,1},{1,0},{2,3},{3,2},{4,5},{5,4},{6,7},{7,6},{8,9},{9,8},{10,11... | collective-permute-start | bytes 159752 | tf_op jit(solution)/shard_map/ppermute | solution.py:277
  58.3 0.8 %shard_map.155 = (f32[400,128]{1,0:T(8,128)}, f32[1,128]{1,0:T(1,128)}) custom-call(f32[400,128]{1,0:T(8,128)S(1)} %get-tuple-element.48.refs_0_, bf16[400,128]{1,0:T(8,128)(2,1)S(1)} %collective-permute-done.12.refs_1_, f32[400,128]{1,0:T(8,128)S(1)} %bitcast.21, f32[1,128]{1,0:T(1,128)S(1)} %bitcast.26), custom_call_target="tpu_custom_call" | custom-call | tf_op jit(solution)/shard_map/pallas_call | solution.py:50
  59.1 1.1 %collective-permute-done.24.refs_3_ = bf16[208,128]{1,0:T(8,128)(2,1)S(1)} collective-permute-done((bf16[208,128]{1,0:T(8,128)(2,1)S(1)}, bf16[208,128]{1,0:T(8,128)(2,1)S(1)}, u32[]{:S(2)}, u32[]{:S(2)}) %collective-permute-start.24) | collective-permute-done | bytes 53280 | tf_op jit(solution)/shard_map/ppermute | solution.py:277
  60.1 1.0 %collective-permute-done.23.refs_2_ = bf16[208,128]{1,0:T(8,128)(2,1)S(1)} collective-permute-done((bf16[208,128]{1,0:T(8,128)(2,1)S(1)}, bf16[208,128]{1,0:T(8,128)(2,1)S(1)}, u32[]{:S(2)}, u32[]{:S(2)}) %collective-permute-start.23) | collective-permute-done | bytes 53280 | tf_op jit(solution)/shard_map/ppermute | solution.py:277
  61.2 0.9 %shard_map.162 = (f32[400,256]{1,0:T(8,128)}, f32[1,256]{1,0:T(1,128)}) custom-call(bf16[208,128]{1,0:T(8,128)(2,1)S(1)} %shard_map.161.refs_0_, bf16[208,128]{1,0:T(8,128)(2,1)S(1)} %collective-permute-done.22.refs_1_, bf16[208,128]{1,0:T(8,128)(2,1)S(1)} %collective-permute-done.23.refs_2_, bf16[208,128]{1,0:T(8,128)(2,1)S(1)} %collective-permute-done.24.refs_3_, ...), custom_call_target="tpu_custom_call" | custom-call | tf_op jit(solution)/shard_map/pallas_call | solution.py:50
  (42 shorter events, 0.4 us)
Async XLA Ops:
  0.6 0.9 %copy-start.3 = (f32[128,400]{0,1:T(8,128)S(1)}, f32[128,400]{0,1:T(8,128)}, u32[]{:S(2)}) copy-start(f32[128,400]{0,1:T(8,128)} %param.12) | copy-start | bytes 614404
  1.6 13.1 %collective-permute-start.3 = (bf16[400,128]{1,0:T(8,128)(2,1)S(1)}, bf16[400,128]{1,0:T(8,128)(2,1)S(1)}, u32[]{:S(2)}, u32[]{:S(2)}) collective-permute-start(bf16[400,128]{1,0:T(8,128)(2,1)S(1)} %shard_map.145.refs_0_), channel_id=1, source_target_pairs={{0,24},{4,28},{8,16},{12,20},{16,8},{20,12},{24,0},{28,4},{1,25},{... | collective-permute-start | bytes 307208 | tf_op jit(solution)/shard_map/ppermute | solution.py:274
  6.7 8.6 %collective-permute-start.2 = (bf16[400,128]{1,0:T(8,128)(2,1)S(1)}, bf16[400,128]{1,0:T(8,128)(2,1)S(1)}, u32[]{:S(2)}, u32[]{:S(2)}) collective-permute-start(bf16[400,128]{1,0:T(8,128)(2,1)S(1)} %shard_map.145.refs_0_), channel_id=1, source_target_pairs={{0,16},{4,20},{8,24},{12,28},{16,0},{20,4},{24,8},{28,12},{1,17},{... | collective-permute-start | bytes 307208 | tf_op jit(solution)/shard_map/ppermute | solution.py:274
  6.7 8.6 %collective-permute-start.1 = (bf16[400,128]{1,0:T(8,128)(2,1)S(1)}, bf16[400,128]{1,0:T(8,128)(2,1)S(1)}, u32[]{:S(2)}, u32[]{:S(2)}) collective-permute-start(bf16[400,128]{1,0:T(8,128)(2,1)S(1)} %shard_map.145.refs_0_), channel_id=1, source_target_pairs={{0,8},{4,12},{8,0},{12,4},{16,24},{20,28},{24,16},{28,20},{1,9},{5... | collective-permute-start | bytes 307208 | tf_op jit(solution)/shard_map/ppermute | solution.py:274
  7.3 4.7 %collective-permute-start = (bf16[400,128]{1,0:T(8,128)(2,1)S(1)}, bf16[400,128]{1,0:T(8,128)(2,1)S(1)}, u32[]{:S(2)}, u32[]{:S(2)}) collective-permute-start(bf16[400,128]{1,0:T(8,128)(2,1)S(1)} %shard_map.145.refs_0_), channel_id=1, source_target_pairs={{0,4},{4,0},{8,12},{12,8},{16,20},{20,16},{24,28},{28,24},{1,5},{5... | collective-permute-start | bytes 307208 | tf_op jit(solution)/shard_map/ppermute | solution.py:274
  9.8 1.7 %collective-permute-start.5 = (s32[5,1024]{1,0:T(8,128)S(1)}, s32[5,1024]{1,0:T(8,128)S(1)}, u32[]{:S(2)}, u32[]{:S(2)}) collective-permute-start(s32[5,1024]{1,0:T(8,128)S(1)} %pad_add_fusion), channel_id=1, source_target_pairs={{0,3},{1,0},{2,1},{3,2},{4,7},{5,4},{6,5},{7,6},{8,11},{9,8},{10,9... | collective-permute-start | bytes 61448 | tf_op jit(solution)/shard_map/ppermute | solution.py:314
  12.0 0.9 %copy-start.1 = (f32[128,400]{0,1:T(8,128)S(1)}, f32[128,400]{0,1:T(8,128)}, u32[]{:S(2)}) copy-start(f32[128,400]{0,1:T(8,128)} %param.10) | copy-start | bytes 614404
  12.9 6.0 %copy-start.4 = (f32[128,400]{0,1:T(8,128)S(1)}, f32[128,400]{0,1:T(8,128)}, u32[]{:S(2)}) copy-start(f32[128,400]{0,1:T(8,128)} %param.12) | copy-start | bytes 614404
  13.0 6.0 %copy-start.6 = (f32[128]{0:T(128)S(1)}, f32[128]{0:T(128)}, u32[]{:S(2)}) copy-start(f32[128]{0:T(128)} %param.13) | copy-start | bytes 1540
  13.0 6.5 %copy-start = (f32[256,400]{0,1:T(8,128)S(1)}, f32[256,400]{0,1:T(8,128)}, u32[]{:S(2)}) copy-start(f32[256,400]{0,1:T(8,128)} %param.14) | copy-start | bytes 1228804
  13.0 5.8 %collective-permute-start.6 = (bf16[400,128]{1,0:T(8,128)(2,1)S(1)}, bf16[400,128]{1,0:T(8,128)(2,1)S(1)}, u32[]{:S(2)}, u32[]{:S(2)}) collective-permute-start(bf16[400,128]{1,0:T(8,128)(2,1)S(1)} %shard_map.147.refs_0_), channel_id=1, source_target_pairs={{0,2},{1,3},{2,0},{3,1},{4,6},{5,7},{6,4},{7,5},{8,10},{9,11},{10,... | collective-permute-start | bytes 307208 | tf_op jit(solution)/shard_map/ppermute | solution.py:277
  15.4 8.5 %collective-permute-start.4 = (bf16[400,384]{1,0:T(8,128)(2,1)S(1)}, bf16[400,384]{1,0:T(8,128)(2,1)S(1)}, u32[]{:S(2)}, u32[]{:S(2)}) collective-permute-start(bf16[400,384]{1,0:T(8,128)(2,1)S(1)} %shard_map.146.refs_2_), channel_id=1, source_target_pairs={{0,4},{4,0},{8,12},{12,8},{16,20},{20,16},{24,28},{28,24},{1,5},{5... | collective-permute-start | bytes 921608 | tf_op jit(solution)/shard_map/ppermute | solution.py:274
  18.8 2.3 %collective-permute-start.7 = (bf16[400,256]{1,0:T(8,128)(2,1)S(1)}, bf16[400,256]{1,0:T(8,128)(2,1)S(1)}, u32[]{:S(2)}, u32[]{:S(2)}) collective-permute-start(bf16[400,256]{1,0:T(8,128)(2,1)S(1)} %pad_maximum_fusion), channel_id=1, source_target_pairs={{0,1},{1,0},{2,3},{3,2},{4,5},{5,4},{6,7},{7,6},{8,9},{9,8},{10,11... | collective-permute-start | bytes 614408 | tf_op jit(solution)/shard_map/ppermute | solution.py:277
  19.0 7.9 %collective-permute-start.8 = (f32[408,128]{1,0:T(8,128)S(1)}, f32[408,128]{1,0:T(8,128)S(1)}, u32[]{:S(2)}, u32[]{:S(2)}) collective-permute-start(f32[408,128]{1,0:T(8,128)S(1)} %shard_map.152), channel_id=1, source_target_pairs={{0,1},{1,2},{2,3},{3,0},{4,5},{5,6},{6,7},{7,4},{8,9},{9,10},{10,1... | collective-permute-start | bytes 626696 | tf_op jit(solution)/shard_map/ppermute | solution.py:284
  25.3 7.5 %collective-permute-start.13 = (bf16[400,256]{1,0:T(8,128)(2,1)S(1)}, bf16[400,256]{1,0:T(8,128)(2,1)S(1)}, u32[]{:S(2)}, u32[]{:S(2)}) collective-permute-start(bf16[400,256]{1,0:T(8,128)(2,1)S(1)} %get-tuple-element.53), channel_id=1, source_target_pairs={{0,4},{4,0},{8,12},{12,8},{16,20},{20,16},{24,28},{28,24},{1,5},{5... | collective-permute-start | bytes 614408 | tf_op jit(solution)/shard_map/ppermute | solution.py:274
  29.1 5.5 %collective-permute-start.10 = (bf16[208,128]{1,0:T(8,128)(2,1)S(1)}, bf16[208,128]{1,0:T(8,128)(2,1)S(1)}, u32[]{:S(2)}, u32[]{:S(2)}) collective-permute-start(bf16[208,128]{1,0:T(8,128)(2,1)S(1)} %get-tuple-element.46), channel_id=1, source_target_pairs={{0,2},{1,3},{2,0},{3,1},{4,6},{5,7},{6,4},{7,5},{8,10},{9,11},{10,... | collective-permute-start | bytes 159752 | tf_op jit(solution)/shard_map/ppermute | solution.py:277
  30.7 6.5 %collective-permute-start.11 = (bf16[208,128]{1,0:T(8,128)(2,1)S(1)}, bf16[208,128]{1,0:T(8,128)(2,1)S(1)}, u32[]{:S(2)}, u32[]{:S(2)}) collective-permute-start(bf16[208,128]{1,0:T(8,128)(2,1)S(1)} %get-tuple-element.47), channel_id=1, source_target_pairs={{0,3},{1,2},{2,1},{3,0},{4,7},{5,6},{6,5},{7,4},{8,11},{9,10},{10,... | collective-permute-start | bytes 159752 | tf_op jit(solution)/shard_map/ppermute | solution.py:277
  30.7 7.6 %collective-permute-start.16 = (bf16[400,256]{1,0:T(8,128)(2,1)S(1)}, bf16[400,256]{1,0:T(8,128)(2,1)S(1)}, u32[]{:S(2)}, u32[]{:S(2)}) collective-permute-start(bf16[400,256]{1,0:T(8,128)(2,1)S(1)} %get-tuple-element.56), channel_id=1, source_target_pairs={{0,4},{4,0},{8,12},{12,8},{16,20},{20,16},{24,28},{28,24},{1,5},{5... | collective-permute-start | bytes 614408 | tf_op jit(solution)/shard_map/ppermute | solution.py:274
  31.3 5.9 %collective-permute-start.9 = (bf16[1008,128]{1,0:T(8,128)(2,1)S(1)}, bf16[1008,128]{1,0:T(8,128)(2,1)S(1)}, u32[]{:S(2)}, u32[]{:S(2)}) collective-permute-start(bf16[1008,128]{1,0:T(8,128)(2,1)S(1)} %get-tuple-element.45), channel_id=1, source_target_pairs={{0,1},{1,0},{2,3},{3,2},{4,5},{5,4},{6,7},{7,6},{8,9},{9,8},{10,11... | collective-permute-start | bytes 774152 | tf_op jit(solution)/shard_map/ppermute | solution.py:277
  32.9 18.5 %collective-permute-start.14 = (bf16[400,128]{1,0:T(8,128)(2,1)S(1)}, bf16[400,128]{1,0:T(8,128)(2,1)S(1)}, u32[]{:S(2)}, u32[]{:S(2)}) collective-permute-start(bf16[400,128]{1,0:T(8,128)(2,1)S(1)} %get-tuple-element.54), channel_id=1, source_target_pairs={{0,17},{1,18},{2,19},{3,16},{4,21},{5,22},{6,23},{7,20},{8,25},{9,... | collective-permute-start | bytes 307208 | tf_op jit(solution)/shard_map/ppermute | solution.py:284
  34.6 17.7 %collective-permute-start.15 = (bf16[400,128]{1,0:T(8,128)(2,1)S(1)}, bf16[400,128]{1,0:T(8,128)(2,1)S(1)}, u32[]{:S(2)}, u32[]{:S(2)}) collective-permute-start(bf16[400,128]{1,0:T(8,128)(2,1)S(1)} %get-tuple-element.55), channel_id=1, source_target_pairs={{0,25},{1,26},{2,27},{3,24},{4,29},{5,30},{6,31},{7,28},{8,17},{9,... | collective-permute-start | bytes 307208 | tf_op jit(solution)/shard_map/ppermute | solution.py:284
  37.3 7.4 %collective-permute-start.19 = (bf16[208,128]{1,0:T(8,128)(2,1)S(1)}, bf16[208,128]{1,0:T(8,128)(2,1)S(1)}, u32[]{:S(2)}, u32[]{:S(2)}) collective-permute-start(bf16[208,128]{1,0:T(8,128)(2,1)S(1)} %get-tuple-element.61.piece_ref), channel_id=1, source_target_pairs={{0,8},{4,12},{8,0},{12,4},{16,24},{20,28},{24,16},{28,20},{1,9},{5... | collective-permute-start | bytes 159752 | tf_op jit(solution)/shard_map/ppermute | solution.py:274
  38.4 14.0 %collective-permute-start.17 = (bf16[400,128]{1,0:T(8,128)(2,1)S(1)}, bf16[400,128]{1,0:T(8,128)(2,1)S(1)}, u32[]{:S(2)}, u32[]{:S(2)}) collective-permute-start(bf16[400,128]{1,0:T(8,128)(2,1)S(1)} %get-tuple-element.57), channel_id=1, source_target_pairs={{0,1},{1,2},{2,3},{3,0},{4,5},{5,6},{6,7},{7,4},{8,9},{9,10},{10,1... | collective-permute-start | bytes 307208 | tf_op jit(solution)/shard_map/ppermute | solution.py:284
  38.4 13.9 %collective-permute-start.18 = (bf16[400,128]{1,0:T(8,128)(2,1)S(1)}, bf16[400,128]{1,0:T(8,128)(2,1)S(1)}, u32[]{:S(2)}, u32[]{:S(2)}) collective-permute-start(bf16[400,128]{1,0:T(8,128)(2,1)S(1)} %get-tuple-element.58), channel_id=1, source_target_pairs={{0,9},{1,10},{2,11},{3,8},{4,13},{5,14},{6,15},{7,12},{8,1},{9,2},... | collective-permute-start | bytes 307208 | tf_op jit(solution)/shard_map/ppermute | solution.py:284
  44.7 5.7 %collective-permute-start.20 = (bf16[208,128]{1,0:T(8,128)(2,1)S(1)}, bf16[208,128]{1,0:T(8,128)(2,1)S(1)}, u32[]{:S(2)}, u32[]{:S(2)}) collective-permute-start(bf16[208,128]{1,0:T(8,128)(2,1)S(1)} %shard_map.159.piece_ref), channel_id=1, source_target_pairs={{0,16},{4,20},{8,24},{12,28},{16,0},{20,4},{24,8},{28,12},{1,17},{... | collective-permute-start | bytes 159752 | tf_op jit(solution)/shard_map/ppermute | solution.py:274
  50.4 7.9 %collective-permute-start.12 = (bf16[400,128]{1,0:T(8,128)(2,1)S(1)}, bf16[400,128]{1,0:T(8,128)(2,1)S(1)}, u32[]{:S(2)}, u32[]{:S(2)}) collective-permute-start(bf16[400,128]{1,0:T(8,128)(2,1)S(1)} %get-tuple-element.49), channel_id=1, source_target_pairs={{0,2},{1,3},{2,0},{3,1},{4,6},{5,7},{6,4},{7,5},{8,10},{9,11},{10,... | collective-permute-start | bytes 307208 | tf_op jit(solution)/shard_map/ppermute | solution.py:277
  51.4 6.9 %copy-start.2 = (f32[128,400]{0,1:T(8,128)S(1)}, f32[128,400]{0,1:T(8,128)}, u32[]{:S(2)}) copy-start(f32[128,400]{0,1:T(8,128)} %param.10) | copy-start | bytes 614404
  51.5 6.8 %copy-start.7 = (f32[128]{0:T(128)S(1)}, f32[128]{0:T(128)}, u32[]{:S(2)}) copy-start(f32[128]{0:T(128)} %param.11) | copy-start | bytes 1540
  51.5 9.7 %copy-start.5 = (f32[256]{0:T(256)S(1)}, f32[256]{0:T(256)}, u32[]{:S(2)}) copy-start(f32[256]{0:T(256)} %param.15) | copy-start | bytes 3076
  51.5 4.2 %collective-permute-start.21 = (bf16[208,128]{1,0:T(8,128)(2,1)S(1)}, bf16[208,128]{1,0:T(8,128)(2,1)S(1)}, u32[]{:S(2)}, u32[]{:S(2)}) collective-permute-start(bf16[208,128]{1,0:T(8,128)(2,1)S(1)} %shard_map.160.refs_0_), channel_id=1, source_target_pairs={{0,4},{4,0},{8,12},{12,8},{16,20},{20,16},{24,28},{28,24},{1,5},{5... | collective-permute-start | bytes 159752 | tf_op jit(solution)/shard_map/ppermute | solution.py:274
  55.7 0.7 %copy-start.8 = (f32[1,128]{1,0:T(1,128)S(1)}, f32[1,128]{1,0:T(1,128)}, u32[]{:S(2)}) copy-start(f32[1,128]{1,0:T(1,128)} %get-tuple-element.60.refs_2_) | copy-start | bytes 1540
  56.4 3.8 %collective-permute-start.24 = (bf16[208,128]{1,0:T(8,128)(2,1)S(1)}, bf16[208,128]{1,0:T(8,128)(2,1)S(1)}, u32[]{:S(2)}, u32[]{:S(2)}) collective-permute-start(bf16[208,128]{1,0:T(8,128)(2,1)S(1)} %shard_map.161.refs_0_), channel_id=1, source_target_pairs={{0,3},{1,2},{2,1},{3,0},{4,7},{5,6},{6,5},{7,4},{8,11},{9,10},{10,... | collective-permute-start | bytes 159752 | tf_op jit(solution)/shard_map/ppermute | solution.py:277
  56.4 4.7 %collective-permute-start.23 = (bf16[208,128]{1,0:T(8,128)(2,1)S(1)}, bf16[208,128]{1,0:T(8,128)(2,1)S(1)}, u32[]{:S(2)}, u32[]{:S(2)}) collective-permute-start(bf16[208,128]{1,0:T(8,128)(2,1)S(1)} %shard_map.161.refs_0_), channel_id=1, source_target_pairs={{0,2},{1,3},{2,0},{3,1},{4,6},{5,7},{6,4},{7,5},{8,10},{9,11},{10,... | collective-permute-start | bytes 159752 | tf_op jit(solution)/shard_map/ppermute | solution.py:277
  57.5 3.7 %collective-permute-start.22 = (bf16[208,128]{1,0:T(8,128)(2,1)S(1)}, bf16[208,128]{1,0:T(8,128)(2,1)S(1)}, u32[]{:S(2)}, u32[]{:S(2)}) collective-permute-start(bf16[208,128]{1,0:T(8,128)(2,1)S(1)} %shard_map.161.refs_0_), channel_id=1, source_target_pairs={{0,1},{1,0},{2,3},{3,2},{4,5},{5,4},{6,7},{7,6},{8,9},{9,8},{10,11... | collective-permute-start | bytes 159752 | tf_op jit(solution)/shard_map/ppermute | solution.py:277

commit v8 on v7

v8 whole, which is shorter than its diff:
```python
import functools

import jax
import jax.numpy as jnp
from jax import lax
from jax.experimental import pallas as pl
from jax.experimental.pallas import tpu as pltpu
from jax.sharding import PartitionSpec as P

LEARN_RATE = 0.1
NEG_WEIGHT = 0.03125
BF = jnp.bfloat16
F32 = jnp.float32
VMEM_LIMIT = 32 * 1024 * 1024
LANES = 128
COST_JOIN = 6e9
COST_UPDATE = 12e9
COST_HIGH = 12e9
COST_LOW = 12e9
COST_SUM = 1e9


def dot(a, b, a_dim, b_dim):
    return lax.dot_general(a, b, (((a_dim,), (b_dim,)), ((), ())), preferred_element_type=F32)


def hot(ids, count):
    spot = lax.broadcasted_iota(jnp.int32, (count, ids.shape[1]), 0)
    return jnp.where(spot == ids, 1.0, 0.0).astype(BF)


def step_of(size, most=256):
    return most if size % most == 0 else size


def call(body, out_shape, scratch=(), here=None, after=(), flops=0, place=pltpu.VMEM):
    def run(*args):
        specs = [pl.BlockSpec(memory_space=place)] * len(args)
        if here is not None:
            specs.append(pl.BlockSpec(memory_space=pltpu.SMEM))
            args = (*args, here)
        inner = body
        if after:
            used = len(args)

            def inner(*refs):
                body(*refs[:used], *refs[used + len(after):])

            specs += [pl.BlockSpec(memory_space=pl.ANY)] * len(after)
            args = (*args, *after)
        return pl.pallas_call(
            inner,
            out_shape=out_shape,
            in_specs=specs,
            scratch_shapes=list(scratch),
            compiler_params=pltpu.CompilerParams(vmem_limit_bytes=VMEM_LIMIT),
            cost_estimate=pl.CostEstimate(flops=int(flops), bytes_accessed=0, transcendentals=0),
        )(*args)

    return run


def shape(*dims, dtype=F32):
    return jax.ShapeDtypeStruct(dims, dtype)


def cast_body(in_ref, out_ref, held_ref, sems):
    rows = held_ref.shape[0] // sems.shape[0]
    copies = []
    for k in range(sems.shape[0]):
        at = slice(k * rows, (k + 1) * rows)
        copies.append(pltpu.make_async_copy(in_ref.at[at], held_ref.at[at], sems.at[k]))
        copies[-1].start()
    for k, copy in enumerate(copies):
        at = slice(k * rows, (k + 1) * rows)
        copy.wait()
        out_ref[at, :] = held_ref[at, :].astype(BF)


def count_body(far_right, outer, rows, slots, ids_ref, relation_ref, place_ref, out_ref, relation_bf_ref, local_ref):
    def local(ids, here, half):
        block = (ids // rows) ^ here
        return (block % 2 * half + block // 2) * rows + ids % rows

    ids = ids_ref[...]
    local_ref[...] = ids
    local_ref[0:1, :] = local(ids[0:1], place_ref[0], far_right)
    local_ref[1:2, :] = local(ids[1:2], place_ref[1], outer)
    for g in range(out_ref.shape[0]):
        negative = local(ids[3 + g:4 + g, :slots], place_ref[1], outer)
        for at in range(0, out_ref.shape[1], LANES):
            spot = lax.broadcasted_iota(jnp.int32, (LANES, slots), 0) + at
            total = jnp.sum(jnp.where(spot == negative, NEG_WEIGHT, 0.0), axis=1, keepdims=True)
            out_ref[g, at:at + LANES, :] = jnp.broadcast_to(total, (LANES, LANES))
    relation_bf_ref[...] = relation_ref[...].astype(BF)


def pack_body(table_ref, state_ref, pack_ref):
    width = table_ref.shape[0]
    pack_ref[:width, :] = table_ref[...]
    pack_ref[width:, :] = jnp.broadcast_to(state_ref[...], (pack_ref.shape[0] - width, LANES))


def join_body(*refs):
    out_ref = refs[-1]
    at = 0
    for ref in refs[:-1]:
        out_ref[:, at:at + ref.shape[1]] = ref[...]
        at += ref.shape[1]


def query_body(blocks, *refs):
    near_refs, refs = refs[:blocks], refs[blocks:]
    sibling_ref, relation_ref, ids_ref, s_ref, o_ref, q_ref = refs
    relation = relation_ref[...]
    half = s_ref.shape[0] // 2
    edges = s_ref.shape[1]
    step = step_of(edges)
    near = jnp.concatenate([ref[...] for ref in near_refs], axis=1)
    half_rows = near.shape[1]
    for at in range(0, edges, step):
        cols = slice(at, at + step)
        pick = hot(ids_ref[0:1, cols], 2 * half_rows)
        s = dot(near, pick[:half_rows], 1, 0) + dot(sibling_ref[...], pick[half_rows:], 1, 0)
        o = dot(relation, hot(ids_ref[2:3, cols], relation.shape[1]), 1, 0)
        s_ref[:, cols] = s.astype(BF)
        o_ref[:, cols] = o.astype(BF)
        s_re, s_im, o_re, o_im = s[:half], s[half:], o[:half], o[half:]
        q = jnp.concatenate([s_re * o_re - s_im * o_im, s_re * o_im + s_im * o_re], axis=0)
        q_ref[:, cols] = q.astype(BF)


def grad_chunk(rows_t, q_ref, weight_ref, ids_ref, base, at, step):
    count = rows_t.shape[0]
    edges = q_ref.shape[1]
    cols = slice(at, at + step)
    scores = dot(rows_t, q_ref[:, cols], 1, 0)
    spot = lax.broadcasted_iota(jnp.int32, (count, step), 0) + base
    h = jnp.where(spot == ids_ref[1:2, cols], 1.0, 0.0)
    w = weight_ref[at // (edges // weight_ref.shape[0]), base:base + count, :]
    w = jnp.concatenate([w] * (step // LANES), axis=1)
    return ((w + h) * (0.5 * jnp.tanh(0.5 * scores) + 0.5) - h).astype(BF)


def complex_back(g, other):
    half = g.shape[0] // 2
    g_re, g_im, o_re, o_im = g[:half], g[half:], other[:half], other[half:]
    return jnp.concatenate([g_re * o_re + g_im * o_im, g_im * o_re - g_re * o_im], axis=0).astype(BF)


def near_body(blocks, *refs):
    block_refs, refs = refs[:blocks], refs[blocks:]
    q_ref, weight_ref, ids_ref, right_ref, qg_ref, rows_ref, m_ref = refs
    join_body(*block_refs, rows_ref)
    rows_t = rows_ref[...].T
    edges = q_ref.shape[1]
    step = step_of(edges // weight_ref.shape[0])
    for at in range(0, edges, step):
        m_ref[:, at:at + step] = grad_chunk(rows_t, q_ref, weight_ref, ids_ref, 0, at, step)
    right_ref[...] = dot(q_ref[...], m_ref[...], 1, 1)
    qg_ref[...] = dot(rows_ref[...], m_ref[...], 1, 0)


def far_body(blocks, pieces, *refs):
    block_refs, refs = refs[:blocks], refs[blocks:]
    q_ref, weight_ref, ids_ref, qg_ref, s_ref, here_ref = refs[:6]
    m_ref, g_ref, mine_ref, theirs_ref, rows_ref, kinds_ref, tall_ref = refs[6:]
    join_body(*block_refs, rows_ref)
    rows_t = rows_ref[...].T
    base = rows_t.shape[0]
    width, edges = qg_ref.shape
    step = step_of(edges // weight_ref.shape[0])
    for at in range(0, edges, step):
        cols = slice(at, at + step)
        m = grad_chunk(rows_t, q_ref, weight_ref, ids_ref, base, at, step)
        m_ref[:, cols] = m
        g = qg_ref[:, cols] + dot(rows_ref[...], m, 1, 0)
        g_ref[:, cols] = g
        by_kind = complex_back(g, s_ref[:, cols].astype(F32))
        kinds = dot(by_kind, hot(ids_ref[2:3, cols], kinds_ref.shape[1]), 1, 1)
        if at == 0:
            kinds_ref[...] = kinds
        else:
            kinds_ref[...] += kinds
    parts = kinds_ref.shape[1] // LANES
    for j in range(parts):
        tall_ref[j * width:(j + 1) * width, :] = kinds_ref[:, j * LANES:(j + 1) * LANES]
    rest = tall_ref.shape[0] - parts * width
    if rest:
        tall_ref[parts * width:, :] = jnp.zeros((rest, LANES), F32)
    here = here_ref[0]
    size = tall_ref.shape[0] // pieces
    for k in range(pieces):
        start = pl.multiple_of((here ^ k) * size, 16)
        piece = tall_ref[pl.ds(start, size), :]
        at = slice(k // 2 * size, (k // 2 + 1) * size)
        if k % 2:
            theirs_ref[at, :] = piece.astype(BF)
        else:
            mine_ref[at, :] = piece


def rest_body(q_ref, m_ref, g_ref, o_ref, ids_ref, hi_ref, lo_ref, near_ref, far_ref, left_ref):
    far = dot(q_ref[...], m_ref[...], 1, 1).astype(BF)
    half = far.shape[1] // 2
    hi_ref[...] = far[:, half:]
    lo_ref[...] = far[:, :half]
    edges = q_ref.shape[1]
    step = step_of(edges)
    for at in range(0, edges, step):
        cols = slice(at, at + step)
        by_source = complex_back(g_ref[:, cols], o_ref[:, cols].astype(F32))
        left = dot(by_source, hot(ids_ref[0:1, cols], left_ref.shape[1]), 1, 1)
        if at == 0:
            left_ref[...] = left
        else:
            left_ref[...] += left
    cut = left_ref.shape[1] // 2
    near_ref[...] = left_ref[:, :cut]
    far_ref[...] = left_ref[:, cut:].astype(BF)


def relation_body(pieces, *refs):
    piece_refs, refs = refs[:pieces // 2], refs[pieces // 2:]
    sibling_ref, table_ref, state_ref, here_ref, new_ref, state_new_ref, tall_ref = refs
    here = here_ref[0]
    size = tall_ref.shape[0] // pieces
    for k in range(pieces):
        start = pl.multiple_of((here ^ k) * size, 16)
        piece = sibling_ref[k // 2 * size:(k // 2 + 1) * size, :] if k % 2 else piece_refs[k // 2][...]
        tall_ref[pl.ds(start, size), :] = piece.astype(F32)
    width, count = table_ref.shape
    for j in range(count // LANES):
        cols = slice(j * LANES, (j + 1) * LANES)
        g = tall_ref[j * width:(j + 1) * width, :]
        state = state_ref[:, cols] + jnp.sum(g * g, axis=0, keepdims=True) * (1.0 / width)
        state_new_ref[:, cols] = state
        new_ref[:, cols] = table_ref[:, cols] - g * (LEARN_RATE * lax.rsqrt(state))


def piece_body(mine_ref, got_ref, own_ref, *other_refs):
    size = own_ref.shape[0]
    for k, ref in enumerate((own_ref, *other_refs)):
        at = slice(k * size, (k + 1) * size)
        ref[...] = (mine_ref[at, :] + got_ref[at, :].astype(F32)).astype(ref.dtype)


def left_body(near_ref, got_ref, own_ref, *other_refs):
    for k, ref in enumerate((own_ref, *other_refs)):
        at = slice(k * LANES, (k + 1) * LANES)
        ref[...] = (near_ref[:, at] + got_ref[:, at].astype(F32)).astype(ref.dtype)


def stack_body(*refs):
    size = refs[0].shape[0]
    for k, ref in enumerate(refs[:-1]):
        refs[-1][k * size:(k + 1) * size, :] = ref[...]


def chunk_body(base, near_ref, got_ref, *block_refs):
    for k, ref in enumerate(block_refs):
        cols = slice(k * LANES, (k + 1) * LANES)
        total = near_ref[:, base + k * LANES:base + (k + 1) * LANES] + got_ref[:, cols].astype(F32)
        ref[...] = total.astype(BF)


def sum_body(*refs):
    total = refs[0][...].astype(F32)
    for ref in refs[1:-1]:
        total = total + ref[...].astype(F32)
    refs[-1][...] = total.astype(BF)


def update_body(parts, *refs):
    part_refs, (table_ref, state_ref, new_ref, state_new_ref) = refs[:parts], refs[parts:]
    g = part_refs[0][...].astype(F32)
    for ref in part_refs[1:]:
        g = g + ref[...].astype(F32)
    width = g.shape[0]
    state = state_ref[state_ref.shape[0] - 1:, :] + jnp.sum(g * g, axis=0, keepdims=True) * (1.0 / width)
    state_new_ref[...] = state
    new_ref[...] = table_ref[:width, :] - g * (LEARN_RATE * lax.rsqrt(state))


def build(mesh):
    n_left, n_right = mesh.shape["left"], mesh.shape["right"]
    for count in (n_left, n_right):
        assert count & (count - 1) == 0 and count > 3
    outer = n_left // 2
    far_right = n_right // 2

    def swap_left(value, by):
        return lax.ppermute(value, "left", [(i, i ^ by) for i in range(n_left)])

    def swap_right(value, by):
        return lax.ppermute(value, "right", [(i, i ^ by) for i in range(n_right)])

    def next_column(value, by):
        perm = []
        for i in range(n_left):
            for r in range(n_right):
                perm.append((i * n_right + r, (i ^ by) * n_right + (r + 1) % n_right))
        return lax.ppermute(value, ("left", "right"), perm)

    def per_device(
        left_table, left_state, right_table, right_state, relation_table, relation_state,
        source_ids, target_ids, relation_ids, negative_ids,
    ):
        rows = left_table.shape[0]
        width = left_table.shape[1]
        left_t, right_t, relation_t = left_table.T, right_table.T, relation_table.T
        nrel = relation_t.shape[1]
        here_l, here_r = lax.axis_index("left"), lax.axis_index("right")
        me = here_r.astype(jnp.int32).reshape(1)
        edges = source_ids.shape[-1]
        groups = negative_ids.shape[2]
        n_rows = n_left * rows
        half = outer * rows
        one_block = shape(width, rows, dtype=BF)
        table_bf = shape(width, edges, dtype=BF)

        def cast(value, after=()):
            parts = 5 if width % 80 == 0 else 1
            scratch = [pltpu.VMEM(value.shape, F32), pltpu.SemaphoreType.DMA((parts,))]
            return call(cast_body, one_block, scratch, after=after, place=pl.ANY)(value)

        right_bf = cast(right_t)
        near = [right_bf] + [swap_left(right_bf, 2 * k) for k in range(1, outer)]
        other_own = swap_left(right_bf, 1)
        blocks = shape(width, half - rows, dtype=BF)
        joined = call(join_body, blocks, flops=COST_JOIN)(*near[1:])
        other_rest = swap_left(joined, 1)

        ids = [source_ids, target_ids, relation_ids, negative_ids]
        longest = max(i.shape[-1] for i in ids)
        ids = [i.reshape(-1, i.shape[-1]) for i in ids]
        ids = jnp.concatenate([jnp.pad(i, ((0, 0), (0, longest - i.shape[-1]))) for i in ids], axis=0)
        ids = lax.ppermute(ids, "right", [(i, (i - 1) % n_right) for i in range(n_right)])
        left_bf = cast(left_t, after=(other_own, ids))
        half_left = [left_bf] + [swap_right(left_bf, 2 * k) for k in range(1, far_right)]
        sibling_left = swap_right(jnp.concatenate(half_left, axis=1), 1)
        place = jnp.stack([here_r, here_l]).astype(jnp.int32)
        weight, relation_bf, ids = call(
            functools.partial(count_body, far_right, outer, rows, negative_ids.shape[-1]),
            (shape(groups, n_rows, LANES), shape(width, nrel, dtype=BF), shape(*ids.shape, dtype=jnp.int32)),
            here=place,
        )(ids, relation_t)
        moved = next_column(call(pack_body, shape(width + 8, rows), after=(joined,))(right_t, right_state[None, :]), 0)

        s, o, q = call(functools.partial(query_body, far_right), (table_bf, table_bf, table_bf))(
            *half_left, sibling_left, relation_bf, ids
        )
        part = pltpu.VMEM((width, half), BF)
        right_near, qg_near = call(
            functools.partial(near_body, outer),
            (shape(width, half), shape(width, edges)),
            [part, pltpu.VMEM((half, edges), BF)],
        )(*near, q, weight, ids)
        chunk = shape(width, half // 2, dtype=BF)
        tall = nrel // LANES * width
        size = -(-tall // (n_right * 16)) * 16
        piece = shape(size, LANES, dtype=BF)
        all_pieces = pltpu.VMEM((size * n_right, LANES), F32)
        m, g, mine, theirs = call(
            functools.partial(far_body, 2, n_right),
            (shape(half, edges, dtype=BF), shape(width, edges), shape(far_right * size, LANES),
             shape(far_right * size, LANES, dtype=BF)),
            [part, pltpu.VMEM((width, nrel), F32), all_pieces],
            me,
            after=(moved,),
        )(other_own, other_rest, q, weight, ids, qg_near, s)
        left_rows = n_right * rows
        left_half = left_rows // 2
        far_hi, far_lo, left_near, left_far = call(
            rest_body,
            (chunk, chunk, shape(width, left_half), shape(width, left_half, dtype=BF)),
            [pltpu.VMEM((width, left_rows), F32)],
        )(q, m, g, o, ids)

        mine, *rest = call(
            piece_body, (shape(size, LANES),) + (piece,) * (far_right - 1), flops=COST_SUM
        )(mine, swap_right(theirs, 1))
        got = [swap_right(p, 2 * (k + 1)) for k, p in enumerate(rest)]
        mine = call(sum_body, piece, flops=COST_SUM)(mine, *got)
        bit = 2
        while bit < n_left:
            mine = call(sum_body, piece, flops=COST_SUM)(mine, swap_left(mine, bit))
            bit *= 2
        mine = call(sum_body, piece, flops=COST_SUM)(mine, swap_left(mine, 1))
        pieces = [mine] + [swap_right(mine, 2 * k) for k in range(1, far_right)]
        sibling = swap_right(call(stack_body, shape(far_right * size, LANES, dtype=BF))(*pieces), 1)

        left_own, *blocks = call(left_body, (shape(width, rows),) + (one_block,) * (far_right - 1))(
            left_near, swap_right(left_far, 1)
        )
        left_got = [swap_right(block, 2 * (k + 1)) for k, block in enumerate(blocks)]

        some = outer // 2
        got_hi = swap_left(far_hi, 1)
        got_lo = swap_left(far_lo, 1)
        outs = (one_block,) * some
        high = call(functools.partial(chunk_body, half // 2), outs, flops=COST_HIGH)(right_near, got_hi)
        low = call(functools.partial(chunk_body, 0), outs, flops=COST_LOW, after=left_got)(right_near, got_lo)
        right_got = [next_column(block, 2 * (some + k)) for k, block in enumerate(high)]
        right_got += [next_column(block, 2 * k) for k, block in enumerate(low)]

        def update(got, table, state, flops=0):
            outs = (shape(width, rows), shape(1, rows))
            return call(functools.partial(update_body, len(got)), outs, flops=flops)(*got, table, state)

        left_new, left_state_new = update([left_own, *left_got], left_t, left_state[None, :])
        right_new, right_state_new = update(right_got, moved, moved, COST_UPDATE)
        relation_new, relation_state_new = call(
            functools.partial(relation_body, n_right), (shape(width, nrel), shape(1, nrel)), [all_pieces], me
        )(*pieces, sibling, relation_t, relation_state[None, :])
        return (
            left_new.T, left_state_new.reshape(-1), right_new.T, right_state_new.reshape(-1),
            relation_new.T, relation_state_new.reshape(-1),
        )

    return per_device


def solution(mesh):
    rows = P(("left", "right"), None)
    vector = P(("left", "right"))
    ids = P("left", "right", None)
    return jax.shard_map(
        build(mesh),
        mesh=mesh,
        in_specs=(rows, vector, rows, vector, P(), P(), ids, ids, ids, P("left", "right", None, None)),
        out_specs=(rows, vector, rows, vector, P(), P()),
        check_vma=False,
    )
```

time: 62.3 us -> 56.9 us (0.913)
  waiting for transfers between devices: 20.4 us -> 10.9 us
  starting transfers between devices: 26.6 us -> 30.5 us
  local copies, waits for them, and re-layouts: 2.55 us -> 1.89 us
    ppermute x10, waiting for transfers between devices: 14.9 us -> 2.05 us  [swap_left(): return lax.ppermute(value, 'left', [(i, i ^ by) for i in range(n_left)])]
    ppermute x9 -> x8, waiting for transfers between devices: 3.89 us -> 7.28 us  [swap_right(): return lax.ppermute(value, 'right', [(i, i ^ by) for i in range(n_right)])]
    ppermute x5, starting transfers between devices: 6.38 us -> 9.62 us  [next_column(): return lax.ppermute(value, ('left', 'right'), perm)]
    ppermute x10, starting transfers between devices: 13.4 us -> 15.3 us  [swap_left(): return lax.ppermute(value, 'left', [(i, i ^ by) for i in range(n_left)])]
    ppermute x9 -> x8, starting transfers between devices: 6.73 us -> 5.54 us  [swap_right(): return lax.ppermute(value, 'right', [(i, i ^ by) for i in range(n_right)])]
    unnamed x18 -> x16, local copies, waits for them, and re-layouts: 2.55 us -> 1.89 us
    pallas_call x18 -> x21, Pallas kernels: 10.8 us -> 11.1 us  [run(): pl.pallas_call(inner, out_shape=out_shape, in_specs=specs, scratch_shapes...]
  transfers between devices with their start and end apart: 25 -> 24, of which waited for: 11 -> 9; matrix products, arithmetic and copies ran while one was open for 1% -> 2% of each run, Pallas kernels for 16% -> 13%
where the time goes in v8:
time: 56.9 us; the launch traced here: 56.2 us
  starting transfers between devices  30.5 us (54%)
  Pallas kernels  11.1 us (20%)
  waiting for transfers between devices  10.9 us (19%)
  local copies, waits for them, and re-layouts  1.89 us (3%)
  between operations  0.9 us (2%)
  other arithmetic  0.86 us (2%)
    ppermute x10, starting transfers between devices, swap_left(): return lax.ppermute(value, 'left', [(i, i ^ by) for i in range(n_left)])  15.3 us
    pallas_call x21, Pallas kernels, run(): pl.pallas_call(inner, out_shape=out_shape, in_specs=specs, scratch_shapes...  11.1 us
    ppermute x5, starting transfers between devices, next_column(): return lax.ppermute(value, ('left', 'right'), perm)  9.62 us
    ppermute x8, waiting for transfers between devices, swap_right(): return lax.ppermute(value, 'right', [(i, i ^ by) for i in range(n_right)])  7.28 us
    ppermute x8, starting transfers between devices, swap_right(): return lax.ppermute(value, 'right', [(i, i ^ by) for i in range(n_right)])  5.54 us
    ppermute x10, waiting for transfers between devices, swap_left(): return lax.ppermute(value, 'left', [(i, i ^ by) for i in range(n_left)])  2.05 us
    unnamed x16, local copies, waits for them, and re-layouts  1.89 us
    ppermute x1, waiting for transfers between devices, per_device(): lax.ppermute(ids, 'right', [(i, (i - 1) % n_right) for i in range(n_right)])  1.59 us
  transfers between devices with their start and end apart: 24, of which 9 were waited for; matrix products, arithmetic and copies ran while one was open for 2% of the time, Pallas kernels for 13%

profile of v8, /device:TPU:0, one launch (start us, length us, event | category | flops | bytes accessed | tf_op | source)
XLA Modules:
  0.0 56.2 jit_solution(4382266987542641)
XLA Ops:
  0.6 0.9 %copy-done.3 = f32[128,400]{0,1:T(8,128)S(1)} copy-done((f32[128,400]{0,1:T(8,128)S(1)}, f32[128,400]{0,1:T(8,128)}, u32[]{:S(2)}) %copy-start.3) | copy-done | bytes 204824
  1.6 0.3 shard_map.145.refs_0_
  1.9 5.1 %collective-permute-start.6 = (bf16[400,128]{1,0:T(8,128)(2,1)S(1)}, bf16[400,128]{1,0:T(8,128)(2,1)S(1)}, u32[]{:S(2)}, u32[]{:S(2)}) collective-permute-start(bf16[400,128]{1,0:T(8,128)(2,1)S(1)} %shard_map.145.refs_0_), channel_id=1, source_target_pairs={{0,24},{4,28},{8,16},{12,20},{16,8},{20,12},{24,0},{28,4},{1,25},{... | collective-permute-start | bytes 307208 | tf_op jit(solution)/shard_map/ppermute | solution.py:293
  7.0 0.6 %collective-permute-start.4 = (bf16[400,128]{1,0:T(8,128)(2,1)S(1)}, bf16[400,128]{1,0:T(8,128)(2,1)S(1)}, u32[]{:S(2)}, u32[]{:S(2)}) collective-permute-start(bf16[400,128]{1,0:T(8,128)(2,1)S(1)} %shard_map.145.refs_0_), channel_id=1, source_target_pairs={{0,8},{4,12},{8,0},{12,4},{16,24},{20,28},{24,16},{28,20},{1,9},{5... | collective-permute-start | bytes 307208 | tf_op jit(solution)/shard_map/ppermute | solution.py:293
  7.6 1.7 %collective-permute-start = (bf16[400,128]{1,0:T(8,128)(2,1)S(1)}, bf16[400,128]{1,0:T(8,128)(2,1)S(1)}, u32[]{:S(2)}, u32[]{:S(2)}) collective-permute-start(bf16[400,128]{1,0:T(8,128)(2,1)S(1)} %shard_map.145.refs_0_), channel_id=1, source_target_pairs={{0,4},{4,0},{8,12},{12,8},{16,20},{20,16},{24,28},{28,24},{1,5},{5... | collective-permute-start | bytes 307208 | tf_op jit(solution)/shard_map/ppermute | solution.py:293
  9.3 0.8 %pad_add_fusion = s32[5,1024]{1,0:T(8,128)S(1)} fusion(s32[2,1024]{1,0:T(2,128)} %bitcast.27, s32[1,1024]{1,0:T(1,128)} %bitcast.28, s32[1,1024]{1,0:T(1,128)} %bitcast.29, s32[1,1024]{1,0:T(1,128)} %bitcast.30), kind=kLoop, calls=%fused_computation.1 | loop fusion | flops 15360 | bytes 40960 | tf_op jit(solution)/shard_map/concatenate | solution.py:337
  10.1 0.1 collective-permute-start.1
  10.1 1.6 %collective-permute-done.1.refs_2_.ids_ref = s32[5,1024]{1,0:T(8,128)S(1)} collective-permute-done((s32[5,1024]{1,0:T(8,128)S(1)}, s32[5,1024]{1,0:T(8,128)S(1)}, u32[]{:S(2)}, u32[]{:S(2)}) %collective-permute-start.1) | collective-permute-done | bytes 20512 | tf_op jit(solution)/shard_map/ppermute | solution.py:338
  11.7 0.6 %collective-permute-done.refs_1_.refs_0_ = bf16[400,128]{1,0:T(8,128)(2,1)S(1)} collective-permute-done((bf16[400,128]{1,0:T(8,128)(2,1)S(1)}, bf16[400,128]{1,0:T(8,128)(2,1)S(1)}, u32[]{:S(2)}, u32[]{:S(2)}) %collective-permute-start) | collective-permute-done | bytes 102432 | tf_op jit(solution)/shard_map/ppermute | solution.py:293
  12.3 0.9 %copy-done.1 = f32[128,400]{0,1:T(8,128)S(1)} copy-done((f32[128,400]{0,1:T(8,128)S(1)}, f32[128,400]{0,1:T(8,128)}, u32[]{:S(2)}) %copy-start.1) | copy-done | bytes 204824
  13.2 0.3 shard_map.146.refs_0_
  13.6 1.7 %collective-permute-start.2 = (bf16[400,128]{1,0:T(8,128)(2,1)S(1)}, bf16[400,128]{1,0:T(8,128)(2,1)S(1)}, u32[]{:S(2)}, u32[]{:S(2)}) collective-permute-start(bf16[400,128]{1,0:T(8,128)(2,1)S(1)} %shard_map.146.refs_0_), channel_id=1, source_target_pairs={{0,2},{1,3},{2,0},{3,1},{4,6},{5,7},{6,4},{7,5},{8,10},{9,11},{10,... | collective-permute-start | bytes 307208 | tf_op jit(solution)/shard_map/ppermute | solution.py:296
  15.3 0.3 collective-permute-done.5.refs_1_.refs_2_
  15.7 1.6 %collective-permute-start.7 = (bf16[400,384]{1,0:T(8,128)(2,1)S(1)}, bf16[400,384]{1,0:T(8,128)(2,1)S(1)}, u32[]{:S(2)}, u32[]{:S(2)}) collective-permute-start(bf16[400,384]{1,0:T(8,128)(2,1)S(1)} %shard_map.149.refs_2_), channel_id=1, source_target_pairs={{0,4},{4,0},{8,12},{12,8},{16,20},{20,16},{24,28},{28,24},{1,5},{5... | collective-permute-start | bytes 921608 | tf_op jit(solution)/shard_map/ppermute | solution.py:293
  17.3 0.1 collective-permute-start.8
  17.3 2.0 %collective-permute-done.2.refs_1_ = bf16[400,128]{1,0:T(8,128)(2,1)S(1)} collective-permute-done((bf16[400,128]{1,0:T(8,128)(2,1)S(1)}, bf16[400,128]{1,0:T(8,128)(2,1)S(1)}, u32[]{:S(2)}, u32[]{:S(2)}) %collective-permute-start.2) | collective-permute-done | bytes 102432 | tf_op jit(solution)/shard_map/ppermute | solution.py:296
  19.4 0.2 collective-permute-start.3
  19.6 0.1 pad_add_fusion.1.place_ref
  19.7 1.6 %shard_map.147 = (f32[2,1024,128]{2,1,0:T(8,128)S(1)}, bf16[400,256]{1,0:T(8,128)(2,1)S(1)}, s32[5,1024]{1,0:T(8,128)S(1)}) custom-call(s32[5,1024]{1,0:T(8,128)S(1)} %collective-permute-done.1.refs_2_.ids_ref, f32[400,256]{1,0:T(8,128)S(1)} %bitcast.18, s32[2]{0:T(128)S(1)} %pad_add_fusion.1.place_ref), custom_call_target="tpu_custom_call" | custom-call | tf_op jit(solution)/shard_map/pallas_call | solution.py:51
  21.2 0.9 %shard_map.148 = (bf16[400,1024]{1,0:T(8,128)(2,1)S(1)}, bf16[400,1024]{1,0:T(8,128)(2,1)S(1)}, bf16[400,1024]{1,0:T(8,128)(2,1)S(1)}) custom-call(bf16[400,128]{1,0:T(8,128)(2,1)S(1)} %shard_map.146.refs_0_, bf16[400,128]{1,0:T(8,128)(2,1)S(1)} %collective-permute-done.2.refs_1_, bf16[400,256]{1,0:T(8,128)(2,1)S(1)} %collective-permute-done.3.refs_2_, ...), custom_call_target="tpu_custom_call" | custom-call | tf_op jit(solution)/shard_map/pallas_call | solution.py:51
  22.1 1.8 %shard_map.150 = (f32[400,512]{1,0:T(8,128)S(1)}, f32[400,1024]{1,0:T(8,128)S(1)}) custom-call(bf16[400,128]{1,0:T(8,128)(2,1)S(1)} %shard_map.145.refs_0_, bf16[400,128]{1,0:T(8,128)(2,1)S(1)} %collective-permute-done.4.refs_0_.refs_1_, bf16[400,128]{1,0:T(8,128)(2,1)S(1)} %collective-permute-done.5.refs_1_.refs_2_, ...), custom_call_target="tpu_custom_call" | custom-call | tf_op jit(solution)/shard_map/pallas_call | solution.py:51
  24.0 0.4 collective-permute-done.7.refs_1_
  24.4 2.3 %shard_map.152 = (bf16[512,1024]{1,0:T(8,128)(2,1)S(1)}, f32[400,1024]{1,0:T(8,128)S(1)}, f32[416,128]{1,0:T(8,128)S(1)}, bf16[416,128]{1,0:T(8,128)(2,1)S(1)}) custom-call(bf16[400,128]{1,0:T(8,128)(2,1)S(1)} %collective-permute-done.refs_1_.refs_0_, bf16[400,384]{1,0:T(8,128)(2,1)S(1)} %collective-permute-done.7.refs_1_, ...), custom_call_target="tpu_custom_call" | custom-call | tf_op jit(solution)/shard_map/pallas_call | solution.py:51
  26.7 0.1 collective-permute-start.17
  26.8 1.1 %shard_map.153 = (bf16[400,256]{1,0:T(8,128)(2,1)S(1)}, bf16[400,256]{1,0:T(8,128)(2,1)S(1)}, f32[400,256]{1,0:T(8,128)S(1)}, bf16[400,256]{1,0:T(8,128)(2,1)S(1)}) custom-call(bf16[400,1024]{1,0:T(8,128)(2,1)S(1)} %get-tuple-element.38.refs_4_.refs_2_.q_ref, bf16[512,1024]{1,0:T(8,128)(2,1)S(1)} %get-tuple-element.42.m_ref, ...), custom_call_target="tpu_custom_call" | custom-call | tf_op jit(solution)/shard_map/pallas_call | solution.py:51
  27.9 0.6 collective-permute-start.9
  28.5 1.4 %collective-permute-start.18 = (bf16[208,128]{1,0:T(8,128)(2,1)S(1)}, bf16[208,128]{1,0:T(8,128)(2,1)S(1)}, u32[]{:S(2)}, u32[]{:S(2)}) collective-permute-start(bf16[208,128]{1,0:T(8,128)(2,1)S(1)} %get-tuple-element.63), channel_id=1, source_target_pairs={{0,2},{1,3},{2,0},{3,1},{4,6},{5,7},{6,4},{7,5},{8,10},{9,11},{10,... | collective-permute-start | bytes 159752 | tf_op jit(solution)/shard_map/ppermute | solution.py:296
  29.9 1.3 %collective-permute-start.11 = (bf16[400,256]{1,0:T(8,128)(2,1)S(1)}, bf16[400,256]{1,0:T(8,128)(2,1)S(1)}, u32[]{:S(2)}, u32[]{:S(2)}) collective-permute-start(bf16[400,256]{1,0:T(8,128)(2,1)S(1)} %get-tuple-element.52), channel_id=1, source_target_pairs={{0,4},{4,0},{8,12},{12,8},{16,20},{20,16},{24,28},{28,24},{1,5},{5... | collective-permute-start | bytes 614408 | tf_op jit(solution)/shard_map/ppermute | solution.py:293
  31.2 1.5 %collective-permute-done.18.refs_1_ = bf16[208,128]{1,0:T(8,128)(2,1)S(1)} collective-permute-done((bf16[208,128]{1,0:T(8,128)(2,1)S(1)}, bf16[208,128]{1,0:T(8,128)(2,1)S(1)}, u32[]{:S(2)}, u32[]{:S(2)}) %collective-permute-start.18) | collective-permute-done | bytes 53280 | tf_op jit(solution)/shard_map/ppermute | solution.py:296
  32.7 1.5 %collective-permute-start.19 = (bf16[208,128]{1,0:T(8,128)(2,1)S(1)}, bf16[208,128]{1,0:T(8,128)(2,1)S(1)}, u32[]{:S(2)}, u32[]{:S(2)}) collective-permute-start(bf16[208,128]{1,0:T(8,128)(2,1)S(1)} %shard_map.160.refs_0_), channel_id=1, source_target_pairs={{0,8},{4,12},{8,0},{12,4},{16,24},{20,28},{24,16},{28,20},{1,9},{5... | collective-permute-start | bytes 159752 | tf_op jit(solution)/shard_map/ppermute | solution.py:293
  34.2 0.5 collective-permute-start.14
  34.8 1.5 %collective-permute-start.10 = (bf16[400,128]{1,0:T(8,128)(2,1)S(1)}, bf16[400,128]{1,0:T(8,128)(2,1)S(1)}, u32[]{:S(2)}, u32[]{:S(2)}) collective-permute-start(bf16[400,128]{1,0:T(8,128)(2,1)S(1)} %get-tuple-element.48), channel_id=1, source_target_pairs={{0,2},{1,3},{2,0},{3,1},{4,6},{5,7},{6,4},{7,5},{8,10},{9,11},{10,... | collective-permute-start | bytes 307208 | tf_op jit(solution)/shard_map/ppermute | solution.py:296
  36.2 0.7 %collective-permute-done.19.refs_1_ = bf16[208,128]{1,0:T(8,128)(2,1)S(1)} collective-permute-done((bf16[208,128]{1,0:T(8,128)(2,1)S(1)}, bf16[208,128]{1,0:T(8,128)(2,1)S(1)}, u32[]{:S(2)}, u32[]{:S(2)}) %collective-permute-start.19) | collective-permute-done | bytes 53280 | tf_op jit(solution)/shard_map/ppermute | solution.py:293
  36.9 2.4 %collective-permute-start.20 = (bf16[208,128]{1,0:T(8,128)(2,1)S(1)}, bf16[208,128]{1,0:T(8,128)(2,1)S(1)}, u32[]{:S(2)}, u32[]{:S(2)}) collective-permute-start(bf16[208,128]{1,0:T(8,128)(2,1)S(1)} %shard_map.161.refs_0_), channel_id=1, source_target_pairs={{0,16},{4,20},{8,24},{12,28},{16,0},{20,4},{24,8},{28,12},{1,17},{... | collective-permute-start | bytes 159752 | tf_op jit(solution)/shard_map/ppermute | solution.py:293
  39.3 0.1 shard_map.156
  39.4 0.1 collective-permute-start.12
  39.5 4.9 %collective-permute-start.13 = (bf16[400,128]{1,0:T(8,128)(2,1)S(1)}, bf16[400,128]{1,0:T(8,128)(2,1)S(1)}, u32[]{:S(2)}, u32[]{:S(2)}) collective-permute-start(bf16[400,128]{1,0:T(8,128)(2,1)S(1)} %get-tuple-element.54), channel_id=1, source_target_pairs={{0,25},{1,26},{2,27},{3,24},{4,29},{5,30},{6,31},{7,28},{8,17},{9,... | collective-permute-start | bytes 307208 | tf_op jit(solution)/shard_map/ppermute | solution.py:303
  44.4 0.5 collective-permute-start.21
  45.0 0.1 shard_map.157
  45.0 0.1 collective-permute-start.15
  45.1 4.5 %collective-permute-start.16 = (bf16[400,128]{1,0:T(8,128)(2,1)S(1)}, bf16[400,128]{1,0:T(8,128)(2,1)S(1)}, u32[]{:S(2)}, u32[]{:S(2)}) collective-permute-start(bf16[400,128]{1,0:T(8,128)(2,1)S(1)} %get-tuple-element.57), channel_id=1, source_target_pairs={{0,9},{1,10},{2,11},{3,8},{4,13},{5,14},{6,15},{7,12},{8,1},{9,2},... | collective-permute-start | bytes 307208 | tf_op jit(solution)/shard_map/ppermute | solution.py:303
  49.7 0.1 collective-permute-start.22
  49.8 0.8 %shard_map.155 = (f32[400,128]{1,0:T(8,128)}, f32[1,128]{1,0:T(1,128)}) custom-call(f32[400,128]{1,0:T(8,128)S(1)} %get-tuple-element.47.refs_0_, bf16[400,128]{1,0:T(8,128)(2,1)S(1)} %collective-permute-done.10.refs_1_.refs_2_, f32[400,128]{1,0:T(8,128)S(1)} %bitcast.21, f32[1,128]{1,0:T(1,128)S(1)} %bitcast.26), custom_call_target="tpu_custom_call" | custom-call | tf_op jit(solution)/shard_map/pallas_call | solution.py:51
  50.5 3.3 %collective-permute-done.22.refs_1_ = bf16[208,128]{1,0:T(8,128)(2,1)S(1)} collective-permute-done((bf16[208,128]{1,0:T(8,128)(2,1)S(1)}, bf16[208,128]{1,0:T(8,128)(2,1)S(1)}, u32[]{:S(2)}, u32[]{:S(2)}) %collective-permute-start.22) | collective-permute-done | bytes 53280 | tf_op jit(solution)/shard_map/ppermute | solution.py:296
  53.9 0.1 collective-permute-start.23
  54.0 0.8 %shard_map.158 = (f32[400,128]{1,0:T(8,128)}, f32[1,128]{1,0:T(1,128)}) custom-call(bf16[400,128]{1,0:T(8,128)(2,1)S(1)} %collective-permute-done.12.refs_0_, bf16[400,128]{1,0:T(8,128)(2,1)S(1)} %collective-permute-done.13.refs_1_, bf16[400,128]{1,0:T(8,128)(2,1)S(1)} %collective-permute-done.15.refs_2_, ...), custom_call_target="tpu_custom_call" | custom-call | flops 12000000000 | tf_op jit(solution)/shard_map/pallas_call | solution.py:51
  54.8 0.5 collective-permute-done.23.refs_2_
  55.3 0.9 %shard_map.165 = (f32[400,256]{1,0:T(8,128)}, f32[1,256]{1,0:T(1,128)}) custom-call(bf16[208,128]{1,0:T(8,128)(2,1)S(1)} %shard_map.163.refs_0_, bf16[208,128]{1,0:T(8,128)(2,1)S(1)} %collective-permute-done.22.refs_1_, bf16[416,128]{1,0:T(8,128)(2,1)S(1)} %collective-permute-done.23.refs_2_, f32[400,256]{1,0:T(8,128)S(1)} %bitcast.19, ...), custom_call_target="tpu_custom_call" | custom-call | tf_op jit(solution)/shard_map/pallas_call | solution.py:51
  (40 shorter events, 0.3 us)
Async XLA Ops:
  0.6 0.9 %copy-start.3 = (f32[128,400]{0,1:T(8,128)S(1)}, f32[128,400]{0,1:T(8,128)}, u32[]{:S(2)}) copy-start(f32[128,400]{0,1:T(8,128)} %param.12) | copy-start | bytes 614404
  1.9 13.4 %collective-permute-start.6 = (bf16[400,128]{1,0:T(8,128)(2,1)S(1)}, bf16[400,128]{1,0:T(8,128)(2,1)S(1)}, u32[]{:S(2)}, u32[]{:S(2)}) collective-permute-start(bf16[400,128]{1,0:T(8,128)(2,1)S(1)} %shard_map.145.refs_0_), channel_id=1, source_target_pairs={{0,24},{4,28},{8,16},{12,20},{16,8},{20,12},{24,0},{28,4},{1,25},{... | collective-permute-start | bytes 307208 | tf_op jit(solution)/shard_map/ppermute | solution.py:293
  7.0 8.6 %collective-permute-start.5 = (bf16[400,128]{1,0:T(8,128)(2,1)S(1)}, bf16[400,128]{1,0:T(8,128)(2,1)S(1)}, u32[]{:S(2)}, u32[]{:S(2)}) collective-permute-start(bf16[400,128]{1,0:T(8,128)(2,1)S(1)} %shard_map.145.refs_0_), channel_id=1, source_target_pairs={{0,16},{4,20},{8,24},{12,28},{16,0},{20,4},{24,8},{28,12},{1,17},{... | collective-permute-start | bytes 307208 | tf_op jit(solution)/shard_map/ppermute | solution.py:293
  7.0 8.6 %collective-permute-start.4 = (bf16[400,128]{1,0:T(8,128)(2,1)S(1)}, bf16[400,128]{1,0:T(8,128)(2,1)S(1)}, u32[]{:S(2)}, u32[]{:S(2)}) collective-permute-start(bf16[400,128]{1,0:T(8,128)(2,1)S(1)} %shard_map.145.refs_0_), channel_id=1, source_target_pairs={{0,8},{4,12},{8,0},{12,4},{16,24},{20,28},{24,16},{28,20},{1,9},{5... | collective-permute-start | bytes 307208 | tf_op jit(solution)/shard_map/ppermute | solution.py:293
  7.6 4.7 %collective-permute-start = (bf16[400,128]{1,0:T(8,128)(2,1)S(1)}, bf16[400,128]{1,0:T(8,128)(2,1)S(1)}, u32[]{:S(2)}, u32[]{:S(2)}) collective-permute-start(bf16[400,128]{1,0:T(8,128)(2,1)S(1)} %shard_map.145.refs_0_), channel_id=1, source_target_pairs={{0,4},{4,0},{8,12},{12,8},{16,20},{20,16},{24,28},{28,24},{1,5},{5... | collective-permute-start | bytes 307208 | tf_op jit(solution)/shard_map/ppermute | solution.py:293
  10.1 1.7 %collective-permute-start.1 = (s32[5,1024]{1,0:T(8,128)S(1)}, s32[5,1024]{1,0:T(8,128)S(1)}, u32[]{:S(2)}, u32[]{:S(2)}) collective-permute-start(s32[5,1024]{1,0:T(8,128)S(1)} %pad_add_fusion), channel_id=1, source_target_pairs={{0,3},{1,0},{2,1},{3,2},{4,7},{5,4},{6,5},{7,6},{8,11},{9,8},{10,9... | collective-permute-start | bytes 61448 | tf_op jit(solution)/shard_map/ppermute | solution.py:338
  12.3 0.9 %copy-start.1 = (f32[128,400]{0,1:T(8,128)S(1)}, f32[128,400]{0,1:T(8,128)}, u32[]{:S(2)}) copy-start(f32[128,400]{0,1:T(8,128)} %param.10) | copy-start | bytes 614404
  13.5 3.7 %copy-start.4 = (f32[128,400]{0,1:T(8,128)S(1)}, f32[128,400]{0,1:T(8,128)}, u32[]{:S(2)}) copy-start(f32[128,400]{0,1:T(8,128)} %param.12) | copy-start | bytes 614404
  13.5 3.7 %copy-start.6 = (f32[128]{0:T(128)S(1)}, f32[128]{0:T(128)}, u32[]{:S(2)}) copy-start(f32[128]{0:T(128)} %param.13) | copy-start | bytes 1540
  13.6 6.1 %copy-start = (f32[256,400]{0,1:T(8,128)S(1)}, f32[256,400]{0,1:T(8,128)}, u32[]{:S(2)}) copy-start(f32[256,400]{0,1:T(8,128)} %param.14) | copy-start | bytes 1228804
  13.6 5.8 %collective-permute-start.2 = (bf16[400,128]{1,0:T(8,128)(2,1)S(1)}, bf16[400,128]{1,0:T(8,128)(2,1)S(1)}, u32[]{:S(2)}, u32[]{:S(2)}) collective-permute-start(bf16[400,128]{1,0:T(8,128)(2,1)S(1)} %shard_map.146.refs_0_), channel_id=1, source_target_pairs={{0,2},{1,3},{2,0},{3,1},{4,6},{5,7},{6,4},{7,5},{8,10},{9,11},{10,... | collective-permute-start | bytes 307208 | tf_op jit(solution)/shard_map/ppermute | solution.py:296
  15.7 8.8 %collective-permute-start.7 = (bf16[400,384]{1,0:T(8,128)(2,1)S(1)}, bf16[400,384]{1,0:T(8,128)(2,1)S(1)}, u32[]{:S(2)}, u32[]{:S(2)}) collective-permute-start(bf16[400,384]{1,0:T(8,128)(2,1)S(1)} %shard_map.149.refs_2_), channel_id=1, source_target_pairs={{0,4},{4,0},{8,12},{12,8},{16,20},{20,16},{24,28},{28,24},{1,5},{5... | collective-permute-start | bytes 921608 | tf_op jit(solution)/shard_map/ppermute | solution.py:293
  17.3 6.7 %collective-permute-start.8 = (f32[408,128]{1,0:T(8,128)S(1)}, f32[408,128]{1,0:T(8,128)S(1)}, u32[]{:S(2)}, u32[]{:S(2)}) collective-permute-start(f32[408,128]{1,0:T(8,128)S(1)} %shard_map.151), channel_id=1, source_target_pairs={{0,1},{1,2},{2,3},{3,0},{4,5},{5,6},{6,7},{7,4},{8,9},{9,10},{10,1... | collective-permute-start | bytes 626696 | tf_op jit(solution)/shard_map/ppermute | solution.py:303
  19.4 1.9 %collective-permute-start.3 = (bf16[400,256]{1,0:T(8,128)(2,1)S(1)}, bf16[400,256]{1,0:T(8,128)(2,1)S(1)}, u32[]{:S(2)}, u32[]{:S(2)}) collective-permute-start(bf16[400,256]{1,0:T(8,128)(2,1)S(1)} %pad_maximum_fusion), channel_id=1, source_target_pairs={{0,1},{1,0},{2,3},{3,2},{4,5},{5,4},{6,7},{7,6},{8,9},{9,8},{10,11... | collective-permute-start | bytes 614408 | tf_op jit(solution)/shard_map/ppermute | solution.py:296
  26.7 1.7 %collective-permute-start.17 = (bf16[416,128]{1,0:T(8,128)(2,1)S(1)}, bf16[416,128]{1,0:T(8,128)(2,1)S(1)}, u32[]{:S(2)}, u32[]{:S(2)}) collective-permute-start(bf16[416,128]{1,0:T(8,128)(2,1)S(1)} %get-tuple-element.61), channel_id=1, source_target_pairs={{0,1},{1,0},{2,3},{3,2},{4,5},{5,4},{6,7},{7,6},{8,9},{9,8},{10,11... | collective-permute-start | bytes 319496 | tf_op jit(solution)/shard_map/ppermute | solution.py:296
  27.9 6.8 %collective-permute-start.9 = (bf16[400,256]{1,0:T(8,128)(2,1)S(1)}, bf16[400,256]{1,0:T(8,128)(2,1)S(1)}, u32[]{:S(2)}, u32[]{:S(2)}) collective-permute-start(bf16[400,256]{1,0:T(8,128)(2,1)S(1)} %get-tuple-element.46), channel_id=1, source_target_pairs={{0,1},{1,0},{2,3},{3,2},{4,5},{5,4},{6,7},{7,6},{8,9},{9,8},{10,11... | collective-permute-start | bytes 614408 | tf_op jit(solution)/shard_map/ppermute | solution.py:296
  28.5 4.2 %collective-permute-start.18 = (bf16[208,128]{1,0:T(8,128)(2,1)S(1)}, bf16[208,128]{1,0:T(8,128)(2,1)S(1)}, u32[]{:S(2)}, u32[]{:S(2)}) collective-permute-start(bf16[208,128]{1,0:T(8,128)(2,1)S(1)} %get-tuple-element.63), channel_id=1, source_target_pairs={{0,2},{1,3},{2,0},{3,1},{4,6},{5,7},{6,4},{7,5},{8,10},{9,11},{10,... | collective-permute-start | bytes 159752 | tf_op jit(solution)/shard_map/ppermute | solution.py:296
  29.9 9.5 %collective-permute-start.11 = (bf16[400,256]{1,0:T(8,128)(2,1)S(1)}, bf16[400,256]{1,0:T(8,128)(2,1)S(1)}, u32[]{:S(2)}, u32[]{:S(2)}) collective-permute-start(bf16[400,256]{1,0:T(8,128)(2,1)S(1)} %get-tuple-element.52), channel_id=1, source_target_pairs={{0,4},{4,0},{8,12},{12,8},{16,20},{20,16},{24,28},{28,24},{1,5},{5... | collective-permute-start | bytes 614408 | tf_op jit(solution)/shard_map/ppermute | solution.py:293
  32.7 4.2 %collective-permute-start.19 = (bf16[208,128]{1,0:T(8,128)(2,1)S(1)}, bf16[208,128]{1,0:T(8,128)(2,1)S(1)}, u32[]{:S(2)}, u32[]{:S(2)}) collective-permute-start(bf16[208,128]{1,0:T(8,128)(2,1)S(1)} %shard_map.160.refs_0_), channel_id=1, source_target_pairs={{0,8},{4,12},{8,0},{12,4},{16,24},{20,28},{24,16},{28,20},{1,9},{5... | collective-permute-start | bytes 159752 | tf_op jit(solution)/shard_map/ppermute | solution.py:293
  34.2 10.8 %collective-permute-start.14 = (bf16[400,256]{1,0:T(8,128)(2,1)S(1)}, bf16[400,256]{1,0:T(8,128)(2,1)S(1)}, u32[]{:S(2)}, u32[]{:S(2)}) collective-permute-start(bf16[400,256]{1,0:T(8,128)(2,1)S(1)} %get-tuple-element.55), channel_id=1, source_target_pairs={{0,4},{4,0},{8,12},{12,8},{16,20},{20,16},{24,28},{28,24},{1,5},{5... | collective-permute-start | bytes 614408 | tf_op jit(solution)/shard_map/ppermute | solution.py:293
  34.8 10.2 %collective-permute-start.10 = (bf16[400,128]{1,0:T(8,128)(2,1)S(1)}, bf16[400,128]{1,0:T(8,128)(2,1)S(1)}, u32[]{:S(2)}, u32[]{:S(2)}) collective-permute-start(bf16[400,128]{1,0:T(8,128)(2,1)S(1)} %get-tuple-element.48), channel_id=1, source_target_pairs={{0,2},{1,3},{2,0},{3,1},{4,6},{5,7},{6,4},{7,5},{8,10},{9,11},{10,... | collective-permute-start | bytes 307208 | tf_op jit(solution)/shard_map/ppermute | solution.py:296
  36.9 7.5 %collective-permute-start.20 = (bf16[208,128]{1,0:T(8,128)(2,1)S(1)}, bf16[208,128]{1,0:T(8,128)(2,1)S(1)}, u32[]{:S(2)}, u32[]{:S(2)}) collective-permute-start(bf16[208,128]{1,0:T(8,128)(2,1)S(1)} %shard_map.161.refs_0_), channel_id=1, source_target_pairs={{0,16},{4,20},{8,24},{12,28},{16,0},{20,4},{24,8},{28,12},{1,17},{... | collective-permute-start | bytes 159752 | tf_op jit(solution)/shard_map/ppermute | solution.py:293
  39.4 14.6 %collective-permute-start.12 = (bf16[400,128]{1,0:T(8,128)(2,1)S(1)}, bf16[400,128]{1,0:T(8,128)(2,1)S(1)}, u32[]{:S(2)}, u32[]{:S(2)}) collective-permute-start(bf16[400,128]{1,0:T(8,128)(2,1)S(1)} %get-tuple-element.53), channel_id=1, source_target_pairs={{0,17},{1,18},{2,19},{3,16},{4,21},{5,22},{6,23},{7,20},{8,25},{9,... | collective-permute-start | bytes 307208 | tf_op jit(solution)/shard_map/ppermute | solution.py:303
  39.5 14.5 %collective-permute-start.13 = (bf16[400,128]{1,0:T(8,128)(2,1)S(1)}, bf16[400,128]{1,0:T(8,128)(2,1)S(1)}, u32[]{:S(2)}, u32[]{:S(2)}) collective-permute-start(bf16[400,128]{1,0:T(8,128)(2,1)S(1)} %get-tuple-element.54), channel_id=1, source_target_pairs={{0,25},{1,26},{2,27},{3,24},{4,29},{5,30},{6,31},{7,28},{8,17},{9,... | collective-permute-start | bytes 307208 | tf_op jit(solution)/shard_map/ppermute | solution.py:303
  44.4 5.2 %collective-permute-start.21 = (bf16[208,128]{1,0:T(8,128)(2,1)S(1)}, bf16[208,128]{1,0:T(8,128)(2,1)S(1)}, u32[]{:S(2)}, u32[]{:S(2)}) collective-permute-start(bf16[208,128]{1,0:T(8,128)(2,1)S(1)} %shard_map.162.refs_0_), channel_id=1, source_target_pairs={{0,4},{4,0},{8,12},{12,8},{16,20},{20,16},{24,28},{28,24},{1,5},{5... | collective-permute-start | bytes 159752 | tf_op jit(solution)/shard_map/ppermute | solution.py:293
  45.0 9.0 %collective-permute-start.15 = (bf16[400,128]{1,0:T(8,128)(2,1)S(1)}, bf16[400,128]{1,0:T(8,128)(2,1)S(1)}, u32[]{:S(2)}, u32[]{:S(2)}) collective-permute-start(bf16[400,128]{1,0:T(8,128)(2,1)S(1)} %get-tuple-element.56), channel_id=1, source_target_pairs={{0,1},{1,2},{2,3},{3,0},{4,5},{5,6},{6,7},{7,4},{8,9},{9,10},{10,1... | collective-permute-start | bytes 307208 | tf_op jit(solution)/shard_map/ppermute | solution.py:303
  45.1 4.6 %copy-start.2 = (f32[128,400]{0,1:T(8,128)S(1)}, f32[128,400]{0,1:T(8,128)}, u32[]{:S(2)}) copy-start(f32[128,400]{0,1:T(8,128)} %param.10) | copy-start | bytes 614404
  45.1 4.6 %copy-start.7 = (f32[128]{0:T(128)S(1)}, f32[128]{0:T(128)}, u32[]{:S(2)}) copy-start(f32[128]{0:T(128)} %param.11) | copy-start | bytes 1540
  45.1 8.9 %collective-permute-start.16 = (bf16[400,128]{1,0:T(8,128)(2,1)S(1)}, bf16[400,128]{1,0:T(8,128)(2,1)S(1)}, u32[]{:S(2)}, u32[]{:S(2)}) collective-permute-start(bf16[400,128]{1,0:T(8,128)(2,1)S(1)} %get-tuple-element.57), channel_id=1, source_target_pairs={{0,9},{1,10},{2,11},{3,8},{4,13},{5,14},{6,15},{7,12},{8,1},{9,2},... | collective-permute-start | bytes 307208 | tf_op jit(solution)/shard_map/ppermute | solution.py:303
  49.7 4.2 %collective-permute-start.22 = (bf16[208,128]{1,0:T(8,128)(2,1)S(1)}, bf16[208,128]{1,0:T(8,128)(2,1)S(1)}, u32[]{:S(2)}, u32[]{:S(2)}) collective-permute-start(bf16[208,128]{1,0:T(8,128)(2,1)S(1)} %shard_map.163.refs_0_), channel_id=1, source_target_pairs={{0,2},{1,3},{2,0},{3,1},{4,6},{5,7},{6,4},{7,5},{8,10},{9,11},{10,... | collective-permute-start | bytes 159752 | tf_op jit(solution)/shard_map/ppermute | solution.py:296
  53.9 1.4 %copy-start.5 = (f32[256]{0:T(256)S(1)}, f32[256]{0:T(256)}, u32[]{:S(2)}) copy-start(f32[256]{0:T(256)} %param.15) | copy-start | bytes 3076
  53.9 1.4 %collective-permute-start.23 = (bf16[416,128]{1,0:T(8,128)(2,1)S(1)}, bf16[416,128]{1,0:T(8,128)(2,1)S(1)}, u32[]{:S(2)}, u32[]{:S(2)}) collective-permute-start(bf16[416,128]{1,0:T(8,128)(2,1)S(1)} %shard_map.164), channel_id=1, source_target_pairs={{0,1},{1,0},{2,3},{3,2},{4,5},{5,4},{6,7},{7,6},{8,9},{9,8},{10,11... | collective-permute-start | bytes 319496 | tf_op jit(solution)/shard_map/ppermute | solution.py:296

commit v9 on v8

--- a/solution.py
+++ b/solution.py
@@ -13,11 +13,13 @@
 F32 = jnp.float32
 VMEM_LIMIT = 32 * 1024 * 1024
 LANES = 128
-COST_JOIN = 6e9
-COST_UPDATE = 12e9
+COST_JOIN_LOW = 6e9
+COST_JOIN_HIGH = 6e9
+COST_ADD = 6e9
 COST_HIGH = 12e9
-COST_LOW = 12e9
+COST_LOW = 6e9
 COST_SUM = 1e9
+COST_MIDDLE = 6e9
 
 
 def dot(a, b, a_dim, b_dim):
@@ -148,26 +150,33 @@
     return jnp.concatenate([g_re * o_re + g_im * o_im, g_im * o_re - g_re * o_im], axis=0).astype(BF)
 
 
+def products(rows_ref, q_ref, weight_ref, ids_ref, m_ref, base):
+    rows_t = rows_ref[...].T
+    step = step_of(q_ref.shape[1] // weight_ref.shape[0])
+    for at in range(0, q_ref.shape[1], step):
+        m_ref[:, at:at + step] = grad_chunk(rows_t, q_ref, weight_ref, ids_ref, base, at, step)
+
+
 def near_body(blocks, *refs):
     block_refs, refs = refs[:blocks], refs[blocks:]
     q_ref, weight_ref, ids_ref, right_ref, qg_ref, rows_ref, m_ref = refs
     join_body(*block_refs, rows_ref)
-    rows_t = rows_ref[...].T
-    edges = q_ref.shape[1]
-    step = step_of(edges // weight_ref.shape[0])
-    for at in range(0, edges, step):
-        m_ref[:, at:at + step] = grad_chunk(rows_t, q_ref, weight_ref, ids_ref, 0, at, step)
+    products(rows_ref, q_ref, weight_ref, ids_ref, m_ref, 0)
     right_ref[...] = dot(q_ref[...], m_ref[...], 1, 1)
     qg_ref[...] = dot(rows_ref[...], m_ref[...], 1, 0)
 
 
-def far_body(blocks, pieces, *refs):
-    block_refs, refs = refs[:blocks], refs[blocks:]
-    q_ref, weight_ref, ids_ref, qg_ref, s_ref, here_ref = refs[:6]
-    m_ref, g_ref, mine_ref, theirs_ref, rows_ref, kinds_ref, tall_ref = refs[6:]
-    join_body(*block_refs, rows_ref)
+def middle_body(base, rows_ref, q_ref, weight_ref, ids_ref, qg_ref, right_ref, qg_out_ref, m_ref):
+    products(rows_ref, q_ref, weight_ref, ids_ref, m_ref, base)
+    right_ref[...] = dot(q_ref[...], m_ref[...], 1, 1).astype(BF)
+    qg_out_ref[...] = qg_ref[...] + dot(rows_ref[...], m_ref[...], 1, 0)
+
+
+def far_body(
+    base, pieces, rows_ref, q_ref, weight_ref, ids_ref, qg_ref, s_ref, here_ref,
+    m_ref, g_ref, mine_ref, theirs_ref, kinds_ref, tall_ref,
+):
     rows_t = rows_ref[...].T
-    base = rows_t.shape[0]
     width, edges = qg_ref.shape
     step = step_of(edges // weight_ref.shape[0])
     for at in range(0, edges, step):
@@ -200,11 +209,8 @@
             mine_ref[at, :] = piece
 
 
-def rest_body(q_ref, m_ref, g_ref, o_ref, ids_ref, hi_ref, lo_ref, near_ref, far_ref, left_ref):
-    far = dot(q_ref[...], m_ref[...], 1, 1).astype(BF)
-    half = far.shape[1] // 2
-    hi_ref[...] = far[:, half:]
-    lo_ref[...] = far[:, :half]
+def rest_body(q_ref, m_ref, g_ref, o_ref, ids_ref, right_ref, near_ref, far_ref, left_ref):
+    right_ref[...] = dot(q_ref[...], m_ref[...], 1, 1).astype(BF)
     edges = q_ref.shape[1]
     step = step_of(edges)
     for at in range(0, edges, step):
@@ -271,6 +277,13 @@
     refs[-1][...] = total.astype(BF)
 
 
+def add_body(*refs):
+    total = refs[0][...].astype(F32)
+    for ref in refs[1:-1]:
+        total = total + ref[...].astype(F32)
+    refs[-1][...] = total
+
+
 def update_body(parts, *refs):
     part_refs, (table_ref, state_ref, new_ref, state_new_ref) = refs[:parts], refs[parts:]
     g = part_refs[0][...].astype(F32)
@@ -326,19 +339,23 @@
 
         right_bf = cast(right_t)
         near = [right_bf] + [swap_left(right_bf, 2 * k) for k in range(1, outer)]
-        other_own = swap_left(right_bf, 1)
-        blocks = shape(width, half - rows, dtype=BF)
-        joined = call(join_body, blocks, flops=COST_JOIN)(*near[1:])
-        other_rest = swap_left(joined, 1)
+        some = outer // 2
+        cut = some * rows
+        chunk = shape(width, cut, dtype=BF)
+        joined = call(join_body, chunk, flops=COST_JOIN_LOW)(*near[:some])
+        other_low = swap_left(joined, 1)
+        joined = call(join_body, chunk, flops=COST_JOIN_HIGH, after=(joined,))(*near[some:])
+        other_high = swap_left(joined, 1)
 
         ids = [source_ids, target_ids, relation_ids, negative_ids]
         longest = max(i.shape[-1] for i in ids)
         ids = [i.reshape(-1, i.shape[-1]) for i in ids]
         ids = jnp.concatenate([jnp.pad(i, ((0, 0), (0, longest - i.shape[-1]))) for i in ids], axis=0)
         ids = lax.ppermute(ids, "right", [(i, (i - 1) % n_right) for i in range(n_right)])
-        left_bf = cast(left_t, after=(other_own, ids))
+        left_bf = cast(left_t)
         half_left = [left_bf] + [swap_right(left_bf, 2 * k) for k in range(1, far_right)]
-        sibling_left = swap_right(jnp.concatenate(half_left, axis=1), 1)
+        half_joined = call(join_body, shape(width, far_right * rows, dtype=BF), after=(ids,))(*half_left)
+        sibling_left = swap_right(half_joined, 1)
         place = jnp.stack([here_r, here_l]).astype(jnp.int32)
         weight, relation_bf, ids = call(
             functools.partial(count_body, far_right, outer, rows, negative_ids.shape[-1]),
@@ -350,66 +367,70 @@
         s, o, q = call(functools.partial(query_body, far_right), (table_bf, table_bf, table_bf))(
             *half_left, sibling_left, relation_bf, ids
         )
-        part = pltpu.VMEM((width, half), BF)
-        right_near, qg_near = call(
+        right_near, qg = call(
             functools.partial(near_body, outer),
             (shape(width, half), shape(width, edges)),
-            [part, pltpu.VMEM((half, edges), BF)],
+            [pltpu.VMEM((width, half), BF), pltpu.VMEM((half, edges), BF)],
         )(*near, q, weight, ids)
-        chunk = shape(width, half // 2, dtype=BF)
+        right_low, qg = call(
+            functools.partial(middle_body, half), (chunk, shape(width, edges)), [pltpu.VMEM((cut, edges), BF)],
+            flops=COST_MIDDLE,
+        )(other_low, q, weight, ids, qg)
+        got_low = swap_left(right_low, 1)
         tall = nrel // LANES * width
         size = -(-tall // (n_right * 16)) * 16
         piece = shape(size, LANES, dtype=BF)
         all_pieces = pltpu.VMEM((size * n_right, LANES), F32)
         m, g, mine, theirs = call(
-            functools.partial(far_body, 2, n_right),
-            (shape(half, edges, dtype=BF), shape(width, edges), shape(far_right * size, LANES),
+            functools.partial(far_body, half + cut, n_right),
+            (shape(cut, edges, dtype=BF), shape(width, edges), shape(far_right * size, LANES),
              shape(far_right * size, LANES, dtype=BF)),
-            [part, pltpu.VMEM((width, nrel), F32), all_pieces],
+            [pltpu.VMEM((width, nrel), F32), all_pieces],
             me,
             after=(moved,),
-        )(other_own, other_rest, q, weight, ids, qg_near, s)
+        )(other_high, q, weight, ids, qg, s)
         left_rows = n_right * rows
         left_half = left_rows // 2
-        far_hi, far_lo, left_near, left_far = call(
+        right_high, left_near, left_far = call(
             rest_body,
-            (chunk, chunk, shape(width, left_half), shape(width, left_half, dtype=BF)),
+            (chunk, shape(width, left_half), shape(width, left_half, dtype=BF)),
             [pltpu.VMEM((width, left_rows), F32)],
         )(q, m, g, o, ids)
 
+        got_high = swap_left(right_high, 1)
+        outs = (one_block,) * some
+        low = call(functools.partial(chunk_body, 0), outs, flops=COST_LOW)(right_near, got_low)
+        low = [next_column(block, 2 * k) for k, block in enumerate(low)]
+        low = call(add_body, shape(width, rows), flops=COST_ADD)(*low)
+        high = call(functools.partial(chunk_body, cut), outs, flops=COST_HIGH)(right_near, got_high)
+        high = [next_column(block, 2 * (some + k)) for k, block in enumerate(high)]
+        high = call(add_body, shape(width, rows), flops=COST_ADD)(*high)
+
+        left_own, *blocks = call(left_body, (shape(width, rows),) + (one_block,) * (far_right - 1))(
+            left_near, swap_right(left_far, 1)
+        )
+        left_got = [swap_right(block, 2 * (k + 1)) for k, block in enumerate(blocks)]
+
         mine, *rest = call(
-            piece_body, (shape(size, LANES),) + (piece,) * (far_right - 1), flops=COST_SUM
+            piece_body, (shape(size, LANES),) + (piece,) * (far_right - 1), flops=COST_SUM, after=(got_low, right_high)
         )(mine, swap_right(theirs, 1))
         got = [swap_right(p, 2 * (k + 1)) for k, p in enumerate(rest)]
         mine = call(sum_body, piece, flops=COST_SUM)(mine, *got)
         bit = 2
         while bit < n_left:
-            mine = call(sum_body, piece, flops=COST_SUM)(mine, swap_left(mine, bit))
+            after = (low, left_own, got_high) if bit == 2 else ()
+            mine = call(sum_body, piece, flops=COST_SUM, after=after)(mine, swap_left(mine, bit))
             bit *= 2
-        mine = call(sum_body, piece, flops=COST_SUM)(mine, swap_left(mine, 1))
+        mine = call(sum_body, piece, flops=COST_SUM, after=(high, *left_got))(mine, swap_left(mine, 1))
         pieces = [mine] + [swap_right(mine, 2 * k) for k in range(1, far_right)]
         sibling = swap_right(call(stack_body, shape(far_right * size, LANES, dtype=BF))(*pieces), 1)
-
-        left_own, *blocks = call(left_body, (shape(width, rows),) + (one_block,) * (far_right - 1))(
-            left_near, swap_right(left_far, 1)
-        )
-        left_got = [swap_right(block, 2 * (k + 1)) for k, block in enumerate(blocks)]
-
-        some = outer // 2
-        got_hi = swap_left(far_hi, 1)
-        got_lo = swap_left(far_lo, 1)
-        outs = (one_block,) * some
-        high = call(functools.partial(chunk_body, half // 2), outs, flops=COST_HIGH)(right_near, got_hi)
-        low = call(functools.partial(chunk_body, 0), outs, flops=COST_LOW, after=left_got)(right_near, got_lo)
-        right_got = [next_column(block, 2 * (some + k)) for k, block in enumerate(high)]
-        right_got += [next_column(block, 2 * k) for k, block in enumerate(low)]
 
         def update(got, table, state, flops=0):
             outs = (shape(width, rows), shape(1, rows))
             return call(functools.partial(update_body, len(got)), outs, flops=flops)(*got, table, state)
 
         left_new, left_state_new = update([left_own, *left_got], left_t, left_state[None, :])
-        right_new, right_state_new = update(right_got, moved, moved, COST_UPDATE)
+        right_new, right_state_new = update([low, high], moved, moved)
         relation_new, relation_state_new = call(
             functools.partial(relation_body, n_right), (shape(width, nrel), shape(1, nrel)), [all_pieces], me
         )(*pieces, sibling, relation_t, relation_state[None, :])

time: 56.9 us -> 63 us (1.11)
  waiting for transfers between devices: 10.9 us -> 16.6 us
  local copies, waits for them, and re-layouts: 1.89 us -> 2.89 us
  starting transfers between devices: 30.5 us -> 29.8 us
    ppermute x5, waiting for transfers between devices: 0.01 us -> 6.18 us  [next_column(): return lax.ppermute(value, ('left', 'right'), perm)]
    ppermute x10, waiting for transfers between devices: 2.05 us -> 7.13 us  [swap_left(): return lax.ppermute(value, 'left', [(i, i ^ by) for i in range(n_left)])]
    ppermute x8, waiting for transfers between devices: 7.28 us -> 3.28 us  [swap_right(): return lax.ppermute(value, 'right', [(i, i ^ by) for i in range(n_right)])]
    ppermute x5, starting transfers between devices: 9.62 us -> 6.55 us  [next_column(): return lax.ppermute(value, ('left', 'right'), perm)]
    ppermute x1, waiting for transfers between devices: 1.59 us -> 0.01 us  [per_device(): lax.ppermute(ids, 'right', [(i, (i - 1) % n_right) for i in range(n_right)])]
    ppermute x8, starting transfers between devices: 5.54 us -> 6.84 us  [swap_right(): return lax.ppermute(value, 'right', [(i, i ^ by) for i in range(n_right)])]
    unnamed x16 -> x18, local copies, waits for them, and re-layouts: 1.89 us -> 2.89 us
    ppermute x10, starting transfers between devices: 15.3 us -> 16 us  [swap_left(): return lax.ppermute(value, 'left', [(i, i ^ by) for i in range(n_left)])]
  transfers between devices with their start and end apart: 24 -> 24, of which waited for: 9 -> 8; matrix products, arithmetic and copies ran while one was open for 2% -> 1% of each run, Pallas kernels for 13% -> 17%
where the time goes in v9:
time: 63 us; the launch traced here: 62.7 us
  starting transfers between devices  29.8 us (47%)
  waiting for transfers between devices  16.6 us (26%)
  Pallas kernels  11.6 us (18%)
  local copies, waits for them, and re-layouts  2.89 us (5%)
  between operations  0.92 us (1%)
  other arithmetic  0.83 us (1%)
    ppermute x10, starting transfers between devices, swap_left(): return lax.ppermute(value, 'left', [(i, i ^ by) for i in range(n_left)])  16 us
    pallas_call x26, Pallas kernels, run(): pl.pallas_call(inner, out_shape=out_shape, in_specs=specs, scratch_shapes...  11.6 us
    ppermute x10, waiting for transfers between devices, swap_left(): return lax.ppermute(value, 'left', [(i, i ^ by) for i in range(n_left)])  7.13 us
    ppermute x8, starting transfers between devices, swap_right(): return lax.ppermute(value, 'right', [(i, i ^ by) for i in range(n_right)])  6.84 us
    ppermute x5, starting transfers between devices, next_column(): return lax.ppermute(value, ('left', 'right'), perm)  6.55 us
    ppermute x5, waiting for transfers between devices, next_column(): return lax.ppermute(value, ('left', 'right'), perm)  6.18 us
    ppermute x8, waiting for transfers between devices, swap_right(): return lax.ppermute(value, 'right', [(i, i ^ by) for i in range(n_right)])  3.28 us
    unnamed x18, local copies, waits for them, and re-layouts  2.89 us
  transfers between devices with their start and end apart: 24, of which 8 were waited for; matrix products, arithmetic and copies ran while one was open for 1% of the time, Pallas kernels for 17%

profile of v9, /device:TPU:0, one launch (start us, length us, event | category | flops | bytes accessed | tf_op | source)
XLA Modules:
  0.0 62.7 jit_solution(16976989927458724624)
XLA Ops:
  0.6 0.9 %copy-done.4 = f32[128,400]{0,1:T(8,128)S(1)} copy-done((f32[128,400]{0,1:T(8,128)S(1)}, f32[128,400]{0,1:T(8,128)}, u32[]{:S(2)}) %copy-start.4) | copy-done | bytes 204824
  1.6 0.3 shard_map.149.refs_0_
  1.9 3.1 %collective-permute-start.5 = (bf16[400,128]{1,0:T(8,128)(2,1)S(1)}, bf16[400,128]{1,0:T(8,128)(2,1)S(1)}, u32[]{:S(2)}, u32[]{:S(2)}) collective-permute-start(bf16[400,128]{1,0:T(8,128)(2,1)S(1)} %shard_map.149.refs_0_), channel_id=1, source_target_pairs={{0,8},{4,12},{8,0},{12,4},{16,24},{20,28},{24,16},{28,20},{1,9},{5... | collective-permute-start | bytes 307208 | tf_op jit(solution)/shard_map/ppermute | solution.py:306
  5.0 2.5 %collective-permute-start.4 = (bf16[400,128]{1,0:T(8,128)(2,1)S(1)}, bf16[400,128]{1,0:T(8,128)(2,1)S(1)}, u32[]{:S(2)}, u32[]{:S(2)}) collective-permute-start(bf16[400,128]{1,0:T(8,128)(2,1)S(1)} %shard_map.149.refs_0_), channel_id=1, source_target_pairs={{0,24},{4,28},{8,16},{12,20},{16,8},{20,12},{24,0},{28,4},{1,25},{... | collective-permute-start | bytes 307208 | tf_op jit(solution)/shard_map/ppermute | solution.py:306
  7.4 0.1 collective-permute-start.3
  7.6 0.8 %pad_add_fusion = s32[5,1024]{1,0:T(8,128)S(1)} fusion(s32[2,1024]{1,0:T(2,128)} %bitcast.27, s32[1,1024]{1,0:T(1,128)} %bitcast.28, s32[1,1024]{1,0:T(1,128)} %bitcast.29, s32[1,1024]{1,0:T(1,128)} %bitcast.30), kind=kLoop, calls=%fused_computation | loop fusion | flops 15360 | bytes 40960 | tf_op jit(solution)/shard_map/concatenate | solution.py:353
  8.3 0.4 collective-permute-start.1
  8.7 0.9 %copy-done.2 = f32[128,400]{0,1:T(8,128)S(1)} copy-done((f32[128,400]{0,1:T(8,128)S(1)}, f32[128,400]{0,1:T(8,128)}, u32[]{:S(2)}) %copy-start.2) | copy-done | bytes 204824
  9.7 0.3 shard_map.145.refs_0_
  10.0 1.2 %collective-permute-start = (bf16[400,128]{1,0:T(8,128)(2,1)S(1)}, bf16[400,128]{1,0:T(8,128)(2,1)S(1)}, u32[]{:S(2)}, u32[]{:S(2)}) collective-permute-start(bf16[400,128]{1,0:T(8,128)(2,1)S(1)} %shard_map.145.refs_0_), channel_id=1, source_target_pairs={{0,2},{1,3},{2,0},{3,1},{4,6},{5,7},{6,4},{7,5},{8,10},{9,11},{10,... | collective-permute-start | bytes 307208 | tf_op jit(solution)/shard_map/ppermute | solution.py:309
  11.2 0.1 pad_add_fusion.1.place_ref
  11.3 1.0 %copy-done = f32[256,400]{0,1:T(8,128)S(1)} copy-done((f32[256,400]{0,1:T(8,128)S(1)}, f32[256,400]{0,1:T(8,128)}, u32[]{:S(2)}) %copy-start) | copy-done | bytes 409624
  12.3 1.6 %shard_map.147 = (f32[2,1024,128]{2,1,0:T(8,128)S(1)}, bf16[400,256]{1,0:T(8,128)(2,1)S(1)}, s32[5,1024]{1,0:T(8,128)S(1)}) custom-call(s32[5,1024]{1,0:T(8,128)S(1)} %collective-permute-done.1.refs_2_.ids_ref, f32[400,256]{1,0:T(8,128)S(1)} %bitcast.18, s32[2]{0:T(128)S(1)} %pad_add_fusion.1.place_ref), custom_call_target="tpu_custom_call" | custom-call | tf_op jit(solution)/shard_map/pallas_call | solution.py:53
  13.8 1.2 %collective-permute-done.refs_1_ = bf16[400,128]{1,0:T(8,128)(2,1)S(1)} collective-permute-done((bf16[400,128]{1,0:T(8,128)(2,1)S(1)}, bf16[400,128]{1,0:T(8,128)(2,1)S(1)}, u32[]{:S(2)}, u32[]{:S(2)}) %collective-permute-start) | collective-permute-done | bytes 102432 | tf_op jit(solution)/shard_map/ppermute | solution.py:309
  15.0 0.1 collective-permute-start.2
  15.2 1.6 %collective-permute-start.7 = (bf16[400,256]{1,0:T(8,128)(2,1)S(1)}, bf16[400,256]{1,0:T(8,128)(2,1)S(1)}, u32[]{:S(2)}, u32[]{:S(2)}) collective-permute-start(bf16[400,256]{1,0:T(8,128)(2,1)S(1)} %shard_map.150.refs_2_), channel_id=1, source_target_pairs={{0,4},{4,0},{8,12},{12,8},{16,20},{20,16},{24,28},{28,24},{1,5},{5... | collective-permute-start | bytes 614408 | tf_op jit(solution)/shard_map/ppermute | solution.py:306
  16.8 1.6 %collective-permute-start.6 = (bf16[400,256]{1,0:T(8,128)(2,1)S(1)}, bf16[400,256]{1,0:T(8,128)(2,1)S(1)}, u32[]{:S(2)}, u32[]{:S(2)}) collective-permute-start(bf16[400,256]{1,0:T(8,128)(2,1)S(1)} %shard_map.151.refs_2_), channel_id=1, source_target_pairs={{0,4},{4,0},{8,12},{12,8},{16,20},{20,16},{24,28},{28,24},{1,5},{5... | collective-permute-start | bytes 614408 | tf_op jit(solution)/shard_map/ppermute | solution.py:306
  18.5 0.9 %shard_map.148 = (bf16[400,1024]{1,0:T(8,128)(2,1)S(1)}, bf16[400,1024]{1,0:T(8,128)(2,1)S(1)}, bf16[400,1024]{1,0:T(8,128)(2,1)S(1)}) custom-call(bf16[400,128]{1,0:T(8,128)(2,1)S(1)} %shard_map.145.refs_0_, bf16[400,128]{1,0:T(8,128)(2,1)S(1)} %collective-permute-done.refs_1_, bf16[400,256]{1,0:T(8,128)(2,1)S(1)} %collective-permute-done.2.refs_2_, ...), custom_call_target="tpu_custom_call" | custom-call | tf_op jit(solution)/shard_map/pallas_call | solution.py:53
  19.4 1.8 %shard_map.152 = (f32[400,512]{1,0:T(8,128)S(1)}, f32[400,1024]{1,0:T(8,128)S(1)}) custom-call(bf16[400,128]{1,0:T(8,128)(2,1)S(1)} %shard_map.149.refs_0_, bf16[400,128]{1,0:T(8,128)(2,1)S(1)} %collective-permute-done.5.refs_1_, bf16[400,128]{1,0:T(8,128)(2,1)S(1)} %collective-permute-done.3.refs_0_.refs_2_, ...), custom_call_target="tpu_custom_call" | custom-call | tf_op jit(solution)/shard_map/pallas_call | solution.py:53
  21.2 1.9 %collective-permute-done.7.rows_ref = bf16[400,256]{1,0:T(8,128)(2,1)S(1)} collective-permute-done((bf16[400,256]{1,0:T(8,128)(2,1)S(1)}, bf16[400,256]{1,0:T(8,128)(2,1)S(1)}, u32[]{:S(2)}, u32[]{:S(2)}) %collective-permute-start.7) | collective-permute-done | bytes 204832 | tf_op jit(solution)/shard_map/ppermute | solution.py:306
  23.1 1.0 %shard_map.153 = (bf16[400,256]{1,0:T(8,128)(2,1)S(1)}, f32[400,1024]{1,0:T(8,128)S(1)}) custom-call(bf16[400,256]{1,0:T(8,128)(2,1)S(1)} %collective-permute-done.7.rows_ref, bf16[400,1024]{1,0:T(8,128)(2,1)S(1)} %get-tuple-element.39.refs_4_.q_ref.refs_1_, f32[2,1024,128]{2,1,0:T(8,128)S(1)} %get-tuple-element.40.refs_5_.weight_ref.refs_2_, ...), custom_call_target="tpu_custom_call" | custom-call | flops 6000000000 | tf_op jit(solution)/shard_map/pallas_call | solution.py:53
  24.2 1.6 %collective-permute-start.11 = (bf16[400,256]{1,0:T(8,128)(2,1)S(1)}, bf16[400,256]{1,0:T(8,128)(2,1)S(1)}, u32[]{:S(2)}, u32[]{:S(2)}) collective-permute-start(bf16[400,256]{1,0:T(8,128)(2,1)S(1)} %get-tuple-element.54), channel_id=1, source_target_pairs={{0,4},{4,0},{8,12},{12,8},{16,20},{20,16},{24,28},{28,24},{1,5},{5... | collective-permute-start | bytes 614408 | tf_op jit(solution)/shard_map/ppermute | solution.py:306
  25.7 1.7 %collective-permute-done.6.refs_0_ = bf16[400,256]{1,0:T(8,128)(2,1)S(1)} collective-permute-done((bf16[400,256]{1,0:T(8,128)(2,1)S(1)}, bf16[400,256]{1,0:T(8,128)(2,1)S(1)}, u32[]{:S(2)}, u32[]{:S(2)}) %collective-permute-start.6) | collective-permute-done | bytes 204832 | tf_op jit(solution)/shard_map/ppermute | solution.py:306
  27.5 1.9 %shard_map.155 = (bf16[256,1024]{1,0:T(8,128)(2,1)S(1)}, f32[400,1024]{1,0:T(8,128)S(1)}, f32[416,128]{1,0:T(8,128)S(1)}, bf16[416,128]{1,0:T(8,128)(2,1)S(1)}) custom-call(bf16[400,256]{1,0:T(8,128)(2,1)S(1)} %collective-permute-done.6.refs_0_, bf16[400,1024]{1,0:T(8,128)(2,1)S(1)} %get-tuple-element.39.refs_4_.q_ref.refs_1_, ...), custom_call_target="tpu_custom_call" | custom-call | tf_op jit(solution)/shard_map/pallas_call | solution.py:53
  29.4 0.1 collective-permute-start.17
  29.4 0.9 %shard_map.156 = (bf16[400,256]{1,0:T(8,128)(2,1)S(1)}, f32[400,256]{1,0:T(8,128)S(1)}, bf16[400,256]{1,0:T(8,128)(2,1)S(1)}) custom-call(bf16[400,1024]{1,0:T(8,128)(2,1)S(1)} %get-tuple-element.39.refs_4_.q_ref.refs_1_, bf16[256,1024]{1,0:T(8,128)(2,1)S(1)} %get-tuple-element.44.m_ref, f32[400,1024]{1,0:T(8,128)S(1)} %get-tuple-element.45.g_ref, ...), custom_call_target="tpu_custom_call" | custom-call | tf_op jit(solution)/shard_map/pallas_call | solution.py:53
  30.4 0.6 collective-permute-start.9
  31.0 0.5 collective-permute-done.11.got_ref.refs_2_
  31.5 1.6 %collective-permute-start.18 = (bf16[208,128]{1,0:T(8,128)(2,1)S(1)}, bf16[208,128]{1,0:T(8,128)(2,1)S(1)}, u32[]{:S(2)}, u32[]{:S(2)}) collective-permute-start(bf16[208,128]{1,0:T(8,128)(2,1)S(1)} %get-tuple-element.65), channel_id=1, source_target_pairs={{0,2},{1,3},{2,0},{3,1},{4,6},{5,7},{6,4},{7,5},{8,10},{9,11},{10,... | collective-permute-start | bytes 159752 | tf_op jit(solution)/shard_map/ppermute | solution.py:309
  33.1 0.1 shard_map.159
  33.2 2.1 %collective-permute-start.13 = (bf16[400,128]{1,0:T(8,128)(2,1)S(1)}, bf16[400,128]{1,0:T(8,128)(2,1)S(1)}, u32[]{:S(2)}, u32[]{:S(2)}) collective-permute-start(bf16[400,128]{1,0:T(8,128)(2,1)S(1)} %get-tuple-element.56), channel_id=1, source_target_pairs={{0,9},{1,10},{2,11},{3,8},{4,13},{5,14},{6,15},{7,12},{8,1},{9,2},... | collective-permute-start | bytes 307208 | tf_op jit(solution)/shard_map/ppermute | solution.py:316
  35.2 1.5 %collective-permute-start.14 = (bf16[400,256]{1,0:T(8,128)(2,1)S(1)}, bf16[400,256]{1,0:T(8,128)(2,1)S(1)}, u32[]{:S(2)}, u32[]{:S(2)}) collective-permute-start(bf16[400,256]{1,0:T(8,128)(2,1)S(1)} %get-tuple-element.57.refs_3_), channel_id=1, source_target_pairs={{0,4},{4,0},{8,12},{12,8},{16,20},{20,16},{24,28},{28,24},{1,5},{5... | collective-permute-start | bytes 614408 | tf_op jit(solution)/shard_map/ppermute | solution.py:306
  36.8 0.7 %collective-permute-start.19 = (bf16[208,128]{1,0:T(8,128)(2,1)S(1)}, bf16[208,128]{1,0:T(8,128)(2,1)S(1)}, u32[]{:S(2)}, u32[]{:S(2)}) collective-permute-start(bf16[208,128]{1,0:T(8,128)(2,1)S(1)} %shard_map.165.refs_0_), channel_id=1, source_target_pairs={{0,8},{4,12},{8,0},{12,4},{16,24},{20,28},{24,16},{28,20},{1,9},{5... | collective-permute-start | bytes 159752 | tf_op jit(solution)/shard_map/ppermute | solution.py:306
  37.6 1.5 %collective-permute-done.13.refs_1_ = bf16[400,128]{1,0:T(8,128)(2,1)S(1)} collective-permute-done((bf16[400,128]{1,0:T(8,128)(2,1)S(1)}, bf16[400,128]{1,0:T(8,128)(2,1)S(1)}, u32[]{:S(2)}, u32[]{:S(2)}) %collective-permute-start.13) | collective-permute-done | bytes 102432 | tf_op jit(solution)/shard_map/ppermute | solution.py:316
  39.2 3.0 %collective-permute-done.14.got_ref.refs_4_ = bf16[400,256]{1,0:T(8,128)(2,1)S(1)} collective-permute-done((bf16[400,256]{1,0:T(8,128)(2,1)S(1)}, bf16[400,256]{1,0:T(8,128)(2,1)S(1)}, u32[]{:S(2)}, u32[]{:S(2)}) %collective-permute-start.14) | collective-permute-done | bytes 204832 | tf_op jit(solution)/shard_map/ppermute | solution.py:306
  42.1 1.8 %collective-permute-start.20 = (bf16[208,128]{1,0:T(8,128)(2,1)S(1)}, bf16[208,128]{1,0:T(8,128)(2,1)S(1)}, u32[]{:S(2)}, u32[]{:S(2)}) collective-permute-start(bf16[208,128]{1,0:T(8,128)(2,1)S(1)} %shard_map.166.refs_0_), channel_id=1, source_target_pairs={{0,16},{4,20},{8,24},{12,28},{16,0},{20,4},{24,8},{28,12},{1,17},{... | collective-permute-start | bytes 159752 | tf_op jit(solution)/shard_map/ppermute | solution.py:306
  43.9 0.1 shard_map.161
  44.0 0.1 collective-permute-start.15
  44.0 4.3 %collective-permute-start.16 = (bf16[400,128]{1,0:T(8,128)(2,1)S(1)}, bf16[400,128]{1,0:T(8,128)(2,1)S(1)}, u32[]{:S(2)}, u32[]{:S(2)}) collective-permute-start(bf16[400,128]{1,0:T(8,128)(2,1)S(1)} %get-tuple-element.59), channel_id=1, source_target_pairs={{0,25},{1,26},{2,27},{3,24},{4,29},{5,30},{6,31},{7,28},{8,17},{9,... | collective-permute-start | bytes 307208 | tf_op jit(solution)/shard_map/ppermute | solution.py:316
  48.4 0.5 collective-permute-start.10
  48.9 1.6 %collective-permute-start.21 = (bf16[208,128]{1,0:T(8,128)(2,1)S(1)}, bf16[208,128]{1,0:T(8,128)(2,1)S(1)}, u32[]{:S(2)}, u32[]{:S(2)}) collective-permute-start(bf16[208,128]{1,0:T(8,128)(2,1)S(1)} %shard_map.167.refs_0_), channel_id=1, source_target_pairs={{0,4},{4,0},{8,12},{12,8},{16,20},{20,16},{24,28},{28,24},{1,5},{5... | collective-permute-start | bytes 159752 | tf_op jit(solution)/shard_map/ppermute | solution.py:306
  50.5 4.6 %collective-permute-done.15.refs_0_ = bf16[400,128]{1,0:T(8,128)(2,1)S(1)} collective-permute-done((bf16[400,128]{1,0:T(8,128)(2,1)S(1)}, bf16[400,128]{1,0:T(8,128)(2,1)S(1)}, u32[]{:S(2)}, u32[]{:S(2)}) %collective-permute-start.15) | collective-permute-done | bytes 102432 | tf_op jit(solution)/shard_map/ppermute | solution.py:316
  55.3 2.8 %collective-permute-start.22 = (bf16[208,128]{1,0:T(8,128)(2,1)S(1)}, bf16[208,128]{1,0:T(8,128)(2,1)S(1)}, u32[]{:S(2)}, u32[]{:S(2)}) collective-permute-start(bf16[208,128]{1,0:T(8,128)(2,1)S(1)} %shard_map.168.refs_0_), channel_id=1, source_target_pairs={{0,2},{1,3},{2,0},{3,1},{4,6},{5,7},{6,4},{7,5},{8,10},{9,11},{10,... | collective-permute-start | bytes 159752 | tf_op jit(solution)/shard_map/ppermute | solution.py:309
  58.0 2.1 %collective-permute-done.22.refs_1_ = bf16[208,128]{1,0:T(8,128)(2,1)S(1)} collective-permute-done((bf16[208,128]{1,0:T(8,128)(2,1)S(1)}, bf16[208,128]{1,0:T(8,128)(2,1)S(1)}, u32[]{:S(2)}, u32[]{:S(2)}) %collective-permute-start.22) | collective-permute-done | bytes 53280 | tf_op jit(solution)/shard_map/ppermute | solution.py:309
  60.2 0.1 collective-permute-start.23
  60.2 0.8 %shard_map.163 = (f32[400,128]{1,0:T(8,128)}, f32[1,128]{1,0:T(1,128)}) custom-call(f32[400,128]{1,0:T(8,128)S(1)} %shard_map.160.refs_0_.refs_2_, f32[400,128]{1,0:T(8,128)S(1)} %shard_map.162.refs_1_.refs_2_, f32[408,128]{1,0:T(8,128)S(1)} %collective-permute-done.8.refs_7_.refs_2_.refs_3_, f32[408,128]{1,0:T(8,128)S(1)} %collective-permute-done.8.refs_7_.refs_2_.refs_3_), custom_call_target="tpu_custom_call" | custom-call | tf_op jit(solution)/shard_map/pallas_call | solution.py:53
  61.0 0.8 %shard_map.158 = (f32[400,128]{1,0:T(8,128)}, f32[1,128]{1,0:T(1,128)}) custom-call(f32[400,128]{1,0:T(8,128)S(1)} %get-tuple-element.49.refs_0_.refs_3_, bf16[400,128]{1,0:T(8,128)(2,1)S(1)} %collective-permute-done.10.refs_1_.refs_3_, f32[400,128]{1,0:T(8,128)S(1)} %bitcast.21, f32[1,128]{1,0:T(1,128)S(1)} %bitcast.25), custom_call_target="tpu_custom_call" | custom-call | tf_op jit(solution)/shard_map/pallas_call | solution.py:53
  61.8 0.9 %shard_map.170 = (f32[400,256]{1,0:T(8,128)}, f32[1,256]{1,0:T(1,128)}) custom-call(bf16[208,128]{1,0:T(8,128)(2,1)S(1)} %shard_map.168.refs_0_, bf16[208,128]{1,0:T(8,128)(2,1)S(1)} %collective-permute-done.22.refs_1_, bf16[416,128]{1,0:T(8,128)(2,1)S(1)} %collective-permute-done.23.refs_2_, f32[400,256]{1,0:T(8,128)S(1)} %bitcast.19, ...), custom_call_target="tpu_custom_call" | custom-call | tf_op jit(solution)/shard_map/pallas_call | solution.py:53
  (46 shorter events, 0.5 us)
Async XLA Ops:
  0.6 0.9 %copy-start.4 = (f32[128,400]{0,1:T(8,128)S(1)}, f32[128,400]{0,1:T(8,128)}, u32[]{:S(2)}) copy-start(f32[128,400]{0,1:T(8,128)} %param.12) | copy-start | bytes 614404
  1.9 13.2 %collective-permute-start.5 = (bf16[400,128]{1,0:T(8,128)(2,1)S(1)}, bf16[400,128]{1,0:T(8,128)(2,1)S(1)}, u32[]{:S(2)}, u32[]{:S(2)}) collective-permute-start(bf16[400,128]{1,0:T(8,128)(2,1)S(1)} %shard_map.149.refs_0_), channel_id=1, source_target_pairs={{0,8},{4,12},{8,0},{12,4},{16,24},{20,28},{24,16},{28,20},{1,9},{5... | collective-permute-start | bytes 307208 | tf_op jit(solution)/shard_map/ppermute | solution.py:306
  5.0 11.8 %collective-permute-start.4 = (bf16[400,128]{1,0:T(8,128)(2,1)S(1)}, bf16[400,128]{1,0:T(8,128)(2,1)S(1)}, u32[]{:S(2)}, u32[]{:S(2)}) collective-permute-start(bf16[400,128]{1,0:T(8,128)(2,1)S(1)} %shard_map.149.refs_0_), channel_id=1, source_target_pairs={{0,24},{4,28},{8,16},{12,20},{16,8},{20,12},{24,0},{28,4},{1,25},{... | collective-permute-start | bytes 307208 | tf_op jit(solution)/shard_map/ppermute | solution.py:306
  7.4 9.3 %collective-permute-start.3 = (bf16[400,128]{1,0:T(8,128)(2,1)S(1)}, bf16[400,128]{1,0:T(8,128)(2,1)S(1)}, u32[]{:S(2)}, u32[]{:S(2)}) collective-permute-start(bf16[400,128]{1,0:T(8,128)(2,1)S(1)} %shard_map.149.refs_0_), channel_id=1, source_target_pairs={{0,16},{4,20},{8,24},{12,28},{16,0},{20,4},{24,8},{28,12},{1,17},{... | collective-permute-start | bytes 307208 | tf_op jit(solution)/shard_map/ppermute | solution.py:306
  8.3 2.9 %collective-permute-start.1 = (s32[5,1024]{1,0:T(8,128)S(1)}, s32[5,1024]{1,0:T(8,128)S(1)}, u32[]{:S(2)}, u32[]{:S(2)}) collective-permute-start(s32[5,1024]{1,0:T(8,128)S(1)} %pad_add_fusion), channel_id=1, source_target_pairs={{0,3},{1,0},{2,1},{3,2},{4,7},{5,4},{6,5},{7,6},{8,11},{9,8},{10,9... | collective-permute-start | bytes 61448 | tf_op jit(solution)/shard_map/ppermute | solution.py:354
  8.7 0.9 %copy-start.2 = (f32[128,400]{0,1:T(8,128)S(1)}, f32[128,400]{0,1:T(8,128)}, u32[]{:S(2)}) copy-start(f32[128,400]{0,1:T(8,128)} %param.10) | copy-start | bytes 614404
  10.0 5.0 %collective-permute-start = (bf16[400,128]{1,0:T(8,128)(2,1)S(1)}, bf16[400,128]{1,0:T(8,128)(2,1)S(1)}, u32[]{:S(2)}, u32[]{:S(2)}) collective-permute-start(bf16[400,128]{1,0:T(8,128)(2,1)S(1)} %shard_map.145.refs_0_), channel_id=1, source_target_pairs={{0,2},{1,3},{2,0},{3,1},{4,6},{5,7},{6,4},{7,5},{8,10},{9,11},{10,... | collective-permute-start | bytes 307208 | tf_op jit(solution)/shard_map/ppermute | solution.py:309
  11.3 1.0 %copy-start = (f32[256,400]{0,1:T(8,128)S(1)}, f32[256,400]{0,1:T(8,128)}, u32[]{:S(2)}) copy-start(f32[256,400]{0,1:T(8,128)} %param.14) | copy-start | bytes 1228804
  15.0 3.4 %collective-permute-start.2 = (bf16[400,256]{1,0:T(8,128)(2,1)S(1)}, bf16[400,256]{1,0:T(8,128)(2,1)S(1)}, u32[]{:S(2)}, u32[]{:S(2)}) collective-permute-start(bf16[400,256]{1,0:T(8,128)(2,1)S(1)} %shard_map.146), channel_id=1, source_target_pairs={{0,1},{1,0},{2,3},{3,2},{4,5},{5,4},{6,7},{7,6},{8,9},{9,8},{10,11... | collective-permute-start | bytes 614408 | tf_op jit(solution)/shard_map/ppermute | solution.py:309
  15.1 3.2 %copy-start.5 = (f32[128,400]{0,1:T(8,128)S(1)}, f32[128,400]{0,1:T(8,128)}, u32[]{:S(2)}) copy-start(f32[128,400]{0,1:T(8,128)} %param.12) | copy-start | bytes 614404
  15.2 3.2 %copy-start.8 = (f32[128]{0:T(128)S(1)}, f32[128]{0:T(128)}, u32[]{:S(2)}) copy-start(f32[128]{0:T(128)} %param.13) | copy-start | bytes 1540
  15.2 7.9 %collective-permute-start.7 = (bf16[400,256]{1,0:T(8,128)(2,1)S(1)}, bf16[400,256]{1,0:T(8,128)(2,1)S(1)}, u32[]{:S(2)}, u32[]{:S(2)}) collective-permute-start(bf16[400,256]{1,0:T(8,128)(2,1)S(1)} %shard_map.150.refs_2_), channel_id=1, source_target_pairs={{0,4},{4,0},{8,12},{12,8},{16,20},{20,16},{24,28},{28,24},{1,5},{5... | collective-permute-start | bytes 614408 | tf_op jit(solution)/shard_map/ppermute | solution.py:306
  16.8 10.7 %collective-permute-start.6 = (bf16[400,256]{1,0:T(8,128)(2,1)S(1)}, bf16[400,256]{1,0:T(8,128)(2,1)S(1)}, u32[]{:S(2)}, u32[]{:S(2)}) collective-permute-start(bf16[400,256]{1,0:T(8,128)(2,1)S(1)} %shard_map.151.refs_2_), channel_id=1, source_target_pairs={{0,4},{4,0},{8,12},{12,8},{16,20},{20,16},{24,28},{28,24},{1,5},{5... | collective-permute-start | bytes 614408 | tf_op jit(solution)/shard_map/ppermute | solution.py:306
  18.4 9.1 %collective-permute-start.8 = (f32[408,128]{1,0:T(8,128)S(1)}, f32[408,128]{1,0:T(8,128)S(1)}, u32[]{:S(2)}, u32[]{:S(2)}) collective-permute-start(f32[408,128]{1,0:T(8,128)S(1)} %shard_map.154), channel_id=1, source_target_pairs={{0,1},{1,2},{2,3},{3,0},{4,5},{5,6},{6,7},{7,4},{8,9},{9,10},{10,1... | collective-permute-start | bytes 626696 | tf_op jit(solution)/shard_map/ppermute | solution.py:316
  24.2 7.3 %collective-permute-start.11 = (bf16[400,256]{1,0:T(8,128)(2,1)S(1)}, bf16[400,256]{1,0:T(8,128)(2,1)S(1)}, u32[]{:S(2)}, u32[]{:S(2)}) collective-permute-start(bf16[400,256]{1,0:T(8,128)(2,1)S(1)} %get-tuple-element.54), channel_id=1, source_target_pairs={{0,4},{4,0},{8,12},{12,8},{16,20},{20,16},{24,28},{28,24},{1,5},{5... | collective-permute-start | bytes 614408 | tf_op jit(solution)/shard_map/ppermute | solution.py:306
  29.4 1.6 %collective-permute-start.17 = (bf16[416,128]{1,0:T(8,128)(2,1)S(1)}, bf16[416,128]{1,0:T(8,128)(2,1)S(1)}, u32[]{:S(2)}, u32[]{:S(2)}) collective-permute-start(bf16[416,128]{1,0:T(8,128)(2,1)S(1)} %get-tuple-element.63), channel_id=1, source_target_pairs={{0,1},{1,0},{2,3},{3,2},{4,5},{5,4},{6,7},{7,6},{8,9},{9,8},{10,11... | collective-permute-start | bytes 319496 | tf_op jit(solution)/shard_map/ppermute | solution.py:309
  30.4 6.4 %collective-permute-start.9 = (bf16[400,256]{1,0:T(8,128)(2,1)S(1)}, bf16[400,256]{1,0:T(8,128)(2,1)S(1)}, u32[]{:S(2)}, u32[]{:S(2)}) collective-permute-start(bf16[400,256]{1,0:T(8,128)(2,1)S(1)} %get-tuple-element.48), channel_id=1, source_target_pairs={{0,1},{1,0},{2,3},{3,2},{4,5},{5,4},{6,7},{7,6},{8,9},{9,8},{10,11... | collective-permute-start | bytes 614408 | tf_op jit(solution)/shard_map/ppermute | solution.py:309
  31.5 5.3 %collective-permute-start.18 = (bf16[208,128]{1,0:T(8,128)(2,1)S(1)}, bf16[208,128]{1,0:T(8,128)(2,1)S(1)}, u32[]{:S(2)}, u32[]{:S(2)}) collective-permute-start(bf16[208,128]{1,0:T(8,128)(2,1)S(1)} %get-tuple-element.65), channel_id=1, source_target_pairs={{0,2},{1,3},{2,0},{3,1},{4,6},{5,7},{6,4},{7,5},{8,10},{9,11},{10,... | collective-permute-start | bytes 159752 | tf_op jit(solution)/shard_map/ppermute | solution.py:309
  33.1 4.5 %collective-permute-start.12 = (bf16[400,128]{1,0:T(8,128)(2,1)S(1)}, bf16[400,128]{1,0:T(8,128)(2,1)S(1)}, u32[]{:S(2)}, u32[]{:S(2)}) collective-permute-start(bf16[400,128]{1,0:T(8,128)(2,1)S(1)} %get-tuple-element.55), channel_id=1, source_target_pairs={{0,1},{1,2},{2,3},{3,0},{4,5},{5,6},{6,7},{7,4},{8,9},{9,10},{10,1... | collective-permute-start | bytes 307208 | tf_op jit(solution)/shard_map/ppermute | solution.py:316
  33.2 5.9 %collective-permute-start.13 = (bf16[400,128]{1,0:T(8,128)(2,1)S(1)}, bf16[400,128]{1,0:T(8,128)(2,1)S(1)}, u32[]{:S(2)}, u32[]{:S(2)}) collective-permute-start(bf16[400,128]{1,0:T(8,128)(2,1)S(1)} %get-tuple-element.56), channel_id=1, source_target_pairs={{0,9},{1,10},{2,11},{3,8},{4,13},{5,14},{6,15},{7,12},{8,1},{9,2},... | collective-permute-start | bytes 307208 | tf_op jit(solution)/shard_map/ppermute | solution.py:316
  35.2 6.9 %collective-permute-start.14 = (bf16[400,256]{1,0:T(8,128)(2,1)S(1)}, bf16[400,256]{1,0:T(8,128)(2,1)S(1)}, u32[]{:S(2)}, u32[]{:S(2)}) collective-permute-start(bf16[400,256]{1,0:T(8,128)(2,1)S(1)} %get-tuple-element.57.refs_3_), channel_id=1, source_target_pairs={{0,4},{4,0},{8,12},{12,8},{16,20},{20,16},{24,28},{28,24},{1,5},{5... | collective-permute-start | bytes 614408 | tf_op jit(solution)/shard_map/ppermute | solution.py:306
  36.8 5.3 %collective-permute-start.19 = (bf16[208,128]{1,0:T(8,128)(2,1)S(1)}, bf16[208,128]{1,0:T(8,128)(2,1)S(1)}, u32[]{:S(2)}, u32[]{:S(2)}) collective-permute-start(bf16[208,128]{1,0:T(8,128)(2,1)S(1)} %shard_map.165.refs_0_), channel_id=1, source_target_pairs={{0,8},{4,12},{8,0},{12,4},{16,24},{20,28},{24,16},{28,20},{1,9},{5... | collective-permute-start | bytes 159752 | tf_op jit(solution)/shard_map/ppermute | solution.py:306
  42.1 6.8 %collective-permute-start.20 = (bf16[208,128]{1,0:T(8,128)(2,1)S(1)}, bf16[208,128]{1,0:T(8,128)(2,1)S(1)}, u32[]{:S(2)}, u32[]{:S(2)}) collective-permute-start(bf16[208,128]{1,0:T(8,128)(2,1)S(1)} %shard_map.166.refs_0_), channel_id=1, source_target_pairs={{0,16},{4,20},{8,24},{12,28},{16,0},{20,4},{24,8},{28,12},{1,17},{... | collective-permute-start | bytes 159752 | tf_op jit(solution)/shard_map/ppermute | solution.py:306
  44.0 11.2 %collective-permute-start.15 = (bf16[400,128]{1,0:T(8,128)(2,1)S(1)}, bf16[400,128]{1,0:T(8,128)(2,1)S(1)}, u32[]{:S(2)}, u32[]{:S(2)}) collective-permute-start(bf16[400,128]{1,0:T(8,128)(2,1)S(1)} %get-tuple-element.58), channel_id=1, source_target_pairs={{0,17},{1,18},{2,19},{3,16},{4,21},{5,22},{6,23},{7,20},{8,25},{9,... | collective-permute-start | bytes 307208 | tf_op jit(solution)/shard_map/ppermute | solution.py:316
  44.0 11.1 %collective-permute-start.16 = (bf16[400,128]{1,0:T(8,128)(2,1)S(1)}, bf16[400,128]{1,0:T(8,128)(2,1)S(1)}, u32[]{:S(2)}, u32[]{:S(2)}) collective-permute-start(bf16[400,128]{1,0:T(8,128)(2,1)S(1)} %get-tuple-element.59), channel_id=1, source_target_pairs={{0,25},{1,26},{2,27},{3,24},{4,29},{5,30},{6,31},{7,28},{8,17},{9,... | collective-permute-start | bytes 307208 | tf_op jit(solution)/shard_map/ppermute | solution.py:316
  48.4 6.9 %collective-permute-start.10 = (bf16[400,128]{1,0:T(8,128)(2,1)S(1)}, bf16[400,128]{1,0:T(8,128)(2,1)S(1)}, u32[]{:S(2)}, u32[]{:S(2)}) collective-permute-start(bf16[400,128]{1,0:T(8,128)(2,1)S(1)} %get-tuple-element.50), channel_id=1, source_target_pairs={{0,2},{1,3},{2,0},{3,1},{4,6},{5,7},{6,4},{7,5},{8,10},{9,11},{10,... | collective-permute-start | bytes 307208 | tf_op jit(solution)/shard_map/ppermute | solution.py:309
  48.9 6.3 %collective-permute-start.21 = (bf16[208,128]{1,0:T(8,128)(2,1)S(1)}, bf16[208,128]{1,0:T(8,128)(2,1)S(1)}, u32[]{:S(2)}, u32[]{:S(2)}) collective-permute-start(bf16[208,128]{1,0:T(8,128)(2,1)S(1)} %shard_map.167.refs_0_), channel_id=1, source_target_pairs={{0,4},{4,0},{8,12},{12,8},{16,20},{20,16},{24,28},{28,24},{1,5},{5... | collective-permute-start | bytes 159752 | tf_op jit(solution)/shard_map/ppermute | solution.py:306
  55.2 5.8 %copy-start.3 = (f32[128,400]{0,1:T(8,128)S(1)}, f32[128,400]{0,1:T(8,128)}, u32[]{:S(2)}) copy-start(f32[128,400]{0,1:T(8,128)} %param.10) | copy-start | bytes 614404
  55.2 5.8 %copy-start.7 = (f32[128]{0:T(128)S(1)}, f32[128]{0:T(128)}, u32[]{:S(2)}) copy-start(f32[128]{0:T(128)} %param.11) | copy-start | bytes 1540
  55.2 6.6 %copy-start.6 = (f32[256]{0:T(256)S(1)}, f32[256]{0:T(256)}, u32[]{:S(2)}) copy-start(f32[256]{0:T(256)} %param.15) | copy-start | bytes 3076
  55.3 6.5 %copy-start.1 = (f32[256,400]{0,1:T(8,128)S(1)}, f32[256,400]{0,1:T(8,128)}, u32[]{:S(2)}) copy-start(f32[256,400]{0,1:T(8,128)} %param.14) | copy-start | bytes 1228804
  55.3 4.9 %collective-permute-start.22 = (bf16[208,128]{1,0:T(8,128)(2,1)S(1)}, bf16[208,128]{1,0:T(8,128)(2,1)S(1)}, u32[]{:S(2)}, u32[]{:S(2)}) collective-permute-start(bf16[208,128]{1,0:T(8,128)(2,1)S(1)} %shard_map.168.refs_0_), channel_id=1, source_target_pairs={{0,2},{1,3},{2,0},{3,1},{4,6},{5,7},{6,4},{7,5},{8,10},{9,11},{10,... | collective-permute-start | bytes 159752 | tf_op jit(solution)/shard_map/ppermute | solution.py:309
  60.2 1.6 %collective-permute-start.23 = (bf16[416,128]{1,0:T(8,128)(2,1)S(1)}, bf16[416,128]{1,0:T(8,128)(2,1)S(1)}, u32[]{:S(2)}, u32[]{:S(2)}) collective-permute-start(bf16[416,128]{1,0:T(8,128)(2,1)S(1)} %shard_map.169), channel_id=1, source_target_pairs={{0,1},{1,0},{2,3},{3,2},{4,5},{5,4},{6,7},{7,6},{8,9},{9,8},{10,11... | collective-permute-start | bytes 319496 | tf_op jit(solution)/shard_map/ppermute | solution.py:309

commit v10 on v8

--- a/solution.py
+++ b/solution.py
@@ -14,9 +14,7 @@
 VMEM_LIMIT = 32 * 1024 * 1024
 LANES = 128
 COST_JOIN = 6e9
-COST_UPDATE = 12e9
-COST_HIGH = 12e9
-COST_LOW = 12e9
+COST_UPDATE = 6e9
 COST_SUM = 1e9
 
 
@@ -200,11 +198,8 @@
             mine_ref[at, :] = piece
 
 
-def rest_body(q_ref, m_ref, g_ref, o_ref, ids_ref, hi_ref, lo_ref, near_ref, far_ref, left_ref):
-    far = dot(q_ref[...], m_ref[...], 1, 1).astype(BF)
-    half = far.shape[1] // 2
-    hi_ref[...] = far[:, half:]
-    lo_ref[...] = far[:, :half]
+def rest_body(q_ref, m_ref, g_ref, o_ref, ids_ref, right_ref, near_ref, far_ref, left_ref):
+    right_ref[...] = dot(q_ref[...], m_ref[...], 1, 1).astype(BF)
     edges = q_ref.shape[1]
     step = step_of(edges)
     for at in range(0, edges, step):
@@ -257,11 +252,10 @@
         refs[-1][k * size:(k + 1) * size, :] = ref[...]
 
 
-def chunk_body(base, near_ref, got_ref, *block_refs):
+def chunk_body(near_ref, got_ref, *block_refs):
     for k, ref in enumerate(block_refs):
         cols = slice(k * LANES, (k + 1) * LANES)
-        total = near_ref[:, base + k * LANES:base + (k + 1) * LANES] + got_ref[:, cols].astype(F32)
-        ref[...] = total.astype(BF)
+        ref[...] = (near_ref[:, cols] + got_ref[:, cols].astype(F32)).astype(BF)
 
 
 def sum_body(*refs):
@@ -336,7 +330,7 @@
         ids = [i.reshape(-1, i.shape[-1]) for i in ids]
         ids = jnp.concatenate([jnp.pad(i, ((0, 0), (0, longest - i.shape[-1]))) for i in ids], axis=0)
         ids = lax.ppermute(ids, "right", [(i, (i - 1) % n_right) for i in range(n_right)])
-        left_bf = cast(left_t, after=(other_own, ids))
+        left_bf = call(join_body, one_block, after=(other_own, ids))(cast(left_t))
         half_left = [left_bf] + [swap_right(left_bf, 2 * k) for k in range(1, far_right)]
         sibling_left = swap_right(jnp.concatenate(half_left, axis=1), 1)
         place = jnp.stack([here_r, here_l]).astype(jnp.int32)
@@ -356,7 +350,6 @@
             (shape(width, half), shape(width, edges)),
             [part, pltpu.VMEM((half, edges), BF)],
         )(*near, q, weight, ids)
-        chunk = shape(width, half // 2, dtype=BF)
         tall = nrel // LANES * width
         size = -(-tall // (n_right * 16)) * 16
         piece = shape(size, LANES, dtype=BF)
@@ -371,14 +364,19 @@
         )(other_own, other_rest, q, weight, ids, qg_near, s)
         left_rows = n_right * rows
         left_half = left_rows // 2
-        far_hi, far_lo, left_near, left_far = call(
+        right_far, left_near, left_far = call(
             rest_body,
-            (chunk, chunk, shape(width, left_half), shape(width, left_half, dtype=BF)),
+            (shape(width, half, dtype=BF), shape(width, left_half), shape(width, left_half, dtype=BF)),
             [pltpu.VMEM((width, left_rows), F32)],
         )(q, m, g, o, ids)
 
+        left_own, *blocks = call(left_body, (shape(width, rows),) + (one_block,) * (far_right - 1))(
+            left_near, swap_right(left_far, 1)
+        )
+        left_got = [swap_right(block, 2 * (k + 1)) for k, block in enumerate(blocks)]
+
         mine, *rest = call(
-            piece_body, (shape(size, LANES),) + (piece,) * (far_right - 1), flops=COST_SUM
+            piece_body, (shape(size, LANES),) + (piece,) * (far_right - 1), flops=COST_SUM, after=(right_far,)
         )(mine, swap_right(theirs, 1))
         got = [swap_right(p, 2 * (k + 1)) for k, p in enumerate(rest)]
         mine = call(sum_body, piece, flops=COST_SUM)(mine, *got)
@@ -386,24 +384,14 @@
         while bit < n_left:
             mine = call(sum_body, piece, flops=COST_SUM)(mine, swap_left(mine, bit))
             bit *= 2
+        right_got = swap_left(right_far, 1)
+        blocks = call(chunk_body, (one_block,) * outer, after=(*left_got, mine))(right_near, right_got)
+        right_got = [next_column(block, 2 * k) for k, block in enumerate(blocks)]
+
         mine = call(sum_body, piece, flops=COST_SUM)(mine, swap_left(mine, 1))
         pieces = [mine] + [swap_right(mine, 2 * k) for k in range(1, far_right)]
         sibling = swap_right(call(stack_body, shape(far_right * size, LANES, dtype=BF))(*pieces), 1)
 
-        left_own, *blocks = call(left_body, (shape(width, rows),) + (one_block,) * (far_right - 1))(
-            left_near, swap_right(left_far, 1)
-        )
-        left_got = [swap_right(block, 2 * (k + 1)) for k, block in enumerate(blocks)]
-
-        some = outer // 2
-        got_hi = swap_left(far_hi, 1)
-        got_lo = swap_left(far_lo, 1)
-        outs = (one_block,) * some
-        high = call(functools.partial(chunk_body, half // 2), outs, flops=COST_HIGH)(right_near, got_hi)
-        low = call(functools.partial(chunk_body, 0), outs, flops=COST_LOW, after=left_got)(right_near, got_lo)
-        right_got = [next_column(block, 2 * (some + k)) for k, block in enumerate(high)]
-        right_got += [next_column(block, 2 * k) for k, block in enumerate(low)]
-
         def update(got, table, state, flops=0):
             outs = (shape(width, rows), shape(1, rows))
             return call(functools.partial(update_body, len(got)), outs, flops=flops)(*got, table, state)
@@ -411,7 +399,11 @@
         left_new, left_state_new = update([left_own, *left_got], left_t, left_state[None, :])
         right_new, right_state_new = update(right_got, moved, moved, COST_UPDATE)
         relation_new, relation_state_new = call(
-            functools.partial(relation_body, n_right), (shape(width, nrel), shape(1, nrel)), [all_pieces], me
+            functools.partial(relation_body, n_right),
+            (shape(width, nrel), shape(1, nrel)),
+            [all_pieces],
+            me,
+            after=(right_state_new,),
         )(*pieces, sibling, relation_t, relation_state[None, :])
         return (
             left_new.T, left_state_new.reshape(-1), right_new.T, right_state_new.reshape(-1),

time: 56.9 us -> 59.3 us (1.042)
  waiting for transfers between devices: 10.9 us -> 16.9 us
  starting transfers between devices: 30.5 us -> 26.8 us
  local copies, waits for them, and re-layouts: 1.89 us -> 2.53 us
    ppermute x10 -> x9, waiting for transfers between devices: 2.05 us -> 8.97 us  [swap_left(): return lax.ppermute(value, 'left', [(i, i ^ by) for i in range(n_left)])]
    ppermute x5, starting transfers between devices: 9.62 us -> 5.39 us  [next_column(): return lax.ppermute(value, ('left', 'right'), perm)]
    ppermute x5, waiting for transfers between devices: 0.01 us -> 2.59 us  [next_column(): return lax.ppermute(value, ('left', 'right'), perm)]
    ppermute x8, waiting for transfers between devices: 7.28 us -> 5.02 us  [swap_right(): return lax.ppermute(value, 'right', [(i, i ^ by) for i in range(n_right)])]
    ppermute x8, starting transfers between devices: 5.54 us -> 7.33 us  [swap_right(): return lax.ppermute(value, 'right', [(i, i ^ by) for i in range(n_right)])]
    ppermute x10 -> x9, starting transfers between devices: 15.3 us -> 14 us  [swap_left(): return lax.ppermute(value, 'left', [(i, i ^ by) for i in range(n_left)])]
    ppermute x1, waiting for transfers between devices: 1.59 us -> 0.35 us  [per_device(): lax.ppermute(ids, 'right', [(i, (i - 1) % n_right) for i in range(n_right)])]
    unnamed x16 -> x18, local copies, waits for them, and re-layouts: 1.89 us -> 2.53 us
  transfers between devices with their start and end apart: 24 -> 23, of which waited for: 9 -> 11; matrix products, arithmetic and copies ran while one was open for 2% -> 1% of each run, Pallas kernels for 13% -> 13%
where the time goes in v10:
time: 59.3 us; the launch traced here: 59 us
  starting transfers between devices  26.8 us (45%)
  waiting for transfers between devices  16.9 us (28%)
  Pallas kernels  11.1 us (19%)
  local copies, waits for them, and re-layouts  2.53 us (4%)
  other arithmetic  0.86 us (1%)
  between operations  0.86 us (1%)
    ppermute x9, starting transfers between devices, swap_left(): return lax.ppermute(value, 'left', [(i, i ^ by) for i in range(n_left)])  14 us
    pallas_call x21, Pallas kernels, run(): pl.pallas_call(inner, out_shape=out_shape, in_specs=specs, scratch_shapes...  11.1 us
    ppermute x9, waiting for transfers between devices, swap_left(): return lax.ppermute(value, 'left', [(i, i ^ by) for i in range(n_left)])  8.97 us
    ppermute x8, starting transfers between devices, swap_right(): return lax.ppermute(value, 'right', [(i, i ^ by) for i in range(n_right)])  7.33 us
    ppermute x5, starting transfers between devices, next_column(): return lax.ppermute(value, ('left', 'right'), perm)  5.39 us
    ppermute x8, waiting for transfers between devices, swap_right(): return lax.ppermute(value, 'right', [(i, i ^ by) for i in range(n_right)])  5.02 us
    ppermute x5, waiting for transfers between devices, next_column(): return lax.ppermute(value, ('left', 'right'), perm)  2.59 us
    unnamed x18, local copies, waits for them, and re-layouts  2.53 us
  transfers between devices with their start and end apart: 23, of which 11 were waited for; matrix products, arithmetic and copies ran while one was open for 1% of the time, Pallas kernels for 13%

profile of v10, /device:TPU:0, one launch (start us, length us, event | category | flops | bytes accessed | tf_op | source)
XLA Modules:
  0.0 59.0 jit_solution(6405859440752209387)
XLA Ops:
  0.6 0.9 %copy-done.1 = f32[128,400]{0,1:T(8,128)S(1)} copy-done((f32[128,400]{0,1:T(8,128)S(1)}, f32[128,400]{0,1:T(8,128)}, u32[]{:S(2)}) %copy-start.1) | copy-done | bytes 204824
  1.6 0.3 shard_map.146.refs_0_
  1.9 5.1 %collective-permute-start.6 = (bf16[400,128]{1,0:T(8,128)(2,1)S(1)}, bf16[400,128]{1,0:T(8,128)(2,1)S(1)}, u32[]{:S(2)}, u32[]{:S(2)}) collective-permute-start(bf16[400,128]{1,0:T(8,128)(2,1)S(1)} %shard_map.146.refs_0_), channel_id=1, source_target_pairs={{0,24},{4,28},{8,16},{12,20},{16,8},{20,12},{24,0},{28,4},{1,25},{... | collective-permute-start | bytes 307208 | tf_op jit(solution)/shard_map/ppermute | solution.py:287
  7.0 0.6 %collective-permute-start.4 = (bf16[400,128]{1,0:T(8,128)(2,1)S(1)}, bf16[400,128]{1,0:T(8,128)(2,1)S(1)}, u32[]{:S(2)}, u32[]{:S(2)}) collective-permute-start(bf16[400,128]{1,0:T(8,128)(2,1)S(1)} %shard_map.146.refs_0_), channel_id=1, source_target_pairs={{0,8},{4,12},{8,0},{12,4},{16,24},{20,28},{24,16},{28,20},{1,9},{5... | collective-permute-start | bytes 307208 | tf_op jit(solution)/shard_map/ppermute | solution.py:287
  7.6 1.7 %collective-permute-start = (bf16[400,128]{1,0:T(8,128)(2,1)S(1)}, bf16[400,128]{1,0:T(8,128)(2,1)S(1)}, u32[]{:S(2)}, u32[]{:S(2)}) collective-permute-start(bf16[400,128]{1,0:T(8,128)(2,1)S(1)} %shard_map.146.refs_0_), channel_id=1, source_target_pairs={{0,4},{4,0},{8,12},{12,8},{16,20},{20,16},{24,28},{28,24},{1,5},{5... | collective-permute-start | bytes 307208 | tf_op jit(solution)/shard_map/ppermute | solution.py:287
  9.3 0.8 %pad_add_fusion = s32[5,1024]{1,0:T(8,128)S(1)} fusion(s32[2,1024]{1,0:T(2,128)} %bitcast.28, s32[1,1024]{1,0:T(1,128)} %bitcast.29, s32[1,1024]{1,0:T(1,128)} %bitcast.30, s32[1,1024]{1,0:T(1,128)} %bitcast.31), kind=kLoop, calls=%fused_computation.1 | loop fusion | flops 15360 | bytes 40960 | tf_op jit(solution)/shard_map/concatenate | solution.py:331
  10.1 0.1 collective-permute-start.1
  10.1 0.9 %copy-done.3 = f32[128,400]{0,1:T(8,128)S(1)} copy-done((f32[128,400]{0,1:T(8,128)S(1)}, f32[128,400]{0,1:T(8,128)}, u32[]{:S(2)}) %copy-start.3) | copy-done | bytes 204824
  11.1 0.3 shard_map.145.refs_0_
  11.4 0.3 collective-permute-done.1.refs_2_.ids_ref
  11.7 0.6 collective-permute-done.refs_1_.refs_0_
  12.3 1.7 %collective-permute-start.2 = (bf16[400,128]{1,0:T(8,128)(2,1)S(1)}, bf16[400,128]{1,0:T(8,128)(2,1)S(1)}, u32[]{:S(2)}, u32[]{:S(2)}) collective-permute-start(bf16[400,128]{1,0:T(8,128)(2,1)S(1)} %shard_map.147.refs_0_), channel_id=1, source_target_pairs={{0,2},{1,3},{2,0},{3,1},{4,6},{5,7},{6,4},{7,5},{8,10},{9,11},{10,... | collective-permute-start | bytes 307208 | tf_op jit(solution)/shard_map/ppermute | solution.py:290
  14.0 1.6 %collective-permute-done.5.refs_1_.refs_2_ = bf16[400,128]{1,0:T(8,128)(2,1)S(1)} collective-permute-done((bf16[400,128]{1,0:T(8,128)(2,1)S(1)}, bf16[400,128]{1,0:T(8,128)(2,1)S(1)}, u32[]{:S(2)}, u32[]{:S(2)}) %collective-permute-start.5) | collective-permute-done | bytes 102432 | tf_op jit(solution)/shard_map/ppermute | solution.py:287
  15.7 1.6 %collective-permute-start.7 = (bf16[400,384]{1,0:T(8,128)(2,1)S(1)}, bf16[400,384]{1,0:T(8,128)(2,1)S(1)}, u32[]{:S(2)}, u32[]{:S(2)}) collective-permute-start(bf16[400,384]{1,0:T(8,128)(2,1)S(1)} %shard_map.150.refs_2_), channel_id=1, source_target_pairs={{0,4},{4,0},{8,12},{12,8},{16,20},{20,16},{24,28},{28,24},{1,5},{5... | collective-permute-start | bytes 921608 | tf_op jit(solution)/shard_map/ppermute | solution.py:287
  17.3 0.1 collective-permute-start.8
  17.3 0.8 %collective-permute-done.2.refs_1_ = bf16[400,128]{1,0:T(8,128)(2,1)S(1)} collective-permute-done((bf16[400,128]{1,0:T(8,128)(2,1)S(1)}, bf16[400,128]{1,0:T(8,128)(2,1)S(1)}, u32[]{:S(2)}, u32[]{:S(2)}) %collective-permute-start.2) | collective-permute-done | bytes 102432 | tf_op jit(solution)/shard_map/ppermute | solution.py:290
  18.1 0.9 %collective-permute-start.3 = (bf16[400,256]{1,0:T(8,128)(2,1)S(1)}, bf16[400,256]{1,0:T(8,128)(2,1)S(1)}, u32[]{:S(2)}, u32[]{:S(2)}) collective-permute-start(bf16[400,256]{1,0:T(8,128)(2,1)S(1)} %pad_maximum_fusion), channel_id=1, source_target_pairs={{0,1},{1,0},{2,3},{3,2},{4,5},{5,4},{6,7},{7,6},{8,9},{9,8},{10,11... | collective-permute-start | bytes 614408 | tf_op jit(solution)/shard_map/ppermute | solution.py:290
  19.0 0.1 pad_add_fusion.1.place_ref
  19.1 1.6 %shard_map.148 = (f32[2,1024,128]{2,1,0:T(8,128)S(1)}, bf16[400,256]{1,0:T(8,128)(2,1)S(1)}, s32[5,1024]{1,0:T(8,128)S(1)}) custom-call(s32[5,1024]{1,0:T(8,128)S(1)} %collective-permute-done.1.refs_2_.ids_ref, f32[400,256]{1,0:T(8,128)S(1)} %bitcast.18, s32[2]{0:T(128)S(1)} %pad_add_fusion.1.place_ref), custom_call_target="tpu_custom_call" | custom-call | tf_op jit(solution)/shard_map/pallas_call | solution.py:49
  20.7 0.9 %shard_map.149 = (bf16[400,1024]{1,0:T(8,128)(2,1)S(1)}, bf16[400,1024]{1,0:T(8,128)(2,1)S(1)}, bf16[400,1024]{1,0:T(8,128)(2,1)S(1)}) custom-call(bf16[400,128]{1,0:T(8,128)(2,1)S(1)} %shard_map.147.refs_0_, bf16[400,128]{1,0:T(8,128)(2,1)S(1)} %collective-permute-done.2.refs_1_, bf16[400,256]{1,0:T(8,128)(2,1)S(1)} %collective-permute-done.3.refs_2_, ...), custom_call_target="tpu_custom_call" | custom-call | tf_op jit(solution)/shard_map/pallas_call | solution.py:49
  21.6 1.8 %shard_map.151 = (f32[400,512]{1,0:T(8,128)S(1)}, f32[400,1024]{1,0:T(8,128)S(1)}) custom-call(bf16[400,128]{1,0:T(8,128)(2,1)S(1)} %shard_map.146.refs_0_, bf16[400,128]{1,0:T(8,128)(2,1)S(1)} %collective-permute-done.4.refs_0_.refs_1_, bf16[400,128]{1,0:T(8,128)(2,1)S(1)} %collective-permute-done.5.refs_1_.refs_2_, ...), custom_call_target="tpu_custom_call" | custom-call | tf_op jit(solution)/shard_map/pallas_call | solution.py:49
  23.4 0.6 %collective-permute-done.7.refs_1_ = bf16[400,384]{1,0:T(8,128)(2,1)S(1)} collective-permute-done((bf16[400,384]{1,0:T(8,128)(2,1)S(1)}, bf16[400,384]{1,0:T(8,128)(2,1)S(1)}, u32[]{:S(2)}, u32[]{:S(2)}) %collective-permute-start.7) | collective-permute-done | bytes 307232 | tf_op jit(solution)/shard_map/ppermute | solution.py:287
  24.1 2.3 %shard_map.153 = (bf16[512,1024]{1,0:T(8,128)(2,1)S(1)}, f32[400,1024]{1,0:T(8,128)S(1)}, f32[416,128]{1,0:T(8,128)S(1)}, bf16[416,128]{1,0:T(8,128)(2,1)S(1)}) custom-call(bf16[400,128]{1,0:T(8,128)(2,1)S(1)} %collective-permute-done.refs_1_.refs_0_, bf16[400,384]{1,0:T(8,128)(2,1)S(1)} %collective-permute-done.7.refs_1_, ...), custom_call_target="tpu_custom_call" | custom-call | tf_op jit(solution)/shard_map/pallas_call | solution.py:49
  26.4 0.1 collective-permute-start.12
  26.5 1.1 %shard_map.154 = (bf16[400,512]{1,0:T(8,128)(2,1)S(1)}, f32[400,256]{1,0:T(8,128)S(1)}, bf16[400,256]{1,0:T(8,128)(2,1)S(1)}) custom-call(bf16[400,1024]{1,0:T(8,128)(2,1)S(1)} %get-tuple-element.37.refs_4_.refs_2_.q_ref, bf16[512,1024]{1,0:T(8,128)(2,1)S(1)} %get-tuple-element.41.m_ref, f32[400,1024]{1,0:T(8,128)S(1)} %get-tuple-element.42.g_ref, ...), custom_call_target="tpu_custom_call" | custom-call | tf_op jit(solution)/shard_map/pallas_call | solution.py:49
  27.5 0.2 collective-permute-done.12.refs_1_
  27.8 1.6 %collective-permute-start.13 = (bf16[208,128]{1,0:T(8,128)(2,1)S(1)}, bf16[208,128]{1,0:T(8,128)(2,1)S(1)}, u32[]{:S(2)}, u32[]{:S(2)}) collective-permute-start(bf16[208,128]{1,0:T(8,128)(2,1)S(1)} %get-tuple-element.55), channel_id=1, source_target_pairs={{0,2},{1,3},{2,0},{3,1},{4,6},{5,7},{6,4},{7,5},{8,10},{9,11},{10,... | collective-permute-start | bytes 159752 | tf_op jit(solution)/shard_map/ppermute | solution.py:290
  29.3 1.5 %collective-permute-start.11 = (bf16[400,512]{1,0:T(8,128)(2,1)S(1)}, bf16[400,512]{1,0:T(8,128)(2,1)S(1)}, u32[]{:S(2)}, u32[]{:S(2)}) collective-permute-start(bf16[400,512]{1,0:T(8,128)(2,1)S(1)} %get-tuple-element.51.refs_2_), channel_id=1, source_target_pairs={{0,4},{4,0},{8,12},{12,8},{16,20},{20,16},{24,28},{28,24},{1,5},{5... | collective-permute-start | bytes 1228808 | tf_op jit(solution)/shard_map/ppermute | solution.py:287
  30.9 1.1 %collective-permute-done.13.refs_1_ = bf16[208,128]{1,0:T(8,128)(2,1)S(1)} collective-permute-done((bf16[208,128]{1,0:T(8,128)(2,1)S(1)}, bf16[208,128]{1,0:T(8,128)(2,1)S(1)}, u32[]{:S(2)}, u32[]{:S(2)}) %collective-permute-start.13) | collective-permute-done | bytes 53280 | tf_op jit(solution)/shard_map/ppermute | solution.py:290
  32.0 0.6 %collective-permute-start.14 = (bf16[208,128]{1,0:T(8,128)(2,1)S(1)}, bf16[208,128]{1,0:T(8,128)(2,1)S(1)}, u32[]{:S(2)}, u32[]{:S(2)}) collective-permute-start(bf16[208,128]{1,0:T(8,128)(2,1)S(1)} %shard_map.158.refs_0_), channel_id=1, source_target_pairs={{0,8},{4,12},{8,0},{12,4},{16,24},{20,28},{24,16},{28,20},{1,9},{5... | collective-permute-start | bytes 159752 | tf_op jit(solution)/shard_map/ppermute | solution.py:287
  32.6 3.6 %collective-permute-done.14.refs_1_ = bf16[208,128]{1,0:T(8,128)(2,1)S(1)} collective-permute-done((bf16[208,128]{1,0:T(8,128)(2,1)S(1)}, bf16[208,128]{1,0:T(8,128)(2,1)S(1)}, u32[]{:S(2)}, u32[]{:S(2)}) %collective-permute-start.14) | collective-permute-done | bytes 53280 | tf_op jit(solution)/shard_map/ppermute | solution.py:287
  36.2 1.5 %collective-permute-start.15 = (bf16[208,128]{1,0:T(8,128)(2,1)S(1)}, bf16[208,128]{1,0:T(8,128)(2,1)S(1)}, u32[]{:S(2)}, u32[]{:S(2)}) collective-permute-start(bf16[208,128]{1,0:T(8,128)(2,1)S(1)} %shard_map.159.refs_0_), channel_id=1, source_target_pairs={{0,16},{4,20},{8,24},{12,28},{16,0},{20,4},{24,8},{28,12},{1,17},{... | collective-permute-start | bytes 159752 | tf_op jit(solution)/shard_map/ppermute | solution.py:287
  37.8 1.5 %collective-permute-start.10 = (bf16[400,128]{1,0:T(8,128)(2,1)S(1)}, bf16[400,128]{1,0:T(8,128)(2,1)S(1)}, u32[]{:S(2)}, u32[]{:S(2)}) collective-permute-start(bf16[400,128]{1,0:T(8,128)(2,1)S(1)} %get-tuple-element.47), channel_id=1, source_target_pairs={{0,2},{1,3},{2,0},{3,1},{4,6},{5,7},{6,4},{7,5},{8,10},{9,11},{10,... | collective-permute-start | bytes 307208 | tf_op jit(solution)/shard_map/ppermute | solution.py:290
  39.3 2.6 %collective-permute-done.15.refs_1_ = bf16[208,128]{1,0:T(8,128)(2,1)S(1)} collective-permute-done((bf16[208,128]{1,0:T(8,128)(2,1)S(1)}, bf16[208,128]{1,0:T(8,128)(2,1)S(1)}, u32[]{:S(2)}, u32[]{:S(2)}) %collective-permute-start.15) | collective-permute-done | bytes 53280 | tf_op jit(solution)/shard_map/ppermute | solution.py:287
  41.9 1.3 %collective-permute-start.20 = (bf16[208,128]{1,0:T(8,128)(2,1)S(1)}, bf16[208,128]{1,0:T(8,128)(2,1)S(1)}, u32[]{:S(2)}, u32[]{:S(2)}) collective-permute-start(bf16[208,128]{1,0:T(8,128)(2,1)S(1)} %shard_map.160.refs_3_.refs_0_), channel_id=1, source_target_pairs={{0,4},{4,0},{8,12},{12,8},{16,20},{20,16},{24,28},{28,24},{1,5},{5... | collective-permute-start | bytes 159752 | tf_op jit(solution)/shard_map/ppermute | solution.py:287
  43.2 0.1 shard_map.161
  43.3 0.1 collective-permute-start.16
  43.4 2.4 %collective-permute-start.17 = (bf16[400,128]{1,0:T(8,128)(2,1)S(1)}, bf16[400,128]{1,0:T(8,128)(2,1)S(1)}, u32[]{:S(2)}, u32[]{:S(2)}) collective-permute-start(bf16[400,128]{1,0:T(8,128)(2,1)S(1)} %get-tuple-element.57), channel_id=1, source_target_pairs={{0,9},{1,10},{2,11},{3,8},{4,13},{5,14},{6,15},{7,12},{8,1},{9,2},... | collective-permute-start | bytes 307208 | tf_op jit(solution)/shard_map/ppermute | solution.py:297
  45.9 0.5 collective-permute-start.18
  46.4 2.3 %collective-permute-start.19 = (bf16[400,128]{1,0:T(8,128)(2,1)S(1)}, bf16[400,128]{1,0:T(8,128)(2,1)S(1)}, u32[]{:S(2)}, u32[]{:S(2)}) collective-permute-start(bf16[400,128]{1,0:T(8,128)(2,1)S(1)} %get-tuple-element.59), channel_id=1, source_target_pairs={{0,25},{1,26},{2,27},{3,24},{4,29},{5,30},{6,31},{7,28},{8,17},{9,... | collective-permute-start | bytes 307208 | tf_op jit(solution)/shard_map/ppermute | solution.py:297
  48.7 1.6 %collective-permute-start.21 = (bf16[208,128]{1,0:T(8,128)(2,1)S(1)}, bf16[208,128]{1,0:T(8,128)(2,1)S(1)}, u32[]{:S(2)}, u32[]{:S(2)}) collective-permute-start(bf16[208,128]{1,0:T(8,128)(2,1)S(1)} %shard_map.163.refs_0_), channel_id=1, source_target_pairs={{0,2},{1,3},{2,0},{3,1},{4,6},{5,7},{6,4},{7,5},{8,10},{9,11},{10,... | collective-permute-start | bytes 159752 | tf_op jit(solution)/shard_map/ppermute | solution.py:290
  50.3 0.8 %shard_map.156 = (f32[400,128]{1,0:T(8,128)}, f32[1,128]{1,0:T(1,128)}) custom-call(f32[400,128]{1,0:T(8,128)S(1)} %get-tuple-element.46.refs_0_, bf16[400,128]{1,0:T(8,128)(2,1)S(1)} %collective-permute-done.10.refs_1_.refs_2_, f32[400,128]{1,0:T(8,128)S(1)} %bitcast.23, f32[1,128]{1,0:T(1,128)S(1)} %bitcast.26), custom_call_target="tpu_custom_call" | custom-call | tf_op jit(solution)/shard_map/pallas_call | solution.py:49
  51.0 2.9 %collective-permute-done.21.refs_1_ = bf16[208,128]{1,0:T(8,128)(2,1)S(1)} collective-permute-done((bf16[208,128]{1,0:T(8,128)(2,1)S(1)}, bf16[208,128]{1,0:T(8,128)(2,1)S(1)}, u32[]{:S(2)}, u32[]{:S(2)}) %collective-permute-start.21) | collective-permute-done | bytes 53280 | tf_op jit(solution)/shard_map/ppermute | solution.py:290
  54.0 0.1 collective-permute-start.22
  54.1 2.6 %collective-permute-done.18.refs_2_ = bf16[400,128]{1,0:T(8,128)(2,1)S(1)} collective-permute-done((bf16[400,128]{1,0:T(8,128)(2,1)S(1)}, bf16[400,128]{1,0:T(8,128)(2,1)S(1)}, u32[]{:S(2)}, u32[]{:S(2)}) %collective-permute-start.18) | collective-permute-done | bytes 102432 | tf_op jit(solution)/shard_map/ppermute | solution.py:297
  56.7 0.8 %shard_map.162 = (f32[400,128]{1,0:T(8,128)}, f32[1,128]{1,0:T(1,128)}) custom-call(bf16[400,128]{1,0:T(8,128)(2,1)S(1)} %collective-permute-done.16.refs_0_, bf16[400,128]{1,0:T(8,128)(2,1)S(1)} %collective-permute-done.17.refs_1_, bf16[400,128]{1,0:T(8,128)(2,1)S(1)} %collective-permute-done.18.refs_2_, ...), custom_call_target="tpu_custom_call" | custom-call | flops 6000000000 | tf_op jit(solution)/shard_map/pallas_call | solution.py:49
  57.5 0.6 %copy-done.8 = f32[1,128]{1,0:T(1,128)S(1)} copy-done((f32[1,128]{1,0:T(1,128)S(1)}, f32[1,128]{1,0:T(1,128)}, u32[]{:S(2)}) %copy-start.8) | copy-done | bytes 536
  58.1 0.9 %shard_map.165 = (f32[400,256]{1,0:T(8,128)}, f32[1,256]{1,0:T(1,128)}) custom-call(bf16[208,128]{1,0:T(8,128)(2,1)S(1)} %shard_map.163.refs_0_, bf16[208,128]{1,0:T(8,128)(2,1)S(1)} %collective-permute-done.21.refs_1_, bf16[416,128]{1,0:T(8,128)(2,1)S(1)} %collective-permute-done.22.refs_2_, f32[400,256]{1,0:T(8,128)S(1)} %bitcast.19, ...), custom_call_target="tpu_custom_call" | custom-call | tf_op jit(solution)/shard_map/pallas_call | solution.py:49
  (40 shorter events, 0.3 us)
Async XLA Ops:
  0.6 0.9 %copy-start.1 = (f32[128,400]{0,1:T(8,128)S(1)}, f32[128,400]{0,1:T(8,128)}, u32[]{:S(2)}) copy-start(f32[128,400]{0,1:T(8,128)} %param.12) | copy-start | bytes 614404
  1.9 12.2 %collective-permute-start.6 = (bf16[400,128]{1,0:T(8,128)(2,1)S(1)}, bf16[400,128]{1,0:T(8,128)(2,1)S(1)}, u32[]{:S(2)}, u32[]{:S(2)}) collective-permute-start(bf16[400,128]{1,0:T(8,128)(2,1)S(1)} %shard_map.146.refs_0_), channel_id=1, source_target_pairs={{0,24},{4,28},{8,16},{12,20},{16,8},{20,12},{24,0},{28,4},{1,25},{... | collective-permute-start | bytes 307208 | tf_op jit(solution)/shard_map/ppermute | solution.py:287
  7.0 8.6 %collective-permute-start.5 = (bf16[400,128]{1,0:T(8,128)(2,1)S(1)}, bf16[400,128]{1,0:T(8,128)(2,1)S(1)}, u32[]{:S(2)}, u32[]{:S(2)}) collective-permute-start(bf16[400,128]{1,0:T(8,128)(2,1)S(1)} %shard_map.146.refs_0_), channel_id=1, source_target_pairs={{0,16},{4,20},{8,24},{12,28},{16,0},{20,4},{24,8},{28,12},{1,17},{... | collective-permute-start | bytes 307208 | tf_op jit(solution)/shard_map/ppermute | solution.py:287
  7.0 8.6 %collective-permute-start.4 = (bf16[400,128]{1,0:T(8,128)(2,1)S(1)}, bf16[400,128]{1,0:T(8,128)(2,1)S(1)}, u32[]{:S(2)}, u32[]{:S(2)}) collective-permute-start(bf16[400,128]{1,0:T(8,128)(2,1)S(1)} %shard_map.146.refs_0_), channel_id=1, source_target_pairs={{0,8},{4,12},{8,0},{12,4},{16,24},{20,28},{24,16},{28,20},{1,9},{5... | collective-permute-start | bytes 307208 | tf_op jit(solution)/shard_map/ppermute | solution.py:287
  7.6 4.7 %collective-permute-start = (bf16[400,128]{1,0:T(8,128)(2,1)S(1)}, bf16[400,128]{1,0:T(8,128)(2,1)S(1)}, u32[]{:S(2)}, u32[]{:S(2)}) collective-permute-start(bf16[400,128]{1,0:T(8,128)(2,1)S(1)} %shard_map.146.refs_0_), channel_id=1, source_target_pairs={{0,4},{4,0},{8,12},{12,8},{16,20},{20,16},{24,28},{28,24},{1,5},{5... | collective-permute-start | bytes 307208 | tf_op jit(solution)/shard_map/ppermute | solution.py:287
  10.1 1.7 %collective-permute-start.1 = (s32[5,1024]{1,0:T(8,128)S(1)}, s32[5,1024]{1,0:T(8,128)S(1)}, u32[]{:S(2)}, u32[]{:S(2)}) collective-permute-start(s32[5,1024]{1,0:T(8,128)S(1)} %pad_add_fusion), channel_id=1, source_target_pairs={{0,3},{1,0},{2,1},{3,2},{4,7},{5,4},{6,5},{7,6},{8,11},{9,8},{10,9... | collective-permute-start | bytes 61448 | tf_op jit(solution)/shard_map/ppermute | solution.py:332
  10.1 0.9 %copy-start.3 = (f32[128,400]{0,1:T(8,128)S(1)}, f32[128,400]{0,1:T(8,128)}, u32[]{:S(2)}) copy-start(f32[128,400]{0,1:T(8,128)} %param.10) | copy-start | bytes 614404
  12.3 5.0 %copy-start.2 = (f32[128,400]{0,1:T(8,128)S(1)}, f32[128,400]{0,1:T(8,128)}, u32[]{:S(2)}) copy-start(f32[128,400]{0,1:T(8,128)} %param.12) | copy-start | bytes 614404
  12.3 4.9 %copy-start.6 = (f32[128]{0:T(128)S(1)}, f32[128]{0:T(128)}, u32[]{:S(2)}) copy-start(f32[128]{0:T(128)} %param.13) | copy-start | bytes 1540
  12.3 6.8 %copy-start = (f32[256,400]{0,1:T(8,128)S(1)}, f32[256,400]{0,1:T(8,128)}, u32[]{:S(2)}) copy-start(f32[256,400]{0,1:T(8,128)} %param.14) | copy-start | bytes 1228804
  12.3 5.8 %collective-permute-start.2 = (bf16[400,128]{1,0:T(8,128)(2,1)S(1)}, bf16[400,128]{1,0:T(8,128)(2,1)S(1)}, u32[]{:S(2)}, u32[]{:S(2)}) collective-permute-start(bf16[400,128]{1,0:T(8,128)(2,1)S(1)} %shard_map.147.refs_0_), channel_id=1, source_target_pairs={{0,2},{1,3},{2,0},{3,1},{4,6},{5,7},{6,4},{7,5},{8,10},{9,11},{10,... | collective-permute-start | bytes 307208 | tf_op jit(solution)/shard_map/ppermute | solution.py:290
  15.7 8.4 %collective-permute-start.7 = (bf16[400,384]{1,0:T(8,128)(2,1)S(1)}, bf16[400,384]{1,0:T(8,128)(2,1)S(1)}, u32[]{:S(2)}, u32[]{:S(2)}) collective-permute-start(bf16[400,384]{1,0:T(8,128)(2,1)S(1)} %shard_map.150.refs_2_), channel_id=1, source_target_pairs={{0,4},{4,0},{8,12},{12,8},{16,20},{20,16},{24,28},{28,24},{1,5},{5... | collective-permute-start | bytes 921608 | tf_op jit(solution)/shard_map/ppermute | solution.py:287
  17.3 6.1 %collective-permute-start.8 = (f32[408,128]{1,0:T(8,128)S(1)}, f32[408,128]{1,0:T(8,128)S(1)}, u32[]{:S(2)}, u32[]{:S(2)}) collective-permute-start(f32[408,128]{1,0:T(8,128)S(1)} %shard_map.152), channel_id=1, source_target_pairs={{0,1},{1,2},{2,3},{3,0},{4,5},{5,6},{6,7},{7,4},{8,9},{9,10},{10,1... | collective-permute-start | bytes 626696 | tf_op jit(solution)/shard_map/ppermute | solution.py:297
  18.1 2.5 %collective-permute-start.3 = (bf16[400,256]{1,0:T(8,128)(2,1)S(1)}, bf16[400,256]{1,0:T(8,128)(2,1)S(1)}, u32[]{:S(2)}, u32[]{:S(2)}) collective-permute-start(bf16[400,256]{1,0:T(8,128)(2,1)S(1)} %pad_maximum_fusion), channel_id=1, source_target_pairs={{0,1},{1,0},{2,3},{3,2},{4,5},{5,4},{6,7},{7,6},{8,9},{9,8},{10,11... | collective-permute-start | bytes 614408 | tf_op jit(solution)/shard_map/ppermute | solution.py:290
  26.4 1.4 %collective-permute-start.12 = (bf16[416,128]{1,0:T(8,128)(2,1)S(1)}, bf16[416,128]{1,0:T(8,128)(2,1)S(1)}, u32[]{:S(2)}, u32[]{:S(2)}) collective-permute-start(bf16[416,128]{1,0:T(8,128)(2,1)S(1)} %get-tuple-element.53), channel_id=1, source_target_pairs={{0,1},{1,0},{2,3},{3,2},{4,5},{5,4},{6,7},{7,6},{8,9},{9,8},{10,11... | collective-permute-start | bytes 319496 | tf_op jit(solution)/shard_map/ppermute | solution.py:290
  27.8 4.2 %collective-permute-start.13 = (bf16[208,128]{1,0:T(8,128)(2,1)S(1)}, bf16[208,128]{1,0:T(8,128)(2,1)S(1)}, u32[]{:S(2)}, u32[]{:S(2)}) collective-permute-start(bf16[208,128]{1,0:T(8,128)(2,1)S(1)} %get-tuple-element.55), channel_id=1, source_target_pairs={{0,2},{1,3},{2,0},{3,1},{4,6},{5,7},{6,4},{7,5},{8,10},{9,11},{10,... | collective-permute-start | bytes 159752 | tf_op jit(solution)/shard_map/ppermute | solution.py:290
  29.3 13.9 %collective-permute-start.11 = (bf16[400,512]{1,0:T(8,128)(2,1)S(1)}, bf16[400,512]{1,0:T(8,128)(2,1)S(1)}, u32[]{:S(2)}, u32[]{:S(2)}) collective-permute-start(bf16[400,512]{1,0:T(8,128)(2,1)S(1)} %get-tuple-element.51.refs_2_), channel_id=1, source_target_pairs={{0,4},{4,0},{8,12},{12,8},{16,20},{20,16},{24,28},{28,24},{1,5},{5... | collective-permute-start | bytes 1228808 | tf_op jit(solution)/shard_map/ppermute | solution.py:287
  30.9 6.9 %collective-permute-start.9 = (bf16[400,256]{1,0:T(8,128)(2,1)S(1)}, bf16[400,256]{1,0:T(8,128)(2,1)S(1)}, u32[]{:S(2)}, u32[]{:S(2)}) collective-permute-start(bf16[400,256]{1,0:T(8,128)(2,1)S(1)} %get-tuple-element.45), channel_id=1, source_target_pairs={{0,1},{1,0},{2,3},{3,2},{4,5},{5,4},{6,7},{7,6},{8,9},{9,8},{10,11... | collective-permute-start | bytes 614408 | tf_op jit(solution)/shard_map/ppermute | solution.py:290
  32.0 4.2 %collective-permute-start.14 = (bf16[208,128]{1,0:T(8,128)(2,1)S(1)}, bf16[208,128]{1,0:T(8,128)(2,1)S(1)}, u32[]{:S(2)}, u32[]{:S(2)}) collective-permute-start(bf16[208,128]{1,0:T(8,128)(2,1)S(1)} %shard_map.158.refs_0_), channel_id=1, source_target_pairs={{0,8},{4,12},{8,0},{12,4},{16,24},{20,28},{24,16},{28,20},{1,9},{5... | collective-permute-start | bytes 159752 | tf_op jit(solution)/shard_map/ppermute | solution.py:287
  36.2 5.7 %collective-permute-start.15 = (bf16[208,128]{1,0:T(8,128)(2,1)S(1)}, bf16[208,128]{1,0:T(8,128)(2,1)S(1)}, u32[]{:S(2)}, u32[]{:S(2)}) collective-permute-start(bf16[208,128]{1,0:T(8,128)(2,1)S(1)} %shard_map.159.refs_0_), channel_id=1, source_target_pairs={{0,16},{4,20},{8,24},{12,28},{16,0},{20,4},{24,8},{28,12},{1,17},{... | collective-permute-start | bytes 159752 | tf_op jit(solution)/shard_map/ppermute | solution.py:287
  37.8 5.4 %collective-permute-start.10 = (bf16[400,128]{1,0:T(8,128)(2,1)S(1)}, bf16[400,128]{1,0:T(8,128)(2,1)S(1)}, u32[]{:S(2)}, u32[]{:S(2)}) collective-permute-start(bf16[400,128]{1,0:T(8,128)(2,1)S(1)} %get-tuple-element.47), channel_id=1, source_target_pairs={{0,2},{1,3},{2,0},{3,1},{4,6},{5,7},{6,4},{7,5},{8,10},{9,11},{10,... | collective-permute-start | bytes 307208 | tf_op jit(solution)/shard_map/ppermute | solution.py:290
  41.9 6.8 %collective-permute-start.20 = (bf16[208,128]{1,0:T(8,128)(2,1)S(1)}, bf16[208,128]{1,0:T(8,128)(2,1)S(1)}, u32[]{:S(2)}, u32[]{:S(2)}) collective-permute-start(bf16[208,128]{1,0:T(8,128)(2,1)S(1)} %shard_map.160.refs_3_.refs_0_), channel_id=1, source_target_pairs={{0,4},{4,0},{8,12},{12,8},{16,20},{20,16},{24,28},{28,24},{1,5},{5... | collective-permute-start | bytes 159752 | tf_op jit(solution)/shard_map/ppermute | solution.py:287
  43.3 10.7 %collective-permute-start.16 = (bf16[400,128]{1,0:T(8,128)(2,1)S(1)}, bf16[400,128]{1,0:T(8,128)(2,1)S(1)}, u32[]{:S(2)}, u32[]{:S(2)}) collective-permute-start(bf16[400,128]{1,0:T(8,128)(2,1)S(1)} %get-tuple-element.56), channel_id=1, source_target_pairs={{0,1},{1,2},{2,3},{3,0},{4,5},{5,6},{6,7},{7,4},{8,9},{9,10},{10,1... | collective-permute-start | bytes 307208 | tf_op jit(solution)/shard_map/ppermute | solution.py:297
  43.4 10.7 %collective-permute-start.17 = (bf16[400,128]{1,0:T(8,128)(2,1)S(1)}, bf16[400,128]{1,0:T(8,128)(2,1)S(1)}, u32[]{:S(2)}, u32[]{:S(2)}) collective-permute-start(bf16[400,128]{1,0:T(8,128)(2,1)S(1)} %get-tuple-element.57), channel_id=1, source_target_pairs={{0,9},{1,10},{2,11},{3,8},{4,13},{5,14},{6,15},{7,12},{8,1},{9,2},... | collective-permute-start | bytes 307208 | tf_op jit(solution)/shard_map/ppermute | solution.py:297
  45.9 10.8 %collective-permute-start.18 = (bf16[400,128]{1,0:T(8,128)(2,1)S(1)}, bf16[400,128]{1,0:T(8,128)(2,1)S(1)}, u32[]{:S(2)}, u32[]{:S(2)}) collective-permute-start(bf16[400,128]{1,0:T(8,128)(2,1)S(1)} %get-tuple-element.58), channel_id=1, source_target_pairs={{0,17},{1,18},{2,19},{3,16},{4,21},{5,22},{6,23},{7,20},{8,25},{9,... | collective-permute-start | bytes 307208 | tf_op jit(solution)/shard_map/ppermute | solution.py:297
  46.4 3.9 %copy-start.4 = (f32[128,400]{0,1:T(8,128)S(1)}, f32[128,400]{0,1:T(8,128)}, u32[]{:S(2)}) copy-start(f32[128,400]{0,1:T(8,128)} %param.10) | copy-start | bytes 614404
  46.4 3.9 %copy-start.7 = (f32[128]{0:T(128)S(1)}, f32[128]{0:T(128)}, u32[]{:S(2)}) copy-start(f32[128]{0:T(128)} %param.11) | copy-start | bytes 1540
  46.4 10.3 %collective-permute-start.19 = (bf16[400,128]{1,0:T(8,128)(2,1)S(1)}, bf16[400,128]{1,0:T(8,128)(2,1)S(1)}, u32[]{:S(2)}, u32[]{:S(2)}) collective-permute-start(bf16[400,128]{1,0:T(8,128)(2,1)S(1)} %get-tuple-element.59), channel_id=1, source_target_pairs={{0,25},{1,26},{2,27},{3,24},{4,29},{5,30},{6,31},{7,28},{8,17},{9,... | collective-permute-start | bytes 307208 | tf_op jit(solution)/shard_map/ppermute | solution.py:297
  48.7 5.3 %collective-permute-start.21 = (bf16[208,128]{1,0:T(8,128)(2,1)S(1)}, bf16[208,128]{1,0:T(8,128)(2,1)S(1)}, u32[]{:S(2)}, u32[]{:S(2)}) collective-permute-start(bf16[208,128]{1,0:T(8,128)(2,1)S(1)} %shard_map.163.refs_0_), channel_id=1, source_target_pairs={{0,2},{1,3},{2,0},{3,1},{4,6},{5,7},{6,4},{7,5},{8,10},{9,11},{10,... | collective-permute-start | bytes 159752 | tf_op jit(solution)/shard_map/ppermute | solution.py:290
  54.0 3.5 %copy-start.5 = (f32[256]{0:T(256)S(1)}, f32[256]{0:T(256)}, u32[]{:S(2)}) copy-start(f32[256]{0:T(256)} %param.15) | copy-start | bytes 3076
  54.0 3.5 %collective-permute-start.22 = (bf16[416,128]{1,0:T(8,128)(2,1)S(1)}, bf16[416,128]{1,0:T(8,128)(2,1)S(1)}, u32[]{:S(2)}, u32[]{:S(2)}) collective-permute-start(bf16[416,128]{1,0:T(8,128)(2,1)S(1)} %shard_map.164), channel_id=1, source_target_pairs={{0,1},{1,0},{2,3},{3,2},{4,5},{5,4},{6,7},{7,6},{8,9},{9,8},{10,11... | collective-permute-start | bytes 319496 | tf_op jit(solution)/shard_map/ppermute | solution.py:290
  57.5 0.7 %copy-start.8 = (f32[1,128]{1,0:T(1,128)S(1)}, f32[1,128]{1,0:T(1,128)}, u32[]{:S(2)}) copy-start(f32[1,128]{1,0:T(1,128)} %get-tuple-element.61.refs_6_) | copy-start | bytes 1540

commit v11 on v10

--- a/solution.py
+++ b/solution.py
@@ -14,7 +14,7 @@
 VMEM_LIMIT = 32 * 1024 * 1024
 LANES = 128
 COST_JOIN = 6e9
-COST_UPDATE = 6e9
+COST_UPDATE = 0
 COST_SUM = 1e9
 
 
@@ -155,7 +155,7 @@
     step = step_of(edges // weight_ref.shape[0])
     for at in range(0, edges, step):
         m_ref[:, at:at + step] = grad_chunk(rows_t, q_ref, weight_ref, ids_ref, 0, at, step)
-    right_ref[...] = dot(q_ref[...], m_ref[...], 1, 1)
+    right_ref[...] = dot(q_ref[...], m_ref[...], 1, 1).astype(BF)
     qg_ref[...] = dot(rows_ref[...], m_ref[...], 1, 0)
 
 
@@ -252,10 +252,9 @@
         refs[-1][k * size:(k + 1) * size, :] = ref[...]
 
 
-def chunk_body(near_ref, got_ref, *block_refs):
-    for k, ref in enumerate(block_refs):
-        cols = slice(k * LANES, (k + 1) * LANES)
-        ref[...] = (near_ref[:, cols] + got_ref[:, cols].astype(F32)).astype(BF)
+def block_body(k, near_ref, got_ref, block_ref):
+    cols = slice(k * LANES, (k + 1) * LANES)
+    block_ref[...] = (near_ref[:, cols].astype(F32) + got_ref[:, cols].astype(F32)).astype(block_ref.dtype)
 
 
 def sum_body(*refs):
@@ -318,27 +317,27 @@
             scratch = [pltpu.VMEM(value.shape, F32), pltpu.SemaphoreType.DMA((parts,))]
             return call(cast_body, one_block, scratch, after=after, place=pl.ANY)(value)
 
-        right_bf = cast(right_t)
-        near = [right_bf] + [swap_left(right_bf, 2 * k) for k in range(1, outer)]
-        other_own = swap_left(right_bf, 1)
-        blocks = shape(width, half - rows, dtype=BF)
-        joined = call(join_body, blocks, flops=COST_JOIN)(*near[1:])
-        other_rest = swap_left(joined, 1)
+        right_bf = right_t.astype(BF)
+        near = [next_column(right_bf, 2 * k) for k in range(outer)]
+        other_own = next_column(right_bf, 1)
 
         ids = [source_ids, target_ids, relation_ids, negative_ids]
         longest = max(i.shape[-1] for i in ids)
         ids = [i.reshape(-1, i.shape[-1]) for i in ids]
         ids = jnp.concatenate([jnp.pad(i, ((0, 0), (0, longest - i.shape[-1]))) for i in ids], axis=0)
-        ids = lax.ppermute(ids, "right", [(i, (i - 1) % n_right) for i in range(n_right)])
-        left_bf = call(join_body, one_block, after=(other_own, ids))(cast(left_t))
-        half_left = [left_bf] + [swap_right(left_bf, 2 * k) for k in range(1, far_right)]
-        sibling_left = swap_right(jnp.concatenate(half_left, axis=1), 1)
         place = jnp.stack([here_r, here_l]).astype(jnp.int32)
         weight, relation_bf, ids = call(
             functools.partial(count_body, far_right, outer, rows, negative_ids.shape[-1]),
             (shape(groups, n_rows, LANES), shape(width, nrel, dtype=BF), shape(*ids.shape, dtype=jnp.int32)),
             here=place,
         )(ids, relation_t)
+
+        blocks = shape(width, half - rows, dtype=BF)
+        joined = call(join_body, blocks, flops=COST_JOIN, after=(weight,))(*near[1:])
+        other_rest = swap_left(joined, 1)
+        left_bf = call(join_body, one_block, after=(other_own, near[0]))(cast(left_t))
+        half_left = [left_bf] + [swap_right(left_bf, 2 * k) for k in range(1, far_right)]
+        sibling_left = swap_right(jnp.concatenate(half_left, axis=1), 1)
         moved = next_column(call(pack_body, shape(width + 8, rows), after=(joined,))(right_t, right_state[None, :]), 0)
 
         s, o, q = call(functools.partial(query_body, far_right), (table_bf, table_bf, table_bf))(
@@ -347,7 +346,7 @@
         part = pltpu.VMEM((width, half), BF)
         right_near, qg_near = call(
             functools.partial(near_body, outer),
-            (shape(width, half), shape(width, edges)),
+            (shape(width, half, dtype=BF), shape(width, edges)),
             [part, pltpu.VMEM((half, edges), BF)],
         )(*near, q, weight, ids)
         tall = nrel // LANES * width
@@ -380,17 +379,26 @@
         )(mine, swap_right(theirs, 1))
         got = [swap_right(p, 2 * (k + 1)) for k, p in enumerate(rest)]
         mine = call(sum_body, piece, flops=COST_SUM)(mine, *got)
-        bit = 2
-        while bit < n_left:
-            mine = call(sum_body, piece, flops=COST_SUM)(mine, swap_left(mine, bit))
-            bit *= 2
-        right_got = swap_left(right_far, 1)
-        blocks = call(chunk_body, (one_block,) * outer, after=(*left_got, mine))(right_near, right_got)
-        right_got = [next_column(block, 2 * k) for k, block in enumerate(blocks)]
-
-        mine = call(sum_body, piece, flops=COST_SUM)(mine, swap_left(mine, 1))
+
+        far_got = swap_left(right_far, 1)
+
+        def block(k, dtype=BF, after=()):
+            body = functools.partial(block_body, k)
+            return call(body, shape(width, rows, dtype=dtype), after=after)(right_near, far_got)
+
+        bits = [1 << b for b in range(1, n_left.bit_length() - 1)] + [1]
+        arrived = {step: [] for step in range(len(bits))}
+        for step, bit in enumerate(bits):
+            after = arrived[0] if step == len(bits) - 1 else ()
+            mine = call(sum_body, piece, flops=COST_SUM, after=after)(mine, swap_left(mine, bit))
+            for k in range(outer - 1, 0, -1):
+                if (outer - 1 - k) * len(bits) // (outer - 1) == step:
+                    arrived[step].append(swap_left(block(k, after=(mine,)), 2 * k))
+        right_got = [block(0, F32)] + [a for step in arrived.values() for a in step]
+
         pieces = [mine] + [swap_right(mine, 2 * k) for k in range(1, far_right)]
-        sibling = swap_right(call(stack_body, shape(far_right * size, LANES, dtype=BF))(*pieces), 1)
+        stacked = call(stack_body, shape(far_right * size, LANES, dtype=BF), after=arrived[1])(*pieces)
+        sibling = swap_right(stacked, 1)
 
         def update(got, table, state, flops=0):
             outs = (shape(width, rows), shape(1, rows))

time: 59.3 us -> 64 us (1.079)
  starting transfers between devices: 26.8 us -> 30.8 us
  other arithmetic: 0.86 us -> 1.81 us
    ppermute x5 -> x6, starting transfers between devices: 5.39 us -> 8.21 us  [next_column(): return lax.ppermute(value, ('left', 'right'), perm)]
    ppermute x9 -> x8, starting transfers between devices: 14 us -> 15.8 us  [swap_left(): return lax.ppermute(value, 'left', [(i, i ^ by) for i in range(n_left)])]
    ppermute x5 -> x6, waiting for transfers between devices: 2.59 us -> 1.05 us  [next_column(): return lax.ppermute(value, ('left', 'right'), perm)]
    ppermute x8, waiting for transfers between devices: 5.02 us -> 6.26 us  [swap_right(): return lax.ppermute(value, 'right', [(i, i ^ by) for i in range(n_right)])]
    convert_element_type x0 -> x1, other arithmetic: none -> 0.94 us  [per_device(): right_bf = right_t.astype(BF)]
    ppermute x9 -> x8, waiting for transfers between devices: 8.97 us -> 9.54 us  [swap_left(): return lax.ppermute(value, 'left', [(i, i ^ by) for i in range(n_left)])]
    pallas_call x21 -> x23, Pallas kernels: 11.1 us -> 10.8 us  [run(): pl.pallas_call(inner, out_shape=out_shape, in_specs=specs, scratch_shapes...]
  transfers between devices with their start and end apart: 23 -> 22, of which waited for: 11 -> 11; matrix products, arithmetic and copies ran while one was open for 1% -> 1% of each run, Pallas kernels for 13% -> 12%
where the time goes in v11:
time: 64 us; the launch traced here: 63.7 us
  starting transfers between devices  30.8 us (48%)
  waiting for transfers between devices  16.9 us (26%)
  Pallas kernels  10.8 us (17%)
  local copies, waits for them, and re-layouts  2.61 us (4%)
  other arithmetic  1.81 us (3%)
  between operations  0.84 us (1%)
    ppermute x8, starting transfers between devices, swap_left(): return lax.ppermute(value, 'left', [(i, i ^ by) for i in range(n_left)])  15.8 us
    pallas_call x23, Pallas kernels, run(): pl.pallas_call(inner, out_shape=out_shape, in_specs=specs, scratch_shapes...  10.8 us
    ppermute x8, waiting for transfers between devices, swap_left(): return lax.ppermute(value, 'left', [(i, i ^ by) for i in range(n_left)])  9.54 us
    ppermute x6, starting transfers between devices, next_column(): return lax.ppermute(value, ('left', 'right'), perm)  8.21 us
    ppermute x8, starting transfers between devices, swap_right(): return lax.ppermute(value, 'right', [(i, i ^ by) for i in range(n_right)])  6.84 us
    ppermute x8, waiting for transfers between devices, swap_right(): return lax.ppermute(value, 'right', [(i, i ^ by) for i in range(n_right)])  6.26 us
    unnamed x18, local copies, waits for them, and re-layouts  2.61 us
  transfers between devices with their start and end apart: 22, of which 11 were waited for; matrix products, arithmetic and copies ran while one was open for 1% of the time, Pallas kernels for 12%

profile of v11, /device:TPU:0, one launch (start us, length us, event | category | flops | bytes accessed | tf_op | source)
XLA Modules:
  0.0 63.7 jit_solution(7846950662133919138)
XLA Ops:
  0.6 0.9 %bitcast_convert_fusion = bf16[400,128]{1,0:T(8,128)(2,1)S(1)} fusion(f32[128,400]{0,1:T(8,128)} %param.12), kind=kLoop, calls=%fused_computation.3 | loop fusion | flops 51200 | bytes 307200 | tf_op jit(solution)/shard_map/convert_element_type | solution.py:320
  1.6 4.5 %collective-permute-start.6 = (bf16[400,128]{1,0:T(8,128)(2,1)S(1)}, bf16[400,128]{1,0:T(8,128)(2,1)S(1)}, u32[]{:S(2)}, u32[]{:S(2)}) collective-permute-start(bf16[400,128]{1,0:T(8,128)(2,1)S(1)} %bitcast_convert_fusion), channel_id=1, source_target_pairs={{0,25},{1,26},{2,27},{3,24},{4,29},{5,30},{6,31},{7,28},{8,17},{9,... | collective-permute-start | bytes 307208 | tf_op jit(solution)/shard_map/ppermute | solution.py:296
  6.1 0.6 %collective-permute-start.5 = (bf16[400,128]{1,0:T(8,128)(2,1)S(1)}, bf16[400,128]{1,0:T(8,128)(2,1)S(1)}, u32[]{:S(2)}, u32[]{:S(2)}) collective-permute-start(bf16[400,128]{1,0:T(8,128)(2,1)S(1)} %bitcast_convert_fusion), channel_id=1, source_target_pairs={{0,17},{1,18},{2,19},{3,16},{4,21},{5,22},{6,23},{7,20},{8,25},{9,... | collective-permute-start | bytes 307208 | tf_op jit(solution)/shard_map/ppermute | solution.py:296
  6.8 1.2 %collective-permute-start.4 = (bf16[400,128]{1,0:T(8,128)(2,1)S(1)}, bf16[400,128]{1,0:T(8,128)(2,1)S(1)}, u32[]{:S(2)}, u32[]{:S(2)}) collective-permute-start(bf16[400,128]{1,0:T(8,128)(2,1)S(1)} %bitcast_convert_fusion), channel_id=1, source_target_pairs={{0,9},{1,10},{2,11},{3,8},{4,13},{5,14},{6,15},{7,12},{8,1},{9,2},... | collective-permute-start | bytes 307208 | tf_op jit(solution)/shard_map/ppermute | solution.py:296
  8.0 1.8 %collective-permute-start = (bf16[400,128]{1,0:T(8,128)(2,1)S(1)}, bf16[400,128]{1,0:T(8,128)(2,1)S(1)}, u32[]{:S(2)}, u32[]{:S(2)}) collective-permute-start(bf16[400,128]{1,0:T(8,128)(2,1)S(1)} %bitcast_convert_fusion), channel_id=1, source_target_pairs={{0,5},{1,6},{2,7},{3,4},{4,1},{5,2},{6,3},{7,0},{8,13},{9,14},{10,... | collective-permute-start | bytes 307208 | tf_op jit(solution)/shard_map/ppermute | solution.py:296
  9.7 0.9 %copy-done.3 = f32[128,400]{0,1:T(8,128)S(1)} copy-done((f32[128,400]{0,1:T(8,128)S(1)}, f32[128,400]{0,1:T(8,128)}, u32[]{:S(2)}) %copy-start.3) | copy-done | bytes 204824
  10.7 0.3 shard_map.145.refs_0_
  11.0 0.8 %pad_add_fusion.ids_ref = s32[5,1024]{1,0:T(8,128)S(1)} fusion(s32[2,1024]{1,0:T(2,128)} %bitcast.28, s32[1,1024]{1,0:T(1,128)} %bitcast.29, s32[1,1024]{1,0:T(1,128)} %bitcast.30, s32[1,1024]{1,0:T(1,128)} %bitcast.31), kind=kLoop, calls=%fused_computation.1 | loop fusion | flops 15360 | bytes 40960 | tf_op jit(solution)/shard_map/concatenate | solution.py:327
  11.7 0.1 pad_add_fusion.1.place_ref
  11.8 1.0 %copy-done = f32[256,400]{0,1:T(8,128)S(1)} copy-done((f32[256,400]{0,1:T(8,128)S(1)}, f32[256,400]{0,1:T(8,128)}, u32[]{:S(2)}) %copy-start) | copy-done | bytes 409624
  12.8 1.6 %shard_map.147 = (f32[2,1024,128]{2,1,0:T(8,128)S(1)}, bf16[400,256]{1,0:T(8,128)(2,1)S(1)}, s32[5,1024]{1,0:T(8,128)S(1)}) custom-call(s32[5,1024]{1,0:T(8,128)S(1)} %pad_add_fusion.ids_ref, f32[400,256]{1,0:T(8,128)S(1)} %bitcast.19, s32[2]{0:T(128)S(1)} %pad_add_fusion.1.place_ref), custom_call_target="tpu_custom_call" | custom-call | tf_op jit(solution)/shard_map/pallas_call | solution.py:49
  14.4 0.8 %collective-permute-done.refs_1_.refs_0_ = bf16[400,128]{1,0:T(8,128)(2,1)S(1)} collective-permute-done((bf16[400,128]{1,0:T(8,128)(2,1)S(1)}, bf16[400,128]{1,0:T(8,128)(2,1)S(1)}, u32[]{:S(2)}, u32[]{:S(2)}) %collective-permute-start) | collective-permute-done | bytes 102432 | tf_op jit(solution)/shard_map/ppermute | solution.py:296
  15.1 1.2 %collective-permute-start.2 = (bf16[400,128]{1,0:T(8,128)(2,1)S(1)}, bf16[400,128]{1,0:T(8,128)(2,1)S(1)}, u32[]{:S(2)}, u32[]{:S(2)}) collective-permute-start(bf16[400,128]{1,0:T(8,128)(2,1)S(1)} %shard_map.146.refs_0_), channel_id=1, source_target_pairs={{0,2},{1,3},{2,0},{3,1},{4,6},{5,7},{6,4},{7,5},{8,10},{9,11},{10,... | collective-permute-start | bytes 307208 | tf_op jit(solution)/shard_map/ppermute | solution.py:289
  16.3 0.3 collective-permute-done.5.refs_1_.refs_2_
  16.6 0.1 shard_map.149.refs_2_
  16.7 1.6 %collective-permute-start.7 = (bf16[400,384]{1,0:T(8,128)(2,1)S(1)}, bf16[400,384]{1,0:T(8,128)(2,1)S(1)}, u32[]{:S(2)}, u32[]{:S(2)}) collective-permute-start(bf16[400,384]{1,0:T(8,128)(2,1)S(1)} %shard_map.149.refs_2_), channel_id=1, source_target_pairs={{0,4},{4,0},{8,12},{12,8},{16,20},{20,16},{24,28},{28,24},{1,5},{5... | collective-permute-start | bytes 921608 | tf_op jit(solution)/shard_map/ppermute | solution.py:286
  18.3 0.1 collective-permute-start.8
  18.3 1.9 %collective-permute-done.2.refs_1_ = bf16[400,128]{1,0:T(8,128)(2,1)S(1)} collective-permute-done((bf16[400,128]{1,0:T(8,128)(2,1)S(1)}, bf16[400,128]{1,0:T(8,128)(2,1)S(1)}, u32[]{:S(2)}, u32[]{:S(2)}) %collective-permute-start.2) | collective-permute-done | bytes 102432 | tf_op jit(solution)/shard_map/ppermute | solution.py:289
  20.3 0.1 collective-permute-start.3
  20.4 1.4 %collective-permute-done.3.refs_2_ = bf16[400,256]{1,0:T(8,128)(2,1)S(1)} collective-permute-done((bf16[400,256]{1,0:T(8,128)(2,1)S(1)}, bf16[400,256]{1,0:T(8,128)(2,1)S(1)}, u32[]{:S(2)}, u32[]{:S(2)}) %collective-permute-start.3) | collective-permute-done | bytes 204832 | tf_op jit(solution)/shard_map/ppermute | solution.py:289
  21.8 0.9 %shard_map.148 = (bf16[400,1024]{1,0:T(8,128)(2,1)S(1)}, bf16[400,1024]{1,0:T(8,128)(2,1)S(1)}, bf16[400,1024]{1,0:T(8,128)(2,1)S(1)}) custom-call(bf16[400,128]{1,0:T(8,128)(2,1)S(1)} %shard_map.146.refs_0_, bf16[400,128]{1,0:T(8,128)(2,1)S(1)} %collective-permute-done.2.refs_1_, bf16[400,256]{1,0:T(8,128)(2,1)S(1)} %collective-permute-done.3.refs_2_, ...), custom_call_target="tpu_custom_call" | custom-call | tf_op jit(solution)/shard_map/pallas_call | solution.py:49
  22.7 1.8 %shard_map.150 = (bf16[400,512]{1,0:T(8,128)(2,1)S(1)}, f32[400,1024]{1,0:T(8,128)S(1)}) custom-call(bf16[400,128]{1,0:T(8,128)(2,1)S(1)} %collective-permute-done.1.refs_2_.refs_0_, bf16[400,128]{1,0:T(8,128)(2,1)S(1)} %collective-permute-done.4.refs_0_.refs_1_, bf16[400,128]{1,0:T(8,128)(2,1)S(1)} %collective-permute-done.5.refs_1_.refs_2_, ...), custom_call_target="tpu_custom_call" | custom-call | tf_op jit(solution)/shard_map/pallas_call | solution.py:49
  24.6 0.5 collective-permute-done.7.refs_1_
  25.1 2.3 %shard_map.152 = (bf16[512,1024]{1,0:T(8,128)(2,1)S(1)}, f32[400,1024]{1,0:T(8,128)S(1)}, f32[416,128]{1,0:T(8,128)S(1)}, bf16[416,128]{1,0:T(8,128)(2,1)S(1)}) custom-call(bf16[400,128]{1,0:T(8,128)(2,1)S(1)} %collective-permute-done.refs_1_.refs_0_, bf16[400,384]{1,0:T(8,128)(2,1)S(1)} %collective-permute-done.7.refs_1_, ...), custom_call_target="tpu_custom_call" | custom-call | tf_op jit(solution)/shard_map/pallas_call | solution.py:49
  27.4 0.1 collective-permute-start.12
  27.5 1.1 %shard_map.153 = (bf16[400,512]{1,0:T(8,128)(2,1)S(1)}, f32[400,256]{1,0:T(8,128)S(1)}, bf16[400,256]{1,0:T(8,128)(2,1)S(1)}) custom-call(bf16[400,1024]{1,0:T(8,128)(2,1)S(1)} %get-tuple-element.33.refs_4_.refs_2_.q_ref, bf16[512,1024]{1,0:T(8,128)(2,1)S(1)} %get-tuple-element.37.m_ref, f32[400,1024]{1,0:T(8,128)S(1)} %get-tuple-element.38.g_ref, ...), custom_call_target="tpu_custom_call" | custom-call | tf_op jit(solution)/shard_map/pallas_call | solution.py:49
  28.5 1.1 %collective-permute-start.11 = (bf16[400,512]{1,0:T(8,128)(2,1)S(1)}, bf16[400,512]{1,0:T(8,128)(2,1)S(1)}, u32[]{:S(2)}, u32[]{:S(2)}) collective-permute-start(bf16[400,512]{1,0:T(8,128)(2,1)S(1)} %get-tuple-element.47.refs_2_), channel_id=1, source_target_pairs={{0,4},{4,0},{8,12},{12,8},{16,20},{20,16},{24,28},{28,24},{1,5},{5... | collective-permute-start | bytes 1228808 | tf_op jit(solution)/shard_map/ppermute | solution.py:286
  29.7 2.2 %collective-permute-start.13 = (bf16[208,128]{1,0:T(8,128)(2,1)S(1)}, bf16[208,128]{1,0:T(8,128)(2,1)S(1)}, u32[]{:S(2)}, u32[]{:S(2)}) collective-permute-start(bf16[208,128]{1,0:T(8,128)(2,1)S(1)} %get-tuple-element.51), channel_id=1, source_target_pairs={{0,2},{1,3},{2,0},{3,1},{4,6},{5,7},{6,4},{7,5},{8,10},{9,11},{10,... | collective-permute-start | bytes 159752 | tf_op jit(solution)/shard_map/ppermute | solution.py:289
  31.9 2.2 %collective-permute-done.13.refs_1_ = bf16[208,128]{1,0:T(8,128)(2,1)S(1)} collective-permute-done((bf16[208,128]{1,0:T(8,128)(2,1)S(1)}, bf16[208,128]{1,0:T(8,128)(2,1)S(1)}, u32[]{:S(2)}, u32[]{:S(2)}) %collective-permute-start.13) | collective-permute-done | bytes 53280 | tf_op jit(solution)/shard_map/ppermute | solution.py:289
  34.1 1.2 %collective-permute-start.14 = (bf16[208,128]{1,0:T(8,128)(2,1)S(1)}, bf16[208,128]{1,0:T(8,128)(2,1)S(1)}, u32[]{:S(2)}, u32[]{:S(2)}) collective-permute-start(bf16[208,128]{1,0:T(8,128)(2,1)S(1)} %shard_map.158.refs_0_), channel_id=1, source_target_pairs={{0,8},{4,12},{8,0},{12,4},{16,24},{20,28},{24,16},{28,20},{1,9},{5... | collective-permute-start | bytes 159752 | tf_op jit(solution)/shard_map/ppermute | solution.py:286
  35.4 3.0 %collective-permute-done.14.refs_1_ = bf16[208,128]{1,0:T(8,128)(2,1)S(1)} collective-permute-done((bf16[208,128]{1,0:T(8,128)(2,1)S(1)}, bf16[208,128]{1,0:T(8,128)(2,1)S(1)}, u32[]{:S(2)}, u32[]{:S(2)}) %collective-permute-start.14) | collective-permute-done | bytes 53280 | tf_op jit(solution)/shard_map/ppermute | solution.py:286
  38.3 2.1 %collective-permute-start.16 = (bf16[208,128]{1,0:T(8,128)(2,1)S(1)}, bf16[208,128]{1,0:T(8,128)(2,1)S(1)}, u32[]{:S(2)}, u32[]{:S(2)}) collective-permute-start(bf16[208,128]{1,0:T(8,128)(2,1)S(1)} %shard_map.159.refs_2_.refs_0_), channel_id=1, source_target_pairs={{0,16},{4,20},{8,24},{12,28},{16,0},{20,4},{24,8},{28,12},{1,17},{... | collective-permute-start | bytes 159752 | tf_op jit(solution)/shard_map/ppermute | solution.py:286
  40.5 3.7 %collective-permute-start.15 = (bf16[400,128]{1,0:T(8,128)(2,1)S(1)}, bf16[400,128]{1,0:T(8,128)(2,1)S(1)}, u32[]{:S(2)}, u32[]{:S(2)}) collective-permute-start(bf16[400,128]{1,0:T(8,128)(2,1)S(1)} %shard_map.160), channel_id=1, source_target_pairs={{0,24},{4,28},{8,16},{12,20},{16,8},{20,12},{24,0},{28,4},{1,25},{... | collective-permute-start | bytes 307208 | tf_op jit(solution)/shard_map/ppermute | solution.py:286
  44.2 0.6 collective-permute-start.18
  44.8 2.5 %collective-permute-start.17 = (bf16[400,128]{1,0:T(8,128)(2,1)S(1)}, bf16[400,128]{1,0:T(8,128)(2,1)S(1)}, u32[]{:S(2)}, u32[]{:S(2)}) collective-permute-start(bf16[400,128]{1,0:T(8,128)(2,1)S(1)} %shard_map.162), channel_id=1, source_target_pairs={{0,16},{4,20},{8,24},{12,28},{16,0},{20,4},{24,8},{28,12},{1,17},{... | collective-permute-start | bytes 307208 | tf_op jit(solution)/shard_map/ppermute | solution.py:286
  47.3 1.1 %collective-permute-done.18.refs_1_ = bf16[208,128]{1,0:T(8,128)(2,1)S(1)} collective-permute-done((bf16[208,128]{1,0:T(8,128)(2,1)S(1)}, bf16[208,128]{1,0:T(8,128)(2,1)S(1)}, u32[]{:S(2)}, u32[]{:S(2)}) %collective-permute-start.18) | collective-permute-done | bytes 53280 | tf_op jit(solution)/shard_map/ppermute | solution.py:286
  48.4 1.7 %collective-permute-start.20 = (bf16[208,128]{1,0:T(8,128)(2,1)S(1)}, bf16[208,128]{1,0:T(8,128)(2,1)S(1)}, u32[]{:S(2)}, u32[]{:S(2)}) collective-permute-start(bf16[208,128]{1,0:T(8,128)(2,1)S(1)} %shard_map.163.refs_2_.refs_0_), channel_id=1, source_target_pairs={{0,2},{1,3},{2,0},{3,1},{4,6},{5,7},{6,4},{7,5},{8,10},{9,11},{10,... | collective-permute-start | bytes 159752 | tf_op jit(solution)/shard_map/ppermute | solution.py:289
  50.1 3.1 %collective-permute-done.17.refs_2_ = bf16[400,128]{1,0:T(8,128)(2,1)S(1)} collective-permute-done((bf16[400,128]{1,0:T(8,128)(2,1)S(1)}, bf16[400,128]{1,0:T(8,128)(2,1)S(1)}, u32[]{:S(2)}, u32[]{:S(2)}) %collective-permute-start.17) | collective-permute-done | bytes 102432 | tf_op jit(solution)/shard_map/ppermute | solution.py:286
  53.3 0.1 collective-permute-start.21
  53.3 0.1 shard_map.154
  53.4 1.6 %collective-permute-start.10 = (bf16[400,128]{1,0:T(8,128)(2,1)S(1)}, bf16[400,128]{1,0:T(8,128)(2,1)S(1)}, u32[]{:S(2)}, u32[]{:S(2)}) collective-permute-start(bf16[400,128]{1,0:T(8,128)(2,1)S(1)} %get-tuple-element.43), channel_id=1, source_target_pairs={{0,2},{1,3},{2,0},{3,1},{4,6},{5,7},{6,4},{7,5},{8,10},{9,11},{10,... | collective-permute-start | bytes 307208 | tf_op jit(solution)/shard_map/ppermute | solution.py:289
  55.1 3.0 %collective-permute-start.19 = (bf16[400,128]{1,0:T(8,128)(2,1)S(1)}, bf16[400,128]{1,0:T(8,128)(2,1)S(1)}, u32[]{:S(2)}, u32[]{:S(2)}) collective-permute-start(bf16[400,128]{1,0:T(8,128)(2,1)S(1)} %shard_map.164), channel_id=1, source_target_pairs={{0,8},{4,12},{8,0},{12,4},{16,24},{20,28},{24,16},{28,20},{1,9},{5... | collective-permute-start | bytes 307208 | tf_op jit(solution)/shard_map/ppermute | solution.py:286
  58.1 0.7 %collective-permute-done.10.refs_1_ = bf16[400,128]{1,0:T(8,128)(2,1)S(1)} collective-permute-done((bf16[400,128]{1,0:T(8,128)(2,1)S(1)}, bf16[400,128]{1,0:T(8,128)(2,1)S(1)}, u32[]{:S(2)}, u32[]{:S(2)}) %collective-permute-start.10) | collective-permute-done | bytes 102432 | tf_op jit(solution)/shard_map/ppermute | solution.py:289
  58.8 0.8 %shard_map.155 = (f32[400,128]{1,0:T(8,128)}, f32[1,128]{1,0:T(1,128)}) custom-call(f32[400,128]{1,0:T(8,128)S(1)} %get-tuple-element.42.refs_0_, bf16[400,128]{1,0:T(8,128)(2,1)S(1)} %collective-permute-done.10.refs_1_, f32[400,128]{1,0:T(8,128)S(1)} %bitcast.23, f32[1,128]{1,0:T(1,128)S(1)} %bitcast.26), custom_call_target="tpu_custom_call" | custom-call | tf_op jit(solution)/shard_map/pallas_call | solution.py:49
  59.6 1.8 %collective-permute-done.19.refs_3_ = bf16[400,128]{1,0:T(8,128)(2,1)S(1)} collective-permute-done((bf16[400,128]{1,0:T(8,128)(2,1)S(1)}, bf16[400,128]{1,0:T(8,128)(2,1)S(1)}, u32[]{:S(2)}, u32[]{:S(2)}) %collective-permute-start.19) | collective-permute-done | bytes 102432 | tf_op jit(solution)/shard_map/ppermute | solution.py:286
  61.4 0.8 %shard_map.165 = (f32[400,128]{1,0:T(8,128)}, f32[1,128]{1,0:T(1,128)}) custom-call(f32[400,128]{1,0:T(8,128)S(1)} %shard_map.156.refs_0_, bf16[400,128]{1,0:T(8,128)(2,1)S(1)} %collective-permute-done.15.refs_2_.refs_1_, bf16[400,128]{1,0:T(8,128)(2,1)S(1)} %collective-permute-done.17.refs_2_, bf16[400,128]{1,0:T(8,128)(2,1)S(1)} %collective-permute-done.19.refs_3_, ...), custom_call_target="tpu_custom_call" | custom-call | tf_op jit(solution)/shard_map/pallas_call | solution.py:49
  62.2 0.6 %copy-done.8 = f32[1,128]{1,0:T(1,128)S(1)} copy-done((f32[1,128]{1,0:T(1,128)S(1)}, f32[1,128]{1,0:T(1,128)}, u32[]{:S(2)}) %copy-start.8) | copy-done | bytes 536
  62.8 0.9 %shard_map.167 = (f32[400,256]{1,0:T(8,128)}, f32[1,256]{1,0:T(1,128)}) custom-call(bf16[208,128]{1,0:T(8,128)(2,1)S(1)} %shard_map.163.refs_2_.refs_0_, bf16[208,128]{1,0:T(8,128)(2,1)S(1)} %collective-permute-done.20.refs_1_, bf16[416,128]{1,0:T(8,128)(2,1)S(1)} %collective-permute-done.21.refs_2_, f32[400,256]{1,0:T(8,128)S(1)} %bitcast.20, ...), custom_call_target="tpu_custom_call" | custom-call | tf_op jit(solution)/shard_map/pallas_call | solution.py:49
  (41 shorter events, 0.4 us)
Async XLA Ops:
  1.6 14.7 %collective-permute-start.6 = (bf16[400,128]{1,0:T(8,128)(2,1)S(1)}, bf16[400,128]{1,0:T(8,128)(2,1)S(1)}, u32[]{:S(2)}, u32[]{:S(2)}) collective-permute-start(bf16[400,128]{1,0:T(8,128)(2,1)S(1)} %bitcast_convert_fusion), channel_id=1, source_target_pairs={{0,25},{1,26},{2,27},{3,24},{4,29},{5,30},{6,31},{7,28},{8,17},{9,... | collective-permute-start | bytes 307208 | tf_op jit(solution)/shard_map/ppermute | solution.py:296
  6.1 10.5 %collective-permute-start.5 = (bf16[400,128]{1,0:T(8,128)(2,1)S(1)}, bf16[400,128]{1,0:T(8,128)(2,1)S(1)}, u32[]{:S(2)}, u32[]{:S(2)}) collective-permute-start(bf16[400,128]{1,0:T(8,128)(2,1)S(1)} %bitcast_convert_fusion), channel_id=1, source_target_pairs={{0,17},{1,18},{2,19},{3,16},{4,21},{5,22},{6,23},{7,20},{8,25},{9,... | collective-permute-start | bytes 307208 | tf_op jit(solution)/shard_map/ppermute | solution.py:296
  6.8 9.8 %collective-permute-start.4 = (bf16[400,128]{1,0:T(8,128)(2,1)S(1)}, bf16[400,128]{1,0:T(8,128)(2,1)S(1)}, u32[]{:S(2)}, u32[]{:S(2)}) collective-permute-start(bf16[400,128]{1,0:T(8,128)(2,1)S(1)} %bitcast_convert_fusion), channel_id=1, source_target_pairs={{0,9},{1,10},{2,11},{3,8},{4,13},{5,14},{6,15},{7,12},{8,1},{9,2},... | collective-permute-start | bytes 307208 | tf_op jit(solution)/shard_map/ppermute | solution.py:296
  8.0 6.4 %collective-permute-start.1 = (bf16[400,128]{1,0:T(8,128)(2,1)S(1)}, bf16[400,128]{1,0:T(8,128)(2,1)S(1)}, u32[]{:S(2)}, u32[]{:S(2)}) collective-permute-start(bf16[400,128]{1,0:T(8,128)(2,1)S(1)} %bitcast_convert_fusion), channel_id=1, source_target_pairs={{0,1},{1,2},{2,3},{3,0},{4,5},{5,6},{6,7},{7,4},{8,9},{9,10},{10,1... | collective-permute-start | bytes 307208 | tf_op jit(solution)/shard_map/ppermute | solution.py:296
  8.0 7.2 %collective-permute-start = (bf16[400,128]{1,0:T(8,128)(2,1)S(1)}, bf16[400,128]{1,0:T(8,128)(2,1)S(1)}, u32[]{:S(2)}, u32[]{:S(2)}) collective-permute-start(bf16[400,128]{1,0:T(8,128)(2,1)S(1)} %bitcast_convert_fusion), channel_id=1, source_target_pairs={{0,5},{1,6},{2,7},{3,4},{4,1},{5,2},{6,3},{7,0},{8,13},{9,14},{10,... | collective-permute-start | bytes 307208 | tf_op jit(solution)/shard_map/ppermute | solution.py:296
  9.7 0.9 %copy-start.3 = (f32[128,400]{0,1:T(8,128)S(1)}, f32[128,400]{0,1:T(8,128)}, u32[]{:S(2)}) copy-start(f32[128,400]{0,1:T(8,128)} %param.10) | copy-start | bytes 614404
  11.8 1.0 %copy-start = (f32[256,400]{0,1:T(8,128)S(1)}, f32[256,400]{0,1:T(8,128)}, u32[]{:S(2)}) copy-start(f32[256,400]{0,1:T(8,128)} %param.14) | copy-start | bytes 1228804
  15.1 5.1 %collective-permute-start.2 = (bf16[400,128]{1,0:T(8,128)(2,1)S(1)}, bf16[400,128]{1,0:T(8,128)(2,1)S(1)}, u32[]{:S(2)}, u32[]{:S(2)}) collective-permute-start(bf16[400,128]{1,0:T(8,128)(2,1)S(1)} %shard_map.146.refs_0_), channel_id=1, source_target_pairs={{0,2},{1,3},{2,0},{3,1},{4,6},{5,7},{6,4},{7,5},{8,10},{9,11},{10,... | collective-permute-start | bytes 307208 | tf_op jit(solution)/shard_map/ppermute | solution.py:289
  16.6 1.7 %copy-start.2 = (f32[128,400]{0,1:T(8,128)S(1)}, f32[128,400]{0,1:T(8,128)}, u32[]{:S(2)}) copy-start(f32[128,400]{0,1:T(8,128)} %param.12) | copy-start | bytes 614404
  16.6 1.7 %copy-start.6 = (f32[128]{0:T(128)S(1)}, f32[128]{0:T(128)}, u32[]{:S(2)}) copy-start(f32[128]{0:T(128)} %param.13) | copy-start | bytes 1540
  16.7 8.4 %collective-permute-start.7 = (bf16[400,384]{1,0:T(8,128)(2,1)S(1)}, bf16[400,384]{1,0:T(8,128)(2,1)S(1)}, u32[]{:S(2)}, u32[]{:S(2)}) collective-permute-start(bf16[400,384]{1,0:T(8,128)(2,1)S(1)} %shard_map.149.refs_2_), channel_id=1, source_target_pairs={{0,4},{4,0},{8,12},{12,8},{16,20},{20,16},{24,28},{28,24},{1,5},{5... | collective-permute-start | bytes 921608 | tf_op jit(solution)/shard_map/ppermute | solution.py:286
  18.3 6.3 %collective-permute-start.8 = (f32[408,128]{1,0:T(8,128)S(1)}, f32[408,128]{1,0:T(8,128)S(1)}, u32[]{:S(2)}, u32[]{:S(2)}) collective-permute-start(f32[408,128]{1,0:T(8,128)S(1)} %shard_map.151), channel_id=1, source_target_pairs={{0,1},{1,2},{2,3},{3,0},{4,5},{5,6},{6,7},{7,4},{8,9},{9,10},{10,1... | collective-permute-start | bytes 626696 | tf_op jit(solution)/shard_map/ppermute | solution.py:296
  20.3 1.5 %collective-permute-start.3 = (bf16[400,256]{1,0:T(8,128)(2,1)S(1)}, bf16[400,256]{1,0:T(8,128)(2,1)S(1)}, u32[]{:S(2)}, u32[]{:S(2)}) collective-permute-start(bf16[400,256]{1,0:T(8,128)(2,1)S(1)} %pad_maximum_fusion), channel_id=1, source_target_pairs={{0,1},{1,0},{2,3},{3,2},{4,5},{5,4},{6,7},{7,6},{8,9},{9,8},{10,11... | collective-permute-start | bytes 614408 | tf_op jit(solution)/shard_map/ppermute | solution.py:289
  27.4 2.3 %collective-permute-start.12 = (bf16[416,128]{1,0:T(8,128)(2,1)S(1)}, bf16[416,128]{1,0:T(8,128)(2,1)S(1)}, u32[]{:S(2)}, u32[]{:S(2)}) collective-permute-start(bf16[416,128]{1,0:T(8,128)(2,1)S(1)} %get-tuple-element.49), channel_id=1, source_target_pairs={{0,1},{1,0},{2,3},{3,2},{4,5},{5,4},{6,7},{7,6},{8,9},{9,8},{10,11... | collective-permute-start | bytes 319496 | tf_op jit(solution)/shard_map/ppermute | solution.py:289
  28.5 11.9 %collective-permute-start.11 = (bf16[400,512]{1,0:T(8,128)(2,1)S(1)}, bf16[400,512]{1,0:T(8,128)(2,1)S(1)}, u32[]{:S(2)}, u32[]{:S(2)}) collective-permute-start(bf16[400,512]{1,0:T(8,128)(2,1)S(1)} %get-tuple-element.47.refs_2_), channel_id=1, source_target_pairs={{0,4},{4,0},{8,12},{12,8},{16,20},{20,16},{24,28},{28,24},{1,5},{5... | collective-permute-start | bytes 1228808 | tf_op jit(solution)/shard_map/ppermute | solution.py:286
  29.7 4.4 %collective-permute-start.13 = (bf16[208,128]{1,0:T(8,128)(2,1)S(1)}, bf16[208,128]{1,0:T(8,128)(2,1)S(1)}, u32[]{:S(2)}, u32[]{:S(2)}) collective-permute-start(bf16[208,128]{1,0:T(8,128)(2,1)S(1)} %get-tuple-element.51), channel_id=1, source_target_pairs={{0,2},{1,3},{2,0},{3,1},{4,6},{5,7},{6,4},{7,5},{8,10},{9,11},{10,... | collective-permute-start | bytes 159752 | tf_op jit(solution)/shard_map/ppermute | solution.py:289
  34.1 4.2 %collective-permute-start.14 = (bf16[208,128]{1,0:T(8,128)(2,1)S(1)}, bf16[208,128]{1,0:T(8,128)(2,1)S(1)}, u32[]{:S(2)}, u32[]{:S(2)}) collective-permute-start(bf16[208,128]{1,0:T(8,128)(2,1)S(1)} %shard_map.158.refs_0_), channel_id=1, source_target_pairs={{0,8},{4,12},{8,0},{12,4},{16,24},{20,28},{24,16},{28,20},{1,9},{5... | collective-permute-start | bytes 159752 | tf_op jit(solution)/shard_map/ppermute | solution.py:286
  38.3 5.8 %collective-permute-start.16 = (bf16[208,128]{1,0:T(8,128)(2,1)S(1)}, bf16[208,128]{1,0:T(8,128)(2,1)S(1)}, u32[]{:S(2)}, u32[]{:S(2)}) collective-permute-start(bf16[208,128]{1,0:T(8,128)(2,1)S(1)} %shard_map.159.refs_2_.refs_0_), channel_id=1, source_target_pairs={{0,16},{4,20},{8,24},{12,28},{16,0},{20,4},{24,8},{28,12},{1,17},{... | collective-permute-start | bytes 159752 | tf_op jit(solution)/shard_map/ppermute | solution.py:286
  40.4 12.9 %collective-permute-start.9 = (bf16[400,256]{1,0:T(8,128)(2,1)S(1)}, bf16[400,256]{1,0:T(8,128)(2,1)S(1)}, u32[]{:S(2)}, u32[]{:S(2)}) collective-permute-start(bf16[400,256]{1,0:T(8,128)(2,1)S(1)} %get-tuple-element.41), channel_id=1, source_target_pairs={{0,1},{1,0},{2,3},{3,2},{4,5},{5,4},{6,7},{7,6},{8,9},{9,8},{10,11... | collective-permute-start | bytes 614408 | tf_op jit(solution)/shard_map/ppermute | solution.py:289
  40.5 7.9 %collective-permute-start.15 = (bf16[400,128]{1,0:T(8,128)(2,1)S(1)}, bf16[400,128]{1,0:T(8,128)(2,1)S(1)}, u32[]{:S(2)}, u32[]{:S(2)}) collective-permute-start(bf16[400,128]{1,0:T(8,128)(2,1)S(1)} %shard_map.160), channel_id=1, source_target_pairs={{0,24},{4,28},{8,16},{12,20},{16,8},{20,12},{24,0},{28,4},{1,25},{... | collective-permute-start | bytes 307208 | tf_op jit(solution)/shard_map/ppermute | solution.py:286
  44.2 4.2 %collective-permute-start.18 = (bf16[208,128]{1,0:T(8,128)(2,1)S(1)}, bf16[208,128]{1,0:T(8,128)(2,1)S(1)}, u32[]{:S(2)}, u32[]{:S(2)}) collective-permute-start(bf16[208,128]{1,0:T(8,128)(2,1)S(1)} %shard_map.161.refs_2_.refs_0_), channel_id=1, source_target_pairs={{0,4},{4,0},{8,12},{12,8},{16,20},{20,16},{24,28},{28,24},{1,5},{5... | collective-permute-start | bytes 159752 | tf_op jit(solution)/shard_map/ppermute | solution.py:286
  44.8 8.4 %collective-permute-start.17 = (bf16[400,128]{1,0:T(8,128)(2,1)S(1)}, bf16[400,128]{1,0:T(8,128)(2,1)S(1)}, u32[]{:S(2)}, u32[]{:S(2)}) collective-permute-start(bf16[400,128]{1,0:T(8,128)(2,1)S(1)} %shard_map.162), channel_id=1, source_target_pairs={{0,16},{4,20},{8,24},{12,28},{16,0},{20,4},{24,8},{28,12},{1,17},{... | collective-permute-start | bytes 307208 | tf_op jit(solution)/shard_map/ppermute | solution.py:286
  48.4 10.3 %copy-start.4 = (f32[128,400]{0,1:T(8,128)S(1)}, f32[128,400]{0,1:T(8,128)}, u32[]{:S(2)}) copy-start(f32[128,400]{0,1:T(8,128)} %param.10) | copy-start | bytes 614404
  48.4 10.3 %copy-start.7 = (f32[128]{0:T(128)S(1)}, f32[128]{0:T(128)}, u32[]{:S(2)}) copy-start(f32[128]{0:T(128)} %param.11) | copy-start | bytes 1540
  48.4 4.8 %collective-permute-start.20 = (bf16[208,128]{1,0:T(8,128)(2,1)S(1)}, bf16[208,128]{1,0:T(8,128)(2,1)S(1)}, u32[]{:S(2)}, u32[]{:S(2)}) collective-permute-start(bf16[208,128]{1,0:T(8,128)(2,1)S(1)} %shard_map.163.refs_2_.refs_0_), channel_id=1, source_target_pairs={{0,2},{1,3},{2,0},{3,1},{4,6},{5,7},{6,4},{7,5},{8,10},{9,11},{10,... | collective-permute-start | bytes 159752 | tf_op jit(solution)/shard_map/ppermute | solution.py:289
  53.3 8.9 %collective-permute-start.21 = (bf16[416,128]{1,0:T(8,128)(2,1)S(1)}, bf16[416,128]{1,0:T(8,128)(2,1)S(1)}, u32[]{:S(2)}, u32[]{:S(2)}) collective-permute-start(bf16[416,128]{1,0:T(8,128)(2,1)S(1)} %shard_map.166), channel_id=1, source_target_pairs={{0,1},{1,0},{2,3},{3,2},{4,5},{5,4},{6,7},{7,6},{8,9},{9,8},{10,11... | collective-permute-start | bytes 319496 | tf_op jit(solution)/shard_map/ppermute | solution.py:289
  53.4 8.8 %copy-start.1 = (f32[256,400]{0,1:T(8,128)S(1)}, f32[256,400]{0,1:T(8,128)}, u32[]{:S(2)}) copy-start(f32[256,400]{0,1:T(8,128)} %param.14) | copy-start | bytes 1228804
  53.4 8.7 %copy-start.5 = (f32[256]{0:T(256)S(1)}, f32[256]{0:T(256)}, u32[]{:S(2)}) copy-start(f32[256]{0:T(256)} %param.15) | copy-start | bytes 3076
  53.4 5.3 %collective-permute-start.10 = (bf16[400,128]{1,0:T(8,128)(2,1)S(1)}, bf16[400,128]{1,0:T(8,128)(2,1)S(1)}, u32[]{:S(2)}, u32[]{:S(2)}) collective-permute-start(bf16[400,128]{1,0:T(8,128)(2,1)S(1)} %get-tuple-element.43), channel_id=1, source_target_pairs={{0,2},{1,3},{2,0},{3,1},{4,6},{5,7},{6,4},{7,5},{8,10},{9,11},{10,... | collective-permute-start | bytes 307208 | tf_op jit(solution)/shard_map/ppermute | solution.py:289
  55.1 6.3 %collective-permute-start.19 = (bf16[400,128]{1,0:T(8,128)(2,1)S(1)}, bf16[400,128]{1,0:T(8,128)(2,1)S(1)}, u32[]{:S(2)}, u32[]{:S(2)}) collective-permute-start(bf16[400,128]{1,0:T(8,128)(2,1)S(1)} %shard_map.164), channel_id=1, source_target_pairs={{0,8},{4,12},{8,0},{12,4},{16,24},{20,28},{24,16},{28,20},{1,9},{5... | collective-permute-start | bytes 307208 | tf_op jit(solution)/shard_map/ppermute | solution.py:286
  62.2 0.7 %copy-start.8 = (f32[1,128]{1,0:T(1,128)S(1)}, f32[1,128]{1,0:T(1,128)}, u32[]{:S(2)}) copy-start(f32[1,128]{1,0:T(1,128)} %get-tuple-element.53.refs_6_) | copy-start | bytes 1540

commit v12 on v10

--- a/solution.py
+++ b/solution.py
@@ -15,7 +15,7 @@
 LANES = 128
 COST_JOIN = 6e9
 COST_UPDATE = 6e9
-COST_SUM = 1e9
+COST_CHUNK = 12e9
 
 
 def dot(a, b, a_dim, b_dim):
@@ -159,20 +159,27 @@
     qg_ref[...] = dot(rows_ref[...], m_ref[...], 1, 0)
 
 
-def far_body(blocks, pieces, *refs):
+def far_body(blocks, *refs):
     block_refs, refs = refs[:blocks], refs[blocks:]
-    q_ref, weight_ref, ids_ref, qg_ref, s_ref, here_ref = refs[:6]
-    m_ref, g_ref, mine_ref, theirs_ref, rows_ref, kinds_ref, tall_ref = refs[6:]
+    q_ref, weight_ref, ids_ref, m_ref, right_ref, rows_ref = refs
     join_body(*block_refs, rows_ref)
     rows_t = rows_ref[...].T
     base = rows_t.shape[0]
+    step = step_of(q_ref.shape[1] // weight_ref.shape[0])
+    for at in range(0, q_ref.shape[1], step):
+        m_ref[:, at:at + step] = grad_chunk(rows_t, q_ref, weight_ref, ids_ref, base, at, step)
+    right_ref[...] = dot(q_ref[...], m_ref[...], 1, 1).astype(BF)
+
+
+def back_body(blocks, *refs):
+    block_refs, refs = refs[:blocks], refs[blocks:]
+    m_ref, qg_ref, s_ref, ids_ref, g_ref, tall_ref, rows_ref, kinds_ref = refs
+    join_body(*block_refs, rows_ref)
     width, edges = qg_ref.shape
-    step = step_of(edges // weight_ref.shape[0])
+    step = step_of(edges)
     for at in range(0, edges, step):
         cols = slice(at, at + step)
-        m = grad_chunk(rows_t, q_ref, weight_ref, ids_ref, base, at, step)
-        m_ref[:, cols] = m
-        g = qg_ref[:, cols] + dot(rows_ref[...], m, 1, 0)
+        g = qg_ref[:, cols] + dot(rows_ref[...], m_ref[:, cols], 1, 0)
         g_ref[:, cols] = g
         by_kind = complex_back(g, s_ref[:, cols].astype(F32))
         kinds = dot(by_kind, hot(ids_ref[2:3, cols], kinds_ref.shape[1]), 1, 1)
@@ -182,25 +189,14 @@
             kinds_ref[...] += kinds
     parts = kinds_ref.shape[1] // LANES
     for j in range(parts):
-        tall_ref[j * width:(j + 1) * width, :] = kinds_ref[:, j * LANES:(j + 1) * LANES]
+        tall_ref[j * width:(j + 1) * width, :] = kinds_ref[:, j * LANES:(j + 1) * LANES].astype(BF)
     rest = tall_ref.shape[0] - parts * width
     if rest:
-        tall_ref[parts * width:, :] = jnp.zeros((rest, LANES), F32)
-    here = here_ref[0]
-    size = tall_ref.shape[0] // pieces
-    for k in range(pieces):
-        start = pl.multiple_of((here ^ k) * size, 16)
-        piece = tall_ref[pl.ds(start, size), :]
-        at = slice(k // 2 * size, (k // 2 + 1) * size)
-        if k % 2:
-            theirs_ref[at, :] = piece.astype(BF)
-        else:
-            mine_ref[at, :] = piece
-
-
-def rest_body(q_ref, m_ref, g_ref, o_ref, ids_ref, right_ref, near_ref, far_ref, left_ref):
-    right_ref[...] = dot(q_ref[...], m_ref[...], 1, 1).astype(BF)
-    edges = q_ref.shape[1]
+        tall_ref[parts * width:, :] = jnp.zeros((rest, LANES), BF)
+
+
+def source_body(g_ref, o_ref, ids_ref, near_ref, far_ref, left_ref):
+    edges = g_ref.shape[1]
     step = step_of(edges)
     for at in range(0, edges, step):
         cols = slice(at, at + step)
@@ -215,29 +211,20 @@
     far_ref[...] = left_ref[:, cut:].astype(BF)
 
 
-def relation_body(pieces, *refs):
-    piece_refs, refs = refs[:pieces // 2], refs[pieces // 2:]
-    sibling_ref, table_ref, state_ref, here_ref, new_ref, state_new_ref, tall_ref = refs
-    here = here_ref[0]
-    size = tall_ref.shape[0] // pieces
-    for k in range(pieces):
-        start = pl.multiple_of((here ^ k) * size, 16)
-        piece = sibling_ref[k // 2 * size:(k // 2 + 1) * size, :] if k % 2 else piece_refs[k // 2][...]
-        tall_ref[pl.ds(start, size), :] = piece.astype(F32)
+def relation_body(tall_ref, table_ref, state_ref, new_ref, state_new_ref):
     width, count = table_ref.shape
     for j in range(count // LANES):
         cols = slice(j * LANES, (j + 1) * LANES)
-        g = tall_ref[j * width:(j + 1) * width, :]
+        g = tall_ref[j * width:(j + 1) * width, :].astype(F32)
         state = state_ref[:, cols] + jnp.sum(g * g, axis=0, keepdims=True) * (1.0 / width)
         state_new_ref[:, cols] = state
         new_ref[:, cols] = table_ref[:, cols] - g * (LEARN_RATE * lax.rsqrt(state))
 
 
-def piece_body(mine_ref, got_ref, own_ref, *other_refs):
-    size = own_ref.shape[0]
-    for k, ref in enumerate((own_ref, *other_refs)):
-        at = slice(k * size, (k + 1) * size)
-        ref[...] = (mine_ref[at, :] + got_ref[at, :].astype(F32)).astype(ref.dtype)
+def pieces_body(pieces_ref, out_ref):
+    total = jnp.sum(pieces_ref[...].astype(F32), axis=0).astype(BF)
+    for k in range(out_ref.shape[0]):
+        out_ref[k] = total
 
 
 def left_body(near_ref, got_ref, own_ref, *other_refs):
@@ -246,23 +233,10 @@
         ref[...] = (near_ref[:, at] + got_ref[:, at].astype(F32)).astype(ref.dtype)
 
 
-def stack_body(*refs):
-    size = refs[0].shape[0]
-    for k, ref in enumerate(refs[:-1]):
-        refs[-1][k * size:(k + 1) * size, :] = ref[...]
-
-
 def chunk_body(near_ref, got_ref, *block_refs):
     for k, ref in enumerate(block_refs):
         cols = slice(k * LANES, (k + 1) * LANES)
         ref[...] = (near_ref[:, cols] + got_ref[:, cols].astype(F32)).astype(BF)
-
-
-def sum_body(*refs):
-    total = refs[0][...].astype(F32)
-    for ref in refs[1:-1]:
-        total = total + ref[...].astype(F32)
-    refs[-1][...] = total.astype(BF)
 
 
 def update_body(parts, *refs):
@@ -305,7 +279,6 @@
         left_t, right_t, relation_t = left_table.T, right_table.T, relation_table.T
         nrel = relation_t.shape[1]
         here_l, here_r = lax.axis_index("left"), lax.axis_index("right")
-        me = here_r.astype(jnp.int32).reshape(1)
         edges = source_ids.shape[-1]
         groups = negative_ids.shape[2]
         n_rows = n_left * rows
@@ -350,47 +323,43 @@
             (shape(width, half), shape(width, edges)),
             [part, pltpu.VMEM((half, edges), BF)],
         )(*near, q, weight, ids)
+        m, right_far = call(
+            functools.partial(far_body, 2), (shape(half, edges, dtype=BF), shape(width, half, dtype=BF)), [part],
+            after=(qg_near, moved),
+        )(other_own, other_rest, q, weight, ids)
+        right_got = swap_left(right_far, 1)
+
+        devices = n_left * n_right
         tall = nrel // LANES * width
-        size = -(-tall // (n_right * 16)) * 16
-        piece = shape(size, LANES, dtype=BF)
-        all_pieces = pltpu.VMEM((size * n_right, LANES), F32)
-        m, g, mine, theirs = call(
-            functools.partial(far_body, 2, n_right),
-            (shape(half, edges, dtype=BF), shape(width, edges), shape(far_right * size, LANES),
-             shape(far_right * size, LANES, dtype=BF)),
-            [part, pltpu.VMEM((width, nrel), F32), all_pieces],
-            me,
-            after=(moved,),
-        )(other_own, other_rest, q, weight, ids, qg_near, s)
+        size = -(-tall // (devices * 16)) * 16
         left_rows = n_right * rows
         left_half = left_rows // 2
-        right_far, left_near, left_far = call(
-            rest_body,
-            (shape(width, half, dtype=BF), shape(width, left_half), shape(width, left_half, dtype=BF)),
+        g, kinds = call(
+            functools.partial(back_body, 2),
+            (shape(width, edges), shape(devices * size, LANES, dtype=BF)),
+            [part, pltpu.VMEM((width, nrel), F32)],
+        )(other_own, other_rest, m, qg_near, s, ids)
+
+        def exchange(value):
+            return lax.all_to_all(value, ("left", "right"), 0, 0, tiled=True)
+
+        pieces = shape(devices, size, LANES, dtype=BF)
+        kinds = exchange(kinds.reshape(devices, size, LANES))
+        left_near, left_far = call(
+            source_body,
+            (shape(width, left_half), shape(width, left_half, dtype=BF)),
             [pltpu.VMEM((width, left_rows), F32)],
-        )(q, m, g, o, ids)
-
-        left_own, *blocks = call(left_body, (shape(width, rows),) + (one_block,) * (far_right - 1))(
+            after=(kinds,),
+        )(g, o, ids)
+        left_own, *halves = call(left_body, (shape(width, rows),) + (one_block,) * (far_right - 1))(
             left_near, swap_right(left_far, 1)
         )
-        left_got = [swap_right(block, 2 * (k + 1)) for k, block in enumerate(blocks)]
-
-        mine, *rest = call(
-            piece_body, (shape(size, LANES),) + (piece,) * (far_right - 1), flops=COST_SUM, after=(right_far,)
-        )(mine, swap_right(theirs, 1))
-        got = [swap_right(p, 2 * (k + 1)) for k, p in enumerate(rest)]
-        mine = call(sum_body, piece, flops=COST_SUM)(mine, *got)
-        bit = 2
-        while bit < n_left:
-            mine = call(sum_body, piece, flops=COST_SUM)(mine, swap_left(mine, bit))
-            bit *= 2
-        right_got = swap_left(right_far, 1)
-        blocks = call(chunk_body, (one_block,) * outer, after=(*left_got, mine))(right_near, right_got)
+        left_got = [swap_right(block, 2 * (k + 1)) for k, block in enumerate(halves)]
+
+        blocks = call(chunk_body, (one_block,) * outer, after=(kinds,), flops=COST_CHUNK)(right_near, right_got)
+        kinds = call(pieces_body, pieces, after=(blocks[0],))(kinds)
         right_got = [next_column(block, 2 * k) for k, block in enumerate(blocks)]
-
-        mine = call(sum_body, piece, flops=COST_SUM)(mine, swap_left(mine, 1))
-        pieces = [mine] + [swap_right(mine, 2 * k) for k in range(1, far_right)]
-        sibling = swap_right(call(stack_body, shape(far_right * size, LANES, dtype=BF))(*pieces), 1)
+        kinds = exchange(kinds).reshape(devices * size, LANES)
 
         def update(got, table, state, flops=0):
             outs = (shape(width, rows), shape(1, rows))
@@ -398,13 +367,9 @@
 
         left_new, left_state_new = update([left_own, *left_got], left_t, left_state[None, :])
         right_new, right_state_new = update(right_got, moved, moved, COST_UPDATE)
-        relation_new, relation_state_new = call(
-            functools.partial(relation_body, n_right),
-            (shape(width, nrel), shape(1, nrel)),
-            [all_pieces],
-            me,
-            after=(right_state_new,),
-        )(*pieces, sibling, relation_t, relation_state[None, :])
+        relation_new, relation_state_new = call(relation_body, (shape(width, nrel), shape(1, nrel)))(
+            kinds, relation_t, relation_state[None, :]
+        )
         return (
             left_new.T, left_state_new.reshape(-1), right_new.T, right_state_new.reshape(-1),
             relation_new.T, relation_state_new.reshape(-1),

time: 59.3 us -> 70.9 us (1.20)
  waiting for transfers between devices: 16.9 us -> 21.7 us
  starting transfers between devices: 26.8 us -> 29.3 us
  local copies, waits for them, and re-layouts: 2.53 us -> 5.02 us
  Pallas kernels: 11.1 us -> 12.8 us
    all_to_all x0 -> x2, waiting for transfers between devices: none -> 11.4 us  [exchange(): return lax.all_to_all(value, ('left', 'right'), 0, 0, tiled=True)]
    all_to_all x0 -> x2, starting transfers between devices: none -> 8.7 us  [exchange(): return lax.all_to_all(value, ('left', 'right'), 0, 0, tiled=True)]
    ppermute x9 -> x6, waiting for transfers between devices: 8.97 us -> 4.75 us  [swap_left(): return lax.ppermute(value, 'left', [(i, i ^ by) for i in range(n_left)])]
    ppermute x9 -> x6, starting transfers between devices: 14 us -> 10.8 us  [swap_left(): return lax.ppermute(value, 'left', [(i, i ^ by) for i in range(n_left)])]
    ppermute x8 -> x4, starting transfers between devices: 7.33 us -> 4.43 us  [swap_right(): return lax.ppermute(value, 'right', [(i, i ^ by) for i in range(n_right)])]
    ppermute x5, waiting for transfers between devices: 2.59 us -> 0.03 us  [next_column(): return lax.ppermute(value, ('left', 'right'), perm)]
    unnamed x18 -> x32, local copies, waits for them, and re-layouts: 2.53 us -> 5.02 us
    pallas_call x21 -> x17, Pallas kernels: 11.1 us -> 12.8 us  [run(): pl.pallas_call(inner, out_shape=out_shape, in_specs=specs, scratch_shapes...]
  transfers between devices with their start and end apart: 23 -> 18, of which waited for: 11 -> 8; matrix products, arithmetic and copies ran while one was open for 1% -> 1% of each run, Pallas kernels for 13% -> 13%
where the time goes in v12:
time: 70.9 us; the launch traced here: 70.6 us
  starting transfers between devices  29.3 us (41%)
  waiting for transfers between devices  21.7 us (31%)
  Pallas kernels  12.8 us (18%)
  local copies, waits for them, and re-layouts  5.02 us (7%)
  between operations  0.89 us (1%)
  other arithmetic  0.85 us (1%)
    pallas_call x17, Pallas kernels, run(): pl.pallas_call(inner, out_shape=out_shape, in_specs=specs, scratch_shapes...  12.8 us
    all_to_all x2, waiting for transfers between devices, exchange(): return lax.all_to_all(value, ('left', 'right'), 0, 0, tiled=True)  11.4 us
    ppermute x6, starting transfers between devices, swap_left(): return lax.ppermute(value, 'left', [(i, i ^ by) for i in range(n_left)])  10.8 us
    all_to_all x2, starting transfers between devices, exchange(): return lax.all_to_all(value, ('left', 'right'), 0, 0, tiled=True)  8.7 us
    ppermute x5, starting transfers between devices, next_column(): return lax.ppermute(value, ('left', 'right'), perm)  5.23 us
    ppermute x4, waiting for transfers between devices, swap_right(): return lax.ppermute(value, 'right', [(i, i ^ by) for i in range(n_right)])  5.19 us
    unnamed x32, local copies, waits for them, and re-layouts  5.02 us
    ppermute x6, waiting for transfers between devices, swap_left(): return lax.ppermute(value, 'left', [(i, i ^ by) for i in range(n_left)])  4.75 us
  transfers between devices with their start and end apart: 18, of which 8 were waited for; matrix products, arithmetic and copies ran while one was open for 1% of the time, Pallas kernels for 13%

profile of v12, /device:TPU:0, one launch (start us, length us, event | category | flops | bytes accessed | tf_op | source)
XLA Modules:
  0.0 70.6 jit_solution(8217650515810854391)
XLA Ops:
  0.6 0.9 %copy-done.1 = f32[128,400]{0,1:T(8,128)S(1)} copy-done((f32[128,400]{0,1:T(8,128)S(1)}, f32[128,400]{0,1:T(8,128)}, u32[]{:S(2)}) %copy-start.1) | copy-done | bytes 204824
  1.6 0.3 shard_map.145.refs_0_
  1.9 5.1 %collective-permute-start.3 = (bf16[400,128]{1,0:T(8,128)(2,1)S(1)}, bf16[400,128]{1,0:T(8,128)(2,1)S(1)}, u32[]{:S(2)}, u32[]{:S(2)}) collective-permute-start(bf16[400,128]{1,0:T(8,128)(2,1)S(1)} %shard_map.145.refs_0_), channel_id=1, source_target_pairs={{0,24},{4,28},{8,16},{12,20},{16,8},{20,12},{24,0},{28,4},{1,25},{... | collective-permute-start | bytes 307208 | tf_op jit(solution)/shard_map/ppermute | solution.py:261
  7.0 0.6 collective-permute-start.1
  7.6 1.7 %collective-permute-start = (bf16[400,128]{1,0:T(8,128)(2,1)S(1)}, bf16[400,128]{1,0:T(8,128)(2,1)S(1)}, u32[]{:S(2)}, u32[]{:S(2)}) collective-permute-start(bf16[400,128]{1,0:T(8,128)(2,1)S(1)} %shard_map.145.refs_0_), channel_id=1, source_target_pairs={{0,4},{4,0},{8,12},{12,8},{16,20},{20,16},{24,28},{28,24},{1,5},{5... | collective-permute-start | bytes 307208 | tf_op jit(solution)/shard_map/ppermute | solution.py:261
  9.3 0.8 %pad_add_fusion = s32[5,1024]{1,0:T(8,128)S(1)} fusion(s32[2,1024]{1,0:T(2,128)} %bitcast.31, s32[1,1024]{1,0:T(1,128)} %bitcast.32, s32[1,1024]{1,0:T(1,128)} %bitcast.33, s32[1,1024]{1,0:T(1,128)} %bitcast.34), kind=kLoop, calls=%fused_computation.1 | loop fusion | flops 15360 | bytes 40960 | tf_op jit(solution)/shard_map/concatenate | solution.py:304
  10.1 0.1 collective-permute-start.5
  10.1 0.9 %copy-done.3 = f32[128,400]{0,1:T(8,128)S(1)} copy-done((f32[128,400]{0,1:T(8,128)S(1)}, f32[128,400]{0,1:T(8,128)}, u32[]{:S(2)}) %copy-start.3) | copy-done | bytes 204824
  11.1 0.3 shard_map.147.refs_0_
  11.4 0.3 collective-permute-done.5.refs_2_.ids_ref
  11.7 0.6 collective-permute-done.refs_1_.refs_0_
  12.3 1.7 %collective-permute-start.6 = (bf16[400,128]{1,0:T(8,128)(2,1)S(1)}, bf16[400,128]{1,0:T(8,128)(2,1)S(1)}, u32[]{:S(2)}, u32[]{:S(2)}) collective-permute-start(bf16[400,128]{1,0:T(8,128)(2,1)S(1)} %shard_map.148.refs_0_), channel_id=1, source_target_pairs={{0,2},{1,3},{2,0},{3,1},{4,6},{5,7},{6,4},{7,5},{8,10},{9,11},{10,... | collective-permute-start | bytes 307208 | tf_op jit(solution)/shard_map/ppermute | solution.py:264
  14.0 1.6 %collective-permute-done.2.refs_1_.refs_2_ = bf16[400,128]{1,0:T(8,128)(2,1)S(1)} collective-permute-done((bf16[400,128]{1,0:T(8,128)(2,1)S(1)}, bf16[400,128]{1,0:T(8,128)(2,1)S(1)}, u32[]{:S(2)}, u32[]{:S(2)}) %collective-permute-start.2) | collective-permute-done | bytes 102432 | tf_op jit(solution)/shard_map/ppermute | solution.py:261
  15.6 0.1 shard_map.146.refs_2_
  15.7 1.6 %collective-permute-start.4 = (bf16[400,384]{1,0:T(8,128)(2,1)S(1)}, bf16[400,384]{1,0:T(8,128)(2,1)S(1)}, u32[]{:S(2)}, u32[]{:S(2)}) collective-permute-start(bf16[400,384]{1,0:T(8,128)(2,1)S(1)} %shard_map.146.refs_2_), channel_id=1, source_target_pairs={{0,4},{4,0},{8,12},{12,8},{16,20},{20,16},{24,28},{28,24},{1,5},{5... | collective-permute-start | bytes 921608 | tf_op jit(solution)/shard_map/ppermute | solution.py:261
  17.3 0.1 collective-permute-start.8
  17.3 0.8 %collective-permute-done.6.refs_1_ = bf16[400,128]{1,0:T(8,128)(2,1)S(1)} collective-permute-done((bf16[400,128]{1,0:T(8,128)(2,1)S(1)}, bf16[400,128]{1,0:T(8,128)(2,1)S(1)}, u32[]{:S(2)}, u32[]{:S(2)}) %collective-permute-start.6) | collective-permute-done | bytes 102432 | tf_op jit(solution)/shard_map/ppermute | solution.py:264
  18.1 0.9 %collective-permute-start.7 = (bf16[400,256]{1,0:T(8,128)(2,1)S(1)}, bf16[400,256]{1,0:T(8,128)(2,1)S(1)}, u32[]{:S(2)}, u32[]{:S(2)}) collective-permute-start(bf16[400,256]{1,0:T(8,128)(2,1)S(1)} %pad_maximum_fusion), channel_id=1, source_target_pairs={{0,1},{1,0},{2,3},{3,2},{4,5},{5,4},{6,7},{7,6},{8,9},{9,8},{10,11... | collective-permute-start | bytes 614408 | tf_op jit(solution)/shard_map/ppermute | solution.py:264
  19.0 0.1 pad_add_fusion.1.place_ref
  19.1 1.6 %shard_map.149 = (f32[2,1024,128]{2,1,0:T(8,128)S(1)}, bf16[400,256]{1,0:T(8,128)(2,1)S(1)}, s32[5,1024]{1,0:T(8,128)S(1)}) custom-call(s32[5,1024]{1,0:T(8,128)S(1)} %collective-permute-done.5.refs_2_.ids_ref, f32[400,256]{1,0:T(8,128)S(1)} %bitcast.20, s32[2]{0:T(128)S(1)} %pad_add_fusion.1.place_ref), custom_call_target="tpu_custom_call" | custom-call | tf_op jit(solution)/shard_map/pallas_call | solution.py:49
  20.7 0.9 %shard_map.150 = (bf16[400,1024]{1,0:T(8,128)(2,1)S(1)}, bf16[400,1024]{1,0:T(8,128)(2,1)S(1)}, bf16[400,1024]{1,0:T(8,128)(2,1)S(1)}) custom-call(bf16[400,128]{1,0:T(8,128)(2,1)S(1)} %shard_map.148.refs_0_, bf16[400,128]{1,0:T(8,128)(2,1)S(1)} %collective-permute-done.6.refs_1_, bf16[400,256]{1,0:T(8,128)(2,1)S(1)} %collective-permute-done.7.refs_2_, ...), custom_call_target="tpu_custom_call" | custom-call | tf_op jit(solution)/shard_map/pallas_call | solution.py:49
  21.6 1.8 %shard_map.151 = (f32[400,512]{1,0:T(8,128)S(1)}, f32[400,1024]{1,0:T(8,128)S(1)}) custom-call(bf16[400,128]{1,0:T(8,128)(2,1)S(1)} %shard_map.145.refs_0_, bf16[400,128]{1,0:T(8,128)(2,1)S(1)} %collective-permute-done.1.refs_0_.refs_1_, bf16[400,128]{1,0:T(8,128)(2,1)S(1)} %collective-permute-done.2.refs_1_.refs_2_, ...), custom_call_target="tpu_custom_call" | custom-call | tf_op jit(solution)/shard_map/pallas_call | solution.py:49
  23.4 0.9 %copy-done.13 = f32[400,512]{1,0:T(8,128)} copy-done((f32[400,512]{1,0:T(8,128)}, f32[400,512]{1,0:T(8,128)S(1)}, u32[]{:S(2)}) %copy-start.13) | copy-done | bytes 819224
  24.3 1.5 %shard_map.153 = (bf16[512,1024]{1,0:T(8,128)(2,1)S(1)}, bf16[400,512]{1,0:T(8,128)(2,1)S(1)}) custom-call(bf16[400,128]{1,0:T(8,128)(2,1)S(1)} %collective-permute-done.refs_1_.refs_0_, bf16[400,384]{1,0:T(8,128)(2,1)S(1)} %collective-permute-done.4.refs_1_, bf16[400,1024]{1,0:T(8,128)(2,1)S(1)} %get-tuple-element.34.refs_4_.refs_2_, ...), custom_call_target="tpu_custom_call" | custom-call | tf_op jit(solution)/shard_map/pallas_call | solution.py:49
  25.8 0.8 %copy-done.15 = bf16[400,512]{1,0:T(8,128)(2,1)} copy-done((bf16[400,512]{1,0:T(8,128)(2,1)}, bf16[400,512]{1,0:T(8,128)(2,1)S(1)}, u32[]{:S(2)}) %copy-start.15) | copy-done | bytes 409624
  26.6 1.3 %shard_map.154 = (f32[400,1024]{1,0:T(8,128)S(1)}, bf16[1024,128]{1,0:T(8,128)(2,1)S(1)}) custom-call(bf16[400,128]{1,0:T(8,128)(2,1)S(1)} %collective-permute-done.refs_1_.refs_0_, bf16[400,384]{1,0:T(8,128)(2,1)S(1)} %collective-permute-done.4.refs_1_, bf16[512,1024]{1,0:T(8,128)(2,1)S(1)} %get-tuple-element.37.refs_2_, ...), custom_call_target="tpu_custom_call" | custom-call | tf_op jit(solution)/shard_map/pallas_call | solution.py:49
  27.9 0.7 copy-done.7
  28.6 4.2 %all-to-all-start = ((bf16[32,32,128]{2,1,0:T(8,128)(2,1)}), bf16[32,32,128]{2,1,0:T(8,128)(2,1)S(1)}, u32[]{:S(2)}, u32[]{:S(2)}) async-start(bf16[32,32,128]{2,1,0:T(8,128)(2,1)} %bitcast.27), calls=%async_computation | async-start | bytes 524288 | tf_op jit(solution)/shard_map/all_to_all | solution.py:344
  32.9 1.8 %collective-permute-start.11 = (bf16[400,512]{1,0:T(8,128)(2,1)}, bf16[400,512]{1,0:T(8,128)(2,1)}, u32[]{:S(2)}, u32[]{:S(2)}) collective-permute-start(bf16[400,512]{1,0:T(8,128)(2,1)} %copy-done.15), channel_id=1, source_target_pairs={{0,4},{4,0},{8,12},{12,8},{16,20},{20,16},{24,28},{28,24},{1,5},{5... | collective-permute-start | bytes 1228808 | tf_op jit(solution)/shard_map/ppermute | solution.py:261
  34.7 8.8 %all-to-all-done.refs_3_.refs_2_.refs_0_ = bf16[32,32,128]{2,1,0:T(8,128)(2,1)S(1)} async-done(((bf16[32,32,128]{2,1,0:T(8,128)(2,1)}), bf16[32,32,128]{2,1,0:T(8,128)(2,1)S(1)}, u32[]{:S(2)}, u32[]{:S(2)}) %all-to-all-start) | async-done | bytes 262176 | tf_op jit(solution)/shard_map/all_to_all | solution.py:344
  43.5 0.7 shard_map.155
  44.2 0.7 %copy-done.5 = f32[400,256]{1,0:T(8,128)} copy-done((f32[400,256]{1,0:T(8,128)}, f32[400,256]{1,0:T(8,128)S(1)}, u32[]{:S(2)}) %copy-start.5) | copy-done | bytes 409624
  44.9 2.6 %collective-permute-done.11.refs_1_ = bf16[400,512]{1,0:T(8,128)(2,1)} collective-permute-done((bf16[400,512]{1,0:T(8,128)(2,1)}, bf16[400,512]{1,0:T(8,128)(2,1)}, u32[]{:S(2)}, u32[]{:S(2)}) %collective-permute-start.11) | collective-permute-done | bytes 409632 | tf_op jit(solution)/shard_map/ppermute | solution.py:261
  47.5 1.2 %shard_map.158 = (bf16[400,128]{1,0:T(8,128)(2,1)S(1)}, bf16[400,128]{1,0:T(8,128)(2,1)S(1)}, bf16[400,128]{1,0:T(8,128)(2,1)S(1)}, bf16[400,128]{1,0:T(8,128)(2,1)S(1)}) custom-call(f32[400,512]{1,0:T(8,128)S(1)} %copy-done.14, bf16[400,512]{1,0:T(8,128)(2,1)} %collective-permute-done.11.refs_1_, bf16[32,32,128]{2,1,0:T(8,128)(2,1)S(1)} %all-to-all-done.refs_3_.refs_2_.refs_0_), custom_call_target="tpu_custom_call" | custom-call | flops 12000000000 | tf_op jit(solution)/shard_map/pallas_call | solution.py:49
  48.7 1.0 %collective-permute-start.13 = (bf16[400,128]{1,0:T(8,128)(2,1)S(1)}, bf16[400,128]{1,0:T(8,128)(2,1)S(1)}, u32[]{:S(2)}, u32[]{:S(2)}) collective-permute-start(bf16[400,128]{1,0:T(8,128)(2,1)S(1)} %get-tuple-element.51), channel_id=1, source_target_pairs={{0,9},{1,10},{2,11},{3,8},{4,13},{5,14},{6,15},{7,12},{8,1},{9,2},... | collective-permute-start | bytes 307208 | tf_op jit(solution)/shard_map/ppermute | solution.py:271
  49.7 3.4 %collective-permute-start.14 = (bf16[400,128]{1,0:T(8,128)(2,1)S(1)}, bf16[400,128]{1,0:T(8,128)(2,1)S(1)}, u32[]{:S(2)}, u32[]{:S(2)}) collective-permute-start(bf16[400,128]{1,0:T(8,128)(2,1)S(1)} %get-tuple-element.52), channel_id=1, source_target_pairs={{0,17},{1,18},{2,19},{3,16},{4,21},{5,22},{6,23},{7,20},{8,25},{9,... | collective-permute-start | bytes 307208 | tf_op jit(solution)/shard_map/ppermute | solution.py:271
  53.1 0.1 collective-permute-start.15
  53.2 0.6 collective-permute-start.12
  53.9 0.8 %shard_map.160 = bf16[32,32,128]{2,1,0:T(8,128)(2,1)} custom-call(bf16[32,32,128]{2,1,0:T(8,128)(2,1)S(1)} %all-to-all-done.refs_3_.refs_2_.refs_0_, bf16[400,128]{1,0:T(8,128)(2,1)S(1)} %get-tuple-element.50.refs_1_), custom_call_target="tpu_custom_call" | custom-call | tf_op jit(solution)/shard_map/pallas_call | solution.py:49
  54.6 4.5 %all-to-all-start.1 = ((bf16[32,32,128]{2,1,0:T(8,128)(2,1)}), bf16[32,32,128]{2,1,0:T(8,128)(2,1)S(1)}, u32[]{:S(2)}, u32[]{:S(2)}) async-start(bf16[32,32,128]{2,1,0:T(8,128)(2,1)} %shard_map.160), calls=%async_computation.1 | async-start | bytes 524288 | tf_op jit(solution)/shard_map/all_to_all | solution.py:344
  59.1 0.1 shard_map.156
  59.2 1.8 %collective-permute-start.10 = (bf16[400,128]{1,0:T(8,128)(2,1)S(1)}, bf16[400,128]{1,0:T(8,128)(2,1)S(1)}, u32[]{:S(2)}, u32[]{:S(2)}) collective-permute-start(bf16[400,128]{1,0:T(8,128)(2,1)S(1)} %get-tuple-element.45), channel_id=1, source_target_pairs={{0,2},{1,3},{2,0},{3,1},{4,6},{5,7},{6,4},{7,5},{8,10},{9,11},{10,... | collective-permute-start | bytes 307208 | tf_op jit(solution)/shard_map/ppermute | solution.py:264
  61.1 0.0 collective-permute-done.15.refs_3_
  61.1 0.8 %shard_map.159 = (f32[400,128]{1,0:T(8,128)}, f32[1,128]{1,0:T(1,128)}) custom-call(bf16[400,128]{1,0:T(8,128)(2,1)S(1)} %collective-permute-done.12.refs_0_, bf16[400,128]{1,0:T(8,128)(2,1)S(1)} %collective-permute-done.13.refs_1_, bf16[400,128]{1,0:T(8,128)(2,1)S(1)} %collective-permute-done.14.refs_2_, ...), custom_call_target="tpu_custom_call" | custom-call | flops 6000000000 | tf_op jit(solution)/shard_map/pallas_call | solution.py:49
  61.9 4.4 %collective-permute-done.10.refs_1_ = bf16[400,128]{1,0:T(8,128)(2,1)S(1)} collective-permute-done((bf16[400,128]{1,0:T(8,128)(2,1)S(1)}, bf16[400,128]{1,0:T(8,128)(2,1)S(1)}, u32[]{:S(2)}, u32[]{:S(2)}) %collective-permute-start.10) | collective-permute-done | bytes 102432 | tf_op jit(solution)/shard_map/ppermute | solution.py:264
  66.3 0.8 %shard_map.157 = (f32[400,128]{1,0:T(8,128)}, f32[1,128]{1,0:T(1,128)}) custom-call(f32[400,128]{1,0:T(8,128)S(1)} %get-tuple-element.44.refs_0_, bf16[400,128]{1,0:T(8,128)(2,1)S(1)} %collective-permute-done.10.refs_1_, f32[400,128]{1,0:T(8,128)S(1)} %bitcast.26, f32[1,128]{1,0:T(1,128)S(1)} %bitcast.30), custom_call_target="tpu_custom_call" | custom-call | tf_op jit(solution)/shard_map/pallas_call | solution.py:49
  67.1 2.6 %all-to-all-done.1 = bf16[32,32,128]{2,1,0:T(8,128)(2,1)S(1)} async-done(((bf16[32,32,128]{2,1,0:T(8,128)(2,1)}), bf16[32,32,128]{2,1,0:T(8,128)(2,1)S(1)}, u32[]{:S(2)}, u32[]{:S(2)}) %all-to-all-start.1) | async-done | bytes 262176 | tf_op jit(solution)/shard_map/all_to_all | solution.py:344
  69.7 0.9 %shard_map.161 = (f32[400,256]{1,0:T(8,128)}, f32[1,256]{1,0:T(1,128)}) custom-call(bf16[1024,128]{1,0:T(8,128)(2,1)S(1)} %bitcast.22, f32[400,256]{1,0:T(8,128)S(1)} %bitcast.21, f32[1,256]{1,0:T(1,128)S(1)} %bitcast.28), custom_call_target="tpu_custom_call" | custom-call | tf_op jit(solution)/shard_map/pallas_call | solution.py:49
  (40 shorter events, 0.1 us)
Async XLA Ops:
  0.6 0.9 %copy-start.1 = (f32[128,400]{0,1:T(8,128)S(1)}, f32[128,400]{0,1:T(8,128)}, u32[]{:S(2)}) copy-start(f32[128,400]{0,1:T(8,128)} %param.12) | copy-start | bytes 614404
  1.9 12.2 %collective-permute-start.3 = (bf16[400,128]{1,0:T(8,128)(2,1)S(1)}, bf16[400,128]{1,0:T(8,128)(2,1)S(1)}, u32[]{:S(2)}, u32[]{:S(2)}) collective-permute-start(bf16[400,128]{1,0:T(8,128)(2,1)S(1)} %shard_map.145.refs_0_), channel_id=1, source_target_pairs={{0,24},{4,28},{8,16},{12,20},{16,8},{20,12},{24,0},{28,4},{1,25},{... | collective-permute-start | bytes 307208 | tf_op jit(solution)/shard_map/ppermute | solution.py:261
  7.0 8.6 %collective-permute-start.2 = (bf16[400,128]{1,0:T(8,128)(2,1)S(1)}, bf16[400,128]{1,0:T(8,128)(2,1)S(1)}, u32[]{:S(2)}, u32[]{:S(2)}) collective-permute-start(bf16[400,128]{1,0:T(8,128)(2,1)S(1)} %shard_map.145.refs_0_), channel_id=1, source_target_pairs={{0,16},{4,20},{8,24},{12,28},{16,0},{20,4},{24,8},{28,12},{1,17},{... | collective-permute-start | bytes 307208 | tf_op jit(solution)/shard_map/ppermute | solution.py:261
  7.0 8.6 %collective-permute-start.1 = (bf16[400,128]{1,0:T(8,128)(2,1)S(1)}, bf16[400,128]{1,0:T(8,128)(2,1)S(1)}, u32[]{:S(2)}, u32[]{:S(2)}) collective-permute-start(bf16[400,128]{1,0:T(8,128)(2,1)S(1)} %shard_map.145.refs_0_), channel_id=1, source_target_pairs={{0,8},{4,12},{8,0},{12,4},{16,24},{20,28},{24,16},{28,20},{1,9},{5... | collective-permute-start | bytes 307208 | tf_op jit(solution)/shard_map/ppermute | solution.py:261
  7.6 4.7 %collective-permute-start = (bf16[400,128]{1,0:T(8,128)(2,1)S(1)}, bf16[400,128]{1,0:T(8,128)(2,1)S(1)}, u32[]{:S(2)}, u32[]{:S(2)}) collective-permute-start(bf16[400,128]{1,0:T(8,128)(2,1)S(1)} %shard_map.145.refs_0_), channel_id=1, source_target_pairs={{0,4},{4,0},{8,12},{12,8},{16,20},{20,16},{24,28},{28,24},{1,5},{5... | collective-permute-start | bytes 307208 | tf_op jit(solution)/shard_map/ppermute | solution.py:261
  10.1 1.7 %collective-permute-start.5 = (s32[5,1024]{1,0:T(8,128)S(1)}, s32[5,1024]{1,0:T(8,128)S(1)}, u32[]{:S(2)}, u32[]{:S(2)}) collective-permute-start(s32[5,1024]{1,0:T(8,128)S(1)} %pad_add_fusion), channel_id=1, source_target_pairs={{0,3},{1,0},{2,1},{3,2},{4,7},{5,4},{6,5},{7,6},{8,11},{9,8},{10,9... | collective-permute-start | bytes 61448 | tf_op jit(solution)/shard_map/ppermute | solution.py:305
  10.1 0.9 %copy-start.3 = (f32[128,400]{0,1:T(8,128)S(1)}, f32[128,400]{0,1:T(8,128)}, u32[]{:S(2)}) copy-start(f32[128,400]{0,1:T(8,128)} %param.10) | copy-start | bytes 614404
  12.3 5.0 %copy-start.2 = (f32[128,400]{0,1:T(8,128)S(1)}, f32[128,400]{0,1:T(8,128)}, u32[]{:S(2)}) copy-start(f32[128,400]{0,1:T(8,128)} %param.12) | copy-start | bytes 614404
  12.3 4.9 %copy-start.11 = (f32[128]{0:T(128)S(1)}, f32[128]{0:T(128)}, u32[]{:S(2)}) copy-start(f32[128]{0:T(128)} %param.13) | copy-start | bytes 1540
  12.3 6.8 %copy-start = (f32[256,400]{0,1:T(8,128)S(1)}, f32[256,400]{0,1:T(8,128)}, u32[]{:S(2)}) copy-start(f32[256,400]{0,1:T(8,128)} %param.14) | copy-start | bytes 1228804
  12.3 5.8 %collective-permute-start.6 = (bf16[400,128]{1,0:T(8,128)(2,1)S(1)}, bf16[400,128]{1,0:T(8,128)(2,1)S(1)}, u32[]{:S(2)}, u32[]{:S(2)}) collective-permute-start(bf16[400,128]{1,0:T(8,128)(2,1)S(1)} %shard_map.148.refs_0_), channel_id=1, source_target_pairs={{0,2},{1,3},{2,0},{3,1},{4,6},{5,7},{6,4},{7,5},{8,10},{9,11},{10,... | collective-permute-start | bytes 307208 | tf_op jit(solution)/shard_map/ppermute | solution.py:264
  15.7 8.7 %collective-permute-start.4 = (bf16[400,384]{1,0:T(8,128)(2,1)S(1)}, bf16[400,384]{1,0:T(8,128)(2,1)S(1)}, u32[]{:S(2)}, u32[]{:S(2)}) collective-permute-start(bf16[400,384]{1,0:T(8,128)(2,1)S(1)} %shard_map.146.refs_2_), channel_id=1, source_target_pairs={{0,4},{4,0},{8,12},{12,8},{16,20},{20,16},{24,28},{28,24},{1,5},{5... | collective-permute-start | bytes 921608 | tf_op jit(solution)/shard_map/ppermute | solution.py:261
  17.3 7.0 %collective-permute-start.8 = (f32[408,128]{1,0:T(8,128)S(1)}, f32[408,128]{1,0:T(8,128)S(1)}, u32[]{:S(2)}, u32[]{:S(2)}) collective-permute-start(f32[408,128]{1,0:T(8,128)S(1)} %shard_map.152), channel_id=1, source_target_pairs={{0,1},{1,2},{2,3},{3,0},{4,5},{5,6},{6,7},{7,4},{8,9},{9,10},{10,1... | collective-permute-start | bytes 626696 | tf_op jit(solution)/shard_map/ppermute | solution.py:271
  18.1 2.5 %collective-permute-start.7 = (bf16[400,256]{1,0:T(8,128)(2,1)S(1)}, bf16[400,256]{1,0:T(8,128)(2,1)S(1)}, u32[]{:S(2)}, u32[]{:S(2)}) collective-permute-start(bf16[400,256]{1,0:T(8,128)(2,1)S(1)} %pad_maximum_fusion), channel_id=1, source_target_pairs={{0,1},{1,0},{2,3},{3,2},{4,5},{5,4},{6,7},{7,6},{8,9},{9,8},{10,11... | collective-permute-start | bytes 614408 | tf_op jit(solution)/shard_map/ppermute | solution.py:264
  23.4 0.9 %copy-start.13 = (f32[400,512]{1,0:T(8,128)}, f32[400,512]{1,0:T(8,128)S(1)}, u32[]{:S(2)}) copy-start(f32[400,512]{1,0:T(8,128)S(1)} %get-tuple-element.48.refs_0_) | copy-start | bytes 2457604
  24.3 1.5 %copy-start.8 = (f32[408,128]{1,0:T(8,128)}, f32[408,128]{1,0:T(8,128)S(1)}, u32[]{:S(2)}) copy-start(f32[408,128]{1,0:T(8,128)S(1)} %collective-permute-done.8.refs_6_.refs_4_.refs_5_) | copy-start | bytes 626692
  25.8 0.8 %copy-start.15 = (bf16[400,512]{1,0:T(8,128)(2,1)}, bf16[400,512]{1,0:T(8,128)(2,1)S(1)}, u32[]{:S(2)}) copy-start(bf16[400,512]{1,0:T(8,128)(2,1)S(1)} %get-tuple-element.49) | copy-start | bytes 1228804
  27.9 0.7 copy-start.7
  28.6 14.8 %all-to-all-start = ((bf16[32,32,128]{2,1,0:T(8,128)(2,1)}), bf16[32,32,128]{2,1,0:T(8,128)(2,1)S(1)}, u32[]{:S(2)}, u32[]{:S(2)}) async-start(bf16[32,32,128]{2,1,0:T(8,128)(2,1)} %bitcast.27), calls=%async_computation | async-start | bytes 524288 | tf_op jit(solution)/shard_map/all_to_all | solution.py:344
  32.9 14.6 %collective-permute-start.11 = (bf16[400,512]{1,0:T(8,128)(2,1)}, bf16[400,512]{1,0:T(8,128)(2,1)}, u32[]{:S(2)}, u32[]{:S(2)}) collective-permute-start(bf16[400,512]{1,0:T(8,128)(2,1)} %copy-done.15), channel_id=1, source_target_pairs={{0,4},{4,0},{8,12},{12,8},{16,20},{20,16},{24,28},{28,24},{1,5},{5... | collective-permute-start | bytes 1228808 | tf_op jit(solution)/shard_map/ppermute | solution.py:261
  43.5 4.0 %copy-start.14 = (f32[400,512]{1,0:T(8,128)S(1)}, f32[400,512]{1,0:T(8,128)}, u32[]{:S(2)}) copy-start(f32[400,512]{1,0:T(8,128)} %copy-done.13) | copy-start | bytes 2457604
  44.1 0.8 %copy-start.5 = (f32[400,256]{1,0:T(8,128)}, f32[400,256]{1,0:T(8,128)S(1)}, u32[]{:S(2)}) copy-start(f32[400,256]{1,0:T(8,128)S(1)} %get-tuple-element.42.near_ref) | copy-start | bytes 1228804
  44.9 14.2 %collective-permute-start.9 = (bf16[400,256]{1,0:T(8,128)(2,1)S(1)}, bf16[400,256]{1,0:T(8,128)(2,1)S(1)}, u32[]{:S(2)}, u32[]{:S(2)}) collective-permute-start(bf16[400,256]{1,0:T(8,128)(2,1)S(1)} %get-tuple-element.43), channel_id=1, source_target_pairs={{0,1},{1,0},{2,3},{3,2},{4,5},{5,4},{6,7},{7,6},{8,9},{9,8},{10,11... | collective-permute-start | bytes 614408 | tf_op jit(solution)/shard_map/ppermute | solution.py:264
  47.5 11.6 %copy-start.6 = (f32[400,256]{1,0:T(8,128)S(1)}, f32[400,256]{1,0:T(8,128)}, u32[]{:S(2)}) copy-start(f32[400,256]{1,0:T(8,128)} %copy-done.5) | copy-start | bytes 1228804
  48.7 12.4 %copy-start.9 = (f32[408,128]{1,0:T(8,128)S(1)}, f32[408,128]{1,0:T(8,128)}, u32[]{:S(2)}) copy-start(f32[408,128]{1,0:T(8,128)} %copy-done.8) | copy-start | bytes 626692
  48.7 12.4 %collective-permute-start.13 = (bf16[400,128]{1,0:T(8,128)(2,1)S(1)}, bf16[400,128]{1,0:T(8,128)(2,1)S(1)}, u32[]{:S(2)}, u32[]{:S(2)}) collective-permute-start(bf16[400,128]{1,0:T(8,128)(2,1)S(1)} %get-tuple-element.51), channel_id=1, source_target_pairs={{0,9},{1,10},{2,11},{3,8},{4,13},{5,14},{6,15},{7,12},{8,1},{9,2},... | collective-permute-start | bytes 307208 | tf_op jit(solution)/shard_map/ppermute | solution.py:271
  49.7 11.4 %collective-permute-start.14 = (bf16[400,128]{1,0:T(8,128)(2,1)S(1)}, bf16[400,128]{1,0:T(8,128)(2,1)S(1)}, u32[]{:S(2)}, u32[]{:S(2)}) collective-permute-start(bf16[400,128]{1,0:T(8,128)(2,1)S(1)} %get-tuple-element.52), channel_id=1, source_target_pairs={{0,17},{1,18},{2,19},{3,16},{4,21},{5,22},{6,23},{7,20},{8,25},{9,... | collective-permute-start | bytes 307208 | tf_op jit(solution)/shard_map/ppermute | solution.py:271
  53.1 8.0 %collective-permute-start.15 = (bf16[400,128]{1,0:T(8,128)(2,1)S(1)}, bf16[400,128]{1,0:T(8,128)(2,1)S(1)}, u32[]{:S(2)}, u32[]{:S(2)}) collective-permute-start(bf16[400,128]{1,0:T(8,128)(2,1)S(1)} %get-tuple-element.53), channel_id=1, source_target_pairs={{0,25},{1,26},{2,27},{3,24},{4,29},{5,30},{6,31},{7,28},{8,17},{9,... | collective-permute-start | bytes 307208 | tf_op jit(solution)/shard_map/ppermute | solution.py:271
  53.2 7.9 %collective-permute-start.12 = (bf16[400,128]{1,0:T(8,128)(2,1)S(1)}, bf16[400,128]{1,0:T(8,128)(2,1)S(1)}, u32[]{:S(2)}, u32[]{:S(2)}) collective-permute-start(bf16[400,128]{1,0:T(8,128)(2,1)S(1)} %get-tuple-element.50.refs_1_), channel_id=1, source_target_pairs={{0,1},{1,2},{2,3},{3,0},{4,5},{5,6},{6,7},{7,4},{8,9},{9,10},{10,1... | collective-permute-start | bytes 307208 | tf_op jit(solution)/shard_map/ppermute | solution.py:271
  54.6 15.1 %all-to-all-start.1 = ((bf16[32,32,128]{2,1,0:T(8,128)(2,1)}), bf16[32,32,128]{2,1,0:T(8,128)(2,1)S(1)}, u32[]{:S(2)}, u32[]{:S(2)}) async-start(bf16[32,32,128]{2,1,0:T(8,128)(2,1)} %shard_map.160), calls=%async_computation.1 | async-start | bytes 524288 | tf_op jit(solution)/shard_map/all_to_all | solution.py:344
  59.2 7.1 %copy-start.4 = (f32[128,400]{0,1:T(8,128)S(1)}, f32[128,400]{0,1:T(8,128)}, u32[]{:S(2)}) copy-start(f32[128,400]{0,1:T(8,128)} %param.10) | copy-start | bytes 614404
  59.2 7.1 %copy-start.12 = (f32[128]{0:T(128)S(1)}, f32[128]{0:T(128)}, u32[]{:S(2)}) copy-start(f32[128]{0:T(128)} %param.11) | copy-start | bytes 1540
  59.2 10.5 %copy-start.10 = (f32[256]{0:T(256)S(1)}, f32[256]{0:T(256)}, u32[]{:S(2)}) copy-start(f32[256]{0:T(256)} %param.15) | copy-start | bytes 3076
  59.2 7.1 %collective-permute-start.10 = (bf16[400,128]{1,0:T(8,128)(2,1)S(1)}, bf16[400,128]{1,0:T(8,128)(2,1)S(1)}, u32[]{:S(2)}, u32[]{:S(2)}) collective-permute-start(bf16[400,128]{1,0:T(8,128)(2,1)S(1)} %get-tuple-element.45), channel_id=1, source_target_pairs={{0,2},{1,3},{2,0},{3,1},{4,6},{5,7},{6,4},{7,5},{8,10},{9,11},{10,... | collective-permute-start | bytes 307208 | tf_op jit(solution)/shard_map/ppermute | solution.py:264

commit v13 on v9

--- a/solution.py
+++ b/solution.py
@@ -15,9 +15,9 @@
 LANES = 128
 COST_JOIN_LOW = 6e9
 COST_JOIN_HIGH = 6e9
-COST_ADD = 6e9
+COST_UPDATE = 12e9
 COST_HIGH = 12e9
-COST_LOW = 6e9
+COST_LOW = 12e9
 COST_SUM = 1e9
 COST_MIDDLE = 6e9
 
@@ -209,7 +209,8 @@
             mine_ref[at, :] = piece
 
 
-def rest_body(q_ref, m_ref, g_ref, o_ref, ids_ref, right_ref, near_ref, far_ref, left_ref):
+def rest_body(q_ref, m_ref, g_ref, o_ref, ids_ref, low_ref, right_ref, low_out_ref, near_ref, far_ref, left_ref):
+    low_out_ref[...] = low_ref[...]
     right_ref[...] = dot(q_ref[...], m_ref[...], 1, 1).astype(BF)
     edges = q_ref.shape[1]
     step = step_of(edges)
@@ -277,13 +278,6 @@
     refs[-1][...] = total.astype(BF)
 
 
-def add_body(*refs):
-    total = refs[0][...].astype(F32)
-    for ref in refs[1:-1]:
-        total = total + ref[...].astype(F32)
-    refs[-1][...] = total
-
-
 def update_body(parts, *refs):
     part_refs, (table_ref, state_ref, new_ref, state_new_ref) = refs[:parts], refs[parts:]
     g = part_refs[0][...].astype(F32)
@@ -337,15 +331,13 @@
             scratch = [pltpu.VMEM(value.shape, F32), pltpu.SemaphoreType.DMA((parts,))]
             return call(cast_body, one_block, scratch, after=after, place=pl.ANY)(value)
 
-        right_bf = cast(right_t)
+        right_bf = right_t.astype(BF)
         near = [right_bf] + [swap_left(right_bf, 2 * k) for k in range(1, outer)]
         some = outer // 2
         cut = some * rows
         chunk = shape(width, cut, dtype=BF)
-        joined = call(join_body, chunk, flops=COST_JOIN_LOW)(*near[:some])
-        other_low = swap_left(joined, 1)
-        joined = call(join_body, chunk, flops=COST_JOIN_HIGH, after=(joined,))(*near[some:])
-        other_high = swap_left(joined, 1)
+        joined_low = call(join_body, chunk, flops=COST_JOIN_LOW)(*near[:some])
+        other_low = call(join_body, chunk, flops=COST_MIDDLE)(swap_left(joined_low, 1))
 
         ids = [source_ids, target_ids, relation_ids, negative_ids]
         longest = max(i.shape[-1] for i in ids)
@@ -354,14 +346,17 @@
         ids = lax.ppermute(ids, "right", [(i, (i - 1) % n_right) for i in range(n_right)])
         left_bf = cast(left_t)
         half_left = [left_bf] + [swap_right(left_bf, 2 * k) for k in range(1, far_right)]
-        half_joined = call(join_body, shape(width, far_right * rows, dtype=BF), after=(ids,))(*half_left)
-        sibling_left = swap_right(half_joined, 1)
         place = jnp.stack([here_r, here_l]).astype(jnp.int32)
         weight, relation_bf, ids = call(
             functools.partial(count_body, far_right, outer, rows, negative_ids.shape[-1]),
             (shape(groups, n_rows, LANES), shape(width, nrel, dtype=BF), shape(*ids.shape, dtype=jnp.int32)),
             here=place,
+            after=(joined_low,),
         )(ids, relation_t)
+        joined = call(join_body, chunk, flops=COST_JOIN_HIGH, after=(weight,))(*near[some:])
+        other_high = swap_left(joined, 1)
+        half_joined = call(join_body, shape(width, far_right * rows, dtype=BF), after=(joined,))(*half_left)
+        sibling_left = swap_right(half_joined, 1)
         moved = next_column(call(pack_body, shape(width + 8, rows), after=(joined,))(right_t, right_state[None, :]), 0)
 
         s, o, q = call(functools.partial(query_body, far_right), (table_bf, table_bf, table_bf))(
@@ -374,9 +369,7 @@
         )(*near, q, weight, ids)
         right_low, qg = call(
             functools.partial(middle_body, half), (chunk, shape(width, edges)), [pltpu.VMEM((cut, edges), BF)],
-            flops=COST_MIDDLE,
         )(other_low, q, weight, ids, qg)
-        got_low = swap_left(right_low, 1)
         tall = nrel // LANES * width
         size = -(-tall // (n_right * 16)) * 16
         piece = shape(size, LANES, dtype=BF)
@@ -391,46 +384,44 @@
         )(other_high, q, weight, ids, qg, s)
         left_rows = n_right * rows
         left_half = left_rows // 2
-        right_high, left_near, left_far = call(
+        right_high, right_low, left_near, left_far = call(
             rest_body,
-            (chunk, shape(width, left_half), shape(width, left_half, dtype=BF)),
+            (chunk, chunk, shape(width, left_half), shape(width, left_half, dtype=BF)),
             [pltpu.VMEM((width, left_rows), F32)],
-        )(q, m, g, o, ids)
-
-        got_high = swap_left(right_high, 1)
-        outs = (one_block,) * some
-        low = call(functools.partial(chunk_body, 0), outs, flops=COST_LOW)(right_near, got_low)
-        low = [next_column(block, 2 * k) for k, block in enumerate(low)]
-        low = call(add_body, shape(width, rows), flops=COST_ADD)(*low)
-        high = call(functools.partial(chunk_body, cut), outs, flops=COST_HIGH)(right_near, got_high)
-        high = [next_column(block, 2 * (some + k)) for k, block in enumerate(high)]
-        high = call(add_body, shape(width, rows), flops=COST_ADD)(*high)
-
-        left_own, *blocks = call(left_body, (shape(width, rows),) + (one_block,) * (far_right - 1))(
-            left_near, swap_right(left_far, 1)
-        )
-        left_got = [swap_right(block, 2 * (k + 1)) for k, block in enumerate(blocks)]
+        )(q, m, g, o, ids, right_low)
 
         mine, *rest = call(
-            piece_body, (shape(size, LANES),) + (piece,) * (far_right - 1), flops=COST_SUM, after=(got_low, right_high)
+            piece_body, (shape(size, LANES),) + (piece,) * (far_right - 1), flops=COST_SUM
         )(mine, swap_right(theirs, 1))
         got = [swap_right(p, 2 * (k + 1)) for k, p in enumerate(rest)]
         mine = call(sum_body, piece, flops=COST_SUM)(mine, *got)
         bit = 2
         while bit < n_left:
-            after = (low, left_own, got_high) if bit == 2 else ()
-            mine = call(sum_body, piece, flops=COST_SUM, after=after)(mine, swap_left(mine, bit))
+            mine = call(sum_body, piece, flops=COST_SUM)(mine, swap_left(mine, bit))
             bit *= 2
-        mine = call(sum_body, piece, flops=COST_SUM, after=(high, *left_got))(mine, swap_left(mine, 1))
+        mine = call(sum_body, piece, flops=COST_SUM)(mine, swap_left(mine, 1))
         pieces = [mine] + [swap_right(mine, 2 * k) for k in range(1, far_right)]
         sibling = swap_right(call(stack_body, shape(far_right * size, LANES, dtype=BF))(*pieces), 1)
+
+        left_own, *blocks = call(left_body, (shape(width, rows),) + (one_block,) * (far_right - 1))(
+            left_near, swap_right(left_far, 1)
+        )
+        left_got = [swap_right(block, 2 * (k + 1)) for k, block in enumerate(blocks)]
+
+        got_low = swap_left(right_low, 1)
+        got_high = swap_left(right_high, 1)
+        outs = (one_block,) * some
+        high = call(functools.partial(chunk_body, cut), outs, flops=COST_HIGH)(right_near, got_high)
+        low = call(functools.partial(chunk_body, 0), outs, flops=COST_LOW, after=left_got)(right_near, got_low)
+        right_got = [next_column(block, 2 * (some + k)) for k, block in enumerate(high)]
+        right_got += [next_column(block, 2 * k) for k, block in enumerate(low)]
 
         def update(got, table, state, flops=0):
             outs = (shape(width, rows), shape(1, rows))
             return call(functools.partial(update_body, len(got)), outs, flops=flops)(*got, table, state)
 
         left_new, left_state_new = update([left_own, *left_got], left_t, left_state[None, :])
-        right_new, right_state_new = update([low, high], moved, moved)
+        right_new, right_state_new = update(right_got, moved, moved, COST_UPDATE)
         relation_new, relation_state_new = call(
             functools.partial(relation_body, n_right), (shape(width, nrel), shape(1, nrel)), [all_pieces], me
         )(*pieces, sibling, relation_t, relation_state[None, :])

time: 63 us -> 56.1 us (0.89)
  waiting for transfers between devices: 16.6 us -> 7.42 us
  starting transfers between devices: 29.8 us -> 33.4 us
  local copies, waits for them, and re-layouts: 2.89 us -> 0.96 us
  other arithmetic: 0.83 us -> 1.78 us
    ppermute x5, waiting for transfers between devices: 6.18 us -> 0.1 us  [next_column(): return lax.ppermute(value, ('left', 'right'), perm)]
    ppermute x10, waiting for transfers between devices: 7.13 us -> 3.08 us  [swap_left(): return lax.ppermute(value, 'left', [(i, i ^ by) for i in range(n_left)])]
    ppermute x5, starting transfers between devices: 6.55 us -> 8.76 us  [next_column(): return lax.ppermute(value, ('left', 'right'), perm)]
    unnamed x18 -> x14, local copies, waits for them, and re-layouts: 2.89 us -> 0.96 us
    ppermute x8, starting transfers between devices: 6.84 us -> 8.73 us  [swap_right(): return lax.ppermute(value, 'right', [(i, i ^ by) for i in range(n_right)])]
    ppermute x8, waiting for transfers between devices: 3.28 us -> 4.24 us  [swap_right(): return lax.ppermute(value, 'right', [(i, i ^ by) for i in range(n_right)])]
    convert_element_type x0 -> x1, other arithmetic: none -> 0.94 us  [per_device(): right_bf = right_t.astype(BF)]
    pallas_call x26 -> x24, Pallas kernels: 11.6 us -> 11.4 us  [run(): pl.pallas_call(inner, out_shape=out_shape, in_specs=specs, scratch_shapes...]
  transfers between devices with their start and end apart: 24 -> 24, of which waited for: 8 -> 7; matrix products, arithmetic and copies ran while one was open for 1% -> 1% of each run, Pallas kernels for 17% -> 15%
where the time goes in v13:
time: 56.1 us; the launch traced here: 55.8 us
  starting transfers between devices  33.4 us (60%)
  Pallas kernels  11.4 us (20%)
  waiting for transfers between devices  7.42 us (13%)
  other arithmetic  1.78 us (3%)
  local copies, waits for them, and re-layouts  0.96 us (2%)
  between operations  0.87 us (2%)
    ppermute x10, starting transfers between devices, swap_left(): return lax.ppermute(value, 'left', [(i, i ^ by) for i in range(n_left)])  15.5 us
    pallas_call x24, Pallas kernels, run(): pl.pallas_call(inner, out_shape=out_shape, in_specs=specs, scratch_shapes...  11.4 us
    ppermute x5, starting transfers between devices, next_column(): return lax.ppermute(value, ('left', 'right'), perm)  8.76 us
    ppermute x8, starting transfers between devices, swap_right(): return lax.ppermute(value, 'right', [(i, i ^ by) for i in range(n_right)])  8.73 us
    ppermute x8, waiting for transfers between devices, swap_right(): return lax.ppermute(value, 'right', [(i, i ^ by) for i in range(n_right)])  4.24 us
    ppermute x10, waiting for transfers between devices, swap_left(): return lax.ppermute(value, 'left', [(i, i ^ by) for i in range(n_left)])  3.08 us
  transfers between devices with their start and end apart: 24, of which 7 were waited for; matrix products, arithmetic and copies ran while one was open for 1% of the time, Pallas kernels for 15%

profile of v13, /device:TPU:0, one launch (start us, length us, event | category | flops | bytes accessed | tf_op | source)
XLA Modules:
  0.0 55.8 jit_solution(629175155407683560)
XLA Ops:
  0.6 0.9 %bitcast_convert_fusion.refs_0_ = bf16[400,128]{1,0:T(8,128)(2,1)S(1)} fusion(f32[128,400]{0,1:T(8,128)} %param.12), kind=kLoop, calls=%fused_computation.2 | loop fusion | flops 51200 | bytes 307200 | tf_op jit(solution)/shard_map/convert_element_type | solution.py:334
  1.6 3.1 %collective-permute-start.4 = (bf16[400,128]{1,0:T(8,128)(2,1)S(1)}, bf16[400,128]{1,0:T(8,128)(2,1)S(1)}, u32[]{:S(2)}, u32[]{:S(2)}) collective-permute-start(bf16[400,128]{1,0:T(8,128)(2,1)S(1)} %bitcast_convert_fusion.refs_0_), channel_id=1, source_target_pairs={{0,8},{4,12},{8,0},{12,4},{16,24},{20,28},{24,16},{28,20},{1,9},{5... | collective-permute-start | bytes 307208 | tf_op jit(solution)/shard_map/ppermute | solution.py:300
  4.7 2.5 %collective-permute-start.2 = (bf16[400,128]{1,0:T(8,128)(2,1)S(1)}, bf16[400,128]{1,0:T(8,128)(2,1)S(1)}, u32[]{:S(2)}, u32[]{:S(2)}) collective-permute-start(bf16[400,128]{1,0:T(8,128)(2,1)S(1)} %bitcast_convert_fusion.refs_0_), channel_id=1, source_target_pairs={{0,24},{4,28},{8,16},{12,20},{16,8},{20,12},{24,0},{28,4},{1,25},{... | collective-permute-start | bytes 307208 | tf_op jit(solution)/shard_map/ppermute | solution.py:300
  7.1 0.1 collective-permute-start.1
  7.3 0.8 %pad_add_fusion = s32[5,1024]{1,0:T(8,128)S(1)} fusion(s32[2,1024]{1,0:T(2,128)} %bitcast.27, s32[1,1024]{1,0:T(1,128)} %bitcast.28, s32[1,1024]{1,0:T(1,128)} %bitcast.29, s32[1,1024]{1,0:T(1,128)} %bitcast.30), kind=kLoop, calls=%fused_computation | loop fusion | flops 15360 | bytes 40960 | tf_op jit(solution)/shard_map/concatenate | solution.py:345
  8.0 0.4 collective-permute-start.3
  8.4 0.9 %copy-done.1 = f32[128,400]{0,1:T(8,128)S(1)} copy-done((f32[128,400]{0,1:T(8,128)S(1)}, f32[128,400]{0,1:T(8,128)}, u32[]{:S(2)}) %copy-start.1) | copy-done | bytes 204824
  9.4 0.3 shard_map.145.refs_0_
  9.7 1.2 %collective-permute-start = (bf16[400,128]{1,0:T(8,128)(2,1)S(1)}, bf16[400,128]{1,0:T(8,128)(2,1)S(1)}, u32[]{:S(2)}, u32[]{:S(2)}) collective-permute-start(bf16[400,128]{1,0:T(8,128)(2,1)S(1)} %shard_map.145.refs_0_), channel_id=1, source_target_pairs={{0,2},{1,3},{2,0},{3,1},{4,6},{5,7},{6,4},{7,5},{8,10},{9,11},{10,... | collective-permute-start | bytes 307208 | tf_op jit(solution)/shard_map/ppermute | solution.py:303
  10.9 0.1 pad_add_fusion.1.refs_2_
  11.0 1.6 %collective-permute-start.7 = (bf16[400,256]{1,0:T(8,128)(2,1)S(1)}, bf16[400,256]{1,0:T(8,128)(2,1)S(1)}, u32[]{:S(2)}, u32[]{:S(2)}) collective-permute-start(bf16[400,256]{1,0:T(8,128)(2,1)S(1)} %shard_map.146.refs_3_), channel_id=1, source_target_pairs={{0,4},{4,0},{8,12},{12,8},{16,20},{20,16},{24,28},{28,24},{1,5},{5... | collective-permute-start | bytes 614408 | tf_op jit(solution)/shard_map/ppermute | solution.py:300
  12.6 1.6 %shard_map.147 = (f32[2,1024,128]{2,1,0:T(8,128)S(1)}, bf16[400,256]{1,0:T(8,128)(2,1)S(1)}, s32[5,1024]{1,0:T(8,128)S(1)}) custom-call(s32[5,1024]{1,0:T(8,128)S(1)} %collective-permute-done.3.refs_0_, f32[400,256]{1,0:T(8,128)S(1)} %bitcast.19, s32[2]{0:T(128)S(1)} %pad_add_fusion.1.refs_2_, bf16[400,256]{1,0:T(8,128)(2,1)S(1)} %shard_map.146.refs_3_), custom_call_target="tpu_custom_call" | custom-call | tf_op jit(solution)/shard_map/pallas_call | solution.py:53
  14.2 2.3 %collective-permute-done.1.refs_0_.refs_2_ = bf16[400,128]{1,0:T(8,128)(2,1)S(1)} collective-permute-done((bf16[400,128]{1,0:T(8,128)(2,1)S(1)}, bf16[400,128]{1,0:T(8,128)(2,1)S(1)}, u32[]{:S(2)}, u32[]{:S(2)}) %collective-permute-start.1) | collective-permute-done | bytes 102432 | tf_op jit(solution)/shard_map/ppermute | solution.py:300
  16.5 1.6 %collective-permute-start.6 = (bf16[400,256]{1,0:T(8,128)(2,1)S(1)}, bf16[400,256]{1,0:T(8,128)(2,1)S(1)}, u32[]{:S(2)}, u32[]{:S(2)}) collective-permute-start(bf16[400,256]{1,0:T(8,128)(2,1)S(1)} %shard_map.148.refs_2_), channel_id=1, source_target_pairs={{0,4},{4,0},{8,12},{12,8},{16,20},{20,16},{24,28},{28,24},{1,5},{5... | collective-permute-start | bytes 614408 | tf_op jit(solution)/shard_map/ppermute | solution.py:300
  18.1 0.1 collective-permute-start.5
  18.2 0.5 collective-permute-start.8
  18.8 0.8 %collective-permute-done.5.refs_2_ = bf16[400,256]{1,0:T(8,128)(2,1)S(1)} collective-permute-done((bf16[400,256]{1,0:T(8,128)(2,1)S(1)}, bf16[400,256]{1,0:T(8,128)(2,1)S(1)}, u32[]{:S(2)}, u32[]{:S(2)}) %collective-permute-start.5) | collective-permute-done | bytes 204832 | tf_op jit(solution)/shard_map/ppermute | solution.py:303
  19.6 0.9 %shard_map.150 = (bf16[400,1024]{1,0:T(8,128)(2,1)S(1)}, bf16[400,1024]{1,0:T(8,128)(2,1)S(1)}, bf16[400,1024]{1,0:T(8,128)(2,1)S(1)}) custom-call(bf16[400,128]{1,0:T(8,128)(2,1)S(1)} %shard_map.145.refs_0_, bf16[400,128]{1,0:T(8,128)(2,1)S(1)} %collective-permute-done.refs_1_, bf16[400,256]{1,0:T(8,128)(2,1)S(1)} %collective-permute-done.5.refs_2_, ...), custom_call_target="tpu_custom_call" | custom-call | tf_op jit(solution)/shard_map/pallas_call | solution.py:53
  20.6 1.8 %shard_map.152 = (f32[400,512]{1,0:T(8,128)S(1)}, f32[400,1024]{1,0:T(8,128)S(1)}) custom-call(bf16[400,128]{1,0:T(8,128)(2,1)S(1)} %bitcast_convert_fusion.refs_0_, bf16[400,128]{1,0:T(8,128)(2,1)S(1)} %collective-permute-done.4.refs_1_, bf16[400,128]{1,0:T(8,128)(2,1)S(1)} %collective-permute-done.1.refs_0_.refs_2_, ...), custom_call_target="tpu_custom_call" | custom-call | tf_op jit(solution)/shard_map/pallas_call | solution.py:53
  22.4 1.0 %shard_map.153 = (bf16[400,256]{1,0:T(8,128)(2,1)S(1)}, f32[400,1024]{1,0:T(8,128)S(1)}) custom-call(bf16[400,256]{1,0:T(8,128)(2,1)S(1)} %shard_map.151.rows_ref, bf16[400,1024]{1,0:T(8,128)(2,1)S(1)} %get-tuple-element.41.refs_4_.q_ref.refs_1_, f32[2,1024,128]{2,1,0:T(8,128)S(1)} %get-tuple-element.38.refs_2_.refs_5_.weight_ref, ...), custom_call_target="tpu_custom_call" | custom-call | tf_op jit(solution)/shard_map/pallas_call | solution.py:53
  23.4 0.1 collective-permute-done.8.refs_7_.refs_4_.refs_5_
  23.5 1.9 %shard_map.155 = (bf16[256,1024]{1,0:T(8,128)(2,1)S(1)}, f32[400,1024]{1,0:T(8,128)S(1)}, f32[416,128]{1,0:T(8,128)S(1)}, bf16[416,128]{1,0:T(8,128)(2,1)S(1)}) custom-call(bf16[400,256]{1,0:T(8,128)(2,1)S(1)} %collective-permute-done.6.refs_0_, bf16[400,1024]{1,0:T(8,128)(2,1)S(1)} %get-tuple-element.41.refs_4_.q_ref.refs_1_, ...), custom_call_target="tpu_custom_call" | custom-call | tf_op jit(solution)/shard_map/pallas_call | solution.py:53
  25.4 0.3 collective-permute-start.17
  25.7 1.0 %shard_map.156 = (bf16[400,256]{1,0:T(8,128)(2,1)S(1)}, bf16[400,256]{1,0:T(8,128)(2,1)S(1)}, f32[400,256]{1,0:T(8,128)S(1)}, bf16[400,256]{1,0:T(8,128)(2,1)S(1)}) custom-call(bf16[400,1024]{1,0:T(8,128)(2,1)S(1)} %get-tuple-element.41.refs_4_.q_ref.refs_1_, bf16[256,1024]{1,0:T(8,128)(2,1)S(1)} %get-tuple-element.45.m_ref, ...), custom_call_target="tpu_custom_call" | custom-call | tf_op jit(solution)/shard_map/pallas_call | solution.py:53
  26.7 0.3 collective-permute-start.9
  27.1 1.6 %collective-permute-start.18 = (bf16[208,128]{1,0:T(8,128)(2,1)S(1)}, bf16[208,128]{1,0:T(8,128)(2,1)S(1)}, u32[]{:S(2)}, u32[]{:S(2)}) collective-permute-start(bf16[208,128]{1,0:T(8,128)(2,1)S(1)} %get-tuple-element.67), channel_id=1, source_target_pairs={{0,2},{1,3},{2,0},{3,1},{4,6},{5,7},{6,4},{7,5},{8,10},{9,11},{10,... | collective-permute-start | bytes 159752 | tf_op jit(solution)/shard_map/ppermute | solution.py:303
  28.6 1.1 %collective-permute-start.11 = (bf16[400,256]{1,0:T(8,128)(2,1)S(1)}, bf16[400,256]{1,0:T(8,128)(2,1)S(1)}, u32[]{:S(2)}, u32[]{:S(2)}) collective-permute-start(bf16[400,256]{1,0:T(8,128)(2,1)S(1)} %get-tuple-element.56), channel_id=1, source_target_pairs={{0,4},{4,0},{8,12},{12,8},{16,20},{20,16},{24,28},{28,24},{1,5},{5... | collective-permute-start | bytes 614408 | tf_op jit(solution)/shard_map/ppermute | solution.py:300
  29.7 1.6 %collective-permute-done.18.refs_1_ = bf16[208,128]{1,0:T(8,128)(2,1)S(1)} collective-permute-done((bf16[208,128]{1,0:T(8,128)(2,1)S(1)}, bf16[208,128]{1,0:T(8,128)(2,1)S(1)}, u32[]{:S(2)}, u32[]{:S(2)}) %collective-permute-start.18) | collective-permute-done | bytes 53280 | tf_op jit(solution)/shard_map/ppermute | solution.py:303
  31.3 1.2 %collective-permute-start.19 = (bf16[208,128]{1,0:T(8,128)(2,1)S(1)}, bf16[208,128]{1,0:T(8,128)(2,1)S(1)}, u32[]{:S(2)}, u32[]{:S(2)}) collective-permute-start(bf16[208,128]{1,0:T(8,128)(2,1)S(1)} %shard_map.163.refs_0_), channel_id=1, source_target_pairs={{0,8},{4,12},{8,0},{12,4},{16,24},{20,28},{24,16},{28,20},{1,9},{5... | collective-permute-start | bytes 159752 | tf_op jit(solution)/shard_map/ppermute | solution.py:300
  32.5 1.5 %collective-permute-start.14 = (bf16[400,256]{1,0:T(8,128)(2,1)S(1)}, bf16[400,256]{1,0:T(8,128)(2,1)S(1)}, u32[]{:S(2)}, u32[]{:S(2)}) collective-permute-start(bf16[400,256]{1,0:T(8,128)(2,1)S(1)} %get-tuple-element.59), channel_id=1, source_target_pairs={{0,4},{4,0},{8,12},{12,8},{16,20},{20,16},{24,28},{28,24},{1,5},{5... | collective-permute-start | bytes 614408 | tf_op jit(solution)/shard_map/ppermute | solution.py:300
  34.0 0.7 %collective-permute-start.10 = (bf16[400,128]{1,0:T(8,128)(2,1)S(1)}, bf16[400,128]{1,0:T(8,128)(2,1)S(1)}, u32[]{:S(2)}, u32[]{:S(2)}) collective-permute-start(bf16[400,128]{1,0:T(8,128)(2,1)S(1)} %get-tuple-element.52), channel_id=1, source_target_pairs={{0,2},{1,3},{2,0},{3,1},{4,6},{5,7},{6,4},{7,5},{8,10},{9,11},{10,... | collective-permute-start | bytes 307208 | tf_op jit(solution)/shard_map/ppermute | solution.py:303
  34.7 0.8 %collective-permute-done.19.refs_1_ = bf16[208,128]{1,0:T(8,128)(2,1)S(1)} collective-permute-done((bf16[208,128]{1,0:T(8,128)(2,1)S(1)}, bf16[208,128]{1,0:T(8,128)(2,1)S(1)}, u32[]{:S(2)}, u32[]{:S(2)}) %collective-permute-start.19) | collective-permute-done | bytes 53280 | tf_op jit(solution)/shard_map/ppermute | solution.py:300
  35.5 2.2 %collective-permute-start.20 = (bf16[208,128]{1,0:T(8,128)(2,1)S(1)}, bf16[208,128]{1,0:T(8,128)(2,1)S(1)}, u32[]{:S(2)}, u32[]{:S(2)}) collective-permute-start(bf16[208,128]{1,0:T(8,128)(2,1)S(1)} %shard_map.164.refs_0_), channel_id=1, source_target_pairs={{0,16},{4,20},{8,24},{12,28},{16,0},{20,4},{24,8},{28,12},{1,17},{... | collective-permute-start | bytes 159752 | tf_op jit(solution)/shard_map/ppermute | solution.py:300
  37.7 0.1 shard_map.159
  37.8 0.1 collective-permute-start.12
  37.8 4.1 %collective-permute-start.13 = (bf16[400,128]{1,0:T(8,128)(2,1)S(1)}, bf16[400,128]{1,0:T(8,128)(2,1)S(1)}, u32[]{:S(2)}, u32[]{:S(2)}) collective-permute-start(bf16[400,128]{1,0:T(8,128)(2,1)S(1)} %get-tuple-element.58), channel_id=1, source_target_pairs={{0,25},{1,26},{2,27},{3,24},{4,29},{5,30},{6,31},{7,28},{8,17},{9,... | collective-permute-start | bytes 307208 | tf_op jit(solution)/shard_map/ppermute | solution.py:310
  41.9 0.7 %collective-permute-start.21 = (bf16[208,128]{1,0:T(8,128)(2,1)S(1)}, bf16[208,128]{1,0:T(8,128)(2,1)S(1)}, u32[]{:S(2)}, u32[]{:S(2)}) collective-permute-start(bf16[208,128]{1,0:T(8,128)(2,1)S(1)} %shard_map.165.refs_0_), channel_id=1, source_target_pairs={{0,4},{4,0},{8,12},{12,8},{16,20},{20,16},{24,28},{28,24},{1,5},{5... | collective-permute-start | bytes 159752 | tf_op jit(solution)/shard_map/ppermute | solution.py:300
  42.7 0.1 shard_map.160
  42.8 0.1 collective-permute-start.15
  42.8 0.0 copy-start.2
  42.8 4.0 %collective-permute-start.16 = (bf16[400,128]{1,0:T(8,128)(2,1)S(1)}, bf16[400,128]{1,0:T(8,128)(2,1)S(1)}, u32[]{:S(2)}, u32[]{:S(2)}) collective-permute-start(bf16[400,128]{1,0:T(8,128)(2,1)S(1)} %get-tuple-element.61), channel_id=1, source_target_pairs={{0,9},{1,10},{2,11},{3,8},{4,13},{5,14},{6,15},{7,12},{8,1},{9,2},... | collective-permute-start | bytes 307208 | tf_op jit(solution)/shard_map/ppermute | solution.py:310
  46.9 4.5 %collective-permute-start.22 = (bf16[208,128]{1,0:T(8,128)(2,1)S(1)}, bf16[208,128]{1,0:T(8,128)(2,1)S(1)}, u32[]{:S(2)}, u32[]{:S(2)}) collective-permute-start(bf16[208,128]{1,0:T(8,128)(2,1)S(1)} %shard_map.166.refs_0_), channel_id=1, source_target_pairs={{0,2},{1,3},{2,0},{3,1},{4,6},{5,7},{6,4},{7,5},{8,10},{9,11},{10,... | collective-permute-start | bytes 159752 | tf_op jit(solution)/shard_map/ppermute | solution.py:303
  51.4 0.8 %shard_map.158 = (f32[400,128]{1,0:T(8,128)}, f32[1,128]{1,0:T(1,128)}) custom-call(f32[400,128]{1,0:T(8,128)S(1)} %get-tuple-element.51.refs_0_, bf16[400,128]{1,0:T(8,128)(2,1)S(1)} %collective-permute-done.10.refs_1_.refs_2_, f32[400,128]{1,0:T(8,128)S(1)} %bitcast.22, f32[1,128]{1,0:T(1,128)S(1)} %bitcast.25), custom_call_target="tpu_custom_call" | custom-call | tf_op jit(solution)/shard_map/pallas_call | solution.py:53
  52.2 1.3 %collective-permute-done.22.refs_1_ = bf16[208,128]{1,0:T(8,128)(2,1)S(1)} collective-permute-done((bf16[208,128]{1,0:T(8,128)(2,1)S(1)}, bf16[208,128]{1,0:T(8,128)(2,1)S(1)}, u32[]{:S(2)}, u32[]{:S(2)}) %collective-permute-start.22) | collective-permute-done | bytes 53280 | tf_op jit(solution)/shard_map/ppermute | solution.py:303
  53.5 0.1 collective-permute-start.23
  53.7 0.8 %shard_map.161 = (f32[400,128]{1,0:T(8,128)}, f32[1,128]{1,0:T(1,128)}) custom-call(bf16[400,128]{1,0:T(8,128)(2,1)S(1)} %collective-permute-done.12.refs_0_, bf16[400,128]{1,0:T(8,128)(2,1)S(1)} %collective-permute-done.13.refs_1_, bf16[400,128]{1,0:T(8,128)(2,1)S(1)} %collective-permute-done.15.refs_2_, ...), custom_call_target="tpu_custom_call" | custom-call | flops 12000000000 | tf_op jit(solution)/shard_map/pallas_call | solution.py:53
  54.5 0.5 collective-permute-done.23.refs_2_
  54.9 0.9 %shard_map.168 = (f32[400,256]{1,0:T(8,128)}, f32[1,256]{1,0:T(1,128)}) custom-call(bf16[208,128]{1,0:T(8,128)(2,1)S(1)} %shard_map.166.refs_0_, bf16[208,128]{1,0:T(8,128)(2,1)S(1)} %collective-permute-done.22.refs_1_, bf16[416,128]{1,0:T(8,128)(2,1)S(1)} %collective-permute-done.23.refs_2_, f32[400,256]{1,0:T(8,128)S(1)} %bitcast.20, ...), custom_call_target="tpu_custom_call" | custom-call | tf_op jit(solution)/shard_map/pallas_call | solution.py:53
  (41 shorter events, 0.4 us)
Async XLA Ops:
  1.6 9.4 %collective-permute-start.4 = (bf16[400,128]{1,0:T(8,128)(2,1)S(1)}, bf16[400,128]{1,0:T(8,128)(2,1)S(1)}, u32[]{:S(2)}, u32[]{:S(2)}) collective-permute-start(bf16[400,128]{1,0:T(8,128)(2,1)S(1)} %bitcast_convert_fusion.refs_0_), channel_id=1, source_target_pairs={{0,8},{4,12},{8,0},{12,4},{16,24},{20,28},{24,16},{28,20},{1,9},{5... | collective-permute-start | bytes 307208 | tf_op jit(solution)/shard_map/ppermute | solution.py:300
  4.7 9.5 %collective-permute-start.2 = (bf16[400,128]{1,0:T(8,128)(2,1)S(1)}, bf16[400,128]{1,0:T(8,128)(2,1)S(1)}, u32[]{:S(2)}, u32[]{:S(2)}) collective-permute-start(bf16[400,128]{1,0:T(8,128)(2,1)S(1)} %bitcast_convert_fusion.refs_0_), channel_id=1, source_target_pairs={{0,24},{4,28},{8,16},{12,20},{16,8},{20,12},{24,0},{28,4},{1,25},{... | collective-permute-start | bytes 307208 | tf_op jit(solution)/shard_map/ppermute | solution.py:300
  7.1 9.3 %collective-permute-start.1 = (bf16[400,128]{1,0:T(8,128)(2,1)S(1)}, bf16[400,128]{1,0:T(8,128)(2,1)S(1)}, u32[]{:S(2)}, u32[]{:S(2)}) collective-permute-start(bf16[400,128]{1,0:T(8,128)(2,1)S(1)} %bitcast_convert_fusion.refs_0_), channel_id=1, source_target_pairs={{0,16},{4,20},{8,24},{12,28},{16,0},{20,4},{24,8},{28,12},{1,17},{... | collective-permute-start | bytes 307208 | tf_op jit(solution)/shard_map/ppermute | solution.py:300
  8.0 4.6 %collective-permute-start.3 = (s32[5,1024]{1,0:T(8,128)S(1)}, s32[5,1024]{1,0:T(8,128)S(1)}, u32[]{:S(2)}, u32[]{:S(2)}) collective-permute-start(s32[5,1024]{1,0:T(8,128)S(1)} %pad_add_fusion), channel_id=1, source_target_pairs={{0,3},{1,0},{2,1},{3,2},{4,7},{5,4},{6,5},{7,6},{8,11},{9,8},{10,9... | collective-permute-start | bytes 61448 | tf_op jit(solution)/shard_map/ppermute | solution.py:346
  8.4 0.9 %copy-start.1 = (f32[128,400]{0,1:T(8,128)S(1)}, f32[128,400]{0,1:T(8,128)}, u32[]{:S(2)}) copy-start(f32[128,400]{0,1:T(8,128)} %param.10) | copy-start | bytes 614404
  9.7 8.4 %collective-permute-start = (bf16[400,128]{1,0:T(8,128)(2,1)S(1)}, bf16[400,128]{1,0:T(8,128)(2,1)S(1)}, u32[]{:S(2)}, u32[]{:S(2)}) collective-permute-start(bf16[400,128]{1,0:T(8,128)(2,1)S(1)} %shard_map.145.refs_0_), channel_id=1, source_target_pairs={{0,2},{1,3},{2,0},{3,1},{4,6},{5,7},{6,4},{7,5},{8,10},{9,11},{10,... | collective-permute-start | bytes 307208 | tf_op jit(solution)/shard_map/ppermute | solution.py:303
  11.0 1.6 %copy-start = (f32[256,400]{0,1:T(8,128)S(1)}, f32[256,400]{0,1:T(8,128)}, u32[]{:S(2)}) copy-start(f32[256,400]{0,1:T(8,128)} %param.14) | copy-start | bytes 1228804
  11.0 7.8 %collective-permute-start.7 = (bf16[400,256]{1,0:T(8,128)(2,1)S(1)}, bf16[400,256]{1,0:T(8,128)(2,1)S(1)}, u32[]{:S(2)}, u32[]{:S(2)}) collective-permute-start(bf16[400,256]{1,0:T(8,128)(2,1)S(1)} %shard_map.146.refs_3_), channel_id=1, source_target_pairs={{0,4},{4,0},{8,12},{12,8},{16,20},{20,16},{24,28},{28,24},{1,5},{5... | collective-permute-start | bytes 614408 | tf_op jit(solution)/shard_map/ppermute | solution.py:300
  16.4 1.8 %copy-start.3 = (f32[128,400]{0,1:T(8,128)S(1)}, f32[128,400]{0,1:T(8,128)}, u32[]{:S(2)}) copy-start(f32[128,400]{0,1:T(8,128)} %param.12) | copy-start | bytes 614404
  16.4 1.8 %copy-start.6 = (f32[128]{0:T(128)S(1)}, f32[128]{0:T(128)}, u32[]{:S(2)}) copy-start(f32[128]{0:T(128)} %param.13) | copy-start | bytes 1540
  16.5 6.9 %collective-permute-start.6 = (bf16[400,256]{1,0:T(8,128)(2,1)S(1)}, bf16[400,256]{1,0:T(8,128)(2,1)S(1)}, u32[]{:S(2)}, u32[]{:S(2)}) collective-permute-start(bf16[400,256]{1,0:T(8,128)(2,1)S(1)} %shard_map.148.refs_2_), channel_id=1, source_target_pairs={{0,4},{4,0},{8,12},{12,8},{16,20},{20,16},{24,28},{28,24},{1,5},{5... | collective-permute-start | bytes 614408 | tf_op jit(solution)/shard_map/ppermute | solution.py:300
  18.1 1.5 %collective-permute-start.5 = (bf16[400,256]{1,0:T(8,128)(2,1)S(1)}, bf16[400,256]{1,0:T(8,128)(2,1)S(1)}, u32[]{:S(2)}, u32[]{:S(2)}) collective-permute-start(bf16[400,256]{1,0:T(8,128)(2,1)S(1)} %shard_map.149), channel_id=1, source_target_pairs={{0,1},{1,0},{2,3},{3,2},{4,5},{5,4},{6,7},{7,6},{8,9},{9,8},{10,11... | collective-permute-start | bytes 614408 | tf_op jit(solution)/shard_map/ppermute | solution.py:303
  18.2 5.3 %collective-permute-start.8 = (f32[408,128]{1,0:T(8,128)S(1)}, f32[408,128]{1,0:T(8,128)S(1)}, u32[]{:S(2)}, u32[]{:S(2)}) collective-permute-start(f32[408,128]{1,0:T(8,128)S(1)} %shard_map.154), channel_id=1, source_target_pairs={{0,1},{1,2},{2,3},{3,0},{4,5},{5,6},{6,7},{7,4},{8,9},{9,10},{10,1... | collective-permute-start | bytes 626696 | tf_op jit(solution)/shard_map/ppermute | solution.py:310
  25.4 1.6 %collective-permute-start.17 = (bf16[416,128]{1,0:T(8,128)(2,1)S(1)}, bf16[416,128]{1,0:T(8,128)(2,1)S(1)}, u32[]{:S(2)}, u32[]{:S(2)}) collective-permute-start(bf16[416,128]{1,0:T(8,128)(2,1)S(1)} %get-tuple-element.65), channel_id=1, source_target_pairs={{0,1},{1,0},{2,3},{3,2},{4,5},{5,4},{6,7},{7,6},{8,9},{9,8},{10,11... | collective-permute-start | bytes 319496 | tf_op jit(solution)/shard_map/ppermute | solution.py:303
  26.7 7.3 %collective-permute-start.9 = (bf16[400,256]{1,0:T(8,128)(2,1)S(1)}, bf16[400,256]{1,0:T(8,128)(2,1)S(1)}, u32[]{:S(2)}, u32[]{:S(2)}) collective-permute-start(bf16[400,256]{1,0:T(8,128)(2,1)S(1)} %get-tuple-element.50), channel_id=1, source_target_pairs={{0,1},{1,0},{2,3},{3,2},{4,5},{5,4},{6,7},{7,6},{8,9},{9,8},{10,11... | collective-permute-start | bytes 614408 | tf_op jit(solution)/shard_map/ppermute | solution.py:303
  27.1 4.2 %collective-permute-start.18 = (bf16[208,128]{1,0:T(8,128)(2,1)S(1)}, bf16[208,128]{1,0:T(8,128)(2,1)S(1)}, u32[]{:S(2)}, u32[]{:S(2)}) collective-permute-start(bf16[208,128]{1,0:T(8,128)(2,1)S(1)} %get-tuple-element.67), channel_id=1, source_target_pairs={{0,2},{1,3},{2,0},{3,1},{4,6},{5,7},{6,4},{7,5},{8,10},{9,11},{10,... | collective-permute-start | bytes 159752 | tf_op jit(solution)/shard_map/ppermute | solution.py:303
  28.6 9.1 %collective-permute-start.11 = (bf16[400,256]{1,0:T(8,128)(2,1)S(1)}, bf16[400,256]{1,0:T(8,128)(2,1)S(1)}, u32[]{:S(2)}, u32[]{:S(2)}) collective-permute-start(bf16[400,256]{1,0:T(8,128)(2,1)S(1)} %get-tuple-element.56), channel_id=1, source_target_pairs={{0,4},{4,0},{8,12},{12,8},{16,20},{20,16},{24,28},{28,24},{1,5},{5... | collective-permute-start | bytes 614408 | tf_op jit(solution)/shard_map/ppermute | solution.py:300
  31.3 4.2 %collective-permute-start.19 = (bf16[208,128]{1,0:T(8,128)(2,1)S(1)}, bf16[208,128]{1,0:T(8,128)(2,1)S(1)}, u32[]{:S(2)}, u32[]{:S(2)}) collective-permute-start(bf16[208,128]{1,0:T(8,128)(2,1)S(1)} %shard_map.163.refs_0_), channel_id=1, source_target_pairs={{0,8},{4,12},{8,0},{12,4},{16,24},{20,28},{24,16},{28,20},{1,9},{5... | collective-permute-start | bytes 159752 | tf_op jit(solution)/shard_map/ppermute | solution.py:300
  32.5 10.2 %collective-permute-start.14 = (bf16[400,256]{1,0:T(8,128)(2,1)S(1)}, bf16[400,256]{1,0:T(8,128)(2,1)S(1)}, u32[]{:S(2)}, u32[]{:S(2)}) collective-permute-start(bf16[400,256]{1,0:T(8,128)(2,1)S(1)} %get-tuple-element.59), channel_id=1, source_target_pairs={{0,4},{4,0},{8,12},{12,8},{16,20},{20,16},{24,28},{28,24},{1,5},{5... | collective-permute-start | bytes 614408 | tf_op jit(solution)/shard_map/ppermute | solution.py:300
  34.0 8.7 %collective-permute-start.10 = (bf16[400,128]{1,0:T(8,128)(2,1)S(1)}, bf16[400,128]{1,0:T(8,128)(2,1)S(1)}, u32[]{:S(2)}, u32[]{:S(2)}) collective-permute-start(bf16[400,128]{1,0:T(8,128)(2,1)S(1)} %get-tuple-element.52), channel_id=1, source_target_pairs={{0,2},{1,3},{2,0},{3,1},{4,6},{5,7},{6,4},{7,5},{8,10},{9,11},{10,... | collective-permute-start | bytes 307208 | tf_op jit(solution)/shard_map/ppermute | solution.py:303
  35.5 6.4 %collective-permute-start.20 = (bf16[208,128]{1,0:T(8,128)(2,1)S(1)}, bf16[208,128]{1,0:T(8,128)(2,1)S(1)}, u32[]{:S(2)}, u32[]{:S(2)}) collective-permute-start(bf16[208,128]{1,0:T(8,128)(2,1)S(1)} %shard_map.164.refs_0_), channel_id=1, source_target_pairs={{0,16},{4,20},{8,24},{12,28},{16,0},{20,4},{24,8},{28,12},{1,17},{... | collective-permute-start | bytes 159752 | tf_op jit(solution)/shard_map/ppermute | solution.py:300
  37.8 15.9 %collective-permute-start.12 = (bf16[400,128]{1,0:T(8,128)(2,1)S(1)}, bf16[400,128]{1,0:T(8,128)(2,1)S(1)}, u32[]{:S(2)}, u32[]{:S(2)}) collective-permute-start(bf16[400,128]{1,0:T(8,128)(2,1)S(1)} %get-tuple-element.57), channel_id=1, source_target_pairs={{0,17},{1,18},{2,19},{3,16},{4,21},{5,22},{6,23},{7,20},{8,25},{9,... | collective-permute-start | bytes 307208 | tf_op jit(solution)/shard_map/ppermute | solution.py:310
  37.8 15.8 %collective-permute-start.13 = (bf16[400,128]{1,0:T(8,128)(2,1)S(1)}, bf16[400,128]{1,0:T(8,128)(2,1)S(1)}, u32[]{:S(2)}, u32[]{:S(2)}) collective-permute-start(bf16[400,128]{1,0:T(8,128)(2,1)S(1)} %get-tuple-element.58), channel_id=1, source_target_pairs={{0,25},{1,26},{2,27},{3,24},{4,29},{5,30},{6,31},{7,28},{8,17},{9,... | collective-permute-start | bytes 307208 | tf_op jit(solution)/shard_map/ppermute | solution.py:310
  41.9 4.9 %collective-permute-start.21 = (bf16[208,128]{1,0:T(8,128)(2,1)S(1)}, bf16[208,128]{1,0:T(8,128)(2,1)S(1)}, u32[]{:S(2)}, u32[]{:S(2)}) collective-permute-start(bf16[208,128]{1,0:T(8,128)(2,1)S(1)} %shard_map.165.refs_0_), channel_id=1, source_target_pairs={{0,4},{4,0},{8,12},{12,8},{16,20},{20,16},{24,28},{28,24},{1,5},{5... | collective-permute-start | bytes 159752 | tf_op jit(solution)/shard_map/ppermute | solution.py:300
  42.8 10.9 %collective-permute-start.15 = (bf16[400,128]{1,0:T(8,128)(2,1)S(1)}, bf16[400,128]{1,0:T(8,128)(2,1)S(1)}, u32[]{:S(2)}, u32[]{:S(2)}) collective-permute-start(bf16[400,128]{1,0:T(8,128)(2,1)S(1)} %get-tuple-element.60), channel_id=1, source_target_pairs={{0,1},{1,2},{2,3},{3,0},{4,5},{5,6},{6,7},{7,4},{8,9},{9,10},{10,1... | collective-permute-start | bytes 307208 | tf_op jit(solution)/shard_map/ppermute | solution.py:310
  42.8 8.6 %copy-start.2 = (f32[128,400]{0,1:T(8,128)S(1)}, f32[128,400]{0,1:T(8,128)}, u32[]{:S(2)}) copy-start(f32[128,400]{0,1:T(8,128)} %param.10) | copy-start | bytes 614404
  42.8 8.6 %copy-start.5 = (f32[128]{0:T(128)S(1)}, f32[128]{0:T(128)}, u32[]{:S(2)}) copy-start(f32[128]{0:T(128)} %param.11) | copy-start | bytes 1540
  42.8 10.8 %collective-permute-start.16 = (bf16[400,128]{1,0:T(8,128)(2,1)S(1)}, bf16[400,128]{1,0:T(8,128)(2,1)S(1)}, u32[]{:S(2)}, u32[]{:S(2)}) collective-permute-start(bf16[400,128]{1,0:T(8,128)(2,1)S(1)} %get-tuple-element.61), channel_id=1, source_target_pairs={{0,9},{1,10},{2,11},{3,8},{4,13},{5,14},{6,15},{7,12},{8,1},{9,2},... | collective-permute-start | bytes 307208 | tf_op jit(solution)/shard_map/ppermute | solution.py:310
  46.9 6.6 %collective-permute-start.22 = (bf16[208,128]{1,0:T(8,128)(2,1)S(1)}, bf16[208,128]{1,0:T(8,128)(2,1)S(1)}, u32[]{:S(2)}, u32[]{:S(2)}) collective-permute-start(bf16[208,128]{1,0:T(8,128)(2,1)S(1)} %shard_map.166.refs_0_), channel_id=1, source_target_pairs={{0,2},{1,3},{2,0},{3,1},{4,6},{5,7},{6,4},{7,5},{8,10},{9,11},{10,... | collective-permute-start | bytes 159752 | tf_op jit(solution)/shard_map/ppermute | solution.py:303
  53.5 1.4 %copy-start.4 = (f32[256]{0:T(256)S(1)}, f32[256]{0:T(256)}, u32[]{:S(2)}) copy-start(f32[256]{0:T(256)} %param.15) | copy-start | bytes 3076
  53.5 1.4 %collective-permute-start.23 = (bf16[416,128]{1,0:T(8,128)(2,1)S(1)}, bf16[416,128]{1,0:T(8,128)(2,1)S(1)}, u32[]{:S(2)}, u32[]{:S(2)}) collective-permute-start(bf16[416,128]{1,0:T(8,128)(2,1)S(1)} %shard_map.167), channel_id=1, source_target_pairs={{0,1},{1,0},{2,3},{3,2},{4,5},{5,4},{6,7},{7,6},{8,9},{9,8},{10,11... | collective-permute-start | bytes 319496 | tf_op jit(solution)/shard_map/ppermute | solution.py:303

commit v14 on v13

--- a/solution.py
+++ b/solution.py
@@ -15,11 +15,11 @@
 LANES = 128
 COST_JOIN_LOW = 6e9
 COST_JOIN_HIGH = 6e9
-COST_UPDATE = 12e9
-COST_HIGH = 12e9
-COST_LOW = 12e9
+COST_UPDATE = 6e9
+COST_CHUNK = 12e9
 COST_SUM = 1e9
 COST_MIDDLE = 6e9
+COST_QUERY = 6e9
 
 
 def dot(a, b, a_dim, b_dim):
@@ -209,9 +209,10 @@
             mine_ref[at, :] = piece
 
 
-def rest_body(q_ref, m_ref, g_ref, o_ref, ids_ref, low_ref, right_ref, low_out_ref, near_ref, far_ref, left_ref):
-    low_out_ref[...] = low_ref[...]
-    right_ref[...] = dot(q_ref[...], m_ref[...], 1, 1).astype(BF)
+def rest_body(q_ref, m_ref, g_ref, o_ref, ids_ref, low_ref, right_ref, near_ref, far_ref, left_ref):
+    cut = low_ref.shape[1]
+    right_ref[:, :cut] = low_ref[...]
+    right_ref[:, cut:] = dot(q_ref[...], m_ref[...], 1, 1).astype(BF)
     edges = q_ref.shape[1]
     step = step_of(edges)
     for at in range(0, edges, step):
@@ -264,11 +265,10 @@
         refs[-1][k * size:(k + 1) * size, :] = ref[...]
 
 
-def chunk_body(base, near_ref, got_ref, *block_refs):
+def chunk_body(near_ref, got_ref, *block_refs):
     for k, ref in enumerate(block_refs):
         cols = slice(k * LANES, (k + 1) * LANES)
-        total = near_ref[:, base + k * LANES:base + (k + 1) * LANES] + got_ref[:, cols].astype(F32)
-        ref[...] = total.astype(BF)
+        ref[...] = (near_ref[:, cols] + got_ref[:, cols].astype(F32)).astype(BF)
 
 
 def sum_body(*refs):
@@ -353,13 +353,13 @@
             here=place,
             after=(joined_low,),
         )(ids, relation_t)
-        joined = call(join_body, chunk, flops=COST_JOIN_HIGH, after=(weight,))(*near[some:])
+        half_joined = call(join_body, shape(width, far_right * rows, dtype=BF), after=(weight,))(*half_left)
+        joined = call(join_body, chunk, flops=COST_JOIN_HIGH, after=(half_joined,))(*near[some:])
         other_high = swap_left(joined, 1)
-        half_joined = call(join_body, shape(width, far_right * rows, dtype=BF), after=(joined,))(*half_left)
         sibling_left = swap_right(half_joined, 1)
         moved = next_column(call(pack_body, shape(width + 8, rows), after=(joined,))(right_t, right_state[None, :]), 0)
 
-        s, o, q = call(functools.partial(query_body, far_right), (table_bf, table_bf, table_bf))(
+        s, o, q = call(functools.partial(query_body, far_right), (table_bf, table_bf, table_bf), flops=COST_QUERY)(
             *half_left, sibling_left, relation_bf, ids
         )
         right_near, qg = call(
@@ -384,21 +384,25 @@
         )(other_high, q, weight, ids, qg, s)
         left_rows = n_right * rows
         left_half = left_rows // 2
-        right_high, right_low, left_near, left_far = call(
+        right_far, left_near, left_far = call(
             rest_body,
-            (chunk, chunk, shape(width, left_half), shape(width, left_half, dtype=BF)),
+            (shape(width, half, dtype=BF), shape(width, left_half), shape(width, left_half, dtype=BF)),
             [pltpu.VMEM((width, left_rows), F32)],
         )(q, m, g, o, ids, right_low)
 
+        right_got = swap_left(right_far, 1)
+
         mine, *rest = call(
-            piece_body, (shape(size, LANES),) + (piece,) * (far_right - 1), flops=COST_SUM
+            piece_body, (shape(size, LANES),) + (piece,) * (far_right - 1), flops=COST_SUM, after=(right_far,)
         )(mine, swap_right(theirs, 1))
         got = [swap_right(p, 2 * (k + 1)) for k, p in enumerate(rest)]
         mine = call(sum_body, piece, flops=COST_SUM)(mine, *got)
         bit = 2
         while bit < n_left:
-            mine = call(sum_body, piece, flops=COST_SUM)(mine, swap_left(mine, bit))
+            after = (right_got,) if 2 * bit == n_left else ()
+            mine = call(sum_body, piece, flops=COST_SUM, after=after)(mine, swap_left(mine, bit))
             bit *= 2
+        over_z = mine
         mine = call(sum_body, piece, flops=COST_SUM)(mine, swap_left(mine, 1))
         pieces = [mine] + [swap_right(mine, 2 * k) for k in range(1, far_right)]
         sibling = swap_right(call(stack_body, shape(far_right * size, LANES, dtype=BF))(*pieces), 1)
@@ -408,13 +412,10 @@
         )
         left_got = [swap_right(block, 2 * (k + 1)) for k, block in enumerate(blocks)]
 
-        got_low = swap_left(right_low, 1)
-        got_high = swap_left(right_high, 1)
-        outs = (one_block,) * some
-        high = call(functools.partial(chunk_body, cut), outs, flops=COST_HIGH)(right_near, got_high)
-        low = call(functools.partial(chunk_body, 0), outs, flops=COST_LOW, after=left_got)(right_near, got_low)
-        right_got = [next_column(block, 2 * (some + k)) for k, block in enumerate(high)]
-        right_got += [next_column(block, 2 * k) for k, block in enumerate(low)]
+        blocks = call(chunk_body, (one_block,) * outer, flops=COST_CHUNK, after=(over_z, *left_got))(
+            right_near, right_got
+        )
+        right_got = [next_column(blocks[k], 2 * k) for k in range(outer - 1, -1, -1)]
 
         def update(got, table, state, flops=0):
             outs = (shape(width, rows), shape(1, rows))

time: 56.1 us -> 58.7 us (1.046)
  waiting for transfers between devices: 7.42 us -> 17.1 us
  starting transfers between devices: 33.4 us -> 26.3 us
    ppermute x10 -> x9, waiting for transfers between devices: 3.08 us -> 8.98 us  [swap_left(): return lax.ppermute(value, 'left', [(i, i ^ by) for i in range(n_left)])]
    ppermute x5, starting transfers between devices: 8.76 us -> 5.23 us  [next_column(): return lax.ppermute(value, ('left', 'right'), perm)]
    ppermute x8, starting transfers between devices: 8.73 us -> 6.46 us  [swap_right(): return lax.ppermute(value, 'right', [(i, i ^ by) for i in range(n_right)])]
    ppermute x5, waiting for transfers between devices: 0.1 us -> 2.06 us  [next_column(): return lax.ppermute(value, ('left', 'right'), perm)]
    ppermute x8, waiting for transfers between devices: 4.24 us -> 6.03 us  [swap_right(): return lax.ppermute(value, 'right', [(i, i ^ by) for i in range(n_right)])]
    ppermute x10 -> x9, starting transfers between devices: 15.5 us -> 14.2 us  [swap_left(): return lax.ppermute(value, 'left', [(i, i ^ by) for i in range(n_left)])]
    pallas_call x24 -> x23, Pallas kernels: 11.4 us -> 11.4 us  [run(): pl.pallas_call(inner, out_shape=out_shape, in_specs=specs, scratch_shapes...]
  transfers between devices with their start and end apart: 24 -> 23, of which waited for: 7 -> 9; matrix products, arithmetic and copies ran while one was open for 1% -> 1% of each run, Pallas kernels for 15% -> 15%
where the time goes in v14:
time: 58.7 us; the launch traced here: 58.5 us
  starting transfers between devices  26.3 us (45%)
  waiting for transfers between devices  17.1 us (29%)
  Pallas kernels  11.4 us (19%)
  other arithmetic  1.78 us (3%)
  local copies, waits for them, and re-layouts  1.15 us (2%)
  between operations  0.83 us (1%)
    ppermute x9, starting transfers between devices, swap_left(): return lax.ppermute(value, 'left', [(i, i ^ by) for i in range(n_left)])  14.2 us
    pallas_call x23, Pallas kernels, run(): pl.pallas_call(inner, out_shape=out_shape, in_specs=specs, scratch_shapes...  11.4 us
    ppermute x9, waiting for transfers between devices, swap_left(): return lax.ppermute(value, 'left', [(i, i ^ by) for i in range(n_left)])  8.98 us
    ppermute x8, starting transfers between devices, swap_right(): return lax.ppermute(value, 'right', [(i, i ^ by) for i in range(n_right)])  6.46 us
    ppermute x8, waiting for transfers between devices, swap_right(): return lax.ppermute(value, 'right', [(i, i ^ by) for i in range(n_right)])  6.03 us
    ppermute x5, starting transfers between devices, next_column(): return lax.ppermute(value, ('left', 'right'), perm)  5.23 us
    ppermute x5, waiting for transfers between devices, next_column(): return lax.ppermute(value, ('left', 'right'), perm)  2.06 us
  transfers between devices with their start and end apart: 23, of which 9 were waited for; matrix products, arithmetic and copies ran while one was open for 1% of the time, Pallas kernels for 15%

profile of v14, /device:TPU:0, one launch (start us, length us, event | category | flops | bytes accessed | tf_op | source)
XLA Modules:
  0.0 58.5 jit_solution(5329959184487861853)
XLA Ops:
  0.6 0.9 %bitcast_convert_fusion.refs_0_ = bf16[400,128]{1,0:T(8,128)(2,1)S(1)} fusion(f32[128,400]{0,1:T(8,128)} %param.12), kind=kLoop, calls=%fused_computation.2 | loop fusion | flops 51200 | bytes 307200 | tf_op jit(solution)/shard_map/convert_element_type | solution.py:334
  1.6 5.1 %collective-permute-start.5 = (bf16[400,128]{1,0:T(8,128)(2,1)S(1)}, bf16[400,128]{1,0:T(8,128)(2,1)S(1)}, u32[]{:S(2)}, u32[]{:S(2)}) collective-permute-start(bf16[400,128]{1,0:T(8,128)(2,1)S(1)} %bitcast_convert_fusion.refs_0_), channel_id=1, source_target_pairs={{0,24},{4,28},{8,16},{12,20},{16,8},{20,12},{24,0},{28,4},{1,25},{... | collective-permute-start | bytes 307208 | tf_op jit(solution)/shard_map/ppermute | solution.py:300
  6.7 0.6 %collective-permute-start.2 = (bf16[400,128]{1,0:T(8,128)(2,1)S(1)}, bf16[400,128]{1,0:T(8,128)(2,1)S(1)}, u32[]{:S(2)}, u32[]{:S(2)}) collective-permute-start(bf16[400,128]{1,0:T(8,128)(2,1)S(1)} %bitcast_convert_fusion.refs_0_), channel_id=1, source_target_pairs={{0,8},{4,12},{8,0},{12,4},{16,24},{20,28},{24,16},{28,20},{1,9},{5... | collective-permute-start | bytes 307208 | tf_op jit(solution)/shard_map/ppermute | solution.py:300
  7.3 0.8 %pad_add_fusion = s32[5,1024]{1,0:T(8,128)S(1)} fusion(s32[2,1024]{1,0:T(2,128)} %bitcast.27, s32[1,1024]{1,0:T(1,128)} %bitcast.28, s32[1,1024]{1,0:T(1,128)} %bitcast.29, s32[1,1024]{1,0:T(1,128)} %bitcast.30), kind=kLoop, calls=%fused_computation | loop fusion | flops 15360 | bytes 40960 | tf_op jit(solution)/shard_map/concatenate | solution.py:345
  8.1 0.4 collective-permute-start.1
  8.5 0.9 %copy-done.1 = f32[128,400]{0,1:T(8,128)S(1)} copy-done((f32[128,400]{0,1:T(8,128)S(1)}, f32[128,400]{0,1:T(8,128)}, u32[]{:S(2)}) %copy-start.1) | copy-done | bytes 204824
  9.4 0.3 shard_map.145.refs_0_
  9.8 1.3 %collective-permute-start = (bf16[400,128]{1,0:T(8,128)(2,1)S(1)}, bf16[400,128]{1,0:T(8,128)(2,1)S(1)}, u32[]{:S(2)}, u32[]{:S(2)}) collective-permute-start(bf16[400,128]{1,0:T(8,128)(2,1)S(1)} %shard_map.145.refs_0_), channel_id=1, source_target_pairs={{0,2},{1,3},{2,0},{3,1},{4,6},{5,7},{6,4},{7,5},{8,10},{9,11},{10,... | collective-permute-start | bytes 307208 | tf_op jit(solution)/shard_map/ppermute | solution.py:303
  11.1 0.1 pad_add_fusion.1.refs_2_
  11.2 2.1 %collective-permute-done.2.refs_1_ = bf16[400,128]{1,0:T(8,128)(2,1)S(1)} collective-permute-done((bf16[400,128]{1,0:T(8,128)(2,1)S(1)}, bf16[400,128]{1,0:T(8,128)(2,1)S(1)}, u32[]{:S(2)}, u32[]{:S(2)}) %collective-permute-start.2) | collective-permute-done | bytes 102432 | tf_op jit(solution)/shard_map/ppermute | solution.py:300
  13.3 1.6 %collective-permute-start.7 = (bf16[400,256]{1,0:T(8,128)(2,1)S(1)}, bf16[400,256]{1,0:T(8,128)(2,1)S(1)}, u32[]{:S(2)}, u32[]{:S(2)}) collective-permute-start(bf16[400,256]{1,0:T(8,128)(2,1)S(1)} %shard_map.146.refs_3_), channel_id=1, source_target_pairs={{0,4},{4,0},{8,12},{12,8},{16,20},{20,16},{24,28},{28,24},{1,5},{5... | collective-permute-start | bytes 614408 | tf_op jit(solution)/shard_map/ppermute | solution.py:300
  14.9 1.6 %shard_map.147 = (f32[2,1024,128]{2,1,0:T(8,128)S(1)}, bf16[400,256]{1,0:T(8,128)(2,1)S(1)}, s32[5,1024]{1,0:T(8,128)S(1)}) custom-call(s32[5,1024]{1,0:T(8,128)S(1)} %collective-permute-done.1.refs_0_, f32[400,256]{1,0:T(8,128)S(1)} %bitcast.19, s32[2]{0:T(128)S(1)} %pad_add_fusion.1.refs_2_, bf16[400,256]{1,0:T(8,128)(2,1)S(1)} %shard_map.146.refs_3_), custom_call_target="tpu_custom_call" | custom-call | tf_op jit(solution)/shard_map/pallas_call | solution.py:53
  16.5 0.0 copy-start.3
  16.5 0.0 copy-start.6
  16.5 0.1 collective-permute-start.3
  16.7 0.6 collective-permute-start.6
  17.2 0.2 copy-done.3
  17.5 0.1 collective-permute-start.8
  17.5 1.8 %collective-permute-done.7.refs_0_ = bf16[400,256]{1,0:T(8,128)(2,1)S(1)} collective-permute-done((bf16[400,256]{1,0:T(8,128)(2,1)S(1)}, bf16[400,256]{1,0:T(8,128)(2,1)S(1)}, u32[]{:S(2)}, u32[]{:S(2)}) %collective-permute-start.7) | collective-permute-done | bytes 204832 | tf_op jit(solution)/shard_map/ppermute | solution.py:300
  19.4 0.9 %shard_map.149 = (bf16[400,1024]{1,0:T(8,128)(2,1)S(1)}, bf16[400,1024]{1,0:T(8,128)(2,1)S(1)}, bf16[400,1024]{1,0:T(8,128)(2,1)S(1)}) custom-call(bf16[400,128]{1,0:T(8,128)(2,1)S(1)} %shard_map.145.refs_0_, bf16[400,128]{1,0:T(8,128)(2,1)S(1)} %collective-permute-done.refs_1_, bf16[400,256]{1,0:T(8,128)(2,1)S(1)} %collective-permute-done.3.refs_2_, ...), custom_call_target="tpu_custom_call" | custom-call | flops 6000000000 | tf_op jit(solution)/shard_map/pallas_call | solution.py:53
  20.3 1.8 %shard_map.152 = (f32[400,512]{1,0:T(8,128)S(1)}, f32[400,1024]{1,0:T(8,128)S(1)}) custom-call(bf16[400,128]{1,0:T(8,128)(2,1)S(1)} %bitcast_convert_fusion.refs_0_, bf16[400,128]{1,0:T(8,128)(2,1)S(1)} %collective-permute-done.2.refs_1_, bf16[400,128]{1,0:T(8,128)(2,1)S(1)} %collective-permute-done.4.refs_0_.refs_2_, ...), custom_call_target="tpu_custom_call" | custom-call | tf_op jit(solution)/shard_map/pallas_call | solution.py:53
  22.2 1.0 %shard_map.153 = (bf16[400,256]{1,0:T(8,128)(2,1)S(1)}, f32[400,1024]{1,0:T(8,128)S(1)}) custom-call(bf16[400,256]{1,0:T(8,128)(2,1)S(1)} %shard_map.151.rows_ref, bf16[400,1024]{1,0:T(8,128)(2,1)S(1)} %get-tuple-element.40.refs_4_.q_ref.refs_1_, f32[2,1024,128]{2,1,0:T(8,128)S(1)} %get-tuple-element.37.refs_2_.refs_5_.weight_ref, ...), custom_call_target="tpu_custom_call" | custom-call | tf_op jit(solution)/shard_map/pallas_call | solution.py:53
  23.2 1.0 %collective-permute-done.6.refs_0_ = bf16[400,256]{1,0:T(8,128)(2,1)S(1)} collective-permute-done((bf16[400,256]{1,0:T(8,128)(2,1)S(1)}, bf16[400,256]{1,0:T(8,128)(2,1)S(1)}, u32[]{:S(2)}, u32[]{:S(2)}) %collective-permute-start.6) | collective-permute-done | bytes 204832 | tf_op jit(solution)/shard_map/ppermute | solution.py:300
  24.2 1.9 %shard_map.155 = (bf16[256,1024]{1,0:T(8,128)(2,1)S(1)}, f32[400,1024]{1,0:T(8,128)S(1)}, f32[416,128]{1,0:T(8,128)S(1)}, bf16[416,128]{1,0:T(8,128)(2,1)S(1)}) custom-call(bf16[400,256]{1,0:T(8,128)(2,1)S(1)} %collective-permute-done.6.refs_0_, bf16[400,1024]{1,0:T(8,128)(2,1)S(1)} %get-tuple-element.40.refs_4_.q_ref.refs_1_, ...), custom_call_target="tpu_custom_call" | custom-call | tf_op jit(solution)/shard_map/pallas_call | solution.py:53
  26.1 0.1 collective-permute-start.12
  26.1 1.0 %shard_map.156 = (bf16[400,512]{1,0:T(8,128)(2,1)S(1)}, f32[400,256]{1,0:T(8,128)S(1)}, bf16[400,256]{1,0:T(8,128)(2,1)S(1)}) custom-call(bf16[400,1024]{1,0:T(8,128)(2,1)S(1)} %get-tuple-element.40.refs_4_.q_ref.refs_1_, bf16[256,1024]{1,0:T(8,128)(2,1)S(1)} %get-tuple-element.44.m_ref, f32[400,1024]{1,0:T(8,128)S(1)} %get-tuple-element.45.g_ref, ...), custom_call_target="tpu_custom_call" | custom-call | tf_op jit(solution)/shard_map/pallas_call | solution.py:53
  27.2 1.1 %collective-permute-start.11 = (bf16[400,512]{1,0:T(8,128)(2,1)S(1)}, bf16[400,512]{1,0:T(8,128)(2,1)S(1)}, u32[]{:S(2)}, u32[]{:S(2)}) collective-permute-start(bf16[400,512]{1,0:T(8,128)(2,1)S(1)} %get-tuple-element.55.refs_2_), channel_id=1, source_target_pairs={{0,4},{4,0},{8,12},{12,8},{16,20},{20,16},{24,28},{28,24},{1,5},{5... | collective-permute-start | bytes 1228808 | tf_op jit(solution)/shard_map/ppermute | solution.py:300
  28.3 1.6 %collective-permute-start.13 = (bf16[208,128]{1,0:T(8,128)(2,1)S(1)}, bf16[208,128]{1,0:T(8,128)(2,1)S(1)}, u32[]{:S(2)}, u32[]{:S(2)}) collective-permute-start(bf16[208,128]{1,0:T(8,128)(2,1)S(1)} %get-tuple-element.59), channel_id=1, source_target_pairs={{0,2},{1,3},{2,0},{3,1},{4,6},{5,7},{6,4},{7,5},{8,10},{9,11},{10,... | collective-permute-start | bytes 159752 | tf_op jit(solution)/shard_map/ppermute | solution.py:303
  29.9 2.6 %collective-permute-done.13.refs_1_ = bf16[208,128]{1,0:T(8,128)(2,1)S(1)} collective-permute-done((bf16[208,128]{1,0:T(8,128)(2,1)S(1)}, bf16[208,128]{1,0:T(8,128)(2,1)S(1)}, u32[]{:S(2)}, u32[]{:S(2)}) %collective-permute-start.13) | collective-permute-done | bytes 53280 | tf_op jit(solution)/shard_map/ppermute | solution.py:303
  32.5 2.5 %collective-permute-start.14 = (bf16[208,128]{1,0:T(8,128)(2,1)S(1)}, bf16[208,128]{1,0:T(8,128)(2,1)S(1)}, u32[]{:S(2)}, u32[]{:S(2)}) collective-permute-start(bf16[208,128]{1,0:T(8,128)(2,1)S(1)} %shard_map.160.refs_0_), channel_id=1, source_target_pairs={{0,8},{4,12},{8,0},{12,4},{16,24},{20,28},{24,16},{28,20},{1,9},{5... | collective-permute-start | bytes 159752 | tf_op jit(solution)/shard_map/ppermute | solution.py:300
  35.1 2.1 %collective-permute-done.14.refs_1_ = bf16[208,128]{1,0:T(8,128)(2,1)S(1)} collective-permute-done((bf16[208,128]{1,0:T(8,128)(2,1)S(1)}, bf16[208,128]{1,0:T(8,128)(2,1)S(1)}, u32[]{:S(2)}, u32[]{:S(2)}) %collective-permute-start.14) | collective-permute-done | bytes 53280 | tf_op jit(solution)/shard_map/ppermute | solution.py:300
  37.2 1.6 %collective-permute-start.15 = (bf16[208,128]{1,0:T(8,128)(2,1)S(1)}, bf16[208,128]{1,0:T(8,128)(2,1)S(1)}, u32[]{:S(2)}, u32[]{:S(2)}) collective-permute-start(bf16[208,128]{1,0:T(8,128)(2,1)S(1)} %shard_map.161.refs_0_), channel_id=1, source_target_pairs={{0,16},{4,20},{8,24},{12,28},{16,0},{20,4},{24,8},{28,12},{1,17},{... | collective-permute-start | bytes 159752 | tf_op jit(solution)/shard_map/ppermute | solution.py:300
  38.8 1.6 %collective-permute-start.10 = (bf16[400,128]{1,0:T(8,128)(2,1)S(1)}, bf16[400,128]{1,0:T(8,128)(2,1)S(1)}, u32[]{:S(2)}, u32[]{:S(2)}) collective-permute-start(bf16[400,128]{1,0:T(8,128)(2,1)S(1)} %get-tuple-element.51), channel_id=1, source_target_pairs={{0,2},{1,3},{2,0},{3,1},{4,6},{5,7},{6,4},{7,5},{8,10},{9,11},{10,... | collective-permute-start | bytes 307208 | tf_op jit(solution)/shard_map/ppermute | solution.py:303
  40.4 1.9 %collective-permute-done.15.refs_1_ = bf16[208,128]{1,0:T(8,128)(2,1)S(1)} collective-permute-done((bf16[208,128]{1,0:T(8,128)(2,1)S(1)}, bf16[208,128]{1,0:T(8,128)(2,1)S(1)}, u32[]{:S(2)}, u32[]{:S(2)}) %collective-permute-start.15) | collective-permute-done | bytes 53280 | tf_op jit(solution)/shard_map/ppermute | solution.py:300
  42.3 1.0 %collective-permute-start.20 = (bf16[208,128]{1,0:T(8,128)(2,1)S(1)}, bf16[208,128]{1,0:T(8,128)(2,1)S(1)}, u32[]{:S(2)}, u32[]{:S(2)}) collective-permute-start(bf16[208,128]{1,0:T(8,128)(2,1)S(1)} %shard_map.162.refs_2_.refs_0_), channel_id=1, source_target_pairs={{0,4},{4,0},{8,12},{12,8},{16,20},{20,16},{24,28},{28,24},{1,5},{5... | collective-permute-start | bytes 159752 | tf_op jit(solution)/shard_map/ppermute | solution.py:300
  43.4 0.2 collective-permute-done.10.refs_1_.refs_3_
  43.6 0.1 shard_map.163
  43.7 0.1 collective-permute-start.16
  43.7 4.1 %collective-permute-start.17 = (bf16[400,128]{1,0:T(8,128)(2,1)S(1)}, bf16[400,128]{1,0:T(8,128)(2,1)S(1)}, u32[]{:S(2)}, u32[]{:S(2)}) collective-permute-start(bf16[400,128]{1,0:T(8,128)(2,1)S(1)} %get-tuple-element.61), channel_id=1, source_target_pairs={{0,17},{1,18},{2,19},{3,16},{4,21},{5,22},{6,23},{7,20},{8,25},{9,... | collective-permute-start | bytes 307208 | tf_op jit(solution)/shard_map/ppermute | solution.py:310
  47.9 0.0 collective-permute-start.18
  47.9 1.0 %collective-permute-start.19 = (bf16[400,128]{1,0:T(8,128)(2,1)S(1)}, bf16[400,128]{1,0:T(8,128)(2,1)S(1)}, u32[]{:S(2)}, u32[]{:S(2)}) collective-permute-start(bf16[400,128]{1,0:T(8,128)(2,1)S(1)} %get-tuple-element.63), channel_id=1, source_target_pairs={{0,1},{1,2},{2,3},{3,0},{4,5},{5,6},{6,7},{7,4},{8,9},{9,10},{10,1... | collective-permute-start | bytes 307208 | tf_op jit(solution)/shard_map/ppermute | solution.py:310
  48.9 1.6 %collective-permute-start.21 = (bf16[208,128]{1,0:T(8,128)(2,1)S(1)}, bf16[208,128]{1,0:T(8,128)(2,1)S(1)}, u32[]{:S(2)}, u32[]{:S(2)}) collective-permute-start(bf16[208,128]{1,0:T(8,128)(2,1)S(1)} %shard_map.165.refs_0_), channel_id=1, source_target_pairs={{0,2},{1,3},{2,0},{3,1},{4,6},{5,7},{6,4},{7,5},{8,10},{9,11},{10,... | collective-permute-start | bytes 159752 | tf_op jit(solution)/shard_map/ppermute | solution.py:303
  50.5 0.8 %shard_map.158 = (f32[400,128]{1,0:T(8,128)}, f32[1,128]{1,0:T(1,128)}) custom-call(f32[400,128]{1,0:T(8,128)S(1)} %get-tuple-element.50.refs_0_, bf16[400,128]{1,0:T(8,128)(2,1)S(1)} %collective-permute-done.10.refs_1_.refs_3_, f32[400,128]{1,0:T(8,128)S(1)} %bitcast.22, f32[1,128]{1,0:T(1,128)S(1)} %bitcast.25), custom_call_target="tpu_custom_call" | custom-call | tf_op jit(solution)/shard_map/pallas_call | solution.py:53
  51.2 3.2 %collective-permute-done.21.refs_1_ = bf16[208,128]{1,0:T(8,128)(2,1)S(1)} collective-permute-done((bf16[208,128]{1,0:T(8,128)(2,1)S(1)}, bf16[208,128]{1,0:T(8,128)(2,1)S(1)}, u32[]{:S(2)}, u32[]{:S(2)}) %collective-permute-start.21) | collective-permute-done | bytes 53280 | tf_op jit(solution)/shard_map/ppermute | solution.py:303
  54.4 0.3 collective-permute-start.22
  54.7 2.0 %collective-permute-done.17.refs_1_ = bf16[400,128]{1,0:T(8,128)(2,1)S(1)} collective-permute-done((bf16[400,128]{1,0:T(8,128)(2,1)S(1)}, bf16[400,128]{1,0:T(8,128)(2,1)S(1)}, u32[]{:S(2)}, u32[]{:S(2)}) %collective-permute-start.17) | collective-permute-done | bytes 102432 | tf_op jit(solution)/shard_map/ppermute | solution.py:310
  56.8 0.8 %shard_map.164 = (f32[400,128]{1,0:T(8,128)}, f32[1,128]{1,0:T(1,128)}) custom-call(bf16[400,128]{1,0:T(8,128)(2,1)S(1)} %collective-permute-done.16.refs_0_, bf16[400,128]{1,0:T(8,128)(2,1)S(1)} %collective-permute-done.17.refs_1_, bf16[400,128]{1,0:T(8,128)(2,1)S(1)} %collective-permute-done.18.refs_2_, ...), custom_call_target="tpu_custom_call" | custom-call | flops 6000000000 | tf_op jit(solution)/shard_map/pallas_call | solution.py:53
  57.6 0.9 %shard_map.167 = (f32[400,256]{1,0:T(8,128)}, f32[1,256]{1,0:T(1,128)}) custom-call(bf16[208,128]{1,0:T(8,128)(2,1)S(1)} %shard_map.165.refs_0_, bf16[208,128]{1,0:T(8,128)(2,1)S(1)} %collective-permute-done.21.refs_1_, bf16[416,128]{1,0:T(8,128)(2,1)S(1)} %collective-permute-done.22.refs_2_, f32[400,256]{1,0:T(8,128)S(1)} %bitcast.20, ...), custom_call_target="tpu_custom_call" | custom-call | tf_op jit(solution)/shard_map/pallas_call | solution.py:53
  (38 shorter events, 0.3 us)
Async XLA Ops:
  1.6 15.0 %collective-permute-start.5 = (bf16[400,128]{1,0:T(8,128)(2,1)S(1)}, bf16[400,128]{1,0:T(8,128)(2,1)S(1)}, u32[]{:S(2)}, u32[]{:S(2)}) collective-permute-start(bf16[400,128]{1,0:T(8,128)(2,1)S(1)} %bitcast_convert_fusion.refs_0_), channel_id=1, source_target_pairs={{0,24},{4,28},{8,16},{12,20},{16,8},{20,12},{24,0},{28,4},{1,25},{... | collective-permute-start | bytes 307208 | tf_op jit(solution)/shard_map/ppermute | solution.py:300
  6.7 9.9 %collective-permute-start.4 = (bf16[400,128]{1,0:T(8,128)(2,1)S(1)}, bf16[400,128]{1,0:T(8,128)(2,1)S(1)}, u32[]{:S(2)}, u32[]{:S(2)}) collective-permute-start(bf16[400,128]{1,0:T(8,128)(2,1)S(1)} %bitcast_convert_fusion.refs_0_), channel_id=1, source_target_pairs={{0,16},{4,20},{8,24},{12,28},{16,0},{20,4},{24,8},{28,12},{1,17},{... | collective-permute-start | bytes 307208 | tf_op jit(solution)/shard_map/ppermute | solution.py:300
  6.7 6.6 %collective-permute-start.2 = (bf16[400,128]{1,0:T(8,128)(2,1)S(1)}, bf16[400,128]{1,0:T(8,128)(2,1)S(1)}, u32[]{:S(2)}, u32[]{:S(2)}) collective-permute-start(bf16[400,128]{1,0:T(8,128)(2,1)S(1)} %bitcast_convert_fusion.refs_0_), channel_id=1, source_target_pairs={{0,8},{4,12},{8,0},{12,4},{16,24},{20,28},{24,16},{28,20},{1,9},{5... | collective-permute-start | bytes 307208 | tf_op jit(solution)/shard_map/ppermute | solution.py:300
  8.1 6.8 %collective-permute-start.1 = (s32[5,1024]{1,0:T(8,128)S(1)}, s32[5,1024]{1,0:T(8,128)S(1)}, u32[]{:S(2)}, u32[]{:S(2)}) collective-permute-start(s32[5,1024]{1,0:T(8,128)S(1)} %pad_add_fusion), channel_id=1, source_target_pairs={{0,3},{1,0},{2,1},{3,2},{4,7},{5,4},{6,5},{7,6},{8,11},{9,8},{10,9... | collective-permute-start | bytes 61448 | tf_op jit(solution)/shard_map/ppermute | solution.py:346
  8.5 0.9 %copy-start.1 = (f32[128,400]{0,1:T(8,128)S(1)}, f32[128,400]{0,1:T(8,128)}, u32[]{:S(2)}) copy-start(f32[128,400]{0,1:T(8,128)} %param.10) | copy-start | bytes 614404
  9.8 6.7 %collective-permute-start = (bf16[400,128]{1,0:T(8,128)(2,1)S(1)}, bf16[400,128]{1,0:T(8,128)(2,1)S(1)}, u32[]{:S(2)}, u32[]{:S(2)}) collective-permute-start(bf16[400,128]{1,0:T(8,128)(2,1)S(1)} %shard_map.145.refs_0_), channel_id=1, source_target_pairs={{0,2},{1,3},{2,0},{3,1},{4,6},{5,7},{6,4},{7,5},{8,10},{9,11},{10,... | collective-permute-start | bytes 307208 | tf_op jit(solution)/shard_map/ppermute | solution.py:303
  11.2 3.7 %copy-start = (f32[256,400]{0,1:T(8,128)S(1)}, f32[256,400]{0,1:T(8,128)}, u32[]{:S(2)}) copy-start(f32[256,400]{0,1:T(8,128)} %param.14) | copy-start | bytes 1228804
  13.3 6.1 %collective-permute-start.7 = (bf16[400,256]{1,0:T(8,128)(2,1)S(1)}, bf16[400,256]{1,0:T(8,128)(2,1)S(1)}, u32[]{:S(2)}, u32[]{:S(2)}) collective-permute-start(bf16[400,256]{1,0:T(8,128)(2,1)S(1)} %shard_map.146.refs_3_), channel_id=1, source_target_pairs={{0,4},{4,0},{8,12},{12,8},{16,20},{20,16},{24,28},{28,24},{1,5},{5... | collective-permute-start | bytes 614408 | tf_op jit(solution)/shard_map/ppermute | solution.py:300
  16.5 0.9 %copy-start.3 = (f32[128,400]{0,1:T(8,128)S(1)}, f32[128,400]{0,1:T(8,128)}, u32[]{:S(2)}) copy-start(f32[128,400]{0,1:T(8,128)} %param.12) | copy-start | bytes 614404
  16.5 0.9 %copy-start.6 = (f32[128]{0:T(128)S(1)}, f32[128]{0:T(128)}, u32[]{:S(2)}) copy-start(f32[128]{0:T(128)} %param.13) | copy-start | bytes 1540
  16.5 2.9 %collective-permute-start.3 = (bf16[400,256]{1,0:T(8,128)(2,1)S(1)}, bf16[400,256]{1,0:T(8,128)(2,1)S(1)}, u32[]{:S(2)}, u32[]{:S(2)}) collective-permute-start(bf16[400,256]{1,0:T(8,128)(2,1)S(1)} %shard_map.148.refs_2_), channel_id=1, source_target_pairs={{0,1},{1,0},{2,3},{3,2},{4,5},{5,4},{6,7},{7,6},{8,9},{9,8},{10,11... | collective-permute-start | bytes 614408 | tf_op jit(solution)/shard_map/ppermute | solution.py:303
  16.7 7.5 %collective-permute-start.6 = (bf16[400,256]{1,0:T(8,128)(2,1)S(1)}, bf16[400,256]{1,0:T(8,128)(2,1)S(1)}, u32[]{:S(2)}, u32[]{:S(2)}) collective-permute-start(bf16[400,256]{1,0:T(8,128)(2,1)S(1)} %shard_map.150.refs_2_), channel_id=1, source_target_pairs={{0,4},{4,0},{8,12},{12,8},{16,20},{20,16},{24,28},{28,24},{1,5},{5... | collective-permute-start | bytes 614408 | tf_op jit(solution)/shard_map/ppermute | solution.py:300
  17.5 6.7 %collective-permute-start.8 = (f32[408,128]{1,0:T(8,128)S(1)}, f32[408,128]{1,0:T(8,128)S(1)}, u32[]{:S(2)}, u32[]{:S(2)}) collective-permute-start(f32[408,128]{1,0:T(8,128)S(1)} %shard_map.154), channel_id=1, source_target_pairs={{0,1},{1,2},{2,3},{3,0},{4,5},{5,6},{6,7},{7,4},{8,9},{9,10},{10,1... | collective-permute-start | bytes 626696 | tf_op jit(solution)/shard_map/ppermute | solution.py:310
  26.1 2.2 %collective-permute-start.12 = (bf16[416,128]{1,0:T(8,128)(2,1)S(1)}, bf16[416,128]{1,0:T(8,128)(2,1)S(1)}, u32[]{:S(2)}, u32[]{:S(2)}) collective-permute-start(bf16[416,128]{1,0:T(8,128)(2,1)S(1)} %get-tuple-element.57), channel_id=1, source_target_pairs={{0,1},{1,0},{2,3},{3,2},{4,5},{5,4},{6,7},{7,6},{8,9},{9,8},{10,11... | collective-permute-start | bytes 319496 | tf_op jit(solution)/shard_map/ppermute | solution.py:303
  27.2 15.2 %collective-permute-start.11 = (bf16[400,512]{1,0:T(8,128)(2,1)S(1)}, bf16[400,512]{1,0:T(8,128)(2,1)S(1)}, u32[]{:S(2)}, u32[]{:S(2)}) collective-permute-start(bf16[400,512]{1,0:T(8,128)(2,1)S(1)} %get-tuple-element.55.refs_2_), channel_id=1, source_target_pairs={{0,4},{4,0},{8,12},{12,8},{16,20},{20,16},{24,28},{28,24},{1,5},{5... | collective-permute-start | bytes 1228808 | tf_op jit(solution)/shard_map/ppermute | solution.py:300
  28.3 4.2 %collective-permute-start.13 = (bf16[208,128]{1,0:T(8,128)(2,1)S(1)}, bf16[208,128]{1,0:T(8,128)(2,1)S(1)}, u32[]{:S(2)}, u32[]{:S(2)}) collective-permute-start(bf16[208,128]{1,0:T(8,128)(2,1)S(1)} %get-tuple-element.59), channel_id=1, source_target_pairs={{0,2},{1,3},{2,0},{3,1},{4,6},{5,7},{6,4},{7,5},{8,10},{9,11},{10,... | collective-permute-start | bytes 159752 | tf_op jit(solution)/shard_map/ppermute | solution.py:303
  29.9 8.9 %collective-permute-start.9 = (bf16[400,256]{1,0:T(8,128)(2,1)S(1)}, bf16[400,256]{1,0:T(8,128)(2,1)S(1)}, u32[]{:S(2)}, u32[]{:S(2)}) collective-permute-start(bf16[400,256]{1,0:T(8,128)(2,1)S(1)} %get-tuple-element.49), channel_id=1, source_target_pairs={{0,1},{1,0},{2,3},{3,2},{4,5},{5,4},{6,7},{7,6},{8,9},{9,8},{10,11... | collective-permute-start | bytes 614408 | tf_op jit(solution)/shard_map/ppermute | solution.py:303
  32.5 4.7 %collective-permute-start.14 = (bf16[208,128]{1,0:T(8,128)(2,1)S(1)}, bf16[208,128]{1,0:T(8,128)(2,1)S(1)}, u32[]{:S(2)}, u32[]{:S(2)}) collective-permute-start(bf16[208,128]{1,0:T(8,128)(2,1)S(1)} %shard_map.160.refs_0_), channel_id=1, source_target_pairs={{0,8},{4,12},{8,0},{12,4},{16,24},{20,28},{24,16},{28,20},{1,9},{5... | collective-permute-start | bytes 159752 | tf_op jit(solution)/shard_map/ppermute | solution.py:300
  37.2 5.1 %collective-permute-start.15 = (bf16[208,128]{1,0:T(8,128)(2,1)S(1)}, bf16[208,128]{1,0:T(8,128)(2,1)S(1)}, u32[]{:S(2)}, u32[]{:S(2)}) collective-permute-start(bf16[208,128]{1,0:T(8,128)(2,1)S(1)} %shard_map.161.refs_0_), channel_id=1, source_target_pairs={{0,16},{4,20},{8,24},{12,28},{16,0},{20,4},{24,8},{28,12},{1,17},{... | collective-permute-start | bytes 159752 | tf_op jit(solution)/shard_map/ppermute | solution.py:300
  38.8 4.7 %collective-permute-start.10 = (bf16[400,128]{1,0:T(8,128)(2,1)S(1)}, bf16[400,128]{1,0:T(8,128)(2,1)S(1)}, u32[]{:S(2)}, u32[]{:S(2)}) collective-permute-start(bf16[400,128]{1,0:T(8,128)(2,1)S(1)} %get-tuple-element.51), channel_id=1, source_target_pairs={{0,2},{1,3},{2,0},{3,1},{4,6},{5,7},{6,4},{7,5},{8,10},{9,11},{10,... | collective-permute-start | bytes 307208 | tf_op jit(solution)/shard_map/ppermute | solution.py:303
  42.3 6.5 %collective-permute-start.20 = (bf16[208,128]{1,0:T(8,128)(2,1)S(1)}, bf16[208,128]{1,0:T(8,128)(2,1)S(1)}, u32[]{:S(2)}, u32[]{:S(2)}) collective-permute-start(bf16[208,128]{1,0:T(8,128)(2,1)S(1)} %shard_map.162.refs_2_.refs_0_), channel_id=1, source_target_pairs={{0,4},{4,0},{8,12},{12,8},{16,20},{20,16},{24,28},{28,24},{1,5},{5... | collective-permute-start | bytes 159752 | tf_op jit(solution)/shard_map/ppermute | solution.py:300
  43.7 11.0 %collective-permute-start.16 = (bf16[400,128]{1,0:T(8,128)(2,1)S(1)}, bf16[400,128]{1,0:T(8,128)(2,1)S(1)}, u32[]{:S(2)}, u32[]{:S(2)}) collective-permute-start(bf16[400,128]{1,0:T(8,128)(2,1)S(1)} %get-tuple-element.60), channel_id=1, source_target_pairs={{0,25},{1,26},{2,27},{3,24},{4,29},{5,30},{6,31},{7,28},{8,17},{9,... | collective-permute-start | bytes 307208 | tf_op jit(solution)/shard_map/ppermute | solution.py:310
  43.7 13.0 %collective-permute-start.17 = (bf16[400,128]{1,0:T(8,128)(2,1)S(1)}, bf16[400,128]{1,0:T(8,128)(2,1)S(1)}, u32[]{:S(2)}, u32[]{:S(2)}) collective-permute-start(bf16[400,128]{1,0:T(8,128)(2,1)S(1)} %get-tuple-element.61), channel_id=1, source_target_pairs={{0,17},{1,18},{2,19},{3,16},{4,21},{5,22},{6,23},{7,20},{8,25},{9,... | collective-permute-start | bytes 307208 | tf_op jit(solution)/shard_map/ppermute | solution.py:310
  47.9 8.9 %collective-permute-start.18 = (bf16[400,128]{1,0:T(8,128)(2,1)S(1)}, bf16[400,128]{1,0:T(8,128)(2,1)S(1)}, u32[]{:S(2)}, u32[]{:S(2)}) collective-permute-start(bf16[400,128]{1,0:T(8,128)(2,1)S(1)} %get-tuple-element.62), channel_id=1, source_target_pairs={{0,9},{1,10},{2,11},{3,8},{4,13},{5,14},{6,15},{7,12},{8,1},{9,2},... | collective-permute-start | bytes 307208 | tf_op jit(solution)/shard_map/ppermute | solution.py:310
  47.9 2.6 %copy-start.2 = (f32[128,400]{0,1:T(8,128)S(1)}, f32[128,400]{0,1:T(8,128)}, u32[]{:S(2)}) copy-start(f32[128,400]{0,1:T(8,128)} %param.10) | copy-start | bytes 614404
  47.9 2.6 %copy-start.5 = (f32[128]{0:T(128)S(1)}, f32[128]{0:T(128)}, u32[]{:S(2)}) copy-start(f32[128]{0:T(128)} %param.11) | copy-start | bytes 1540
  47.9 8.9 %collective-permute-start.19 = (bf16[400,128]{1,0:T(8,128)(2,1)S(1)}, bf16[400,128]{1,0:T(8,128)(2,1)S(1)}, u32[]{:S(2)}, u32[]{:S(2)}) collective-permute-start(bf16[400,128]{1,0:T(8,128)(2,1)S(1)} %get-tuple-element.63), channel_id=1, source_target_pairs={{0,1},{1,2},{2,3},{3,0},{4,5},{5,6},{6,7},{7,4},{8,9},{9,10},{10,1... | collective-permute-start | bytes 307208 | tf_op jit(solution)/shard_map/ppermute | solution.py:310
  48.9 5.5 %collective-permute-start.21 = (bf16[208,128]{1,0:T(8,128)(2,1)S(1)}, bf16[208,128]{1,0:T(8,128)(2,1)S(1)}, u32[]{:S(2)}, u32[]{:S(2)}) collective-permute-start(bf16[208,128]{1,0:T(8,128)(2,1)S(1)} %shard_map.165.refs_0_), channel_id=1, source_target_pairs={{0,2},{1,3},{2,0},{3,1},{4,6},{5,7},{6,4},{7,5},{8,10},{9,11},{10,... | collective-permute-start | bytes 159752 | tf_op jit(solution)/shard_map/ppermute | solution.py:303
  54.4 3.1 %copy-start.4 = (f32[256]{0:T(256)S(1)}, f32[256]{0:T(256)}, u32[]{:S(2)}) copy-start(f32[256]{0:T(256)} %param.15) | copy-start | bytes 3076
  54.4 3.1 %collective-permute-start.22 = (bf16[416,128]{1,0:T(8,128)(2,1)S(1)}, bf16[416,128]{1,0:T(8,128)(2,1)S(1)}, u32[]{:S(2)}, u32[]{:S(2)}) collective-permute-start(bf16[416,128]{1,0:T(8,128)(2,1)S(1)} %shard_map.166), channel_id=1, source_target_pairs={{0,1},{1,0},{2,3},{3,2},{4,5},{5,4},{6,7},{7,6},{8,9},{9,8},{10,11... | collective-permute-start | bytes 319496 | tf_op jit(solution)/shard_map/ppermute | solution.py:303

commit v15 on v13

--- a/solution.py
+++ b/solution.py
@@ -20,6 +20,7 @@
 COST_LOW = 12e9
 COST_SUM = 1e9
 COST_MIDDLE = 6e9
+COST_QUERY = 6e9
 
 
 def dot(a, b, a_dim, b_dim):
@@ -209,7 +210,7 @@
             mine_ref[at, :] = piece
 
 
-def rest_body(q_ref, m_ref, g_ref, o_ref, ids_ref, low_ref, right_ref, low_out_ref, near_ref, far_ref, left_ref):
+def rest_body(m_ref, q_ref, g_ref, o_ref, ids_ref, low_ref, right_ref, low_out_ref, near_ref, far_ref, left_ref):
     low_out_ref[...] = low_ref[...]
     right_ref[...] = dot(q_ref[...], m_ref[...], 1, 1).astype(BF)
     edges = q_ref.shape[1]
@@ -353,13 +354,13 @@
             here=place,
             after=(joined_low,),
         )(ids, relation_t)
-        joined = call(join_body, chunk, flops=COST_JOIN_HIGH, after=(weight,))(*near[some:])
+        half_joined = call(join_body, shape(width, far_right * rows, dtype=BF), after=(weight,))(*half_left)
+        joined = call(join_body, chunk, flops=COST_JOIN_HIGH, after=(half_joined,))(*near[some:])
         other_high = swap_left(joined, 1)
-        half_joined = call(join_body, shape(width, far_right * rows, dtype=BF), after=(joined,))(*half_left)
         sibling_left = swap_right(half_joined, 1)
         moved = next_column(call(pack_body, shape(width + 8, rows), after=(joined,))(right_t, right_state[None, :]), 0)
 
-        s, o, q = call(functools.partial(query_body, far_right), (table_bf, table_bf, table_bf))(
+        s, o, q = call(functools.partial(query_body, far_right), (table_bf, table_bf, table_bf), flops=COST_QUERY)(
             *half_left, sibling_left, relation_bf, ids
         )
         right_near, qg = call(
@@ -388,17 +389,17 @@
             rest_body,
             (chunk, chunk, shape(width, left_half), shape(width, left_half, dtype=BF)),
             [pltpu.VMEM((width, left_rows), F32)],
-        )(q, m, g, o, ids, right_low)
+        )(m, q, g, o, ids, right_low)
 
         mine, *rest = call(
             piece_body, (shape(size, LANES),) + (piece,) * (far_right - 1), flops=COST_SUM
         )(mine, swap_right(theirs, 1))
         got = [swap_right(p, 2 * (k + 1)) for k, p in enumerate(rest)]
         mine = call(sum_body, piece, flops=COST_SUM)(mine, *got)
-        bit = 2
-        while bit < n_left:
+        bit = n_left // 2
+        while bit > 1:
             mine = call(sum_body, piece, flops=COST_SUM)(mine, swap_left(mine, bit))
-            bit *= 2
+            bit //= 2
         mine = call(sum_body, piece, flops=COST_SUM)(mine, swap_left(mine, 1))
         pieces = [mine] + [swap_right(mine, 2 * k) for k in range(1, far_right)]
         sibling = swap_right(call(stack_body, shape(far_right * size, LANES, dtype=BF))(*pieces), 1)

time: 56.1 us -> 53.6 us (0.955)
  starting transfers between devices: 33.4 us -> 27.3 us
  waiting for transfers between devices: 7.42 us -> 11 us
    ppermute x8, starting transfers between devices: 8.73 us -> 5.38 us  [swap_right(): return lax.ppermute(value, 'right', [(i, i ^ by) for i in range(n_right)])]
    ppermute x5, starting transfers between devices: 8.76 us -> 5.93 us  [next_column(): return lax.ppermute(value, ('left', 'right'), perm)]
    ppermute x10, waiting for transfers between devices: 3.08 us -> 4.81 us  [swap_left(): return lax.ppermute(value, 'left', [(i, i ^ by) for i in range(n_left)])]
    ppermute x8, waiting for transfers between devices: 4.24 us -> 5.9 us  [swap_right(): return lax.ppermute(value, 'right', [(i, i ^ by) for i in range(n_right)])]
  transfers between devices with their start and end apart: 24 -> 24, of which waited for: 7 -> 10; matrix products, arithmetic and copies ran while one was open for 1% -> 2% of each run, Pallas kernels for 15% -> 16%
where the time goes in v15:
time: 53.6 us; the launch traced here: 53.4 us
  starting transfers between devices  27.3 us (51%)
  Pallas kernels  11.4 us (21%)
  waiting for transfers between devices  11 us (21%)
  other arithmetic  1.78 us (3%)
  local copies, waits for them, and re-layouts  0.96 us (2%)
  between operations  0.88 us (2%)
    ppermute x10, starting transfers between devices, swap_left(): return lax.ppermute(value, 'left', [(i, i ^ by) for i in range(n_left)])  15.6 us
    pallas_call x24, Pallas kernels, run(): pl.pallas_call(inner, out_shape=out_shape, in_specs=specs, scratch_shapes...  11.4 us
    ppermute x5, starting transfers between devices, next_column(): return lax.ppermute(value, ('left', 'right'), perm)  5.93 us
    ppermute x8, waiting for transfers between devices, swap_right(): return lax.ppermute(value, 'right', [(i, i ^ by) for i in range(n_right)])  5.9 us
    ppermute x8, starting transfers between devices, swap_right(): return lax.ppermute(value, 'right', [(i, i ^ by) for i in range(n_right)])  5.38 us
    ppermute x10, waiting for transfers between devices, swap_left(): return lax.ppermute(value, 'left', [(i, i ^ by) for i in range(n_left)])  4.81 us
  transfers between devices with their start and end apart: 24, of which 10 were waited for; matrix products, arithmetic and copies ran while one was open for 2% of the time, Pallas kernels for 16%

profile of v15, /device:TPU:0, one launch (start us, length us, event | category | flops | bytes accessed | tf_op | source)
XLA Modules:
  0.0 53.4 jit_solution(4346173725890833993)
XLA Ops:
  0.6 0.9 %bitcast_convert_fusion.refs_0_ = bf16[400,128]{1,0:T(8,128)(2,1)S(1)} fusion(f32[128,400]{0,1:T(8,128)} %param.12), kind=kLoop, calls=%fused_computation.2 | loop fusion | flops 51200 | bytes 307200 | tf_op jit(solution)/shard_map/convert_element_type | solution.py:335
  1.6 3.1 %collective-permute-start.4 = (bf16[400,128]{1,0:T(8,128)(2,1)S(1)}, bf16[400,128]{1,0:T(8,128)(2,1)S(1)}, u32[]{:S(2)}, u32[]{:S(2)}) collective-permute-start(bf16[400,128]{1,0:T(8,128)(2,1)S(1)} %bitcast_convert_fusion.refs_0_), channel_id=1, source_target_pairs={{0,8},{4,12},{8,0},{12,4},{16,24},{20,28},{24,16},{28,20},{1,9},{5... | collective-permute-start | bytes 307208 | tf_op jit(solution)/shard_map/ppermute | solution.py:301
  4.7 2.5 %collective-permute-start.1 = (bf16[400,128]{1,0:T(8,128)(2,1)S(1)}, bf16[400,128]{1,0:T(8,128)(2,1)S(1)}, u32[]{:S(2)}, u32[]{:S(2)}) collective-permute-start(bf16[400,128]{1,0:T(8,128)(2,1)S(1)} %bitcast_convert_fusion.refs_0_), channel_id=1, source_target_pairs={{0,24},{4,28},{8,16},{12,20},{16,8},{20,12},{24,0},{28,4},{1,25},{... | collective-permute-start | bytes 307208 | tf_op jit(solution)/shard_map/ppermute | solution.py:301
  7.1 0.1 collective-permute-start
  7.3 0.8 %pad_add_fusion = s32[5,1024]{1,0:T(8,128)S(1)} fusion(s32[2,1024]{1,0:T(2,128)} %bitcast.27, s32[1,1024]{1,0:T(1,128)} %bitcast.28, s32[1,1024]{1,0:T(1,128)} %bitcast.29, s32[1,1024]{1,0:T(1,128)} %bitcast.30), kind=kLoop, calls=%fused_computation | loop fusion | flops 15360 | bytes 40960 | tf_op jit(solution)/shard_map/concatenate | solution.py:346
  8.0 0.4 collective-permute-start.3
  8.4 0.9 %copy-done.1 = f32[128,400]{0,1:T(8,128)S(1)} copy-done((f32[128,400]{0,1:T(8,128)S(1)}, f32[128,400]{0,1:T(8,128)}, u32[]{:S(2)}) %copy-start.1) | copy-done | bytes 204824
  9.4 0.3 shard_map.145.refs_0_
  9.7 1.2 %collective-permute-start.2 = (bf16[400,128]{1,0:T(8,128)(2,1)S(1)}, bf16[400,128]{1,0:T(8,128)(2,1)S(1)}, u32[]{:S(2)}, u32[]{:S(2)}) collective-permute-start(bf16[400,128]{1,0:T(8,128)(2,1)S(1)} %shard_map.145.refs_0_), channel_id=1, source_target_pairs={{0,2},{1,3},{2,0},{3,1},{4,6},{5,7},{6,4},{7,5},{8,10},{9,11},{10,... | collective-permute-start | bytes 307208 | tf_op jit(solution)/shard_map/ppermute | solution.py:304
  10.9 0.1 pad_add_fusion.1.refs_2_
  11.0 1.6 %collective-permute-start.7 = (bf16[400,256]{1,0:T(8,128)(2,1)S(1)}, bf16[400,256]{1,0:T(8,128)(2,1)S(1)}, u32[]{:S(2)}, u32[]{:S(2)}) collective-permute-start(bf16[400,256]{1,0:T(8,128)(2,1)S(1)} %shard_map.146.refs_3_), channel_id=1, source_target_pairs={{0,4},{4,0},{8,12},{12,8},{16,20},{20,16},{24,28},{28,24},{1,5},{5... | collective-permute-start | bytes 614408 | tf_op jit(solution)/shard_map/ppermute | solution.py:301
  12.6 1.6 %shard_map.147 = (f32[2,1024,128]{2,1,0:T(8,128)S(1)}, bf16[400,256]{1,0:T(8,128)(2,1)S(1)}, s32[5,1024]{1,0:T(8,128)S(1)}) custom-call(s32[5,1024]{1,0:T(8,128)S(1)} %collective-permute-done.3.refs_0_, f32[400,256]{1,0:T(8,128)S(1)} %bitcast.19, s32[2]{0:T(128)S(1)} %pad_add_fusion.1.refs_2_, bf16[400,256]{1,0:T(8,128)(2,1)S(1)} %shard_map.146.refs_3_), custom_call_target="tpu_custom_call" | custom-call | tf_op jit(solution)/shard_map/pallas_call | solution.py:54
  14.1 0.5 collective-permute-done.2.refs_1_
  14.7 0.1 collective-permute-start.6
  14.8 1.6 %collective-permute-done.refs_0_.refs_2_ = bf16[400,128]{1,0:T(8,128)(2,1)S(1)} collective-permute-done((bf16[400,128]{1,0:T(8,128)(2,1)S(1)}, bf16[400,128]{1,0:T(8,128)(2,1)S(1)}, u32[]{:S(2)}, u32[]{:S(2)}) %collective-permute-start) | collective-permute-done | bytes 102432 | tf_op jit(solution)/shard_map/ppermute | solution.py:301
  16.5 1.6 %collective-permute-start.5 = (bf16[400,256]{1,0:T(8,128)(2,1)S(1)}, bf16[400,256]{1,0:T(8,128)(2,1)S(1)}, u32[]{:S(2)}, u32[]{:S(2)}) collective-permute-start(bf16[400,256]{1,0:T(8,128)(2,1)S(1)} %shard_map.149.refs_2_), channel_id=1, source_target_pairs={{0,4},{4,0},{8,12},{12,8},{16,20},{20,16},{24,28},{28,24},{1,5},{5... | collective-permute-start | bytes 614408 | tf_op jit(solution)/shard_map/ppermute | solution.py:301
  18.2 0.1 collective-permute-done.7.refs_0_
  18.3 0.9 %shard_map.150 = (bf16[400,1024]{1,0:T(8,128)(2,1)S(1)}, bf16[400,1024]{1,0:T(8,128)(2,1)S(1)}, bf16[400,1024]{1,0:T(8,128)(2,1)S(1)}) custom-call(bf16[400,128]{1,0:T(8,128)(2,1)S(1)} %shard_map.145.refs_0_, bf16[400,128]{1,0:T(8,128)(2,1)S(1)} %collective-permute-done.2.refs_1_, bf16[400,256]{1,0:T(8,128)(2,1)S(1)} %collective-permute-done.6.refs_2_, ...), custom_call_target="tpu_custom_call" | custom-call | flops 6000000000 | tf_op jit(solution)/shard_map/pallas_call | solution.py:54
  19.2 1.8 %shard_map.152 = (f32[400,512]{1,0:T(8,128)S(1)}, f32[400,1024]{1,0:T(8,128)S(1)}) custom-call(bf16[400,128]{1,0:T(8,128)(2,1)S(1)} %bitcast_convert_fusion.refs_0_, bf16[400,128]{1,0:T(8,128)(2,1)S(1)} %collective-permute-done.4.refs_1_, bf16[400,128]{1,0:T(8,128)(2,1)S(1)} %collective-permute-done.refs_0_.refs_2_, ...), custom_call_target="tpu_custom_call" | custom-call | tf_op jit(solution)/shard_map/pallas_call | solution.py:54
  21.0 1.0 %shard_map.153 = (bf16[400,256]{1,0:T(8,128)(2,1)S(1)}, f32[400,1024]{1,0:T(8,128)S(1)}) custom-call(bf16[400,256]{1,0:T(8,128)(2,1)S(1)} %shard_map.151.rows_ref, bf16[400,1024]{1,0:T(8,128)(2,1)S(1)} %get-tuple-element.41.refs_4_.q_ref.refs_1_, f32[2,1024,128]{2,1,0:T(8,128)S(1)} %get-tuple-element.38.refs_2_.refs_5_.weight_ref, ...), custom_call_target="tpu_custom_call" | custom-call | tf_op jit(solution)/shard_map/pallas_call | solution.py:54
  22.1 1.0 %collective-permute-done.5.refs_0_ = bf16[400,256]{1,0:T(8,128)(2,1)S(1)} collective-permute-done((bf16[400,256]{1,0:T(8,128)(2,1)S(1)}, bf16[400,256]{1,0:T(8,128)(2,1)S(1)}, u32[]{:S(2)}, u32[]{:S(2)}) %collective-permute-start.5) | collective-permute-done | bytes 204832 | tf_op jit(solution)/shard_map/ppermute | solution.py:301
  23.0 0.3 collective-permute-done.8.refs_7_.refs_4_.refs_5_
  23.4 1.9 %shard_map.155 = (bf16[256,1024]{1,0:T(8,128)(2,1)S(1)}, f32[400,1024]{1,0:T(8,128)S(1)}, f32[416,128]{1,0:T(8,128)S(1)}, bf16[416,128]{1,0:T(8,128)(2,1)S(1)}) custom-call(bf16[400,256]{1,0:T(8,128)(2,1)S(1)} %collective-permute-done.5.refs_0_, bf16[400,1024]{1,0:T(8,128)(2,1)S(1)} %get-tuple-element.41.refs_4_.q_ref.refs_1_, ...), custom_call_target="tpu_custom_call" | custom-call | tf_op jit(solution)/shard_map/pallas_call | solution.py:54
  25.2 0.3 collective-permute-start.17
  25.5 1.0 %shard_map.156 = (bf16[400,256]{1,0:T(8,128)(2,1)S(1)}, bf16[400,256]{1,0:T(8,128)(2,1)S(1)}, f32[400,256]{1,0:T(8,128)S(1)}, bf16[400,256]{1,0:T(8,128)(2,1)S(1)}) custom-call(bf16[256,1024]{1,0:T(8,128)(2,1)S(1)} %get-tuple-element.45.m_ref, bf16[400,1024]{1,0:T(8,128)(2,1)S(1)} %get-tuple-element.41.refs_4_.q_ref.refs_1_, ...), custom_call_target="tpu_custom_call" | custom-call | tf_op jit(solution)/shard_map/pallas_call | solution.py:54
  26.5 0.4 collective-permute-start.9
  26.9 1.6 %collective-permute-start.18 = (bf16[208,128]{1,0:T(8,128)(2,1)S(1)}, bf16[208,128]{1,0:T(8,128)(2,1)S(1)}, u32[]{:S(2)}, u32[]{:S(2)}) collective-permute-start(bf16[208,128]{1,0:T(8,128)(2,1)S(1)} %get-tuple-element.67), channel_id=1, source_target_pairs={{0,2},{1,3},{2,0},{3,1},{4,6},{5,7},{6,4},{7,5},{8,10},{9,11},{10,... | collective-permute-start | bytes 159752 | tf_op jit(solution)/shard_map/ppermute | solution.py:304
  28.5 1.2 %collective-permute-start.11 = (bf16[400,256]{1,0:T(8,128)(2,1)S(1)}, bf16[400,256]{1,0:T(8,128)(2,1)S(1)}, u32[]{:S(2)}, u32[]{:S(2)}) collective-permute-start(bf16[400,256]{1,0:T(8,128)(2,1)S(1)} %get-tuple-element.56), channel_id=1, source_target_pairs={{0,4},{4,0},{8,12},{12,8},{16,20},{20,16},{24,28},{28,24},{1,5},{5... | collective-permute-start | bytes 614408 | tf_op jit(solution)/shard_map/ppermute | solution.py:301
  29.7 1.4 %collective-permute-done.18.refs_1_ = bf16[208,128]{1,0:T(8,128)(2,1)S(1)} collective-permute-done((bf16[208,128]{1,0:T(8,128)(2,1)S(1)}, bf16[208,128]{1,0:T(8,128)(2,1)S(1)}, u32[]{:S(2)}, u32[]{:S(2)}) %collective-permute-start.18) | collective-permute-done | bytes 53280 | tf_op jit(solution)/shard_map/ppermute | solution.py:304
  31.1 2.2 %collective-permute-start.19 = (bf16[208,128]{1,0:T(8,128)(2,1)S(1)}, bf16[208,128]{1,0:T(8,128)(2,1)S(1)}, u32[]{:S(2)}, u32[]{:S(2)}) collective-permute-start(bf16[208,128]{1,0:T(8,128)(2,1)S(1)} %shard_map.163.refs_0_), channel_id=1, source_target_pairs={{0,16},{4,20},{8,24},{12,28},{16,0},{20,4},{24,8},{28,12},{1,17},{... | collective-permute-start | bytes 159752 | tf_op jit(solution)/shard_map/ppermute | solution.py:301
  33.3 1.5 %collective-permute-start.14 = (bf16[400,256]{1,0:T(8,128)(2,1)S(1)}, bf16[400,256]{1,0:T(8,128)(2,1)S(1)}, u32[]{:S(2)}, u32[]{:S(2)}) collective-permute-start(bf16[400,256]{1,0:T(8,128)(2,1)S(1)} %get-tuple-element.59), channel_id=1, source_target_pairs={{0,4},{4,0},{8,12},{12,8},{16,20},{20,16},{24,28},{28,24},{1,5},{5... | collective-permute-start | bytes 614408 | tf_op jit(solution)/shard_map/ppermute | solution.py:301
  34.9 1.3 %collective-permute-start.10 = (bf16[400,128]{1,0:T(8,128)(2,1)S(1)}, bf16[400,128]{1,0:T(8,128)(2,1)S(1)}, u32[]{:S(2)}, u32[]{:S(2)}) collective-permute-start(bf16[400,128]{1,0:T(8,128)(2,1)S(1)} %get-tuple-element.52), channel_id=1, source_target_pairs={{0,2},{1,3},{2,0},{3,1},{4,6},{5,7},{6,4},{7,5},{8,10},{9,11},{10,... | collective-permute-start | bytes 307208 | tf_op jit(solution)/shard_map/ppermute | solution.py:304
  36.2 0.1 collective-permute-done.19.refs_1_
  36.3 1.2 %collective-permute-start.20 = (bf16[208,128]{1,0:T(8,128)(2,1)S(1)}, bf16[208,128]{1,0:T(8,128)(2,1)S(1)}, u32[]{:S(2)}, u32[]{:S(2)}) collective-permute-start(bf16[208,128]{1,0:T(8,128)(2,1)S(1)} %shard_map.164.refs_0_), channel_id=1, source_target_pairs={{0,8},{4,12},{8,0},{12,4},{16,24},{20,28},{24,16},{28,20},{1,9},{5... | collective-permute-start | bytes 159752 | tf_op jit(solution)/shard_map/ppermute | solution.py:301
  37.5 0.1 shard_map.159
  37.5 0.1 collective-permute-start.12
  37.6 4.5 %collective-permute-start.13 = (bf16[400,128]{1,0:T(8,128)(2,1)S(1)}, bf16[400,128]{1,0:T(8,128)(2,1)S(1)}, u32[]{:S(2)}, u32[]{:S(2)}) collective-permute-start(bf16[400,128]{1,0:T(8,128)(2,1)S(1)} %get-tuple-element.58), channel_id=1, source_target_pairs={{0,25},{1,26},{2,27},{3,24},{4,29},{5,30},{6,31},{7,28},{8,17},{9,... | collective-permute-start | bytes 307208 | tf_op jit(solution)/shard_map/ppermute | solution.py:311
  42.1 0.7 %collective-permute-start.21 = (bf16[208,128]{1,0:T(8,128)(2,1)S(1)}, bf16[208,128]{1,0:T(8,128)(2,1)S(1)}, u32[]{:S(2)}, u32[]{:S(2)}) collective-permute-start(bf16[208,128]{1,0:T(8,128)(2,1)S(1)} %shard_map.165.refs_0_), channel_id=1, source_target_pairs={{0,4},{4,0},{8,12},{12,8},{16,20},{20,16},{24,28},{28,24},{1,5},{5... | collective-permute-start | bytes 159752 | tf_op jit(solution)/shard_map/ppermute | solution.py:301
  42.8 0.1 shard_map.160
  42.9 1.3 %collective-permute-start.16 = (bf16[400,128]{1,0:T(8,128)(2,1)S(1)}, bf16[400,128]{1,0:T(8,128)(2,1)S(1)}, u32[]{:S(2)}, u32[]{:S(2)}) collective-permute-start(bf16[400,128]{1,0:T(8,128)(2,1)S(1)} %get-tuple-element.61), channel_id=1, source_target_pairs={{0,9},{1,10},{2,11},{3,8},{4,13},{5,14},{6,15},{7,12},{8,1},{9,2},... | collective-permute-start | bytes 307208 | tf_op jit(solution)/shard_map/ppermute | solution.py:311
  44.2 2.0 %collective-permute-done.21.refs_1_ = bf16[208,128]{1,0:T(8,128)(2,1)S(1)} collective-permute-done((bf16[208,128]{1,0:T(8,128)(2,1)S(1)}, bf16[208,128]{1,0:T(8,128)(2,1)S(1)}, u32[]{:S(2)}, u32[]{:S(2)}) %collective-permute-start.21) | collective-permute-done | bytes 53280 | tf_op jit(solution)/shard_map/ppermute | solution.py:301
  46.3 0.5 collective-permute-start.22
  46.8 0.8 %shard_map.158 = (f32[400,128]{1,0:T(8,128)}, f32[1,128]{1,0:T(1,128)}) custom-call(f32[400,128]{1,0:T(8,128)S(1)} %get-tuple-element.51.refs_0_, bf16[400,128]{1,0:T(8,128)(2,1)S(1)} %collective-permute-done.10.refs_1_.refs_2_, f32[400,128]{1,0:T(8,128)S(1)} %bitcast.22, f32[1,128]{1,0:T(1,128)S(1)} %bitcast.25), custom_call_target="tpu_custom_call" | custom-call | tf_op jit(solution)/shard_map/pallas_call | solution.py:54
  47.6 3.5 %collective-permute-done.22.refs_1_ = bf16[208,128]{1,0:T(8,128)(2,1)S(1)} collective-permute-done((bf16[208,128]{1,0:T(8,128)(2,1)S(1)}, bf16[208,128]{1,0:T(8,128)(2,1)S(1)}, u32[]{:S(2)}, u32[]{:S(2)}) %collective-permute-start.22) | collective-permute-done | bytes 53280 | tf_op jit(solution)/shard_map/ppermute | solution.py:304
  51.1 0.1 collective-permute-start.23
  51.2 0.8 %shard_map.161 = (f32[400,128]{1,0:T(8,128)}, f32[1,128]{1,0:T(1,128)}) custom-call(bf16[400,128]{1,0:T(8,128)(2,1)S(1)} %collective-permute-done.12.refs_0_, bf16[400,128]{1,0:T(8,128)(2,1)S(1)} %collective-permute-done.13.refs_1_, bf16[400,128]{1,0:T(8,128)(2,1)S(1)} %collective-permute-done.15.refs_2_, ...), custom_call_target="tpu_custom_call" | custom-call | flops 12000000000 | tf_op jit(solution)/shard_map/pallas_call | solution.py:54
  52.0 0.5 collective-permute-done.23.refs_2_
  52.5 0.9 %shard_map.168 = (f32[400,256]{1,0:T(8,128)}, f32[1,256]{1,0:T(1,128)}) custom-call(bf16[208,128]{1,0:T(8,128)(2,1)S(1)} %shard_map.166.refs_0_, bf16[208,128]{1,0:T(8,128)(2,1)S(1)} %collective-permute-done.22.refs_1_, bf16[416,128]{1,0:T(8,128)(2,1)S(1)} %collective-permute-done.23.refs_2_, f32[400,256]{1,0:T(8,128)S(1)} %bitcast.20, ...), custom_call_target="tpu_custom_call" | custom-call | tf_op jit(solution)/shard_map/pallas_call | solution.py:54
  (41 shorter events, 0.5 us)
Async XLA Ops:
  1.6 9.4 %collective-permute-start.4 = (bf16[400,128]{1,0:T(8,128)(2,1)S(1)}, bf16[400,128]{1,0:T(8,128)(2,1)S(1)}, u32[]{:S(2)}, u32[]{:S(2)}) collective-permute-start(bf16[400,128]{1,0:T(8,128)(2,1)S(1)} %bitcast_convert_fusion.refs_0_), channel_id=1, source_target_pairs={{0,8},{4,12},{8,0},{12,4},{16,24},{20,28},{24,16},{28,20},{1,9},{5... | collective-permute-start | bytes 307208 | tf_op jit(solution)/shard_map/ppermute | solution.py:301
  4.7 10.1 %collective-permute-start.1 = (bf16[400,128]{1,0:T(8,128)(2,1)S(1)}, bf16[400,128]{1,0:T(8,128)(2,1)S(1)}, u32[]{:S(2)}, u32[]{:S(2)}) collective-permute-start(bf16[400,128]{1,0:T(8,128)(2,1)S(1)} %bitcast_convert_fusion.refs_0_), channel_id=1, source_target_pairs={{0,24},{4,28},{8,16},{12,20},{16,8},{20,12},{24,0},{28,4},{1,25},{... | collective-permute-start | bytes 307208 | tf_op jit(solution)/shard_map/ppermute | solution.py:301
  7.1 9.3 %collective-permute-start = (bf16[400,128]{1,0:T(8,128)(2,1)S(1)}, bf16[400,128]{1,0:T(8,128)(2,1)S(1)}, u32[]{:S(2)}, u32[]{:S(2)}) collective-permute-start(bf16[400,128]{1,0:T(8,128)(2,1)S(1)} %bitcast_convert_fusion.refs_0_), channel_id=1, source_target_pairs={{0,16},{4,20},{8,24},{12,28},{16,0},{20,4},{24,8},{28,12},{1,17},{... | collective-permute-start | bytes 307208 | tf_op jit(solution)/shard_map/ppermute | solution.py:301
  8.0 4.6 %collective-permute-start.3 = (s32[5,1024]{1,0:T(8,128)S(1)}, s32[5,1024]{1,0:T(8,128)S(1)}, u32[]{:S(2)}, u32[]{:S(2)}) collective-permute-start(s32[5,1024]{1,0:T(8,128)S(1)} %pad_add_fusion), channel_id=1, source_target_pairs={{0,3},{1,0},{2,1},{3,2},{4,7},{5,4},{6,5},{7,6},{8,11},{9,8},{10,9... | collective-permute-start | bytes 61448 | tf_op jit(solution)/shard_map/ppermute | solution.py:347
  8.4 0.9 %copy-start.1 = (f32[128,400]{0,1:T(8,128)S(1)}, f32[128,400]{0,1:T(8,128)}, u32[]{:S(2)}) copy-start(f32[128,400]{0,1:T(8,128)} %param.10) | copy-start | bytes 614404
  9.7 5.0 %collective-permute-start.2 = (bf16[400,128]{1,0:T(8,128)(2,1)S(1)}, bf16[400,128]{1,0:T(8,128)(2,1)S(1)}, u32[]{:S(2)}, u32[]{:S(2)}) collective-permute-start(bf16[400,128]{1,0:T(8,128)(2,1)S(1)} %shard_map.145.refs_0_), channel_id=1, source_target_pairs={{0,2},{1,3},{2,0},{3,1},{4,6},{5,7},{6,4},{7,5},{8,10},{9,11},{10,... | collective-permute-start | bytes 307208 | tf_op jit(solution)/shard_map/ppermute | solution.py:304
  11.0 1.6 %copy-start = (f32[256,400]{0,1:T(8,128)S(1)}, f32[256,400]{0,1:T(8,128)}, u32[]{:S(2)}) copy-start(f32[256,400]{0,1:T(8,128)} %param.14) | copy-start | bytes 1228804
  11.0 7.3 %collective-permute-start.7 = (bf16[400,256]{1,0:T(8,128)(2,1)S(1)}, bf16[400,256]{1,0:T(8,128)(2,1)S(1)}, u32[]{:S(2)}, u32[]{:S(2)}) collective-permute-start(bf16[400,256]{1,0:T(8,128)(2,1)S(1)} %shard_map.146.refs_3_), channel_id=1, source_target_pairs={{0,4},{4,0},{8,12},{12,8},{16,20},{20,16},{24,28},{28,24},{1,5},{5... | collective-permute-start | bytes 614408 | tf_op jit(solution)/shard_map/ppermute | solution.py:301
  14.7 3.4 %copy-start.3 = (f32[128,400]{0,1:T(8,128)S(1)}, f32[128,400]{0,1:T(8,128)}, u32[]{:S(2)}) copy-start(f32[128,400]{0,1:T(8,128)} %param.12) | copy-start | bytes 614404
  14.7 3.3 %copy-start.6 = (f32[128]{0:T(128)S(1)}, f32[128]{0:T(128)}, u32[]{:S(2)}) copy-start(f32[128]{0:T(128)} %param.13) | copy-start | bytes 1540
  14.7 3.5 %collective-permute-start.6 = (bf16[400,256]{1,0:T(8,128)(2,1)S(1)}, bf16[400,256]{1,0:T(8,128)(2,1)S(1)}, u32[]{:S(2)}, u32[]{:S(2)}) collective-permute-start(bf16[400,256]{1,0:T(8,128)(2,1)S(1)} %shard_map.148.refs_2_), channel_id=1, source_target_pairs={{0,1},{1,0},{2,3},{3,2},{4,5},{5,4},{6,7},{7,6},{8,9},{9,8},{10,11... | collective-permute-start | bytes 614408 | tf_op jit(solution)/shard_map/ppermute | solution.py:304
  16.5 6.6 %collective-permute-start.5 = (bf16[400,256]{1,0:T(8,128)(2,1)S(1)}, bf16[400,256]{1,0:T(8,128)(2,1)S(1)}, u32[]{:S(2)}, u32[]{:S(2)}) collective-permute-start(bf16[400,256]{1,0:T(8,128)(2,1)S(1)} %shard_map.149.refs_2_), channel_id=1, source_target_pairs={{0,4},{4,0},{8,12},{12,8},{16,20},{20,16},{24,28},{28,24},{1,5},{5... | collective-permute-start | bytes 614408 | tf_op jit(solution)/shard_map/ppermute | solution.py:301
  18.1 5.3 %collective-permute-start.8 = (f32[408,128]{1,0:T(8,128)S(1)}, f32[408,128]{1,0:T(8,128)S(1)}, u32[]{:S(2)}, u32[]{:S(2)}) collective-permute-start(f32[408,128]{1,0:T(8,128)S(1)} %shard_map.154), channel_id=1, source_target_pairs={{0,1},{1,2},{2,3},{3,0},{4,5},{5,6},{6,7},{7,4},{8,9},{9,10},{10,1... | collective-permute-start | bytes 626696 | tf_op jit(solution)/shard_map/ppermute | solution.py:311
  25.2 1.6 %collective-permute-start.17 = (bf16[416,128]{1,0:T(8,128)(2,1)S(1)}, bf16[416,128]{1,0:T(8,128)(2,1)S(1)}, u32[]{:S(2)}, u32[]{:S(2)}) collective-permute-start(bf16[416,128]{1,0:T(8,128)(2,1)S(1)} %get-tuple-element.65), channel_id=1, source_target_pairs={{0,1},{1,0},{2,3},{3,2},{4,5},{5,4},{6,7},{7,6},{8,9},{9,8},{10,11... | collective-permute-start | bytes 319496 | tf_op jit(solution)/shard_map/ppermute | solution.py:304
  26.5 8.3 %collective-permute-start.9 = (bf16[400,256]{1,0:T(8,128)(2,1)S(1)}, bf16[400,256]{1,0:T(8,128)(2,1)S(1)}, u32[]{:S(2)}, u32[]{:S(2)}) collective-permute-start(bf16[400,256]{1,0:T(8,128)(2,1)S(1)} %get-tuple-element.50), channel_id=1, source_target_pairs={{0,1},{1,0},{2,3},{3,2},{4,5},{5,4},{6,7},{7,6},{8,9},{9,8},{10,11... | collective-permute-start | bytes 614408 | tf_op jit(solution)/shard_map/ppermute | solution.py:304
  26.9 4.2 %collective-permute-start.18 = (bf16[208,128]{1,0:T(8,128)(2,1)S(1)}, bf16[208,128]{1,0:T(8,128)(2,1)S(1)}, u32[]{:S(2)}, u32[]{:S(2)}) collective-permute-start(bf16[208,128]{1,0:T(8,128)(2,1)S(1)} %get-tuple-element.67), channel_id=1, source_target_pairs={{0,2},{1,3},{2,0},{3,1},{4,6},{5,7},{6,4},{7,5},{8,10},{9,11},{10,... | collective-permute-start | bytes 159752 | tf_op jit(solution)/shard_map/ppermute | solution.py:304
  28.5 9.0 %collective-permute-start.11 = (bf16[400,256]{1,0:T(8,128)(2,1)S(1)}, bf16[400,256]{1,0:T(8,128)(2,1)S(1)}, u32[]{:S(2)}, u32[]{:S(2)}) collective-permute-start(bf16[400,256]{1,0:T(8,128)(2,1)S(1)} %get-tuple-element.56), channel_id=1, source_target_pairs={{0,4},{4,0},{8,12},{12,8},{16,20},{20,16},{24,28},{28,24},{1,5},{5... | collective-permute-start | bytes 614408 | tf_op jit(solution)/shard_map/ppermute | solution.py:301
  31.1 5.1 %collective-permute-start.19 = (bf16[208,128]{1,0:T(8,128)(2,1)S(1)}, bf16[208,128]{1,0:T(8,128)(2,1)S(1)}, u32[]{:S(2)}, u32[]{:S(2)}) collective-permute-start(bf16[208,128]{1,0:T(8,128)(2,1)S(1)} %shard_map.163.refs_0_), channel_id=1, source_target_pairs={{0,16},{4,20},{8,24},{12,28},{16,0},{20,4},{24,8},{28,12},{1,17},{... | collective-permute-start | bytes 159752 | tf_op jit(solution)/shard_map/ppermute | solution.py:301
  33.3 9.5 %collective-permute-start.14 = (bf16[400,256]{1,0:T(8,128)(2,1)S(1)}, bf16[400,256]{1,0:T(8,128)(2,1)S(1)}, u32[]{:S(2)}, u32[]{:S(2)}) collective-permute-start(bf16[400,256]{1,0:T(8,128)(2,1)S(1)} %get-tuple-element.59), channel_id=1, source_target_pairs={{0,4},{4,0},{8,12},{12,8},{16,20},{20,16},{24,28},{28,24},{1,5},{5... | collective-permute-start | bytes 614408 | tf_op jit(solution)/shard_map/ppermute | solution.py:301
  34.9 7.9 %collective-permute-start.10 = (bf16[400,128]{1,0:T(8,128)(2,1)S(1)}, bf16[400,128]{1,0:T(8,128)(2,1)S(1)}, u32[]{:S(2)}, u32[]{:S(2)}) collective-permute-start(bf16[400,128]{1,0:T(8,128)(2,1)S(1)} %get-tuple-element.52), channel_id=1, source_target_pairs={{0,2},{1,3},{2,0},{3,1},{4,6},{5,7},{6,4},{7,5},{8,10},{9,11},{10,... | collective-permute-start | bytes 307208 | tf_op jit(solution)/shard_map/ppermute | solution.py:304
  36.3 5.8 %collective-permute-start.20 = (bf16[208,128]{1,0:T(8,128)(2,1)S(1)}, bf16[208,128]{1,0:T(8,128)(2,1)S(1)}, u32[]{:S(2)}, u32[]{:S(2)}) collective-permute-start(bf16[208,128]{1,0:T(8,128)(2,1)S(1)} %shard_map.164.refs_0_), channel_id=1, source_target_pairs={{0,8},{4,12},{8,0},{12,4},{16,24},{20,28},{24,16},{28,20},{1,9},{5... | collective-permute-start | bytes 159752 | tf_op jit(solution)/shard_map/ppermute | solution.py:301
  37.5 13.6 %collective-permute-start.12 = (bf16[400,128]{1,0:T(8,128)(2,1)S(1)}, bf16[400,128]{1,0:T(8,128)(2,1)S(1)}, u32[]{:S(2)}, u32[]{:S(2)}) collective-permute-start(bf16[400,128]{1,0:T(8,128)(2,1)S(1)} %get-tuple-element.57), channel_id=1, source_target_pairs={{0,17},{1,18},{2,19},{3,16},{4,21},{5,22},{6,23},{7,20},{8,25},{9,... | collective-permute-start | bytes 307208 | tf_op jit(solution)/shard_map/ppermute | solution.py:311
  37.6 13.6 %collective-permute-start.13 = (bf16[400,128]{1,0:T(8,128)(2,1)S(1)}, bf16[400,128]{1,0:T(8,128)(2,1)S(1)}, u32[]{:S(2)}, u32[]{:S(2)}) collective-permute-start(bf16[400,128]{1,0:T(8,128)(2,1)S(1)} %get-tuple-element.58), channel_id=1, source_target_pairs={{0,25},{1,26},{2,27},{3,24},{4,29},{5,30},{6,31},{7,28},{8,17},{9,... | collective-permute-start | bytes 307208 | tf_op jit(solution)/shard_map/ppermute | solution.py:311
  42.1 4.2 %collective-permute-start.21 = (bf16[208,128]{1,0:T(8,128)(2,1)S(1)}, bf16[208,128]{1,0:T(8,128)(2,1)S(1)}, u32[]{:S(2)}, u32[]{:S(2)}) collective-permute-start(bf16[208,128]{1,0:T(8,128)(2,1)S(1)} %shard_map.165.refs_0_), channel_id=1, source_target_pairs={{0,4},{4,0},{8,12},{12,8},{16,20},{20,16},{24,28},{28,24},{1,5},{5... | collective-permute-start | bytes 159752 | tf_op jit(solution)/shard_map/ppermute | solution.py:301
  42.8 8.3 %collective-permute-start.15 = (bf16[400,128]{1,0:T(8,128)(2,1)S(1)}, bf16[400,128]{1,0:T(8,128)(2,1)S(1)}, u32[]{:S(2)}, u32[]{:S(2)}) collective-permute-start(bf16[400,128]{1,0:T(8,128)(2,1)S(1)} %get-tuple-element.60), channel_id=1, source_target_pairs={{0,1},{1,2},{2,3},{3,0},{4,5},{5,6},{6,7},{7,4},{8,9},{9,10},{10,1... | collective-permute-start | bytes 307208 | tf_op jit(solution)/shard_map/ppermute | solution.py:311
  42.9 3.9 %copy-start.2 = (f32[128,400]{0,1:T(8,128)S(1)}, f32[128,400]{0,1:T(8,128)}, u32[]{:S(2)}) copy-start(f32[128,400]{0,1:T(8,128)} %param.10) | copy-start | bytes 614404
  42.9 3.9 %copy-start.5 = (f32[128]{0:T(128)S(1)}, f32[128]{0:T(128)}, u32[]{:S(2)}) copy-start(f32[128]{0:T(128)} %param.11) | copy-start | bytes 1540
  42.9 8.3 %collective-permute-start.16 = (bf16[400,128]{1,0:T(8,128)(2,1)S(1)}, bf16[400,128]{1,0:T(8,128)(2,1)S(1)}, u32[]{:S(2)}, u32[]{:S(2)}) collective-permute-start(bf16[400,128]{1,0:T(8,128)(2,1)S(1)} %get-tuple-element.61), channel_id=1, source_target_pairs={{0,9},{1,10},{2,11},{3,8},{4,13},{5,14},{6,15},{7,12},{8,1},{9,2},... | collective-permute-start | bytes 307208 | tf_op jit(solution)/shard_map/ppermute | solution.py:311
  46.3 4.8 %collective-permute-start.22 = (bf16[208,128]{1,0:T(8,128)(2,1)S(1)}, bf16[208,128]{1,0:T(8,128)(2,1)S(1)}, u32[]{:S(2)}, u32[]{:S(2)}) collective-permute-start(bf16[208,128]{1,0:T(8,128)(2,1)S(1)} %shard_map.166.refs_0_), channel_id=1, source_target_pairs={{0,2},{1,3},{2,0},{3,1},{4,6},{5,7},{6,4},{7,5},{8,10},{9,11},{10,... | collective-permute-start | bytes 159752 | tf_op jit(solution)/shard_map/ppermute | solution.py:304
  51.1 1.4 %copy-start.4 = (f32[256]{0:T(256)S(1)}, f32[256]{0:T(256)}, u32[]{:S(2)}) copy-start(f32[256]{0:T(256)} %param.15) | copy-start | bytes 3076
  51.1 1.4 %collective-permute-start.23 = (bf16[416,128]{1,0:T(8,128)(2,1)S(1)}, bf16[416,128]{1,0:T(8,128)(2,1)S(1)}, u32[]{:S(2)}, u32[]{:S(2)}) collective-permute-start(bf16[416,128]{1,0:T(8,128)(2,1)S(1)} %shard_map.167), channel_id=1, source_target_pairs={{0,1},{1,0},{2,3},{3,2},{4,5},{5,4},{6,7},{7,6},{8,9},{9,8},{10,11... | collective-permute-start | bytes 319496 | tf_op jit(solution)/shard_map/ppermute | solution.py:304

commit v16 on v15

--- a/solution.py
+++ b/solution.py
@@ -269,7 +269,7 @@
     for k, ref in enumerate(block_refs):
         cols = slice(k * LANES, (k + 1) * LANES)
         total = near_ref[:, base + k * LANES:base + (k + 1) * LANES] + got_ref[:, cols].astype(F32)
-        ref[...] = total.astype(BF)
+        ref[...] = total.astype(ref.dtype)
 
 
 def sum_body(*refs):
@@ -333,7 +333,7 @@
             return call(cast_body, one_block, scratch, after=after, place=pl.ANY)(value)
 
         right_bf = right_t.astype(BF)
-        near = [right_bf] + [swap_left(right_bf, 2 * k) for k in range(1, outer)]
+        near = [next_column(right_bf, 2 * k) for k in range(outer)]
         some = outer // 2
         cut = some * rows
         chunk = shape(width, cut, dtype=BF)
@@ -344,7 +344,6 @@
         longest = max(i.shape[-1] for i in ids)
         ids = [i.reshape(-1, i.shape[-1]) for i in ids]
         ids = jnp.concatenate([jnp.pad(i, ((0, 0), (0, longest - i.shape[-1]))) for i in ids], axis=0)
-        ids = lax.ppermute(ids, "right", [(i, (i - 1) % n_right) for i in range(n_right)])
         left_bf = cast(left_t)
         half_left = [left_bf] + [swap_right(left_bf, 2 * k) for k in range(1, far_right)]
         place = jnp.stack([here_r, here_l]).astype(jnp.int32)
@@ -413,9 +412,10 @@
         got_high = swap_left(right_high, 1)
         outs = (one_block,) * some
         high = call(functools.partial(chunk_body, cut), outs, flops=COST_HIGH)(right_near, got_high)
+        outs = (shape(width, rows),) + outs[1:]
         low = call(functools.partial(chunk_body, 0), outs, flops=COST_LOW, after=left_got)(right_near, got_low)
-        right_got = [next_column(block, 2 * (some + k)) for k, block in enumerate(high)]
-        right_got += [next_column(block, 2 * k) for k, block in enumerate(low)]
+        right_got = [low[0]] + [swap_left(block, 2 * (some + k)) for k, block in enumerate(high)]
+        right_got += [swap_left(low[k], 2 * k) for k in range(1, some)]
 
         def update(got, table, state, flops=0):
             outs = (shape(width, rows), shape(1, rows))

time: 53.6 us -> 54.1 us (level)
  waiting for transfers between devices: 11 us -> 13.7 us
  starting transfers between devices: 27.3 us -> 25.3 us
    ppermute x5, waiting for transfers between devices: 0.33 us -> 2.57 us  [next_column(): return lax.ppermute(value, ('left', 'right'), perm)]
    ppermute x10, starting transfers between devices: 15.6 us -> 14.4 us  [swap_left(): return lax.ppermute(value, 'left', [(i, i ^ by) for i in range(n_left)])]
    ppermute x8, starting transfers between devices: 5.38 us -> 4.4 us  [swap_right(): return lax.ppermute(value, 'right', [(i, i ^ by) for i in range(n_right)])]
    ppermute x10, waiting for transfers between devices: 4.81 us -> 5.43 us  [swap_left(): return lax.ppermute(value, 'left', [(i, i ^ by) for i in range(n_left)])]
  transfers between devices with their start and end apart: 24 -> 23, of which waited for: 10 -> 8; matrix products, arithmetic and copies ran while one was open for 2% -> 2% of each run, Pallas kernels for 16% -> 16%
where the time goes in v16:
time: 54.1 us; the launch traced here: 53.9 us
  starting transfers between devices  25.3 us (47%)
  waiting for transfers between devices  13.7 us (25%)
  Pallas kernels  11.3 us (21%)
  other arithmetic  1.78 us (3%)
  local copies, waits for them, and re-layouts  0.97 us (2%)
  between operations  0.88 us (2%)
    ppermute x10, starting transfers between devices, swap_left(): return lax.ppermute(value, 'left', [(i, i ^ by) for i in range(n_left)])  14.4 us
    pallas_call x24, Pallas kernels, run(): pl.pallas_call(inner, out_shape=out_shape, in_specs=specs, scratch_shapes...  11.3 us
    ppermute x5, starting transfers between devices, next_column(): return lax.ppermute(value, ('left', 'right'), perm)  6.44 us
    ppermute x8, waiting for transfers between devices, swap_right(): return lax.ppermute(value, 'right', [(i, i ^ by) for i in range(n_right)])  5.68 us
    ppermute x10, waiting for transfers between devices, swap_left(): return lax.ppermute(value, 'left', [(i, i ^ by) for i in range(n_left)])  5.43 us
    ppermute x8, starting transfers between devices, swap_right(): return lax.ppermute(value, 'right', [(i, i ^ by) for i in range(n_right)])  4.4 us
    ppermute x5, waiting for transfers between devices, next_column(): return lax.ppermute(value, ('left', 'right'), perm)  2.57 us
  transfers between devices with their start and end apart: 23, of which 8 were waited for; matrix products, arithmetic and copies ran while one was open for 2% of the time, Pallas kernels for 16%

profile of v16, /device:TPU:0, one launch (start us, length us, event | category | flops | bytes accessed | tf_op | source)
XLA Modules:
  0.0 53.9 jit_solution(263476488797728107)
XLA Ops:
  0.6 0.9 %bitcast_convert_fusion = bf16[400,128]{1,0:T(8,128)(2,1)S(1)} fusion(f32[128,400]{0,1:T(8,128)} %param.12), kind=kLoop, calls=%fused_computation.2 | loop fusion | flops 51200 | bytes 307200 | tf_op jit(solution)/shard_map/convert_element_type | solution.py:335
  1.6 2.5 %collective-permute-start.4 = (bf16[400,128]{1,0:T(8,128)(2,1)S(1)}, bf16[400,128]{1,0:T(8,128)(2,1)S(1)}, u32[]{:S(2)}, u32[]{:S(2)}) collective-permute-start(bf16[400,128]{1,0:T(8,128)(2,1)S(1)} %bitcast_convert_fusion), channel_id=1, source_target_pairs={{0,9},{1,10},{2,11},{3,8},{4,13},{5,14},{6,15},{7,12},{8,1},{9,2},... | collective-permute-start | bytes 307208 | tf_op jit(solution)/shard_map/ppermute | solution.py:311
  4.1 1.6 %collective-permute-start.3 = (bf16[400,128]{1,0:T(8,128)(2,1)S(1)}, bf16[400,128]{1,0:T(8,128)(2,1)S(1)}, u32[]{:S(2)}, u32[]{:S(2)}) collective-permute-start(bf16[400,128]{1,0:T(8,128)(2,1)S(1)} %bitcast_convert_fusion), channel_id=1, source_target_pairs={{0,1},{1,2},{2,3},{3,0},{4,5},{5,6},{6,7},{7,4},{8,9},{9,10},{10,1... | collective-permute-start | bytes 307208 | tf_op jit(solution)/shard_map/ppermute | solution.py:311
  5.7 2.3 %collective-permute-start.1 = (bf16[400,128]{1,0:T(8,128)(2,1)S(1)}, bf16[400,128]{1,0:T(8,128)(2,1)S(1)}, u32[]{:S(2)}, u32[]{:S(2)}) collective-permute-start(bf16[400,128]{1,0:T(8,128)(2,1)S(1)} %bitcast_convert_fusion), channel_id=1, source_target_pairs={{0,25},{1,26},{2,27},{3,24},{4,29},{5,30},{6,31},{7,28},{8,17},{9,... | collective-permute-start | bytes 307208 | tf_op jit(solution)/shard_map/ppermute | solution.py:311
  8.0 0.9 %copy-done.1 = f32[128,400]{0,1:T(8,128)S(1)} copy-done((f32[128,400]{0,1:T(8,128)S(1)}, f32[128,400]{0,1:T(8,128)}, u32[]{:S(2)}) %copy-start.1) | copy-done | bytes 204824
  8.9 0.3 shard_map.145.refs_0_
  9.2 0.9 %collective-permute-start.2 = (bf16[400,128]{1,0:T(8,128)(2,1)S(1)}, bf16[400,128]{1,0:T(8,128)(2,1)S(1)}, u32[]{:S(2)}, u32[]{:S(2)}) collective-permute-start(bf16[400,128]{1,0:T(8,128)(2,1)S(1)} %shard_map.145.refs_0_), channel_id=1, source_target_pairs={{0,2},{1,3},{2,0},{3,1},{4,6},{5,7},{6,4},{7,5},{8,10},{9,11},{10,... | collective-permute-start | bytes 307208 | tf_op jit(solution)/shard_map/ppermute | solution.py:304
  10.1 0.8 %pad_add_fusion.refs_0_ = s32[5,1024]{1,0:T(8,128)S(1)} fusion(s32[2,1024]{1,0:T(2,128)} %bitcast.27, s32[1,1024]{1,0:T(1,128)} %bitcast.28, s32[1,1024]{1,0:T(1,128)} %bitcast.29, s32[1,1024]{1,0:T(1,128)} %bitcast.30), kind=kLoop, calls=%fused_computation | loop fusion | flops 15360 | bytes 40960 | tf_op jit(solution)/shard_map/concatenate | solution.py:346
  10.9 0.1 pad_add_fusion.1.refs_2_
  11.0 1.6 %collective-permute-start.7 = (bf16[400,256]{1,0:T(8,128)(2,1)S(1)}, bf16[400,256]{1,0:T(8,128)(2,1)S(1)}, u32[]{:S(2)}, u32[]{:S(2)}) collective-permute-start(bf16[400,256]{1,0:T(8,128)(2,1)S(1)} %shard_map.146.refs_3_), channel_id=1, source_target_pairs={{0,4},{4,0},{8,12},{12,8},{16,20},{20,16},{24,28},{28,24},{1,5},{5... | collective-permute-start | bytes 614408 | tf_op jit(solution)/shard_map/ppermute | solution.py:301
  12.6 1.6 %shard_map.147 = (f32[2,1024,128]{2,1,0:T(8,128)S(1)}, bf16[400,256]{1,0:T(8,128)(2,1)S(1)}, s32[5,1024]{1,0:T(8,128)S(1)}) custom-call(s32[5,1024]{1,0:T(8,128)S(1)} %pad_add_fusion.refs_0_, f32[400,256]{1,0:T(8,128)S(1)} %bitcast.19, s32[2]{0:T(128)S(1)} %pad_add_fusion.1.refs_2_, bf16[400,256]{1,0:T(8,128)(2,1)S(1)} %shard_map.146.refs_3_), custom_call_target="tpu_custom_call" | custom-call | tf_op jit(solution)/shard_map/pallas_call | solution.py:54
  14.1 1.1 %collective-permute-done.2.refs_1_ = bf16[400,128]{1,0:T(8,128)(2,1)S(1)} collective-permute-done((bf16[400,128]{1,0:T(8,128)(2,1)S(1)}, bf16[400,128]{1,0:T(8,128)(2,1)S(1)}, u32[]{:S(2)}, u32[]{:S(2)}) %collective-permute-start.2) | collective-permute-done | bytes 102432 | tf_op jit(solution)/shard_map/ppermute | solution.py:304
  15.3 0.0 copy-start.6
  15.3 0.1 collective-permute-start.6
  15.4 2.6 %collective-permute-done.refs_0_.refs_2_ = bf16[400,128]{1,0:T(8,128)(2,1)S(1)} collective-permute-done((bf16[400,128]{1,0:T(8,128)(2,1)S(1)}, bf16[400,128]{1,0:T(8,128)(2,1)S(1)}, u32[]{:S(2)}, u32[]{:S(2)}) %collective-permute-start) | collective-permute-done | bytes 102432 | tf_op jit(solution)/shard_map/ppermute | solution.py:311
  18.0 1.6 %collective-permute-start.5 = (bf16[400,256]{1,0:T(8,128)(2,1)S(1)}, bf16[400,256]{1,0:T(8,128)(2,1)S(1)}, u32[]{:S(2)}, u32[]{:S(2)}) collective-permute-start(bf16[400,256]{1,0:T(8,128)(2,1)S(1)} %shard_map.149.refs_2_), channel_id=1, source_target_pairs={{0,4},{4,0},{8,12},{12,8},{16,20},{20,16},{24,28},{28,24},{1,5},{5... | collective-permute-start | bytes 614408 | tf_op jit(solution)/shard_map/ppermute | solution.py:301
  19.6 0.1 collective-permute-start.8
  19.7 0.9 %shard_map.150 = (bf16[400,1024]{1,0:T(8,128)(2,1)S(1)}, bf16[400,1024]{1,0:T(8,128)(2,1)S(1)}, bf16[400,1024]{1,0:T(8,128)(2,1)S(1)}) custom-call(bf16[400,128]{1,0:T(8,128)(2,1)S(1)} %shard_map.145.refs_0_, bf16[400,128]{1,0:T(8,128)(2,1)S(1)} %collective-permute-done.2.refs_1_, bf16[400,256]{1,0:T(8,128)(2,1)S(1)} %collective-permute-done.6.refs_2_, ...), custom_call_target="tpu_custom_call" | custom-call | flops 6000000000 | tf_op jit(solution)/shard_map/pallas_call | solution.py:54
  20.6 1.8 %shard_map.152 = (f32[400,512]{1,0:T(8,128)S(1)}, f32[400,1024]{1,0:T(8,128)S(1)}) custom-call(bf16[400,128]{1,0:T(8,128)(2,1)S(1)} %collective-permute-done.3.refs_0_, bf16[400,128]{1,0:T(8,128)(2,1)S(1)} %collective-permute-done.4.refs_1_, bf16[400,128]{1,0:T(8,128)(2,1)S(1)} %collective-permute-done.refs_0_.refs_2_, ...), custom_call_target="tpu_custom_call" | custom-call | tf_op jit(solution)/shard_map/pallas_call | solution.py:54
  22.4 1.0 %shard_map.153 = (bf16[400,256]{1,0:T(8,128)(2,1)S(1)}, f32[400,1024]{1,0:T(8,128)S(1)}) custom-call(bf16[400,256]{1,0:T(8,128)(2,1)S(1)} %shard_map.151.rows_ref, bf16[400,1024]{1,0:T(8,128)(2,1)S(1)} %get-tuple-element.41.refs_4_.q_ref.refs_1_, f32[2,1024,128]{2,1,0:T(8,128)S(1)} %get-tuple-element.38.refs_2_.refs_5_.weight_ref, ...), custom_call_target="tpu_custom_call" | custom-call | tf_op jit(solution)/shard_map/pallas_call | solution.py:54
  23.5 1.7 %collective-permute-done.5.refs_0_ = bf16[400,256]{1,0:T(8,128)(2,1)S(1)} collective-permute-done((bf16[400,256]{1,0:T(8,128)(2,1)S(1)}, bf16[400,256]{1,0:T(8,128)(2,1)S(1)}, u32[]{:S(2)}, u32[]{:S(2)}) %collective-permute-start.5) | collective-permute-done | bytes 204832 | tf_op jit(solution)/shard_map/ppermute | solution.py:301
  25.1 1.9 %shard_map.155 = (bf16[256,1024]{1,0:T(8,128)(2,1)S(1)}, f32[400,1024]{1,0:T(8,128)S(1)}, f32[416,128]{1,0:T(8,128)S(1)}, bf16[416,128]{1,0:T(8,128)(2,1)S(1)}) custom-call(bf16[400,256]{1,0:T(8,128)(2,1)S(1)} %collective-permute-done.5.refs_0_, bf16[400,1024]{1,0:T(8,128)(2,1)S(1)} %get-tuple-element.41.refs_4_.q_ref.refs_1_, ...), custom_call_target="tpu_custom_call" | custom-call | tf_op jit(solution)/shard_map/pallas_call | solution.py:54
  27.0 0.1 collective-permute-start.16
  27.1 1.0 %shard_map.156 = (bf16[400,256]{1,0:T(8,128)(2,1)S(1)}, bf16[400,256]{1,0:T(8,128)(2,1)S(1)}, f32[400,256]{1,0:T(8,128)S(1)}, bf16[400,256]{1,0:T(8,128)(2,1)S(1)}) custom-call(bf16[256,1024]{1,0:T(8,128)(2,1)S(1)} %get-tuple-element.45.m_ref, bf16[400,1024]{1,0:T(8,128)(2,1)S(1)} %get-tuple-element.41.refs_4_.q_ref.refs_1_, ...), custom_call_target="tpu_custom_call" | custom-call | tf_op jit(solution)/shard_map/pallas_call | solution.py:54
  28.1 0.6 %collective-permute-start.9 = (bf16[400,256]{1,0:T(8,128)(2,1)S(1)}, bf16[400,256]{1,0:T(8,128)(2,1)S(1)}, u32[]{:S(2)}, u32[]{:S(2)}) collective-permute-start(bf16[400,256]{1,0:T(8,128)(2,1)S(1)} %get-tuple-element.50), channel_id=1, source_target_pairs={{0,1},{1,0},{2,3},{3,2},{4,5},{5,4},{6,7},{7,6},{8,9},{9,8},{10,11... | collective-permute-start | bytes 614408 | tf_op jit(solution)/shard_map/ppermute | solution.py:304
  28.7 0.9 %collective-permute-start.17 = (bf16[208,128]{1,0:T(8,128)(2,1)S(1)}, bf16[208,128]{1,0:T(8,128)(2,1)S(1)}, u32[]{:S(2)}, u32[]{:S(2)}) collective-permute-start(bf16[208,128]{1,0:T(8,128)(2,1)S(1)} %get-tuple-element.67), channel_id=1, source_target_pairs={{0,2},{1,3},{2,0},{3,1},{4,6},{5,7},{6,4},{7,5},{8,10},{9,11},{10,... | collective-permute-start | bytes 159752 | tf_op jit(solution)/shard_map/ppermute | solution.py:304
  29.6 1.5 %collective-permute-start.12 = (bf16[400,256]{1,0:T(8,128)(2,1)S(1)}, bf16[400,256]{1,0:T(8,128)(2,1)S(1)}, u32[]{:S(2)}, u32[]{:S(2)}) collective-permute-start(bf16[400,256]{1,0:T(8,128)(2,1)S(1)} %get-tuple-element.58), channel_id=1, source_target_pairs={{0,4},{4,0},{8,12},{12,8},{16,20},{20,16},{24,28},{28,24},{1,5},{5... | collective-permute-start | bytes 614408 | tf_op jit(solution)/shard_map/ppermute | solution.py:301
  31.1 1.8 %collective-permute-done.17.refs_1_ = bf16[208,128]{1,0:T(8,128)(2,1)S(1)} collective-permute-done((bf16[208,128]{1,0:T(8,128)(2,1)S(1)}, bf16[208,128]{1,0:T(8,128)(2,1)S(1)}, u32[]{:S(2)}, u32[]{:S(2)}) %collective-permute-start.17) | collective-permute-done | bytes 53280 | tf_op jit(solution)/shard_map/ppermute | solution.py:304
  32.9 1.8 %collective-permute-start.18 = (bf16[208,128]{1,0:T(8,128)(2,1)S(1)}, bf16[208,128]{1,0:T(8,128)(2,1)S(1)}, u32[]{:S(2)}, u32[]{:S(2)}) collective-permute-start(bf16[208,128]{1,0:T(8,128)(2,1)S(1)} %shard_map.163.refs_0_), channel_id=1, source_target_pairs={{0,16},{4,20},{8,24},{12,28},{16,0},{20,4},{24,8},{28,12},{1,17},{... | collective-permute-start | bytes 159752 | tf_op jit(solution)/shard_map/ppermute | solution.py:301
  34.6 1.5 %collective-permute-start.11 = (bf16[400,256]{1,0:T(8,128)(2,1)S(1)}, bf16[400,256]{1,0:T(8,128)(2,1)S(1)}, u32[]{:S(2)}, u32[]{:S(2)}) collective-permute-start(bf16[400,256]{1,0:T(8,128)(2,1)S(1)} %get-tuple-element.56), channel_id=1, source_target_pairs={{0,4},{4,0},{8,12},{12,8},{16,20},{20,16},{24,28},{28,24},{1,5},{5... | collective-permute-start | bytes 614408 | tf_op jit(solution)/shard_map/ppermute | solution.py:301
  36.2 0.8 %collective-permute-start.10 = (bf16[400,128]{1,0:T(8,128)(2,1)S(1)}, bf16[400,128]{1,0:T(8,128)(2,1)S(1)}, u32[]{:S(2)}, u32[]{:S(2)}) collective-permute-start(bf16[400,128]{1,0:T(8,128)(2,1)S(1)} %get-tuple-element.52), channel_id=1, source_target_pairs={{0,2},{1,3},{2,0},{3,1},{4,6},{5,7},{6,4},{7,5},{8,10},{9,11},{10,... | collective-permute-start | bytes 307208 | tf_op jit(solution)/shard_map/ppermute | solution.py:304
  37.0 1.6 %collective-permute-done.18.refs_1_ = bf16[208,128]{1,0:T(8,128)(2,1)S(1)} collective-permute-done((bf16[208,128]{1,0:T(8,128)(2,1)S(1)}, bf16[208,128]{1,0:T(8,128)(2,1)S(1)}, u32[]{:S(2)}, u32[]{:S(2)}) %collective-permute-start.18) | collective-permute-done | bytes 53280 | tf_op jit(solution)/shard_map/ppermute | solution.py:301
  38.6 0.2 collective-permute-start.19
  38.8 0.1 shard_map.160
  38.9 3.0 %collective-permute-start.13 = (bf16[400,128]{1,0:T(8,128)(2,1)S(1)}, bf16[400,128]{1,0:T(8,128)(2,1)S(1)}, u32[]{:S(2)}, u32[]{:S(2)}) collective-permute-start(bf16[400,128]{1,0:T(8,128)(2,1)S(1)} %get-tuple-element.59), channel_id=1, source_target_pairs={{0,16},{4,20},{8,24},{12,28},{16,0},{20,4},{24,8},{28,12},{1,17},{... | collective-permute-start | bytes 307208 | tf_op jit(solution)/shard_map/ppermute | solution.py:301
  41.9 1.2 %collective-permute-start.14 = (bf16[400,128]{1,0:T(8,128)(2,1)S(1)}, bf16[400,128]{1,0:T(8,128)(2,1)S(1)}, u32[]{:S(2)}, u32[]{:S(2)}) collective-permute-start(bf16[400,128]{1,0:T(8,128)(2,1)S(1)} %get-tuple-element.60), channel_id=1, source_target_pairs={{0,24},{4,28},{8,16},{12,20},{16,8},{20,12},{24,0},{28,4},{1,25},{... | collective-permute-start | bytes 307208 | tf_op jit(solution)/shard_map/ppermute | solution.py:301
  43.2 1.6 %collective-permute-start.20 = (bf16[208,128]{1,0:T(8,128)(2,1)S(1)}, bf16[208,128]{1,0:T(8,128)(2,1)S(1)}, u32[]{:S(2)}, u32[]{:S(2)}) collective-permute-start(bf16[208,128]{1,0:T(8,128)(2,1)S(1)} %shard_map.165.refs_0_), channel_id=1, source_target_pairs={{0,4},{4,0},{8,12},{12,8},{16,20},{20,16},{24,28},{28,24},{1,5},{5... | collective-permute-start | bytes 159752 | tf_op jit(solution)/shard_map/ppermute | solution.py:301
  44.8 0.1 shard_map.159
  44.8 0.0 copy-start.2
  44.9 0.3 collective-permute-start.15
  45.2 2.2 %collective-permute-done.20.refs_1_ = bf16[208,128]{1,0:T(8,128)(2,1)S(1)} collective-permute-done((bf16[208,128]{1,0:T(8,128)(2,1)S(1)}, bf16[208,128]{1,0:T(8,128)(2,1)S(1)}, u32[]{:S(2)}, u32[]{:S(2)}) %collective-permute-start.20) | collective-permute-done | bytes 53280 | tf_op jit(solution)/shard_map/ppermute | solution.py:301
  47.4 1.1 %collective-permute-start.21 = (bf16[208,128]{1,0:T(8,128)(2,1)S(1)}, bf16[208,128]{1,0:T(8,128)(2,1)S(1)}, u32[]{:S(2)}, u32[]{:S(2)}) collective-permute-start(bf16[208,128]{1,0:T(8,128)(2,1)S(1)} %shard_map.166.refs_0_), channel_id=1, source_target_pairs={{0,2},{1,3},{2,0},{3,1},{4,6},{5,7},{6,4},{7,5},{8,10},{9,11},{10,... | collective-permute-start | bytes 159752 | tf_op jit(solution)/shard_map/ppermute | solution.py:304
  48.5 0.8 %shard_map.158 = (f32[400,128]{1,0:T(8,128)}, f32[1,128]{1,0:T(1,128)}) custom-call(f32[400,128]{1,0:T(8,128)S(1)} %get-tuple-element.51.refs_0_, bf16[400,128]{1,0:T(8,128)(2,1)S(1)} %collective-permute-done.10.refs_1_.refs_2_, f32[400,128]{1,0:T(8,128)S(1)} %bitcast.22, f32[1,128]{1,0:T(1,128)S(1)} %bitcast.25), custom_call_target="tpu_custom_call" | custom-call | tf_op jit(solution)/shard_map/pallas_call | solution.py:54
  49.3 2.3 %collective-permute-done.21.refs_1_ = bf16[208,128]{1,0:T(8,128)(2,1)S(1)} collective-permute-done((bf16[208,128]{1,0:T(8,128)(2,1)S(1)}, bf16[208,128]{1,0:T(8,128)(2,1)S(1)}, u32[]{:S(2)}, u32[]{:S(2)}) %collective-permute-start.21) | collective-permute-done | bytes 53280 | tf_op jit(solution)/shard_map/ppermute | solution.py:304
  51.6 0.1 collective-permute-start.22
  51.7 0.8 %shard_map.161 = (f32[400,128]{1,0:T(8,128)}, f32[1,128]{1,0:T(1,128)}) custom-call(f32[400,128]{1,0:T(8,128)S(1)} %get-tuple-element.57.refs_0_, bf16[400,128]{1,0:T(8,128)(2,1)S(1)} %collective-permute-done.13.refs_1_, bf16[400,128]{1,0:T(8,128)(2,1)S(1)} %collective-permute-done.14.refs_2_, bf16[400,128]{1,0:T(8,128)(2,1)S(1)} %collective-permute-done.15.refs_3_, ...), custom_call_target="tpu_custom_call" | custom-call | flops 12000000000 | tf_op jit(solution)/shard_map/pallas_call | solution.py:54
  52.5 0.5 collective-permute-done.22.refs_2_
  53.0 0.9 %shard_map.168 = (f32[400,256]{1,0:T(8,128)}, f32[1,256]{1,0:T(1,128)}) custom-call(bf16[208,128]{1,0:T(8,128)(2,1)S(1)} %shard_map.166.refs_0_, bf16[208,128]{1,0:T(8,128)(2,1)S(1)} %collective-permute-done.21.refs_1_, bf16[416,128]{1,0:T(8,128)(2,1)S(1)} %collective-permute-done.22.refs_2_, f32[400,256]{1,0:T(8,128)S(1)} %bitcast.20, ...), custom_call_target="tpu_custom_call" | custom-call | tf_op jit(solution)/shard_map/pallas_call | solution.py:54
  (39 shorter events, 0.3 us)
Async XLA Ops:
  1.6 9.4 %collective-permute-start.4 = (bf16[400,128]{1,0:T(8,128)(2,1)S(1)}, bf16[400,128]{1,0:T(8,128)(2,1)S(1)}, u32[]{:S(2)}, u32[]{:S(2)}) collective-permute-start(bf16[400,128]{1,0:T(8,128)(2,1)S(1)} %bitcast_convert_fusion), channel_id=1, source_target_pairs={{0,9},{1,10},{2,11},{3,8},{4,13},{5,14},{6,15},{7,12},{8,1},{9,2},... | collective-permute-start | bytes 307208 | tf_op jit(solution)/shard_map/ppermute | solution.py:311
  4.1 6.8 %collective-permute-start.3 = (bf16[400,128]{1,0:T(8,128)(2,1)S(1)}, bf16[400,128]{1,0:T(8,128)(2,1)S(1)}, u32[]{:S(2)}, u32[]{:S(2)}) collective-permute-start(bf16[400,128]{1,0:T(8,128)(2,1)S(1)} %bitcast_convert_fusion), channel_id=1, source_target_pairs={{0,1},{1,2},{2,3},{3,0},{4,5},{5,6},{6,7},{7,4},{8,9},{9,10},{10,1... | collective-permute-start | bytes 307208 | tf_op jit(solution)/shard_map/ppermute | solution.py:311
  5.7 9.7 %collective-permute-start.1 = (bf16[400,128]{1,0:T(8,128)(2,1)S(1)}, bf16[400,128]{1,0:T(8,128)(2,1)S(1)}, u32[]{:S(2)}, u32[]{:S(2)}) collective-permute-start(bf16[400,128]{1,0:T(8,128)(2,1)S(1)} %bitcast_convert_fusion), channel_id=1, source_target_pairs={{0,25},{1,26},{2,27},{3,24},{4,29},{5,30},{6,31},{7,28},{8,17},{9,... | collective-permute-start | bytes 307208 | tf_op jit(solution)/shard_map/ppermute | solution.py:311
  8.0 10.0 %collective-permute-start = (bf16[400,128]{1,0:T(8,128)(2,1)S(1)}, bf16[400,128]{1,0:T(8,128)(2,1)S(1)}, u32[]{:S(2)}, u32[]{:S(2)}) collective-permute-start(bf16[400,128]{1,0:T(8,128)(2,1)S(1)} %bitcast_convert_fusion), channel_id=1, source_target_pairs={{0,17},{1,18},{2,19},{3,16},{4,21},{5,22},{6,23},{7,20},{8,25},{9,... | collective-permute-start | bytes 307208 | tf_op jit(solution)/shard_map/ppermute | solution.py:311
  8.0 0.9 %copy-start.1 = (f32[128,400]{0,1:T(8,128)S(1)}, f32[128,400]{0,1:T(8,128)}, u32[]{:S(2)}) copy-start(f32[128,400]{0,1:T(8,128)} %param.10) | copy-start | bytes 614404
  9.2 6.0 %collective-permute-start.2 = (bf16[400,128]{1,0:T(8,128)(2,1)S(1)}, bf16[400,128]{1,0:T(8,128)(2,1)S(1)}, u32[]{:S(2)}, u32[]{:S(2)}) collective-permute-start(bf16[400,128]{1,0:T(8,128)(2,1)S(1)} %shard_map.145.refs_0_), channel_id=1, source_target_pairs={{0,2},{1,3},{2,0},{3,1},{4,6},{5,7},{6,4},{7,5},{8,10},{9,11},{10,... | collective-permute-start | bytes 307208 | tf_op jit(solution)/shard_map/ppermute | solution.py:304
  10.9 1.6 %copy-start = (f32[256,400]{0,1:T(8,128)S(1)}, f32[256,400]{0,1:T(8,128)}, u32[]{:S(2)}) copy-start(f32[256,400]{0,1:T(8,128)} %param.14) | copy-start | bytes 1228804
  11.0 8.6 %collective-permute-start.7 = (bf16[400,256]{1,0:T(8,128)(2,1)S(1)}, bf16[400,256]{1,0:T(8,128)(2,1)S(1)}, u32[]{:S(2)}, u32[]{:S(2)}) collective-permute-start(bf16[400,256]{1,0:T(8,128)(2,1)S(1)} %shard_map.146.refs_3_), channel_id=1, source_target_pairs={{0,4},{4,0},{8,12},{12,8},{16,20},{20,16},{24,28},{28,24},{1,5},{5... | collective-permute-start | bytes 614408 | tf_op jit(solution)/shard_map/ppermute | solution.py:301
  15.2 4.3 %copy-start.3 = (f32[128,400]{0,1:T(8,128)S(1)}, f32[128,400]{0,1:T(8,128)}, u32[]{:S(2)}) copy-start(f32[128,400]{0,1:T(8,128)} %param.12) | copy-start | bytes 614404
  15.3 4.3 %copy-start.6 = (f32[128]{0:T(128)S(1)}, f32[128]{0:T(128)}, u32[]{:S(2)}) copy-start(f32[128]{0:T(128)} %param.13) | copy-start | bytes 1540
  15.3 4.4 %collective-permute-start.6 = (bf16[400,256]{1,0:T(8,128)(2,1)S(1)}, bf16[400,256]{1,0:T(8,128)(2,1)S(1)}, u32[]{:S(2)}, u32[]{:S(2)}) collective-permute-start(bf16[400,256]{1,0:T(8,128)(2,1)S(1)} %shard_map.148.refs_2_), channel_id=1, source_target_pairs={{0,1},{1,0},{2,3},{3,2},{4,5},{5,4},{6,7},{7,6},{8,9},{9,8},{10,11... | collective-permute-start | bytes 614408 | tf_op jit(solution)/shard_map/ppermute | solution.py:304
  18.0 7.2 %collective-permute-start.5 = (bf16[400,256]{1,0:T(8,128)(2,1)S(1)}, bf16[400,256]{1,0:T(8,128)(2,1)S(1)}, u32[]{:S(2)}, u32[]{:S(2)}) collective-permute-start(bf16[400,256]{1,0:T(8,128)(2,1)S(1)} %shard_map.149.refs_2_), channel_id=1, source_target_pairs={{0,4},{4,0},{8,12},{12,8},{16,20},{20,16},{24,28},{28,24},{1,5},{5... | collective-permute-start | bytes 614408 | tf_op jit(solution)/shard_map/ppermute | solution.py:301
  19.6 5.6 %collective-permute-start.8 = (f32[408,128]{1,0:T(8,128)S(1)}, f32[408,128]{1,0:T(8,128)S(1)}, u32[]{:S(2)}, u32[]{:S(2)}) collective-permute-start(f32[408,128]{1,0:T(8,128)S(1)} %shard_map.154), channel_id=1, source_target_pairs={{0,1},{1,2},{2,3},{3,0},{4,5},{5,6},{6,7},{7,4},{8,9},{9,10},{10,1... | collective-permute-start | bytes 626696 | tf_op jit(solution)/shard_map/ppermute | solution.py:311
  27.0 1.6 %collective-permute-start.16 = (bf16[416,128]{1,0:T(8,128)(2,1)S(1)}, bf16[416,128]{1,0:T(8,128)(2,1)S(1)}, u32[]{:S(2)}, u32[]{:S(2)}) collective-permute-start(bf16[416,128]{1,0:T(8,128)(2,1)S(1)} %get-tuple-element.65), channel_id=1, source_target_pairs={{0,1},{1,0},{2,3},{3,2},{4,5},{5,4},{6,7},{7,6},{8,9},{9,8},{10,11... | collective-permute-start | bytes 319496 | tf_op jit(solution)/shard_map/ppermute | solution.py:304
  28.1 8.1 %collective-permute-start.9 = (bf16[400,256]{1,0:T(8,128)(2,1)S(1)}, bf16[400,256]{1,0:T(8,128)(2,1)S(1)}, u32[]{:S(2)}, u32[]{:S(2)}) collective-permute-start(bf16[400,256]{1,0:T(8,128)(2,1)S(1)} %get-tuple-element.50), channel_id=1, source_target_pairs={{0,1},{1,0},{2,3},{3,2},{4,5},{5,4},{6,7},{7,6},{8,9},{9,8},{10,11... | collective-permute-start | bytes 614408 | tf_op jit(solution)/shard_map/ppermute | solution.py:304
  28.7 4.2 %collective-permute-start.17 = (bf16[208,128]{1,0:T(8,128)(2,1)S(1)}, bf16[208,128]{1,0:T(8,128)(2,1)S(1)}, u32[]{:S(2)}, u32[]{:S(2)}) collective-permute-start(bf16[208,128]{1,0:T(8,128)(2,1)S(1)} %get-tuple-element.67), channel_id=1, source_target_pairs={{0,2},{1,3},{2,0},{3,1},{4,6},{5,7},{6,4},{7,5},{8,10},{9,11},{10,... | collective-permute-start | bytes 159752 | tf_op jit(solution)/shard_map/ppermute | solution.py:304
  29.6 9.3 %collective-permute-start.12 = (bf16[400,256]{1,0:T(8,128)(2,1)S(1)}, bf16[400,256]{1,0:T(8,128)(2,1)S(1)}, u32[]{:S(2)}, u32[]{:S(2)}) collective-permute-start(bf16[400,256]{1,0:T(8,128)(2,1)S(1)} %get-tuple-element.58), channel_id=1, source_target_pairs={{0,4},{4,0},{8,12},{12,8},{16,20},{20,16},{24,28},{28,24},{1,5},{5... | collective-permute-start | bytes 614408 | tf_op jit(solution)/shard_map/ppermute | solution.py:301
  32.9 5.7 %collective-permute-start.18 = (bf16[208,128]{1,0:T(8,128)(2,1)S(1)}, bf16[208,128]{1,0:T(8,128)(2,1)S(1)}, u32[]{:S(2)}, u32[]{:S(2)}) collective-permute-start(bf16[208,128]{1,0:T(8,128)(2,1)S(1)} %shard_map.163.refs_0_), channel_id=1, source_target_pairs={{0,16},{4,20},{8,24},{12,28},{16,0},{20,4},{24,8},{28,12},{1,17},{... | collective-permute-start | bytes 159752 | tf_op jit(solution)/shard_map/ppermute | solution.py:301
  34.6 10.1 %collective-permute-start.11 = (bf16[400,256]{1,0:T(8,128)(2,1)S(1)}, bf16[400,256]{1,0:T(8,128)(2,1)S(1)}, u32[]{:S(2)}, u32[]{:S(2)}) collective-permute-start(bf16[400,256]{1,0:T(8,128)(2,1)S(1)} %get-tuple-element.56), channel_id=1, source_target_pairs={{0,4},{4,0},{8,12},{12,8},{16,20},{20,16},{24,28},{28,24},{1,5},{5... | collective-permute-start | bytes 614408 | tf_op jit(solution)/shard_map/ppermute | solution.py:301
  36.2 8.6 %collective-permute-start.10 = (bf16[400,128]{1,0:T(8,128)(2,1)S(1)}, bf16[400,128]{1,0:T(8,128)(2,1)S(1)}, u32[]{:S(2)}, u32[]{:S(2)}) collective-permute-start(bf16[400,128]{1,0:T(8,128)(2,1)S(1)} %get-tuple-element.52), channel_id=1, source_target_pairs={{0,2},{1,3},{2,0},{3,1},{4,6},{5,7},{6,4},{7,5},{8,10},{9,11},{10,... | collective-permute-start | bytes 307208 | tf_op jit(solution)/shard_map/ppermute | solution.py:304
  38.6 4.6 %collective-permute-start.19 = (bf16[208,128]{1,0:T(8,128)(2,1)S(1)}, bf16[208,128]{1,0:T(8,128)(2,1)S(1)}, u32[]{:S(2)}, u32[]{:S(2)}) collective-permute-start(bf16[208,128]{1,0:T(8,128)(2,1)S(1)} %shard_map.164.refs_0_), channel_id=1, source_target_pairs={{0,8},{4,12},{8,0},{12,4},{16,24},{20,28},{24,16},{28,20},{1,9},{5... | collective-permute-start | bytes 159752 | tf_op jit(solution)/shard_map/ppermute | solution.py:301
  38.9 12.8 %collective-permute-start.13 = (bf16[400,128]{1,0:T(8,128)(2,1)S(1)}, bf16[400,128]{1,0:T(8,128)(2,1)S(1)}, u32[]{:S(2)}, u32[]{:S(2)}) collective-permute-start(bf16[400,128]{1,0:T(8,128)(2,1)S(1)} %get-tuple-element.59), channel_id=1, source_target_pairs={{0,16},{4,20},{8,24},{12,28},{16,0},{20,4},{24,8},{28,12},{1,17},{... | collective-permute-start | bytes 307208 | tf_op jit(solution)/shard_map/ppermute | solution.py:301
  41.9 9.8 %collective-permute-start.14 = (bf16[400,128]{1,0:T(8,128)(2,1)S(1)}, bf16[400,128]{1,0:T(8,128)(2,1)S(1)}, u32[]{:S(2)}, u32[]{:S(2)}) collective-permute-start(bf16[400,128]{1,0:T(8,128)(2,1)S(1)} %get-tuple-element.60), channel_id=1, source_target_pairs={{0,24},{4,28},{8,16},{12,20},{16,8},{20,12},{24,0},{28,4},{1,25},{... | collective-permute-start | bytes 307208 | tf_op jit(solution)/shard_map/ppermute | solution.py:301
  43.2 4.2 %collective-permute-start.20 = (bf16[208,128]{1,0:T(8,128)(2,1)S(1)}, bf16[208,128]{1,0:T(8,128)(2,1)S(1)}, u32[]{:S(2)}, u32[]{:S(2)}) collective-permute-start(bf16[208,128]{1,0:T(8,128)(2,1)S(1)} %shard_map.165.refs_0_), channel_id=1, source_target_pairs={{0,4},{4,0},{8,12},{12,8},{16,20},{20,16},{24,28},{28,24},{1,5},{5... | collective-permute-start | bytes 159752 | tf_op jit(solution)/shard_map/ppermute | solution.py:301
  44.8 3.7 %copy-start.2 = (f32[128,400]{0,1:T(8,128)S(1)}, f32[128,400]{0,1:T(8,128)}, u32[]{:S(2)}) copy-start(f32[128,400]{0,1:T(8,128)} %param.10) | copy-start | bytes 614404
  44.9 3.6 %copy-start.5 = (f32[128]{0:T(128)S(1)}, f32[128]{0:T(128)}, u32[]{:S(2)}) copy-start(f32[128]{0:T(128)} %param.11) | copy-start | bytes 1540
  44.9 6.8 %collective-permute-start.15 = (bf16[400,128]{1,0:T(8,128)(2,1)S(1)}, bf16[400,128]{1,0:T(8,128)(2,1)S(1)}, u32[]{:S(2)}, u32[]{:S(2)}) collective-permute-start(bf16[400,128]{1,0:T(8,128)(2,1)S(1)} %get-tuple-element.61), channel_id=1, source_target_pairs={{0,8},{4,12},{8,0},{12,4},{16,24},{20,28},{24,16},{28,20},{1,9},{5... | collective-permute-start | bytes 307208 | tf_op jit(solution)/shard_map/ppermute | solution.py:301
  47.4 4.2 %collective-permute-start.21 = (bf16[208,128]{1,0:T(8,128)(2,1)S(1)}, bf16[208,128]{1,0:T(8,128)(2,1)S(1)}, u32[]{:S(2)}, u32[]{:S(2)}) collective-permute-start(bf16[208,128]{1,0:T(8,128)(2,1)S(1)} %shard_map.166.refs_0_), channel_id=1, source_target_pairs={{0,2},{1,3},{2,0},{3,1},{4,6},{5,7},{6,4},{7,5},{8,10},{9,11},{10,... | collective-permute-start | bytes 159752 | tf_op jit(solution)/shard_map/ppermute | solution.py:304
  51.6 1.4 %collective-permute-start.22 = (bf16[416,128]{1,0:T(8,128)(2,1)S(1)}, bf16[416,128]{1,0:T(8,128)(2,1)S(1)}, u32[]{:S(2)}, u32[]{:S(2)}) collective-permute-start(bf16[416,128]{1,0:T(8,128)(2,1)S(1)} %shard_map.167), channel_id=1, source_target_pairs={{0,1},{1,0},{2,3},{3,2},{4,5},{5,4},{6,7},{7,6},{8,9},{9,8},{10,11... | collective-permute-start | bytes 319496 | tf_op jit(solution)/shard_map/ppermute | solution.py:304
  51.7 1.3 %copy-start.4 = (f32[256]{0:T(256)S(1)}, f32[256]{0:T(256)}, u32[]{:S(2)}) copy-start(f32[256]{0:T(256)} %param.15) | copy-start | bytes 3076

commit v17 on v16

--- a/solution.py
+++ b/solution.py
@@ -163,7 +163,7 @@
     q_ref, weight_ref, ids_ref, right_ref, qg_ref, rows_ref, m_ref = refs
     join_body(*block_refs, rows_ref)
     products(rows_ref, q_ref, weight_ref, ids_ref, m_ref, 0)
-    right_ref[...] = dot(q_ref[...], m_ref[...], 1, 1)
+    right_ref[...] = dot(q_ref[...], m_ref[...], 1, 1).astype(BF)
     qg_ref[...] = dot(rows_ref[...], m_ref[...], 1, 0)
 
 
@@ -268,7 +268,7 @@
 def chunk_body(base, near_ref, got_ref, *block_refs):
     for k, ref in enumerate(block_refs):
         cols = slice(k * LANES, (k + 1) * LANES)
-        total = near_ref[:, base + k * LANES:base + (k + 1) * LANES] + got_ref[:, cols].astype(F32)
+        total = near_ref[:, base + k * LANES:base + (k + 1) * LANES].astype(F32) + got_ref[:, cols].astype(F32)
         ref[...] = total.astype(ref.dtype)
 
 
@@ -333,7 +333,7 @@
             return call(cast_body, one_block, scratch, after=after, place=pl.ANY)(value)
 
         right_bf = right_t.astype(BF)
-        near = [next_column(right_bf, 2 * k) for k in range(outer)]
+        near = [right_bf] + [swap_left(right_bf, 2 * k) for k in range(1, outer)]
         some = outer // 2
         cut = some * rows
         chunk = shape(width, cut, dtype=BF)
@@ -344,6 +344,7 @@
         longest = max(i.shape[-1] for i in ids)
         ids = [i.reshape(-1, i.shape[-1]) for i in ids]
         ids = jnp.concatenate([jnp.pad(i, ((0, 0), (0, longest - i.shape[-1]))) for i in ids], axis=0)
+        ids = lax.ppermute(ids, "right", [(i, (i - 1) % n_right) for i in range(n_right)])
         left_bf = cast(left_t)
         half_left = [left_bf] + [swap_right(left_bf, 2 * k) for k in range(1, far_right)]
         place = jnp.stack([here_r, here_l]).astype(jnp.int32)
@@ -364,7 +365,7 @@
         )
         right_near, qg = call(
             functools.partial(near_body, outer),
-            (shape(width, half), shape(width, edges)),
+            (shape(width, half, dtype=BF), shape(width, edges)),
             [pltpu.VMEM((width, half), BF), pltpu.VMEM((half, edges), BF)],
         )(*near, q, weight, ids)
         right_low, qg = call(
@@ -390,14 +391,19 @@
             [pltpu.VMEM((width, left_rows), F32)],
         )(m, q, g, o, ids, right_low)
 
+        near_got = next_column(right_near, 0)
+        got_low = next_column(right_low, 1)
+        got_high = next_column(right_high, 1)
+
         mine, *rest = call(
             piece_body, (shape(size, LANES),) + (piece,) * (far_right - 1), flops=COST_SUM
         )(mine, swap_right(theirs, 1))
         got = [swap_right(p, 2 * (k + 1)) for k, p in enumerate(rest)]
-        mine = call(sum_body, piece, flops=COST_SUM)(mine, *got)
+        mine = call(sum_body, piece, flops=COST_SUM, after=(near_got,))(mine, *got)
         bit = n_left // 2
         while bit > 1:
-            mine = call(sum_body, piece, flops=COST_SUM)(mine, swap_left(mine, bit))
+            after = (got_high,) if 2 * bit == n_left else (got_low,)
+            mine = call(sum_body, piece, flops=COST_SUM, after=after)(mine, swap_left(mine, bit))
             bit //= 2
         mine = call(sum_body, piece, flops=COST_SUM)(mine, swap_left(mine, 1))
         pieces = [mine] + [swap_right(mine, 2 * k) for k in range(1, far_right)]
@@ -408,12 +414,10 @@
         )
         left_got = [swap_right(block, 2 * (k + 1)) for k, block in enumerate(blocks)]
 
-        got_low = swap_left(right_low, 1)
-        got_high = swap_left(right_high, 1)
         outs = (one_block,) * some
-        high = call(functools.partial(chunk_body, cut), outs, flops=COST_HIGH)(right_near, got_high)
+        high = call(functools.partial(chunk_body, cut), outs, flops=COST_HIGH)(near_got, got_high)
         outs = (shape(width, rows),) + outs[1:]
-        low = call(functools.partial(chunk_body, 0), outs, flops=COST_LOW, after=left_got)(right_near, got_low)
+        low = call(functools.partial(chunk_body, 0), outs, flops=COST_LOW, after=left_got)(near_got, got_low)
         right_got = [low[0]] + [swap_left(block, 2 * (some + k)) for k, block in enumerate(high)]
         right_got += [swap_left(low[k], 2 * k) for k in range(1, some)]
 
@@ -424,7 +428,11 @@
         left_new, left_state_new = update([left_own, *left_got], left_t, left_state[None, :])
         right_new, right_state_new = update(right_got, moved, moved, COST_UPDATE)
         relation_new, relation_state_new = call(
-            functools.partial(relation_body, n_right), (shape(width, nrel), shape(1, nrel)), [all_pieces], me
+            functools.partial(relation_body, n_right),
+            (shape(width, nrel), shape(1, nrel)),
+            [all_pieces],
+            me,
+            after=(right_state_new,),
         )(*pieces, sibling, relation_t, relation_state[None, :])
         return (
             left_new.T, left_state_new.reshape(-1), right_new.T, right_state_new.reshape(-1),

time: 54.1 us -> 55.7 us (1.030)
  starting transfers between devices: 25.3 us -> 30.3 us
  waiting for transfers between devices: 13.7 us -> 9.62 us
  local copies, waits for them, and re-layouts: 0.97 us -> 1.62 us
    ppermute x8, starting transfers between devices: 4.4 us -> 8.2 us  [swap_right(): return lax.ppermute(value, 'right', [(i, i ^ by) for i in range(n_right)])]
    ppermute x10 -> x11, starting transfers between devices: 14.4 us -> 18.1 us  [swap_left(): return lax.ppermute(value, 'left', [(i, i ^ by) for i in range(n_left)])]
    ppermute x5 -> x4, starting transfers between devices: 6.44 us -> 3.6 us  [next_column(): return lax.ppermute(value, ('left', 'right'), perm)]
    ppermute x5 -> x4, waiting for transfers between devices: 2.57 us -> 0.01 us  [next_column(): return lax.ppermute(value, ('left', 'right'), perm)]
    ppermute x10 -> x11, waiting for transfers between devices: 5.43 us -> 4.08 us  [swap_left(): return lax.ppermute(value, 'left', [(i, i ^ by) for i in range(n_left)])]
    unnamed x14 -> x16, local copies, waits for them, and re-layouts: 0.97 us -> 1.62 us
  transfers between devices with their start and end apart: 23 -> 24, of which waited for: 8 -> 7; matrix products, arithmetic and copies ran while one was open for 2% -> 1% of each run, Pallas kernels for 16% -> 19%
where the time goes in v17:
time: 55.7 us; the launch traced here: 55.5 us
  starting transfers between devices  30.3 us (54%)
  Pallas kernels  11.3 us (20%)
  waiting for transfers between devices  9.62 us (17%)
  other arithmetic  1.78 us (3%)
  local copies, waits for them, and re-layouts  1.62 us (3%)
  between operations  0.88 us (2%)
    ppermute x11, starting transfers between devices, swap_left(): return lax.ppermute(value, 'left', [(i, i ^ by) for i in range(n_left)])  18.1 us
    pallas_call x24, Pallas kernels, run(): pl.pallas_call(inner, out_shape=out_shape, in_specs=specs, scratch_shapes...  11.3 us
    ppermute x8, starting transfers between devices, swap_right(): return lax.ppermute(value, 'right', [(i, i ^ by) for i in range(n_right)])  8.2 us
    ppermute x8, waiting for transfers between devices, swap_right(): return lax.ppermute(value, 'right', [(i, i ^ by) for i in range(n_right)])  5.53 us
    ppermute x11, waiting for transfers between devices, swap_left(): return lax.ppermute(value, 'left', [(i, i ^ by) for i in range(n_left)])  4.08 us
    ppermute x4, starting transfers between devices, next_column(): return lax.ppermute(value, ('left', 'right'), perm)  3.6 us
    unnamed x16, local copies, waits for them, and re-layouts  1.62 us
  transfers between devices with their start and end apart: 24, of which 7 were waited for; matrix products, arithmetic and copies ran while one was open for 1% of the time, Pallas kernels for 19%

profile of v17, /device:TPU:0, one launch (start us, length us, event | category | flops | bytes accessed | tf_op | source)
XLA Modules:
  0.0 55.5 jit_solution(7323345192031194474)
XLA Ops:
  0.6 0.9 %bitcast_convert_fusion.refs_0_ = bf16[400,128]{1,0:T(8,128)(2,1)S(1)} fusion(f32[128,400]{0,1:T(8,128)} %param.12), kind=kLoop, calls=%fused_computation.2 | loop fusion | flops 51200 | bytes 307200 | tf_op jit(solution)/shard_map/convert_element_type | solution.py:335
  1.6 3.1 %collective-permute-start.4 = (bf16[400,128]{1,0:T(8,128)(2,1)S(1)}, bf16[400,128]{1,0:T(8,128)(2,1)S(1)}, u32[]{:S(2)}, u32[]{:S(2)}) collective-permute-start(bf16[400,128]{1,0:T(8,128)(2,1)S(1)} %bitcast_convert_fusion.refs_0_), channel_id=1, source_target_pairs={{0,8},{4,12},{8,0},{12,4},{16,24},{20,28},{24,16},{28,20},{1,9},{5... | collective-permute-start | bytes 307208 | tf_op jit(solution)/shard_map/ppermute | solution.py:301
  4.7 2.5 %collective-permute-start.1 = (bf16[400,128]{1,0:T(8,128)(2,1)S(1)}, bf16[400,128]{1,0:T(8,128)(2,1)S(1)}, u32[]{:S(2)}, u32[]{:S(2)}) collective-permute-start(bf16[400,128]{1,0:T(8,128)(2,1)S(1)} %bitcast_convert_fusion.refs_0_), channel_id=1, source_target_pairs={{0,24},{4,28},{8,16},{12,20},{16,8},{20,12},{24,0},{28,4},{1,25},{... | collective-permute-start | bytes 307208 | tf_op jit(solution)/shard_map/ppermute | solution.py:301
  7.1 0.1 collective-permute-start
  7.3 0.8 %pad_add_fusion = s32[5,1024]{1,0:T(8,128)S(1)} fusion(s32[2,1024]{1,0:T(2,128)} %bitcast.28, s32[1,1024]{1,0:T(1,128)} %bitcast.29, s32[1,1024]{1,0:T(1,128)} %bitcast.30, s32[1,1024]{1,0:T(1,128)} %bitcast.31), kind=kLoop, calls=%fused_computation | loop fusion | flops 15360 | bytes 40960 | tf_op jit(solution)/shard_map/concatenate | solution.py:346
  8.0 0.4 collective-permute-start.3
  8.4 0.9 %copy-done.1 = f32[128,400]{0,1:T(8,128)S(1)} copy-done((f32[128,400]{0,1:T(8,128)S(1)}, f32[128,400]{0,1:T(8,128)}, u32[]{:S(2)}) %copy-start.1) | copy-done | bytes 204824
  9.4 0.3 shard_map.145.refs_0_
  9.7 1.2 %collective-permute-start.2 = (bf16[400,128]{1,0:T(8,128)(2,1)S(1)}, bf16[400,128]{1,0:T(8,128)(2,1)S(1)}, u32[]{:S(2)}, u32[]{:S(2)}) collective-permute-start(bf16[400,128]{1,0:T(8,128)(2,1)S(1)} %shard_map.145.refs_0_), channel_id=1, source_target_pairs={{0,2},{1,3},{2,0},{3,1},{4,6},{5,7},{6,4},{7,5},{8,10},{9,11},{10,... | collective-permute-start | bytes 307208 | tf_op jit(solution)/shard_map/ppermute | solution.py:304
  10.9 0.1 pad_add_fusion.1.refs_2_
  11.0 1.6 %collective-permute-start.7 = (bf16[400,256]{1,0:T(8,128)(2,1)S(1)}, bf16[400,256]{1,0:T(8,128)(2,1)S(1)}, u32[]{:S(2)}, u32[]{:S(2)}) collective-permute-start(bf16[400,256]{1,0:T(8,128)(2,1)S(1)} %shard_map.146.refs_3_), channel_id=1, source_target_pairs={{0,4},{4,0},{8,12},{12,8},{16,20},{20,16},{24,28},{28,24},{1,5},{5... | collective-permute-start | bytes 614408 | tf_op jit(solution)/shard_map/ppermute | solution.py:301
  12.6 1.6 %shard_map.147 = (f32[2,1024,128]{2,1,0:T(8,128)S(1)}, bf16[400,256]{1,0:T(8,128)(2,1)S(1)}, s32[5,1024]{1,0:T(8,128)S(1)}) custom-call(s32[5,1024]{1,0:T(8,128)S(1)} %collective-permute-done.3.refs_0_, f32[400,256]{1,0:T(8,128)S(1)} %bitcast.19, s32[2]{0:T(128)S(1)} %pad_add_fusion.1.refs_2_, bf16[400,256]{1,0:T(8,128)(2,1)S(1)} %shard_map.146.refs_3_), custom_call_target="tpu_custom_call" | custom-call | tf_op jit(solution)/shard_map/pallas_call | solution.py:54
  14.1 0.5 collective-permute-done.2.refs_1_
  14.7 0.1 collective-permute-start.6
  14.8 1.6 %collective-permute-done.refs_0_.refs_2_ = bf16[400,128]{1,0:T(8,128)(2,1)S(1)} collective-permute-done((bf16[400,128]{1,0:T(8,128)(2,1)S(1)}, bf16[400,128]{1,0:T(8,128)(2,1)S(1)}, u32[]{:S(2)}, u32[]{:S(2)}) %collective-permute-start) | collective-permute-done | bytes 102432 | tf_op jit(solution)/shard_map/ppermute | solution.py:301
  16.5 1.6 %collective-permute-start.5 = (bf16[400,256]{1,0:T(8,128)(2,1)S(1)}, bf16[400,256]{1,0:T(8,128)(2,1)S(1)}, u32[]{:S(2)}, u32[]{:S(2)}) collective-permute-start(bf16[400,256]{1,0:T(8,128)(2,1)S(1)} %shard_map.149.refs_2_), channel_id=1, source_target_pairs={{0,4},{4,0},{8,12},{12,8},{16,20},{20,16},{24,28},{28,24},{1,5},{5... | collective-permute-start | bytes 614408 | tf_op jit(solution)/shard_map/ppermute | solution.py:301
  18.1 0.1 collective-permute-start.8
  18.2 0.9 %shard_map.150 = (bf16[400,1024]{1,0:T(8,128)(2,1)S(1)}, bf16[400,1024]{1,0:T(8,128)(2,1)S(1)}, bf16[400,1024]{1,0:T(8,128)(2,1)S(1)}) custom-call(bf16[400,128]{1,0:T(8,128)(2,1)S(1)} %shard_map.145.refs_0_, bf16[400,128]{1,0:T(8,128)(2,1)S(1)} %collective-permute-done.2.refs_1_, bf16[400,256]{1,0:T(8,128)(2,1)S(1)} %collective-permute-done.6.refs_2_, ...), custom_call_target="tpu_custom_call" | custom-call | flops 6000000000 | tf_op jit(solution)/shard_map/pallas_call | solution.py:54
  19.1 1.8 %shard_map.152 = (bf16[400,512]{1,0:T(8,128)(2,1)S(1)}, f32[400,1024]{1,0:T(8,128)S(1)}) custom-call(bf16[400,128]{1,0:T(8,128)(2,1)S(1)} %bitcast_convert_fusion.refs_0_, bf16[400,128]{1,0:T(8,128)(2,1)S(1)} %collective-permute-done.4.refs_1_, bf16[400,128]{1,0:T(8,128)(2,1)S(1)} %collective-permute-done.refs_0_.refs_2_, ...), custom_call_target="tpu_custom_call" | custom-call | tf_op jit(solution)/shard_map/pallas_call | solution.py:54
  20.9 1.6 %collective-permute-start.11 = (bf16[400,512]{1,0:T(8,128)(2,1)S(1)}, bf16[400,512]{1,0:T(8,128)(2,1)S(1)}, u32[]{:S(2)}, u32[]{:S(2)}) collective-permute-start(bf16[400,512]{1,0:T(8,128)(2,1)S(1)} %get-tuple-element.55), channel_id=1, source_target_pairs={{0,1},{1,2},{2,3},{3,0},{4,5},{5,6},{6,7},{7,4},{8,9},{9,10},{10,1... | collective-permute-start | bytes 1228808 | tf_op jit(solution)/shard_map/ppermute | solution.py:311
  22.6 1.0 %shard_map.153 = (bf16[400,256]{1,0:T(8,128)(2,1)S(1)}, f32[400,1024]{1,0:T(8,128)S(1)}) custom-call(bf16[400,256]{1,0:T(8,128)(2,1)S(1)} %shard_map.151.rows_ref, bf16[400,1024]{1,0:T(8,128)(2,1)S(1)} %get-tuple-element.41.refs_4_.q_ref.refs_1_, f32[2,1024,128]{2,1,0:T(8,128)S(1)} %get-tuple-element.38.refs_2_.refs_5_.weight_ref, ...), custom_call_target="tpu_custom_call" | custom-call | tf_op jit(solution)/shard_map/pallas_call | solution.py:54
  23.6 1.9 %shard_map.155 = (bf16[256,1024]{1,0:T(8,128)(2,1)S(1)}, f32[400,1024]{1,0:T(8,128)S(1)}, f32[416,128]{1,0:T(8,128)S(1)}, bf16[416,128]{1,0:T(8,128)(2,1)S(1)}) custom-call(bf16[400,256]{1,0:T(8,128)(2,1)S(1)} %collective-permute-done.5.refs_0_, bf16[400,1024]{1,0:T(8,128)(2,1)S(1)} %get-tuple-element.41.refs_4_.q_ref.refs_1_, ...), custom_call_target="tpu_custom_call" | custom-call | tf_op jit(solution)/shard_map/pallas_call | solution.py:54
  25.4 0.1 collective-permute-start.17
  25.5 1.0 %shard_map.156 = (bf16[400,256]{1,0:T(8,128)(2,1)S(1)}, bf16[400,256]{1,0:T(8,128)(2,1)S(1)}, f32[400,256]{1,0:T(8,128)S(1)}, bf16[400,256]{1,0:T(8,128)(2,1)S(1)}) custom-call(bf16[256,1024]{1,0:T(8,128)(2,1)S(1)} %get-tuple-element.45.m_ref, bf16[400,1024]{1,0:T(8,128)(2,1)S(1)} %get-tuple-element.41.refs_4_.q_ref.refs_1_, ...), custom_call_target="tpu_custom_call" | custom-call | tf_op jit(solution)/shard_map/pallas_call | solution.py:54
  26.5 0.6 collective-permute-start.9
  27.1 0.7 %collective-permute-start.13 = (bf16[400,256]{1,0:T(8,128)(2,1)S(1)}, bf16[400,256]{1,0:T(8,128)(2,1)S(1)}, u32[]{:S(2)}, u32[]{:S(2)}) collective-permute-start(bf16[400,256]{1,0:T(8,128)(2,1)S(1)} %get-tuple-element.58), channel_id=1, source_target_pairs={{0,5},{1,6},{2,7},{3,4},{4,1},{5,2},{6,3},{7,0},{8,13},{9,14},{10,... | collective-permute-start | bytes 614408 | tf_op jit(solution)/shard_map/ppermute | solution.py:311
  27.8 1.6 %collective-permute-start.18 = (bf16[208,128]{1,0:T(8,128)(2,1)S(1)}, bf16[208,128]{1,0:T(8,128)(2,1)S(1)}, u32[]{:S(2)}, u32[]{:S(2)}) collective-permute-start(bf16[208,128]{1,0:T(8,128)(2,1)S(1)} %get-tuple-element.67), channel_id=1, source_target_pairs={{0,2},{1,3},{2,0},{3,1},{4,6},{5,7},{6,4},{7,5},{8,10},{9,11},{10,... | collective-permute-start | bytes 159752 | tf_op jit(solution)/shard_map/ppermute | solution.py:304
  29.3 3.2 %collective-permute-done.18.refs_1_ = bf16[208,128]{1,0:T(8,128)(2,1)S(1)} collective-permute-done((bf16[208,128]{1,0:T(8,128)(2,1)S(1)}, bf16[208,128]{1,0:T(8,128)(2,1)S(1)}, u32[]{:S(2)}, u32[]{:S(2)}) %collective-permute-start.18) | collective-permute-done | bytes 53280 | tf_op jit(solution)/shard_map/ppermute | solution.py:304
  32.6 2.5 %collective-permute-start.19 = (bf16[208,128]{1,0:T(8,128)(2,1)S(1)}, bf16[208,128]{1,0:T(8,128)(2,1)S(1)}, u32[]{:S(2)}, u32[]{:S(2)}) collective-permute-start(bf16[208,128]{1,0:T(8,128)(2,1)S(1)} %shard_map.163.refs_0_), channel_id=1, source_target_pairs={{0,16},{4,20},{8,24},{12,28},{16,0},{20,4},{24,8},{28,12},{1,17},{... | collective-permute-start | bytes 159752 | tf_op jit(solution)/shard_map/ppermute | solution.py:301
  35.0 1.3 %collective-permute-start.12 = (bf16[400,256]{1,0:T(8,128)(2,1)S(1)}, bf16[400,256]{1,0:T(8,128)(2,1)S(1)}, u32[]{:S(2)}, u32[]{:S(2)}) collective-permute-start(bf16[400,256]{1,0:T(8,128)(2,1)S(1)} %get-tuple-element.56), channel_id=1, source_target_pairs={{0,5},{1,6},{2,7},{3,4},{4,1},{5,2},{6,3},{7,0},{8,13},{9,14},{10,... | collective-permute-start | bytes 614408 | tf_op jit(solution)/shard_map/ppermute | solution.py:311
  36.3 0.1 shard_map.157
  36.4 1.3 %collective-permute-start.10 = (bf16[400,128]{1,0:T(8,128)(2,1)S(1)}, bf16[400,128]{1,0:T(8,128)(2,1)S(1)}, u32[]{:S(2)}, u32[]{:S(2)}) collective-permute-start(bf16[400,128]{1,0:T(8,128)(2,1)S(1)} %get-tuple-element.52), channel_id=1, source_target_pairs={{0,2},{1,3},{2,0},{3,1},{4,6},{5,7},{6,4},{7,5},{8,10},{9,11},{10,... | collective-permute-start | bytes 307208 | tf_op jit(solution)/shard_map/ppermute | solution.py:304
  37.7 0.3 collective-permute-done.19.refs_1_
  38.0 1.7 %collective-permute-start.20 = (bf16[208,128]{1,0:T(8,128)(2,1)S(1)}, bf16[208,128]{1,0:T(8,128)(2,1)S(1)}, u32[]{:S(2)}, u32[]{:S(2)}) collective-permute-start(bf16[208,128]{1,0:T(8,128)(2,1)S(1)} %shard_map.164.refs_0_), channel_id=1, source_target_pairs={{0,8},{4,12},{8,0},{12,4},{16,24},{20,28},{24,16},{28,20},{1,9},{5... | collective-permute-start | bytes 159752 | tf_op jit(solution)/shard_map/ppermute | solution.py:301
  39.6 0.1 shard_map.160
  39.7 1.4 %collective-permute-start.14 = (bf16[400,128]{1,0:T(8,128)(2,1)S(1)}, bf16[400,128]{1,0:T(8,128)(2,1)S(1)}, u32[]{:S(2)}, u32[]{:S(2)}) collective-permute-start(bf16[400,128]{1,0:T(8,128)(2,1)S(1)} %get-tuple-element.59), channel_id=1, source_target_pairs={{0,16},{4,20},{8,24},{12,28},{16,0},{20,4},{24,8},{28,12},{1,17},{... | collective-permute-start | bytes 307208 | tf_op jit(solution)/shard_map/ppermute | solution.py:301
  41.1 1.4 %collective-permute-start.15 = (bf16[400,128]{1,0:T(8,128)(2,1)S(1)}, bf16[400,128]{1,0:T(8,128)(2,1)S(1)}, u32[]{:S(2)}, u32[]{:S(2)}) collective-permute-start(bf16[400,128]{1,0:T(8,128)(2,1)S(1)} %get-tuple-element.60), channel_id=1, source_target_pairs={{0,24},{4,28},{8,16},{12,20},{16,8},{20,12},{24,0},{28,4},{1,25},{... | collective-permute-start | bytes 307208 | tf_op jit(solution)/shard_map/ppermute | solution.py:301
  42.6 2.2 %collective-permute-start.21 = (bf16[208,128]{1,0:T(8,128)(2,1)S(1)}, bf16[208,128]{1,0:T(8,128)(2,1)S(1)}, u32[]{:S(2)}, u32[]{:S(2)}) collective-permute-start(bf16[208,128]{1,0:T(8,128)(2,1)S(1)} %shard_map.165.refs_0_), channel_id=1, source_target_pairs={{0,4},{4,0},{8,12},{12,8},{16,20},{20,16},{24,28},{28,24},{1,5},{5... | collective-permute-start | bytes 159752 | tf_op jit(solution)/shard_map/ppermute | solution.py:301
  44.9 0.1 collective-permute-start.16
  44.9 2.1 %collective-permute-done.21.refs_1_ = bf16[208,128]{1,0:T(8,128)(2,1)S(1)} collective-permute-done((bf16[208,128]{1,0:T(8,128)(2,1)S(1)}, bf16[208,128]{1,0:T(8,128)(2,1)S(1)}, u32[]{:S(2)}, u32[]{:S(2)}) %collective-permute-start.21) | collective-permute-done | bytes 53280 | tf_op jit(solution)/shard_map/ppermute | solution.py:301
  47.1 3.3 %collective-permute-start.22 = (bf16[208,128]{1,0:T(8,128)(2,1)S(1)}, bf16[208,128]{1,0:T(8,128)(2,1)S(1)}, u32[]{:S(2)}, u32[]{:S(2)}) collective-permute-start(bf16[208,128]{1,0:T(8,128)(2,1)S(1)} %shard_map.166.refs_0_), channel_id=1, source_target_pairs={{0,2},{1,3},{2,0},{3,1},{4,6},{5,7},{6,4},{7,5},{8,10},{9,11},{10,... | collective-permute-start | bytes 159752 | tf_op jit(solution)/shard_map/ppermute | solution.py:304
  50.4 0.8 %shard_map.158 = (f32[400,128]{1,0:T(8,128)}, f32[1,128]{1,0:T(1,128)}) custom-call(f32[400,128]{1,0:T(8,128)S(1)} %get-tuple-element.51.refs_0_, bf16[400,128]{1,0:T(8,128)(2,1)S(1)} %collective-permute-done.10.refs_1_.refs_2_, f32[400,128]{1,0:T(8,128)S(1)} %bitcast.22, f32[1,128]{1,0:T(1,128)S(1)} %bitcast.25), custom_call_target="tpu_custom_call" | custom-call | tf_op jit(solution)/shard_map/pallas_call | solution.py:54
  51.2 1.3 %collective-permute-done.22.refs_1_ = bf16[208,128]{1,0:T(8,128)(2,1)S(1)} collective-permute-done((bf16[208,128]{1,0:T(8,128)(2,1)S(1)}, bf16[208,128]{1,0:T(8,128)(2,1)S(1)}, u32[]{:S(2)}, u32[]{:S(2)}) %collective-permute-start.22) | collective-permute-done | bytes 53280 | tf_op jit(solution)/shard_map/ppermute | solution.py:304
  52.6 0.1 collective-permute-start.23
  52.7 0.8 %shard_map.161 = (f32[400,128]{1,0:T(8,128)}, f32[1,128]{1,0:T(1,128)}) custom-call(f32[400,128]{1,0:T(8,128)S(1)} %get-tuple-element.57.refs_0_, bf16[400,128]{1,0:T(8,128)(2,1)S(1)} %collective-permute-done.14.refs_1_, bf16[400,128]{1,0:T(8,128)(2,1)S(1)} %collective-permute-done.15.refs_2_, bf16[400,128]{1,0:T(8,128)(2,1)S(1)} %collective-permute-done.16.refs_3_, ...), custom_call_target="tpu_custom_call" | custom-call | flops 12000000000 | tf_op jit(solution)/shard_map/pallas_call | solution.py:54
  53.5 0.5 collective-permute-done.23.refs_2_
  53.9 0.7 %copy-done.6 = f32[1,128]{1,0:T(1,128)S(1)} copy-done((f32[1,128]{1,0:T(1,128)S(1)}, f32[1,128]{1,0:T(1,128)}, u32[]{:S(2)}) %copy-start.6) | copy-done | bytes 536
  54.6 0.9 %shard_map.168 = (f32[400,256]{1,0:T(8,128)}, f32[1,256]{1,0:T(1,128)}) custom-call(bf16[208,128]{1,0:T(8,128)(2,1)S(1)} %shard_map.166.refs_0_, bf16[208,128]{1,0:T(8,128)(2,1)S(1)} %collective-permute-done.22.refs_1_, bf16[416,128]{1,0:T(8,128)(2,1)S(1)} %collective-permute-done.23.refs_2_, f32[400,256]{1,0:T(8,128)S(1)} %bitcast.20, ...), custom_call_target="tpu_custom_call" | custom-call | tf_op jit(solution)/shard_map/pallas_call | solution.py:54
  (43 shorter events, 0.4 us)
Async XLA Ops:
  1.6 9.4 %collective-permute-start.4 = (bf16[400,128]{1,0:T(8,128)(2,1)S(1)}, bf16[400,128]{1,0:T(8,128)(2,1)S(1)}, u32[]{:S(2)}, u32[]{:S(2)}) collective-permute-start(bf16[400,128]{1,0:T(8,128)(2,1)S(1)} %bitcast_convert_fusion.refs_0_), channel_id=1, source_target_pairs={{0,8},{4,12},{8,0},{12,4},{16,24},{20,28},{24,16},{28,20},{1,9},{5... | collective-permute-start | bytes 307208 | tf_op jit(solution)/shard_map/ppermute | solution.py:301
  4.7 10.1 %collective-permute-start.1 = (bf16[400,128]{1,0:T(8,128)(2,1)S(1)}, bf16[400,128]{1,0:T(8,128)(2,1)S(1)}, u32[]{:S(2)}, u32[]{:S(2)}) collective-permute-start(bf16[400,128]{1,0:T(8,128)(2,1)S(1)} %bitcast_convert_fusion.refs_0_), channel_id=1, source_target_pairs={{0,24},{4,28},{8,16},{12,20},{16,8},{20,12},{24,0},{28,4},{1,25},{... | collective-permute-start | bytes 307208 | tf_op jit(solution)/shard_map/ppermute | solution.py:301
  7.1 9.3 %collective-permute-start = (bf16[400,128]{1,0:T(8,128)(2,1)S(1)}, bf16[400,128]{1,0:T(8,128)(2,1)S(1)}, u32[]{:S(2)}, u32[]{:S(2)}) collective-permute-start(bf16[400,128]{1,0:T(8,128)(2,1)S(1)} %bitcast_convert_fusion.refs_0_), channel_id=1, source_target_pairs={{0,16},{4,20},{8,24},{12,28},{16,0},{20,4},{24,8},{28,12},{1,17},{... | collective-permute-start | bytes 307208 | tf_op jit(solution)/shard_map/ppermute | solution.py:301
  8.0 4.6 %collective-permute-start.3 = (s32[5,1024]{1,0:T(8,128)S(1)}, s32[5,1024]{1,0:T(8,128)S(1)}, u32[]{:S(2)}, u32[]{:S(2)}) collective-permute-start(s32[5,1024]{1,0:T(8,128)S(1)} %pad_add_fusion), channel_id=1, source_target_pairs={{0,3},{1,0},{2,1},{3,2},{4,7},{5,4},{6,5},{7,6},{8,11},{9,8},{10,9... | collective-permute-start | bytes 61448 | tf_op jit(solution)/shard_map/ppermute | solution.py:347
  8.4 0.9 %copy-start.1 = (f32[128,400]{0,1:T(8,128)S(1)}, f32[128,400]{0,1:T(8,128)}, u32[]{:S(2)}) copy-start(f32[128,400]{0,1:T(8,128)} %param.10) | copy-start | bytes 614404
  9.7 5.0 %collective-permute-start.2 = (bf16[400,128]{1,0:T(8,128)(2,1)S(1)}, bf16[400,128]{1,0:T(8,128)(2,1)S(1)}, u32[]{:S(2)}, u32[]{:S(2)}) collective-permute-start(bf16[400,128]{1,0:T(8,128)(2,1)S(1)} %shard_map.145.refs_0_), channel_id=1, source_target_pairs={{0,2},{1,3},{2,0},{3,1},{4,6},{5,7},{6,4},{7,5},{8,10},{9,11},{10,... | collective-permute-start | bytes 307208 | tf_op jit(solution)/shard_map/ppermute | solution.py:304
  11.0 1.6 %copy-start = (f32[256,400]{0,1:T(8,128)S(1)}, f32[256,400]{0,1:T(8,128)}, u32[]{:S(2)}) copy-start(f32[256,400]{0,1:T(8,128)} %param.14) | copy-start | bytes 1228804
  11.0 11.5 %collective-permute-start.7 = (bf16[400,256]{1,0:T(8,128)(2,1)S(1)}, bf16[400,256]{1,0:T(8,128)(2,1)S(1)}, u32[]{:S(2)}, u32[]{:S(2)}) collective-permute-start(bf16[400,256]{1,0:T(8,128)(2,1)S(1)} %shard_map.146.refs_3_), channel_id=1, source_target_pairs={{0,4},{4,0},{8,12},{12,8},{16,20},{20,16},{24,28},{28,24},{1,5},{5... | collective-permute-start | bytes 614408 | tf_op jit(solution)/shard_map/ppermute | solution.py:301
  14.7 3.4 %copy-start.3 = (f32[128,400]{0,1:T(8,128)S(1)}, f32[128,400]{0,1:T(8,128)}, u32[]{:S(2)}) copy-start(f32[128,400]{0,1:T(8,128)} %param.12) | copy-start | bytes 614404
  14.7 3.3 %copy-start.7 = (f32[128]{0:T(128)S(1)}, f32[128]{0:T(128)}, u32[]{:S(2)}) copy-start(f32[128]{0:T(128)} %param.13) | copy-start | bytes 1540
  14.7 3.4 %collective-permute-start.6 = (bf16[400,256]{1,0:T(8,128)(2,1)S(1)}, bf16[400,256]{1,0:T(8,128)(2,1)S(1)}, u32[]{:S(2)}, u32[]{:S(2)}) collective-permute-start(bf16[400,256]{1,0:T(8,128)(2,1)S(1)} %shard_map.148.refs_2_), channel_id=1, source_target_pairs={{0,1},{1,0},{2,3},{3,2},{4,5},{5,4},{6,7},{7,6},{8,9},{9,8},{10,11... | collective-permute-start | bytes 614408 | tf_op jit(solution)/shard_map/ppermute | solution.py:304
  16.5 7.1 %collective-permute-start.5 = (bf16[400,256]{1,0:T(8,128)(2,1)S(1)}, bf16[400,256]{1,0:T(8,128)(2,1)S(1)}, u32[]{:S(2)}, u32[]{:S(2)}) collective-permute-start(bf16[400,256]{1,0:T(8,128)(2,1)S(1)} %shard_map.149.refs_2_), channel_id=1, source_target_pairs={{0,4},{4,0},{8,12},{12,8},{16,20},{20,16},{24,28},{28,24},{1,5},{5... | collective-permute-start | bytes 614408 | tf_op jit(solution)/shard_map/ppermute | solution.py:301
  18.1 5.5 %collective-permute-start.8 = (f32[408,128]{1,0:T(8,128)S(1)}, f32[408,128]{1,0:T(8,128)S(1)}, u32[]{:S(2)}, u32[]{:S(2)}) collective-permute-start(f32[408,128]{1,0:T(8,128)S(1)} %shard_map.154), channel_id=1, source_target_pairs={{0,1},{1,2},{2,3},{3,0},{4,5},{5,6},{6,7},{7,4},{8,9},{9,10},{10,1... | collective-permute-start | bytes 626696 | tf_op jit(solution)/shard_map/ppermute | solution.py:311
  20.9 11.6 %collective-permute-start.11 = (bf16[400,512]{1,0:T(8,128)(2,1)S(1)}, bf16[400,512]{1,0:T(8,128)(2,1)S(1)}, u32[]{:S(2)}, u32[]{:S(2)}) collective-permute-start(bf16[400,512]{1,0:T(8,128)(2,1)S(1)} %get-tuple-element.55), channel_id=1, source_target_pairs={{0,1},{1,2},{2,3},{3,0},{4,5},{5,6},{6,7},{7,4},{8,9},{9,10},{10,1... | collective-permute-start | bytes 1228808 | tf_op jit(solution)/shard_map/ppermute | solution.py:311
  25.4 2.3 %collective-permute-start.17 = (bf16[416,128]{1,0:T(8,128)(2,1)S(1)}, bf16[416,128]{1,0:T(8,128)(2,1)S(1)}, u32[]{:S(2)}, u32[]{:S(2)}) collective-permute-start(bf16[416,128]{1,0:T(8,128)(2,1)S(1)} %get-tuple-element.65), channel_id=1, source_target_pairs={{0,1},{1,0},{2,3},{3,2},{4,5},{5,4},{6,7},{7,6},{8,9},{9,8},{10,11... | collective-permute-start | bytes 319496 | tf_op jit(solution)/shard_map/ppermute | solution.py:304
  26.5 9.8 %collective-permute-start.9 = (bf16[400,256]{1,0:T(8,128)(2,1)S(1)}, bf16[400,256]{1,0:T(8,128)(2,1)S(1)}, u32[]{:S(2)}, u32[]{:S(2)}) collective-permute-start(bf16[400,256]{1,0:T(8,128)(2,1)S(1)} %get-tuple-element.50), channel_id=1, source_target_pairs={{0,1},{1,0},{2,3},{3,2},{4,5},{5,4},{6,7},{7,6},{8,9},{9,8},{10,11... | collective-permute-start | bytes 614408 | tf_op jit(solution)/shard_map/ppermute | solution.py:304
  27.1 10.6 %collective-permute-start.13 = (bf16[400,256]{1,0:T(8,128)(2,1)S(1)}, bf16[400,256]{1,0:T(8,128)(2,1)S(1)}, u32[]{:S(2)}, u32[]{:S(2)}) collective-permute-start(bf16[400,256]{1,0:T(8,128)(2,1)S(1)} %get-tuple-element.58), channel_id=1, source_target_pairs={{0,5},{1,6},{2,7},{3,4},{4,1},{5,2},{6,3},{7,0},{8,13},{9,14},{10,... | collective-permute-start | bytes 614408 | tf_op jit(solution)/shard_map/ppermute | solution.py:311
  27.8 4.7 %collective-permute-start.18 = (bf16[208,128]{1,0:T(8,128)(2,1)S(1)}, bf16[208,128]{1,0:T(8,128)(2,1)S(1)}, u32[]{:S(2)}, u32[]{:S(2)}) collective-permute-start(bf16[208,128]{1,0:T(8,128)(2,1)S(1)} %get-tuple-element.67), channel_id=1, source_target_pairs={{0,2},{1,3},{2,0},{3,1},{4,6},{5,7},{6,4},{7,5},{8,10},{9,11},{10,... | collective-permute-start | bytes 159752 | tf_op jit(solution)/shard_map/ppermute | solution.py:304
  32.6 5.4 %collective-permute-start.19 = (bf16[208,128]{1,0:T(8,128)(2,1)S(1)}, bf16[208,128]{1,0:T(8,128)(2,1)S(1)}, u32[]{:S(2)}, u32[]{:S(2)}) collective-permute-start(bf16[208,128]{1,0:T(8,128)(2,1)S(1)} %shard_map.163.refs_0_), channel_id=1, source_target_pairs={{0,16},{4,20},{8,24},{12,28},{16,0},{20,4},{24,8},{28,12},{1,17},{... | collective-permute-start | bytes 159752 | tf_op jit(solution)/shard_map/ppermute | solution.py:301
  35.0 7.5 %collective-permute-start.12 = (bf16[400,256]{1,0:T(8,128)(2,1)S(1)}, bf16[400,256]{1,0:T(8,128)(2,1)S(1)}, u32[]{:S(2)}, u32[]{:S(2)}) collective-permute-start(bf16[400,256]{1,0:T(8,128)(2,1)S(1)} %get-tuple-element.56), channel_id=1, source_target_pairs={{0,5},{1,6},{2,7},{3,4},{4,1},{5,2},{6,3},{7,0},{8,13},{9,14},{10,... | collective-permute-start | bytes 614408 | tf_op jit(solution)/shard_map/ppermute | solution.py:311
  36.4 8.4 %collective-permute-start.10 = (bf16[400,128]{1,0:T(8,128)(2,1)S(1)}, bf16[400,128]{1,0:T(8,128)(2,1)S(1)}, u32[]{:S(2)}, u32[]{:S(2)}) collective-permute-start(bf16[400,128]{1,0:T(8,128)(2,1)S(1)} %get-tuple-element.52), channel_id=1, source_target_pairs={{0,2},{1,3},{2,0},{3,1},{4,6},{5,7},{6,4},{7,5},{8,10},{9,11},{10,... | collective-permute-start | bytes 307208 | tf_op jit(solution)/shard_map/ppermute | solution.py:304
  38.0 4.6 %collective-permute-start.20 = (bf16[208,128]{1,0:T(8,128)(2,1)S(1)}, bf16[208,128]{1,0:T(8,128)(2,1)S(1)}, u32[]{:S(2)}, u32[]{:S(2)}) collective-permute-start(bf16[208,128]{1,0:T(8,128)(2,1)S(1)} %shard_map.164.refs_0_), channel_id=1, source_target_pairs={{0,8},{4,12},{8,0},{12,4},{16,24},{20,28},{24,16},{28,20},{1,9},{5... | collective-permute-start | bytes 159752 | tf_op jit(solution)/shard_map/ppermute | solution.py:301
  39.7 12.9 %collective-permute-start.14 = (bf16[400,128]{1,0:T(8,128)(2,1)S(1)}, bf16[400,128]{1,0:T(8,128)(2,1)S(1)}, u32[]{:S(2)}, u32[]{:S(2)}) collective-permute-start(bf16[400,128]{1,0:T(8,128)(2,1)S(1)} %get-tuple-element.59), channel_id=1, source_target_pairs={{0,16},{4,20},{8,24},{12,28},{16,0},{20,4},{24,8},{28,12},{1,17},{... | collective-permute-start | bytes 307208 | tf_op jit(solution)/shard_map/ppermute | solution.py:301
  41.1 11.5 %collective-permute-start.15 = (bf16[400,128]{1,0:T(8,128)(2,1)S(1)}, bf16[400,128]{1,0:T(8,128)(2,1)S(1)}, u32[]{:S(2)}, u32[]{:S(2)}) collective-permute-start(bf16[400,128]{1,0:T(8,128)(2,1)S(1)} %get-tuple-element.60), channel_id=1, source_target_pairs={{0,24},{4,28},{8,16},{12,20},{16,8},{20,12},{24,0},{28,4},{1,25},{... | collective-permute-start | bytes 307208 | tf_op jit(solution)/shard_map/ppermute | solution.py:301
  42.6 4.5 %collective-permute-start.21 = (bf16[208,128]{1,0:T(8,128)(2,1)S(1)}, bf16[208,128]{1,0:T(8,128)(2,1)S(1)}, u32[]{:S(2)}, u32[]{:S(2)}) collective-permute-start(bf16[208,128]{1,0:T(8,128)(2,1)S(1)} %shard_map.165.refs_0_), channel_id=1, source_target_pairs={{0,4},{4,0},{8,12},{12,8},{16,20},{20,16},{24,28},{28,24},{1,5},{5... | collective-permute-start | bytes 159752 | tf_op jit(solution)/shard_map/ppermute | solution.py:301
  44.8 5.6 %copy-start.2 = (f32[128,400]{0,1:T(8,128)S(1)}, f32[128,400]{0,1:T(8,128)}, u32[]{:S(2)}) copy-start(f32[128,400]{0,1:T(8,128)} %param.10) | copy-start | bytes 614404
  44.8 5.6 %copy-start.5 = (f32[128]{0:T(128)S(1)}, f32[128]{0:T(128)}, u32[]{:S(2)}) copy-start(f32[128]{0:T(128)} %param.11) | copy-start | bytes 1540
  44.9 7.8 %collective-permute-start.16 = (bf16[400,128]{1,0:T(8,128)(2,1)S(1)}, bf16[400,128]{1,0:T(8,128)(2,1)S(1)}, u32[]{:S(2)}, u32[]{:S(2)}) collective-permute-start(bf16[400,128]{1,0:T(8,128)(2,1)S(1)} %get-tuple-element.61), channel_id=1, source_target_pairs={{0,8},{4,12},{8,0},{12,4},{16,24},{20,28},{24,16},{28,20},{1,9},{5... | collective-permute-start | bytes 307208 | tf_op jit(solution)/shard_map/ppermute | solution.py:301
  47.1 5.5 %collective-permute-start.22 = (bf16[208,128]{1,0:T(8,128)(2,1)S(1)}, bf16[208,128]{1,0:T(8,128)(2,1)S(1)}, u32[]{:S(2)}, u32[]{:S(2)}) collective-permute-start(bf16[208,128]{1,0:T(8,128)(2,1)S(1)} %shard_map.166.refs_0_), channel_id=1, source_target_pairs={{0,2},{1,3},{2,0},{3,1},{4,6},{5,7},{6,4},{7,5},{8,10},{9,11},{10,... | collective-permute-start | bytes 159752 | tf_op jit(solution)/shard_map/ppermute | solution.py:304
  52.6 1.4 %collective-permute-start.23 = (bf16[416,128]{1,0:T(8,128)(2,1)S(1)}, bf16[416,128]{1,0:T(8,128)(2,1)S(1)}, u32[]{:S(2)}, u32[]{:S(2)}) collective-permute-start(bf16[416,128]{1,0:T(8,128)(2,1)S(1)} %shard_map.167), channel_id=1, source_target_pairs={{0,1},{1,0},{2,3},{3,2},{4,5},{5,4},{6,7},{7,6},{8,9},{9,8},{10,11... | collective-permute-start | bytes 319496 | tf_op jit(solution)/shard_map/ppermute | solution.py:304
  52.7 1.3 %copy-start.4 = (f32[256]{0:T(256)S(1)}, f32[256]{0:T(256)}, u32[]{:S(2)}) copy-start(f32[256]{0:T(256)} %param.15) | copy-start | bytes 3076
  53.9 0.7 %copy-start.6 = (f32[1,128]{1,0:T(1,128)S(1)}, f32[1,128]{1,0:T(1,128)}, u32[]{:S(2)}) copy-start(f32[1,128]{1,0:T(1,128)} %get-tuple-element.63.refs_6_) | copy-start | bytes 1540

commit v18 on v16

--- a/solution.py
+++ b/solution.py
@@ -36,21 +36,23 @@
     return most if size % most == 0 else size
 
 
-def call(body, out_shape, scratch=(), here=None, after=(), flops=0, place=pltpu.VMEM):
+def call(body, out_shape, scratch=(), here=None, after=(), flops=0, place=pltpu.VMEM, ahead=()):
     def run(*args):
         specs = [pl.BlockSpec(memory_space=place)] * len(args)
         if here is not None:
             specs.append(pl.BlockSpec(memory_space=pltpu.SMEM))
             args = (*args, here)
         inner = body
-        if after:
-            used = len(args)
+        if after or ahead:
+            first = len(ahead)
+            last = first + len(args)
 
             def inner(*refs):
-                body(*refs[:used], *refs[used + len(after):])
-
-            specs += [pl.BlockSpec(memory_space=pl.ANY)] * len(after)
-            args = (*args, *after)
+                body(*refs[first:last], *refs[last + len(after):])
+
+            unread = pl.BlockSpec(memory_space=pl.ANY)
+            specs = [unread] * len(ahead) + specs + [unread] * len(after)
+            args = (*ahead, *args, *after)
         return pl.pallas_call(
             inner,
             out_shape=out_shape,
@@ -265,10 +267,10 @@
         refs[-1][k * size:(k + 1) * size, :] = ref[...]
 
 
-def chunk_body(base, near_ref, got_ref, *block_refs):
+def chunk_body(base, first, near_ref, got_ref, *block_refs):
     for k, ref in enumerate(block_refs):
-        cols = slice(k * LANES, (k + 1) * LANES)
-        total = near_ref[:, base + k * LANES:base + (k + 1) * LANES] + got_ref[:, cols].astype(F32)
+        at = (first + k) * LANES
+        total = near_ref[:, at:at + LANES] + got_ref[:, at - base:at - base + LANES].astype(F32)
         ref[...] = total.astype(ref.dtype)
 
 
@@ -354,7 +356,7 @@
             after=(joined_low,),
         )(ids, relation_t)
         half_joined = call(join_body, shape(width, far_right * rows, dtype=BF), after=(weight,))(*half_left)
-        joined = call(join_body, chunk, flops=COST_JOIN_HIGH, after=(half_joined,))(*near[some:])
+        joined = call(join_body, chunk, flops=COST_JOIN_HIGH, after=(half_joined,), ahead=(near[0],))(*near[some:])
         other_high = swap_left(joined, 1)
         sibling_left = swap_right(half_joined, 1)
         moved = next_column(call(pack_body, shape(width + 8, rows), after=(joined,))(right_t, right_state[None, :]), 0)
@@ -399,6 +401,7 @@
         while bit > 1:
             mine = call(sum_body, piece, flops=COST_SUM)(mine, swap_left(mine, bit))
             bit //= 2
+        over_z = mine
         mine = call(sum_body, piece, flops=COST_SUM)(mine, swap_left(mine, 1))
         pieces = [mine] + [swap_right(mine, 2 * k) for k in range(1, far_right)]
         sibling = swap_right(call(stack_body, shape(far_right * size, LANES, dtype=BF))(*pieces), 1)
@@ -410,12 +413,17 @@
 
         got_low = swap_left(right_low, 1)
         got_high = swap_left(right_high, 1)
-        outs = (one_block,) * some
-        high = call(functools.partial(chunk_body, cut), outs, flops=COST_HIGH)(right_near, got_high)
-        outs = (shape(width, rows),) + outs[1:]
-        low = call(functools.partial(chunk_body, 0), outs, flops=COST_LOW, after=left_got)(right_near, got_low)
-        right_got = [low[0]] + [swap_left(block, 2 * (some + k)) for k, block in enumerate(high)]
-        right_got += [swap_left(low[k], 2 * k) for k in range(1, some)]
+        def chunk_of(first, outs, got, flops, after=()):
+            base = cut if first >= some else 0
+            body = functools.partial(chunk_body, base, first)
+            return call(body, outs, flops=flops, after=after)(right_near, got)
+
+        high = chunk_of(some, (one_block,) * (some - 1), got_high, COST_HIGH)
+        last = chunk_of(outer - 1, (one_block,), got_high, COST_HIGH, (over_z,))
+        high = [swap_left(block, 2 * (some + k)) for k, block in enumerate([*high, *last])]
+        outs = (shape(width, rows),) + (one_block,) * (some - 1)
+        low = chunk_of(0, outs, got_low, COST_LOW, left_got)
+        right_got = [low[0], *high] + [swap_left(low[k], 2 * k) for k in range(1, some)]
 
         def update(got, table, state, flops=0):
             outs = (shape(width, rows), shape(1, rows))

time: 54.1 us -> 53.1 us (0.982)
  waiting for transfers between devices: 13.7 us -> 11.7 us
  starting transfers between devices: 25.3 us -> 26.2 us
    ppermute x8, waiting for transfers between devices: 5.68 us -> 3.93 us  [swap_right(): return lax.ppermute(value, 'right', [(i, i ^ by) for i in range(n_right)])]
    ppermute x10, waiting for transfers between devices: 5.43 us -> 3.77 us  [swap_left(): return lax.ppermute(value, 'left', [(i, i ^ by) for i in range(n_left)])]
    ppermute x5, waiting for transfers between devices: 2.57 us -> 4 us  [next_column(): return lax.ppermute(value, ('left', 'right'), perm)]
    ppermute x8, starting transfers between devices: 4.4 us -> 5.19 us  [swap_right(): return lax.ppermute(value, 'right', [(i, i ^ by) for i in range(n_right)])]
    pallas_call x24 -> x25, Pallas kernels: 11.3 us -> 11.4 us  [run(): pl.pallas_call(inner, out_shape=out_shape, in_specs=specs, scratch_shapes...]
  transfers between devices with their start and end apart: 23 -> 23, of which waited for: 8 -> 9; matrix products, arithmetic and copies ran while one was open for 2% -> 2% of each run, Pallas kernels for 16% -> 16%
where the time goes in v18:
time: 53.1 us; the launch traced here: 52.9 us
  starting transfers between devices  26.2 us (49%)
  waiting for transfers between devices  11.7 us (22%)
  Pallas kernels  11.4 us (21%)
  other arithmetic  1.78 us (3%)
  local copies, waits for them, and re-layouts  0.96 us (2%)
  between operations  0.88 us (2%)
    ppermute x10, starting transfers between devices, swap_left(): return lax.ppermute(value, 'left', [(i, i ^ by) for i in range(n_left)])  14.6 us
    pallas_call x25, Pallas kernels, run(): pl.pallas_call(inner, out_shape=out_shape, in_specs=specs, scratch_shapes...  11.4 us
    ppermute x5, starting transfers between devices, next_column(): return lax.ppermute(value, ('left', 'right'), perm)  6.37 us
    ppermute x8, starting transfers between devices, swap_right(): return lax.ppermute(value, 'right', [(i, i ^ by) for i in range(n_right)])  5.19 us
    ppermute x5, waiting for transfers between devices, next_column(): return lax.ppermute(value, ('left', 'right'), perm)  4 us
    ppermute x8, waiting for transfers between devices, swap_right(): return lax.ppermute(value, 'right', [(i, i ^ by) for i in range(n_right)])  3.93 us
    ppermute x10, waiting for transfers between devices, swap_left(): return lax.ppermute(value, 'left', [(i, i ^ by) for i in range(n_left)])  3.77 us
  transfers between devices with their start and end apart: 23, of which 9 were waited for; matrix products, arithmetic and copies ran while one was open for 2% of the time, Pallas kernels for 16%

profile of v18, /device:TPU:0, one launch (start us, length us, event | category | flops | bytes accessed | tf_op | source)
XLA Modules:
  0.0 52.9 jit_solution(15630406052230575587)
XLA Ops:
  0.6 0.9 %bitcast_convert_fusion = bf16[400,128]{1,0:T(8,128)(2,1)S(1)} fusion(f32[128,400]{0,1:T(8,128)} %param.12), kind=kLoop, calls=%fused_computation.2 | loop fusion | flops 51200 | bytes 307200 | tf_op jit(solution)/shard_map/convert_element_type | solution.py:337
  1.6 2.5 %collective-permute-start.4 = (bf16[400,128]{1,0:T(8,128)(2,1)S(1)}, bf16[400,128]{1,0:T(8,128)(2,1)S(1)}, u32[]{:S(2)}, u32[]{:S(2)}) collective-permute-start(bf16[400,128]{1,0:T(8,128)(2,1)S(1)} %bitcast_convert_fusion), channel_id=1, source_target_pairs={{0,9},{1,10},{2,11},{3,8},{4,13},{5,14},{6,15},{7,12},{8,1},{9,2},... | collective-permute-start | bytes 307208 | tf_op jit(solution)/shard_map/ppermute | solution.py:313
  4.1 3.7 %collective-permute-start.2 = (bf16[400,128]{1,0:T(8,128)(2,1)S(1)}, bf16[400,128]{1,0:T(8,128)(2,1)S(1)}, u32[]{:S(2)}, u32[]{:S(2)}) collective-permute-start(bf16[400,128]{1,0:T(8,128)(2,1)S(1)} %bitcast_convert_fusion), channel_id=1, source_target_pairs={{0,25},{1,26},{2,27},{3,24},{4,29},{5,30},{6,31},{7,28},{8,17},{9,... | collective-permute-start | bytes 307208 | tf_op jit(solution)/shard_map/ppermute | solution.py:313
  7.8 0.1 collective-permute-start.1
  7.9 0.9 %copy-done.1 = f32[128,400]{0,1:T(8,128)S(1)} copy-done((f32[128,400]{0,1:T(8,128)S(1)}, f32[128,400]{0,1:T(8,128)}, u32[]{:S(2)}) %copy-start.1) | copy-done | bytes 204824
  8.8 0.3 shard_map.145.refs_0_
  9.1 1.0 %collective-permute-start.3 = (bf16[400,128]{1,0:T(8,128)(2,1)S(1)}, bf16[400,128]{1,0:T(8,128)(2,1)S(1)}, u32[]{:S(2)}, u32[]{:S(2)}) collective-permute-start(bf16[400,128]{1,0:T(8,128)(2,1)S(1)} %shard_map.145.refs_0_), channel_id=1, source_target_pairs={{0,2},{1,3},{2,0},{3,1},{4,6},{5,7},{6,4},{7,5},{8,10},{9,11},{10,... | collective-permute-start | bytes 307208 | tf_op jit(solution)/shard_map/ppermute | solution.py:306
  10.1 0.8 %pad_add_fusion.refs_0_ = s32[5,1024]{1,0:T(8,128)S(1)} fusion(s32[2,1024]{1,0:T(2,128)} %bitcast.27, s32[1,1024]{1,0:T(1,128)} %bitcast.28, s32[1,1024]{1,0:T(1,128)} %bitcast.29, s32[1,1024]{1,0:T(1,128)} %bitcast.30), kind=kLoop, calls=%fused_computation | loop fusion | flops 15360 | bytes 40960 | tf_op jit(solution)/shard_map/concatenate | solution.py:348
  10.9 0.1 pad_add_fusion.1.refs_2_
  10.9 1.9 %collective-permute-done.refs_0_ = bf16[400,128]{1,0:T(8,128)(2,1)S(1)} collective-permute-done((bf16[400,128]{1,0:T(8,128)(2,1)S(1)}, bf16[400,128]{1,0:T(8,128)(2,1)S(1)}, u32[]{:S(2)}, u32[]{:S(2)}) %collective-permute-start) | collective-permute-done | bytes 102432 | tf_op jit(solution)/shard_map/ppermute | solution.py:313
  12.9 1.6 %collective-permute-start.7 = (bf16[400,256]{1,0:T(8,128)(2,1)S(1)}, bf16[400,256]{1,0:T(8,128)(2,1)S(1)}, u32[]{:S(2)}, u32[]{:S(2)}) collective-permute-start(bf16[400,256]{1,0:T(8,128)(2,1)S(1)} %shard_map.146.refs_3_), channel_id=1, source_target_pairs={{0,4},{4,0},{8,12},{12,8},{16,20},{20,16},{24,28},{28,24},{1,5},{5... | collective-permute-start | bytes 614408 | tf_op jit(solution)/shard_map/ppermute | solution.py:303
  14.5 1.6 %shard_map.147 = (f32[2,1024,128]{2,1,0:T(8,128)S(1)}, bf16[400,256]{1,0:T(8,128)(2,1)S(1)}, s32[5,1024]{1,0:T(8,128)S(1)}) custom-call(s32[5,1024]{1,0:T(8,128)S(1)} %pad_add_fusion.refs_0_, f32[400,256]{1,0:T(8,128)S(1)} %bitcast.19, s32[2]{0:T(128)S(1)} %pad_add_fusion.1.refs_2_, bf16[400,256]{1,0:T(8,128)(2,1)S(1)} %shard_map.146.refs_3_), custom_call_target="tpu_custom_call" | custom-call | tf_op jit(solution)/shard_map/pallas_call | solution.py:56
  16.1 0.0 copy-start.3
  16.1 0.0 copy-start.6
  16.1 0.1 collective-permute-start.6
  16.2 1.7 %collective-permute-done.1.refs_1_.refs_2_ = bf16[400,128]{1,0:T(8,128)(2,1)S(1)} collective-permute-done((bf16[400,128]{1,0:T(8,128)(2,1)S(1)}, bf16[400,128]{1,0:T(8,128)(2,1)S(1)}, u32[]{:S(2)}, u32[]{:S(2)}) %collective-permute-start.1) | collective-permute-done | bytes 102432 | tf_op jit(solution)/shard_map/ppermute | solution.py:313
  17.9 1.6 %collective-permute-start.5 = (bf16[400,256]{1,0:T(8,128)(2,1)S(1)}, bf16[400,256]{1,0:T(8,128)(2,1)S(1)}, u32[]{:S(2)}, u32[]{:S(2)}) collective-permute-start(bf16[400,256]{1,0:T(8,128)(2,1)S(1)} %shard_map.149.refs_2_), channel_id=1, source_target_pairs={{0,4},{4,0},{8,12},{12,8},{16,20},{20,16},{24,28},{28,24},{1,5},{5... | collective-permute-start | bytes 614408 | tf_op jit(solution)/shard_map/ppermute | solution.py:303
  19.5 0.1 collective-permute-start.8
  19.6 0.9 %shard_map.150 = (bf16[400,1024]{1,0:T(8,128)(2,1)S(1)}, bf16[400,1024]{1,0:T(8,128)(2,1)S(1)}, bf16[400,1024]{1,0:T(8,128)(2,1)S(1)}) custom-call(bf16[400,128]{1,0:T(8,128)(2,1)S(1)} %shard_map.145.refs_0_, bf16[400,128]{1,0:T(8,128)(2,1)S(1)} %collective-permute-done.3.refs_1_, bf16[400,256]{1,0:T(8,128)(2,1)S(1)} %collective-permute-done.6.refs_2_, ...), custom_call_target="tpu_custom_call" | custom-call | flops 6000000000 | tf_op jit(solution)/shard_map/pallas_call | solution.py:56
  20.6 1.8 %shard_map.152 = (f32[400,512]{1,0:T(8,128)S(1)}, f32[400,1024]{1,0:T(8,128)S(1)}) custom-call(bf16[400,128]{1,0:T(8,128)(2,1)S(1)} %collective-permute-done.refs_0_, bf16[400,128]{1,0:T(8,128)(2,1)S(1)} %collective-permute-done.4.refs_1_, bf16[400,128]{1,0:T(8,128)(2,1)S(1)} %collective-permute-done.1.refs_1_.refs_2_, ...), custom_call_target="tpu_custom_call" | custom-call | tf_op jit(solution)/shard_map/pallas_call | solution.py:56
  22.4 1.0 %shard_map.153 = (bf16[400,256]{1,0:T(8,128)(2,1)S(1)}, f32[400,1024]{1,0:T(8,128)S(1)}) custom-call(bf16[400,256]{1,0:T(8,128)(2,1)S(1)} %shard_map.151.rows_ref, bf16[400,1024]{1,0:T(8,128)(2,1)S(1)} %get-tuple-element.39.refs_4_.q_ref.refs_1_, f32[2,1024,128]{2,1,0:T(8,128)S(1)} %get-tuple-element.36.refs_2_.refs_5_.weight_ref, ...), custom_call_target="tpu_custom_call" | custom-call | tf_op jit(solution)/shard_map/pallas_call | solution.py:56
  23.4 1.0 %collective-permute-done.5.refs_0_ = bf16[400,256]{1,0:T(8,128)(2,1)S(1)} collective-permute-done((bf16[400,256]{1,0:T(8,128)(2,1)S(1)}, bf16[400,256]{1,0:T(8,128)(2,1)S(1)}, u32[]{:S(2)}, u32[]{:S(2)}) %collective-permute-start.5) | collective-permute-done | bytes 204832 | tf_op jit(solution)/shard_map/ppermute | solution.py:303
  24.4 0.4 collective-permute-done.8.refs_7_.refs_4_.refs_5_
  24.8 1.9 %shard_map.155 = (bf16[256,1024]{1,0:T(8,128)(2,1)S(1)}, f32[400,1024]{1,0:T(8,128)S(1)}, f32[416,128]{1,0:T(8,128)S(1)}, bf16[416,128]{1,0:T(8,128)(2,1)S(1)}) custom-call(bf16[400,256]{1,0:T(8,128)(2,1)S(1)} %collective-permute-done.5.refs_0_, bf16[400,1024]{1,0:T(8,128)(2,1)S(1)} %get-tuple-element.39.refs_4_.q_ref.refs_1_, ...), custom_call_target="tpu_custom_call" | custom-call | tf_op jit(solution)/shard_map/pallas_call | solution.py:56
  26.7 0.1 collective-permute-start.14
  26.8 1.0 %shard_map.156 = (bf16[400,256]{1,0:T(8,128)(2,1)S(1)}, bf16[400,256]{1,0:T(8,128)(2,1)S(1)}, f32[400,256]{1,0:T(8,128)S(1)}, bf16[400,256]{1,0:T(8,128)(2,1)S(1)}) custom-call(bf16[256,1024]{1,0:T(8,128)(2,1)S(1)} %get-tuple-element.43.m_ref, bf16[400,1024]{1,0:T(8,128)(2,1)S(1)} %get-tuple-element.39.refs_4_.q_ref.refs_1_, ...), custom_call_target="tpu_custom_call" | custom-call | tf_op jit(solution)/shard_map/pallas_call | solution.py:56
  27.8 0.6 %collective-permute-start.9 = (bf16[400,256]{1,0:T(8,128)(2,1)S(1)}, bf16[400,256]{1,0:T(8,128)(2,1)S(1)}, u32[]{:S(2)}, u32[]{:S(2)}) collective-permute-start(bf16[400,256]{1,0:T(8,128)(2,1)S(1)} %get-tuple-element.48), channel_id=1, source_target_pairs={{0,1},{1,0},{2,3},{3,2},{4,5},{5,4},{6,7},{7,6},{8,9},{9,8},{10,11... | collective-permute-start | bytes 614408 | tf_op jit(solution)/shard_map/ppermute | solution.py:306
  28.4 1.2 %collective-permute-start.15 = (bf16[208,128]{1,0:T(8,128)(2,1)S(1)}, bf16[208,128]{1,0:T(8,128)(2,1)S(1)}, u32[]{:S(2)}, u32[]{:S(2)}) collective-permute-start(bf16[208,128]{1,0:T(8,128)(2,1)S(1)} %get-tuple-element.60), channel_id=1, source_target_pairs={{0,2},{1,3},{2,0},{3,1},{4,6},{5,7},{6,4},{7,5},{8,10},{9,11},{10,... | collective-permute-start | bytes 159752 | tf_op jit(solution)/shard_map/ppermute | solution.py:306
  29.5 1.2 %collective-permute-start.12 = (bf16[400,256]{1,0:T(8,128)(2,1)S(1)}, bf16[400,256]{1,0:T(8,128)(2,1)S(1)}, u32[]{:S(2)}, u32[]{:S(2)}) collective-permute-start(bf16[400,256]{1,0:T(8,128)(2,1)S(1)} %get-tuple-element.56), channel_id=1, source_target_pairs={{0,4},{4,0},{8,12},{12,8},{16,20},{20,16},{24,28},{28,24},{1,5},{5... | collective-permute-start | bytes 614408 | tf_op jit(solution)/shard_map/ppermute | solution.py:303
  30.7 1.8 %collective-permute-done.15.refs_1_ = bf16[208,128]{1,0:T(8,128)(2,1)S(1)} collective-permute-done((bf16[208,128]{1,0:T(8,128)(2,1)S(1)}, bf16[208,128]{1,0:T(8,128)(2,1)S(1)}, u32[]{:S(2)}, u32[]{:S(2)}) %collective-permute-start.15) | collective-permute-done | bytes 53280 | tf_op jit(solution)/shard_map/ppermute | solution.py:306
  32.6 1.7 %collective-permute-start.16 = (bf16[208,128]{1,0:T(8,128)(2,1)S(1)}, bf16[208,128]{1,0:T(8,128)(2,1)S(1)}, u32[]{:S(2)}, u32[]{:S(2)}) collective-permute-start(bf16[208,128]{1,0:T(8,128)(2,1)S(1)} %shard_map.162.refs_0_), channel_id=1, source_target_pairs={{0,16},{4,20},{8,24},{12,28},{16,0},{20,4},{24,8},{28,12},{1,17},{... | collective-permute-start | bytes 159752 | tf_op jit(solution)/shard_map/ppermute | solution.py:303
  34.2 0.9 %collective-permute-start.11 = (bf16[400,256]{1,0:T(8,128)(2,1)S(1)}, bf16[400,256]{1,0:T(8,128)(2,1)S(1)}, u32[]{:S(2)}, u32[]{:S(2)}) collective-permute-start(bf16[400,256]{1,0:T(8,128)(2,1)S(1)} %get-tuple-element.54), channel_id=1, source_target_pairs={{0,4},{4,0},{8,12},{12,8},{16,20},{20,16},{24,28},{28,24},{1,5},{5... | collective-permute-start | bytes 614408 | tf_op jit(solution)/shard_map/ppermute | solution.py:303
  35.2 1.0 %collective-permute-start.10 = (bf16[400,128]{1,0:T(8,128)(2,1)S(1)}, bf16[400,128]{1,0:T(8,128)(2,1)S(1)}, u32[]{:S(2)}, u32[]{:S(2)}) collective-permute-start(bf16[400,128]{1,0:T(8,128)(2,1)S(1)} %get-tuple-element.50), channel_id=1, source_target_pairs={{0,2},{1,3},{2,0},{3,1},{4,6},{5,7},{6,4},{7,5},{8,10},{9,11},{10,... | collective-permute-start | bytes 307208 | tf_op jit(solution)/shard_map/ppermute | solution.py:306
  36.2 1.5 %collective-permute-done.16.refs_1_ = bf16[208,128]{1,0:T(8,128)(2,1)S(1)} collective-permute-done((bf16[208,128]{1,0:T(8,128)(2,1)S(1)}, bf16[208,128]{1,0:T(8,128)(2,1)S(1)}, u32[]{:S(2)}, u32[]{:S(2)}) %collective-permute-start.16) | collective-permute-done | bytes 53280 | tf_op jit(solution)/shard_map/ppermute | solution.py:303
  37.7 0.4 collective-permute-start.17
  38.2 3.2 %collective-permute-start.13 = (bf16[400,128]{1,0:T(8,128)(2,1)S(1)}, bf16[400,128]{1,0:T(8,128)(2,1)S(1)}, u32[]{:S(2)}, u32[]{:S(2)}) collective-permute-start(bf16[400,128]{1,0:T(8,128)(2,1)S(1)} %shard_map.160), channel_id=1, source_target_pairs={{0,16},{4,20},{8,24},{12,28},{16,0},{20,4},{24,8},{28,12},{1,17},{... | collective-permute-start | bytes 307208 | tf_op jit(solution)/shard_map/ppermute | solution.py:303
  41.4 0.6 %collective-permute-done.17.refs_1_ = bf16[208,128]{1,0:T(8,128)(2,1)S(1)} collective-permute-done((bf16[208,128]{1,0:T(8,128)(2,1)S(1)}, bf16[208,128]{1,0:T(8,128)(2,1)S(1)}, u32[]{:S(2)}, u32[]{:S(2)}) %collective-permute-start.17) | collective-permute-done | bytes 53280 | tf_op jit(solution)/shard_map/ppermute | solution.py:303
  42.0 1.5 %collective-permute-start.20 = (bf16[208,128]{1,0:T(8,128)(2,1)S(1)}, bf16[208,128]{1,0:T(8,128)(2,1)S(1)}, u32[]{:S(2)}, u32[]{:S(2)}) collective-permute-start(bf16[208,128]{1,0:T(8,128)(2,1)S(1)} %shard_map.164.refs_2_.refs_0_), channel_id=1, source_target_pairs={{0,4},{4,0},{8,12},{12,8},{16,20},{20,16},{24,28},{28,24},{1,5},{5... | collective-permute-start | bytes 159752 | tf_op jit(solution)/shard_map/ppermute | solution.py:303
  43.6 2.5 %collective-permute-start.18 = (bf16[400,128]{1,0:T(8,128)(2,1)S(1)}, bf16[400,128]{1,0:T(8,128)(2,1)S(1)}, u32[]{:S(2)}, u32[]{:S(2)}) collective-permute-start(bf16[400,128]{1,0:T(8,128)(2,1)S(1)} %shard_map.165), channel_id=1, source_target_pairs={{0,24},{4,28},{8,16},{12,20},{16,8},{20,12},{24,0},{28,4},{1,25},{... | collective-permute-start | bytes 307208 | tf_op jit(solution)/shard_map/ppermute | solution.py:303
  46.1 0.1 shard_map.159
  46.2 0.1 collective-permute-start.19
  46.3 1.3 %collective-permute-start.21 = (bf16[208,128]{1,0:T(8,128)(2,1)S(1)}, bf16[208,128]{1,0:T(8,128)(2,1)S(1)}, u32[]{:S(2)}, u32[]{:S(2)}) collective-permute-start(bf16[208,128]{1,0:T(8,128)(2,1)S(1)} %shard_map.167.refs_0_), channel_id=1, source_target_pairs={{0,2},{1,3},{2,0},{3,1},{4,6},{5,7},{6,4},{7,5},{8,10},{9,11},{10,... | collective-permute-start | bytes 159752 | tf_op jit(solution)/shard_map/ppermute | solution.py:306
  47.6 0.8 %shard_map.158 = (f32[400,128]{1,0:T(8,128)}, f32[1,128]{1,0:T(1,128)}) custom-call(f32[400,128]{1,0:T(8,128)S(1)} %get-tuple-element.49.refs_0_, bf16[400,128]{1,0:T(8,128)(2,1)S(1)} %collective-permute-done.10.refs_1_.refs_2_, f32[400,128]{1,0:T(8,128)S(1)} %bitcast.22, f32[1,128]{1,0:T(1,128)S(1)} %bitcast.25), custom_call_target="tpu_custom_call" | custom-call | tf_op jit(solution)/shard_map/pallas_call | solution.py:56
  48.4 2.1 %collective-permute-done.21.refs_1_ = bf16[208,128]{1,0:T(8,128)(2,1)S(1)} collective-permute-done((bf16[208,128]{1,0:T(8,128)(2,1)S(1)}, bf16[208,128]{1,0:T(8,128)(2,1)S(1)}, u32[]{:S(2)}, u32[]{:S(2)}) %collective-permute-start.21) | collective-permute-done | bytes 53280 | tf_op jit(solution)/shard_map/ppermute | solution.py:306
  50.5 0.1 collective-permute-start.22
  50.6 0.6 %collective-permute-done.19.refs_3_ = bf16[400,128]{1,0:T(8,128)(2,1)S(1)} collective-permute-done((bf16[400,128]{1,0:T(8,128)(2,1)S(1)}, bf16[400,128]{1,0:T(8,128)(2,1)S(1)}, u32[]{:S(2)}, u32[]{:S(2)}) %collective-permute-start.19) | collective-permute-done | bytes 102432 | tf_op jit(solution)/shard_map/ppermute | solution.py:303
  51.2 0.8 %shard_map.166 = (f32[400,128]{1,0:T(8,128)}, f32[1,128]{1,0:T(1,128)}) custom-call(f32[400,128]{1,0:T(8,128)S(1)} %get-tuple-element.55.refs_0_, bf16[400,128]{1,0:T(8,128)(2,1)S(1)} %collective-permute-done.13.refs_1_, bf16[400,128]{1,0:T(8,128)(2,1)S(1)} %collective-permute-done.18.refs_2_, bf16[400,128]{1,0:T(8,128)(2,1)S(1)} %collective-permute-done.19.refs_3_, ...), custom_call_target="tpu_custom_call" | custom-call | flops 12000000000 | tf_op jit(solution)/shard_map/pallas_call | solution.py:56
  52.0 0.9 %shard_map.169 = (f32[400,256]{1,0:T(8,128)}, f32[1,256]{1,0:T(1,128)}) custom-call(bf16[208,128]{1,0:T(8,128)(2,1)S(1)} %shard_map.167.refs_0_, bf16[208,128]{1,0:T(8,128)(2,1)S(1)} %collective-permute-done.21.refs_1_, bf16[416,128]{1,0:T(8,128)(2,1)S(1)} %collective-permute-done.22.refs_2_, f32[400,256]{1,0:T(8,128)S(1)} %bitcast.20, ...), custom_call_target="tpu_custom_call" | custom-call | tf_op jit(solution)/shard_map/pallas_call | solution.py:56
  (40 shorter events, 0.4 us)
Async XLA Ops:
  1.6 9.4 %collective-permute-start.4 = (bf16[400,128]{1,0:T(8,128)(2,1)S(1)}, bf16[400,128]{1,0:T(8,128)(2,1)S(1)}, u32[]{:S(2)}, u32[]{:S(2)}) collective-permute-start(bf16[400,128]{1,0:T(8,128)(2,1)S(1)} %bitcast_convert_fusion), channel_id=1, source_target_pairs={{0,9},{1,10},{2,11},{3,8},{4,13},{5,14},{6,15},{7,12},{8,1},{9,2},... | collective-permute-start | bytes 307208 | tf_op jit(solution)/shard_map/ppermute | solution.py:313
  4.1 12.1 %collective-permute-start.2 = (bf16[400,128]{1,0:T(8,128)(2,1)S(1)}, bf16[400,128]{1,0:T(8,128)(2,1)S(1)}, u32[]{:S(2)}, u32[]{:S(2)}) collective-permute-start(bf16[400,128]{1,0:T(8,128)(2,1)S(1)} %bitcast_convert_fusion), channel_id=1, source_target_pairs={{0,25},{1,26},{2,27},{3,24},{4,29},{5,30},{6,31},{7,28},{8,17},{9,... | collective-permute-start | bytes 307208 | tf_op jit(solution)/shard_map/ppermute | solution.py:313
  7.8 10.1 %collective-permute-start.1 = (bf16[400,128]{1,0:T(8,128)(2,1)S(1)}, bf16[400,128]{1,0:T(8,128)(2,1)S(1)}, u32[]{:S(2)}, u32[]{:S(2)}) collective-permute-start(bf16[400,128]{1,0:T(8,128)(2,1)S(1)} %bitcast_convert_fusion), channel_id=1, source_target_pairs={{0,17},{1,18},{2,19},{3,16},{4,21},{5,22},{6,23},{7,20},{8,25},{9,... | collective-permute-start | bytes 307208 | tf_op jit(solution)/shard_map/ppermute | solution.py:313
  7.9 4.9 %collective-permute-start = (bf16[400,128]{1,0:T(8,128)(2,1)S(1)}, bf16[400,128]{1,0:T(8,128)(2,1)S(1)}, u32[]{:S(2)}, u32[]{:S(2)}) collective-permute-start(bf16[400,128]{1,0:T(8,128)(2,1)S(1)} %bitcast_convert_fusion), channel_id=1, source_target_pairs={{0,1},{1,2},{2,3},{3,0},{4,5},{5,6},{6,7},{7,4},{8,9},{9,10},{10,1... | collective-permute-start | bytes 307208 | tf_op jit(solution)/shard_map/ppermute | solution.py:313
  7.9 0.9 %copy-start.1 = (f32[128,400]{0,1:T(8,128)S(1)}, f32[128,400]{0,1:T(8,128)}, u32[]{:S(2)}) copy-start(f32[128,400]{0,1:T(8,128)} %param.10) | copy-start | bytes 614404
  9.1 6.9 %collective-permute-start.3 = (bf16[400,128]{1,0:T(8,128)(2,1)S(1)}, bf16[400,128]{1,0:T(8,128)(2,1)S(1)}, u32[]{:S(2)}, u32[]{:S(2)}) collective-permute-start(bf16[400,128]{1,0:T(8,128)(2,1)S(1)} %shard_map.145.refs_0_), channel_id=1, source_target_pairs={{0,2},{1,3},{2,0},{3,1},{4,6},{5,7},{6,4},{7,5},{8,10},{9,11},{10,... | collective-permute-start | bytes 307208 | tf_op jit(solution)/shard_map/ppermute | solution.py:306
  10.9 3.5 %copy-start = (f32[256,400]{0,1:T(8,128)S(1)}, f32[256,400]{0,1:T(8,128)}, u32[]{:S(2)}) copy-start(f32[256,400]{0,1:T(8,128)} %param.14) | copy-start | bytes 1228804
  12.9 6.7 %collective-permute-start.7 = (bf16[400,256]{1,0:T(8,128)(2,1)S(1)}, bf16[400,256]{1,0:T(8,128)(2,1)S(1)}, u32[]{:S(2)}, u32[]{:S(2)}) collective-permute-start(bf16[400,256]{1,0:T(8,128)(2,1)S(1)} %shard_map.146.refs_3_), channel_id=1, source_target_pairs={{0,4},{4,0},{8,12},{12,8},{16,20},{20,16},{24,28},{28,24},{1,5},{5... | collective-permute-start | bytes 614408 | tf_op jit(solution)/shard_map/ppermute | solution.py:303
  16.1 3.5 %copy-start.3 = (f32[128,400]{0,1:T(8,128)S(1)}, f32[128,400]{0,1:T(8,128)}, u32[]{:S(2)}) copy-start(f32[128,400]{0,1:T(8,128)} %param.12) | copy-start | bytes 614404
  16.1 3.4 %copy-start.6 = (f32[128]{0:T(128)S(1)}, f32[128]{0:T(128)}, u32[]{:S(2)}) copy-start(f32[128]{0:T(128)} %param.13) | copy-start | bytes 1540
  16.1 3.6 %collective-permute-start.6 = (bf16[400,256]{1,0:T(8,128)(2,1)S(1)}, bf16[400,256]{1,0:T(8,128)(2,1)S(1)}, u32[]{:S(2)}, u32[]{:S(2)}) collective-permute-start(bf16[400,256]{1,0:T(8,128)(2,1)S(1)} %shard_map.148.refs_3_), channel_id=1, source_target_pairs={{0,1},{1,0},{2,3},{3,2},{4,5},{5,4},{6,7},{7,6},{8,9},{9,8},{10,11... | collective-permute-start | bytes 614408 | tf_op jit(solution)/shard_map/ppermute | solution.py:306
  17.9 6.5 %collective-permute-start.5 = (bf16[400,256]{1,0:T(8,128)(2,1)S(1)}, bf16[400,256]{1,0:T(8,128)(2,1)S(1)}, u32[]{:S(2)}, u32[]{:S(2)}) collective-permute-start(bf16[400,256]{1,0:T(8,128)(2,1)S(1)} %shard_map.149.refs_2_), channel_id=1, source_target_pairs={{0,4},{4,0},{8,12},{12,8},{16,20},{20,16},{24,28},{28,24},{1,5},{5... | collective-permute-start | bytes 614408 | tf_op jit(solution)/shard_map/ppermute | solution.py:303
  19.5 5.3 %collective-permute-start.8 = (f32[408,128]{1,0:T(8,128)S(1)}, f32[408,128]{1,0:T(8,128)S(1)}, u32[]{:S(2)}, u32[]{:S(2)}) collective-permute-start(f32[408,128]{1,0:T(8,128)S(1)} %shard_map.154), channel_id=1, source_target_pairs={{0,1},{1,2},{2,3},{3,0},{4,5},{5,6},{6,7},{7,4},{8,9},{9,10},{10,1... | collective-permute-start | bytes 626696 | tf_op jit(solution)/shard_map/ppermute | solution.py:313
  26.7 1.6 %collective-permute-start.14 = (bf16[416,128]{1,0:T(8,128)(2,1)S(1)}, bf16[416,128]{1,0:T(8,128)(2,1)S(1)}, u32[]{:S(2)}, u32[]{:S(2)}) collective-permute-start(bf16[416,128]{1,0:T(8,128)(2,1)S(1)} %get-tuple-element.58), channel_id=1, source_target_pairs={{0,1},{1,0},{2,3},{3,2},{4,5},{5,4},{6,7},{7,6},{8,9},{9,8},{10,11... | collective-permute-start | bytes 319496 | tf_op jit(solution)/shard_map/ppermute | solution.py:306
  27.8 7.4 %collective-permute-start.9 = (bf16[400,256]{1,0:T(8,128)(2,1)S(1)}, bf16[400,256]{1,0:T(8,128)(2,1)S(1)}, u32[]{:S(2)}, u32[]{:S(2)}) collective-permute-start(bf16[400,256]{1,0:T(8,128)(2,1)S(1)} %get-tuple-element.48), channel_id=1, source_target_pairs={{0,1},{1,0},{2,3},{3,2},{4,5},{5,4},{6,7},{7,6},{8,9},{9,8},{10,11... | collective-permute-start | bytes 614408 | tf_op jit(solution)/shard_map/ppermute | solution.py:306
  28.4 4.2 %collective-permute-start.15 = (bf16[208,128]{1,0:T(8,128)(2,1)S(1)}, bf16[208,128]{1,0:T(8,128)(2,1)S(1)}, u32[]{:S(2)}, u32[]{:S(2)}) collective-permute-start(bf16[208,128]{1,0:T(8,128)(2,1)S(1)} %get-tuple-element.60), channel_id=1, source_target_pairs={{0,2},{1,3},{2,0},{3,1},{4,6},{5,7},{6,4},{7,5},{8,10},{9,11},{10,... | collective-permute-start | bytes 159752 | tf_op jit(solution)/shard_map/ppermute | solution.py:306
  29.5 8.6 %collective-permute-start.12 = (bf16[400,256]{1,0:T(8,128)(2,1)S(1)}, bf16[400,256]{1,0:T(8,128)(2,1)S(1)}, u32[]{:S(2)}, u32[]{:S(2)}) collective-permute-start(bf16[400,256]{1,0:T(8,128)(2,1)S(1)} %get-tuple-element.56), channel_id=1, source_target_pairs={{0,4},{4,0},{8,12},{12,8},{16,20},{20,16},{24,28},{28,24},{1,5},{5... | collective-permute-start | bytes 614408 | tf_op jit(solution)/shard_map/ppermute | solution.py:303
  32.6 5.1 %collective-permute-start.16 = (bf16[208,128]{1,0:T(8,128)(2,1)S(1)}, bf16[208,128]{1,0:T(8,128)(2,1)S(1)}, u32[]{:S(2)}, u32[]{:S(2)}) collective-permute-start(bf16[208,128]{1,0:T(8,128)(2,1)S(1)} %shard_map.162.refs_0_), channel_id=1, source_target_pairs={{0,16},{4,20},{8,24},{12,28},{16,0},{20,4},{24,8},{28,12},{1,17},{... | collective-permute-start | bytes 159752 | tf_op jit(solution)/shard_map/ppermute | solution.py:303
  34.2 11.8 %collective-permute-start.11 = (bf16[400,256]{1,0:T(8,128)(2,1)S(1)}, bf16[400,256]{1,0:T(8,128)(2,1)S(1)}, u32[]{:S(2)}, u32[]{:S(2)}) collective-permute-start(bf16[400,256]{1,0:T(8,128)(2,1)S(1)} %get-tuple-element.54), channel_id=1, source_target_pairs={{0,4},{4,0},{8,12},{12,8},{16,20},{20,16},{24,28},{28,24},{1,5},{5... | collective-permute-start | bytes 614408 | tf_op jit(solution)/shard_map/ppermute | solution.py:303
  35.2 10.9 %collective-permute-start.10 = (bf16[400,128]{1,0:T(8,128)(2,1)S(1)}, bf16[400,128]{1,0:T(8,128)(2,1)S(1)}, u32[]{:S(2)}, u32[]{:S(2)}) collective-permute-start(bf16[400,128]{1,0:T(8,128)(2,1)S(1)} %get-tuple-element.50), channel_id=1, source_target_pairs={{0,2},{1,3},{2,0},{3,1},{4,6},{5,7},{6,4},{7,5},{8,10},{9,11},{10,... | collective-permute-start | bytes 307208 | tf_op jit(solution)/shard_map/ppermute | solution.py:306
  37.7 4.3 %collective-permute-start.17 = (bf16[208,128]{1,0:T(8,128)(2,1)S(1)}, bf16[208,128]{1,0:T(8,128)(2,1)S(1)}, u32[]{:S(2)}, u32[]{:S(2)}) collective-permute-start(bf16[208,128]{1,0:T(8,128)(2,1)S(1)} %shard_map.163.refs_0_), channel_id=1, source_target_pairs={{0,8},{4,12},{8,0},{12,4},{16,24},{20,28},{24,16},{28,20},{1,9},{5... | collective-permute-start | bytes 159752 | tf_op jit(solution)/shard_map/ppermute | solution.py:303
  38.2 12.4 %collective-permute-start.13 = (bf16[400,128]{1,0:T(8,128)(2,1)S(1)}, bf16[400,128]{1,0:T(8,128)(2,1)S(1)}, u32[]{:S(2)}, u32[]{:S(2)}) collective-permute-start(bf16[400,128]{1,0:T(8,128)(2,1)S(1)} %shard_map.160), channel_id=1, source_target_pairs={{0,16},{4,20},{8,24},{12,28},{16,0},{20,4},{24,8},{28,12},{1,17},{... | collective-permute-start | bytes 307208 | tf_op jit(solution)/shard_map/ppermute | solution.py:303
  42.0 4.2 %collective-permute-start.20 = (bf16[208,128]{1,0:T(8,128)(2,1)S(1)}, bf16[208,128]{1,0:T(8,128)(2,1)S(1)}, u32[]{:S(2)}, u32[]{:S(2)}) collective-permute-start(bf16[208,128]{1,0:T(8,128)(2,1)S(1)} %shard_map.164.refs_2_.refs_0_), channel_id=1, source_target_pairs={{0,4},{4,0},{8,12},{12,8},{16,20},{20,16},{24,28},{28,24},{1,5},{5... | collective-permute-start | bytes 159752 | tf_op jit(solution)/shard_map/ppermute | solution.py:303
  43.6 7.0 %collective-permute-start.18 = (bf16[400,128]{1,0:T(8,128)(2,1)S(1)}, bf16[400,128]{1,0:T(8,128)(2,1)S(1)}, u32[]{:S(2)}, u32[]{:S(2)}) collective-permute-start(bf16[400,128]{1,0:T(8,128)(2,1)S(1)} %shard_map.165), channel_id=1, source_target_pairs={{0,24},{4,28},{8,16},{12,20},{16,8},{20,12},{24,0},{28,4},{1,25},{... | collective-permute-start | bytes 307208 | tf_op jit(solution)/shard_map/ppermute | solution.py:303
  46.2 1.5 %copy-start.2 = (f32[128,400]{0,1:T(8,128)S(1)}, f32[128,400]{0,1:T(8,128)}, u32[]{:S(2)}) copy-start(f32[128,400]{0,1:T(8,128)} %param.10) | copy-start | bytes 614404
  46.2 1.5 %copy-start.5 = (f32[128]{0:T(128)S(1)}, f32[128]{0:T(128)}, u32[]{:S(2)}) copy-start(f32[128]{0:T(128)} %param.11) | copy-start | bytes 1540
  46.2 5.0 %collective-permute-start.19 = (bf16[400,128]{1,0:T(8,128)(2,1)S(1)}, bf16[400,128]{1,0:T(8,128)(2,1)S(1)}, u32[]{:S(2)}, u32[]{:S(2)}) collective-permute-start(bf16[400,128]{1,0:T(8,128)(2,1)S(1)} %get-tuple-element.61), channel_id=1, source_target_pairs={{0,8},{4,12},{8,0},{12,4},{16,24},{20,28},{24,16},{28,20},{1,9},{5... | collective-permute-start | bytes 307208 | tf_op jit(solution)/shard_map/ppermute | solution.py:303
  46.3 4.2 %collective-permute-start.21 = (bf16[208,128]{1,0:T(8,128)(2,1)S(1)}, bf16[208,128]{1,0:T(8,128)(2,1)S(1)}, u32[]{:S(2)}, u32[]{:S(2)}) collective-permute-start(bf16[208,128]{1,0:T(8,128)(2,1)S(1)} %shard_map.167.refs_0_), channel_id=1, source_target_pairs={{0,2},{1,3},{2,0},{3,1},{4,6},{5,7},{6,4},{7,5},{8,10},{9,11},{10,... | collective-permute-start | bytes 159752 | tf_op jit(solution)/shard_map/ppermute | solution.py:306
  50.5 1.5 %collective-permute-start.22 = (bf16[416,128]{1,0:T(8,128)(2,1)S(1)}, bf16[416,128]{1,0:T(8,128)(2,1)S(1)}, u32[]{:S(2)}, u32[]{:S(2)}) collective-permute-start(bf16[416,128]{1,0:T(8,128)(2,1)S(1)} %shard_map.168), channel_id=1, source_target_pairs={{0,1},{1,0},{2,3},{3,2},{4,5},{5,4},{6,7},{7,6},{8,9},{9,8},{10,11... | collective-permute-start | bytes 319496 | tf_op jit(solution)/shard_map/ppermute | solution.py:306
  51.2 0.8 %copy-start.4 = (f32[256]{0:T(256)S(1)}, f32[256]{0:T(256)}, u32[]{:S(2)}) copy-start(f32[256]{0:T(256)} %param.15) | copy-start | bytes 3076

commit v19 on v18

--- a/solution.py
+++ b/solution.py
@@ -32,7 +32,7 @@
     return jnp.where(spot == ids, 1.0, 0.0).astype(BF)
 
 
-def step_of(size, most=256):
+def step_of(size, most=512):
     return most if size % most == 0 else size
 
 
@@ -382,7 +382,6 @@
              shape(far_right * size, LANES, dtype=BF)),
             [pltpu.VMEM((width, nrel), F32), all_pieces],
             me,
-            after=(moved,),
         )(other_high, q, weight, ids, qg, s)
         left_rows = n_right * rows
         left_half = left_rows // 2
@@ -390,6 +389,7 @@
             rest_body,
             (chunk, chunk, shape(width, left_half), shape(width, left_half, dtype=BF)),
             [pltpu.VMEM((width, left_rows), F32)],
+            after=(moved,),
         )(m, q, g, o, ids, right_low)
 
         mine, *rest = call(

time: 53.1 us -> 56.5 us (1.064)
  starting transfers between devices: 26.2 us -> 29.9 us
    ppermute x10, starting transfers between devices: 14.6 us -> 17.3 us  [swap_left(): return lax.ppermute(value, 'left', [(i, i ^ by) for i in range(n_left)])]
    ppermute x10, waiting for transfers between devices: 3.77 us -> 2.74 us  [swap_left(): return lax.ppermute(value, 'left', [(i, i ^ by) for i in range(n_left)])]
    ppermute x8, waiting for transfers between devices: 3.93 us -> 4.66 us  [swap_right(): return lax.ppermute(value, 'right', [(i, i ^ by) for i in range(n_right)])]
  transfers between devices with their start and end apart: 23 -> 23, of which waited for: 9 -> 10; matrix products, arithmetic and copies ran while one was open for 2% -> 1% of each run, Pallas kernels for 16% -> 15%
where the time goes in v19:
time: 56.5 us; the launch traced here: 56.3 us
  starting transfers between devices  29.9 us (53%)
  waiting for transfers between devices  11.8 us (21%)
  Pallas kernels  11.1 us (20%)
  other arithmetic  1.78 us (3%)
  local copies, waits for them, and re-layouts  0.96 us (2%)
  between operations  0.86 us (2%)
    ppermute x10, starting transfers between devices, swap_left(): return lax.ppermute(value, 'left', [(i, i ^ by) for i in range(n_left)])  17.3 us
    pallas_call x25, Pallas kernels, run(): pl.pallas_call(inner, out_shape=out_shape, in_specs=specs, scratch_shapes...  11.1 us
    ppermute x5, starting transfers between devices, next_column(): return lax.ppermute(value, ('left', 'right'), perm)  6.91 us
    ppermute x8, starting transfers between devices, swap_right(): return lax.ppermute(value, 'right', [(i, i ^ by) for i in range(n_right)])  5.69 us
    ppermute x8, waiting for transfers between devices, swap_right(): return lax.ppermute(value, 'right', [(i, i ^ by) for i in range(n_right)])  4.66 us
    ppermute x5, waiting for transfers between devices, next_column(): return lax.ppermute(value, ('left', 'right'), perm)  4.37 us
    ppermute x10, waiting for transfers between devices, swap_left(): return lax.ppermute(value, 'left', [(i, i ^ by) for i in range(n_left)])  2.74 us
  transfers between devices with their start and end apart: 23, of which 10 were waited for; matrix products, arithmetic and copies ran while one was open for 1% of the time, Pallas kernels for 15%

profile of v19, /device:TPU:0, one launch (start us, length us, event | category | flops | bytes accessed | tf_op | source)
XLA Modules:
  0.0 56.3 jit_solution(17484061309210091878)
XLA Ops:
  0.6 0.9 %bitcast_convert_fusion = bf16[400,128]{1,0:T(8,128)(2,1)S(1)} fusion(f32[128,400]{0,1:T(8,128)} %param.12), kind=kLoop, calls=%fused_computation.2 | loop fusion | flops 51200 | bytes 307200 | tf_op jit(solution)/shard_map/convert_element_type | solution.py:337
  1.6 0.5 collective-permute-start
  2.1 3.8 %collective-permute-start.4 = (bf16[400,128]{1,0:T(8,128)(2,1)S(1)}, bf16[400,128]{1,0:T(8,128)(2,1)S(1)}, u32[]{:S(2)}, u32[]{:S(2)}) collective-permute-start(bf16[400,128]{1,0:T(8,128)(2,1)S(1)} %bitcast_convert_fusion), channel_id=1, source_target_pairs={{0,9},{1,10},{2,11},{3,8},{4,13},{5,14},{6,15},{7,12},{8,1},{9,2},... | collective-permute-start | bytes 307208 | tf_op jit(solution)/shard_map/ppermute | solution.py:313
  5.9 2.1 %collective-permute-start.1 = (bf16[400,128]{1,0:T(8,128)(2,1)S(1)}, bf16[400,128]{1,0:T(8,128)(2,1)S(1)}, u32[]{:S(2)}, u32[]{:S(2)}) collective-permute-start(bf16[400,128]{1,0:T(8,128)(2,1)S(1)} %bitcast_convert_fusion), channel_id=1, source_target_pairs={{0,17},{1,18},{2,19},{3,16},{4,21},{5,22},{6,23},{7,20},{8,25},{9,... | collective-permute-start | bytes 307208 | tf_op jit(solution)/shard_map/ppermute | solution.py:313
  8.0 0.9 %copy-done.1 = f32[128,400]{0,1:T(8,128)S(1)} copy-done((f32[128,400]{0,1:T(8,128)S(1)}, f32[128,400]{0,1:T(8,128)}, u32[]{:S(2)}) %copy-start.1) | copy-done | bytes 204824
  8.9 0.3 shard_map.145.refs_0_
  9.2 2.0 %collective-permute-start.3 = (bf16[400,128]{1,0:T(8,128)(2,1)S(1)}, bf16[400,128]{1,0:T(8,128)(2,1)S(1)}, u32[]{:S(2)}, u32[]{:S(2)}) collective-permute-start(bf16[400,128]{1,0:T(8,128)(2,1)S(1)} %shard_map.145.refs_0_), channel_id=1, source_target_pairs={{0,2},{1,3},{2,0},{3,1},{4,6},{5,7},{6,4},{7,5},{8,10},{9,11},{10,... | collective-permute-start | bytes 307208 | tf_op jit(solution)/shard_map/ppermute | solution.py:306
  11.2 0.8 %pad_add_fusion.refs_0_ = s32[5,1024]{1,0:T(8,128)S(1)} fusion(s32[2,1024]{1,0:T(2,128)} %bitcast.27, s32[1,1024]{1,0:T(1,128)} %bitcast.28, s32[1,1024]{1,0:T(1,128)} %bitcast.29, s32[1,1024]{1,0:T(1,128)} %bitcast.30), kind=kLoop, calls=%fused_computation | loop fusion | flops 15360 | bytes 40960 | tf_op jit(solution)/shard_map/concatenate | solution.py:348
  11.9 0.1 pad_add_fusion.1.refs_2_
  12.1 1.6 %collective-permute-start.7 = (bf16[400,256]{1,0:T(8,128)(2,1)S(1)}, bf16[400,256]{1,0:T(8,128)(2,1)S(1)}, u32[]{:S(2)}, u32[]{:S(2)}) collective-permute-start(bf16[400,256]{1,0:T(8,128)(2,1)S(1)} %shard_map.146.refs_3_), channel_id=1, source_target_pairs={{0,4},{4,0},{8,12},{12,8},{16,20},{20,16},{24,28},{28,24},{1,5},{5... | collective-permute-start | bytes 614408 | tf_op jit(solution)/shard_map/ppermute | solution.py:303
  13.6 1.6 %shard_map.147 = (f32[2,1024,128]{2,1,0:T(8,128)S(1)}, bf16[400,256]{1,0:T(8,128)(2,1)S(1)}, s32[5,1024]{1,0:T(8,128)S(1)}) custom-call(s32[5,1024]{1,0:T(8,128)S(1)} %pad_add_fusion.refs_0_, f32[400,256]{1,0:T(8,128)S(1)} %bitcast.19, s32[2]{0:T(128)S(1)} %pad_add_fusion.1.refs_2_, bf16[400,256]{1,0:T(8,128)(2,1)S(1)} %shard_map.146.refs_3_), custom_call_target="tpu_custom_call" | custom-call | tf_op jit(solution)/shard_map/pallas_call | solution.py:56
  15.2 0.6 collective-permute-done.3.refs_1_
  15.8 0.1 collective-permute-start.6
  15.9 1.3 %collective-permute-done.1.refs_1_.refs_2_ = bf16[400,128]{1,0:T(8,128)(2,1)S(1)} collective-permute-done((bf16[400,128]{1,0:T(8,128)(2,1)S(1)}, bf16[400,128]{1,0:T(8,128)(2,1)S(1)}, u32[]{:S(2)}, u32[]{:S(2)}) %collective-permute-start.1) | collective-permute-done | bytes 102432 | tf_op jit(solution)/shard_map/ppermute | solution.py:313
  17.2 1.6 %collective-permute-start.5 = (bf16[400,256]{1,0:T(8,128)(2,1)S(1)}, bf16[400,256]{1,0:T(8,128)(2,1)S(1)}, u32[]{:S(2)}, u32[]{:S(2)}) collective-permute-start(bf16[400,256]{1,0:T(8,128)(2,1)S(1)} %shard_map.149.refs_2_), channel_id=1, source_target_pairs={{0,4},{4,0},{8,12},{12,8},{16,20},{20,16},{24,28},{28,24},{1,5},{5... | collective-permute-start | bytes 614408 | tf_op jit(solution)/shard_map/ppermute | solution.py:303
  18.8 0.2 collective-permute-done.7.refs_0_
  19.0 0.9 %shard_map.150 = (bf16[400,1024]{1,0:T(8,128)(2,1)S(1)}, bf16[400,1024]{1,0:T(8,128)(2,1)S(1)}, bf16[400,1024]{1,0:T(8,128)(2,1)S(1)}) custom-call(bf16[400,128]{1,0:T(8,128)(2,1)S(1)} %shard_map.145.refs_0_, bf16[400,128]{1,0:T(8,128)(2,1)S(1)} %collective-permute-done.3.refs_1_, bf16[400,256]{1,0:T(8,128)(2,1)S(1)} %collective-permute-done.6.refs_2_, ...), custom_call_target="tpu_custom_call" | custom-call | flops 6000000000 | tf_op jit(solution)/shard_map/pallas_call | solution.py:56
  20.0 1.8 %shard_map.152 = (f32[400,512]{1,0:T(8,128)S(1)}, f32[400,1024]{1,0:T(8,128)S(1)}) custom-call(bf16[400,128]{1,0:T(8,128)(2,1)S(1)} %collective-permute-done.refs_0_, bf16[400,128]{1,0:T(8,128)(2,1)S(1)} %collective-permute-done.4.refs_1_, bf16[400,128]{1,0:T(8,128)(2,1)S(1)} %collective-permute-done.1.refs_1_.refs_2_, ...), custom_call_target="tpu_custom_call" | custom-call | tf_op jit(solution)/shard_map/pallas_call | solution.py:56
  21.8 1.1 %shard_map.153 = (bf16[400,256]{1,0:T(8,128)(2,1)S(1)}, f32[400,1024]{1,0:T(8,128)S(1)}) custom-call(bf16[400,256]{1,0:T(8,128)(2,1)S(1)} %shard_map.151.rows_ref, bf16[400,1024]{1,0:T(8,128)(2,1)S(1)} %get-tuple-element.39.refs_4_.q_ref.refs_1_, f32[2,1024,128]{2,1,0:T(8,128)S(1)} %get-tuple-element.36.refs_2_.refs_5_.weight_ref, ...), custom_call_target="tpu_custom_call" | custom-call | tf_op jit(solution)/shard_map/pallas_call | solution.py:56
  22.9 0.9 %collective-permute-done.5.rows_ref = bf16[400,256]{1,0:T(8,128)(2,1)S(1)} collective-permute-done((bf16[400,256]{1,0:T(8,128)(2,1)S(1)}, bf16[400,256]{1,0:T(8,128)(2,1)S(1)}, u32[]{:S(2)}, u32[]{:S(2)}) %collective-permute-start.5) | collective-permute-done | bytes 204832 | tf_op jit(solution)/shard_map/ppermute | solution.py:303
  23.8 1.5 %shard_map.154 = (bf16[256,1024]{1,0:T(8,128)(2,1)S(1)}, f32[400,1024]{1,0:T(8,128)S(1)}, f32[416,128]{1,0:T(8,128)S(1)}, bf16[416,128]{1,0:T(8,128)(2,1)S(1)}) custom-call(bf16[400,256]{1,0:T(8,128)(2,1)S(1)} %collective-permute-done.5.rows_ref, bf16[400,1024]{1,0:T(8,128)(2,1)S(1)} %get-tuple-element.39.refs_4_.q_ref.refs_1_, ...), custom_call_target="tpu_custom_call" | custom-call | tf_op jit(solution)/shard_map/pallas_call | solution.py:56
  25.3 0.1 collective-permute-start.14
  25.5 0.5 collective-permute-start.8
  26.0 0.7 %collective-permute-done.14.got_ref = bf16[416,128]{1,0:T(8,128)(2,1)S(1)} collective-permute-done((bf16[416,128]{1,0:T(8,128)(2,1)S(1)}, bf16[416,128]{1,0:T(8,128)(2,1)S(1)}, u32[]{:S(2)}, u32[]{:S(2)}) %collective-permute-start.14) | collective-permute-done | bytes 106528 | tf_op jit(solution)/shard_map/ppermute | solution.py:306
  26.7 1.2 %collective-permute-start.15 = (bf16[208,128]{1,0:T(8,128)(2,1)S(1)}, bf16[208,128]{1,0:T(8,128)(2,1)S(1)}, u32[]{:S(2)}, u32[]{:S(2)}) collective-permute-start(bf16[208,128]{1,0:T(8,128)(2,1)S(1)} %get-tuple-element.60), channel_id=1, source_target_pairs={{0,2},{1,3},{2,0},{3,1},{4,6},{5,7},{6,4},{7,5},{8,10},{9,11},{10,... | collective-permute-start | bytes 159752 | tf_op jit(solution)/shard_map/ppermute | solution.py:306
  28.0 3.1 %collective-permute-done.8.refs_6_.refs_4_.refs_5_ = f32[408,128]{1,0:T(8,128)S(1)} collective-permute-done((f32[408,128]{1,0:T(8,128)S(1)}, f32[408,128]{1,0:T(8,128)S(1)}, u32[]{:S(2)}, u32[]{:S(2)}) %collective-permute-start.8) | collective-permute-done | bytes 208928 | tf_op jit(solution)/shard_map/ppermute | solution.py:313
  31.0 0.9 %shard_map.156 = (bf16[400,256]{1,0:T(8,128)(2,1)S(1)}, bf16[400,256]{1,0:T(8,128)(2,1)S(1)}, f32[400,256]{1,0:T(8,128)S(1)}, bf16[400,256]{1,0:T(8,128)(2,1)S(1)}) custom-call(bf16[256,1024]{1,0:T(8,128)(2,1)S(1)} %get-tuple-element.43.refs_0_, bf16[400,1024]{1,0:T(8,128)(2,1)S(1)} %get-tuple-element.39.refs_4_.q_ref.refs_1_, ...), custom_call_target="tpu_custom_call" | custom-call | tf_op jit(solution)/shard_map/pallas_call | solution.py:56
  32.0 1.6 %collective-permute-start.12 = (bf16[400,256]{1,0:T(8,128)(2,1)S(1)}, bf16[400,256]{1,0:T(8,128)(2,1)S(1)}, u32[]{:S(2)}, u32[]{:S(2)}) collective-permute-start(bf16[400,256]{1,0:T(8,128)(2,1)S(1)} %get-tuple-element.56), channel_id=1, source_target_pairs={{0,4},{4,0},{8,12},{12,8},{16,20},{20,16},{24,28},{28,24},{1,5},{5... | collective-permute-start | bytes 614408 | tf_op jit(solution)/shard_map/ppermute | solution.py:303
  33.6 3.6 %collective-permute-start.16 = (bf16[208,128]{1,0:T(8,128)(2,1)S(1)}, bf16[208,128]{1,0:T(8,128)(2,1)S(1)}, u32[]{:S(2)}, u32[]{:S(2)}) collective-permute-start(bf16[208,128]{1,0:T(8,128)(2,1)S(1)} %shard_map.162.refs_0_), channel_id=1, source_target_pairs={{0,16},{4,20},{8,24},{12,28},{16,0},{20,4},{24,8},{28,12},{1,17},{... | collective-permute-start | bytes 159752 | tf_op jit(solution)/shard_map/ppermute | solution.py:303
  37.2 0.5 collective-permute-start.11
  37.7 1.6 %collective-permute-done.16.refs_1_ = bf16[208,128]{1,0:T(8,128)(2,1)S(1)} collective-permute-done((bf16[208,128]{1,0:T(8,128)(2,1)S(1)}, bf16[208,128]{1,0:T(8,128)(2,1)S(1)}, u32[]{:S(2)}, u32[]{:S(2)}) %collective-permute-start.16) | collective-permute-done | bytes 53280 | tf_op jit(solution)/shard_map/ppermute | solution.py:303
  39.3 1.9 %collective-permute-start.17 = (bf16[208,128]{1,0:T(8,128)(2,1)S(1)}, bf16[208,128]{1,0:T(8,128)(2,1)S(1)}, u32[]{:S(2)}, u32[]{:S(2)}) collective-permute-start(bf16[208,128]{1,0:T(8,128)(2,1)S(1)} %shard_map.163.refs_0_), channel_id=1, source_target_pairs={{0,8},{4,12},{8,0},{12,4},{16,24},{20,28},{24,16},{28,20},{1,9},{5... | collective-permute-start | bytes 159752 | tf_op jit(solution)/shard_map/ppermute | solution.py:303
  41.3 2.1 %collective-permute-start.13 = (bf16[400,128]{1,0:T(8,128)(2,1)S(1)}, bf16[400,128]{1,0:T(8,128)(2,1)S(1)}, u32[]{:S(2)}, u32[]{:S(2)}) collective-permute-start(bf16[400,128]{1,0:T(8,128)(2,1)S(1)} %shard_map.160), channel_id=1, source_target_pairs={{0,16},{4,20},{8,24},{12,28},{16,0},{20,4},{24,8},{28,12},{1,17},{... | collective-permute-start | bytes 307208 | tf_op jit(solution)/shard_map/ppermute | solution.py:303
  43.4 0.1 shard_map.157
  43.4 1.6 %collective-permute-start.10 = (bf16[400,128]{1,0:T(8,128)(2,1)S(1)}, bf16[400,128]{1,0:T(8,128)(2,1)S(1)}, u32[]{:S(2)}, u32[]{:S(2)}) collective-permute-start(bf16[400,128]{1,0:T(8,128)(2,1)S(1)} %get-tuple-element.50), channel_id=1, source_target_pairs={{0,2},{1,3},{2,0},{3,1},{4,6},{5,7},{6,4},{7,5},{8,10},{9,11},{10,... | collective-permute-start | bytes 307208 | tf_op jit(solution)/shard_map/ppermute | solution.py:306
  45.0 1.0 %collective-permute-start.20 = (bf16[208,128]{1,0:T(8,128)(2,1)S(1)}, bf16[208,128]{1,0:T(8,128)(2,1)S(1)}, u32[]{:S(2)}, u32[]{:S(2)}) collective-permute-start(bf16[208,128]{1,0:T(8,128)(2,1)S(1)} %shard_map.164.refs_2_.refs_0_), channel_id=1, source_target_pairs={{0,4},{4,0},{8,12},{12,8},{16,20},{20,16},{24,28},{28,24},{1,5},{5... | collective-permute-start | bytes 159752 | tf_op jit(solution)/shard_map/ppermute | solution.py:303
  46.1 2.1 %collective-permute-start.18 = (bf16[400,128]{1,0:T(8,128)(2,1)S(1)}, bf16[400,128]{1,0:T(8,128)(2,1)S(1)}, u32[]{:S(2)}, u32[]{:S(2)}) collective-permute-start(bf16[400,128]{1,0:T(8,128)(2,1)S(1)} %shard_map.165), channel_id=1, source_target_pairs={{0,24},{4,28},{8,16},{12,20},{16,8},{20,12},{24,0},{28,4},{1,25},{... | collective-permute-start | bytes 307208 | tf_op jit(solution)/shard_map/ppermute | solution.py:303
  48.2 0.2 collective-permute-done.10.refs_1_.refs_2_
  48.4 0.1 shard_map.159
  48.5 0.0 copy-start.2
  48.5 1.2 %collective-permute-start.19 = (bf16[400,128]{1,0:T(8,128)(2,1)S(1)}, bf16[400,128]{1,0:T(8,128)(2,1)S(1)}, u32[]{:S(2)}, u32[]{:S(2)}) collective-permute-start(bf16[400,128]{1,0:T(8,128)(2,1)S(1)} %get-tuple-element.61), channel_id=1, source_target_pairs={{0,8},{4,12},{8,0},{12,4},{16,24},{20,28},{24,16},{28,20},{1,9},{5... | collective-permute-start | bytes 307208 | tf_op jit(solution)/shard_map/ppermute | solution.py:303
  49.8 0.7 %collective-permute-start.21 = (bf16[208,128]{1,0:T(8,128)(2,1)S(1)}, bf16[208,128]{1,0:T(8,128)(2,1)S(1)}, u32[]{:S(2)}, u32[]{:S(2)}) collective-permute-start(bf16[208,128]{1,0:T(8,128)(2,1)S(1)} %shard_map.167.refs_0_), channel_id=1, source_target_pairs={{0,2},{1,3},{2,0},{3,1},{4,6},{5,7},{6,4},{7,5},{8,10},{9,11},{10,... | collective-permute-start | bytes 159752 | tf_op jit(solution)/shard_map/ppermute | solution.py:306
  50.5 0.8 %shard_map.158 = (f32[400,128]{1,0:T(8,128)}, f32[1,128]{1,0:T(1,128)}) custom-call(f32[400,128]{1,0:T(8,128)S(1)} %get-tuple-element.49.refs_0_, bf16[400,128]{1,0:T(8,128)(2,1)S(1)} %collective-permute-done.10.refs_1_.refs_2_, f32[400,128]{1,0:T(8,128)S(1)} %bitcast.22, f32[1,128]{1,0:T(1,128)S(1)} %bitcast.25), custom_call_target="tpu_custom_call" | custom-call | tf_op jit(solution)/shard_map/pallas_call | solution.py:56
  51.3 2.7 %collective-permute-done.21.refs_1_ = bf16[208,128]{1,0:T(8,128)(2,1)S(1)} collective-permute-done((bf16[208,128]{1,0:T(8,128)(2,1)S(1)}, bf16[208,128]{1,0:T(8,128)(2,1)S(1)}, u32[]{:S(2)}, u32[]{:S(2)}) %collective-permute-start.21) | collective-permute-done | bytes 53280 | tf_op jit(solution)/shard_map/ppermute | solution.py:306
  54.0 0.1 collective-permute-start.22
  54.1 0.8 %shard_map.166 = (f32[400,128]{1,0:T(8,128)}, f32[1,128]{1,0:T(1,128)}) custom-call(f32[400,128]{1,0:T(8,128)S(1)} %get-tuple-element.55.refs_0_, bf16[400,128]{1,0:T(8,128)(2,1)S(1)} %collective-permute-done.13.refs_1_, bf16[400,128]{1,0:T(8,128)(2,1)S(1)} %collective-permute-done.18.refs_2_, bf16[400,128]{1,0:T(8,128)(2,1)S(1)} %collective-permute-done.19.refs_3_, ...), custom_call_target="tpu_custom_call" | custom-call | flops 12000000000 | tf_op jit(solution)/shard_map/pallas_call | solution.py:56
  54.9 0.5 collective-permute-done.22.refs_2_
  55.4 0.9 %shard_map.169 = (f32[400,256]{1,0:T(8,128)}, f32[1,256]{1,0:T(1,128)}) custom-call(bf16[208,128]{1,0:T(8,128)(2,1)S(1)} %shard_map.167.refs_0_, bf16[208,128]{1,0:T(8,128)(2,1)S(1)} %collective-permute-done.21.refs_1_, bf16[416,128]{1,0:T(8,128)(2,1)S(1)} %collective-permute-done.22.refs_2_, f32[400,256]{1,0:T(8,128)S(1)} %bitcast.20, ...), custom_call_target="tpu_custom_call" | custom-call | tf_op jit(solution)/shard_map/pallas_call | solution.py:56
  (40 shorter events, 0.4 us)
Async XLA Ops:
  1.6 10.4 %collective-permute-start = (bf16[400,128]{1,0:T(8,128)(2,1)S(1)}, bf16[400,128]{1,0:T(8,128)(2,1)S(1)}, u32[]{:S(2)}, u32[]{:S(2)}) collective-permute-start(bf16[400,128]{1,0:T(8,128)(2,1)S(1)} %bitcast_convert_fusion), channel_id=1, source_target_pairs={{0,1},{1,2},{2,3},{3,0},{4,5},{5,6},{6,7},{7,4},{8,9},{9,10},{10,1... | collective-permute-start | bytes 307208 | tf_op jit(solution)/shard_map/ppermute | solution.py:313
  2.1 9.9 %collective-permute-start.4 = (bf16[400,128]{1,0:T(8,128)(2,1)S(1)}, bf16[400,128]{1,0:T(8,128)(2,1)S(1)}, u32[]{:S(2)}, u32[]{:S(2)}) collective-permute-start(bf16[400,128]{1,0:T(8,128)(2,1)S(1)} %bitcast_convert_fusion), channel_id=1, source_target_pairs={{0,9},{1,10},{2,11},{3,8},{4,13},{5,14},{6,15},{7,12},{8,1},{9,2},... | collective-permute-start | bytes 307208 | tf_op jit(solution)/shard_map/ppermute | solution.py:313
  5.9 11.3 %collective-permute-start.1 = (bf16[400,128]{1,0:T(8,128)(2,1)S(1)}, bf16[400,128]{1,0:T(8,128)(2,1)S(1)}, u32[]{:S(2)}, u32[]{:S(2)}) collective-permute-start(bf16[400,128]{1,0:T(8,128)(2,1)S(1)} %bitcast_convert_fusion), channel_id=1, source_target_pairs={{0,17},{1,18},{2,19},{3,16},{4,21},{5,22},{6,23},{7,20},{8,25},{9,... | collective-permute-start | bytes 307208 | tf_op jit(solution)/shard_map/ppermute | solution.py:313
  8.0 9.2 %collective-permute-start.2 = (bf16[400,128]{1,0:T(8,128)(2,1)S(1)}, bf16[400,128]{1,0:T(8,128)(2,1)S(1)}, u32[]{:S(2)}, u32[]{:S(2)}) collective-permute-start(bf16[400,128]{1,0:T(8,128)(2,1)S(1)} %bitcast_convert_fusion), channel_id=1, source_target_pairs={{0,25},{1,26},{2,27},{3,24},{4,29},{5,30},{6,31},{7,28},{8,17},{9,... | collective-permute-start | bytes 307208 | tf_op jit(solution)/shard_map/ppermute | solution.py:313
  8.0 0.9 %copy-start.1 = (f32[128,400]{0,1:T(8,128)S(1)}, f32[128,400]{0,1:T(8,128)}, u32[]{:S(2)}) copy-start(f32[128,400]{0,1:T(8,128)} %param.10) | copy-start | bytes 614404
  9.2 6.6 %collective-permute-start.3 = (bf16[400,128]{1,0:T(8,128)(2,1)S(1)}, bf16[400,128]{1,0:T(8,128)(2,1)S(1)}, u32[]{:S(2)}, u32[]{:S(2)}) collective-permute-start(bf16[400,128]{1,0:T(8,128)(2,1)S(1)} %shard_map.145.refs_0_), channel_id=1, source_target_pairs={{0,2},{1,3},{2,0},{3,1},{4,6},{5,7},{6,4},{7,5},{8,10},{9,11},{10,... | collective-permute-start | bytes 307208 | tf_op jit(solution)/shard_map/ppermute | solution.py:306
  12.0 1.6 %copy-start = (f32[256,400]{0,1:T(8,128)S(1)}, f32[256,400]{0,1:T(8,128)}, u32[]{:S(2)}) copy-start(f32[256,400]{0,1:T(8,128)} %param.14) | copy-start | bytes 1228804
  12.1 6.9 %collective-permute-start.7 = (bf16[400,256]{1,0:T(8,128)(2,1)S(1)}, bf16[400,256]{1,0:T(8,128)(2,1)S(1)}, u32[]{:S(2)}, u32[]{:S(2)}) collective-permute-start(bf16[400,256]{1,0:T(8,128)(2,1)S(1)} %shard_map.146.refs_3_), channel_id=1, source_target_pairs={{0,4},{4,0},{8,12},{12,8},{16,20},{20,16},{24,28},{28,24},{1,5},{5... | collective-permute-start | bytes 614408 | tf_op jit(solution)/shard_map/ppermute | solution.py:303
  15.8 3.2 %collective-permute-start.6 = (bf16[400,256]{1,0:T(8,128)(2,1)S(1)}, bf16[400,256]{1,0:T(8,128)(2,1)S(1)}, u32[]{:S(2)}, u32[]{:S(2)}) collective-permute-start(bf16[400,256]{1,0:T(8,128)(2,1)S(1)} %shard_map.148.refs_3_), channel_id=1, source_target_pairs={{0,1},{1,0},{2,3},{3,2},{4,5},{5,4},{6,7},{7,6},{8,9},{9,8},{10,11... | collective-permute-start | bytes 614408 | tf_op jit(solution)/shard_map/ppermute | solution.py:306
  17.2 6.6 %collective-permute-start.5 = (bf16[400,256]{1,0:T(8,128)(2,1)S(1)}, bf16[400,256]{1,0:T(8,128)(2,1)S(1)}, u32[]{:S(2)}, u32[]{:S(2)}) collective-permute-start(bf16[400,256]{1,0:T(8,128)(2,1)S(1)} %shard_map.149.refs_2_), channel_id=1, source_target_pairs={{0,4},{4,0},{8,12},{12,8},{16,20},{20,16},{24,28},{28,24},{1,5},{5... | collective-permute-start | bytes 614408 | tf_op jit(solution)/shard_map/ppermute | solution.py:303
  23.8 1.6 %copy-start.3 = (f32[128,400]{0,1:T(8,128)S(1)}, f32[128,400]{0,1:T(8,128)}, u32[]{:S(2)}) copy-start(f32[128,400]{0,1:T(8,128)} %param.12) | copy-start | bytes 614404
  23.8 1.6 %copy-start.6 = (f32[128]{0:T(128)S(1)}, f32[128]{0:T(128)}, u32[]{:S(2)}) copy-start(f32[128]{0:T(128)} %param.13) | copy-start | bytes 1540
  25.3 1.4 %collective-permute-start.14 = (bf16[416,128]{1,0:T(8,128)(2,1)S(1)}, bf16[416,128]{1,0:T(8,128)(2,1)S(1)}, u32[]{:S(2)}, u32[]{:S(2)}) collective-permute-start(bf16[416,128]{1,0:T(8,128)(2,1)S(1)} %get-tuple-element.58), channel_id=1, source_target_pairs={{0,1},{1,0},{2,3},{3,2},{4,5},{5,4},{6,7},{7,6},{8,9},{9,8},{10,11... | collective-permute-start | bytes 319496 | tf_op jit(solution)/shard_map/ppermute | solution.py:306
  25.5 5.6 %collective-permute-start.8 = (f32[408,128]{1,0:T(8,128)S(1)}, f32[408,128]{1,0:T(8,128)S(1)}, u32[]{:S(2)}, u32[]{:S(2)}) collective-permute-start(f32[408,128]{1,0:T(8,128)S(1)} %shard_map.155), channel_id=1, source_target_pairs={{0,1},{1,2},{2,3},{3,0},{4,5},{5,6},{6,7},{7,4},{8,9},{9,10},{10,1... | collective-permute-start | bytes 626696 | tf_op jit(solution)/shard_map/ppermute | solution.py:313
  26.7 6.8 %collective-permute-start.15 = (bf16[208,128]{1,0:T(8,128)(2,1)S(1)}, bf16[208,128]{1,0:T(8,128)(2,1)S(1)}, u32[]{:S(2)}, u32[]{:S(2)}) collective-permute-start(bf16[208,128]{1,0:T(8,128)(2,1)S(1)} %get-tuple-element.60), channel_id=1, source_target_pairs={{0,2},{1,3},{2,0},{3,1},{4,6},{5,7},{6,4},{7,5},{8,10},{9,11},{10,... | collective-permute-start | bytes 159752 | tf_op jit(solution)/shard_map/ppermute | solution.py:306
  32.0 9.3 %collective-permute-start.12 = (bf16[400,256]{1,0:T(8,128)(2,1)S(1)}, bf16[400,256]{1,0:T(8,128)(2,1)S(1)}, u32[]{:S(2)}, u32[]{:S(2)}) collective-permute-start(bf16[400,256]{1,0:T(8,128)(2,1)S(1)} %get-tuple-element.56), channel_id=1, source_target_pairs={{0,4},{4,0},{8,12},{12,8},{16,20},{20,16},{24,28},{28,24},{1,5},{5... | collective-permute-start | bytes 614408 | tf_op jit(solution)/shard_map/ppermute | solution.py:303
  33.6 5.7 %collective-permute-start.16 = (bf16[208,128]{1,0:T(8,128)(2,1)S(1)}, bf16[208,128]{1,0:T(8,128)(2,1)S(1)}, u32[]{:S(2)}, u32[]{:S(2)}) collective-permute-start(bf16[208,128]{1,0:T(8,128)(2,1)S(1)} %shard_map.162.refs_0_), channel_id=1, source_target_pairs={{0,16},{4,20},{8,24},{12,28},{16,0},{20,4},{24,8},{28,12},{1,17},{... | collective-permute-start | bytes 159752 | tf_op jit(solution)/shard_map/ppermute | solution.py:303
  37.2 6.2 %collective-permute-start.9 = (bf16[400,256]{1,0:T(8,128)(2,1)S(1)}, bf16[400,256]{1,0:T(8,128)(2,1)S(1)}, u32[]{:S(2)}, u32[]{:S(2)}) collective-permute-start(bf16[400,256]{1,0:T(8,128)(2,1)S(1)} %get-tuple-element.48), channel_id=1, source_target_pairs={{0,1},{1,0},{2,3},{3,2},{4,5},{5,4},{6,7},{7,6},{8,9},{9,8},{10,11... | collective-permute-start | bytes 614408 | tf_op jit(solution)/shard_map/ppermute | solution.py:306
  37.2 11.0 %collective-permute-start.11 = (bf16[400,256]{1,0:T(8,128)(2,1)S(1)}, bf16[400,256]{1,0:T(8,128)(2,1)S(1)}, u32[]{:S(2)}, u32[]{:S(2)}) collective-permute-start(bf16[400,256]{1,0:T(8,128)(2,1)S(1)} %get-tuple-element.54), channel_id=1, source_target_pairs={{0,4},{4,0},{8,12},{12,8},{16,20},{20,16},{24,28},{28,24},{1,5},{5... | collective-permute-start | bytes 614408 | tf_op jit(solution)/shard_map/ppermute | solution.py:303
  39.3 5.7 %collective-permute-start.17 = (bf16[208,128]{1,0:T(8,128)(2,1)S(1)}, bf16[208,128]{1,0:T(8,128)(2,1)S(1)}, u32[]{:S(2)}, u32[]{:S(2)}) collective-permute-start(bf16[208,128]{1,0:T(8,128)(2,1)S(1)} %shard_map.163.refs_0_), channel_id=1, source_target_pairs={{0,8},{4,12},{8,0},{12,4},{16,24},{20,28},{24,16},{28,20},{1,9},{5... | collective-permute-start | bytes 159752 | tf_op jit(solution)/shard_map/ppermute | solution.py:303
  41.3 12.8 %collective-permute-start.13 = (bf16[400,128]{1,0:T(8,128)(2,1)S(1)}, bf16[400,128]{1,0:T(8,128)(2,1)S(1)}, u32[]{:S(2)}, u32[]{:S(2)}) collective-permute-start(bf16[400,128]{1,0:T(8,128)(2,1)S(1)} %shard_map.160), channel_id=1, source_target_pairs={{0,16},{4,20},{8,24},{12,28},{16,0},{20,4},{24,8},{28,12},{1,17},{... | collective-permute-start | bytes 307208 | tf_op jit(solution)/shard_map/ppermute | solution.py:303
  43.4 5.0 %collective-permute-start.10 = (bf16[400,128]{1,0:T(8,128)(2,1)S(1)}, bf16[400,128]{1,0:T(8,128)(2,1)S(1)}, u32[]{:S(2)}, u32[]{:S(2)}) collective-permute-start(bf16[400,128]{1,0:T(8,128)(2,1)S(1)} %get-tuple-element.50), channel_id=1, source_target_pairs={{0,2},{1,3},{2,0},{3,1},{4,6},{5,7},{6,4},{7,5},{8,10},{9,11},{10,... | collective-permute-start | bytes 307208 | tf_op jit(solution)/shard_map/ppermute | solution.py:306
  45.0 4.7 %collective-permute-start.20 = (bf16[208,128]{1,0:T(8,128)(2,1)S(1)}, bf16[208,128]{1,0:T(8,128)(2,1)S(1)}, u32[]{:S(2)}, u32[]{:S(2)}) collective-permute-start(bf16[208,128]{1,0:T(8,128)(2,1)S(1)} %shard_map.164.refs_2_.refs_0_), channel_id=1, source_target_pairs={{0,4},{4,0},{8,12},{12,8},{16,20},{20,16},{24,28},{28,24},{1,5},{5... | collective-permute-start | bytes 159752 | tf_op jit(solution)/shard_map/ppermute | solution.py:303
  46.1 8.0 %collective-permute-start.18 = (bf16[400,128]{1,0:T(8,128)(2,1)S(1)}, bf16[400,128]{1,0:T(8,128)(2,1)S(1)}, u32[]{:S(2)}, u32[]{:S(2)}) collective-permute-start(bf16[400,128]{1,0:T(8,128)(2,1)S(1)} %shard_map.165), channel_id=1, source_target_pairs={{0,24},{4,28},{8,16},{12,20},{16,8},{20,12},{24,0},{28,4},{1,25},{... | collective-permute-start | bytes 307208 | tf_op jit(solution)/shard_map/ppermute | solution.py:303
  48.5 2.0 %copy-start.2 = (f32[128,400]{0,1:T(8,128)S(1)}, f32[128,400]{0,1:T(8,128)}, u32[]{:S(2)}) copy-start(f32[128,400]{0,1:T(8,128)} %param.10) | copy-start | bytes 614404
  48.5 2.0 %copy-start.5 = (f32[128]{0:T(128)S(1)}, f32[128]{0:T(128)}, u32[]{:S(2)}) copy-start(f32[128]{0:T(128)} %param.11) | copy-start | bytes 1540
  48.5 5.6 %collective-permute-start.19 = (bf16[400,128]{1,0:T(8,128)(2,1)S(1)}, bf16[400,128]{1,0:T(8,128)(2,1)S(1)}, u32[]{:S(2)}, u32[]{:S(2)}) collective-permute-start(bf16[400,128]{1,0:T(8,128)(2,1)S(1)} %get-tuple-element.61), channel_id=1, source_target_pairs={{0,8},{4,12},{8,0},{12,4},{16,24},{20,28},{24,16},{28,20},{1,9},{5... | collective-permute-start | bytes 307208 | tf_op jit(solution)/shard_map/ppermute | solution.py:303
  49.8 4.2 %collective-permute-start.21 = (bf16[208,128]{1,0:T(8,128)(2,1)S(1)}, bf16[208,128]{1,0:T(8,128)(2,1)S(1)}, u32[]{:S(2)}, u32[]{:S(2)}) collective-permute-start(bf16[208,128]{1,0:T(8,128)(2,1)S(1)} %shard_map.167.refs_0_), channel_id=1, source_target_pairs={{0,2},{1,3},{2,0},{3,1},{4,6},{5,7},{6,4},{7,5},{8,10},{9,11},{10,... | collective-permute-start | bytes 159752 | tf_op jit(solution)/shard_map/ppermute | solution.py:306
  54.0 1.4 %collective-permute-start.22 = (bf16[416,128]{1,0:T(8,128)(2,1)S(1)}, bf16[416,128]{1,0:T(8,128)(2,1)S(1)}, u32[]{:S(2)}, u32[]{:S(2)}) collective-permute-start(bf16[416,128]{1,0:T(8,128)(2,1)S(1)} %shard_map.168), channel_id=1, source_target_pairs={{0,1},{1,0},{2,3},{3,2},{4,5},{5,4},{6,7},{7,6},{8,9},{9,8},{10,11... | collective-permute-start | bytes 319496 | tf_op jit(solution)/shard_map/ppermute | solution.py:306
  54.1 1.3 %copy-start.4 = (f32[256]{0:T(256)S(1)}, f32[256]{0:T(256)}, u32[]{:S(2)}) copy-start(f32[256]{0:T(256)} %param.15) | copy-start | bytes 3076

commit v20 on v19

--- a/solution.py
+++ b/solution.py
@@ -382,6 +382,7 @@
              shape(far_right * size, LANES, dtype=BF)),
             [pltpu.VMEM((width, nrel), F32), all_pieces],
             me,
+            after=(moved,),
         )(other_high, q, weight, ids, qg, s)
         left_rows = n_right * rows
         left_half = left_rows // 2
@@ -389,7 +390,6 @@
             rest_body,
             (chunk, chunk, shape(width, left_half), shape(width, left_half, dtype=BF)),
             [pltpu.VMEM((width, left_rows), F32)],
-            after=(moved,),
         )(m, q, g, o, ids, right_low)
 
         mine, *rest = call(

time: 56.5 us -> 52.7 us (0.933)
  starting transfers between devices: 29.9 us -> 26.2 us
    ppermute x10, starting transfers between devices: 17.3 us -> 14.7 us  [swap_left(): return lax.ppermute(value, 'left', [(i, i ^ by) for i in range(n_left)])]
    ppermute x10, waiting for transfers between devices: 2.74 us -> 3.75 us  [swap_left(): return lax.ppermute(value, 'left', [(i, i ^ by) for i in range(n_left)])]
    ppermute x8, waiting for transfers between devices: 4.66 us -> 3.93 us  [swap_right(): return lax.ppermute(value, 'right', [(i, i ^ by) for i in range(n_right)])]
  transfers between devices with their start and end apart: 23 -> 23, of which waited for: 10 -> 9; matrix products, arithmetic and copies ran while one was open for 1% -> 2% of each run, Pallas kernels for 15% -> 16%
where the time goes in v20:
time: 52.7 us; the launch traced here: 52.4 us
  starting transfers between devices  26.2 us (50%)
  waiting for transfers between devices  11.7 us (22%)
  Pallas kernels  10.9 us (21%)
  other arithmetic  1.78 us (3%)
  local copies, waits for them, and re-layouts  0.96 us (2%)
  between operations  0.88 us (2%)
    ppermute x10, starting transfers between devices, swap_left(): return lax.ppermute(value, 'left', [(i, i ^ by) for i in range(n_left)])  14.7 us
    pallas_call x25, Pallas kernels, run(): pl.pallas_call(inner, out_shape=out_shape, in_specs=specs, scratch_shapes...  10.9 us
    ppermute x5, starting transfers between devices, next_column(): return lax.ppermute(value, ('left', 'right'), perm)  6.37 us
    ppermute x8, starting transfers between devices, swap_right(): return lax.ppermute(value, 'right', [(i, i ^ by) for i in range(n_right)])  5.18 us
    ppermute x5, waiting for transfers between devices, next_column(): return lax.ppermute(value, ('left', 'right'), perm)  4 us
    ppermute x8, waiting for transfers between devices, swap_right(): return lax.ppermute(value, 'right', [(i, i ^ by) for i in range(n_right)])  3.93 us
    ppermute x10, waiting for transfers between devices, swap_left(): return lax.ppermute(value, 'left', [(i, i ^ by) for i in range(n_left)])  3.75 us
  transfers between devices with their start and end apart: 23, of which 9 were waited for; matrix products, arithmetic and copies ran while one was open for 2% of the time, Pallas kernels for 16%

profile of v20, /device:TPU:0, one launch (start us, length us, event | category | flops | bytes accessed | tf_op | source)
XLA Modules:
  0.0 52.4 jit_solution(18379453279282305298)
XLA Ops:
  0.6 0.9 %bitcast_convert_fusion = bf16[400,128]{1,0:T(8,128)(2,1)S(1)} fusion(f32[128,400]{0,1:T(8,128)} %param.12), kind=kLoop, calls=%fused_computation.2 | loop fusion | flops 51200 | bytes 307200 | tf_op jit(solution)/shard_map/convert_element_type | solution.py:337
  1.6 2.5 %collective-permute-start.4 = (bf16[400,128]{1,0:T(8,128)(2,1)S(1)}, bf16[400,128]{1,0:T(8,128)(2,1)S(1)}, u32[]{:S(2)}, u32[]{:S(2)}) collective-permute-start(bf16[400,128]{1,0:T(8,128)(2,1)S(1)} %bitcast_convert_fusion), channel_id=1, source_target_pairs={{0,9},{1,10},{2,11},{3,8},{4,13},{5,14},{6,15},{7,12},{8,1},{9,2},... | collective-permute-start | bytes 307208 | tf_op jit(solution)/shard_map/ppermute | solution.py:313
  4.1 3.7 %collective-permute-start.2 = (bf16[400,128]{1,0:T(8,128)(2,1)S(1)}, bf16[400,128]{1,0:T(8,128)(2,1)S(1)}, u32[]{:S(2)}, u32[]{:S(2)}) collective-permute-start(bf16[400,128]{1,0:T(8,128)(2,1)S(1)} %bitcast_convert_fusion), channel_id=1, source_target_pairs={{0,25},{1,26},{2,27},{3,24},{4,29},{5,30},{6,31},{7,28},{8,17},{9,... | collective-permute-start | bytes 307208 | tf_op jit(solution)/shard_map/ppermute | solution.py:313
  7.8 0.1 collective-permute-start.1
  7.9 0.9 %copy-done.1 = f32[128,400]{0,1:T(8,128)S(1)} copy-done((f32[128,400]{0,1:T(8,128)S(1)}, f32[128,400]{0,1:T(8,128)}, u32[]{:S(2)}) %copy-start.1) | copy-done | bytes 204824
  8.8 0.3 shard_map.145.refs_0_
  9.1 1.0 %collective-permute-start.3 = (bf16[400,128]{1,0:T(8,128)(2,1)S(1)}, bf16[400,128]{1,0:T(8,128)(2,1)S(1)}, u32[]{:S(2)}, u32[]{:S(2)}) collective-permute-start(bf16[400,128]{1,0:T(8,128)(2,1)S(1)} %shard_map.145.refs_0_), channel_id=1, source_target_pairs={{0,2},{1,3},{2,0},{3,1},{4,6},{5,7},{6,4},{7,5},{8,10},{9,11},{10,... | collective-permute-start | bytes 307208 | tf_op jit(solution)/shard_map/ppermute | solution.py:306
  10.1 0.8 %pad_add_fusion.refs_0_ = s32[5,1024]{1,0:T(8,128)S(1)} fusion(s32[2,1024]{1,0:T(2,128)} %bitcast.27, s32[1,1024]{1,0:T(1,128)} %bitcast.28, s32[1,1024]{1,0:T(1,128)} %bitcast.29, s32[1,1024]{1,0:T(1,128)} %bitcast.30), kind=kLoop, calls=%fused_computation | loop fusion | flops 15360 | bytes 40960 | tf_op jit(solution)/shard_map/concatenate | solution.py:348
  10.9 0.1 pad_add_fusion.1.refs_2_
  10.9 1.9 %collective-permute-done.refs_0_ = bf16[400,128]{1,0:T(8,128)(2,1)S(1)} collective-permute-done((bf16[400,128]{1,0:T(8,128)(2,1)S(1)}, bf16[400,128]{1,0:T(8,128)(2,1)S(1)}, u32[]{:S(2)}, u32[]{:S(2)}) %collective-permute-start) | collective-permute-done | bytes 102432 | tf_op jit(solution)/shard_map/ppermute | solution.py:313
  12.9 1.6 %collective-permute-start.7 = (bf16[400,256]{1,0:T(8,128)(2,1)S(1)}, bf16[400,256]{1,0:T(8,128)(2,1)S(1)}, u32[]{:S(2)}, u32[]{:S(2)}) collective-permute-start(bf16[400,256]{1,0:T(8,128)(2,1)S(1)} %shard_map.146.refs_3_), channel_id=1, source_target_pairs={{0,4},{4,0},{8,12},{12,8},{16,20},{20,16},{24,28},{28,24},{1,5},{5... | collective-permute-start | bytes 614408 | tf_op jit(solution)/shard_map/ppermute | solution.py:303
  14.5 1.6 %shard_map.147 = (f32[2,1024,128]{2,1,0:T(8,128)S(1)}, bf16[400,256]{1,0:T(8,128)(2,1)S(1)}, s32[5,1024]{1,0:T(8,128)S(1)}) custom-call(s32[5,1024]{1,0:T(8,128)S(1)} %pad_add_fusion.refs_0_, f32[400,256]{1,0:T(8,128)S(1)} %bitcast.19, s32[2]{0:T(128)S(1)} %pad_add_fusion.1.refs_2_, bf16[400,256]{1,0:T(8,128)(2,1)S(1)} %shard_map.146.refs_3_), custom_call_target="tpu_custom_call" | custom-call | tf_op jit(solution)/shard_map/pallas_call | solution.py:56
  16.1 0.0 copy-start.3
  16.1 0.0 copy-start.6
  16.1 0.1 collective-permute-start.6
  16.2 1.7 %collective-permute-done.1.refs_1_.refs_2_ = bf16[400,128]{1,0:T(8,128)(2,1)S(1)} collective-permute-done((bf16[400,128]{1,0:T(8,128)(2,1)S(1)}, bf16[400,128]{1,0:T(8,128)(2,1)S(1)}, u32[]{:S(2)}, u32[]{:S(2)}) %collective-permute-start.1) | collective-permute-done | bytes 102432 | tf_op jit(solution)/shard_map/ppermute | solution.py:313
  17.9 1.6 %collective-permute-start.5 = (bf16[400,256]{1,0:T(8,128)(2,1)S(1)}, bf16[400,256]{1,0:T(8,128)(2,1)S(1)}, u32[]{:S(2)}, u32[]{:S(2)}) collective-permute-start(bf16[400,256]{1,0:T(8,128)(2,1)S(1)} %shard_map.149.refs_2_), channel_id=1, source_target_pairs={{0,4},{4,0},{8,12},{12,8},{16,20},{20,16},{24,28},{28,24},{1,5},{5... | collective-permute-start | bytes 614408 | tf_op jit(solution)/shard_map/ppermute | solution.py:303
  19.5 0.1 collective-permute-start.8
  19.6 0.9 %shard_map.150 = (bf16[400,1024]{1,0:T(8,128)(2,1)S(1)}, bf16[400,1024]{1,0:T(8,128)(2,1)S(1)}, bf16[400,1024]{1,0:T(8,128)(2,1)S(1)}) custom-call(bf16[400,128]{1,0:T(8,128)(2,1)S(1)} %shard_map.145.refs_0_, bf16[400,128]{1,0:T(8,128)(2,1)S(1)} %collective-permute-done.3.refs_1_, bf16[400,256]{1,0:T(8,128)(2,1)S(1)} %collective-permute-done.6.refs_2_, ...), custom_call_target="tpu_custom_call" | custom-call | flops 6000000000 | tf_op jit(solution)/shard_map/pallas_call | solution.py:56
  20.6 1.8 %shard_map.152 = (f32[400,512]{1,0:T(8,128)S(1)}, f32[400,1024]{1,0:T(8,128)S(1)}) custom-call(bf16[400,128]{1,0:T(8,128)(2,1)S(1)} %collective-permute-done.refs_0_, bf16[400,128]{1,0:T(8,128)(2,1)S(1)} %collective-permute-done.4.refs_1_, bf16[400,128]{1,0:T(8,128)(2,1)S(1)} %collective-permute-done.1.refs_1_.refs_2_, ...), custom_call_target="tpu_custom_call" | custom-call | tf_op jit(solution)/shard_map/pallas_call | solution.py:56
  22.4 1.0 %shard_map.153 = (bf16[400,256]{1,0:T(8,128)(2,1)S(1)}, f32[400,1024]{1,0:T(8,128)S(1)}) custom-call(bf16[400,256]{1,0:T(8,128)(2,1)S(1)} %shard_map.151.rows_ref, bf16[400,1024]{1,0:T(8,128)(2,1)S(1)} %get-tuple-element.39.refs_4_.q_ref.refs_1_, f32[2,1024,128]{2,1,0:T(8,128)S(1)} %get-tuple-element.36.refs_2_.refs_5_.weight_ref, ...), custom_call_target="tpu_custom_call" | custom-call | tf_op jit(solution)/shard_map/pallas_call | solution.py:56
  23.4 1.0 %collective-permute-done.5.refs_0_ = bf16[400,256]{1,0:T(8,128)(2,1)S(1)} collective-permute-done((bf16[400,256]{1,0:T(8,128)(2,1)S(1)}, bf16[400,256]{1,0:T(8,128)(2,1)S(1)}, u32[]{:S(2)}, u32[]{:S(2)}) %collective-permute-start.5) | collective-permute-done | bytes 204832 | tf_op jit(solution)/shard_map/ppermute | solution.py:303
  24.4 0.4 collective-permute-done.8.refs_7_.refs_4_.refs_5_
  24.8 1.5 %shard_map.155 = (bf16[256,1024]{1,0:T(8,128)(2,1)S(1)}, f32[400,1024]{1,0:T(8,128)S(1)}, f32[416,128]{1,0:T(8,128)S(1)}, bf16[416,128]{1,0:T(8,128)(2,1)S(1)}) custom-call(bf16[400,256]{1,0:T(8,128)(2,1)S(1)} %collective-permute-done.5.refs_0_, bf16[400,1024]{1,0:T(8,128)(2,1)S(1)} %get-tuple-element.39.refs_4_.q_ref.refs_1_, ...), custom_call_target="tpu_custom_call" | custom-call | tf_op jit(solution)/shard_map/pallas_call | solution.py:56
  26.3 0.1 collective-permute-start.14
  26.4 0.9 %shard_map.156 = (bf16[400,256]{1,0:T(8,128)(2,1)S(1)}, bf16[400,256]{1,0:T(8,128)(2,1)S(1)}, f32[400,256]{1,0:T(8,128)S(1)}, bf16[400,256]{1,0:T(8,128)(2,1)S(1)}) custom-call(bf16[256,1024]{1,0:T(8,128)(2,1)S(1)} %get-tuple-element.43.m_ref, bf16[400,1024]{1,0:T(8,128)(2,1)S(1)} %get-tuple-element.39.refs_4_.q_ref.refs_1_, ...), custom_call_target="tpu_custom_call" | custom-call | tf_op jit(solution)/shard_map/pallas_call | solution.py:56
  27.3 0.6 %collective-permute-start.9 = (bf16[400,256]{1,0:T(8,128)(2,1)S(1)}, bf16[400,256]{1,0:T(8,128)(2,1)S(1)}, u32[]{:S(2)}, u32[]{:S(2)}) collective-permute-start(bf16[400,256]{1,0:T(8,128)(2,1)S(1)} %get-tuple-element.48), channel_id=1, source_target_pairs={{0,1},{1,0},{2,3},{3,2},{4,5},{5,4},{6,7},{7,6},{8,9},{9,8},{10,11... | collective-permute-start | bytes 614408 | tf_op jit(solution)/shard_map/ppermute | solution.py:306
  27.9 1.2 %collective-permute-start.15 = (bf16[208,128]{1,0:T(8,128)(2,1)S(1)}, bf16[208,128]{1,0:T(8,128)(2,1)S(1)}, u32[]{:S(2)}, u32[]{:S(2)}) collective-permute-start(bf16[208,128]{1,0:T(8,128)(2,1)S(1)} %get-tuple-element.60), channel_id=1, source_target_pairs={{0,2},{1,3},{2,0},{3,1},{4,6},{5,7},{6,4},{7,5},{8,10},{9,11},{10,... | collective-permute-start | bytes 159752 | tf_op jit(solution)/shard_map/ppermute | solution.py:306
  29.1 1.2 %collective-permute-start.12 = (bf16[400,256]{1,0:T(8,128)(2,1)S(1)}, bf16[400,256]{1,0:T(8,128)(2,1)S(1)}, u32[]{:S(2)}, u32[]{:S(2)}) collective-permute-start(bf16[400,256]{1,0:T(8,128)(2,1)S(1)} %get-tuple-element.56), channel_id=1, source_target_pairs={{0,4},{4,0},{8,12},{12,8},{16,20},{20,16},{24,28},{28,24},{1,5},{5... | collective-permute-start | bytes 614408 | tf_op jit(solution)/shard_map/ppermute | solution.py:303
  30.3 1.8 %collective-permute-done.15.refs_1_ = bf16[208,128]{1,0:T(8,128)(2,1)S(1)} collective-permute-done((bf16[208,128]{1,0:T(8,128)(2,1)S(1)}, bf16[208,128]{1,0:T(8,128)(2,1)S(1)}, u32[]{:S(2)}, u32[]{:S(2)}) %collective-permute-start.15) | collective-permute-done | bytes 53280 | tf_op jit(solution)/shard_map/ppermute | solution.py:306
  32.1 1.7 %collective-permute-start.16 = (bf16[208,128]{1,0:T(8,128)(2,1)S(1)}, bf16[208,128]{1,0:T(8,128)(2,1)S(1)}, u32[]{:S(2)}, u32[]{:S(2)}) collective-permute-start(bf16[208,128]{1,0:T(8,128)(2,1)S(1)} %shard_map.162.refs_0_), channel_id=1, source_target_pairs={{0,16},{4,20},{8,24},{12,28},{16,0},{20,4},{24,8},{28,12},{1,17},{... | collective-permute-start | bytes 159752 | tf_op jit(solution)/shard_map/ppermute | solution.py:303
  33.8 0.9 %collective-permute-start.11 = (bf16[400,256]{1,0:T(8,128)(2,1)S(1)}, bf16[400,256]{1,0:T(8,128)(2,1)S(1)}, u32[]{:S(2)}, u32[]{:S(2)}) collective-permute-start(bf16[400,256]{1,0:T(8,128)(2,1)S(1)} %get-tuple-element.54), channel_id=1, source_target_pairs={{0,4},{4,0},{8,12},{12,8},{16,20},{20,16},{24,28},{28,24},{1,5},{5... | collective-permute-start | bytes 614408 | tf_op jit(solution)/shard_map/ppermute | solution.py:303
  34.8 1.0 %collective-permute-start.10 = (bf16[400,128]{1,0:T(8,128)(2,1)S(1)}, bf16[400,128]{1,0:T(8,128)(2,1)S(1)}, u32[]{:S(2)}, u32[]{:S(2)}) collective-permute-start(bf16[400,128]{1,0:T(8,128)(2,1)S(1)} %get-tuple-element.50), channel_id=1, source_target_pairs={{0,2},{1,3},{2,0},{3,1},{4,6},{5,7},{6,4},{7,5},{8,10},{9,11},{10,... | collective-permute-start | bytes 307208 | tf_op jit(solution)/shard_map/ppermute | solution.py:306
  35.7 1.5 %collective-permute-done.16.refs_1_ = bf16[208,128]{1,0:T(8,128)(2,1)S(1)} collective-permute-done((bf16[208,128]{1,0:T(8,128)(2,1)S(1)}, bf16[208,128]{1,0:T(8,128)(2,1)S(1)}, u32[]{:S(2)}, u32[]{:S(2)}) %collective-permute-start.16) | collective-permute-done | bytes 53280 | tf_op jit(solution)/shard_map/ppermute | solution.py:303
  37.3 0.4 collective-permute-start.17
  37.7 3.2 %collective-permute-start.13 = (bf16[400,128]{1,0:T(8,128)(2,1)S(1)}, bf16[400,128]{1,0:T(8,128)(2,1)S(1)}, u32[]{:S(2)}, u32[]{:S(2)}) collective-permute-start(bf16[400,128]{1,0:T(8,128)(2,1)S(1)} %shard_map.160), channel_id=1, source_target_pairs={{0,16},{4,20},{8,24},{12,28},{16,0},{20,4},{24,8},{28,12},{1,17},{... | collective-permute-start | bytes 307208 | tf_op jit(solution)/shard_map/ppermute | solution.py:303
  40.9 0.6 %collective-permute-done.17.refs_1_ = bf16[208,128]{1,0:T(8,128)(2,1)S(1)} collective-permute-done((bf16[208,128]{1,0:T(8,128)(2,1)S(1)}, bf16[208,128]{1,0:T(8,128)(2,1)S(1)}, u32[]{:S(2)}, u32[]{:S(2)}) %collective-permute-start.17) | collective-permute-done | bytes 53280 | tf_op jit(solution)/shard_map/ppermute | solution.py:303
  41.6 1.5 %collective-permute-start.20 = (bf16[208,128]{1,0:T(8,128)(2,1)S(1)}, bf16[208,128]{1,0:T(8,128)(2,1)S(1)}, u32[]{:S(2)}, u32[]{:S(2)}) collective-permute-start(bf16[208,128]{1,0:T(8,128)(2,1)S(1)} %shard_map.164.refs_2_.refs_0_), channel_id=1, source_target_pairs={{0,4},{4,0},{8,12},{12,8},{16,20},{20,16},{24,28},{28,24},{1,5},{5... | collective-permute-start | bytes 159752 | tf_op jit(solution)/shard_map/ppermute | solution.py:303
  43.1 2.5 %collective-permute-start.18 = (bf16[400,128]{1,0:T(8,128)(2,1)S(1)}, bf16[400,128]{1,0:T(8,128)(2,1)S(1)}, u32[]{:S(2)}, u32[]{:S(2)}) collective-permute-start(bf16[400,128]{1,0:T(8,128)(2,1)S(1)} %shard_map.165), channel_id=1, source_target_pairs={{0,24},{4,28},{8,16},{12,20},{16,8},{20,12},{24,0},{28,4},{1,25},{... | collective-permute-start | bytes 307208 | tf_op jit(solution)/shard_map/ppermute | solution.py:303
  45.6 0.1 shard_map.159
  45.7 0.1 collective-permute-start.19
  45.8 1.3 %collective-permute-start.21 = (bf16[208,128]{1,0:T(8,128)(2,1)S(1)}, bf16[208,128]{1,0:T(8,128)(2,1)S(1)}, u32[]{:S(2)}, u32[]{:S(2)}) collective-permute-start(bf16[208,128]{1,0:T(8,128)(2,1)S(1)} %shard_map.167.refs_0_), channel_id=1, source_target_pairs={{0,2},{1,3},{2,0},{3,1},{4,6},{5,7},{6,4},{7,5},{8,10},{9,11},{10,... | collective-permute-start | bytes 159752 | tf_op jit(solution)/shard_map/ppermute | solution.py:306
  47.2 0.8 %shard_map.158 = (f32[400,128]{1,0:T(8,128)}, f32[1,128]{1,0:T(1,128)}) custom-call(f32[400,128]{1,0:T(8,128)S(1)} %get-tuple-element.49.refs_0_, bf16[400,128]{1,0:T(8,128)(2,1)S(1)} %collective-permute-done.10.refs_1_.refs_2_, f32[400,128]{1,0:T(8,128)S(1)} %bitcast.22, f32[1,128]{1,0:T(1,128)S(1)} %bitcast.25), custom_call_target="tpu_custom_call" | custom-call | tf_op jit(solution)/shard_map/pallas_call | solution.py:56
  47.9 2.1 %collective-permute-done.21.refs_1_ = bf16[208,128]{1,0:T(8,128)(2,1)S(1)} collective-permute-done((bf16[208,128]{1,0:T(8,128)(2,1)S(1)}, bf16[208,128]{1,0:T(8,128)(2,1)S(1)}, u32[]{:S(2)}, u32[]{:S(2)}) %collective-permute-start.21) | collective-permute-done | bytes 53280 | tf_op jit(solution)/shard_map/ppermute | solution.py:306
  50.1 0.1 collective-permute-start.22
  50.2 0.6 %collective-permute-done.19.refs_3_ = bf16[400,128]{1,0:T(8,128)(2,1)S(1)} collective-permute-done((bf16[400,128]{1,0:T(8,128)(2,1)S(1)}, bf16[400,128]{1,0:T(8,128)(2,1)S(1)}, u32[]{:S(2)}, u32[]{:S(2)}) %collective-permute-start.19) | collective-permute-done | bytes 102432 | tf_op jit(solution)/shard_map/ppermute | solution.py:303
  50.7 0.8 %shard_map.166 = (f32[400,128]{1,0:T(8,128)}, f32[1,128]{1,0:T(1,128)}) custom-call(f32[400,128]{1,0:T(8,128)S(1)} %get-tuple-element.55.refs_0_, bf16[400,128]{1,0:T(8,128)(2,1)S(1)} %collective-permute-done.13.refs_1_, bf16[400,128]{1,0:T(8,128)(2,1)S(1)} %collective-permute-done.18.refs_2_, bf16[400,128]{1,0:T(8,128)(2,1)S(1)} %collective-permute-done.19.refs_3_, ...), custom_call_target="tpu_custom_call" | custom-call | flops 12000000000 | tf_op jit(solution)/shard_map/pallas_call | solution.py:56
  51.5 0.9 %shard_map.169 = (f32[400,256]{1,0:T(8,128)}, f32[1,256]{1,0:T(1,128)}) custom-call(bf16[208,128]{1,0:T(8,128)(2,1)S(1)} %shard_map.167.refs_0_, bf16[208,128]{1,0:T(8,128)(2,1)S(1)} %collective-permute-done.21.refs_1_, bf16[416,128]{1,0:T(8,128)(2,1)S(1)} %collective-permute-done.22.refs_2_, f32[400,256]{1,0:T(8,128)S(1)} %bitcast.20, ...), custom_call_target="tpu_custom_call" | custom-call | tf_op jit(solution)/shard_map/pallas_call | solution.py:56
  (40 shorter events, 0.4 us)
Async XLA Ops:
  1.6 9.4 %collective-permute-start.4 = (bf16[400,128]{1,0:T(8,128)(2,1)S(1)}, bf16[400,128]{1,0:T(8,128)(2,1)S(1)}, u32[]{:S(2)}, u32[]{:S(2)}) collective-permute-start(bf16[400,128]{1,0:T(8,128)(2,1)S(1)} %bitcast_convert_fusion), channel_id=1, source_target_pairs={{0,9},{1,10},{2,11},{3,8},{4,13},{5,14},{6,15},{7,12},{8,1},{9,2},... | collective-permute-start | bytes 307208 | tf_op jit(solution)/shard_map/ppermute | solution.py:313
  4.1 12.1 %collective-permute-start.2 = (bf16[400,128]{1,0:T(8,128)(2,1)S(1)}, bf16[400,128]{1,0:T(8,128)(2,1)S(1)}, u32[]{:S(2)}, u32[]{:S(2)}) collective-permute-start(bf16[400,128]{1,0:T(8,128)(2,1)S(1)} %bitcast_convert_fusion), channel_id=1, source_target_pairs={{0,25},{1,26},{2,27},{3,24},{4,29},{5,30},{6,31},{7,28},{8,17},{9,... | collective-permute-start | bytes 307208 | tf_op jit(solution)/shard_map/ppermute | solution.py:313
  7.8 10.1 %collective-permute-start.1 = (bf16[400,128]{1,0:T(8,128)(2,1)S(1)}, bf16[400,128]{1,0:T(8,128)(2,1)S(1)}, u32[]{:S(2)}, u32[]{:S(2)}) collective-permute-start(bf16[400,128]{1,0:T(8,128)(2,1)S(1)} %bitcast_convert_fusion), channel_id=1, source_target_pairs={{0,17},{1,18},{2,19},{3,16},{4,21},{5,22},{6,23},{7,20},{8,25},{9,... | collective-permute-start | bytes 307208 | tf_op jit(solution)/shard_map/ppermute | solution.py:313
  7.9 4.9 %collective-permute-start = (bf16[400,128]{1,0:T(8,128)(2,1)S(1)}, bf16[400,128]{1,0:T(8,128)(2,1)S(1)}, u32[]{:S(2)}, u32[]{:S(2)}) collective-permute-start(bf16[400,128]{1,0:T(8,128)(2,1)S(1)} %bitcast_convert_fusion), channel_id=1, source_target_pairs={{0,1},{1,2},{2,3},{3,0},{4,5},{5,6},{6,7},{7,4},{8,9},{9,10},{10,1... | collective-permute-start | bytes 307208 | tf_op jit(solution)/shard_map/ppermute | solution.py:313
  7.9 0.9 %copy-start.1 = (f32[128,400]{0,1:T(8,128)S(1)}, f32[128,400]{0,1:T(8,128)}, u32[]{:S(2)}) copy-start(f32[128,400]{0,1:T(8,128)} %param.10) | copy-start | bytes 614404
  9.1 6.9 %collective-permute-start.3 = (bf16[400,128]{1,0:T(8,128)(2,1)S(1)}, bf16[400,128]{1,0:T(8,128)(2,1)S(1)}, u32[]{:S(2)}, u32[]{:S(2)}) collective-permute-start(bf16[400,128]{1,0:T(8,128)(2,1)S(1)} %shard_map.145.refs_0_), channel_id=1, source_target_pairs={{0,2},{1,3},{2,0},{3,1},{4,6},{5,7},{6,4},{7,5},{8,10},{9,11},{10,... | collective-permute-start | bytes 307208 | tf_op jit(solution)/shard_map/ppermute | solution.py:306
  10.9 3.5 %copy-start = (f32[256,400]{0,1:T(8,128)S(1)}, f32[256,400]{0,1:T(8,128)}, u32[]{:S(2)}) copy-start(f32[256,400]{0,1:T(8,128)} %param.14) | copy-start | bytes 1228804
  12.9 6.7 %collective-permute-start.7 = (bf16[400,256]{1,0:T(8,128)(2,1)S(1)}, bf16[400,256]{1,0:T(8,128)(2,1)S(1)}, u32[]{:S(2)}, u32[]{:S(2)}) collective-permute-start(bf16[400,256]{1,0:T(8,128)(2,1)S(1)} %shard_map.146.refs_3_), channel_id=1, source_target_pairs={{0,4},{4,0},{8,12},{12,8},{16,20},{20,16},{24,28},{28,24},{1,5},{5... | collective-permute-start | bytes 614408 | tf_op jit(solution)/shard_map/ppermute | solution.py:303
  16.1 3.5 %copy-start.3 = (f32[128,400]{0,1:T(8,128)S(1)}, f32[128,400]{0,1:T(8,128)}, u32[]{:S(2)}) copy-start(f32[128,400]{0,1:T(8,128)} %param.12) | copy-start | bytes 614404
  16.1 3.4 %copy-start.6 = (f32[128]{0:T(128)S(1)}, f32[128]{0:T(128)}, u32[]{:S(2)}) copy-start(f32[128]{0:T(128)} %param.13) | copy-start | bytes 1540
  16.1 3.6 %collective-permute-start.6 = (bf16[400,256]{1,0:T(8,128)(2,1)S(1)}, bf16[400,256]{1,0:T(8,128)(2,1)S(1)}, u32[]{:S(2)}, u32[]{:S(2)}) collective-permute-start(bf16[400,256]{1,0:T(8,128)(2,1)S(1)} %shard_map.148.refs_3_), channel_id=1, source_target_pairs={{0,1},{1,0},{2,3},{3,2},{4,5},{5,4},{6,7},{7,6},{8,9},{9,8},{10,11... | collective-permute-start | bytes 614408 | tf_op jit(solution)/shard_map/ppermute | solution.py:306
  17.9 6.5 %collective-permute-start.5 = (bf16[400,256]{1,0:T(8,128)(2,1)S(1)}, bf16[400,256]{1,0:T(8,128)(2,1)S(1)}, u32[]{:S(2)}, u32[]{:S(2)}) collective-permute-start(bf16[400,256]{1,0:T(8,128)(2,1)S(1)} %shard_map.149.refs_2_), channel_id=1, source_target_pairs={{0,4},{4,0},{8,12},{12,8},{16,20},{20,16},{24,28},{28,24},{1,5},{5... | collective-permute-start | bytes 614408 | tf_op jit(solution)/shard_map/ppermute | solution.py:303
  19.5 5.3 %collective-permute-start.8 = (f32[408,128]{1,0:T(8,128)S(1)}, f32[408,128]{1,0:T(8,128)S(1)}, u32[]{:S(2)}, u32[]{:S(2)}) collective-permute-start(f32[408,128]{1,0:T(8,128)S(1)} %shard_map.154), channel_id=1, source_target_pairs={{0,1},{1,2},{2,3},{3,0},{4,5},{5,6},{6,7},{7,4},{8,9},{9,10},{10,1... | collective-permute-start | bytes 626696 | tf_op jit(solution)/shard_map/ppermute | solution.py:313
  26.3 1.6 %collective-permute-start.14 = (bf16[416,128]{1,0:T(8,128)(2,1)S(1)}, bf16[416,128]{1,0:T(8,128)(2,1)S(1)}, u32[]{:S(2)}, u32[]{:S(2)}) collective-permute-start(bf16[416,128]{1,0:T(8,128)(2,1)S(1)} %get-tuple-element.58), channel_id=1, source_target_pairs={{0,1},{1,0},{2,3},{3,2},{4,5},{5,4},{6,7},{7,6},{8,9},{9,8},{10,11... | collective-permute-start | bytes 319496 | tf_op jit(solution)/shard_map/ppermute | solution.py:306
  27.3 7.4 %collective-permute-start.9 = (bf16[400,256]{1,0:T(8,128)(2,1)S(1)}, bf16[400,256]{1,0:T(8,128)(2,1)S(1)}, u32[]{:S(2)}, u32[]{:S(2)}) collective-permute-start(bf16[400,256]{1,0:T(8,128)(2,1)S(1)} %get-tuple-element.48), channel_id=1, source_target_pairs={{0,1},{1,0},{2,3},{3,2},{4,5},{5,4},{6,7},{7,6},{8,9},{9,8},{10,11... | collective-permute-start | bytes 614408 | tf_op jit(solution)/shard_map/ppermute | solution.py:306
  27.9 4.2 %collective-permute-start.15 = (bf16[208,128]{1,0:T(8,128)(2,1)S(1)}, bf16[208,128]{1,0:T(8,128)(2,1)S(1)}, u32[]{:S(2)}, u32[]{:S(2)}) collective-permute-start(bf16[208,128]{1,0:T(8,128)(2,1)S(1)} %get-tuple-element.60), channel_id=1, source_target_pairs={{0,2},{1,3},{2,0},{3,1},{4,6},{5,7},{6,4},{7,5},{8,10},{9,11},{10,... | collective-permute-start | bytes 159752 | tf_op jit(solution)/shard_map/ppermute | solution.py:306
  29.1 8.6 %collective-permute-start.12 = (bf16[400,256]{1,0:T(8,128)(2,1)S(1)}, bf16[400,256]{1,0:T(8,128)(2,1)S(1)}, u32[]{:S(2)}, u32[]{:S(2)}) collective-permute-start(bf16[400,256]{1,0:T(8,128)(2,1)S(1)} %get-tuple-element.56), channel_id=1, source_target_pairs={{0,4},{4,0},{8,12},{12,8},{16,20},{20,16},{24,28},{28,24},{1,5},{5... | collective-permute-start | bytes 614408 | tf_op jit(solution)/shard_map/ppermute | solution.py:303
  32.1 5.1 %collective-permute-start.16 = (bf16[208,128]{1,0:T(8,128)(2,1)S(1)}, bf16[208,128]{1,0:T(8,128)(2,1)S(1)}, u32[]{:S(2)}, u32[]{:S(2)}) collective-permute-start(bf16[208,128]{1,0:T(8,128)(2,1)S(1)} %shard_map.162.refs_0_), channel_id=1, source_target_pairs={{0,16},{4,20},{8,24},{12,28},{16,0},{20,4},{24,8},{28,12},{1,17},{... | collective-permute-start | bytes 159752 | tf_op jit(solution)/shard_map/ppermute | solution.py:303
  33.8 11.8 %collective-permute-start.11 = (bf16[400,256]{1,0:T(8,128)(2,1)S(1)}, bf16[400,256]{1,0:T(8,128)(2,1)S(1)}, u32[]{:S(2)}, u32[]{:S(2)}) collective-permute-start(bf16[400,256]{1,0:T(8,128)(2,1)S(1)} %get-tuple-element.54), channel_id=1, source_target_pairs={{0,4},{4,0},{8,12},{12,8},{16,20},{20,16},{24,28},{28,24},{1,5},{5... | collective-permute-start | bytes 614408 | tf_op jit(solution)/shard_map/ppermute | solution.py:303
  34.8 10.9 %collective-permute-start.10 = (bf16[400,128]{1,0:T(8,128)(2,1)S(1)}, bf16[400,128]{1,0:T(8,128)(2,1)S(1)}, u32[]{:S(2)}, u32[]{:S(2)}) collective-permute-start(bf16[400,128]{1,0:T(8,128)(2,1)S(1)} %get-tuple-element.50), channel_id=1, source_target_pairs={{0,2},{1,3},{2,0},{3,1},{4,6},{5,7},{6,4},{7,5},{8,10},{9,11},{10,... | collective-permute-start | bytes 307208 | tf_op jit(solution)/shard_map/ppermute | solution.py:306
  37.3 4.3 %collective-permute-start.17 = (bf16[208,128]{1,0:T(8,128)(2,1)S(1)}, bf16[208,128]{1,0:T(8,128)(2,1)S(1)}, u32[]{:S(2)}, u32[]{:S(2)}) collective-permute-start(bf16[208,128]{1,0:T(8,128)(2,1)S(1)} %shard_map.163.refs_0_), channel_id=1, source_target_pairs={{0,8},{4,12},{8,0},{12,4},{16,24},{20,28},{24,16},{28,20},{1,9},{5... | collective-permute-start | bytes 159752 | tf_op jit(solution)/shard_map/ppermute | solution.py:303
  37.7 12.4 %collective-permute-start.13 = (bf16[400,128]{1,0:T(8,128)(2,1)S(1)}, bf16[400,128]{1,0:T(8,128)(2,1)S(1)}, u32[]{:S(2)}, u32[]{:S(2)}) collective-permute-start(bf16[400,128]{1,0:T(8,128)(2,1)S(1)} %shard_map.160), channel_id=1, source_target_pairs={{0,16},{4,20},{8,24},{12,28},{16,0},{20,4},{24,8},{28,12},{1,17},{... | collective-permute-start | bytes 307208 | tf_op jit(solution)/shard_map/ppermute | solution.py:303
  41.6 4.2 %collective-permute-start.20 = (bf16[208,128]{1,0:T(8,128)(2,1)S(1)}, bf16[208,128]{1,0:T(8,128)(2,1)S(1)}, u32[]{:S(2)}, u32[]{:S(2)}) collective-permute-start(bf16[208,128]{1,0:T(8,128)(2,1)S(1)} %shard_map.164.refs_2_.refs_0_), channel_id=1, source_target_pairs={{0,4},{4,0},{8,12},{12,8},{16,20},{20,16},{24,28},{28,24},{1,5},{5... | collective-permute-start | bytes 159752 | tf_op jit(solution)/shard_map/ppermute | solution.py:303
  43.1 7.0 %collective-permute-start.18 = (bf16[400,128]{1,0:T(8,128)(2,1)S(1)}, bf16[400,128]{1,0:T(8,128)(2,1)S(1)}, u32[]{:S(2)}, u32[]{:S(2)}) collective-permute-start(bf16[400,128]{1,0:T(8,128)(2,1)S(1)} %shard_map.165), channel_id=1, source_target_pairs={{0,24},{4,28},{8,16},{12,20},{16,8},{20,12},{24,0},{28,4},{1,25},{... | collective-permute-start | bytes 307208 | tf_op jit(solution)/shard_map/ppermute | solution.py:303
  45.7 1.5 %copy-start.2 = (f32[128,400]{0,1:T(8,128)S(1)}, f32[128,400]{0,1:T(8,128)}, u32[]{:S(2)}) copy-start(f32[128,400]{0,1:T(8,128)} %param.10) | copy-start | bytes 614404
  45.7 1.5 %copy-start.5 = (f32[128]{0:T(128)S(1)}, f32[128]{0:T(128)}, u32[]{:S(2)}) copy-start(f32[128]{0:T(128)} %param.11) | copy-start | bytes 1540
  45.7 5.0 %collective-permute-start.19 = (bf16[400,128]{1,0:T(8,128)(2,1)S(1)}, bf16[400,128]{1,0:T(8,128)(2,1)S(1)}, u32[]{:S(2)}, u32[]{:S(2)}) collective-permute-start(bf16[400,128]{1,0:T(8,128)(2,1)S(1)} %get-tuple-element.61), channel_id=1, source_target_pairs={{0,8},{4,12},{8,0},{12,4},{16,24},{20,28},{24,16},{28,20},{1,9},{5... | collective-permute-start | bytes 307208 | tf_op jit(solution)/shard_map/ppermute | solution.py:303
  45.8 4.2 %collective-permute-start.21 = (bf16[208,128]{1,0:T(8,128)(2,1)S(1)}, bf16[208,128]{1,0:T(8,128)(2,1)S(1)}, u32[]{:S(2)}, u32[]{:S(2)}) collective-permute-start(bf16[208,128]{1,0:T(8,128)(2,1)S(1)} %shard_map.167.refs_0_), channel_id=1, source_target_pairs={{0,2},{1,3},{2,0},{3,1},{4,6},{5,7},{6,4},{7,5},{8,10},{9,11},{10,... | collective-permute-start | bytes 159752 | tf_op jit(solution)/shard_map/ppermute | solution.py:306
  50.1 1.5 %collective-permute-start.22 = (bf16[416,128]{1,0:T(8,128)(2,1)S(1)}, bf16[416,128]{1,0:T(8,128)(2,1)S(1)}, u32[]{:S(2)}, u32[]{:S(2)}) collective-permute-start(bf16[416,128]{1,0:T(8,128)(2,1)S(1)} %shard_map.168), channel_id=1, source_target_pairs={{0,1},{1,0},{2,3},{3,2},{4,5},{5,4},{6,7},{7,6},{8,9},{9,8},{10,11... | collective-permute-start | bytes 319496 | tf_op jit(solution)/shard_map/ppermute | solution.py:306
  50.7 0.8 %copy-start.4 = (f32[256]{0:T(256)S(1)}, f32[256]{0:T(256)}, u32[]{:S(2)}) copy-start(f32[256]{0:T(256)} %param.15) | copy-start | bytes 3076

commit v21 on v20

--- a/solution.py
+++ b/solution.py
@@ -346,7 +346,7 @@
         longest = max(i.shape[-1] for i in ids)
         ids = [i.reshape(-1, i.shape[-1]) for i in ids]
         ids = jnp.concatenate([jnp.pad(i, ((0, 0), (0, longest - i.shape[-1]))) for i in ids], axis=0)
-        left_bf = cast(left_t)
+        left_bf = call(join_body, one_block, after=(joined_low,))(cast(left_t))
         half_left = [left_bf] + [swap_right(left_bf, 2 * k) for k in range(1, far_right)]
         place = jnp.stack([here_r, here_l]).astype(jnp.int32)
         weight, relation_bf, ids = call(
@@ -355,11 +355,11 @@
             here=place,
             after=(joined_low,),
         )(ids, relation_t)
-        half_joined = call(join_body, shape(width, far_right * rows, dtype=BF), after=(weight,))(*half_left)
-        joined = call(join_body, chunk, flops=COST_JOIN_HIGH, after=(half_joined,), ahead=(near[0],))(*near[some:])
+        joined = call(join_body, chunk, flops=COST_JOIN_HIGH, after=(weight,), ahead=(near[0],))(*near[some:])
         other_high = swap_left(joined, 1)
+        half_joined = call(join_body, shape(width, far_right * rows, dtype=BF), after=(joined,))(*half_left)
         sibling_left = swap_right(half_joined, 1)
-        moved = next_column(call(pack_body, shape(width + 8, rows), after=(joined,))(right_t, right_state[None, :]), 0)
+        moved = next_column(call(pack_body, shape(width + 8, rows), after=(half_joined,))(right_t, right_state[None, :]), 0)
 
         s, o, q = call(functools.partial(query_body, far_right), (table_bf, table_bf, table_bf), flops=COST_QUERY)(
             *half_left, sibling_left, relation_bf, ids

time: 52.7 us -> 53 us (level)
  waiting for transfers between devices: 11.7 us -> 13.1 us
  starting transfers between devices: 26.2 us -> 25.2 us
    ppermute x8, waiting for transfers between devices: 3.93 us -> 5.7 us  [swap_right(): return lax.ppermute(value, 'right', [(i, i ^ by) for i in range(n_right)])]
    ppermute x8, starting transfers between devices: 5.18 us -> 4.05 us  [swap_right(): return lax.ppermute(value, 'right', [(i, i ^ by) for i in range(n_right)])]
    ppermute x10, waiting for transfers between devices: 3.75 us -> 3.18 us  [swap_left(): return lax.ppermute(value, 'left', [(i, i ^ by) for i in range(n_left)])]
    pallas_call x25 -> x26, Pallas kernels: 10.9 us -> 10.9 us  [run(): pl.pallas_call(inner, out_shape=out_shape, in_specs=specs, scratch_shapes...]
  transfers between devices with their start and end apart: 23 -> 23, of which waited for: 9 -> 10; matrix products, arithmetic and copies ran while one was open for 2% -> 2% of each run, Pallas kernels for 16% -> 16%
where the time goes in v21:
time: 53 us; the launch traced here: 52.8 us
  starting transfers between devices  25.2 us (48%)
  waiting for transfers between devices  13.1 us (25%)
  Pallas kernels  10.9 us (21%)
  other arithmetic  1.78 us (3%)
  local copies, waits for them, and re-layouts  0.96 us (2%)
  between operations  0.85 us (2%)
    ppermute x10, starting transfers between devices, swap_left(): return lax.ppermute(value, 'left', [(i, i ^ by) for i in range(n_left)])  14.3 us
    pallas_call x26, Pallas kernels, run(): pl.pallas_call(inner, out_shape=out_shape, in_specs=specs, scratch_shapes...  10.9 us
    ppermute x5, starting transfers between devices, next_column(): return lax.ppermute(value, ('left', 'right'), perm)  6.85 us
    ppermute x8, waiting for transfers between devices, swap_right(): return lax.ppermute(value, 'right', [(i, i ^ by) for i in range(n_right)])  5.7 us
    ppermute x5, waiting for transfers between devices, next_column(): return lax.ppermute(value, ('left', 'right'), perm)  4.19 us
    ppermute x8, starting transfers between devices, swap_right(): return lax.ppermute(value, 'right', [(i, i ^ by) for i in range(n_right)])  4.05 us
    ppermute x10, waiting for transfers between devices, swap_left(): return lax.ppermute(value, 'left', [(i, i ^ by) for i in range(n_left)])  3.18 us
  transfers between devices with their start and end apart: 23, of which 10 were waited for; matrix products, arithmetic and copies ran while one was open for 2% of the time, Pallas kernels for 16%

profile of v21, /device:TPU:0, one launch (start us, length us, event | category | flops | bytes accessed | tf_op | source)
XLA Modules:
  0.0 52.8 jit_solution(12953230676831176167)
XLA Ops:
  0.6 0.9 %bitcast_convert_fusion = bf16[400,128]{1,0:T(8,128)(2,1)S(1)} fusion(f32[128,400]{0,1:T(8,128)} %param.12), kind=kLoop, calls=%fused_computation.2 | loop fusion | flops 51200 | bytes 307200 | tf_op jit(solution)/shard_map/convert_element_type | solution.py:337
  1.6 2.5 %collective-permute-start.3 = (bf16[400,128]{1,0:T(8,128)(2,1)S(1)}, bf16[400,128]{1,0:T(8,128)(2,1)S(1)}, u32[]{:S(2)}, u32[]{:S(2)}) collective-permute-start(bf16[400,128]{1,0:T(8,128)(2,1)S(1)} %bitcast_convert_fusion), channel_id=1, source_target_pairs={{0,9},{1,10},{2,11},{3,8},{4,13},{5,14},{6,15},{7,12},{8,1},{9,2},... | collective-permute-start | bytes 307208 | tf_op jit(solution)/shard_map/ppermute | solution.py:313
  4.1 3.7 %collective-permute-start.2 = (bf16[400,128]{1,0:T(8,128)(2,1)S(1)}, bf16[400,128]{1,0:T(8,128)(2,1)S(1)}, u32[]{:S(2)}, u32[]{:S(2)}) collective-permute-start(bf16[400,128]{1,0:T(8,128)(2,1)S(1)} %bitcast_convert_fusion), channel_id=1, source_target_pairs={{0,25},{1,26},{2,27},{3,24},{4,29},{5,30},{6,31},{7,28},{8,17},{9,... | collective-permute-start | bytes 307208 | tf_op jit(solution)/shard_map/ppermute | solution.py:313
  7.8 0.1 collective-permute-start.1
  7.9 0.9 %copy-done.1 = f32[128,400]{0,1:T(8,128)S(1)} copy-done((f32[128,400]{0,1:T(8,128)S(1)}, f32[128,400]{0,1:T(8,128)}, u32[]{:S(2)}) %copy-start.1) | copy-done | bytes 204824
  8.8 0.3 shard_map.148.refs_0_
  9.1 0.8 %pad_add_fusion.refs_0_ = s32[5,1024]{1,0:T(8,128)S(1)} fusion(s32[2,1024]{1,0:T(2,128)} %bitcast.27, s32[1,1024]{1,0:T(1,128)} %bitcast.28, s32[1,1024]{1,0:T(1,128)} %bitcast.29, s32[1,1024]{1,0:T(1,128)} %bitcast.30), kind=kLoop, calls=%fused_computation | loop fusion | flops 15360 | bytes 40960 | tf_op jit(solution)/shard_map/concatenate | solution.py:348
  9.9 0.1 pad_add_fusion.1.refs_2_
  10.0 2.8 %collective-permute-done.refs_0_ = bf16[400,128]{1,0:T(8,128)(2,1)S(1)} collective-permute-done((bf16[400,128]{1,0:T(8,128)(2,1)S(1)}, bf16[400,128]{1,0:T(8,128)(2,1)S(1)}, u32[]{:S(2)}, u32[]{:S(2)}) %collective-permute-start) | collective-permute-done | bytes 102432 | tf_op jit(solution)/shard_map/ppermute | solution.py:313
  12.9 1.6 %collective-permute-start.7 = (bf16[400,256]{1,0:T(8,128)(2,1)S(1)}, bf16[400,256]{1,0:T(8,128)(2,1)S(1)}, u32[]{:S(2)}, u32[]{:S(2)}) collective-permute-start(bf16[400,256]{1,0:T(8,128)(2,1)S(1)} %shard_map.145.refs_3_.refs_1_), channel_id=1, source_target_pairs={{0,4},{4,0},{8,12},{12,8},{16,20},{20,16},{24,28},{28,24},{1,5},{5... | collective-permute-start | bytes 614408 | tf_op jit(solution)/shard_map/ppermute | solution.py:303
  14.5 0.6 %collective-permute-start.5 = (bf16[400,128]{1,0:T(8,128)(2,1)S(1)}, bf16[400,128]{1,0:T(8,128)(2,1)S(1)}, u32[]{:S(2)}, u32[]{:S(2)}) collective-permute-start(bf16[400,128]{1,0:T(8,128)(2,1)S(1)} %shard_map.149.refs_0_), channel_id=1, source_target_pairs={{0,2},{1,3},{2,0},{3,1},{4,6},{5,7},{6,4},{7,5},{8,10},{9,11},{10,... | collective-permute-start | bytes 307208 | tf_op jit(solution)/shard_map/ppermute | solution.py:306
  15.1 1.6 %shard_map.146 = (f32[2,1024,128]{2,1,0:T(8,128)S(1)}, bf16[400,256]{1,0:T(8,128)(2,1)S(1)}, s32[5,1024]{1,0:T(8,128)S(1)}) custom-call(s32[5,1024]{1,0:T(8,128)S(1)} %pad_add_fusion.refs_0_, f32[400,256]{1,0:T(8,128)S(1)} %bitcast.19, s32[2]{0:T(128)S(1)} %pad_add_fusion.1.refs_2_, bf16[400,256]{1,0:T(8,128)(2,1)S(1)} %shard_map.145.refs_3_.refs_1_), custom_call_target="tpu_custom_call" | custom-call | tf_op jit(solution)/shard_map/pallas_call | solution.py:56
  16.6 1.3 %collective-permute-done.1.refs_1_.refs_2_ = bf16[400,128]{1,0:T(8,128)(2,1)S(1)} collective-permute-done((bf16[400,128]{1,0:T(8,128)(2,1)S(1)}, bf16[400,128]{1,0:T(8,128)(2,1)S(1)}, u32[]{:S(2)}, u32[]{:S(2)}) %collective-permute-start.1) | collective-permute-done | bytes 102432 | tf_op jit(solution)/shard_map/ppermute | solution.py:313
  17.9 1.7 %collective-permute-start.4 = (bf16[400,256]{1,0:T(8,128)(2,1)S(1)}, bf16[400,256]{1,0:T(8,128)(2,1)S(1)}, u32[]{:S(2)}, u32[]{:S(2)}) collective-permute-start(bf16[400,256]{1,0:T(8,128)(2,1)S(1)} %shard_map.147.refs_2_), channel_id=1, source_target_pairs={{0,4},{4,0},{8,12},{12,8},{16,20},{20,16},{24,28},{28,24},{1,5},{5... | collective-permute-start | bytes 614408 | tf_op jit(solution)/shard_map/ppermute | solution.py:303
  19.7 0.1 collective-permute-start.6
  19.8 0.5 collective-permute-start.8
  20.3 0.8 %collective-permute-done.6.refs_2_ = bf16[400,256]{1,0:T(8,128)(2,1)S(1)} collective-permute-done((bf16[400,256]{1,0:T(8,128)(2,1)S(1)}, bf16[400,256]{1,0:T(8,128)(2,1)S(1)}, u32[]{:S(2)}, u32[]{:S(2)}) %collective-permute-start.6) | collective-permute-done | bytes 204832 | tf_op jit(solution)/shard_map/ppermute | solution.py:306
  21.2 0.9 %shard_map.151 = (bf16[400,1024]{1,0:T(8,128)(2,1)S(1)}, bf16[400,1024]{1,0:T(8,128)(2,1)S(1)}, bf16[400,1024]{1,0:T(8,128)(2,1)S(1)}) custom-call(bf16[400,128]{1,0:T(8,128)(2,1)S(1)} %shard_map.149.refs_0_, bf16[400,128]{1,0:T(8,128)(2,1)S(1)} %collective-permute-done.5.refs_1_, bf16[400,256]{1,0:T(8,128)(2,1)S(1)} %collective-permute-done.6.refs_2_, ...), custom_call_target="tpu_custom_call" | custom-call | flops 6000000000 | tf_op jit(solution)/shard_map/pallas_call | solution.py:56
  22.1 1.8 %shard_map.153 = (f32[400,512]{1,0:T(8,128)S(1)}, f32[400,1024]{1,0:T(8,128)S(1)}) custom-call(bf16[400,128]{1,0:T(8,128)(2,1)S(1)} %collective-permute-done.refs_0_, bf16[400,128]{1,0:T(8,128)(2,1)S(1)} %collective-permute-done.3.refs_1_, bf16[400,128]{1,0:T(8,128)(2,1)S(1)} %collective-permute-done.1.refs_1_.refs_2_, ...), custom_call_target="tpu_custom_call" | custom-call | tf_op jit(solution)/shard_map/pallas_call | solution.py:56
  23.9 1.0 %shard_map.154 = (bf16[400,256]{1,0:T(8,128)(2,1)S(1)}, f32[400,1024]{1,0:T(8,128)S(1)}) custom-call(bf16[400,256]{1,0:T(8,128)(2,1)S(1)} %shard_map.152.rows_ref, bf16[400,1024]{1,0:T(8,128)(2,1)S(1)} %get-tuple-element.39.refs_4_.q_ref.refs_1_, f32[2,1024,128]{2,1,0:T(8,128)S(1)} %get-tuple-element.36.refs_3_.refs_5_.weight_ref.refs_2_, ...), custom_call_target="tpu_custom_call" | custom-call | tf_op jit(solution)/shard_map/pallas_call | solution.py:56
  25.0 0.1 collective-permute-done.8.refs_7_.refs_4_.refs_5_
  25.1 1.5 %shard_map.156 = (bf16[256,1024]{1,0:T(8,128)(2,1)S(1)}, f32[400,1024]{1,0:T(8,128)S(1)}, f32[416,128]{1,0:T(8,128)S(1)}, bf16[416,128]{1,0:T(8,128)(2,1)S(1)}) custom-call(bf16[400,256]{1,0:T(8,128)(2,1)S(1)} %collective-permute-done.4.refs_0_, bf16[400,1024]{1,0:T(8,128)(2,1)S(1)} %get-tuple-element.39.refs_4_.q_ref.refs_1_, ...), custom_call_target="tpu_custom_call" | custom-call | tf_op jit(solution)/shard_map/pallas_call | solution.py:56
  26.6 0.2 collective-permute-start.14
  26.7 0.9 %shard_map.157 = (bf16[400,256]{1,0:T(8,128)(2,1)S(1)}, bf16[400,256]{1,0:T(8,128)(2,1)S(1)}, f32[400,256]{1,0:T(8,128)S(1)}, bf16[400,256]{1,0:T(8,128)(2,1)S(1)}) custom-call(bf16[256,1024]{1,0:T(8,128)(2,1)S(1)} %get-tuple-element.43.m_ref, bf16[400,1024]{1,0:T(8,128)(2,1)S(1)} %get-tuple-element.39.refs_4_.q_ref.refs_1_, ...), custom_call_target="tpu_custom_call" | custom-call | tf_op jit(solution)/shard_map/pallas_call | solution.py:56
  27.6 0.5 collective-permute-start.9
  28.2 1.2 %collective-permute-start.15 = (bf16[208,128]{1,0:T(8,128)(2,1)S(1)}, bf16[208,128]{1,0:T(8,128)(2,1)S(1)}, u32[]{:S(2)}, u32[]{:S(2)}) collective-permute-start(bf16[208,128]{1,0:T(8,128)(2,1)S(1)} %get-tuple-element.60), channel_id=1, source_target_pairs={{0,2},{1,3},{2,0},{3,1},{4,6},{5,7},{6,4},{7,5},{8,10},{9,11},{10,... | collective-permute-start | bytes 159752 | tf_op jit(solution)/shard_map/ppermute | solution.py:306
  29.3 1.0 %collective-permute-start.12 = (bf16[400,256]{1,0:T(8,128)(2,1)S(1)}, bf16[400,256]{1,0:T(8,128)(2,1)S(1)}, u32[]{:S(2)}, u32[]{:S(2)}) collective-permute-start(bf16[400,256]{1,0:T(8,128)(2,1)S(1)} %get-tuple-element.56), channel_id=1, source_target_pairs={{0,4},{4,0},{8,12},{12,8},{16,20},{20,16},{24,28},{28,24},{1,5},{5... | collective-permute-start | bytes 614408 | tf_op jit(solution)/shard_map/ppermute | solution.py:303
  30.3 2.1 %collective-permute-done.15.refs_1_ = bf16[208,128]{1,0:T(8,128)(2,1)S(1)} collective-permute-done((bf16[208,128]{1,0:T(8,128)(2,1)S(1)}, bf16[208,128]{1,0:T(8,128)(2,1)S(1)}, u32[]{:S(2)}, u32[]{:S(2)}) %collective-permute-start.15) | collective-permute-done | bytes 53280 | tf_op jit(solution)/shard_map/ppermute | solution.py:306
  32.4 2.3 %collective-permute-start.16 = (bf16[208,128]{1,0:T(8,128)(2,1)S(1)}, bf16[208,128]{1,0:T(8,128)(2,1)S(1)}, u32[]{:S(2)}, u32[]{:S(2)}) collective-permute-start(bf16[208,128]{1,0:T(8,128)(2,1)S(1)} %shard_map.163.refs_0_), channel_id=1, source_target_pairs={{0,16},{4,20},{8,24},{12,28},{16,0},{20,4},{24,8},{28,12},{1,17},{... | collective-permute-start | bytes 159752 | tf_op jit(solution)/shard_map/ppermute | solution.py:303
  34.7 0.5 collective-permute-start.11
  35.2 0.7 %collective-permute-start.10 = (bf16[400,128]{1,0:T(8,128)(2,1)S(1)}, bf16[400,128]{1,0:T(8,128)(2,1)S(1)}, u32[]{:S(2)}, u32[]{:S(2)}) collective-permute-start(bf16[400,128]{1,0:T(8,128)(2,1)S(1)} %get-tuple-element.50), channel_id=1, source_target_pairs={{0,2},{1,3},{2,0},{3,1},{4,6},{5,7},{6,4},{7,5},{8,10},{9,11},{10,... | collective-permute-start | bytes 307208 | tf_op jit(solution)/shard_map/ppermute | solution.py:306
  35.9 1.5 %collective-permute-done.16.refs_1_ = bf16[208,128]{1,0:T(8,128)(2,1)S(1)} collective-permute-done((bf16[208,128]{1,0:T(8,128)(2,1)S(1)}, bf16[208,128]{1,0:T(8,128)(2,1)S(1)}, u32[]{:S(2)}, u32[]{:S(2)}) %collective-permute-start.16) | collective-permute-done | bytes 53280 | tf_op jit(solution)/shard_map/ppermute | solution.py:303
  37.5 0.2 collective-permute-start.17
  37.8 2.7 %collective-permute-start.13 = (bf16[400,128]{1,0:T(8,128)(2,1)S(1)}, bf16[400,128]{1,0:T(8,128)(2,1)S(1)}, u32[]{:S(2)}, u32[]{:S(2)}) collective-permute-start(bf16[400,128]{1,0:T(8,128)(2,1)S(1)} %shard_map.161), channel_id=1, source_target_pairs={{0,16},{4,20},{8,24},{12,28},{16,0},{20,4},{24,8},{28,12},{1,17},{... | collective-permute-start | bytes 307208 | tf_op jit(solution)/shard_map/ppermute | solution.py:303
  40.4 1.3 %collective-permute-done.17.refs_1_ = bf16[208,128]{1,0:T(8,128)(2,1)S(1)} collective-permute-done((bf16[208,128]{1,0:T(8,128)(2,1)S(1)}, bf16[208,128]{1,0:T(8,128)(2,1)S(1)}, u32[]{:S(2)}, u32[]{:S(2)}) %collective-permute-start.17) | collective-permute-done | bytes 53280 | tf_op jit(solution)/shard_map/ppermute | solution.py:303
  41.7 1.6 %collective-permute-start.20 = (bf16[208,128]{1,0:T(8,128)(2,1)S(1)}, bf16[208,128]{1,0:T(8,128)(2,1)S(1)}, u32[]{:S(2)}, u32[]{:S(2)}) collective-permute-start(bf16[208,128]{1,0:T(8,128)(2,1)S(1)} %shard_map.165.refs_2_.refs_0_), channel_id=1, source_target_pairs={{0,4},{4,0},{8,12},{12,8},{16,20},{20,16},{24,28},{28,24},{1,5},{5... | collective-permute-start | bytes 159752 | tf_op jit(solution)/shard_map/ppermute | solution.py:303
  43.3 2.8 %collective-permute-start.18 = (bf16[400,128]{1,0:T(8,128)(2,1)S(1)}, bf16[400,128]{1,0:T(8,128)(2,1)S(1)}, u32[]{:S(2)}, u32[]{:S(2)}) collective-permute-start(bf16[400,128]{1,0:T(8,128)(2,1)S(1)} %shard_map.166), channel_id=1, source_target_pairs={{0,24},{4,28},{8,16},{12,20},{16,8},{20,12},{24,0},{28,4},{1,25},{... | collective-permute-start | bytes 307208 | tf_op jit(solution)/shard_map/ppermute | solution.py:303
  46.1 0.1 shard_map.160
  46.2 0.0 copy-start.2
  46.2 0.1 collective-permute-start.19
  46.3 0.8 %collective-permute-start.21 = (bf16[208,128]{1,0:T(8,128)(2,1)S(1)}, bf16[208,128]{1,0:T(8,128)(2,1)S(1)}, u32[]{:S(2)}, u32[]{:S(2)}) collective-permute-start(bf16[208,128]{1,0:T(8,128)(2,1)S(1)} %shard_map.168.refs_0_), channel_id=1, source_target_pairs={{0,2},{1,3},{2,0},{3,1},{4,6},{5,7},{6,4},{7,5},{8,10},{9,11},{10,... | collective-permute-start | bytes 159752 | tf_op jit(solution)/shard_map/ppermute | solution.py:306
  47.1 0.8 %shard_map.159 = (f32[400,128]{1,0:T(8,128)}, f32[1,128]{1,0:T(1,128)}) custom-call(f32[400,128]{1,0:T(8,128)S(1)} %get-tuple-element.49.refs_0_, bf16[400,128]{1,0:T(8,128)(2,1)S(1)} %collective-permute-done.10.refs_1_.refs_2_, f32[400,128]{1,0:T(8,128)S(1)} %bitcast.22, f32[1,128]{1,0:T(1,128)S(1)} %bitcast.25), custom_call_target="tpu_custom_call" | custom-call | tf_op jit(solution)/shard_map/pallas_call | solution.py:56
  47.9 2.6 %collective-permute-done.21.refs_1_ = bf16[208,128]{1,0:T(8,128)(2,1)S(1)} collective-permute-done((bf16[208,128]{1,0:T(8,128)(2,1)S(1)}, bf16[208,128]{1,0:T(8,128)(2,1)S(1)}, u32[]{:S(2)}, u32[]{:S(2)}) %collective-permute-start.21) | collective-permute-done | bytes 53280 | tf_op jit(solution)/shard_map/ppermute | solution.py:306
  50.5 0.1 collective-permute-start.22
  50.6 0.3 collective-permute-done.19.refs_3_
  51.0 0.8 %shard_map.167 = (f32[400,128]{1,0:T(8,128)}, f32[1,128]{1,0:T(1,128)}) custom-call(f32[400,128]{1,0:T(8,128)S(1)} %get-tuple-element.55.refs_0_, bf16[400,128]{1,0:T(8,128)(2,1)S(1)} %collective-permute-done.13.refs_1_, bf16[400,128]{1,0:T(8,128)(2,1)S(1)} %collective-permute-done.18.refs_2_, bf16[400,128]{1,0:T(8,128)(2,1)S(1)} %collective-permute-done.19.refs_3_, ...), custom_call_target="tpu_custom_call" | custom-call | flops 12000000000 | tf_op jit(solution)/shard_map/pallas_call | solution.py:56
  51.8 0.2 collective-permute-done.22.refs_2_
  51.9 0.9 %shard_map.170 = (f32[400,256]{1,0:T(8,128)}, f32[1,256]{1,0:T(1,128)}) custom-call(bf16[208,128]{1,0:T(8,128)(2,1)S(1)} %shard_map.168.refs_0_, bf16[208,128]{1,0:T(8,128)(2,1)S(1)} %collective-permute-done.21.refs_1_, bf16[416,128]{1,0:T(8,128)(2,1)S(1)} %collective-permute-done.22.refs_2_, f32[400,256]{1,0:T(8,128)S(1)} %bitcast.20, ...), custom_call_target="tpu_custom_call" | custom-call | tf_op jit(solution)/shard_map/pallas_call | solution.py:56
  (41 shorter events, 0.4 us)
Async XLA Ops:
  1.6 8.4 %collective-permute-start.3 = (bf16[400,128]{1,0:T(8,128)(2,1)S(1)}, bf16[400,128]{1,0:T(8,128)(2,1)S(1)}, u32[]{:S(2)}, u32[]{:S(2)}) collective-permute-start(bf16[400,128]{1,0:T(8,128)(2,1)S(1)} %bitcast_convert_fusion), channel_id=1, source_target_pairs={{0,9},{1,10},{2,11},{3,8},{4,13},{5,14},{6,15},{7,12},{8,1},{9,2},... | collective-permute-start | bytes 307208 | tf_op jit(solution)/shard_map/ppermute | solution.py:313
  4.1 12.5 %collective-permute-start.2 = (bf16[400,128]{1,0:T(8,128)(2,1)S(1)}, bf16[400,128]{1,0:T(8,128)(2,1)S(1)}, u32[]{:S(2)}, u32[]{:S(2)}) collective-permute-start(bf16[400,128]{1,0:T(8,128)(2,1)S(1)} %bitcast_convert_fusion), channel_id=1, source_target_pairs={{0,25},{1,26},{2,27},{3,24},{4,29},{5,30},{6,31},{7,28},{8,17},{9,... | collective-permute-start | bytes 307208 | tf_op jit(solution)/shard_map/ppermute | solution.py:313
  7.8 10.1 %collective-permute-start.1 = (bf16[400,128]{1,0:T(8,128)(2,1)S(1)}, bf16[400,128]{1,0:T(8,128)(2,1)S(1)}, u32[]{:S(2)}, u32[]{:S(2)}) collective-permute-start(bf16[400,128]{1,0:T(8,128)(2,1)S(1)} %bitcast_convert_fusion), channel_id=1, source_target_pairs={{0,17},{1,18},{2,19},{3,16},{4,21},{5,22},{6,23},{7,20},{8,25},{9,... | collective-permute-start | bytes 307208 | tf_op jit(solution)/shard_map/ppermute | solution.py:313
  7.9 4.9 %collective-permute-start = (bf16[400,128]{1,0:T(8,128)(2,1)S(1)}, bf16[400,128]{1,0:T(8,128)(2,1)S(1)}, u32[]{:S(2)}, u32[]{:S(2)}) collective-permute-start(bf16[400,128]{1,0:T(8,128)(2,1)S(1)} %bitcast_convert_fusion), channel_id=1, source_target_pairs={{0,1},{1,2},{2,3},{3,0},{4,5},{5,6},{6,7},{7,4},{8,9},{9,10},{10,1... | collective-permute-start | bytes 307208 | tf_op jit(solution)/shard_map/ppermute | solution.py:313
  7.9 0.9 %copy-start.1 = (f32[128,400]{0,1:T(8,128)S(1)}, f32[128,400]{0,1:T(8,128)}, u32[]{:S(2)}) copy-start(f32[128,400]{0,1:T(8,128)} %param.10) | copy-start | bytes 614404
  10.0 5.1 %copy-start = (f32[256,400]{0,1:T(8,128)S(1)}, f32[256,400]{0,1:T(8,128)}, u32[]{:S(2)}) copy-start(f32[256,400]{0,1:T(8,128)} %param.14) | copy-start | bytes 1228804
  12.9 7.4 %collective-permute-start.7 = (bf16[400,256]{1,0:T(8,128)(2,1)S(1)}, bf16[400,256]{1,0:T(8,128)(2,1)S(1)}, u32[]{:S(2)}, u32[]{:S(2)}) collective-permute-start(bf16[400,256]{1,0:T(8,128)(2,1)S(1)} %shard_map.145.refs_3_.refs_1_), channel_id=1, source_target_pairs={{0,4},{4,0},{8,12},{12,8},{16,20},{20,16},{24,28},{28,24},{1,5},{5... | collective-permute-start | bytes 614408 | tf_op jit(solution)/shard_map/ppermute | solution.py:303
  14.5 5.1 %collective-permute-start.5 = (bf16[400,128]{1,0:T(8,128)(2,1)S(1)}, bf16[400,128]{1,0:T(8,128)(2,1)S(1)}, u32[]{:S(2)}, u32[]{:S(2)}) collective-permute-start(bf16[400,128]{1,0:T(8,128)(2,1)S(1)} %shard_map.149.refs_0_), channel_id=1, source_target_pairs={{0,2},{1,3},{2,0},{3,1},{4,6},{5,7},{6,4},{7,5},{8,10},{9,11},{10,... | collective-permute-start | bytes 307208 | tf_op jit(solution)/shard_map/ppermute | solution.py:306
  17.9 1.9 %copy-start.3 = (f32[128,400]{0,1:T(8,128)S(1)}, f32[128,400]{0,1:T(8,128)}, u32[]{:S(2)}) copy-start(f32[128,400]{0,1:T(8,128)} %param.12) | copy-start | bytes 614404
  17.9 1.9 %copy-start.6 = (f32[128]{0:T(128)S(1)}, f32[128]{0:T(128)}, u32[]{:S(2)}) copy-start(f32[128]{0:T(128)} %param.13) | copy-start | bytes 1540
  17.9 7.0 %collective-permute-start.4 = (bf16[400,256]{1,0:T(8,128)(2,1)S(1)}, bf16[400,256]{1,0:T(8,128)(2,1)S(1)}, u32[]{:S(2)}, u32[]{:S(2)}) collective-permute-start(bf16[400,256]{1,0:T(8,128)(2,1)S(1)} %shard_map.147.refs_2_), channel_id=1, source_target_pairs={{0,4},{4,0},{8,12},{12,8},{16,20},{20,16},{24,28},{28,24},{1,5},{5... | collective-permute-start | bytes 614408 | tf_op jit(solution)/shard_map/ppermute | solution.py:303
  19.7 1.5 %collective-permute-start.6 = (bf16[400,256]{1,0:T(8,128)(2,1)S(1)}, bf16[400,256]{1,0:T(8,128)(2,1)S(1)}, u32[]{:S(2)}, u32[]{:S(2)}) collective-permute-start(bf16[400,256]{1,0:T(8,128)(2,1)S(1)} %shard_map.150.refs_2_), channel_id=1, source_target_pairs={{0,1},{1,0},{2,3},{3,2},{4,5},{5,4},{6,7},{7,6},{8,9},{9,8},{10,11... | collective-permute-start | bytes 614408 | tf_op jit(solution)/shard_map/ppermute | solution.py:306
  19.8 5.3 %collective-permute-start.8 = (f32[408,128]{1,0:T(8,128)S(1)}, f32[408,128]{1,0:T(8,128)S(1)}, u32[]{:S(2)}, u32[]{:S(2)}) collective-permute-start(f32[408,128]{1,0:T(8,128)S(1)} %shard_map.155), channel_id=1, source_target_pairs={{0,1},{1,2},{2,3},{3,0},{4,5},{5,6},{6,7},{7,4},{8,9},{9,10},{10,1... | collective-permute-start | bytes 626696 | tf_op jit(solution)/shard_map/ppermute | solution.py:313
  26.6 1.6 %collective-permute-start.14 = (bf16[416,128]{1,0:T(8,128)(2,1)S(1)}, bf16[416,128]{1,0:T(8,128)(2,1)S(1)}, u32[]{:S(2)}, u32[]{:S(2)}) collective-permute-start(bf16[416,128]{1,0:T(8,128)(2,1)S(1)} %get-tuple-element.58), channel_id=1, source_target_pairs={{0,1},{1,0},{2,3},{3,2},{4,5},{5,4},{6,7},{7,6},{8,9},{9,8},{10,11... | collective-permute-start | bytes 319496 | tf_op jit(solution)/shard_map/ppermute | solution.py:306
  27.6 7.5 %collective-permute-start.9 = (bf16[400,256]{1,0:T(8,128)(2,1)S(1)}, bf16[400,256]{1,0:T(8,128)(2,1)S(1)}, u32[]{:S(2)}, u32[]{:S(2)}) collective-permute-start(bf16[400,256]{1,0:T(8,128)(2,1)S(1)} %get-tuple-element.48), channel_id=1, source_target_pairs={{0,1},{1,0},{2,3},{3,2},{4,5},{5,4},{6,7},{7,6},{8,9},{9,8},{10,11... | collective-permute-start | bytes 614408 | tf_op jit(solution)/shard_map/ppermute | solution.py:306
  28.2 4.2 %collective-permute-start.15 = (bf16[208,128]{1,0:T(8,128)(2,1)S(1)}, bf16[208,128]{1,0:T(8,128)(2,1)S(1)}, u32[]{:S(2)}, u32[]{:S(2)}) collective-permute-start(bf16[208,128]{1,0:T(8,128)(2,1)S(1)} %get-tuple-element.60), channel_id=1, source_target_pairs={{0,2},{1,3},{2,0},{3,1},{4,6},{5,7},{6,4},{7,5},{8,10},{9,11},{10,... | collective-permute-start | bytes 159752 | tf_op jit(solution)/shard_map/ppermute | solution.py:306
  29.3 8.4 %collective-permute-start.12 = (bf16[400,256]{1,0:T(8,128)(2,1)S(1)}, bf16[400,256]{1,0:T(8,128)(2,1)S(1)}, u32[]{:S(2)}, u32[]{:S(2)}) collective-permute-start(bf16[400,256]{1,0:T(8,128)(2,1)S(1)} %get-tuple-element.56), channel_id=1, source_target_pairs={{0,4},{4,0},{8,12},{12,8},{16,20},{20,16},{24,28},{28,24},{1,5},{5... | collective-permute-start | bytes 614408 | tf_op jit(solution)/shard_map/ppermute | solution.py:303
  32.4 5.1 %collective-permute-start.16 = (bf16[208,128]{1,0:T(8,128)(2,1)S(1)}, bf16[208,128]{1,0:T(8,128)(2,1)S(1)}, u32[]{:S(2)}, u32[]{:S(2)}) collective-permute-start(bf16[208,128]{1,0:T(8,128)(2,1)S(1)} %shard_map.163.refs_0_), channel_id=1, source_target_pairs={{0,16},{4,20},{8,24},{12,28},{16,0},{20,4},{24,8},{28,12},{1,17},{... | collective-permute-start | bytes 159752 | tf_op jit(solution)/shard_map/ppermute | solution.py:303
  34.7 11.4 %collective-permute-start.11 = (bf16[400,256]{1,0:T(8,128)(2,1)S(1)}, bf16[400,256]{1,0:T(8,128)(2,1)S(1)}, u32[]{:S(2)}, u32[]{:S(2)}) collective-permute-start(bf16[400,256]{1,0:T(8,128)(2,1)S(1)} %get-tuple-element.54), channel_id=1, source_target_pairs={{0,4},{4,0},{8,12},{12,8},{16,20},{20,16},{24,28},{28,24},{1,5},{5... | collective-permute-start | bytes 614408 | tf_op jit(solution)/shard_map/ppermute | solution.py:303
  35.2 10.9 %collective-permute-start.10 = (bf16[400,128]{1,0:T(8,128)(2,1)S(1)}, bf16[400,128]{1,0:T(8,128)(2,1)S(1)}, u32[]{:S(2)}, u32[]{:S(2)}) collective-permute-start(bf16[400,128]{1,0:T(8,128)(2,1)S(1)} %get-tuple-element.50), channel_id=1, source_target_pairs={{0,2},{1,3},{2,0},{3,1},{4,6},{5,7},{6,4},{7,5},{8,10},{9,11},{10,... | collective-permute-start | bytes 307208 | tf_op jit(solution)/shard_map/ppermute | solution.py:306
  37.5 4.2 %collective-permute-start.17 = (bf16[208,128]{1,0:T(8,128)(2,1)S(1)}, bf16[208,128]{1,0:T(8,128)(2,1)S(1)}, u32[]{:S(2)}, u32[]{:S(2)}) collective-permute-start(bf16[208,128]{1,0:T(8,128)(2,1)S(1)} %shard_map.164.refs_0_), channel_id=1, source_target_pairs={{0,8},{4,12},{8,0},{12,4},{16,24},{20,28},{24,16},{28,20},{1,9},{5... | collective-permute-start | bytes 159752 | tf_op jit(solution)/shard_map/ppermute | solution.py:303
  37.8 12.9 %collective-permute-start.13 = (bf16[400,128]{1,0:T(8,128)(2,1)S(1)}, bf16[400,128]{1,0:T(8,128)(2,1)S(1)}, u32[]{:S(2)}, u32[]{:S(2)}) collective-permute-start(bf16[400,128]{1,0:T(8,128)(2,1)S(1)} %shard_map.161), channel_id=1, source_target_pairs={{0,16},{4,20},{8,24},{12,28},{16,0},{20,4},{24,8},{28,12},{1,17},{... | collective-permute-start | bytes 307208 | tf_op jit(solution)/shard_map/ppermute | solution.py:303
  41.7 4.6 %collective-permute-start.20 = (bf16[208,128]{1,0:T(8,128)(2,1)S(1)}, bf16[208,128]{1,0:T(8,128)(2,1)S(1)}, u32[]{:S(2)}, u32[]{:S(2)}) collective-permute-start(bf16[208,128]{1,0:T(8,128)(2,1)S(1)} %shard_map.165.refs_2_.refs_0_), channel_id=1, source_target_pairs={{0,4},{4,0},{8,12},{12,8},{16,20},{20,16},{24,28},{28,24},{1,5},{5... | collective-permute-start | bytes 159752 | tf_op jit(solution)/shard_map/ppermute | solution.py:303
  43.3 7.3 %collective-permute-start.18 = (bf16[400,128]{1,0:T(8,128)(2,1)S(1)}, bf16[400,128]{1,0:T(8,128)(2,1)S(1)}, u32[]{:S(2)}, u32[]{:S(2)}) collective-permute-start(bf16[400,128]{1,0:T(8,128)(2,1)S(1)} %shard_map.166), channel_id=1, source_target_pairs={{0,24},{4,28},{8,16},{12,20},{16,8},{20,12},{24,0},{28,4},{1,25},{... | collective-permute-start | bytes 307208 | tf_op jit(solution)/shard_map/ppermute | solution.py:303
  46.2 0.9 %copy-start.2 = (f32[128,400]{0,1:T(8,128)S(1)}, f32[128,400]{0,1:T(8,128)}, u32[]{:S(2)}) copy-start(f32[128,400]{0,1:T(8,128)} %param.10) | copy-start | bytes 614404
  46.2 0.9 %copy-start.5 = (f32[128]{0:T(128)S(1)}, f32[128]{0:T(128)}, u32[]{:S(2)}) copy-start(f32[128]{0:T(128)} %param.11) | copy-start | bytes 1540
  46.2 4.8 %collective-permute-start.19 = (bf16[400,128]{1,0:T(8,128)(2,1)S(1)}, bf16[400,128]{1,0:T(8,128)(2,1)S(1)}, u32[]{:S(2)}, u32[]{:S(2)}) collective-permute-start(bf16[400,128]{1,0:T(8,128)(2,1)S(1)} %get-tuple-element.61), channel_id=1, source_target_pairs={{0,8},{4,12},{8,0},{12,4},{16,24},{20,28},{24,16},{28,20},{1,9},{5... | collective-permute-start | bytes 307208 | tf_op jit(solution)/shard_map/ppermute | solution.py:303
  46.3 4.2 %collective-permute-start.21 = (bf16[208,128]{1,0:T(8,128)(2,1)S(1)}, bf16[208,128]{1,0:T(8,128)(2,1)S(1)}, u32[]{:S(2)}, u32[]{:S(2)}) collective-permute-start(bf16[208,128]{1,0:T(8,128)(2,1)S(1)} %shard_map.168.refs_0_), channel_id=1, source_target_pairs={{0,2},{1,3},{2,0},{3,1},{4,6},{5,7},{6,4},{7,5},{8,10},{9,11},{10,... | collective-permute-start | bytes 159752 | tf_op jit(solution)/shard_map/ppermute | solution.py:306
  50.5 1.4 %collective-permute-start.22 = (bf16[416,128]{1,0:T(8,128)(2,1)S(1)}, bf16[416,128]{1,0:T(8,128)(2,1)S(1)}, u32[]{:S(2)}, u32[]{:S(2)}) collective-permute-start(bf16[416,128]{1,0:T(8,128)(2,1)S(1)} %shard_map.169), channel_id=1, source_target_pairs={{0,1},{1,0},{2,3},{3,2},{4,5},{5,4},{6,7},{7,6},{8,9},{9,8},{10,11... | collective-permute-start | bytes 319496 | tf_op jit(solution)/shard_map/ppermute | solution.py:306
  51.0 0.9 %copy-start.4 = (f32[256]{0:T(256)S(1)}, f32[256]{0:T(256)}, u32[]{:S(2)}) copy-start(f32[256]{0:T(256)} %param.15) | copy-start | bytes 3076

commit v22 on v20

--- a/solution.py
+++ b/solution.py
@@ -205,11 +205,9 @@
     for k in range(pieces):
         start = pl.multiple_of((here ^ k) * size, 16)
         piece = tall_ref[pl.ds(start, size), :]
-        at = slice(k // 2 * size, (k // 2 + 1) * size)
-        if k % 2:
-            theirs_ref[at, :] = piece.astype(BF)
-        else:
-            mine_ref[at, :] = piece
+        at = slice(k * size, (k + 1) * size)
+        mine_ref[at, :] = piece
+        theirs_ref[at, :] = piece.astype(BF)
 
 
 def rest_body(m_ref, q_ref, g_ref, o_ref, ids_ref, low_ref, right_ref, low_out_ref, near_ref, far_ref, left_ref):
@@ -230,15 +228,14 @@
     far_ref[...] = left_ref[:, cut:].astype(BF)
 
 
-def relation_body(pieces, *refs):
-    piece_refs, refs = refs[:pieces // 2], refs[pieces // 2:]
-    sibling_ref, table_ref, state_ref, here_ref, new_ref, state_new_ref, tall_ref = refs
+def relation_body(pieces, own_ref, got_ref, table_ref, state_ref, here_ref, new_ref, state_new_ref, tall_ref):
     here = here_ref[0]
+    second = here_ref[1] == 1
     size = tall_ref.shape[0] // pieces
     for k in range(pieces):
         start = pl.multiple_of((here ^ k) * size, 16)
-        piece = sibling_ref[k // 2 * size:(k // 2 + 1) * size, :] if k % 2 else piece_refs[k // 2][...]
-        tall_ref[pl.ds(start, size), :] = piece.astype(F32)
+        at = slice(k * size, (k + 1) * size)
+        tall_ref[pl.ds(start, size), :] = jnp.where(second, own_ref[at, :].astype(F32), got_ref[at, :].astype(F32))
     width, count = table_ref.shape
     for j in range(count // LANES):
         cols = slice(j * LANES, (j + 1) * LANES)
@@ -305,6 +302,14 @@
     def swap_right(value, by):
         return lax.ppermute(value, "right", [(i, i ^ by) for i in range(n_right)])
 
+    def between(value, core, to):
+        perm = []
+        for i in range(n_left):
+            for r in range(core, n_right, 2):
+                left, right = to(i, r)
+                perm.append((i * n_right + r, left * n_right + right))
+        return lax.ppermute(value, ("left", "right"), perm)
+
     def next_column(value, by):
         perm = []
         for i in range(n_left):
@@ -321,7 +326,7 @@
         left_t, right_t, relation_t = left_table.T, right_table.T, relation_table.T
         nrel = relation_t.shape[1]
         here_l, here_r = lax.axis_index("left"), lax.axis_index("right")
-        me = here_r.astype(jnp.int32).reshape(1)
+        me = jnp.stack([here_r // 2, here_r % 2]).astype(jnp.int32)
         edges = source_ids.shape[-1]
         groups = negative_ids.shape[2]
         n_rows = n_left * rows
@@ -373,11 +378,11 @@
             functools.partial(middle_body, half), (chunk, shape(width, edges)), [pltpu.VMEM((cut, edges), BF)],
         )(other_low, q, weight, ids, qg)
         tall = nrel // LANES * width
-        size = -(-tall // (n_right * 16)) * 16
+        size = -(-tall // (far_right * 16)) * 16
         piece = shape(size, LANES, dtype=BF)
-        all_pieces = pltpu.VMEM((size * n_right, LANES), F32)
+        all_pieces = pltpu.VMEM((size * far_right, LANES), F32)
         m, g, mine, theirs = call(
-            functools.partial(far_body, half + cut, n_right),
+            functools.partial(far_body, half + cut, far_right),
             (shape(cut, edges, dtype=BF), shape(width, edges), shape(far_right * size, LANES),
              shape(far_right * size, LANES, dtype=BF)),
             [pltpu.VMEM((width, nrel), F32), all_pieces],
@@ -394,17 +399,18 @@
 
         mine, *rest = call(
             piece_body, (shape(size, LANES),) + (piece,) * (far_right - 1), flops=COST_SUM
-        )(mine, swap_right(theirs, 1))
-        got = [swap_right(p, 2 * (k + 1)) for k, p in enumerate(rest)]
+        )(mine, between(theirs, 0, lambda l, r: (l, r + 1)))
+        got = [between(p, 1, lambda l, r, k=k: (l, r ^ 2 * (k + 1))) for k, p in enumerate(rest)]
         mine = call(sum_body, piece, flops=COST_SUM)(mine, *got)
         bit = n_left // 2
-        while bit > 1:
-            mine = call(sum_body, piece, flops=COST_SUM)(mine, swap_left(mine, bit))
+        while bit > 0:
+            over_z = mine
+            got = between(mine, 1, lambda l, r: (l ^ bit, r))
+            mine = call(sum_body, piece, flops=COST_SUM)(mine, got)
             bit //= 2
-        over_z = mine
-        mine = call(sum_body, piece, flops=COST_SUM)(mine, swap_left(mine, 1))
-        pieces = [mine] + [swap_right(mine, 2 * k) for k in range(1, far_right)]
-        sibling = swap_right(call(stack_body, shape(far_right * size, LANES, dtype=BF))(*pieces), 1)
+        pieces = [mine] + [between(mine, 1, lambda l, r, k=k: (l, r ^ 2 * k)) for k in range(1, far_right)]
+        stacked = call(stack_body, shape(far_right * size, LANES, dtype=BF))(*pieces)
+        sibling = between(stacked, 1, lambda l, r: (l, r - 1))
 
         left_own, *blocks = call(left_body, (shape(width, rows),) + (one_block,) * (far_right - 1))(
             left_near, swap_right(left_far, 1)
@@ -432,8 +438,8 @@
         left_new, left_state_new = update([left_own, *left_got], left_t, left_state[None, :])
         right_new, right_state_new = update(right_got, moved, moved, COST_UPDATE)
         relation_new, relation_state_new = call(
-            functools.partial(relation_body, n_right), (shape(width, nrel), shape(1, nrel)), [all_pieces], me
-        )(*pieces, sibling, relation_t, relation_state[None, :])
+            functools.partial(relation_body, far_right), (shape(width, nrel), shape(1, nrel)), [all_pieces], me
+        )(stacked, sibling, relation_t, relation_state[None, :])
         return (
             left_new.T, left_state_new.reshape(-1), right_new.T, right_state_new.reshape(-1),
             relation_new.T, relation_state_new.reshape(-1),

time: 52.7 us -> 66.4 us (1.26)
  waiting for transfers between devices: 11.7 us -> 23.6 us
  Pallas kernels: 10.9 us -> 12.1 us
    ppermute x0 -> x7, waiting for transfers between devices: none -> 11.9 us  [between(): return lax.ppermute(value, ('left', 'right'), perm)]
    ppermute x0 -> x7, starting transfers between devices: none -> 6.5 us  [between(): return lax.ppermute(value, ('left', 'right'), perm)]
    ppermute x10 -> x7, starting transfers between devices: 14.7 us -> 8.81 us  [swap_left(): return lax.ppermute(value, 'left', [(i, i ^ by) for i in range(n_left)])]
    ppermute x10 -> x7, waiting for transfers between devices: 3.75 us -> 7.79 us  [swap_left(): return lax.ppermute(value, 'left', [(i, i ^ by) for i in range(n_left)])]
    ppermute x8 -> x4, waiting for transfers between devices: 3.93 us -> 0.01 us  [swap_right(): return lax.ppermute(value, 'right', [(i, i ^ by) for i in range(n_right)])]
    pallas_call x25, Pallas kernels: 10.9 us -> 12.1 us  [run(): pl.pallas_call(inner, out_shape=out_shape, in_specs=specs, scratch_shapes...]
    ppermute x8 -> x4, starting transfers between devices: 5.18 us -> 4.52 us  [swap_right(): return lax.ppermute(value, 'right', [(i, i ^ by) for i in range(n_right)])]
  transfers between devices with their start and end apart: 23 -> 23, of which waited for: 9 -> 10; matrix products, arithmetic and copies ran while one was open for 2% -> 1% of each run, Pallas kernels for 16% -> 13%
where the time goes in v22:
time: 66.4 us; the launch traced here: 65.7 us
  starting transfers between devices  26.2 us (39%)
  waiting for transfers between devices  23.6 us (36%)
  Pallas kernels  12.1 us (18%)
  other arithmetic  1.85 us (3%)
  local copies, waits for them, and re-layouts  0.96 us (1%)
  between operations  0.92 us (1%)
    pallas_call x25, Pallas kernels, run(): pl.pallas_call(inner, out_shape=out_shape, in_specs=specs, scratch_shapes...  12.1 us
    ppermute x7, waiting for transfers between devices, between(): return lax.ppermute(value, ('left', 'right'), perm)  11.9 us
    ppermute x7, starting transfers between devices, swap_left(): return lax.ppermute(value, 'left', [(i, i ^ by) for i in range(n_left)])  8.81 us
    ppermute x7, waiting for transfers between devices, swap_left(): return lax.ppermute(value, 'left', [(i, i ^ by) for i in range(n_left)])  7.79 us
    ppermute x7, starting transfers between devices, between(): return lax.ppermute(value, ('left', 'right'), perm)  6.5 us
    ppermute x5, starting transfers between devices, next_column(): return lax.ppermute(value, ('left', 'right'), perm)  6.37 us
    ppermute x4, starting transfers between devices, swap_right(): return lax.ppermute(value, 'right', [(i, i ^ by) for i in range(n_right)])  4.52 us
    ppermute x5, waiting for transfers between devices, next_column(): return lax.ppermute(value, ('left', 'right'), perm)  3.92 us
  transfers between devices with their start and end apart: 23, of which 10 were waited for; matrix products, arithmetic and copies ran while one was open for 1% of the time, Pallas kernels for 13%

profile of v22, /device:TPU:0, one launch (start us, length us, event | category | flops | bytes accessed | tf_op | source)
XLA Modules:
  0.0 65.7 jit_solution(11249705229423372912)
XLA Ops:
  0.6 0.9 %bitcast_convert_fusion = bf16[400,128]{1,0:T(8,128)(2,1)S(1)} fusion(f32[128,400]{0,1:T(8,128)} %param.12), kind=kLoop, calls=%fused_computation.3 | loop fusion | flops 51200 | bytes 307200 | tf_op jit(solution)/shard_map/convert_element_type | solution.py:342
  1.6 2.5 %collective-permute-start.4 = (bf16[400,128]{1,0:T(8,128)(2,1)S(1)}, bf16[400,128]{1,0:T(8,128)(2,1)S(1)}, u32[]{:S(2)}, u32[]{:S(2)}) collective-permute-start(bf16[400,128]{1,0:T(8,128)(2,1)S(1)} %bitcast_convert_fusion), channel_id=1, source_target_pairs={{0,9},{1,10},{2,11},{3,8},{4,13},{5,14},{6,15},{7,12},{8,1},{9,2},... | collective-permute-start | bytes 307208 | tf_op jit(solution)/shard_map/ppermute | solution.py:318
  4.1 3.7 %collective-permute-start.2 = (bf16[400,128]{1,0:T(8,128)(2,1)S(1)}, bf16[400,128]{1,0:T(8,128)(2,1)S(1)}, u32[]{:S(2)}, u32[]{:S(2)}) collective-permute-start(bf16[400,128]{1,0:T(8,128)(2,1)S(1)} %bitcast_convert_fusion), channel_id=1, source_target_pairs={{0,25},{1,26},{2,27},{3,24},{4,29},{5,30},{6,31},{7,28},{8,17},{9,... | collective-permute-start | bytes 307208 | tf_op jit(solution)/shard_map/ppermute | solution.py:318
  7.8 0.1 collective-permute-start.1
  7.9 0.9 %copy-done.1 = f32[128,400]{0,1:T(8,128)S(1)} copy-done((f32[128,400]{0,1:T(8,128)S(1)}, f32[128,400]{0,1:T(8,128)}, u32[]{:S(2)}) %copy-start.1) | copy-done | bytes 204824
  8.8 0.3 shard_map.145.refs_0_
  9.1 1.0 %collective-permute-start.3 = (bf16[400,128]{1,0:T(8,128)(2,1)S(1)}, bf16[400,128]{1,0:T(8,128)(2,1)S(1)}, u32[]{:S(2)}, u32[]{:S(2)}) collective-permute-start(bf16[400,128]{1,0:T(8,128)(2,1)S(1)} %shard_map.145.refs_0_), channel_id=1, source_target_pairs={{0,2},{1,3},{2,0},{3,1},{4,6},{5,7},{6,4},{7,5},{8,10},{9,11},{10,... | collective-permute-start | bytes 307208 | tf_op jit(solution)/shard_map/ppermute | solution.py:303
  10.1 0.1 pad_add_fusion.2.refs_6_.here_ref
  10.2 0.8 %pad_add_fusion.refs_0_ = s32[5,1024]{1,0:T(8,128)S(1)} fusion(s32[2,1024]{1,0:T(2,128)} %bitcast.29, s32[1,1024]{1,0:T(1,128)} %bitcast.30, s32[1,1024]{1,0:T(1,128)} %bitcast.31, s32[1,1024]{1,0:T(1,128)} %bitcast.32), kind=kLoop, calls=%fused_computation | loop fusion | flops 15360 | bytes 40960 | tf_op jit(solution)/shard_map/concatenate | solution.py:353
  10.9 0.1 pad_add_fusion.1.refs_2_
  11.0 1.8 %collective-permute-done.refs_0_ = bf16[400,128]{1,0:T(8,128)(2,1)S(1)} collective-permute-done((bf16[400,128]{1,0:T(8,128)(2,1)S(1)}, bf16[400,128]{1,0:T(8,128)(2,1)S(1)}, u32[]{:S(2)}, u32[]{:S(2)}) %collective-permute-start) | collective-permute-done | bytes 102432 | tf_op jit(solution)/shard_map/ppermute | solution.py:318
  12.9 1.6 %collective-permute-start.7 = (bf16[400,256]{1,0:T(8,128)(2,1)S(1)}, bf16[400,256]{1,0:T(8,128)(2,1)S(1)}, u32[]{:S(2)}, u32[]{:S(2)}) collective-permute-start(bf16[400,256]{1,0:T(8,128)(2,1)S(1)} %shard_map.146.refs_3_), channel_id=1, source_target_pairs={{0,4},{4,0},{8,12},{12,8},{16,20},{20,16},{24,28},{28,24},{1,5},{5... | collective-permute-start | bytes 614408 | tf_op jit(solution)/shard_map/ppermute | solution.py:300
  14.5 1.6 %shard_map.147 = (f32[2,1024,128]{2,1,0:T(8,128)S(1)}, bf16[400,256]{1,0:T(8,128)(2,1)S(1)}, s32[5,1024]{1,0:T(8,128)S(1)}) custom-call(s32[5,1024]{1,0:T(8,128)S(1)} %pad_add_fusion.refs_0_, f32[400,256]{1,0:T(8,128)S(1)} %bitcast.21, s32[2]{0:T(128)S(1)} %pad_add_fusion.1.refs_2_, bf16[400,256]{1,0:T(8,128)(2,1)S(1)} %shard_map.146.refs_3_), custom_call_target="tpu_custom_call" | custom-call | tf_op jit(solution)/shard_map/pallas_call | solution.py:56
  16.1 0.1 collective-permute-start.6
  16.2 1.7 %collective-permute-done.1.refs_1_.refs_2_ = bf16[400,128]{1,0:T(8,128)(2,1)S(1)} collective-permute-done((bf16[400,128]{1,0:T(8,128)(2,1)S(1)}, bf16[400,128]{1,0:T(8,128)(2,1)S(1)}, u32[]{:S(2)}, u32[]{:S(2)}) %collective-permute-start.1) | collective-permute-done | bytes 102432 | tf_op jit(solution)/shard_map/ppermute | solution.py:318
  17.9 1.6 %collective-permute-start.5 = (bf16[400,256]{1,0:T(8,128)(2,1)S(1)}, bf16[400,256]{1,0:T(8,128)(2,1)S(1)}, u32[]{:S(2)}, u32[]{:S(2)}) collective-permute-start(bf16[400,256]{1,0:T(8,128)(2,1)S(1)} %shard_map.149.refs_2_), channel_id=1, source_target_pairs={{0,4},{4,0},{8,12},{12,8},{16,20},{20,16},{24,28},{28,24},{1,5},{5... | collective-permute-start | bytes 614408 | tf_op jit(solution)/shard_map/ppermute | solution.py:300
  19.5 0.1 collective-permute-start.8
  19.6 0.9 %shard_map.150 = (bf16[400,1024]{1,0:T(8,128)(2,1)S(1)}, bf16[400,1024]{1,0:T(8,128)(2,1)S(1)}, bf16[400,1024]{1,0:T(8,128)(2,1)S(1)}) custom-call(bf16[400,128]{1,0:T(8,128)(2,1)S(1)} %shard_map.145.refs_0_, bf16[400,128]{1,0:T(8,128)(2,1)S(1)} %collective-permute-done.3.refs_1_, bf16[400,256]{1,0:T(8,128)(2,1)S(1)} %collective-permute-done.6.refs_2_, ...), custom_call_target="tpu_custom_call" | custom-call | flops 6000000000 | tf_op jit(solution)/shard_map/pallas_call | solution.py:56
  20.6 1.8 %shard_map.152 = (f32[400,512]{1,0:T(8,128)S(1)}, f32[400,1024]{1,0:T(8,128)S(1)}) custom-call(bf16[400,128]{1,0:T(8,128)(2,1)S(1)} %collective-permute-done.refs_0_, bf16[400,128]{1,0:T(8,128)(2,1)S(1)} %collective-permute-done.4.refs_1_, bf16[400,128]{1,0:T(8,128)(2,1)S(1)} %collective-permute-done.1.refs_1_.refs_2_, ...), custom_call_target="tpu_custom_call" | custom-call | tf_op jit(solution)/shard_map/pallas_call | solution.py:56
  22.4 1.0 %shard_map.153 = (bf16[400,256]{1,0:T(8,128)(2,1)S(1)}, f32[400,1024]{1,0:T(8,128)S(1)}) custom-call(bf16[400,256]{1,0:T(8,128)(2,1)S(1)} %shard_map.151.rows_ref, bf16[400,1024]{1,0:T(8,128)(2,1)S(1)} %get-tuple-element.39.refs_4_.q_ref.refs_1_, f32[2,1024,128]{2,1,0:T(8,128)S(1)} %get-tuple-element.36.refs_2_.refs_5_.weight_ref, ...), custom_call_target="tpu_custom_call" | custom-call | tf_op jit(solution)/shard_map/pallas_call | solution.py:56
  23.4 1.0 %collective-permute-done.5.refs_0_ = bf16[400,256]{1,0:T(8,128)(2,1)S(1)} collective-permute-done((bf16[400,256]{1,0:T(8,128)(2,1)S(1)}, bf16[400,256]{1,0:T(8,128)(2,1)S(1)}, u32[]{:S(2)}, u32[]{:S(2)}) %collective-permute-start.5) | collective-permute-done | bytes 204832 | tf_op jit(solution)/shard_map/ppermute | solution.py:300
  24.4 0.4 collective-permute-done.8.refs_7_.refs_4_.refs_5_
  24.8 2.0 %shard_map.155 = (bf16[256,1024]{1,0:T(8,128)(2,1)S(1)}, f32[400,1024]{1,0:T(8,128)S(1)}, f32[800,128]{1,0:T(8,128)S(1)}, bf16[800,128]{1,0:T(8,128)(2,1)S(1)}) custom-call(bf16[400,256]{1,0:T(8,128)(2,1)S(1)} %collective-permute-done.5.refs_0_, bf16[400,1024]{1,0:T(8,128)(2,1)S(1)} %get-tuple-element.39.refs_4_.q_ref.refs_1_, ...), custom_call_target="tpu_custom_call" | custom-call | tf_op jit(solution)/shard_map/pallas_call | solution.py:56
  26.9 1.7 %collective-permute-start.14 = (bf16[800,128]{1,0:T(8,128)(2,1)S(1)}, bf16[800,128]{1,0:T(8,128)(2,1)S(1)}, u32[]{:S(2)}, u32[]{:S(2)}) collective-permute-start(bf16[800,128]{1,0:T(8,128)(2,1)S(1)} %get-tuple-element.58), channel_id=1, source_target_pairs={{0,1},{2,3},{4,5},{6,7},{8,9},{10,11},{12,13},{14,15},{16,17},{18,... | collective-permute-start | bytes 614408 | tf_op jit(solution)/shard_map/ppermute | solution.py:311
  28.6 1.1 %collective-permute-done.14.got_ref = bf16[800,128]{1,0:T(8,128)(2,1)S(1)} collective-permute-done((bf16[800,128]{1,0:T(8,128)(2,1)S(1)}, bf16[800,128]{1,0:T(8,128)(2,1)S(1)}, u32[]{:S(2)}, u32[]{:S(2)}) %collective-permute-start.14) | collective-permute-done | bytes 204832 | tf_op jit(solution)/shard_map/ppermute | solution.py:311
  29.7 0.7 %collective-permute-start.15 = (bf16[400,128]{1,0:T(8,128)(2,1)S(1)}, bf16[400,128]{1,0:T(8,128)(2,1)S(1)}, u32[]{:S(2)}, u32[]{:S(2)}) collective-permute-start(bf16[400,128]{1,0:T(8,128)(2,1)S(1)} %get-tuple-element.60), channel_id=1, source_target_pairs={{1,3},{3,1},{5,7},{7,5},{9,11},{11,9},{13,15},{15,13},{17,19},{19,... | collective-permute-start | bytes 307208 | tf_op jit(solution)/shard_map/ppermute | solution.py:311
  30.4 0.9 %shard_map.156 = (bf16[400,256]{1,0:T(8,128)(2,1)S(1)}, bf16[400,256]{1,0:T(8,128)(2,1)S(1)}, f32[400,256]{1,0:T(8,128)S(1)}, bf16[400,256]{1,0:T(8,128)(2,1)S(1)}) custom-call(bf16[256,1024]{1,0:T(8,128)(2,1)S(1)} %get-tuple-element.43.m_ref, bf16[400,1024]{1,0:T(8,128)(2,1)S(1)} %get-tuple-element.39.refs_4_.q_ref.refs_1_, ...), custom_call_target="tpu_custom_call" | custom-call | tf_op jit(solution)/shard_map/pallas_call | solution.py:56
  31.3 2.3 %collective-permute-start.9 = (bf16[400,256]{1,0:T(8,128)(2,1)S(1)}, bf16[400,256]{1,0:T(8,128)(2,1)S(1)}, u32[]{:S(2)}, u32[]{:S(2)}) collective-permute-start(bf16[400,256]{1,0:T(8,128)(2,1)S(1)} %get-tuple-element.48), channel_id=1, source_target_pairs={{0,1},{1,0},{2,3},{3,2},{4,5},{5,4},{6,7},{7,6},{8,9},{9,8},{10,11... | collective-permute-start | bytes 614408 | tf_op jit(solution)/shard_map/ppermute | solution.py:303
  33.6 1.0 %collective-permute-start.12 = (bf16[400,256]{1,0:T(8,128)(2,1)S(1)}, bf16[400,256]{1,0:T(8,128)(2,1)S(1)}, u32[]{:S(2)}, u32[]{:S(2)}) collective-permute-start(bf16[400,256]{1,0:T(8,128)(2,1)S(1)} %get-tuple-element.56), channel_id=1, source_target_pairs={{0,4},{4,0},{8,12},{12,8},{16,20},{20,16},{24,28},{28,24},{1,5},{5... | collective-permute-start | bytes 614408 | tf_op jit(solution)/shard_map/ppermute | solution.py:300
  34.6 0.7 %collective-permute-start.16 = (bf16[400,128]{1,0:T(8,128)(2,1)S(1)}, bf16[400,128]{1,0:T(8,128)(2,1)S(1)}, u32[]{:S(2)}, u32[]{:S(2)}) collective-permute-start(bf16[400,128]{1,0:T(8,128)(2,1)S(1)} %shard_map.162.refs_0_), channel_id=1, source_target_pairs={{1,17},{3,19},{5,21},{7,23},{9,25},{11,27},{13,29},{15,31},{17,1},... | collective-permute-start | bytes 307208 | tf_op jit(solution)/shard_map/ppermute | solution.py:311
  35.3 1.1 %collective-permute-start.11 = (bf16[400,256]{1,0:T(8,128)(2,1)S(1)}, bf16[400,256]{1,0:T(8,128)(2,1)S(1)}, u32[]{:S(2)}, u32[]{:S(2)}) collective-permute-start(bf16[400,256]{1,0:T(8,128)(2,1)S(1)} %get-tuple-element.54), channel_id=1, source_target_pairs={{0,4},{4,0},{8,12},{12,8},{16,20},{20,16},{24,28},{28,24},{1,5},{5... | collective-permute-start | bytes 614408 | tf_op jit(solution)/shard_map/ppermute | solution.py:300
  36.5 1.2 %collective-permute-start.10 = (bf16[400,128]{1,0:T(8,128)(2,1)S(1)}, bf16[400,128]{1,0:T(8,128)(2,1)S(1)}, u32[]{:S(2)}, u32[]{:S(2)}) collective-permute-start(bf16[400,128]{1,0:T(8,128)(2,1)S(1)} %get-tuple-element.50), channel_id=1, source_target_pairs={{0,2},{1,3},{2,0},{3,1},{4,6},{5,7},{6,4},{7,5},{8,10},{9,11},{10,... | collective-permute-start | bytes 307208 | tf_op jit(solution)/shard_map/ppermute | solution.py:303
  37.7 0.7 %collective-permute-start.17 = (bf16[400,128]{1,0:T(8,128)(2,1)S(1)}, bf16[400,128]{1,0:T(8,128)(2,1)S(1)}, u32[]{:S(2)}, u32[]{:S(2)}) collective-permute-start(bf16[400,128]{1,0:T(8,128)(2,1)S(1)} %shard_map.163.refs_0_), channel_id=1, source_target_pairs={{1,9},{3,11},{5,13},{7,15},{9,1},{11,3},{13,5},{15,7},{17,25},{19,... | collective-permute-start | bytes 307208 | tf_op jit(solution)/shard_map/ppermute | solution.py:311
  38.4 2.3 %collective-permute-done.12.got_ref.refs_1_ = bf16[400,256]{1,0:T(8,128)(2,1)S(1)} collective-permute-done((bf16[400,256]{1,0:T(8,128)(2,1)S(1)}, bf16[400,256]{1,0:T(8,128)(2,1)S(1)}, u32[]{:S(2)}, u32[]{:S(2)}) %collective-permute-start.12) | collective-permute-done | bytes 204832 | tf_op jit(solution)/shard_map/ppermute | solution.py:300
  40.7 0.9 %collective-permute-start.13 = (bf16[400,128]{1,0:T(8,128)(2,1)S(1)}, bf16[400,128]{1,0:T(8,128)(2,1)S(1)}, u32[]{:S(2)}, u32[]{:S(2)}) collective-permute-start(bf16[400,128]{1,0:T(8,128)(2,1)S(1)} %shard_map.160), channel_id=1, source_target_pairs={{0,16},{4,20},{8,24},{12,28},{16,0},{20,4},{24,8},{28,12},{1,17},{... | collective-permute-start | bytes 307208 | tf_op jit(solution)/shard_map/ppermute | solution.py:300
  41.7 0.7 %collective-permute-start.20 = (bf16[400,128]{1,0:T(8,128)(2,1)S(1)}, bf16[400,128]{1,0:T(8,128)(2,1)S(1)}, u32[]{:S(2)}, u32[]{:S(2)}) collective-permute-start(bf16[400,128]{1,0:T(8,128)(2,1)S(1)} %shard_map.164.refs_2_.refs_0_), channel_id=1, source_target_pairs={{1,5},{3,7},{5,1},{7,3},{9,13},{11,15},{13,9},{15,11},{17,21},{19,... | collective-permute-start | bytes 307208 | tf_op jit(solution)/shard_map/ppermute | solution.py:311
  42.4 2.1 %collective-permute-done.11.refs_1_ = bf16[400,256]{1,0:T(8,128)(2,1)S(1)} collective-permute-done((bf16[400,256]{1,0:T(8,128)(2,1)S(1)}, bf16[400,256]{1,0:T(8,128)(2,1)S(1)}, u32[]{:S(2)}, u32[]{:S(2)}) %collective-permute-start.11) | collective-permute-done | bytes 204832 | tf_op jit(solution)/shard_map/ppermute | solution.py:300
  44.4 0.1 shard_map.159
  44.5 0.1 collective-permute-start.19
  44.6 0.8 %collective-permute-start.21 = (bf16[400,128]{1,0:T(8,128)(2,1)S(1)}, bf16[400,128]{1,0:T(8,128)(2,1)S(1)}, u32[]{:S(2)}, u32[]{:S(2)}) collective-permute-start(bf16[400,128]{1,0:T(8,128)(2,1)S(1)} %shard_map.167.refs_0_), channel_id=1, source_target_pairs={{1,3},{3,1},{5,7},{7,5},{9,11},{11,9},{13,15},{15,13},{17,19},{19,... | collective-permute-start | bytes 307208 | tf_op jit(solution)/shard_map/ppermute | solution.py:311
  45.5 2.6 %collective-permute-start.18 = (bf16[400,128]{1,0:T(8,128)(2,1)S(1)}, bf16[400,128]{1,0:T(8,128)(2,1)S(1)}, u32[]{:S(2)}, u32[]{:S(2)}) collective-permute-start(bf16[400,128]{1,0:T(8,128)(2,1)S(1)} %shard_map.165), channel_id=1, source_target_pairs={{0,24},{4,28},{8,16},{12,20},{16,8},{20,12},{24,0},{28,4},{1,25},{... | collective-permute-start | bytes 307208 | tf_op jit(solution)/shard_map/ppermute | solution.py:300
  48.1 0.8 %shard_map.158 = (f32[400,128]{1,0:T(8,128)}, f32[1,128]{1,0:T(1,128)}) custom-call(f32[400,128]{1,0:T(8,128)S(1)} %get-tuple-element.49.refs_0_, bf16[400,128]{1,0:T(8,128)(2,1)S(1)} %collective-permute-done.10.refs_1_.refs_2_, f32[400,128]{1,0:T(8,128)S(1)} %bitcast.24, f32[1,128]{1,0:T(1,128)S(1)} %bitcast.27), custom_call_target="tpu_custom_call" | custom-call | tf_op jit(solution)/shard_map/pallas_call | solution.py:56
  48.9 1.3 %collective-permute-start.22 = (bf16[800,128]{1,0:T(8,128)(2,1)S(1)}, bf16[800,128]{1,0:T(8,128)(2,1)S(1)}, u32[]{:S(2)}, u32[]{:S(2)}) collective-permute-start(bf16[800,128]{1,0:T(8,128)(2,1)S(1)} %shard_map.168.own_ref), channel_id=1, source_target_pairs={{1,0},{3,2},{5,4},{7,6},{9,8},{11,10},{13,12},{15,14},{17,16},{19,... | collective-permute-start | bytes 614408 | tf_op jit(solution)/shard_map/ppermute | solution.py:311
  50.2 0.3 collective-permute-done.19.refs_3_
  50.5 2.1 %collective-permute-done.18.refs_2_ = bf16[400,128]{1,0:T(8,128)(2,1)S(1)} collective-permute-done((bf16[400,128]{1,0:T(8,128)(2,1)S(1)}, bf16[400,128]{1,0:T(8,128)(2,1)S(1)}, u32[]{:S(2)}, u32[]{:S(2)}) %collective-permute-start.18) | collective-permute-done | bytes 102432 | tf_op jit(solution)/shard_map/ppermute | solution.py:300
  52.6 0.8 %shard_map.166 = (f32[400,128]{1,0:T(8,128)}, f32[1,128]{1,0:T(1,128)}) custom-call(f32[400,128]{1,0:T(8,128)S(1)} %get-tuple-element.55.refs_0_, bf16[400,128]{1,0:T(8,128)(2,1)S(1)} %collective-permute-done.13.refs_1_, bf16[400,128]{1,0:T(8,128)(2,1)S(1)} %collective-permute-done.18.refs_2_, bf16[400,128]{1,0:T(8,128)(2,1)S(1)} %collective-permute-done.19.refs_3_, ...), custom_call_target="tpu_custom_call" | custom-call | flops 12000000000 | tf_op jit(solution)/shard_map/pallas_call | solution.py:56
  53.4 10.8 %collective-permute-done.22.got_ref = bf16[800,128]{1,0:T(8,128)(2,1)S(1)} collective-permute-done((bf16[800,128]{1,0:T(8,128)(2,1)S(1)}, bf16[800,128]{1,0:T(8,128)(2,1)S(1)}, u32[]{:S(2)}, u32[]{:S(2)}) %collective-permute-start.22) | collective-permute-done | bytes 204832 | tf_op jit(solution)/shard_map/ppermute | solution.py:311
  64.2 1.5 %shard_map.169 = (f32[400,256]{1,0:T(8,128)}, f32[1,256]{1,0:T(1,128)}) custom-call(bf16[800,128]{1,0:T(8,128)(2,1)S(1)} %shard_map.168.own_ref, bf16[800,128]{1,0:T(8,128)(2,1)S(1)} %collective-permute-done.22.got_ref, f32[400,256]{1,0:T(8,128)S(1)} %bitcast.22, f32[1,256]{1,0:T(1,128)S(1)} %bitcast.26, s32[2]{0:T(128)S(1)} %pad_add_fusion.2.refs_6_.here_ref), custom_call_target="tpu_custom_call" | custom-call | tf_op jit(solution)/shard_map/pallas_call | solution.py:56
  (41 shorter events, 0.5 us)
Async XLA Ops:
  1.6 9.4 %collective-permute-start.4 = (bf16[400,128]{1,0:T(8,128)(2,1)S(1)}, bf16[400,128]{1,0:T(8,128)(2,1)S(1)}, u32[]{:S(2)}, u32[]{:S(2)}) collective-permute-start(bf16[400,128]{1,0:T(8,128)(2,1)S(1)} %bitcast_convert_fusion), channel_id=1, source_target_pairs={{0,9},{1,10},{2,11},{3,8},{4,13},{5,14},{6,15},{7,12},{8,1},{9,2},... | collective-permute-start | bytes 307208 | tf_op jit(solution)/shard_map/ppermute | solution.py:318
  4.1 12.1 %collective-permute-start.2 = (bf16[400,128]{1,0:T(8,128)(2,1)S(1)}, bf16[400,128]{1,0:T(8,128)(2,1)S(1)}, u32[]{:S(2)}, u32[]{:S(2)}) collective-permute-start(bf16[400,128]{1,0:T(8,128)(2,1)S(1)} %bitcast_convert_fusion), channel_id=1, source_target_pairs={{0,25},{1,26},{2,27},{3,24},{4,29},{5,30},{6,31},{7,28},{8,17},{9,... | collective-permute-start | bytes 307208 | tf_op jit(solution)/shard_map/ppermute | solution.py:318
  7.8 10.1 %collective-permute-start.1 = (bf16[400,128]{1,0:T(8,128)(2,1)S(1)}, bf16[400,128]{1,0:T(8,128)(2,1)S(1)}, u32[]{:S(2)}, u32[]{:S(2)}) collective-permute-start(bf16[400,128]{1,0:T(8,128)(2,1)S(1)} %bitcast_convert_fusion), channel_id=1, source_target_pairs={{0,17},{1,18},{2,19},{3,16},{4,21},{5,22},{6,23},{7,20},{8,25},{9,... | collective-permute-start | bytes 307208 | tf_op jit(solution)/shard_map/ppermute | solution.py:318
  7.9 4.9 %collective-permute-start = (bf16[400,128]{1,0:T(8,128)(2,1)S(1)}, bf16[400,128]{1,0:T(8,128)(2,1)S(1)}, u32[]{:S(2)}, u32[]{:S(2)}) collective-permute-start(bf16[400,128]{1,0:T(8,128)(2,1)S(1)} %bitcast_convert_fusion), channel_id=1, source_target_pairs={{0,1},{1,2},{2,3},{3,0},{4,5},{5,6},{6,7},{7,4},{8,9},{9,10},{10,1... | collective-permute-start | bytes 307208 | tf_op jit(solution)/shard_map/ppermute | solution.py:318
  7.9 0.9 %copy-start.1 = (f32[128,400]{0,1:T(8,128)S(1)}, f32[128,400]{0,1:T(8,128)}, u32[]{:S(2)}) copy-start(f32[128,400]{0,1:T(8,128)} %param.10) | copy-start | bytes 614404
  9.1 6.9 %collective-permute-start.3 = (bf16[400,128]{1,0:T(8,128)(2,1)S(1)}, bf16[400,128]{1,0:T(8,128)(2,1)S(1)}, u32[]{:S(2)}, u32[]{:S(2)}) collective-permute-start(bf16[400,128]{1,0:T(8,128)(2,1)S(1)} %shard_map.145.refs_0_), channel_id=1, source_target_pairs={{0,2},{1,3},{2,0},{3,1},{4,6},{5,7},{6,4},{7,5},{8,10},{9,11},{10,... | collective-permute-start | bytes 307208 | tf_op jit(solution)/shard_map/ppermute | solution.py:303
  11.0 3.5 %copy-start = (f32[256,400]{0,1:T(8,128)S(1)}, f32[256,400]{0,1:T(8,128)}, u32[]{:S(2)}) copy-start(f32[256,400]{0,1:T(8,128)} %param.14) | copy-start | bytes 1228804
  12.9 6.7 %collective-permute-start.7 = (bf16[400,256]{1,0:T(8,128)(2,1)S(1)}, bf16[400,256]{1,0:T(8,128)(2,1)S(1)}, u32[]{:S(2)}, u32[]{:S(2)}) collective-permute-start(bf16[400,256]{1,0:T(8,128)(2,1)S(1)} %shard_map.146.refs_3_), channel_id=1, source_target_pairs={{0,4},{4,0},{8,12},{12,8},{16,20},{20,16},{24,28},{28,24},{1,5},{5... | collective-permute-start | bytes 614408 | tf_op jit(solution)/shard_map/ppermute | solution.py:300
  16.1 3.5 %copy-start.3 = (f32[128,400]{0,1:T(8,128)S(1)}, f32[128,400]{0,1:T(8,128)}, u32[]{:S(2)}) copy-start(f32[128,400]{0,1:T(8,128)} %param.12) | copy-start | bytes 614404
  16.1 3.4 %copy-start.6 = (f32[128]{0:T(128)S(1)}, f32[128]{0:T(128)}, u32[]{:S(2)}) copy-start(f32[128]{0:T(128)} %param.13) | copy-start | bytes 1540
  16.1 3.6 %collective-permute-start.6 = (bf16[400,256]{1,0:T(8,128)(2,1)S(1)}, bf16[400,256]{1,0:T(8,128)(2,1)S(1)}, u32[]{:S(2)}, u32[]{:S(2)}) collective-permute-start(bf16[400,256]{1,0:T(8,128)(2,1)S(1)} %shard_map.148.refs_3_), channel_id=1, source_target_pairs={{0,1},{1,0},{2,3},{3,2},{4,5},{5,4},{6,7},{7,6},{8,9},{9,8},{10,11... | collective-permute-start | bytes 614408 | tf_op jit(solution)/shard_map/ppermute | solution.py:303
  17.9 6.5 %collective-permute-start.5 = (bf16[400,256]{1,0:T(8,128)(2,1)S(1)}, bf16[400,256]{1,0:T(8,128)(2,1)S(1)}, u32[]{:S(2)}, u32[]{:S(2)}) collective-permute-start(bf16[400,256]{1,0:T(8,128)(2,1)S(1)} %shard_map.149.refs_2_), channel_id=1, source_target_pairs={{0,4},{4,0},{8,12},{12,8},{16,20},{20,16},{24,28},{28,24},{1,5},{5... | collective-permute-start | bytes 614408 | tf_op jit(solution)/shard_map/ppermute | solution.py:300
  19.5 5.3 %collective-permute-start.8 = (f32[408,128]{1,0:T(8,128)S(1)}, f32[408,128]{1,0:T(8,128)S(1)}, u32[]{:S(2)}, u32[]{:S(2)}) collective-permute-start(f32[408,128]{1,0:T(8,128)S(1)} %shard_map.154), channel_id=1, source_target_pairs={{0,1},{1,2},{2,3},{3,0},{4,5},{5,6},{6,7},{7,4},{8,9},{9,10},{10,1... | collective-permute-start | bytes 626696 | tf_op jit(solution)/shard_map/ppermute | solution.py:318
  26.9 2.8 %collective-permute-start.14 = (bf16[800,128]{1,0:T(8,128)(2,1)S(1)}, bf16[800,128]{1,0:T(8,128)(2,1)S(1)}, u32[]{:S(2)}, u32[]{:S(2)}) collective-permute-start(bf16[800,128]{1,0:T(8,128)(2,1)S(1)} %get-tuple-element.58), channel_id=1, source_target_pairs={{0,1},{2,3},{4,5},{6,7},{8,9},{10,11},{12,13},{14,15},{16,17},{18,... | collective-permute-start | bytes 614408 | tf_op jit(solution)/shard_map/ppermute | solution.py:311
  29.7 4.9 %collective-permute-start.15 = (bf16[400,128]{1,0:T(8,128)(2,1)S(1)}, bf16[400,128]{1,0:T(8,128)(2,1)S(1)}, u32[]{:S(2)}, u32[]{:S(2)}) collective-permute-start(bf16[400,128]{1,0:T(8,128)(2,1)S(1)} %get-tuple-element.60), channel_id=1, source_target_pairs={{1,3},{3,1},{5,7},{7,5},{9,11},{11,9},{13,15},{15,13},{17,19},{19,... | collective-permute-start | bytes 307208 | tf_op jit(solution)/shard_map/ppermute | solution.py:311
  31.3 5.1 %collective-permute-start.9 = (bf16[400,256]{1,0:T(8,128)(2,1)S(1)}, bf16[400,256]{1,0:T(8,128)(2,1)S(1)}, u32[]{:S(2)}, u32[]{:S(2)}) collective-permute-start(bf16[400,256]{1,0:T(8,128)(2,1)S(1)} %get-tuple-element.48), channel_id=1, source_target_pairs={{0,1},{1,0},{2,3},{3,2},{4,5},{5,4},{6,7},{7,6},{8,9},{9,8},{10,11... | collective-permute-start | bytes 614408 | tf_op jit(solution)/shard_map/ppermute | solution.py:303
  33.6 7.1 %collective-permute-start.12 = (bf16[400,256]{1,0:T(8,128)(2,1)S(1)}, bf16[400,256]{1,0:T(8,128)(2,1)S(1)}, u32[]{:S(2)}, u32[]{:S(2)}) collective-permute-start(bf16[400,256]{1,0:T(8,128)(2,1)S(1)} %get-tuple-element.56), channel_id=1, source_target_pairs={{0,4},{4,0},{8,12},{12,8},{16,20},{20,16},{24,28},{28,24},{1,5},{5... | collective-permute-start | bytes 614408 | tf_op jit(solution)/shard_map/ppermute | solution.py:300
  34.6 3.0 %collective-permute-start.16 = (bf16[400,128]{1,0:T(8,128)(2,1)S(1)}, bf16[400,128]{1,0:T(8,128)(2,1)S(1)}, u32[]{:S(2)}, u32[]{:S(2)}) collective-permute-start(bf16[400,128]{1,0:T(8,128)(2,1)S(1)} %shard_map.162.refs_0_), channel_id=1, source_target_pairs={{1,17},{3,19},{5,21},{7,23},{9,25},{11,27},{13,29},{15,31},{17,1},... | collective-permute-start | bytes 307208 | tf_op jit(solution)/shard_map/ppermute | solution.py:311
  35.3 9.1 %collective-permute-start.11 = (bf16[400,256]{1,0:T(8,128)(2,1)S(1)}, bf16[400,256]{1,0:T(8,128)(2,1)S(1)}, u32[]{:S(2)}, u32[]{:S(2)}) collective-permute-start(bf16[400,256]{1,0:T(8,128)(2,1)S(1)} %get-tuple-element.54), channel_id=1, source_target_pairs={{0,4},{4,0},{8,12},{12,8},{16,20},{20,16},{24,28},{28,24},{1,5},{5... | collective-permute-start | bytes 614408 | tf_op jit(solution)/shard_map/ppermute | solution.py:300
  36.5 7.9 %collective-permute-start.10 = (bf16[400,128]{1,0:T(8,128)(2,1)S(1)}, bf16[400,128]{1,0:T(8,128)(2,1)S(1)}, u32[]{:S(2)}, u32[]{:S(2)}) collective-permute-start(bf16[400,128]{1,0:T(8,128)(2,1)S(1)} %get-tuple-element.50), channel_id=1, source_target_pairs={{0,2},{1,3},{2,0},{3,1},{4,6},{5,7},{6,4},{7,5},{8,10},{9,11},{10,... | collective-permute-start | bytes 307208 | tf_op jit(solution)/shard_map/ppermute | solution.py:303
  37.7 4.0 %collective-permute-start.17 = (bf16[400,128]{1,0:T(8,128)(2,1)S(1)}, bf16[400,128]{1,0:T(8,128)(2,1)S(1)}, u32[]{:S(2)}, u32[]{:S(2)}) collective-permute-start(bf16[400,128]{1,0:T(8,128)(2,1)S(1)} %shard_map.163.refs_0_), channel_id=1, source_target_pairs={{1,9},{3,11},{5,13},{7,15},{9,1},{11,3},{13,5},{15,7},{17,25},{19,... | collective-permute-start | bytes 307208 | tf_op jit(solution)/shard_map/ppermute | solution.py:311
  40.7 9.4 %collective-permute-start.13 = (bf16[400,128]{1,0:T(8,128)(2,1)S(1)}, bf16[400,128]{1,0:T(8,128)(2,1)S(1)}, u32[]{:S(2)}, u32[]{:S(2)}) collective-permute-start(bf16[400,128]{1,0:T(8,128)(2,1)S(1)} %shard_map.160), channel_id=1, source_target_pairs={{0,16},{4,20},{8,24},{12,28},{16,0},{20,4},{24,8},{28,12},{1,17},{... | collective-permute-start | bytes 307208 | tf_op jit(solution)/shard_map/ppermute | solution.py:300
  41.7 2.9 %collective-permute-start.20 = (bf16[400,128]{1,0:T(8,128)(2,1)S(1)}, bf16[400,128]{1,0:T(8,128)(2,1)S(1)}, u32[]{:S(2)}, u32[]{:S(2)}) collective-permute-start(bf16[400,128]{1,0:T(8,128)(2,1)S(1)} %shard_map.164.refs_2_.refs_0_), channel_id=1, source_target_pairs={{1,5},{3,7},{5,1},{7,3},{9,13},{11,15},{13,9},{15,11},{17,21},{19,... | collective-permute-start | bytes 307208 | tf_op jit(solution)/shard_map/ppermute | solution.py:311
  44.5 6.0 %collective-permute-start.19 = (bf16[400,128]{1,0:T(8,128)(2,1)S(1)}, bf16[400,128]{1,0:T(8,128)(2,1)S(1)}, u32[]{:S(2)}, u32[]{:S(2)}) collective-permute-start(bf16[400,128]{1,0:T(8,128)(2,1)S(1)} %get-tuple-element.61), channel_id=1, source_target_pairs={{0,8},{4,12},{8,0},{12,4},{16,24},{20,28},{24,16},{28,20},{1,9},{5... | collective-permute-start | bytes 307208 | tf_op jit(solution)/shard_map/ppermute | solution.py:300
  44.6 3.4 %copy-start.2 = (f32[128,400]{0,1:T(8,128)S(1)}, f32[128,400]{0,1:T(8,128)}, u32[]{:S(2)}) copy-start(f32[128,400]{0,1:T(8,128)} %param.10) | copy-start | bytes 614404
  44.6 3.4 %copy-start.5 = (f32[128]{0:T(128)S(1)}, f32[128]{0:T(128)}, u32[]{:S(2)}) copy-start(f32[128]{0:T(128)} %param.11) | copy-start | bytes 1540
  44.6 4.2 %collective-permute-start.21 = (bf16[400,128]{1,0:T(8,128)(2,1)S(1)}, bf16[400,128]{1,0:T(8,128)(2,1)S(1)}, u32[]{:S(2)}, u32[]{:S(2)}) collective-permute-start(bf16[400,128]{1,0:T(8,128)(2,1)S(1)} %shard_map.167.refs_0_), channel_id=1, source_target_pairs={{1,3},{3,1},{5,7},{7,5},{9,11},{11,9},{13,15},{15,13},{17,19},{19,... | collective-permute-start | bytes 307208 | tf_op jit(solution)/shard_map/ppermute | solution.py:311
  45.5 7.1 %collective-permute-start.18 = (bf16[400,128]{1,0:T(8,128)(2,1)S(1)}, bf16[400,128]{1,0:T(8,128)(2,1)S(1)}, u32[]{:S(2)}, u32[]{:S(2)}) collective-permute-start(bf16[400,128]{1,0:T(8,128)(2,1)S(1)} %shard_map.165), channel_id=1, source_target_pairs={{0,24},{4,28},{8,16},{12,20},{16,8},{20,12},{24,0},{28,4},{1,25},{... | collective-permute-start | bytes 307208 | tf_op jit(solution)/shard_map/ppermute | solution.py:300
  48.9 15.3 %collective-permute-start.22 = (bf16[800,128]{1,0:T(8,128)(2,1)S(1)}, bf16[800,128]{1,0:T(8,128)(2,1)S(1)}, u32[]{:S(2)}, u32[]{:S(2)}) collective-permute-start(bf16[800,128]{1,0:T(8,128)(2,1)S(1)} %shard_map.168.own_ref), channel_id=1, source_target_pairs={{1,0},{3,2},{5,4},{7,6},{9,8},{11,10},{13,12},{15,14},{17,16},{19,... | collective-permute-start | bytes 614408 | tf_op jit(solution)/shard_map/ppermute | solution.py:311
  52.6 11.6 %copy-start.4 = (f32[256]{0:T(256)S(1)}, f32[256]{0:T(256)}, u32[]{:S(2)}) copy-start(f32[256]{0:T(256)} %param.15) | copy-start | bytes 3076

commit v23 on v19

--- a/solution.py
+++ b/solution.py
@@ -21,6 +21,7 @@
 COST_SUM = 1e9
 COST_MIDDLE = 6e9
 COST_QUERY = 6e9
+COST_MOVED = 12e9
 
 
 def dot(a, b, a_dim, b_dim):
@@ -359,7 +360,8 @@
         joined = call(join_body, chunk, flops=COST_JOIN_HIGH, after=(half_joined,), ahead=(near[0],))(*near[some:])
         other_high = swap_left(joined, 1)
         sibling_left = swap_right(half_joined, 1)
-        moved = next_column(call(pack_body, shape(width + 8, rows), after=(joined,))(right_t, right_state[None, :]), 0)
+        pack = call(pack_body, shape(width + 8, rows), after=(joined,))(right_t, right_state[None, :])
+        moved = call(join_body, shape(width + 8, rows), flops=COST_MOVED)(next_column(pack, 0))
 
         s, o, q = call(functools.partial(query_body, far_right), (table_bf, table_bf, table_bf), flops=COST_QUERY)(
             *half_left, sibling_left, relation_bf, ids

time: 56.5 us -> 53.6 us (0.949)
  waiting for transfers between devices: 11.8 us -> 8.33 us
    ppermute x5, waiting for transfers between devices: 4.37 us -> 1.27 us  [next_column(): return lax.ppermute(value, ('left', 'right'), perm)]
    ppermute x10, starting transfers between devices: 17.3 us -> 18.3 us  [swap_left(): return lax.ppermute(value, 'left', [(i, i ^ by) for i in range(n_left)])]
    ppermute x10, waiting for transfers between devices: 2.74 us -> 1.89 us  [swap_left(): return lax.ppermute(value, 'left', [(i, i ^ by) for i in range(n_left)])]
    pallas_call x25 -> x26, Pallas kernels: 11.1 us -> 11.1 us  [run(): pl.pallas_call(inner, out_shape=out_shape, in_specs=specs, scratch_shapes...]
  transfers between devices with their start and end apart: 23 -> 23, of which waited for: 10 -> 10; matrix products, arithmetic and copies ran while one was open for 1% -> 2% of each run, Pallas kernels for 15% -> 19%
where the time goes in v23:
time: 53.6 us; the launch traced here: 53.3 us
  starting transfers between devices  30.3 us (57%)
  Pallas kernels  11.1 us (21%)
  waiting for transfers between devices  8.33 us (16%)
  other arithmetic  1.78 us (3%)
  local copies, waits for them, and re-layouts  1.04 us (2%)
  between operations  0.85 us (2%)
    ppermute x10, starting transfers between devices, swap_left(): return lax.ppermute(value, 'left', [(i, i ^ by) for i in range(n_left)])  18.3 us
    pallas_call x26, Pallas kernels, run(): pl.pallas_call(inner, out_shape=out_shape, in_specs=specs, scratch_shapes...  11.1 us
    ppermute x5, starting transfers between devices, next_column(): return lax.ppermute(value, ('left', 'right'), perm)  6.44 us
    ppermute x8, starting transfers between devices, swap_right(): return lax.ppermute(value, 'right', [(i, i ^ by) for i in range(n_right)])  5.55 us
    ppermute x8, waiting for transfers between devices, swap_right(): return lax.ppermute(value, 'right', [(i, i ^ by) for i in range(n_right)])  5.17 us
    ppermute x10, waiting for transfers between devices, swap_left(): return lax.ppermute(value, 'left', [(i, i ^ by) for i in range(n_left)])  1.89 us
    ppermute x5, waiting for transfers between devices, next_column(): return lax.ppermute(value, ('left', 'right'), perm)  1.27 us
  transfers between devices with their start and end apart: 23, of which 10 were waited for; matrix products, arithmetic and copies ran while one was open for 2% of the time, Pallas kernels for 19%

profile of v23, /device:TPU:0, one launch (start us, length us, event | category | flops | bytes accessed | tf_op | source)
XLA Modules:
  0.0 53.3 jit_solution(8113548139585220415)
XLA Ops:
  0.6 0.9 %bitcast_convert_fusion = bf16[400,128]{1,0:T(8,128)(2,1)S(1)} fusion(f32[128,400]{0,1:T(8,128)} %param.12), kind=kLoop, calls=%fused_computation.2 | loop fusion | flops 51200 | bytes 307200 | tf_op jit(solution)/shard_map/convert_element_type | solution.py:338
  1.6 0.5 collective-permute-start
  2.1 3.8 %collective-permute-start.4 = (bf16[400,128]{1,0:T(8,128)(2,1)S(1)}, bf16[400,128]{1,0:T(8,128)(2,1)S(1)}, u32[]{:S(2)}, u32[]{:S(2)}) collective-permute-start(bf16[400,128]{1,0:T(8,128)(2,1)S(1)} %bitcast_convert_fusion), channel_id=1, source_target_pairs={{0,9},{1,10},{2,11},{3,8},{4,13},{5,14},{6,15},{7,12},{8,1},{9,2},... | collective-permute-start | bytes 307208 | tf_op jit(solution)/shard_map/ppermute | solution.py:314
  5.9 2.1 %collective-permute-start.1 = (bf16[400,128]{1,0:T(8,128)(2,1)S(1)}, bf16[400,128]{1,0:T(8,128)(2,1)S(1)}, u32[]{:S(2)}, u32[]{:S(2)}) collective-permute-start(bf16[400,128]{1,0:T(8,128)(2,1)S(1)} %bitcast_convert_fusion), channel_id=1, source_target_pairs={{0,17},{1,18},{2,19},{3,16},{4,21},{5,22},{6,23},{7,20},{8,25},{9,... | collective-permute-start | bytes 307208 | tf_op jit(solution)/shard_map/ppermute | solution.py:314
  8.0 0.9 %copy-done.1 = f32[128,400]{0,1:T(8,128)S(1)} copy-done((f32[128,400]{0,1:T(8,128)S(1)}, f32[128,400]{0,1:T(8,128)}, u32[]{:S(2)}) %copy-start.1) | copy-done | bytes 204824
  8.9 0.3 shard_map.145.refs_0_
  9.2 2.0 %collective-permute-start.3 = (bf16[400,128]{1,0:T(8,128)(2,1)S(1)}, bf16[400,128]{1,0:T(8,128)(2,1)S(1)}, u32[]{:S(2)}, u32[]{:S(2)}) collective-permute-start(bf16[400,128]{1,0:T(8,128)(2,1)S(1)} %shard_map.145.refs_0_), channel_id=1, source_target_pairs={{0,2},{1,3},{2,0},{3,1},{4,6},{5,7},{6,4},{7,5},{8,10},{9,11},{10,... | collective-permute-start | bytes 307208 | tf_op jit(solution)/shard_map/ppermute | solution.py:307
  11.2 0.8 %pad_add_fusion.refs_0_ = s32[5,1024]{1,0:T(8,128)S(1)} fusion(s32[2,1024]{1,0:T(2,128)} %bitcast.27, s32[1,1024]{1,0:T(1,128)} %bitcast.28, s32[1,1024]{1,0:T(1,128)} %bitcast.29, s32[1,1024]{1,0:T(1,128)} %bitcast.30), kind=kLoop, calls=%fused_computation | loop fusion | flops 15360 | bytes 40960 | tf_op jit(solution)/shard_map/concatenate | solution.py:349
  11.9 0.1 pad_add_fusion.1.refs_2_
  12.1 1.6 %collective-permute-start.7 = (bf16[400,256]{1,0:T(8,128)(2,1)S(1)}, bf16[400,256]{1,0:T(8,128)(2,1)S(1)}, u32[]{:S(2)}, u32[]{:S(2)}) collective-permute-start(bf16[400,256]{1,0:T(8,128)(2,1)S(1)} %shard_map.146.refs_3_), channel_id=1, source_target_pairs={{0,4},{4,0},{8,12},{12,8},{16,20},{20,16},{24,28},{28,24},{1,5},{5... | collective-permute-start | bytes 614408 | tf_op jit(solution)/shard_map/ppermute | solution.py:304
  13.6 1.6 %shard_map.147 = (f32[2,1024,128]{2,1,0:T(8,128)S(1)}, bf16[400,256]{1,0:T(8,128)(2,1)S(1)}, s32[5,1024]{1,0:T(8,128)S(1)}) custom-call(s32[5,1024]{1,0:T(8,128)S(1)} %pad_add_fusion.refs_0_, f32[400,256]{1,0:T(8,128)S(1)} %bitcast.19, s32[2]{0:T(128)S(1)} %pad_add_fusion.1.refs_2_, bf16[400,256]{1,0:T(8,128)(2,1)S(1)} %shard_map.146.refs_3_), custom_call_target="tpu_custom_call" | custom-call | tf_op jit(solution)/shard_map/pallas_call | solution.py:57
  15.2 0.6 %collective-permute-done.3.refs_1_ = bf16[400,128]{1,0:T(8,128)(2,1)S(1)} collective-permute-done((bf16[400,128]{1,0:T(8,128)(2,1)S(1)}, bf16[400,128]{1,0:T(8,128)(2,1)S(1)}, u32[]{:S(2)}, u32[]{:S(2)}) %collective-permute-start.3) | collective-permute-done | bytes 102432 | tf_op jit(solution)/shard_map/ppermute | solution.py:307
  15.8 0.1 collective-permute-start.6
  15.9 1.3 %collective-permute-done.1.refs_1_.refs_2_ = bf16[400,128]{1,0:T(8,128)(2,1)S(1)} collective-permute-done((bf16[400,128]{1,0:T(8,128)(2,1)S(1)}, bf16[400,128]{1,0:T(8,128)(2,1)S(1)}, u32[]{:S(2)}, u32[]{:S(2)}) %collective-permute-start.1) | collective-permute-done | bytes 102432 | tf_op jit(solution)/shard_map/ppermute | solution.py:314
  17.2 1.6 %collective-permute-start.5 = (bf16[400,256]{1,0:T(8,128)(2,1)S(1)}, bf16[400,256]{1,0:T(8,128)(2,1)S(1)}, u32[]{:S(2)}, u32[]{:S(2)}) collective-permute-start(bf16[400,256]{1,0:T(8,128)(2,1)S(1)} %shard_map.149.refs_2_), channel_id=1, source_target_pairs={{0,4},{4,0},{8,12},{12,8},{16,20},{20,16},{24,28},{28,24},{1,5},{5... | collective-permute-start | bytes 614408 | tf_op jit(solution)/shard_map/ppermute | solution.py:304
  18.8 0.1 collective-permute-start.8
  18.9 0.1 collective-permute-done.7.refs_0_
  19.0 0.9 %shard_map.150 = (bf16[400,1024]{1,0:T(8,128)(2,1)S(1)}, bf16[400,1024]{1,0:T(8,128)(2,1)S(1)}, bf16[400,1024]{1,0:T(8,128)(2,1)S(1)}) custom-call(bf16[400,128]{1,0:T(8,128)(2,1)S(1)} %shard_map.145.refs_0_, bf16[400,128]{1,0:T(8,128)(2,1)S(1)} %collective-permute-done.3.refs_1_, bf16[400,256]{1,0:T(8,128)(2,1)S(1)} %collective-permute-done.6.refs_2_, ...), custom_call_target="tpu_custom_call" | custom-call | flops 6000000000 | tf_op jit(solution)/shard_map/pallas_call | solution.py:57
  20.0 1.8 %shard_map.152 = (f32[400,512]{1,0:T(8,128)S(1)}, f32[400,1024]{1,0:T(8,128)S(1)}) custom-call(bf16[400,128]{1,0:T(8,128)(2,1)S(1)} %collective-permute-done.refs_0_, bf16[400,128]{1,0:T(8,128)(2,1)S(1)} %collective-permute-done.4.refs_1_, bf16[400,128]{1,0:T(8,128)(2,1)S(1)} %collective-permute-done.1.refs_1_.refs_2_, ...), custom_call_target="tpu_custom_call" | custom-call | tf_op jit(solution)/shard_map/pallas_call | solution.py:57
  21.8 1.1 %shard_map.153 = (bf16[400,256]{1,0:T(8,128)(2,1)S(1)}, f32[400,1024]{1,0:T(8,128)S(1)}) custom-call(bf16[400,256]{1,0:T(8,128)(2,1)S(1)} %shard_map.151.rows_ref, bf16[400,1024]{1,0:T(8,128)(2,1)S(1)} %get-tuple-element.39.refs_4_.q_ref.refs_1_, f32[2,1024,128]{2,1,0:T(8,128)S(1)} %get-tuple-element.36.refs_2_.refs_5_.weight_ref, ...), custom_call_target="tpu_custom_call" | custom-call | tf_op jit(solution)/shard_map/pallas_call | solution.py:57
  22.9 0.9 %collective-permute-done.5.rows_ref = bf16[400,256]{1,0:T(8,128)(2,1)S(1)} collective-permute-done((bf16[400,256]{1,0:T(8,128)(2,1)S(1)}, bf16[400,256]{1,0:T(8,128)(2,1)S(1)}, u32[]{:S(2)}, u32[]{:S(2)}) %collective-permute-start.5) | collective-permute-done | bytes 204832 | tf_op jit(solution)/shard_map/ppermute | solution.py:304
  23.8 1.5 %shard_map.154 = (bf16[256,1024]{1,0:T(8,128)(2,1)S(1)}, f32[400,1024]{1,0:T(8,128)S(1)}, f32[416,128]{1,0:T(8,128)S(1)}, bf16[416,128]{1,0:T(8,128)(2,1)S(1)}) custom-call(bf16[400,256]{1,0:T(8,128)(2,1)S(1)} %collective-permute-done.5.rows_ref, bf16[400,1024]{1,0:T(8,128)(2,1)S(1)} %get-tuple-element.39.refs_4_.q_ref.refs_1_, ...), custom_call_target="tpu_custom_call" | custom-call | tf_op jit(solution)/shard_map/pallas_call | solution.py:57
  25.3 0.1 collective-permute-start.14
  25.4 1.3 %collective-permute-done.14.got_ref = bf16[416,128]{1,0:T(8,128)(2,1)S(1)} collective-permute-done((bf16[416,128]{1,0:T(8,128)(2,1)S(1)}, bf16[416,128]{1,0:T(8,128)(2,1)S(1)}, u32[]{:S(2)}, u32[]{:S(2)}) %collective-permute-start.14) | collective-permute-done | bytes 106528 | tf_op jit(solution)/shard_map/ppermute | solution.py:307
  26.7 1.2 %collective-permute-start.15 = (bf16[208,128]{1,0:T(8,128)(2,1)S(1)}, bf16[208,128]{1,0:T(8,128)(2,1)S(1)}, u32[]{:S(2)}, u32[]{:S(2)}) collective-permute-start(bf16[208,128]{1,0:T(8,128)(2,1)S(1)} %get-tuple-element.60), channel_id=1, source_target_pairs={{0,2},{1,3},{2,0},{3,1},{4,6},{5,7},{6,4},{7,5},{8,10},{9,11},{10,... | collective-permute-start | bytes 159752 | tf_op jit(solution)/shard_map/ppermute | solution.py:307
  28.0 0.9 %shard_map.157 = (bf16[400,256]{1,0:T(8,128)(2,1)S(1)}, bf16[400,256]{1,0:T(8,128)(2,1)S(1)}, f32[400,256]{1,0:T(8,128)S(1)}, bf16[400,256]{1,0:T(8,128)(2,1)S(1)}) custom-call(bf16[256,1024]{1,0:T(8,128)(2,1)S(1)} %get-tuple-element.43.refs_0_, bf16[400,1024]{1,0:T(8,128)(2,1)S(1)} %get-tuple-element.39.refs_4_.q_ref.refs_1_, ...), custom_call_target="tpu_custom_call" | custom-call | tf_op jit(solution)/shard_map/pallas_call | solution.py:57
  28.9 1.6 %collective-permute-start.12 = (bf16[400,256]{1,0:T(8,128)(2,1)S(1)}, bf16[400,256]{1,0:T(8,128)(2,1)S(1)}, u32[]{:S(2)}, u32[]{:S(2)}) collective-permute-start(bf16[400,256]{1,0:T(8,128)(2,1)S(1)} %get-tuple-element.56), channel_id=1, source_target_pairs={{0,4},{4,0},{8,12},{12,8},{16,20},{20,16},{24,28},{28,24},{1,5},{5... | collective-permute-start | bytes 614408 | tf_op jit(solution)/shard_map/ppermute | solution.py:304
  30.5 0.4 collective-permute-done.15.refs_1_
  30.9 3.6 %collective-permute-start.16 = (bf16[208,128]{1,0:T(8,128)(2,1)S(1)}, bf16[208,128]{1,0:T(8,128)(2,1)S(1)}, u32[]{:S(2)}, u32[]{:S(2)}) collective-permute-start(bf16[208,128]{1,0:T(8,128)(2,1)S(1)} %shard_map.163.refs_0_), channel_id=1, source_target_pairs={{0,16},{4,20},{8,24},{12,28},{16,0},{20,4},{24,8},{28,12},{1,17},{... | collective-permute-start | bytes 159752 | tf_op jit(solution)/shard_map/ppermute | solution.py:304
  34.5 1.5 %collective-permute-start.11 = (bf16[400,256]{1,0:T(8,128)(2,1)S(1)}, bf16[400,256]{1,0:T(8,128)(2,1)S(1)}, u32[]{:S(2)}, u32[]{:S(2)}) collective-permute-start(bf16[400,256]{1,0:T(8,128)(2,1)S(1)} %get-tuple-element.54), channel_id=1, source_target_pairs={{0,4},{4,0},{8,12},{12,8},{16,20},{20,16},{24,28},{28,24},{1,5},{5... | collective-permute-start | bytes 614408 | tf_op jit(solution)/shard_map/ppermute | solution.py:304
  36.1 0.6 %collective-permute-done.16.refs_1_ = bf16[208,128]{1,0:T(8,128)(2,1)S(1)} collective-permute-done((bf16[208,128]{1,0:T(8,128)(2,1)S(1)}, bf16[208,128]{1,0:T(8,128)(2,1)S(1)}, u32[]{:S(2)}, u32[]{:S(2)}) %collective-permute-start.16) | collective-permute-done | bytes 53280 | tf_op jit(solution)/shard_map/ppermute | solution.py:304
  36.7 1.9 %collective-permute-start.17 = (bf16[208,128]{1,0:T(8,128)(2,1)S(1)}, bf16[208,128]{1,0:T(8,128)(2,1)S(1)}, u32[]{:S(2)}, u32[]{:S(2)}) collective-permute-start(bf16[208,128]{1,0:T(8,128)(2,1)S(1)} %shard_map.164.refs_0_), channel_id=1, source_target_pairs={{0,8},{4,12},{8,0},{12,4},{16,24},{20,28},{24,16},{28,20},{1,9},{5... | collective-permute-start | bytes 159752 | tf_op jit(solution)/shard_map/ppermute | solution.py:304
  38.6 2.1 %collective-permute-start.13 = (bf16[400,128]{1,0:T(8,128)(2,1)S(1)}, bf16[400,128]{1,0:T(8,128)(2,1)S(1)}, u32[]{:S(2)}, u32[]{:S(2)}) collective-permute-start(bf16[400,128]{1,0:T(8,128)(2,1)S(1)} %shard_map.161), channel_id=1, source_target_pairs={{0,16},{4,20},{8,24},{12,28},{16,0},{20,4},{24,8},{28,12},{1,17},{... | collective-permute-start | bytes 307208 | tf_op jit(solution)/shard_map/ppermute | solution.py:304
  40.8 0.1 shard_map.158
  40.8 1.5 %collective-permute-start.10 = (bf16[400,128]{1,0:T(8,128)(2,1)S(1)}, bf16[400,128]{1,0:T(8,128)(2,1)S(1)}, u32[]{:S(2)}, u32[]{:S(2)}) collective-permute-start(bf16[400,128]{1,0:T(8,128)(2,1)S(1)} %get-tuple-element.50), channel_id=1, source_target_pairs={{0,2},{1,3},{2,0},{3,1},{4,6},{5,7},{6,4},{7,5},{8,10},{9,11},{10,... | collective-permute-start | bytes 307208 | tf_op jit(solution)/shard_map/ppermute | solution.py:307
  42.3 1.3 %collective-permute-start.20 = (bf16[208,128]{1,0:T(8,128)(2,1)S(1)}, bf16[208,128]{1,0:T(8,128)(2,1)S(1)}, u32[]{:S(2)}, u32[]{:S(2)}) collective-permute-start(bf16[208,128]{1,0:T(8,128)(2,1)S(1)} %shard_map.165.refs_2_.refs_0_), channel_id=1, source_target_pairs={{0,4},{4,0},{8,12},{12,8},{16,20},{20,16},{24,28},{28,24},{1,5},{5... | collective-permute-start | bytes 159752 | tf_op jit(solution)/shard_map/ppermute | solution.py:304
  43.6 3.0 %collective-permute-start.18 = (bf16[400,128]{1,0:T(8,128)(2,1)S(1)}, bf16[400,128]{1,0:T(8,128)(2,1)S(1)}, u32[]{:S(2)}, u32[]{:S(2)}) collective-permute-start(bf16[400,128]{1,0:T(8,128)(2,1)S(1)} %shard_map.166), channel_id=1, source_target_pairs={{0,24},{4,28},{8,16},{12,20},{16,8},{20,12},{24,0},{28,4},{1,25},{... | collective-permute-start | bytes 307208 | tf_op jit(solution)/shard_map/ppermute | solution.py:304
  46.6 0.1 shard_map.160
  46.7 0.1 collective-permute-start.19
  46.8 0.7 %collective-permute-start.21 = (bf16[208,128]{1,0:T(8,128)(2,1)S(1)}, bf16[208,128]{1,0:T(8,128)(2,1)S(1)}, u32[]{:S(2)}, u32[]{:S(2)}) collective-permute-start(bf16[208,128]{1,0:T(8,128)(2,1)S(1)} %shard_map.168.refs_0_), channel_id=1, source_target_pairs={{0,2},{1,3},{2,0},{3,1},{4,6},{5,7},{6,4},{7,5},{8,10},{9,11},{10,... | collective-permute-start | bytes 159752 | tf_op jit(solution)/shard_map/ppermute | solution.py:307
  47.5 0.1 copy-done.2
  47.6 0.8 %shard_map.159 = (f32[400,128]{1,0:T(8,128)}, f32[1,128]{1,0:T(1,128)}) custom-call(f32[400,128]{1,0:T(8,128)S(1)} %get-tuple-element.49.refs_0_, bf16[400,128]{1,0:T(8,128)(2,1)S(1)} %collective-permute-done.10.refs_1_.refs_2_, f32[400,128]{1,0:T(8,128)S(1)} %bitcast.22, f32[1,128]{1,0:T(1,128)S(1)} %bitcast.25), custom_call_target="tpu_custom_call" | custom-call | tf_op jit(solution)/shard_map/pallas_call | solution.py:57
  48.4 2.7 %collective-permute-done.21.refs_1_ = bf16[208,128]{1,0:T(8,128)(2,1)S(1)} collective-permute-done((bf16[208,128]{1,0:T(8,128)(2,1)S(1)}, bf16[208,128]{1,0:T(8,128)(2,1)S(1)}, u32[]{:S(2)}, u32[]{:S(2)}) %collective-permute-start.21) | collective-permute-done | bytes 53280 | tf_op jit(solution)/shard_map/ppermute | solution.py:307
  51.0 0.1 collective-permute-start.22
  51.1 0.3 collective-permute-done.19.refs_3_
  51.4 0.8 %shard_map.167 = (f32[400,128]{1,0:T(8,128)}, f32[1,128]{1,0:T(1,128)}) custom-call(f32[400,128]{1,0:T(8,128)S(1)} %get-tuple-element.55.refs_0_, bf16[400,128]{1,0:T(8,128)(2,1)S(1)} %collective-permute-done.13.refs_1_, bf16[400,128]{1,0:T(8,128)(2,1)S(1)} %collective-permute-done.18.refs_2_, bf16[400,128]{1,0:T(8,128)(2,1)S(1)} %collective-permute-done.19.refs_3_, ...), custom_call_target="tpu_custom_call" | custom-call | flops 12000000000 | tf_op jit(solution)/shard_map/pallas_call | solution.py:57
  52.2 0.2 collective-permute-done.22.refs_2_
  52.4 0.9 %shard_map.170 = (f32[400,256]{1,0:T(8,128)}, f32[1,256]{1,0:T(1,128)}) custom-call(bf16[208,128]{1,0:T(8,128)(2,1)S(1)} %shard_map.168.refs_0_, bf16[208,128]{1,0:T(8,128)(2,1)S(1)} %collective-permute-done.21.refs_1_, bf16[416,128]{1,0:T(8,128)(2,1)S(1)} %collective-permute-done.22.refs_2_, f32[400,256]{1,0:T(8,128)S(1)} %bitcast.20, ...), custom_call_target="tpu_custom_call" | custom-call | tf_op jit(solution)/shard_map/pallas_call | solution.py:57
  (41 shorter events, 0.4 us)
Async XLA Ops:
  1.6 10.4 %collective-permute-start = (bf16[400,128]{1,0:T(8,128)(2,1)S(1)}, bf16[400,128]{1,0:T(8,128)(2,1)S(1)}, u32[]{:S(2)}, u32[]{:S(2)}) collective-permute-start(bf16[400,128]{1,0:T(8,128)(2,1)S(1)} %bitcast_convert_fusion), channel_id=1, source_target_pairs={{0,1},{1,2},{2,3},{3,0},{4,5},{5,6},{6,7},{7,4},{8,9},{9,10},{10,1... | collective-permute-start | bytes 307208 | tf_op jit(solution)/shard_map/ppermute | solution.py:314
  2.1 9.9 %collective-permute-start.4 = (bf16[400,128]{1,0:T(8,128)(2,1)S(1)}, bf16[400,128]{1,0:T(8,128)(2,1)S(1)}, u32[]{:S(2)}, u32[]{:S(2)}) collective-permute-start(bf16[400,128]{1,0:T(8,128)(2,1)S(1)} %bitcast_convert_fusion), channel_id=1, source_target_pairs={{0,9},{1,10},{2,11},{3,8},{4,13},{5,14},{6,15},{7,12},{8,1},{9,2},... | collective-permute-start | bytes 307208 | tf_op jit(solution)/shard_map/ppermute | solution.py:314
  5.9 11.3 %collective-permute-start.1 = (bf16[400,128]{1,0:T(8,128)(2,1)S(1)}, bf16[400,128]{1,0:T(8,128)(2,1)S(1)}, u32[]{:S(2)}, u32[]{:S(2)}) collective-permute-start(bf16[400,128]{1,0:T(8,128)(2,1)S(1)} %bitcast_convert_fusion), channel_id=1, source_target_pairs={{0,17},{1,18},{2,19},{3,16},{4,21},{5,22},{6,23},{7,20},{8,25},{9,... | collective-permute-start | bytes 307208 | tf_op jit(solution)/shard_map/ppermute | solution.py:314
  8.0 9.2 %collective-permute-start.2 = (bf16[400,128]{1,0:T(8,128)(2,1)S(1)}, bf16[400,128]{1,0:T(8,128)(2,1)S(1)}, u32[]{:S(2)}, u32[]{:S(2)}) collective-permute-start(bf16[400,128]{1,0:T(8,128)(2,1)S(1)} %bitcast_convert_fusion), channel_id=1, source_target_pairs={{0,25},{1,26},{2,27},{3,24},{4,29},{5,30},{6,31},{7,28},{8,17},{9,... | collective-permute-start | bytes 307208 | tf_op jit(solution)/shard_map/ppermute | solution.py:314
  8.0 0.9 %copy-start.1 = (f32[128,400]{0,1:T(8,128)S(1)}, f32[128,400]{0,1:T(8,128)}, u32[]{:S(2)}) copy-start(f32[128,400]{0,1:T(8,128)} %param.10) | copy-start | bytes 614404
  9.2 6.6 %collective-permute-start.3 = (bf16[400,128]{1,0:T(8,128)(2,1)S(1)}, bf16[400,128]{1,0:T(8,128)(2,1)S(1)}, u32[]{:S(2)}, u32[]{:S(2)}) collective-permute-start(bf16[400,128]{1,0:T(8,128)(2,1)S(1)} %shard_map.145.refs_0_), channel_id=1, source_target_pairs={{0,2},{1,3},{2,0},{3,1},{4,6},{5,7},{6,4},{7,5},{8,10},{9,11},{10,... | collective-permute-start | bytes 307208 | tf_op jit(solution)/shard_map/ppermute | solution.py:307
  12.0 1.6 %copy-start = (f32[256,400]{0,1:T(8,128)S(1)}, f32[256,400]{0,1:T(8,128)}, u32[]{:S(2)}) copy-start(f32[256,400]{0,1:T(8,128)} %param.14) | copy-start | bytes 1228804
  12.1 6.9 %collective-permute-start.7 = (bf16[400,256]{1,0:T(8,128)(2,1)S(1)}, bf16[400,256]{1,0:T(8,128)(2,1)S(1)}, u32[]{:S(2)}, u32[]{:S(2)}) collective-permute-start(bf16[400,256]{1,0:T(8,128)(2,1)S(1)} %shard_map.146.refs_3_), channel_id=1, source_target_pairs={{0,4},{4,0},{8,12},{12,8},{16,20},{20,16},{24,28},{28,24},{1,5},{5... | collective-permute-start | bytes 614408 | tf_op jit(solution)/shard_map/ppermute | solution.py:304
  15.8 3.0 %copy-start.3 = (f32[128,400]{0,1:T(8,128)S(1)}, f32[128,400]{0,1:T(8,128)}, u32[]{:S(2)}) copy-start(f32[128,400]{0,1:T(8,128)} %param.12) | copy-start | bytes 614404
  15.8 3.0 %copy-start.6 = (f32[128]{0:T(128)S(1)}, f32[128]{0:T(128)}, u32[]{:S(2)}) copy-start(f32[128]{0:T(128)} %param.13) | copy-start | bytes 1540
  15.8 3.2 %collective-permute-start.6 = (bf16[400,256]{1,0:T(8,128)(2,1)S(1)}, bf16[400,256]{1,0:T(8,128)(2,1)S(1)}, u32[]{:S(2)}, u32[]{:S(2)}) collective-permute-start(bf16[400,256]{1,0:T(8,128)(2,1)S(1)} %shard_map.148.refs_3_), channel_id=1, source_target_pairs={{0,1},{1,0},{2,3},{3,2},{4,5},{5,4},{6,7},{7,6},{8,9},{9,8},{10,11... | collective-permute-start | bytes 614408 | tf_op jit(solution)/shard_map/ppermute | solution.py:307
  17.2 6.6 %collective-permute-start.5 = (bf16[400,256]{1,0:T(8,128)(2,1)S(1)}, bf16[400,256]{1,0:T(8,128)(2,1)S(1)}, u32[]{:S(2)}, u32[]{:S(2)}) collective-permute-start(bf16[400,256]{1,0:T(8,128)(2,1)S(1)} %shard_map.149.refs_2_), channel_id=1, source_target_pairs={{0,4},{4,0},{8,12},{12,8},{16,20},{20,16},{24,28},{28,24},{1,5},{5... | collective-permute-start | bytes 614408 | tf_op jit(solution)/shard_map/ppermute | solution.py:304
  18.8 9.1 %collective-permute-start.8 = (f32[408,128]{1,0:T(8,128)S(1)}, f32[408,128]{1,0:T(8,128)S(1)}, u32[]{:S(2)}, u32[]{:S(2)}) collective-permute-start(f32[408,128]{1,0:T(8,128)S(1)} %shard_map.155), channel_id=1, source_target_pairs={{0,1},{1,2},{2,3},{3,0},{4,5},{5,6},{6,7},{7,4},{8,9},{9,10},{10,1... | collective-permute-start | bytes 626696 | tf_op jit(solution)/shard_map/ppermute | solution.py:314
  25.3 1.4 %collective-permute-start.14 = (bf16[416,128]{1,0:T(8,128)(2,1)S(1)}, bf16[416,128]{1,0:T(8,128)(2,1)S(1)}, u32[]{:S(2)}, u32[]{:S(2)}) collective-permute-start(bf16[416,128]{1,0:T(8,128)(2,1)S(1)} %get-tuple-element.58), channel_id=1, source_target_pairs={{0,1},{1,0},{2,3},{3,2},{4,5},{5,4},{6,7},{7,6},{8,9},{9,8},{10,11... | collective-permute-start | bytes 319496 | tf_op jit(solution)/shard_map/ppermute | solution.py:307
  26.7 4.2 %collective-permute-start.15 = (bf16[208,128]{1,0:T(8,128)(2,1)S(1)}, bf16[208,128]{1,0:T(8,128)(2,1)S(1)}, u32[]{:S(2)}, u32[]{:S(2)}) collective-permute-start(bf16[208,128]{1,0:T(8,128)(2,1)S(1)} %get-tuple-element.60), channel_id=1, source_target_pairs={{0,2},{1,3},{2,0},{3,1},{4,6},{5,7},{6,4},{7,5},{8,10},{9,11},{10,... | collective-permute-start | bytes 159752 | tf_op jit(solution)/shard_map/ppermute | solution.py:307
  28.9 9.7 %collective-permute-start.12 = (bf16[400,256]{1,0:T(8,128)(2,1)S(1)}, bf16[400,256]{1,0:T(8,128)(2,1)S(1)}, u32[]{:S(2)}, u32[]{:S(2)}) collective-permute-start(bf16[400,256]{1,0:T(8,128)(2,1)S(1)} %get-tuple-element.56), channel_id=1, source_target_pairs={{0,4},{4,0},{8,12},{12,8},{16,20},{20,16},{24,28},{28,24},{1,5},{5... | collective-permute-start | bytes 614408 | tf_op jit(solution)/shard_map/ppermute | solution.py:304
  30.9 5.7 %collective-permute-start.16 = (bf16[208,128]{1,0:T(8,128)(2,1)S(1)}, bf16[208,128]{1,0:T(8,128)(2,1)S(1)}, u32[]{:S(2)}, u32[]{:S(2)}) collective-permute-start(bf16[208,128]{1,0:T(8,128)(2,1)S(1)} %shard_map.163.refs_0_), channel_id=1, source_target_pairs={{0,16},{4,20},{8,24},{12,28},{16,0},{20,4},{24,8},{28,12},{1,17},{... | collective-permute-start | bytes 159752 | tf_op jit(solution)/shard_map/ppermute | solution.py:304
  34.5 6.2 %collective-permute-start.9 = (bf16[400,256]{1,0:T(8,128)(2,1)S(1)}, bf16[400,256]{1,0:T(8,128)(2,1)S(1)}, u32[]{:S(2)}, u32[]{:S(2)}) collective-permute-start(bf16[400,256]{1,0:T(8,128)(2,1)S(1)} %get-tuple-element.48), channel_id=1, source_target_pairs={{0,1},{1,0},{2,3},{3,2},{4,5},{5,4},{6,7},{7,6},{8,9},{9,8},{10,11... | collective-permute-start | bytes 614408 | tf_op jit(solution)/shard_map/ppermute | solution.py:307
  34.5 12.0 %collective-permute-start.11 = (bf16[400,256]{1,0:T(8,128)(2,1)S(1)}, bf16[400,256]{1,0:T(8,128)(2,1)S(1)}, u32[]{:S(2)}, u32[]{:S(2)}) collective-permute-start(bf16[400,256]{1,0:T(8,128)(2,1)S(1)} %get-tuple-element.54), channel_id=1, source_target_pairs={{0,4},{4,0},{8,12},{12,8},{16,20},{20,16},{24,28},{28,24},{1,5},{5... | collective-permute-start | bytes 614408 | tf_op jit(solution)/shard_map/ppermute | solution.py:304
  36.7 5.6 %collective-permute-start.17 = (bf16[208,128]{1,0:T(8,128)(2,1)S(1)}, bf16[208,128]{1,0:T(8,128)(2,1)S(1)}, u32[]{:S(2)}, u32[]{:S(2)}) collective-permute-start(bf16[208,128]{1,0:T(8,128)(2,1)S(1)} %shard_map.164.refs_0_), channel_id=1, source_target_pairs={{0,8},{4,12},{8,0},{12,4},{16,24},{20,28},{24,16},{28,20},{1,9},{5... | collective-permute-start | bytes 159752 | tf_op jit(solution)/shard_map/ppermute | solution.py:304
  38.6 12.5 %collective-permute-start.13 = (bf16[400,128]{1,0:T(8,128)(2,1)S(1)}, bf16[400,128]{1,0:T(8,128)(2,1)S(1)}, u32[]{:S(2)}, u32[]{:S(2)}) collective-permute-start(bf16[400,128]{1,0:T(8,128)(2,1)S(1)} %shard_map.161), channel_id=1, source_target_pairs={{0,16},{4,20},{8,24},{12,28},{16,0},{20,4},{24,8},{28,12},{1,17},{... | collective-permute-start | bytes 307208 | tf_op jit(solution)/shard_map/ppermute | solution.py:304
  40.8 5.8 %collective-permute-start.10 = (bf16[400,128]{1,0:T(8,128)(2,1)S(1)}, bf16[400,128]{1,0:T(8,128)(2,1)S(1)}, u32[]{:S(2)}, u32[]{:S(2)}) collective-permute-start(bf16[400,128]{1,0:T(8,128)(2,1)S(1)} %get-tuple-element.50), channel_id=1, source_target_pairs={{0,2},{1,3},{2,0},{3,1},{4,6},{5,7},{6,4},{7,5},{8,10},{9,11},{10,... | collective-permute-start | bytes 307208 | tf_op jit(solution)/shard_map/ppermute | solution.py:307
  42.3 4.5 %collective-permute-start.20 = (bf16[208,128]{1,0:T(8,128)(2,1)S(1)}, bf16[208,128]{1,0:T(8,128)(2,1)S(1)}, u32[]{:S(2)}, u32[]{:S(2)}) collective-permute-start(bf16[208,128]{1,0:T(8,128)(2,1)S(1)} %shard_map.165.refs_2_.refs_0_), channel_id=1, source_target_pairs={{0,4},{4,0},{8,12},{12,8},{16,20},{20,16},{24,28},{28,24},{1,5},{5... | collective-permute-start | bytes 159752 | tf_op jit(solution)/shard_map/ppermute | solution.py:304
  43.6 7.5 %collective-permute-start.18 = (bf16[400,128]{1,0:T(8,128)(2,1)S(1)}, bf16[400,128]{1,0:T(8,128)(2,1)S(1)}, u32[]{:S(2)}, u32[]{:S(2)}) collective-permute-start(bf16[400,128]{1,0:T(8,128)(2,1)S(1)} %shard_map.166), channel_id=1, source_target_pairs={{0,24},{4,28},{8,16},{12,20},{16,8},{20,12},{24,0},{28,4},{1,25},{... | collective-permute-start | bytes 307208 | tf_op jit(solution)/shard_map/ppermute | solution.py:304
  46.7 0.9 %copy-start.2 = (f32[128,400]{0,1:T(8,128)S(1)}, f32[128,400]{0,1:T(8,128)}, u32[]{:S(2)}) copy-start(f32[128,400]{0,1:T(8,128)} %param.10) | copy-start | bytes 614404
  46.7 0.9 %copy-start.5 = (f32[128]{0:T(128)S(1)}, f32[128]{0:T(128)}, u32[]{:S(2)}) copy-start(f32[128]{0:T(128)} %param.11) | copy-start | bytes 1540
  46.7 4.7 %collective-permute-start.19 = (bf16[400,128]{1,0:T(8,128)(2,1)S(1)}, bf16[400,128]{1,0:T(8,128)(2,1)S(1)}, u32[]{:S(2)}, u32[]{:S(2)}) collective-permute-start(bf16[400,128]{1,0:T(8,128)(2,1)S(1)} %get-tuple-element.61), channel_id=1, source_target_pairs={{0,8},{4,12},{8,0},{12,4},{16,24},{20,28},{24,16},{28,20},{1,9},{5... | collective-permute-start | bytes 307208 | tf_op jit(solution)/shard_map/ppermute | solution.py:304
  46.8 4.2 %collective-permute-start.21 = (bf16[208,128]{1,0:T(8,128)(2,1)S(1)}, bf16[208,128]{1,0:T(8,128)(2,1)S(1)}, u32[]{:S(2)}, u32[]{:S(2)}) collective-permute-start(bf16[208,128]{1,0:T(8,128)(2,1)S(1)} %shard_map.168.refs_0_), channel_id=1, source_target_pairs={{0,2},{1,3},{2,0},{3,1},{4,6},{5,7},{6,4},{7,5},{8,10},{9,11},{10,... | collective-permute-start | bytes 159752 | tf_op jit(solution)/shard_map/ppermute | solution.py:307
  51.0 1.4 %collective-permute-start.22 = (bf16[416,128]{1,0:T(8,128)(2,1)S(1)}, bf16[416,128]{1,0:T(8,128)(2,1)S(1)}, u32[]{:S(2)}, u32[]{:S(2)}) collective-permute-start(bf16[416,128]{1,0:T(8,128)(2,1)S(1)} %shard_map.169), channel_id=1, source_target_pairs={{0,1},{1,0},{2,3},{3,2},{4,5},{5,4},{6,7},{7,6},{8,9},{9,8},{10,11... | collective-permute-start | bytes 319496 | tf_op jit(solution)/shard_map/ppermute | solution.py:307
  51.4 1.0 %copy-start.4 = (f32[256]{0:T(256)S(1)}, f32[256]{0:T(256)}, u32[]{:S(2)}) copy-start(f32[256]{0:T(256)} %param.15) | copy-start | bytes 3076
